TPU v7x, 32 devices: a whole 2x2x4 slice. The times are simulated.
32 devices in a mesh: row: 4 (over y, x), col: 8 (over z, core).
Axes of the slice: x: 2, y: 2, z: 4, core: 2. Of those that a mesh axis runs over, the one named last changes fastest.
Arguments:
- homolog_tensor: float32 [256, 256, 256], P('row', 'col'), may hold values from -6 to 6
- couplings: float32 [256, 256, 128], P('row', 'col'), may hold values from -6 to 6
- attention_probe_matrix: bfloat16 [256, 256], replicated, may hold values from -4 to 4
- attention_extra_matrices: bfloat16 [256, 768], replicated, may hold values from -0.375 to 0.375
- attention_final_matrix: bfloat16 [256, 256], replicated, may hold values from -0.375 to 0.375
- tensor_entry_matrices: bfloat16 [256, 64], replicated, may hold values from -0.375 to 0.375
- tensor_final_matrix: bfloat16 [1024, 128], replicated, may hold values from -3 to 3
- incoming_entry_matrices: bfloat16 [128, 512], replicated, may hold values from -0.5 to 0.5
- incoming_switch_matrix: bfloat16 [128, 128], replicated, may hold values from -0.5 to 0.5
- incoming_final_matrix: bfloat16 [128, 128], replicated, may hold values from -0.5 to 0.5
Outputs:
- refreshed_homologs: float32 [256, 256, 256], P('row', 'col')
- pair_output: float32 [256, 256, 128], P('row', 'col')
All inputs are finite; a program needn't handle non-finite values.
Results may differ from a plain program's by a relative error of at most 0.017.
The roundings to bfloat16 on the way count: a program that leaves them out, or rounds other values in their place, can miss the bound.
Values may be sent and summed in bfloat16 or wider, within the bound.
No kernel may reach another device: no remote copies, remote signals or barrier semaphores. Data moves between devices by JAX's collectives and lax.ppermute only.
A program may use at most 128 MiB of HBM per device.

v0:
```python
import jax
import jax.numpy as jnp
from jax import lax
from jax.sharding import PartitionSpec as P

FEATURE_DEPTH = 256
C_Z = 128
TENSOR_FEATURES = 32
C_TRI = 128
ATTENTION_UNITS = 8
UNIT_WIDTH = 32


def broadcast(block, axis, owner):
    block = jnp.where(lax.axis_index(axis) == owner, block, jnp.zeros_like(block))
    return lax.psum(block, axis)


def standardise_features(attended_contents):
    centre = jnp.mean(attended_contents, axis=-1, keepdims=True)
    centred = attended_contents - centre
    spread = jnp.mean(centred * centred, axis=-1, keepdims=True)
    return centred * lax.rsqrt(spread + 1e-05)


def attend_column(column, attention_probe_matrix, attention_extra_matrices):
    homolog_amount = column.shape[0]
    inner_width = ATTENTION_UNITS * UNIT_WIDTH
    queries = (
        jnp.dot(column, attention_probe_matrix, preferred_element_type=jnp.float32)
        * UNIT_WIDTH ** (-0.5)
    ).astype(jnp.bfloat16)
    projected_rows = jnp.dot(column, attention_extra_matrices, preferred_element_type=jnp.float32)
    key_rows = projected_rows[:, :inner_width].astype(jnp.bfloat16)
    value_rows = projected_rows[:, inner_width : 2 * inner_width].astype(jnp.bfloat16)
    gate_cols = jax.nn.sigmoid(projected_rows[:, 2 * inner_width :])
    queries = queries.reshape(homolog_amount, ATTENTION_UNITS, UNIT_WIDTH)
    key_rows = key_rows.reshape(homolog_amount, ATTENTION_UNITS, UNIT_WIDTH)
    value_rows = value_rows.reshape(homolog_amount, ATTENTION_UNITS, UNIT_WIDTH)
    scores = jnp.einsum("shd,thd->hst", queries, key_rows, preferred_element_type=jnp.float32)
    weights = jax.nn.softmax(scores, axis=-1).astype(jnp.bfloat16)
    attended = jnp.einsum("hst,thd->shd", weights, value_rows, preferred_element_type=jnp.float32)
    attended = attended.reshape(homolog_amount, inner_width)
    return (attended * gate_cols).astype(jnp.bfloat16)


def route_alignment(left_piece, right_piece):
    group_ratio = lax.axis_size("col") // lax.axis_size("row")
    left_rows, right_gathered = (
        lax.all_gather(left_piece, "row", axis=0, tiled=True),
        lax.all_gather(right_piece, "row", axis=0, tiled=True),
    )
    pieces = []
    for offset in range(group_ratio):
        pieces.append(broadcast(left_rows, "col", group_ratio * lax.axis_index("row") + offset))
    left_gathered = jnp.concatenate(pieces, axis=1)
    return (left_gathered, right_gathered)


def route_pair(left_piece, right_piece):
    group_ratio = lax.axis_size("col") // lax.axis_size("row")
    left_rows, right_gathered = (
        lax.all_gather(left_piece, "row", axis=0, tiled=True),
        lax.all_gather(right_piece, "row", axis=0, tiled=True),
    )
    pieces = []
    for offset in range(group_ratio):
        pieces.append(broadcast(left_rows, "col", group_ratio * lax.axis_index("row") + offset))
    left_gathered = jnp.concatenate(pieces, axis=1)
    return (left_gathered, right_gathered)


def body(
    homolog_tensor,
    couplings,
    attention_probe_matrix,
    attention_extra_matrices,
    attention_final_matrix,
    tensor_entry_matrices,
    tensor_final_matrix,
    incoming_entry_matrices,
    incoming_switch_matrix,
    incoming_final_matrix,
):
    homolog_lines = homolog_tensor.shape[0]
    amino_positions = homolog_tensor.shape[1]
    standardised = standardise_features(homolog_tensor).astype(jnp.bfloat16)
    by_residue = lax.all_to_all(standardised, "row", split_axis=1, concat_axis=0, tiled=True)
    attended = lax.map(
        lambda column: attend_column(column, attention_probe_matrix, attention_extra_matrices),
        jnp.transpose(by_residue, (1, 0, 2)),
    )
    gated = lax.all_to_all(
        jnp.transpose(attended, (1, 0, 2)), "row", split_axis=0, concat_axis=1, tiled=True
    )
    residual_change = jnp.dot(
        gated.reshape(-1, ATTENTION_UNITS * UNIT_WIDTH),
        attention_final_matrix,
        preferred_element_type=jnp.float32,
    )
    refreshed_homologs = homolog_tensor + residual_change.reshape(homolog_tensor.shape)
    standardised_result = (
        standardise_features(refreshed_homologs).astype(jnp.bfloat16).reshape(-1, FEATURE_DEPTH)
    )
    projected_rows = jnp.dot(
        standardised_result, tensor_entry_matrices, preferred_element_type=jnp.float32
    ).astype(jnp.bfloat16)
    projected_rows = projected_rows.reshape(homolog_lines, amino_positions, 2 * TENSOR_FEATURES)
    left_piece = projected_rows[:, :, :TENSOR_FEATURES].reshape(
        homolog_lines, amino_positions * TENSOR_FEATURES
    )
    right_piece = projected_rows[:, :, TENSOR_FEATURES:].reshape(
        homolog_lines, amino_positions * TENSOR_FEATURES
    )
    left_gathered, right_gathered = route_alignment(left_piece, right_piece)
    total_seqs = left_gathered.shape[0]
    row_res = left_gathered.shape[1] // TENSOR_FEATURES
    outer_product_sum = lax.dot_general(
        left_gathered, right_gathered, (((0,), (0,)), ((), ())), preferred_element_type=jnp.float32
    )
    outer_product_sum = outer_product_sum.reshape(
        row_res, TENSOR_FEATURES, amino_positions, TENSOR_FEATURES
    )
    outer_product_sum = jnp.transpose(outer_product_sum, (0, 2, 1, 3)).reshape(
        row_res * amino_positions, TENSOR_FEATURES * TENSOR_FEATURES
    )
    outer_mean = (outer_product_sum / total_seqs).astype(jnp.bfloat16)
    opm_update = jnp.dot(outer_mean, tensor_final_matrix, preferred_element_type=jnp.float32)
    pair_mid = couplings + opm_update.reshape(couplings.shape)
    pair_rows = couplings.shape[0]
    pair_normed = standardise_features(pair_mid).astype(jnp.bfloat16).reshape(-1, C_Z)
    projected_rows = jnp.dot(
        pair_normed, incoming_entry_matrices, preferred_element_type=jnp.float32
    )
    left_pair = (
        jax.nn.sigmoid(projected_rows[:, C_TRI : 2 * C_TRI]) * projected_rows[:, :C_TRI]
    ).astype(jnp.bfloat16)
    right_pair = (
        jax.nn.sigmoid(projected_rows[:, 3 * C_TRI :]) * projected_rows[:, 2 * C_TRI : 3 * C_TRI]
    ).astype(jnp.bfloat16)
    gate_pair = jax.nn.sigmoid(
        jnp.dot(pair_normed, incoming_switch_matrix, preferred_element_type=jnp.float32)
    )
    left_gathered, right_gathered = route_pair(
        left_pair.reshape(pair_rows, amino_positions * C_TRI),
        right_pair.reshape(pair_rows, amino_positions * C_TRI),
    )
    k_count = left_gathered.shape[0]
    product = jnp.einsum(
        "kic,kjc->ijc",
        left_gathered.reshape(k_count, -1, C_TRI),
        right_gathered.reshape(k_count, -1, C_TRI),
        preferred_element_type=jnp.float32,
    )
    product_normed = standardise_features(product).astype(jnp.bfloat16).reshape(-1, C_TRI)
    tri_update = jnp.dot(product_normed, incoming_final_matrix, preferred_element_type=jnp.float32)
    pair_output = pair_mid + (gate_pair * tri_update).reshape(couplings.shape)
    return (refreshed_homologs, pair_output)


def solution(mesh):
    in_specs = (
        P("row", "col", None),
        P("row", "col", None),
        P(),
        P(),
        P(),
        P(),
        P(),
        P(),
        P(),
        P(),
    )
    out_specs = (P("row", "col", None), P("row", "col", None))
    return jax.shard_map(body, mesh=mesh, in_specs=in_specs, out_specs=out_specs, check_vma=False)
```

profile of v0, /device:TPU:0, one launch (start us, length us, event | category | flops | bytes accessed | tf_op | source)
XLA Modules:
  0.0 464.8 jit_solution(8731346595426141003)
XLA Ops:
  7.2 2.1 reduce_sum.81
  9.4 1.6 multiply_reduce_fusion.2
  11.0 2.2 multiply_convert_fusion.3
  13.2 5.3 %all-to-all-start = ((bf16[64,32,256]{2,0,1:T(8,128)(2,1)}), bf16[64,32,256]{2,0,1:T(8,128)(2,1)S(1)}, u32[]{:S(2)}, u32[]{:S(2)}) async-start(bf16[64,32,256]{2,0,1:T(8,128)(2,1)} %multiply_convert_fusion.3), calls=%async_computation | async-start | bytes 2097152 | tf_op jit(solution)/shard_map/all_to_all | solution.py:88
  18.5 13.6 %all-to-all-done = bf16[64,32,256]{2,0,1:T(8,128)(2,1)S(1)} async-done(((bf16[64,32,256]{2,0,1:T(8,128)(2,1)}), bf16[64,32,256]{2,0,1:T(8,128)(2,1)S(1)}, u32[]{:S(2)}, u32[]{:S(2)}) %all-to-all-start) | async-done | bytes 1048608 | tf_op jit(solution)/shard_map/all_to_all | solution.py:88
  33.2 86.3 %while.10 = (s32[]{:T(128)}, bf16[8,256,256]{2,1,0:T(8,128)(2,1)}, bf16[8,256,256]{2,1,0:T(8,128)(2,1)}, bf16[256,768]{1,0:T(8,128)(2,1)}, bf16[256,256]{1,0:T(8,128)(2,1)S(1)}, /*index=5*/s32[]{:T(128)}) while((s32[]{:T(128)}, bf16[8,256,256]{2,1,0:T(8,128)(2,1)}, bf16[8,256,256]{2,1,0:T(8,128)(2,1)}, bf16[256,768]{1,0:T(8,128)(2,1)}, ...), condition=%wide.region_5.6_spmd, body=%wide.region_2.5_spmd.sunk | while | flops 238160384 | bytes 6307985 | solution.py:89
  33.2 1.8 fusion.93
  35.0 1.3 fusion.91
  37.9 1.7 fusion.94
  39.6 2.5 fusion.95
  44.0 1.8 fusion.93
  45.8 1.3 fusion.91
  48.6 1.7 fusion.94
  50.4 2.5 fusion.95
  52.9 1.1 copy.220
  54.8 1.8 fusion.93
  56.6 1.3 fusion.91
  59.4 1.7 fusion.94
  61.2 2.5 fusion.95
  63.7 1.1 copy.220
  65.6 1.8 fusion.93
  67.3 1.3 fusion.91
  70.2 1.7 fusion.94
  72.0 2.5 fusion.95
  76.3 1.8 fusion.93
  78.1 1.3 fusion.91
  81.0 1.7 fusion.94
  82.8 2.5 fusion.95
  87.1 1.8 fusion.93
  88.9 1.3 fusion.91
  91.8 1.7 fusion.94
  93.6 2.5 fusion.95
  97.9 1.8 fusion.93
  99.7 1.3 fusion.91
  102.6 1.7 fusion.94
  104.3 2.5 fusion.95
  108.7 1.8 fusion.93
  110.5 1.3 fusion.91
  113.4 1.7 fusion.94
  115.1 2.5 fusion.95
  119.5 2.8 copy.214
  122.3 3.5 all-to-all-start.1
  125.9 13.0 %all-to-all-done.1 = bf16[256,8,256]{2,1,0:T(8,128)(2,1)S(1)} async-done(((bf16[256,8,256]{2,1,0:T(8,128)(2,1)}), bf16[256,8,256]{2,1,0:T(8,128)(2,1)S(1)}, u32[]{:S(2)}, u32[]{:S(2)}) %all-to-all-start.1) | async-done | bytes 1048608 | tf_op jit(solution)/shard_map/all_to_all | solution.py:93
  138.9 2.7 fusion.48
  141.7 2.4 multiply_reduce_fusion.1
  146.6 10.7 %all_gather.12 = bf16[256,1024]{1,0:T(8,128)(2,1)S(1)} all-gather(bf16[64,1024]{1,0:T(8,128)(2,1)S(1)} %copy.175), channel_id=1, replica_groups=mesh['row'=4,'col'=8] {'row'}, dimensions={0}, use_global_device_ids=true | all-gather | bytes 655360 | tf_op jit(solution)/shard_map/all_gather | solution.py:50
  159.2 9.3 %all_gather.13 = bf16[256,1024]{1,0:T(8,128)(2,1)S(1)} all-gather(bf16[64,1024]{1,0:T(8,128)(2,1)S(1)} %copy.177), channel_id=1, replica_groups=mesh['row'=4,'col'=8] {'row'}, dimensions={0}, use_global_device_ids=true | all-gather | bytes 655360 | tf_op jit(solution)/shard_map/all_gather | solution.py:51
  168.4 49.5 %all-reduce.7.cloned.1.call-done = (bf16[256,1024]{1,0:T(8,128)(2,1)}, bf16[256,1024]{1,0:T(8,128)(2,1)}) async-done(((bf16[256,1024]{1,0:T(8,128)(2,1)}, bf16[256,1024]{1,0:T(8,128)(2,1)}), (bf16[256,1024]{1,0:T(8,128)(2,1)}, bf16[256,1024]{1,0:T(8,128)(2,1)})) %all-reduce.7.cloned.1.call-update) | async-done | bytes 1048592 | tf_op jit(solution)/shard_map/psum | solution.py:16
  217.9 4.4 multiply_convert_fusion
  222.4 20.3 %convert_element_type.49 = bf16[64,32,32,32]{3,2,1,0:T(8,128)(2,1)} reshape(bf16[2048,1024]{1,0:T(8,128)(2,1)} %multiply_convert_fusion) | data formatting | bytes 8388608 | tf_op jit(solution)/shard_map/convert_element_type | solution.py:127
  242.7 21.7 %copy.178 = bf16[64,32,32,32]{0,3,2,1:T(8,128)(2,1)} copy(bf16[64,32,32,32]{3,1,2,0:T(8,128)(2,1)} %bitcast.105) | data formatting | bytes 8388608 | tf_op jit(solution)/shard_map/convert_element_type | solution.py:127
  264.4 6.3 %fusion.49 = (f32[64,32]{0,1:T(8,128)S(1)}, f32[64,32,128]{2,0,1:T(8,128)S(1)}) fusion(bf16[64,32,1024]{0,2,1:T(8,128)(2,1)} %bitcast.106, bf16[1024,128]{1,0:T(8,128)(2,1)S(1)} %copy-done, f32[64,32,128]{2,1,0:T(8,128)S(1)} %copy-done.3), kind=kOutput, calls=%fused_computation.85 | convolution fusion | flops 537393152 | bytes 6561792 | tf_op jit(solution)/shard_map/dot_general | solution.py:128
  276.8 33.1 %all-gather.5.cloned.1.call-done = bf16[256,4096]{1,0:T(8,128)(2,1)} async-done(((bf16[64,4096]{1,0:T(8,128)(2,1)}), bf16[256,4096]{1,0:T(8,128)(2,1)}) %all-gather.5.cloned.1.call-update) | async-done | bytes 2097168 | tf_op jit(solution)/shard_map/all_gather | solution.py:63
  309.9 3.3 copy.183
  313.2 2.3 broadcast_select_fusion.1
  316.5 1.4 fusion.26
  317.9 29.2 %all-gather.3.cloned.1.call-done = bf16[256,4096]{1,0:T(8,128)(2,1)} async-done(((bf16[64,4096]{1,0:T(8,128)(2,1)}), bf16[256,4096]{1,0:T(8,128)(2,1)}) %all-gather.3.cloned.1.call-update) | async-done | bytes 2097168 | tf_op jit(solution)/shard_map/all_gather | solution.py:64
  347.1 3.3 copy.182
  350.4 95.9 %all-reduce.5.cloned.1.call-done = (bf16[256,4096]{0,1:T(8,128)(2,1)}, bf16[256,4096]{0,1:T(8,128)(2,1)}) async-done(((bf16[256,4096]{0,1:T(8,128)(2,1)}, bf16[256,4096]{0,1:T(8,128)(2,1)}), (bf16[256,4096]{0,1:T(8,128)(2,1)}, bf16[256,4096]{0,1:T(8,128)(2,1)})) %all-reduce.5.cloned.1.call-update) | async-done | bytes 4194320 | tf_op jit(solution)/shard_map/psum | solution.py:16
  446.3 2.5 pad_maximum_fusion
  448.8 3.5 bitcast_reduce_fusion
  452.9 1.5 copy.187
  454.5 1.5 convolution_multiply_fusion.1
  456.7 1.6 copy.189
  (134 shorter events, 38.8 us)
Async XLA Ops:
  7.2 257.2 %copy-start = (bf16[1024,128]{1,0:T(8,128)(2,1)S(1)}, bf16[1024,128]{1,0:T(8,128)(2,1)}, u32[]{:S(2)}) copy-start(bf16[1024,128]{1,0:T(8,128)(2,1)} %param.18) | copy-start | bytes 786436
  7.2 2.3 copy-start.1
  13.2 20.0 %copy-start.4 = (bf16[256,256]{1,0:T(8,128)(2,1)S(1)}, bf16[256,256]{1,0:T(8,128)(2,1)}, u32[]{:S(2)}) copy-start(bf16[256,256]{1,0:T(8,128)(2,1)} %param.14) | copy-start | bytes 393220
  13.2 18.9 %all-to-all-start = ((bf16[64,32,256]{2,0,1:T(8,128)(2,1)}), bf16[64,32,256]{2,0,1:T(8,128)(2,1)S(1)}, u32[]{:S(2)}, u32[]{:S(2)}) async-start(bf16[64,32,256]{2,0,1:T(8,128)(2,1)} %multiply_convert_fusion.3), calls=%async_computation | async-start | bytes 2097152 | tf_op jit(solution)/shard_map/all_to_all | solution.py:88
  37.1 2.5 copy-start.5
  37.9 1.7 copy-start.6
  47.9 2.5 copy-start.5
  48.6 1.7 copy-start.6
  58.7 2.5 copy-start.5
  59.4 1.7 copy-start.6
  69.5 2.5 copy-start.5
  70.2 1.7 copy-start.6
  80.3 2.5 copy-start.5
  81.0 1.7 copy-start.6
  91.0 2.5 copy-start.5
  91.8 1.7 copy-start.6
  101.8 2.5 copy-start.5
  102.6 1.7 copy-start.6
  112.6 2.5 copy-start.5
  113.4 1.7 copy-start.6
  122.3 16.6 %all-to-all-start.1 = ((bf16[256,8,256]{2,1,0:T(8,128)(2,1)}), bf16[256,8,256]{2,1,0:T(8,128)(2,1)S(1)}, u32[]{:S(2)}, u32[]{:S(2)}) async-start(bf16[256,8,256]{2,1,0:T(8,128)(2,1)} %bitcast.76), calls=%async_computation.1 | async-start | bytes 2097152 | tf_op jit(solution)/shard_map/all_to_all | solution.py:93
  125.8 92.1 %all-reduce.7.cloned.1.call-start = ((), (), s32[]{:S(2)}) async-start(), calls=%async_computation.5 | async-start | bytes 2097152 | tf_op jit(solution)/shard_map/psum | solution.py:16
  141.5 2.7 copy-start.2
  144.0 0.9 copy-start.10
  158.4 151.5 %all-gather.5.cloned.1.call-start = ((), (), s32[]{:S(2)}) async-start(), calls=%async_computation.3 | async-start | bytes 2621440 | tf_op jit(solution)/shard_map/all_gather | solution.py:63
  242.7 21.7 %copy-start.3 = (f32[64,32,128]{2,1,0:T(8,128)S(1)}, f32[64,32,128]{2,1,0:T(8,128)}, u32[]{:S(2)}) copy-start(f32[64,32,128]{2,1,0:T(8,128)} %param.13) | copy-start | bytes 3145732
  270.7 2.5 copy-start.9
  272.3 0.8 copy-start.7
  275.5 71.6 %all-gather.3.cloned.1.call-start = ((), (), s32[]{:S(2)}) async-start(), calls=%async_computation.2 | async-start | bytes 2621440 | tf_op jit(solution)/shard_map/all_gather | solution.py:64
  276.6 169.7 %all-reduce.5.cloned.1.call-start = ((), (), s32[]{:S(2)}) async-start(), calls=%async_computation.4 | async-start | bytes 8388608 | tf_op jit(solution)/shard_map/psum | solution.py:16
  315.5 1.0 copy-start.8
  315.5 1.0 copy-start.12
  452.7 1.8 copy-start.11
Sparse Core Ops, SparseCore 0:
  158.5 59.3 all-reduce.6
  275.6 34.2 all-gather.4
  311.8 35.2 all-gather.2
  349.4 96.8 all-reduce.4
where the time goes:
time: 467 us; the launch traced here: 465 us
  waiting for transfers between devices  234 us (50%)
  local copies, waits for them, and re-layouts  83 us (18%)
  matrix products  80.1 us (17%)
  other arithmetic  23.7 us (5%)
  blocking collectives  19.9 us (4%)
  between operations  14.1 us (3%)
  starting transfers between devices  9.2 us (2%)
    psum x2, waiting for transfers between devices, broadcast(): return lax.psum(block, axis)  145 us
    convert_element_type x2, local copies, waits for them, and re-layouts, body(): outer_mean = (outer_product_sum / total_seqs).astype(jnp.bfloat16)  42 us
    all_gather x1, waiting for transfers between devices, route_pair(): lax.all_gather(left_piece, 'row', axis=0, tiled=True)  33.1 us
    all_gather x1, waiting for transfers between devices, route_pair(): lax.all_gather(right_piece, 'row', axis=0, tiled=True)  29.2 us
    dot_general x8, matrix products, attend_column(): jnp.einsum('hst,thd->shd', weights, value_rows, preferred_element_type=jn...  20.3 us
    dot_general x8, matrix products, attend_column(): jnp.dot(column, attention_probe_matrix, preferred_element_type=jnp.float32)  14.3 us
    sub x8, matrix products, attend_column(): weights = jax.nn.softmax(scores, axis=-1).astype(jnp.bfloat16)  13.9 us
    all_to_all x1, waiting for transfers between devices, body(): lax.all_to_all(standardised, 'row', split_axis=1, concat_axis=0, tiled=True)  13.6 us
  transfers between devices with their start and end apart: 6, of which 6 were waited for; matrix products, arithmetic and copies ran while one was open for 3% of the time, Pallas kernels for 0%

commit v1 on v0

v1 whole, which is shorter than its diff:
```python
import functools

import jax
import jax.numpy as jnp
from jax import lax
from jax.experimental import pallas as pl
from jax.experimental.pallas import tpu as pltpu
from jax.sharding import PartitionSpec as P

FEATURE_DEPTH = 256
C_Z = 128
TENSOR_FEATURES = 32
C_TRI = 128
ATTENTION_UNITS = 8
UNIT_WIDTH = 32
EPS = 1e-05
HALF = C_TRI // 2
GROUP = 4
F32 = jnp.float32
BF16 = jnp.bfloat16
NT = (((1,), (1,)), ((), ()))
VMEM_LIMIT = 56 * 1024 * 1024


def matmul(left, right):
    return jnp.dot(left, right, preferred_element_type=F32)


def matmul_nt(left, right):
    return lax.dot_general(left, right, NT, preferred_element_type=F32)


def sigmoid(values):
    return 1.0 / (1.0 + jnp.exp(-values))


def params(*semantics):
    return pltpu.CompilerParams(
        dimension_semantics=semantics or None, vmem_limit_bytes=VMEM_LIMIT
    )


def standardise_kernel(first_ref, second_ref, high_ref, low_ref):
    seqs, residues, lanes = first_ref.shape
    first_rows = first_ref.reshape(seqs * residues, lanes)
    second_rows = second_ref.reshape(seqs * residues, lanes)
    lane = lax.broadcasted_iota(jnp.int32, (seqs, 128), 1)
    spreads = jnp.zeros((seqs, 128), F32)
    for n in range(residues):
        rows = pl.ds(n, seqs, stride=residues)
        column = jnp.concatenate([first_rows[rows, :], second_rows[rows, :]], axis=1)
        centred = column - jnp.mean(column, axis=1, keepdims=True)
        variance = jnp.mean(centred * centred, axis=1, keepdims=True) + EPS
        scale = lax.rsqrt(variance)
        normed = centred * scale
        high = normed.astype(BF16)
        high_ref[n] = high
        low_ref[n, :seqs, :] = (normed - high.astype(F32)).astype(BF16)
        spreads = jnp.where(lane == n, variance * scale, spreads)
    spreads = spreads.T
    row = lax.broadcasted_iota(jnp.int32, (16, seqs), 0)
    for n in range(residues):
        spread = jnp.broadcast_to(spreads[n : n + 1, :], (16, seqs))
        coarse = spread.astype(BF16).astype(F32)
        kept = jnp.where(row == 0, coarse, jnp.where(row == 1, spread - coarse, 0.0))
        kept = jnp.concatenate([kept, jnp.zeros((16, 2 * lanes - seqs), F32)], axis=1)
        low_ref[n, seqs:, :] = kept.astype(BF16)


def standardise(block):
    seqs, residues, depth = block.shape
    half = depth // 2
    return pl.pallas_call(
        standardise_kernel,
        grid=(residues // 8,),
        in_specs=[
            pl.BlockSpec((seqs, 8, half), lambda g: (0, g, 0)),
            pl.BlockSpec((seqs, 8, half), lambda g: (0, g, 1)),
        ],
        out_specs=[
            pl.BlockSpec((8, seqs, depth), lambda g: (g, 0, 0)),
            pl.BlockSpec((8, seqs + 16, depth), lambda g: (g, 0, 0)),
        ],
        out_shape=[
            jax.ShapeDtypeStruct((residues, seqs, depth), BF16),
            jax.ShapeDtypeStruct((residues, seqs + 16, depth), BF16),
        ],
        compiler_params=params("arbitrary"),
        name="standardise",
    )(block, block)


def attention_kernel(normed_ref, key_ref, others_ref, gated_ref, turned_ref):
    blocks, _, seqs, depth = normed_ref.shape
    total = blocks * seqs
    inner = ATTENTION_UNITS * UNIT_WIDTH
    column = normed_ref[...].reshape(total, depth)
    key_rows = matmul(column, key_ref[...]).astype(BF16)
    projected = matmul_nt(others_ref[...], column)
    queries = (projected[:inner] * UNIT_WIDTH ** (-0.5)).astype(BF16)
    value_rows = projected[inner : 2 * inner].astype(BF16)
    gates = sigmoid(projected[2 * inner :])
    ones = jnp.ones((16, total), BF16)
    parts = []
    for h in range(ATTENTION_UNITS):
        low, high = h * UNIT_WIDTH, (h + 1) * UNIT_WIDTH
        pieces = [queries[low:high]]
        if low > 0:
            pieces.insert(0, jnp.zeros((low, total), BF16))
        if high < inner:
            pieces.append(jnp.zeros((inner - high, total), BF16))
        scores = matmul(key_rows, jnp.concatenate(pieces, axis=0))
        weights = jnp.exp(scores - jnp.max(scores, axis=0, keepdims=True)).astype(BF16)
        attended = matmul(jnp.concatenate([value_rows[low:high], ones], axis=0), weights)
        parts.append(
            attended[:UNIT_WIDTH] * (gates[low:high] / attended[UNIT_WIDTH : UNIT_WIDTH + 1])
        )
    gated = jnp.concatenate(parts, axis=0)
    turned_ref[0] = gated.astype(BF16)
    gated_ref[...] = gated.T.astype(BF16).reshape(gated_ref.shape)


def attention(normed, key_matrix, other_matrices):
    blocks, residues, seqs, depth = normed.shape
    total = blocks * seqs
    inner = ATTENTION_UNITS * UNIT_WIDTH
    return pl.pallas_call(
        attention_kernel,
        grid=(residues,),
        in_specs=[
            pl.BlockSpec((blocks, 1, seqs, depth), lambda n: (0, n, 0, 0)),
            pl.BlockSpec((depth, inner), lambda n: (0, 0)),
            pl.BlockSpec((3 * inner, depth), lambda n: (0, 0)),
        ],
        out_specs=[
            pl.BlockSpec((blocks, 1, seqs, inner), lambda n: (0, n, 0, 0)),
            pl.BlockSpec((1, inner, total), lambda n: (n, 0, 0)),
        ],
        out_shape=[
            jax.ShapeDtypeStruct((blocks, residues, seqs, inner), BF16),
            jax.ShapeDtypeStruct((residues, inner, total), BF16),
        ],
        compiler_params=params("arbitrary"),
        name="attention",
    )(normed, key_matrix, other_matrices)


def alignment_kernel(high_ref, low_ref, turned_ref, final_ref, entry_ref, left_ref, right_ref):
    blocks, _, seqs, depth = high_ref.shape
    total = blocks * seqs
    low = low_ref[:, 0, :seqs, :].reshape(total, depth)
    column = high_ref[...].reshape(total, depth).astype(F32) + low.astype(F32)
    spreads = []
    for block in range(blocks):
        kept = low_ref[block, 0, seqs:, :seqs].astype(F32)
        spreads.append(jnp.sum(kept, axis=0, keepdims=True))
    spread = jnp.concatenate(spreads, axis=1)
    updated = column.T * spread + matmul(final_ref[...], turned_ref[0])
    centred = updated - jnp.mean(updated, axis=0, keepdims=True)
    variance = jnp.mean(centred * centred, axis=0, keepdims=True)
    normed = (centred * lax.rsqrt(variance + EPS)).astype(BF16)
    projected = matmul(entry_ref[...], normed).astype(BF16)
    left_ref[0] = projected[:TENSOR_FEATURES]
    right_ref[0] = projected[TENSOR_FEATURES:]


def alignment(high, low, turned, final_matrix, entry_matrices):
    blocks, residues, seqs, depth = high.shape
    total = blocks * seqs
    side = jax.ShapeDtypeStruct((residues, TENSOR_FEATURES, total), BF16)
    side_spec = pl.BlockSpec((1, TENSOR_FEATURES, total), lambda n: (n, 0, 0))
    return pl.pallas_call(
        alignment_kernel,
        grid=(residues,),
        in_specs=[
            pl.BlockSpec((blocks, 1, seqs, depth), lambda n: (0, n, 0, 0)),
            pl.BlockSpec((blocks, 1, seqs + 16, depth), lambda n: (0, n, 0, 0)),
            pl.BlockSpec((1, depth, total), lambda n: (n, 0, 0)),
            pl.BlockSpec(final_matrix.shape, lambda n: (0, 0)),
            pl.BlockSpec(entry_matrices.shape, lambda n: (0, 0)),
        ],
        out_specs=[side_spec, side_spec],
        out_shape=[side, side],
        compiler_params=params("arbitrary"),
        name="alignment",
    )(high, low, turned, final_matrix, entry_matrices)


def pair_kernel(
    left_ref,
    right_ref,
    spread_ref,
    couplings_ref,
    entry_ref,
    switch_ref,
    mid_ref,
    gate_ref,
    left_pair_ref,
    right_pair_ref,
    outer_ref,
    sum_ref,
    left_rows_ref,
    right_rows_ref,
):
    features = TENSOR_FEATURES
    total = left_ref.shape[1]
    rows = left_ref.shape[0] // features
    columns = right_ref.shape[0] // features
    groups = columns // GROUP
    pairs = features // 2
    step = 512

    def outer_step(m, carry):
        piece = left_ref[pl.ds(pl.multiple_of(m * step, step), step), :]
        for g in range(0, groups, 2):
            wide = right_ref[g * 128 : (g + 2) * 128, :]
            outer = matmul_nt(piece, wide) * (1.0 / total)
            target = pl.ds(pl.multiple_of(m * step, step), step)
            outer_ref[g, target, :] = outer[:, :128]
            outer_ref[g + 1, target, :] = outer[:, 128:]
        return carry

    lax.fori_loop(0, left_ref.shape[0] // step, outer_step, 0)

    def channel_step(p, carry):
        pieces = []
        for g in range(groups):
            first = outer_ref[g, pl.ds(2 * p, rows, stride=features), :]
            second = outer_ref[g, pl.ds(2 * p + 1, rows, stride=features), :]
            pieces.append(jnp.concatenate([first, second], axis=1).astype(BF16))
        update = matmul(jnp.concatenate(pieces, axis=0), spread_ref[p])

        @pl.when(p == 0)
        def _():
            sum_ref[...] = update

        @pl.when(p > 0)
        def _():
            sum_ref[...] += update

        return carry

    lax.fori_loop(0, pairs, channel_step, 0)

    for b in range(columns):
        g, place = b // GROUP, b % GROUP
        mid = sum_ref[g * rows : (g + 1) * rows, place * C_Z : (place + 1) * C_Z]
        mid = mid + couplings_ref[pl.ds(b, rows, stride=columns), :]
        mid_ref[b] = mid
        centred = mid - jnp.mean(mid, axis=1, keepdims=True)
        variance = jnp.mean(centred * centred, axis=1, keepdims=True)
        normed = (centred * lax.rsqrt(variance + EPS)).astype(BF16)
        gate_ref[b] = sigmoid(matmul(normed, switch_ref[...]))
        blank = jnp.zeros_like(normed)
        twice = jnp.concatenate(
            [
                jnp.concatenate([normed, blank], axis=1),
                jnp.concatenate([blank, normed], axis=1),
            ],
            axis=0,
        )
        sides = matmul_nt(entry_ref[...], twice)
        target = slice(b * HALF, (b + 1) * HALF)
        left_rows_ref[target, :] = sigmoid(sides[HALF : 2 * HALF]) * sides[:HALF]
        right_rows_ref[target, :] = sigmoid(sides[3 * HALF :]) * sides[2 * HALF : 3 * HALF]

    def turn_step(c, carry):
        chosen = pl.ds(c, columns, stride=HALF)
        left_pair_ref[c] = left_rows_ref[chosen, :].astype(BF16)
        right_pair_ref[c] = right_rows_ref[chosen, :].astype(BF16)
        return carry

    lax.fori_loop(0, HALF, turn_step, 0)


def pair_update(left, right, spread, couplings, entry_matrices, switch_matrix):
    rows, columns, depth = couplings.shape
    side = jax.ShapeDtypeStruct((HALF, columns, 2 * rows), BF16)
    whole = jax.ShapeDtypeStruct((columns, rows, depth), F32)
    vmem = pl.BlockSpec(memory_space=pltpu.VMEM)
    return pl.pallas_call(
        pair_kernel,
        in_specs=[vmem] * 6,
        out_specs=[vmem] * 4,
        out_shape=[whole, whole, side, side],
        scratch_shapes=[
            pltpu.VMEM((columns // GROUP, rows * TENSOR_FEATURES, 128), F32),
            pltpu.VMEM((columns // GROUP * rows, GROUP * depth), F32),
            pltpu.VMEM((columns * HALF, 2 * rows), F32),
            pltpu.VMEM((columns * HALF, 2 * rows), F32),
        ],
        compiler_params=params(),
        name="pair_update",
    )(left, right, spread, couplings.reshape(rows * columns, depth), entry_matrices, switch_matrix)


def triangle_kernel(left_ref, right_ref, mid_ref, gate_ref, final_ref, out_ref, product_ref):
    halves, blocks, channels, part, lanes = left_ref.shape
    rows = halves * part
    columns = right_ref.shape[2]
    step = pl.program_id(0)
    lane = lax.broadcasted_iota(jnp.int32, (rows, blocks * lanes), 1)
    front = lax.rem(lane, lanes) < lanes // 2
    for c in range(channels):
        left = jnp.concatenate(
            [
                jnp.concatenate([left_ref[h, k, c] for k in range(blocks)], axis=1)
                for h in range(halves)
            ],
            axis=0,
        )
        right = jnp.concatenate([right_ref[k, c] for k in range(blocks)], axis=1)
        blank = jnp.zeros_like(left)
        masked = jnp.concatenate(
            [jnp.where(front, left, blank), jnp.where(front, blank, left)], axis=0
        )
        first = pl.multiple_of((step * channels + c) * columns, columns)
        product_ref[pl.ds(first, columns), :] = matmul_nt(right, masked)

    @pl.when(step == pl.num_programs(0) - 1)
    def _():
        for j in range(columns):
            product = product_ref[pl.ds(j, HALF, stride=columns), :]
            mean = jnp.sum(product, axis=0, keepdims=True)
            mean = (mean + pltpu.roll(mean, rows, 1)) * (1.0 / C_TRI)
            centred = product - mean
            variance = jnp.sum(centred * centred, axis=0, keepdims=True)
            variance = (variance + pltpu.roll(variance, rows, 1)) * (1.0 / C_TRI)
            normed = (centred * lax.rsqrt(variance + EPS)).T.astype(BF16)
            update = matmul(normed[:rows], final_ref[:HALF, :])
            update = update + matmul(normed[rows:], final_ref[HALF:, :])
            out_ref[pl.ds(j, rows, stride=columns), :] = mid_ref[j] + gate_ref[j] * update


def triangle(left, right, mid, gate, final_matrix):
    halves, blocks, _, part, lanes = left.shape
    columns, rows, depth = mid.shape
    channels = 8
    whole = pl.BlockSpec((columns, rows, depth), lambda c: (0, 0, 0))
    out = pl.pallas_call(
        triangle_kernel,
        grid=(HALF // channels,),
        in_specs=[
            pl.BlockSpec((halves, blocks, channels, part, lanes), lambda c: (0, 0, c, 0, 0)),
            pl.BlockSpec((blocks, channels, columns, lanes), lambda c: (0, c, 0, 0)),
            whole,
            whole,
            pl.BlockSpec(final_matrix.shape, lambda c: (0, 0)),
        ],
        out_specs=pl.BlockSpec((rows * columns, depth), lambda c: (0, 0)),
        out_shape=jax.ShapeDtypeStruct((rows * columns, depth), F32),
        scratch_shapes=[pltpu.VMEM((HALF * columns, 2 * rows), F32)],
        compiler_params=params("arbitrary"),
        name="triangle",
    )(left, right, mid, gate, final_matrix)
    return out.reshape(rows, columns, depth)


def swap_cores(block):
    count = lax.axis_size("col")
    return lax.ppermute(block, "col", [(c, c ^ 1) for c in range(count)])


def in_core_order(own, other):
    first = lax.rem(lax.axis_index("col"), 2) == 0
    return jnp.where(first, jnp.stack([own, other]), jnp.stack([other, own]))


def gather_turned_direct(block):
    rows, columns = lax.axis_size("row"), lax.axis_size("col")
    me = lax.axis_index("col") // 2
    arrived = []
    for shift in range(rows):
        moves = []
        for r in range(rows):
            for q in range(rows):
                for core in range(columns // rows):
                    source = r * columns + 2 * q + core
                    moves.append((source, q * columns + 2 * ((r + shift) % rows) + core))
        arrived.append(lax.ppermute(block, ("row", "col"), moves))
    arrived = jnp.stack(arrived)
    order = lax.rem(me - jnp.arange(rows) + rows, rows)
    own = jnp.take(arrived, order, axis=0)
    return in_core_order(own, swap_cores(own))


def gather_turned(block):
    columns = lax.axis_size("col")
    same_core = [list(range(core, columns, 2)) for core in range(2)]
    gathered = lax.all_gather(block, "col", axis_index_groups=same_core)
    own = lax.all_to_all(gathered, "row", split_axis=0, concat_axis=0)
    return in_core_order(own, swap_cores(own))


def spread_weights(matrix):
    weights = matrix.reshape(TENSOR_FEATURES // 2, 2, 1, TENSOR_FEATURES, 1, C_Z)
    same = jnp.eye(GROUP, dtype=matrix.dtype).reshape(1, 1, GROUP, 1, GROUP, 1)
    return (weights * same).reshape(TENSOR_FEATURES // 2, 2 * 128, GROUP * C_Z)


def paired_entries(matrices):
    turned = matrices.reshape(C_Z, 4, 2, HALF)
    return jnp.transpose(turned, (1, 3, 2, 0)).reshape(4 * HALF, 2 * C_Z)


def body(
    homolog_tensor,
    couplings,
    attention_probe_matrix,
    attention_extra_matrices,
    attention_final_matrix,
    tensor_entry_matrices,
    tensor_final_matrix,
    incoming_entry_matrices,
    incoming_switch_matrix,
    incoming_final_matrix,
):
    inner = ATTENTION_UNITS * UNIT_WIDTH
    row_count = lax.axis_size("row")
    seqs, residues, depth = homolog_tensor.shape
    own_residues = residues // row_count
    high, low = standardise(homolog_tensor)
    high = high.reshape(row_count, own_residues, seqs, depth)
    low = low.reshape(row_count, own_residues, seqs + 16, depth)
    high = lax.all_to_all(high, "row", split_axis=0, concat_axis=0)
    low = lax.all_to_all(low, "row", split_axis=0, concat_axis=0)
    others = jnp.concatenate(
        [attention_probe_matrix.T, attention_extra_matrices[:, inner:].T], axis=0
    )
    gated, turned = attention(high, attention_extra_matrices[:, :inner], others)
    left_piece, right_piece = alignment(
        high, low, turned, attention_final_matrix.T, tensor_entry_matrices.T
    )
    gated = lax.all_to_all(gated, "row", split_axis=0, concat_axis=0)
    gated = jnp.transpose(gated.reshape(residues, seqs, inner), (1, 0, 2))
    change = jnp.dot(
        gated.reshape(-1, inner), attention_final_matrix, preferred_element_type=F32
    )
    refreshed_homologs = homolog_tensor + change.reshape(homolog_tensor.shape)

    right = lax.all_gather(right_piece, "row")
    left = gather_turned_direct(left_piece)
    total = left.shape[-1]
    mid, gate, left_pair, right_pair = pair_update(
        left.reshape(-1, total),
        right.reshape(-1, total),
        spread_weights(tensor_final_matrix),
        couplings,
        paired_entries(incoming_entry_matrices),
        incoming_switch_matrix,
    )
    right_pair = lax.all_gather(right_pair, "row")
    left_pair = gather_turned(left_pair)
    pair_output = triangle(left_pair, right_pair, mid, gate, incoming_final_matrix)
    return (refreshed_homologs, pair_output)


def solution(mesh):
    in_specs = (
        P("row", "col", None),
        P("row", "col", None),
        P(),
        P(),
        P(),
        P(),
        P(),
        P(),
        P(),
        P(),
    )
    out_specs = (P("row", "col", None), P("row", "col", None))
    return jax.shard_map(body, mesh=mesh, in_specs=in_specs, out_specs=out_specs, check_vma=False)
```

time: 467 us -> 265 us (0.57)
  waiting for transfers between devices: 234 us -> 77.3 us
  matrix products: 80.1 us -> 2.24 us
  local copies, waits for them, and re-layouts: 83 us -> 15.8 us
  Pallas kernels: 0 us -> 64.2 us
  blocking collectives: 19.9 us -> 60.8 us
  other arithmetic: 23.7 us -> 11.3 us
  starting transfers between devices: 9.2 us -> 16.4 us
    psum x2 -> x0, waiting for transfers between devices: 145 us -> none  [broadcast(): return lax.psum(block, axis)]
    pallas_call x0 -> x5, Pallas kernels: none -> 64.2 us  [the longest x1 22.4 us: attention(): pl.pallas_call(attention_kernel, grid=(residues,), in_specs=[pl.BlockSpec...]
    dot_general x32 -> x1, matrix products: 66.2 us -> 2.24 us  [body(): jnp.dot(gated.reshape(-1, inner), attention_final_matrix, preferred_eleme...]
    all_to_all x0 -> x2, blocking collectives: none -> 48.1 us  [the longest x1 28 us: body(): gated = lax.all_to_all(gated, 'row', split_axis=0, concat_axis=0)]
    convert_element_type x5 -> x0, local copies, waits for them, and re-layouts: 44.2 us -> none  [the longest x2 42 us: body(): outer_mean = (outer_product_sum / total_seqs).astype(jnp.bfloat16)]
    all_gather x2, waiting for transfers between devices: 62.3 us -> 46.5 us  [the longest x1 46.5 us: gather_turned(): gathered = lax.all_gather(block, 'col', axis_index_groups=same_core)]
    sub x8 -> x0, matrix products: 13.9 us -> none  [attend_column(): weights = jax.nn.softmax(scores, axis=-1).astype(jnp.bfloat16)]
    slice x27 -> x3, local copies, waits for them, and re-layouts: 13.6 us -> 0.68 us  [the longest x1 0.67 us: body(): gated, turned = attention(high, attention_extra_matrices[:, :inner], others)]
  transfers between devices with their start and end apart: 6 -> 10, of which waited for: 6 -> 2; matrix products, arithmetic and copies ran while one was open for 3% -> 10% of each run, Pallas kernels for 0% -> 8%
where the time goes in v1:
time: 265 us; the launch traced here: 264 us
  waiting for transfers between devices  77.3 us (29%)
  Pallas kernels  64.2 us (24%)
  blocking collectives  60.8 us (23%)
  starting transfers between devices  16.4 us (6%)
  local copies, waits for them, and re-layouts  15.8 us (6%)
  between operations  15.7 us (6%)
  other arithmetic  11.3 us (4%)
    all_gather x1, waiting for transfers between devices, gather_turned(): gathered = lax.all_gather(block, 'col', axis_index_groups=same_core)  46.5 us
    all_to_all x1, waiting for transfers between devices, gather_turned(): own = lax.all_to_all(gathered, 'row', split_axis=0, concat_axis=0)  30.2 us
    all_to_all x1, blocking collectives, body(): gated = lax.all_to_all(gated, 'row', split_axis=0, concat_axis=0)  28 us
    pallas_call x1, Pallas kernels, attention(): pl.pallas_call(attention_kernel, grid=(residues,), in_specs=[pl.BlockSpec...  22.4 us
    all_to_all x1, blocking collectives, body(): high = lax.all_to_all(high, 'row', split_axis=0, concat_axis=0)  20.1 us
    pallas_call x1, Pallas kernels, pair_update(): pl.pallas_call(pair_kernel, in_specs=[vmem] * 6, out_specs=[vmem] * 4, ou...  19.4 us
    all_gather x1, blocking collectives, body(): right = lax.all_gather(right_piece, 'row')  12.7 us
    mul x3, local copies, waits for them, and re-layouts, spread_weights(): return (weights * same).reshape(TENSOR_FEATURES // 2, 2 * 128, GROUP * C_Z)  11.5 us
  transfers between devices with their start and end apart: 10, of which 2 were waited for; matrix products, arithmetic and copies ran while one was open for 10% of the time, Pallas kernels for 8%

profile of v1, /device:TPU:0, one launch (start us, length us, event | category | flops | bytes accessed | tf_op | source)
XLA Modules:
  0.0 263.8 jit_solution(14789178551994180540)
XLA Ops:
  8.0 0.0 copy-start.3
  8.0 0.0 slice-start
  8.0 0.0 copy-start.7
  8.0 4.4 %standardise.1 = (bf16[32,64,256]{2,1,0:T(8,128)(2,1)}, bf16[32,80,256]{2,1,0:T(8,128)(2,1)}) custom-call(f32[64,32,256]{2,1,0:T(8,128)} %second_ref.1, f32[64,32,256]{2,1,0:T(8,128)} %second_ref.1), custom_call_target="tpu_custom_call" | custom-call | tf_op jit(solution)/shard_map/standardise/pallas_call | solution.py:73
  12.4 20.1 %all_to_all.20.normed_ref.high_ref = bf16[4,8,64,256]{3,2,1,0:T(8,128)(2,1)} all-to-all(bf16[4,8,64,256]{3,2,1,0:T(8,128)(2,1)} %bitcast.54), channel_id=1, replica_groups=mesh['row'=4,'col'=8] {'row'}, dimensions={0} | all-to-all | bytes 2097152 | tf_op jit(solution)/shard_map/all_to_all | solution.py:425
  32.6 3.5 %all-to-all-start.2 = ((bf16[4,8,80,256]{3,2,1,0:T(8,128)(2,1)}), bf16[4,8,80,256]{3,2,1,0:T(8,128)(2,1)S(1)}, u32[]{:S(2)}, u32[]{:S(2)}) async-start(bf16[4,8,80,256]{3,2,1,0:T(8,128)(2,1)} %bitcast.50), calls=%async_computation.2 | async-start | bytes 2621440 | tf_op jit(solution)/shard_map/all_to_all | solution.py:426
  36.1 0.0 copy-start.5
  36.1 0.0 all-gather.6.cloned.1.call-start
  36.2 0.0 copy-done.3
  36.2 0.7 slice.6.key_ref
  36.9 0.0 slice-done
  36.9 0.1 copy.29
  37.0 0.0 copy-done.7
  37.0 0.1 copy.23
  37.1 0.0 copy-done.4
  37.1 0.8 copy.26
  37.9 0.8 pad_maximum_fusion.1.others_ref
  38.7 22.4 %attention.1 = (bf16[4,8,64,256]{3,2,1,0:T(8,128)(2,1)}, bf16[8,256,256]{2,1,0:T(8,128)(2,1)}) custom-call(bf16[4,8,64,256]{3,2,1,0:T(8,128)(2,1)} %all_to_all.20.normed_ref.high_ref, bf16[256,256]{1,0:T(8,128)(2,1)} %slice.6.key_ref, bf16[768,256]{1,0:T(8,128)(2,1)} %pad_maximum_fusion.1.others_ref), custom_call_target="tpu_custom_call" | custom-call | tf_op jit(solution)/shard_map/attention/pallas_call | solution.py:127
  61.0 0.0 all-to-all-done.2.low_ref
  61.0 1.1 copy-done.1
  62.1 7.3 %alignment.1 = (bf16[8,32,256]{2,1,0:T(8,128)(2,1)}, bf16[8,32,256]{2,1,0:T(8,128)(2,1)}) custom-call(bf16[4,8,64,256]{3,2,1,0:T(8,128)(2,1)} %all_to_all.20.normed_ref.high_ref, bf16[4,8,80,256]{3,2,1,0:T(8,128)(2,1)} %copy-done.1, bf16[8,256,256]{2,1,0:T(8,128)(2,1)} %get-tuple-element.15.turned_ref, bf16[256,256]{1,0:T(8,128)(2,1)} %bitcast.57, ...), custom_call_target="tpu_custom_call" | custom-call | tf_op jit(solution)/shard_map/alignment/pallas_call | solution.py:172
  69.4 1.7 collective-permute-start.1
  71.2 2.8 %collective-permute-start.2 = (bf16[8,32,256]{2,1,0:T(8,128)(2,1)}, bf16[8,32,256]{2,1,0:T(8,128)(2,1)S(1)}, u32[]{:S(2)}, u32[]{:S(2)}) collective-permute-start(bf16[8,32,256]{2,1,0:T(8,128)(2,1)} %get-tuple-element.16), channel_id=1, source_target_pairs={{0,4},{1,5},{2,12},{3,13},{4,20},{5,21},{6,28},{7,29},{8,6},{9,7},... | collective-permute-start | bytes 393224 | tf_op jit(solution)/shard_map/ppermute | solution.py:380
  74.0 2.1 collective-permute-start.3
  76.1 1.6 collective-permute-start
  77.6 0.0 copy-done.5
  77.7 4.1 %mul.23 = bf16[16,2,4,32,4,128]{5,4,3,2,1,0:T(4,128)(2,1)} broadcast(bf16[16,2,32,128]{3,2,1,0:T(8,128)(2,1)S(1)} %bitcast.63), dimensions={0,1,3,5} | broadcast | bytes 4456448 | tf_op jit(solution)/shard_map/mul | solution.py:398
  81.8 7.2 %mul.24 = bf16[16,256,512]{2,1,0:T(8,128)(2,1)} reshape(bf16[16,2,4,32,4,128]{5,4,3,2,1,0:T(4,128)(2,1)} %mul.23) | data formatting | bytes 8388608 | tf_op jit(solution)/shard_map/mul | solution.py:398
  89.0 0.1 mul.25
  89.2 0.0 collective-permute-done.1
  89.2 0.0 collective-permute-done.2
  89.2 0.0 collective-permute-done.3
  89.2 0.0 collective-permute-done
  89.2 0.1 pad_maximum_fusion
  89.3 0.6 gather_fusion
  89.9 0.1 broadcast_select_fusion
  90.0 0.1 collective-permute-start.4
  90.1 0.0 copy-start.8
  90.1 0.0 copy-start.6
  90.1 4.6 %broadcast_multiply_fusion.spread_ref = bf16[16,256,512]{2,1,0:T(8,128)(2,1)} fusion(bf16[16,256,512]{2,1,0:T(8,128)(2,1)} %mul.24, bf16[256,512]{1,0:T(8,128)(2,1)S(1)} %bitcast.52), kind=kLoop, calls=%fused_computation.2 | loop fusion | flops 2097152 | bytes 8650752 | tf_op jit(solution)/shard_map/mul | solution.py:398
  94.7 0.0 copy-done.8
  94.7 0.1 copy.27
  94.8 0.1 copy.28
  94.9 0.7 copy.39
  95.6 0.0 copy-done.6
  95.6 12.7 %all-gather = bf16[32,32,256]{2,1,0:T(8,128)(2,1)} all-gather(bf16[8,32,256]{2,1,0:T(8,128)(2,1)S(1)} %copy-done.6), channel_id=2, replica_groups=mesh['row'=4,'col'=8] {'row'}, dimensions={0}, use_global_device_ids=true | all-gather | bytes 655360 | tf_op jit(solution)/shard_map/all_gather | solution.py:441
  108.3 0.1 bitcast_select_fusion
  108.5 0.0 collective-permute-done.4
  108.5 1.1 maximum_select_fusion.1
  109.6 19.4 %pair_update.1 = (f32[32,64,128]{2,1,0:T(8,128)}, f32[32,64,128]{2,1,0:T(8,128)}, bf16[64,32,128]{2,1,0:T(8,128)(2,1)}, bf16[64,32,128]{2,1,0:T(8,128)(2,1)}) custom-call(bf16[2048,256]{1,0:T(8,128)(2,1)} %bitcast.44, bf16[1024,256]{1,0:T(8,128)(2,1)} %bitcast.49, bf16[16,256,512]{2,1,0:T(8,128)(2,1)} %broadcast_multiply_fusion.spread_ref, ...), custom_call_target="tpu_custom_call" | custom-call | tf_op jit(solution)/shard_map/pair_update/pallas_call | solution.py:281
  129.0 0.0 all-gather.6.cloned.1.call-update
  129.0 46.5 %all-gather.6.cloned.1.call-done = bf16[256,32,128]{2,1,0:T(8,128)(2,1)} async-done(((bf16[64,32,128]{2,1,0:T(8,128)(2,1)}), bf16[256,32,128]{2,1,0:T(8,128)(2,1)}) %all-gather.6.cloned.1.call-update) | async-done | bytes 2097168 | tf_op jit(solution)/shard_map/all_gather | solution.py:390
  175.5 4.5 %all-to-all-start.3 = ((bf16[4,64,32,128]{3,2,1,0:T(8,128)(2,1)}), bf16[4,64,32,128]{3,2,1,0:T(8,128)(2,1)}, u32[]{:S(2)}, u32[]{:S(2)}) async-start(bf16[4,64,32,128]{3,2,1,0:T(8,128)(2,1)} %bitcast.46), calls=%async_computation.3 | async-start | bytes 4194304 | tf_op jit(solution)/shard_map/all_to_all | solution.py:391
  180.0 0.0 all-gather.8.cloned.1.call-start
  180.1 0.5 all-gather.8.cloned.1.call-update
  180.6 30.2 %all-to-all-done.3 = bf16[4,64,32,128]{3,2,1,0:T(8,128)(2,1)} async-done(((bf16[4,64,32,128]{3,2,1,0:T(8,128)(2,1)}), bf16[4,64,32,128]{3,2,1,0:T(8,128)(2,1)}, u32[]{:S(2)}, u32[]{:S(2)}) %all-to-all-start.3) | async-done | bytes 2097184 | tf_op jit(solution)/shard_map/all_to_all | solution.py:391
  210.8 0.0 collective-permute-start.5
  210.8 0.0 copy-done.2
  210.8 28.0 %all_to_all.21 = bf16[4,8,64,256]{3,2,1,0:T(8,128)(2,1)S(1)} all-to-all(bf16[4,8,64,256]{3,2,1,0:T(8,128)(2,1)S(1)} %copy-done.2), channel_id=1, replica_groups=mesh['row'=4,'col'=8] {'row'}, dimensions={0} | all-to-all | bytes 2097152 | tf_op jit(solution)/shard_map/all_to_all | solution.py:434
  238.8 0.0 copy-done
  238.8 2.2 convolution_add_fusion
  241.0 0.0 collective-permute-done.5
  241.1 4.5 %maximum_select_fusion.left_ref = bf16[2,4,64,32,128]{4,3,2,1,0:T(8,128)(2,1)} fusion(bf16[1,4,64,32,128]{4,3,2,1,0:T(8,128)(2,1)S(1)} %bitcast.48, bf16[1,4,64,32,128]{4,3,2,1,0:T(8,128)(2,1)} %bitcast.23, pred[]{:T(512)S(6)} %eq.11), kind=kLoop, calls=%fused_computation.1 | loop fusion | flops 6291456 | bytes 8388609 | tf_op jit(solution)/shard_map/jit(_where)/select_n | solution.py:366
  245.5 10.8 %triangle.1 = f32[2048,128]{1,0:T(8,128)} custom-call(bf16[2,4,64,32,128]{4,3,2,1,0:T(8,128)(2,1)} %maximum_select_fusion.left_ref, bf16[4,64,32,128]{3,2,1,0:T(8,128)(2,1)} %bitcast.47, f32[32,64,128]{2,1,0:T(8,128)} %get-tuple-element.20.mid_ref, f32[32,64,128]{2,1,0:T(8,128)} %get-tuple-element.21.gate_ref, bf16[128,128]{1,0:T(8,128)(2,1)} %final_ref.1), custom_call_target="tpu_custom_call" | custom-call | tf_op jit(solution)/shard_map/triangle/pallas_call | solution.py:340
  (10 shorter events, 0.1 us)
Async XLA Ops:
  8.0 28.2 %copy-start.3 = (bf16[256,768]{1,0:T(8,128)(2,1)S(1)}, bf16[256,768]{1,0:T(8,128)(2,1)}, u32[]{:S(2)}) copy-start(bf16[256,768]{1,0:T(8,128)(2,1)} %param.13) | copy-start | bytes 1179652
  8.0 28.9 %slice-start = ((bf16[256,768]{1,0:T(8,128)(2,1)}), bf16[256,512]{1,0:T(8,128)(2,1)S(1)}, s32[]{:S(2)}) async-start(bf16[256,768]{1,0:T(8,128)(2,1)} %param.13), calls=%async_computation.6 | async-start | bytes 524288 | tf_op jit(solution)/shard_map/slice | solution.py:428
  8.0 29.0 %copy-start.7 = (bf16[256,256]{1,0:T(8,128)(2,1)S(1)}, bf16[256,256]{1,0:T(8,128)(2,1)}, u32[]{:S(2)}) copy-start(bf16[256,256]{1,0:T(8,128)(2,1)} %param.12) | copy-start | bytes 393220
  12.4 24.7 %copy-start.4 = (bf16[256,256]{1,0:T(8,128)(2,1)S(1)}, bf16[256,256]{1,0:T(8,128)(2,1)}, u32[]{:S(2)}) copy-start(bf16[256,256]{1,0:T(8,128)(2,1)} %param.14) | copy-start | bytes 393220
  32.6 28.5 %all-to-all-start.2 = ((bf16[4,8,80,256]{3,2,1,0:T(8,128)(2,1)}), bf16[4,8,80,256]{3,2,1,0:T(8,128)(2,1)S(1)}, u32[]{:S(2)}, u32[]{:S(2)}) async-start(bf16[4,8,80,256]{3,2,1,0:T(8,128)(2,1)} %bitcast.50), calls=%async_computation.2 | async-start | bytes 2621440 | tf_op jit(solution)/shard_map/all_to_all | solution.py:426
  36.1 41.5 %copy-start.5 = (bf16[1024,128]{1,0:T(8,128)(2,1)S(1)}, bf16[1024,128]{1,0:T(8,128)(2,1)}, u32[]{:S(2)}) copy-start(bf16[1024,128]{1,0:T(8,128)(2,1)} %param.16) | copy-start | bytes 786436
  36.1 139.4 %all-gather.6.cloned.1.call-start = ((), (), s32[]{:S(2)}) async-start(), calls=%async_computation.4 | async-start | bytes 2621440 | tf_op jit(solution)/shard_map/all_gather | solution.py:390
  61.0 1.1 copy-start.1
  69.4 19.7 %collective-permute-start.1 = (bf16[8,32,256]{2,1,0:T(8,128)(2,1)}, bf16[8,32,256]{2,1,0:T(8,128)(2,1)S(1)}, u32[]{:S(2)}, u32[]{:S(2)}) collective-permute-start(bf16[8,32,256]{2,1,0:T(8,128)(2,1)} %get-tuple-element.16), channel_id=1, source_target_pairs={{0,2},{1,3},{2,10},{3,11},{4,18},{5,19},{6,26},{7,27},{8,4},{9,5},... | collective-permute-start | bytes 393224 | tf_op jit(solution)/shard_map/ppermute | solution.py:380
  71.2 18.0 %collective-permute-start.2 = (bf16[8,32,256]{2,1,0:T(8,128)(2,1)}, bf16[8,32,256]{2,1,0:T(8,128)(2,1)S(1)}, u32[]{:S(2)}, u32[]{:S(2)}) collective-permute-start(bf16[8,32,256]{2,1,0:T(8,128)(2,1)} %get-tuple-element.16), channel_id=1, source_target_pairs={{0,4},{1,5},{2,12},{3,13},{4,20},{5,21},{6,28},{7,29},{8,6},{9,7},... | collective-permute-start | bytes 393224 | tf_op jit(solution)/shard_map/ppermute | solution.py:380
  74.0 15.2 %collective-permute-start.3 = (bf16[8,32,256]{2,1,0:T(8,128)(2,1)}, bf16[8,32,256]{2,1,0:T(8,128)(2,1)S(1)}, u32[]{:S(2)}, u32[]{:S(2)}) collective-permute-start(bf16[8,32,256]{2,1,0:T(8,128)(2,1)} %get-tuple-element.16), channel_id=1, source_target_pairs={{0,6},{1,7},{2,14},{3,15},{4,22},{5,23},{6,30},{7,31},{8,0},{9,1},... | collective-permute-start | bytes 393224 | tf_op jit(solution)/shard_map/ppermute | solution.py:380
  76.1 13.1 %collective-permute-start = (bf16[8,32,256]{2,1,0:T(8,128)(2,1)}, bf16[8,32,256]{2,1,0:T(8,128)(2,1)S(1)}, u32[]{:S(2)}, u32[]{:S(2)}) collective-permute-start(bf16[8,32,256]{2,1,0:T(8,128)(2,1)} %get-tuple-element.16), channel_id=1, source_target_pairs={{0,0},{1,1},{2,8},{3,9},{4,16},{5,17},{6,24},{7,25},{8,2},{9,3},{1... | collective-permute-start | bytes 393224 | tf_op jit(solution)/shard_map/ppermute | solution.py:380
  90.0 18.5 %collective-permute-start.4 = (bf16[4,8,32,256]{3,2,1,0:T(8,128)(2,1)S(1)}, bf16[4,8,32,256]{3,2,1,0:T(8,128)(2,1)S(1)}, u32[]{:S(2)}, u32[]{:S(2)}) collective-permute-start(bf16[4,8,32,256]{3,2,1,0:T(8,128)(2,1)S(1)} %broadcast_select_fusion), channel_id=1, source_target_pairs={{0,1},{1,0},{2,3},{3,2},{4,5},{5,4},{6,7},{7,6},{8,9},{9,8},{10,11... | collective-permute-start | bytes 1572872 | tf_op jit(solution)/shard_map/ppermute | solution.py:361
  90.1 4.6 %copy-start.8 = (bf16[128,512]{1,0:T(8,128)(2,1)S(1)}, bf16[128,512]{1,0:T(8,128)(2,1)}, u32[]{:S(2)}) copy-start(bf16[128,512]{1,0:T(8,128)(2,1)} %param.17) | copy-start | bytes 393220
  90.1 5.5 %copy-start.6 = (bf16[8,32,256]{2,1,0:T(8,128)(2,1)S(1)}, bf16[8,32,256]{2,1,0:T(8,128)(2,1)}, u32[]{:S(2)}) copy-start(bf16[8,32,256]{2,1,0:T(8,128)(2,1)} %get-tuple-element.17) | copy-start | bytes 393220
  129.0 81.9 %copy-start.2 = (bf16[4,8,64,256]{3,2,1,0:T(8,128)(2,1)S(1)}, bf16[4,8,64,256]{3,2,1,0:T(8,128)(2,1)}, u32[]{:S(2)}) copy-start(bf16[4,8,64,256]{3,2,1,0:T(8,128)(2,1)} %get-tuple-element.13) | copy-start | bytes 3145732
  129.0 109.8 %copy-start = (f32[64,32,256]{2,1,0:T(8,128)S(1)}, f32[64,32,256]{2,1,0:T(8,128)}, u32[]{:S(2)}) copy-start(f32[64,32,256]{2,1,0:T(8,128)} %second_ref.1) | copy-start | bytes 6291460
  175.5 35.3 %all-to-all-start.3 = ((bf16[4,64,32,128]{3,2,1,0:T(8,128)(2,1)}), bf16[4,64,32,128]{3,2,1,0:T(8,128)(2,1)}, u32[]{:S(2)}, u32[]{:S(2)}) async-start(bf16[4,64,32,128]{3,2,1,0:T(8,128)(2,1)} %bitcast.46), calls=%async_computation.3 | async-start | bytes 4194304 | tf_op jit(solution)/shard_map/all_to_all | solution.py:391
  180.0 65.5 %all-gather.8.cloned.1.call-start = ((), (), s32[]{:S(2)}) async-start(), calls=%async_computation.5 | async-start | bytes 2621440 | tf_op jit(solution)/shard_map/all_gather | solution.py:452
  210.8 30.2 %collective-permute-start.5 = (bf16[4,64,32,128]{3,2,1,0:T(8,128)(2,1)}, bf16[4,64,32,128]{3,2,1,0:T(8,128)(2,1)S(1)}, u32[]{:S(2)}, u32[]{:S(2)}) collective-permute-start(bf16[4,64,32,128]{3,2,1,0:T(8,128)(2,1)} %all-to-all-done.3), channel_id=1, source_target_pairs={{0,1},{1,0},{2,3},{3,2},{4,5},{5,4},{6,7},{7,6},{8,9},{9,8},{10,11... | collective-permute-start | bytes 6291464 | tf_op jit(solution)/shard_map/ppermute | solution.py:361
Sparse Core Ops, SparseCore 0:
  129.1 46.3 all-gather.5
Sparse Core Ops, SparseCore 1:
  182.3 56.7 all-gather.7

commit v2 on v1

--- a/solution.py
+++ b/solution.py
@@ -14,7 +14,6 @@
 ATTENTION_UNITS = 8
 UNIT_WIDTH = 32
 EPS = 1e-05
-HALF = C_TRI // 2
 GROUP = 4
 F32 = jnp.float32
 BF16 = jnp.bfloat16
@@ -32,6 +31,12 @@
 
 def sigmoid(values):
     return 1.0 / (1.0 + jnp.exp(-values))
+
+
+def cost(microseconds):
+    return pl.CostEstimate(
+        flops=int(microseconds * 1e9), bytes_accessed=int(microseconds * 1e6), transcendentals=0
+    )
 
 
 def params(*semantics):
@@ -86,6 +91,7 @@
             jax.ShapeDtypeStruct((residues, seqs + 16, depth), BF16),
         ],
         compiler_params=params("arbitrary"),
+        cost_estimate=cost(4),
         name="standardise",
     )(block, block)
 
@@ -141,6 +147,7 @@
             jax.ShapeDtypeStruct((residues, inner, total), BF16),
         ],
         compiler_params=params("arbitrary"),
+        cost_estimate=cost(20),
         name="attention",
     )(normed, key_matrix, other_matrices)
 
@@ -182,6 +189,7 @@
         out_specs=[side_spec, side_spec],
         out_shape=[side, side],
         compiler_params=params("arbitrary"),
+        cost_estimate=cost(6),
         name="alignment",
     )(high, low, turned, final_matrix, entry_matrices)
 
@@ -189,18 +197,17 @@
 def pair_kernel(
     left_ref,
     right_ref,
-    spread_ref,
+    weights_ref,
     couplings_ref,
     entry_ref,
     switch_ref,
     mid_ref,
     gate_ref,
-    left_pair_ref,
-    right_pair_ref,
+    sides_ref,
     outer_ref,
+    spread_ref,
     sum_ref,
-    left_rows_ref,
-    right_rows_ref,
+    rows_ref,
 ):
     features = TENSOR_FEATURES
     total = left_ref.shape[1]
@@ -211,16 +218,18 @@
     step = 512
 
     def outer_step(m, carry):
-        piece = left_ref[pl.ds(pl.multiple_of(m * step, step), step), :]
+        target = pl.ds(pl.multiple_of(m * step, step), step)
+        piece = left_ref[target, :]
         for g in range(0, groups, 2):
             wide = right_ref[g * 128 : (g + 2) * 128, :]
             outer = matmul_nt(piece, wide) * (1.0 / total)
-            target = pl.ds(pl.multiple_of(m * step, step), step)
             outer_ref[g, target, :] = outer[:, :128]
             outer_ref[g + 1, target, :] = outer[:, 128:]
         return carry
 
     lax.fori_loop(0, left_ref.shape[0] // step, outer_step, 0)
+
+    spread_ref[...] = jnp.zeros_like(spread_ref)
 
     def channel_step(p, carry):
         pieces = []
@@ -228,7 +237,14 @@
             first = outer_ref[g, pl.ds(2 * p, rows, stride=features), :]
             second = outer_ref[g, pl.ds(2 * p + 1, rows, stride=features), :]
             pieces.append(jnp.concatenate([first, second], axis=1).astype(BF16))
-        update = matmul(jnp.concatenate(pieces, axis=0), spread_ref[p])
+        slot = lax.rem(p, 2)
+        for half in range(2):
+            source = pl.multiple_of((2 * p + half) * features, features)
+            piece = weights_ref[pl.ds(source, features), :]
+            for place in range(GROUP):
+                low = half * 128 + place * features
+                spread_ref[slot, low : low + features, place * C_Z : (place + 1) * C_Z] = piece
+        update = matmul(jnp.concatenate(pieces, axis=0), spread_ref[slot])
 
         @pl.when(p == 0)
         def _():
@@ -260,99 +276,108 @@
             axis=0,
         )
         sides = matmul_nt(entry_ref[...], twice)
-        target = slice(b * HALF, (b + 1) * HALF)
-        left_rows_ref[target, :] = sigmoid(sides[HALF : 2 * HALF]) * sides[:HALF]
-        right_rows_ref[target, :] = sigmoid(sides[3 * HALF :]) * sides[2 * HALF : 3 * HALF]
+        rows_ref[b * C_TRI : (b + 1) * C_TRI, :] = sigmoid(sides[C_TRI:]) * sides[:C_TRI]
 
     def turn_step(c, carry):
-        chosen = pl.ds(c, columns, stride=HALF)
-        left_pair_ref[c] = left_rows_ref[chosen, :].astype(BF16)
-        right_pair_ref[c] = right_rows_ref[chosen, :].astype(BF16)
+        sides_ref[c] = rows_ref[pl.ds(c, columns, stride=C_TRI), :].astype(BF16)
         return carry
 
-    lax.fori_loop(0, HALF, turn_step, 0)
-
-
-def pair_update(left, right, spread, couplings, entry_matrices, switch_matrix):
+    lax.fori_loop(0, C_TRI, turn_step, 0)
+
+
+def pair_update(left, right, weights, couplings, entry_matrices, switch_matrix):
     rows, columns, depth = couplings.shape
-    side = jax.ShapeDtypeStruct((HALF, columns, 2 * rows), BF16)
     whole = jax.ShapeDtypeStruct((columns, rows, depth), F32)
     vmem = pl.BlockSpec(memory_space=pltpu.VMEM)
     return pl.pallas_call(
         pair_kernel,
         in_specs=[vmem] * 6,
-        out_specs=[vmem] * 4,
-        out_shape=[whole, whole, side, side],
+        out_specs=[vmem] * 3,
+        out_shape=[whole, whole, jax.ShapeDtypeStruct((C_TRI, columns, 2 * rows), BF16)],
         scratch_shapes=[
             pltpu.VMEM((columns // GROUP, rows * TENSOR_FEATURES, 128), F32),
+            pltpu.VMEM((2, 2 * 128, GROUP * depth), BF16),
             pltpu.VMEM((columns // GROUP * rows, GROUP * depth), F32),
-            pltpu.VMEM((columns * HALF, 2 * rows), F32),
-            pltpu.VMEM((columns * HALF, 2 * rows), F32),
+            pltpu.VMEM((columns * C_TRI, 2 * rows), F32),
         ],
         compiler_params=params(),
+        cost_estimate=cost(15),
         name="pair_update",
-    )(left, right, spread, couplings.reshape(rows * columns, depth), entry_matrices, switch_matrix)
-
-
-def triangle_kernel(left_ref, right_ref, mid_ref, gate_ref, final_ref, out_ref, product_ref):
-    halves, blocks, channels, part, lanes = left_ref.shape
-    rows = halves * part
-    columns = right_ref.shape[2]
-    step = pl.program_id(0)
-    lane = lax.broadcasted_iota(jnp.int32, (rows, blocks * lanes), 1)
-    front = lax.rem(lane, lanes) < lanes // 2
-    for c in range(channels):
-        left = jnp.concatenate(
-            [
-                jnp.concatenate([left_ref[h, k, c] for k in range(blocks)], axis=1)
-                for h in range(halves)
-            ],
-            axis=0,
-        )
-        right = jnp.concatenate([right_ref[k, c] for k in range(blocks)], axis=1)
-        blank = jnp.zeros_like(left)
-        masked = jnp.concatenate(
-            [jnp.where(front, left, blank), jnp.where(front, blank, left)], axis=0
-        )
-        first = pl.multiple_of((step * channels + c) * columns, columns)
-        product_ref[pl.ds(first, columns), :] = matmul_nt(right, masked)
-
-    @pl.when(step == pl.num_programs(0) - 1)
-    def _():
-        for j in range(columns):
-            product = product_ref[pl.ds(j, HALF, stride=columns), :]
-            mean = jnp.sum(product, axis=0, keepdims=True)
-            mean = (mean + pltpu.roll(mean, rows, 1)) * (1.0 / C_TRI)
-            centred = product - mean
-            variance = jnp.sum(centred * centred, axis=0, keepdims=True)
-            variance = (variance + pltpu.roll(variance, rows, 1)) * (1.0 / C_TRI)
-            normed = (centred * lax.rsqrt(variance + EPS)).T.astype(BF16)
-            update = matmul(normed[:rows], final_ref[:HALF, :])
-            update = update + matmul(normed[rows:], final_ref[HALF:, :])
-            out_ref[pl.ds(j, rows, stride=columns), :] = mid_ref[j] + gate_ref[j] * update
-
-
-def triangle(left, right, mid, gate, final_matrix):
-    halves, blocks, _, part, lanes = left.shape
+    )(left, right, weights, couplings.reshape(rows * columns, depth), entry_matrices, switch_matrix)
+
+
+def product_kernel(sides_ref, out_ref, *, grid_rows, grid_columns):
+    part, lanes = sides_ref.shape[2:]
+    half = lanes // 2
+    lane = lax.broadcasted_iota(jnp.int32, (grid_columns * part, lanes), 1)
+    front = lane < half
+    lefts, rights = [], []
+    for r in range(0, grid_rows, 2):
+        even, odd = [
+            jnp.concatenate(
+                [sides_ref[(r + e) * grid_columns + c, 0] for c in range(grid_columns)], axis=0
+            )
+            for e in range(2)
+        ]
+        lefts.append(jnp.where(front, even, pltpu.roll(odd, half, 1)))
+        rights.append(jnp.where(front, pltpu.roll(even, half, 1), odd))
+    product = matmul_nt(jnp.concatenate(rights, axis=1), jnp.concatenate(lefts, axis=1))
+    product = product.astype(BF16)
+    front = front[: part // 2]
+    for c in range(grid_columns):
+        for r in range(0, grid_rows, 2):
+            block = product[c * part : (c + 1) * part, r * half : (r + 2) * half]
+            top, bottom = block[: part // 2], block[part // 2 :]
+            even = jnp.where(front, top, pltpu.roll(bottom, half, 1))
+            out_ref[r * grid_columns + c, 0] = even
+            odd = jnp.where(front, pltpu.roll(top, half, 1), bottom)
+            out_ref[(r + 1) * grid_columns + c, 0] = odd
+
+
+def triangle_product(sides, grid_rows, grid_columns):
+    devices, channels, part, lanes = sides.shape
+    return pl.pallas_call(
+        functools.partial(product_kernel, grid_rows=grid_rows, grid_columns=grid_columns),
+        grid=(channels,),
+        in_specs=[pl.BlockSpec((devices, 1, part, lanes), lambda c: (0, c, 0, 0))],
+        out_specs=pl.BlockSpec((devices, 1, part // 2, lanes), lambda c: (0, c, 0, 0)),
+        out_shape=jax.ShapeDtypeStruct((devices, channels, part // 2, lanes), BF16),
+        compiler_params=params("arbitrary"),
+        cost_estimate=cost(3),
+        name="triangle_product",
+    )(sides)
+
+
+def output_kernel(product_ref, mid_ref, gate_ref, final_ref, out_ref, wide_ref):
+    channels, part, lanes = product_ref.shape
+    columns, rows, _ = mid_ref.shape
+    wide_ref[...] = product_ref[...].astype(F32).reshape(channels * part, lanes)
+    for j in range(part):
+        product = wide_ref[pl.ds(j, channels, stride=part), :]
+        centred = product - jnp.mean(product, axis=0, keepdims=True)
+        variance = jnp.mean(centred * centred, axis=0, keepdims=True)
+        normed = (centred * lax.rsqrt(variance + EPS)).T.astype(BF16)
+        update = matmul(normed, final_ref[...])
+        for half in range(2):
+            b = half * part + j
+            piece = update[half * rows : (half + 1) * rows]
+            out_ref[pl.ds(b, rows, stride=columns), :] = mid_ref[b] + gate_ref[b] * piece
+
+
+def pair_result(product, mid, gate, final_matrix):
+    channels, part, lanes = product.shape
     columns, rows, depth = mid.shape
-    channels = 8
-    whole = pl.BlockSpec((columns, rows, depth), lambda c: (0, 0, 0))
+    vmem = pl.BlockSpec(memory_space=pltpu.VMEM)
     out = pl.pallas_call(
-        triangle_kernel,
-        grid=(HALF // channels,),
-        in_specs=[
-            pl.BlockSpec((halves, blocks, channels, part, lanes), lambda c: (0, 0, c, 0, 0)),
-            pl.BlockSpec((blocks, channels, columns, lanes), lambda c: (0, c, 0, 0)),
-            whole,
-            whole,
-            pl.BlockSpec(final_matrix.shape, lambda c: (0, 0)),
-        ],
-        out_specs=pl.BlockSpec((rows * columns, depth), lambda c: (0, 0)),
+        output_kernel,
+        in_specs=[vmem] * 4,
+        out_specs=vmem,
         out_shape=jax.ShapeDtypeStruct((rows * columns, depth), F32),
-        scratch_shapes=[pltpu.VMEM((HALF * columns, 2 * rows), F32)],
-        compiler_params=params("arbitrary"),
-        name="triangle",
-    )(left, right, mid, gate, final_matrix)
+        scratch_shapes=[pltpu.VMEM((channels * part, lanes), F32)],
+        compiler_params=params(),
+        cost_estimate=cost(5),
+        name="pair_result",
+    )(product, mid, gate, final_matrix)
     return out.reshape(rows, columns, depth)
 
 
@@ -384,23 +409,18 @@
     return in_core_order(own, swap_cores(own))
 
 
-def gather_turned(block):
-    columns = lax.axis_size("col")
-    same_core = [list(range(core, columns, 2)) for core in range(2)]
-    gathered = lax.all_gather(block, "col", axis_index_groups=same_core)
-    own = lax.all_to_all(gathered, "row", split_axis=0, concat_axis=0)
-    return in_core_order(own, swap_cores(own))
-
-
-def spread_weights(matrix):
-    weights = matrix.reshape(TENSOR_FEATURES // 2, 2, 1, TENSOR_FEATURES, 1, C_Z)
-    same = jnp.eye(GROUP, dtype=matrix.dtype).reshape(1, 1, GROUP, 1, GROUP, 1)
-    return (weights * same).reshape(TENSOR_FEATURES // 2, 2 * 128, GROUP * C_Z)
+def gather_rows(block):
+    rows = lax.axis_size("row")
+    me = lax.axis_index("row")
+    arrived = [block]
+    for shift in range(1, rows):
+        arrived.append(lax.ppermute(block, "row", [(r, r ^ shift) for r in range(rows)]))
+    return jnp.take(jnp.stack(arrived), me ^ jnp.arange(rows), axis=0)
 
 
 def paired_entries(matrices):
-    turned = matrices.reshape(C_Z, 4, 2, HALF)
-    return jnp.transpose(turned, (1, 3, 2, 0)).reshape(4 * HALF, 2 * C_Z)
+    turned = matrices.reshape(C_Z, 2, 2, C_TRI)
+    return jnp.transpose(turned, (2, 3, 1, 0)).reshape(2 * C_TRI, 2 * C_Z)
 
 
 def body(
@@ -431,27 +451,35 @@
     left_piece, right_piece = alignment(
         high, low, turned, attention_final_matrix.T, tensor_entry_matrices.T
     )
+
+    right = gather_rows(right_piece)
+    left = gather_turned_direct(left_piece)
+    left, right, gated = lax.optimization_barrier((left, right, gated))
     gated = lax.all_to_all(gated, "row", split_axis=0, concat_axis=0)
+    total = left.shape[-1]
+    mid, gate, sides = pair_update(
+        left.reshape(-1, total),
+        right.reshape(-1, total),
+        tensor_final_matrix,
+        couplings,
+        paired_entries(incoming_entry_matrices),
+        incoming_switch_matrix,
+    )
+    column_count = lax.axis_size("col")
+    devices = row_count * column_count
+    sides = sides.reshape(devices, C_TRI // devices, *sides.shape[1:])
+    sides = lax.all_to_all(sides, ("row", "col"), split_axis=0, concat_axis=0)
+    product = triangle_product(sides, row_count, column_count)
+
     gated = jnp.transpose(gated.reshape(residues, seqs, inner), (1, 0, 2))
     change = jnp.dot(
         gated.reshape(-1, inner), attention_final_matrix, preferred_element_type=F32
     )
     refreshed_homologs = homolog_tensor + change.reshape(homolog_tensor.shape)
 
-    right = lax.all_gather(right_piece, "row")
-    left = gather_turned_direct(left_piece)
-    total = left.shape[-1]
-    mid, gate, left_pair, right_pair = pair_update(
-        left.reshape(-1, total),
-        right.reshape(-1, total),
-        spread_weights(tensor_final_matrix),
-        couplings,
-        paired_entries(incoming_entry_matrices),
-        incoming_switch_matrix,
-    )
-    right_pair = lax.all_gather(right_pair, "row")
-    left_pair = gather_turned(left_pair)
-    pair_output = triangle(left_pair, right_pair, mid, gate, incoming_final_matrix)
+    product = lax.all_to_all(product, ("row", "col"), split_axis=0, concat_axis=0)
+    product = product.reshape(C_TRI, *product.shape[2:])
+    pair_output = pair_result(product, mid, gate, incoming_final_matrix)
     return (refreshed_homologs, pair_output)
 
 

time: 265 us -> 177 us (0.67)
  waiting for transfers between devices: 77.3 us -> 40 us
  blocking collectives: 60.8 us -> 31.9 us
  starting transfers between devices: 16.4 us -> 32.5 us
  between operations: 15.7 us -> 0.81 us
  local copies, waits for them, and re-layouts: 15.8 us -> 4.73 us
  other arithmetic: 11.3 us -> 3.25 us
  Pallas kernels: 64.2 us -> 60.9 us
    all_gather x2 -> x0, waiting for transfers between devices: 46.5 us -> none  [the longest x1 46.5 us: gather_turned(): gathered = lax.all_gather(block, 'col', axis_index_groups=same_core)]
    all_to_all x2 -> x1, blocking collectives: 48.1 us -> 31.9 us  [body(): sides = lax.all_to_all(sides, ('row', 'col'), split_axis=0, concat_axis=0)]
    all_gather x1 -> x0, blocking collectives: 12.7 us -> none  [body(): right = lax.all_gather(right_piece, 'row')]
    mul x3 -> x0, local copies, waits for them, and re-layouts: 11.5 us -> none  [spread_weights(): return (weights * same).reshape(TENSOR_FEATURES // 2, 2 * 128, GROUP * C_Z)]
    all_to_all x1 -> x3, starting transfers between devices: 4.46 us -> 12.2 us  [the longest x1 5.31 us: body(): high = lax.all_to_all(high, 'row', split_axis=0, concat_axis=0)]
    ppermute x0 -> x3, starting transfers between devices: none -> 5.75 us  [gather_rows(): lax.ppermute(block, 'row', [(r, r ^ shift) for r in range(rows)])]
    mul x1 -> x0, other arithmetic: 4.56 us -> none  [spread_weights(): return (weights * same).reshape(TENSOR_FEATURES // 2, 2 * 128, GROUP * C_Z)]
    all_to_all x1 -> x3, waiting for transfers between devices: 30.2 us -> 34.8 us  [the longest x1 14.1 us: body(): lax.all_to_all(product, ('row', 'col'), split_axis=0, concat_axis=0)]
  transfers between devices with their start and end apart: 10 -> 12, of which waited for: 2 -> 6; matrix products, arithmetic and copies ran while one was open for 10% -> 5% of each run, Pallas kernels for 8% -> 15%
where the time goes in v2:
time: 177 us; the launch traced here: 176 us
  Pallas kernels  60.9 us (34%)
  waiting for transfers between devices  40 us (23%)
  starting transfers between devices  32.5 us (18%)
  blocking collectives  31.9 us (18%)
  local copies, waits for them, and re-layouts  4.73 us (3%)
  other arithmetic  3.25 us (2%)
  matrix products  2.2 us (1%)
    all_to_all x1, blocking collectives, body(): sides = lax.all_to_all(sides, ('row', 'col'), split_axis=0, concat_axis=0)  31.9 us
    pallas_call x1, Pallas kernels, attention(): pl.pallas_call(attention_kernel, grid=(residues,), in_specs=[pl.BlockSpec...  22.4 us
    pallas_call x1, Pallas kernels, pair_update(): pl.pallas_call(pair_kernel, in_specs=[vmem] * 6, out_specs=[vmem] * 3, ou...  18.6 us
    all_to_all x1, waiting for transfers between devices, body(): lax.all_to_all(product, ('row', 'col'), split_axis=0, concat_axis=0)  14.1 us
    all_to_all x1, waiting for transfers between devices, body(): high = lax.all_to_all(high, 'row', split_axis=0, concat_axis=0)  11.1 us
    ppermute x4, starting transfers between devices, gather_turned_direct(): arrived.append(lax.ppermute(block, ('row', 'col'), moves))  11 us
    all_to_all x1, waiting for transfers between devices, body(): gated = lax.all_to_all(gated, 'row', split_axis=0, concat_axis=0)  9.56 us
    pallas_call x1, Pallas kernels, alignment(): pl.pallas_call(alignment_kernel, grid=(residues,), in_specs=[pl.BlockSpec...  7.37 us
  transfers between devices with their start and end apart: 12, of which 6 were waited for; matrix products, arithmetic and copies ran while one was open for 5% of the time, Pallas kernels for 15%

profile of v2, /device:TPU:0, one launch (start us, length us, event | category | flops | bytes accessed | tf_op | source)
XLA Modules:
  0.0 176.3 jit_solution(7910812924212009492)
XLA Ops:
  0.6 4.3 %standardise.1 = (bf16[32,64,256]{2,1,0:T(8,128)(2,1)}, bf16[32,80,256]{2,1,0:T(8,128)(2,1)}) custom-call(f32[64,32,256]{2,1,0:T(8,128)} %second_ref.1, f32[64,32,256]{2,1,0:T(8,128)} %second_ref.1), custom_call_target="tpu_custom_call" | custom-call | flops 4000000000 | bytes 4000000 | tf_op jit(solution)/shard_map/standardise/pallas_call | solution.py:78
  5.0 0.0 copy-start.3
  5.0 0.0 slice-start
  5.0 0.0 copy-start.5
  5.0 0.0 copy-start.4
  5.0 5.3 %all-to-all-start = ((bf16[4,8,64,256]{3,2,1,0:T(8,128)(2,1)}), bf16[4,8,64,256]{3,2,1,0:T(8,128)(2,1)S(1)}, u32[]{:S(2)}, u32[]{:S(2)}) async-start(bf16[4,8,64,256]{3,2,1,0:T(8,128)(2,1)} %bitcast.39), calls=%async_computation | async-start | bytes 2097152 | tf_op jit(solution)/shard_map/all_to_all | solution.py:445
  10.3 0.0 copy-done.3
  10.3 0.7 slice.6.key_ref
  10.9 0.0 slice-done
  11.0 0.1 copy.17
  11.1 0.0 copy-done.5
  11.1 0.1 copy.12
  11.2 0.0 copy-done.4
  11.2 0.8 copy.14
  12.0 0.8 pad_maximum_fusion.2.others_ref
  12.8 11.1 %all-to-all-done.normed_ref.high_ref = bf16[4,8,64,256]{3,2,1,0:T(8,128)(2,1)S(1)} async-done(((bf16[4,8,64,256]{3,2,1,0:T(8,128)(2,1)}), bf16[4,8,64,256]{3,2,1,0:T(8,128)(2,1)S(1)}, u32[]{:S(2)}, u32[]{:S(2)}) %all-to-all-start) | async-done | bytes 1048608 | tf_op jit(solution)/shard_map/all_to_all | solution.py:445
  23.9 0.0 copy-start.2
  23.9 3.5 %all-to-all-start.1 = ((bf16[4,8,80,256]{3,2,1,0:T(8,128)(2,1)}), bf16[4,8,80,256]{3,2,1,0:T(8,128)(2,1)S(1)}, u32[]{:S(2)}, u32[]{:S(2)}) async-start(bf16[4,8,80,256]{3,2,1,0:T(8,128)(2,1)} %bitcast.1), calls=%async_computation.1 | async-start | bytes 2621440 | tf_op jit(solution)/shard_map/all_to_all | solution.py:446
  27.5 0.0 copy-done.2
  27.5 22.4 %attention.1 = (bf16[4,8,64,256]{3,2,1,0:T(8,128)(2,1)}, bf16[8,256,256]{2,1,0:T(8,128)(2,1)}) custom-call(bf16[4,8,64,256]{3,2,1,0:T(8,128)(2,1)} %copy-done.2, bf16[256,256]{1,0:T(8,128)(2,1)} %slice.6.key_ref, bf16[768,256]{1,0:T(8,128)(2,1)} %pad_maximum_fusion.2.others_ref), custom_call_target="tpu_custom_call" | custom-call | flops 20000000000 | bytes 20000000 | tf_op jit(solution)/shard_map/attention/pallas_call | solution.py:133
  49.9 0.0 all-to-all-done.1.low_ref
  49.9 0.0 copy-start.1
  49.9 1.1 copy-done.1
  50.9 0.0 copy-start.6
  50.9 7.4 %alignment.1 = (bf16[8,32,256]{2,1,0:T(8,128)(2,1)}, bf16[8,32,256]{2,1,0:T(8,128)(2,1)}) custom-call(bf16[4,8,64,256]{3,2,1,0:T(8,128)(2,1)} %copy-done.2, bf16[4,8,80,256]{3,2,1,0:T(8,128)(2,1)} %copy-done.1, bf16[8,256,256]{2,1,0:T(8,128)(2,1)} %get-tuple-element.17.turned_ref, bf16[256,256]{1,0:T(8,128)(2,1)} %bitcast.46, bf16[64,256]{1,0:T(8,128)(2,1)} %bitcast.56), custom_call_target="tpu_custom_call" | custom-call | flops 6000000000 | bytes 6000000 | tf_op jit(solution)/shard_map/alignment/pallas_call | solution.py:179
  58.3 1.7 collective-permute-start
  60.0 3.8 %collective-permute-start.1 = (bf16[8,32,256]{2,1,0:T(8,128)(2,1)}, bf16[8,32,256]{2,1,0:T(8,128)(2,1)S(1)}, u32[]{:S(2)}, u32[]{:S(2)}) collective-permute-start(bf16[8,32,256]{2,1,0:T(8,128)(2,1)} %get-tuple-element.18), channel_id=1, source_target_pairs={{0,2},{1,3},{2,10},{3,11},{4,18},{5,19},{6,26},{7,27},{8,4},{9,5},... | collective-permute-start | bytes 393224 | tf_op jit(solution)/shard_map/ppermute | solution.py:405
  63.8 3.5 %collective-permute-start.2 = (bf16[8,32,256]{2,1,0:T(8,128)(2,1)}, bf16[8,32,256]{2,1,0:T(8,128)(2,1)S(1)}, u32[]{:S(2)}, u32[]{:S(2)}) collective-permute-start(bf16[8,32,256]{2,1,0:T(8,128)(2,1)} %get-tuple-element.18), channel_id=1, source_target_pairs={{0,4},{1,5},{2,12},{3,13},{4,20},{5,21},{6,28},{7,29},{8,6},{9,7},... | collective-permute-start | bytes 393224 | tf_op jit(solution)/shard_map/ppermute | solution.py:405
  67.4 1.9 %collective-permute-start.3 = (bf16[8,32,256]{2,1,0:T(8,128)(2,1)}, bf16[8,32,256]{2,1,0:T(8,128)(2,1)S(1)}, u32[]{:S(2)}, u32[]{:S(2)}) collective-permute-start(bf16[8,32,256]{2,1,0:T(8,128)(2,1)} %get-tuple-element.18), channel_id=1, source_target_pairs={{0,6},{1,7},{2,14},{3,15},{4,22},{5,23},{6,30},{7,31},{8,0},{9,1},... | collective-permute-start | bytes 393224 | tf_op jit(solution)/shard_map/ppermute | solution.py:405
  69.3 0.0 copy-done.6
  69.3 0.1 copy.16
  69.5 0.7 copy.24
  70.1 1.5 collective-permute-start.5
  71.6 0.0 collective-permute-done
  71.6 4.3 %collective-permute-start.6 = (bf16[8,32,256]{2,1,0:T(8,128)(2,1)}, bf16[8,32,256]{2,1,0:T(8,128)(2,1)S(1)}, u32[]{:S(2)}, u32[]{:S(2)}) collective-permute-start(bf16[8,32,256]{2,1,0:T(8,128)(2,1)} %get-tuple-element.19), channel_id=1, source_target_pairs={{0,16},{8,24},{16,0},{24,8},{1,17},{9,25},{17,1},{25,9},{2,18},{10... | collective-permute-start | bytes 393224 | tf_op jit(solution)/shard_map/ppermute | solution.py:417
  75.9 0.0 collective-permute-done.1
  75.9 0.0 collective-permute-start.7
  75.9 0.0 collective-permute-done.2
  75.9 2.0 %collective-permute-done.3 = bf16[8,32,256]{2,1,0:T(8,128)(2,1)S(1)} collective-permute-done((bf16[8,32,256]{2,1,0:T(8,128)(2,1)}, bf16[8,32,256]{2,1,0:T(8,128)(2,1)S(1)}, u32[]{:S(2)}, u32[]{:S(2)}) %collective-permute-start.3) | collective-permute-done | bytes 131104 | tf_op jit(solution)/shard_map/ppermute | solution.py:405
  77.9 0.1 pad_maximum_fusion
  78.0 0.6 gather_fusion
  78.5 0.1 broadcast_select_fusion.1
  78.7 0.1 collective-permute-start.4
  78.7 0.8 collective-permute-done.5
  79.5 0.0 collective-permute-done.6
  79.6 2.4 %collective-permute-done.7 = bf16[8,32,256]{2,1,0:T(8,128)(2,1)S(1)} collective-permute-done((bf16[8,32,256]{2,1,0:T(8,128)(2,1)}, bf16[8,32,256]{2,1,0:T(8,128)(2,1)S(1)}, u32[]{:S(2)}, u32[]{:S(2)}) %collective-permute-start.7) | collective-permute-done | bytes 131104 | tf_op jit(solution)/shard_map/ppermute | solution.py:417
  82.0 0.0 copy-done.7
  82.0 0.1 pad_maximum_fusion.1
  82.0 0.6 gather_fusion.1
  82.6 0.1 fusion.4
  82.7 0.9 broadcast_select_fusion
  83.7 0.0 collective-permute-done.4
  83.7 1.1 maximum_select_fusion
  84.8 18.6 %pair_update.1 = (f32[32,64,128]{2,1,0:T(8,128)}, f32[32,64,128]{2,1,0:T(8,128)}, bf16[128,32,128]{2,1,0:T(8,128)(2,1)}) custom-call(bf16[2048,256]{1,0:T(8,128)(2,1)} %bitcast.37, bf16[1024,256]{1,0:T(8,128)(2,1)} %bitcast.43, bf16[1024,128]{1,0:T(8,128)(2,1)} %weights_ref.1, f32[2048,128]{1,0:T(8,128)} %bitcast.55, bf16[256,256]{1,0:T(8,128)(2,1)} %bitcast.45, ...), custom_call_target="tpu_custom_call" | custom-call | flops 15000000512 | bytes 15000000 | tf_op jit(solution)/shard_map/pair_update/pallas_call | solution.py:292
  103.4 31.9 %all_to_all.25.sides_ref = bf16[32,4,32,128]{3,2,1,0:T(8,128)(2,1)} all-to-all(bf16[32,4,32,128]{3,2,1,0:T(8,128)(2,1)} %bitcast.40), channel_id=1, replica_groups=mesh['row'=4,'col'=8] {'row','col'}, dimensions={0} | all-to-all | bytes 2097152 | tf_op jit(solution)/shard_map/all_to_all | solution.py:471
  135.3 3.5 %all-to-all-start.2 = ((bf16[4,8,64,256]{3,2,1,0:T(8,128)(2,1)}), bf16[4,8,64,256]{3,2,1,0:T(8,128)(2,1)S(1)}, u32[]{:S(2)}, u32[]{:S(2)}) async-start(bf16[4,8,64,256]{3,2,1,0:T(8,128)(2,1)} %get-tuple-element.21), calls=%async_computation.2 | async-start | bytes 2097152 | tf_op jit(solution)/shard_map/all_to_all | solution.py:458
  138.9 0.0 copy-start
  138.9 4.1 %triangle_product.1 = bf16[32,4,16,128]{3,2,1,0:T(8,128)(2,1)} custom-call(bf16[32,4,32,128]{3,2,1,0:T(8,128)(2,1)} %all_to_all.25.sides_ref), custom_call_target="tpu_custom_call" | custom-call | flops 3000000000 | bytes 3000000 | tf_op jit(solution)/shard_map/triangle_product/pallas_call | solution.py:339
  143.0 9.6 %all-to-all-done.2 = bf16[4,8,64,256]{3,2,1,0:T(8,128)(2,1)S(1)} async-done(((bf16[4,8,64,256]{3,2,1,0:T(8,128)(2,1)}), bf16[4,8,64,256]{3,2,1,0:T(8,128)(2,1)S(1)}, u32[]{:S(2)}, u32[]{:S(2)}) %all-to-all-start.2) | async-done | bytes 1048608 | tf_op jit(solution)/shard_map/all_to_all | solution.py:458
  152.6 3.3 %all-to-all-start.4 = ((bf16[32,4,16,128]{3,2,1,0:T(8,128)(2,1)}), bf16[32,4,16,128]{3,2,1,0:T(8,128)(2,1)}, u32[]{:S(2)}, u32[]{:S(2)}) async-start(bf16[32,4,16,128]{3,2,1,0:T(8,128)(2,1)} %triangle_product.1), calls=%async_computation.4 | async-start | bytes 1048576 | tf_op jit(solution)/shard_map/all_to_all | solution.py:480
  155.9 0.0 copy-done
  155.9 2.2 %convolution_add_fusion = f32[64,32,256]{2,1,0:T(8,128)} fusion(f32[64,32,256]{2,1,0:T(8,128)S(1)} %copy-done, bf16[32,64,256]{2,1,0:T(8,128)(2,1)S(1)} %bitcast.36, bf16[256,256]{1,0:T(8,128)(2,1)S(1)} %copy-done.4), kind=kOutput, calls=%fused_computation.2 | convolution fusion | flops 268959744 | bytes 5373952 | tf_op jit(solution)/shard_map/dot_general | solution.py:475
  158.1 14.1 %all-to-all-done.4 = bf16[32,4,16,128]{3,2,1,0:T(8,128)(2,1)} async-done(((bf16[32,4,16,128]{3,2,1,0:T(8,128)(2,1)}), bf16[32,4,16,128]{3,2,1,0:T(8,128)(2,1)}, u32[]{:S(2)}, u32[]{:S(2)}) %all-to-all-start.4) | async-done | bytes 524320 | tf_op jit(solution)/shard_map/all_to_all | solution.py:480
  172.2 4.1 %pair_result.1 = f32[2048,128]{1,0:T(8,128)} custom-call(bf16[128,16,128]{2,1,0:T(8,128)(2,1)} %bitcast.24.product_ref, f32[32,64,128]{2,1,0:T(8,128)} %get-tuple-element.25.mid_ref, f32[32,64,128]{2,1,0:T(8,128)} %get-tuple-element.26.gate_ref, bf16[128,128]{1,0:T(8,128)(2,1)} %final_ref.1), custom_call_target="tpu_custom_call" | custom-call | flops 5000000000 | bytes 5000000 | tf_op jit(solution)/shard_map/pair_result/pallas_call | solution.py:371
  (8 shorter events, 0.1 us)
Async XLA Ops:
  5.0 5.3 %copy-start.3 = (bf16[256,768]{1,0:T(8,128)(2,1)S(1)}, bf16[256,768]{1,0:T(8,128)(2,1)}, u32[]{:S(2)}) copy-start(bf16[256,768]{1,0:T(8,128)(2,1)} %param.15) | copy-start | bytes 1179652
  5.0 6.0 %slice-start = ((bf16[256,768]{1,0:T(8,128)(2,1)}), bf16[256,512]{1,0:T(8,128)(2,1)S(1)}, s32[]{:S(2)}) async-start(bf16[256,768]{1,0:T(8,128)(2,1)} %param.15), calls=%async_computation.5 | async-start | bytes 524288 | tf_op jit(solution)/shard_map/slice | solution.py:448
  5.0 6.1 %copy-start.5 = (bf16[256,256]{1,0:T(8,128)(2,1)S(1)}, bf16[256,256]{1,0:T(8,128)(2,1)}, u32[]{:S(2)}) copy-start(bf16[256,256]{1,0:T(8,128)(2,1)} %param.14) | copy-start | bytes 393220
  5.0 6.2 %copy-start.4 = (bf16[256,256]{1,0:T(8,128)(2,1)S(1)}, bf16[256,256]{1,0:T(8,128)(2,1)}, u32[]{:S(2)}) copy-start(bf16[256,256]{1,0:T(8,128)(2,1)} %param.16) | copy-start | bytes 393220
  5.0 18.9 %all-to-all-start = ((bf16[4,8,64,256]{3,2,1,0:T(8,128)(2,1)}), bf16[4,8,64,256]{3,2,1,0:T(8,128)(2,1)S(1)}, u32[]{:S(2)}, u32[]{:S(2)}) async-start(bf16[4,8,64,256]{3,2,1,0:T(8,128)(2,1)} %bitcast.39), calls=%async_computation | async-start | bytes 2097152 | tf_op jit(solution)/shard_map/all_to_all | solution.py:445
  23.9 3.6 %copy-start.2 = (bf16[4,8,64,256]{3,2,1,0:T(8,128)(2,1)}, bf16[4,8,64,256]{3,2,1,0:T(8,128)(2,1)S(1)}, u32[]{:S(2)}) copy-start(bf16[4,8,64,256]{3,2,1,0:T(8,128)(2,1)S(1)} %all-to-all-done.normed_ref.high_ref) | copy-start | bytes 3145732
  23.9 25.9 %all-to-all-start.1 = ((bf16[4,8,80,256]{3,2,1,0:T(8,128)(2,1)}), bf16[4,8,80,256]{3,2,1,0:T(8,128)(2,1)S(1)}, u32[]{:S(2)}, u32[]{:S(2)}) async-start(bf16[4,8,80,256]{3,2,1,0:T(8,128)(2,1)} %bitcast.1), calls=%async_computation.1 | async-start | bytes 2621440 | tf_op jit(solution)/shard_map/all_to_all | solution.py:446
  49.9 1.1 copy-start.1
  50.9 18.4 %copy-start.6 = (bf16[128,512]{1,0:T(8,128)(2,1)S(1)}, bf16[128,512]{1,0:T(8,128)(2,1)}, u32[]{:S(2)}) copy-start(bf16[128,512]{1,0:T(8,128)(2,1)} %param.19) | copy-start | bytes 393220
  58.3 23.7 %copy-start.7 = (bf16[8,32,256]{2,1,0:T(8,128)(2,1)S(1)}, bf16[8,32,256]{2,1,0:T(8,128)(2,1)}, u32[]{:S(2)}) copy-start(bf16[8,32,256]{2,1,0:T(8,128)(2,1)} %get-tuple-element.19) | copy-start | bytes 393220
  58.3 13.3 %collective-permute-start = (bf16[8,32,256]{2,1,0:T(8,128)(2,1)}, bf16[8,32,256]{2,1,0:T(8,128)(2,1)S(1)}, u32[]{:S(2)}, u32[]{:S(2)}) collective-permute-start(bf16[8,32,256]{2,1,0:T(8,128)(2,1)} %get-tuple-element.18), channel_id=1, source_target_pairs={{0,0},{1,1},{2,8},{3,9},{4,16},{5,17},{6,24},{7,25},{8,2},{9,3},{1... | collective-permute-start | bytes 393224 | tf_op jit(solution)/shard_map/ppermute | solution.py:405
  60.0 15.9 %collective-permute-start.1 = (bf16[8,32,256]{2,1,0:T(8,128)(2,1)}, bf16[8,32,256]{2,1,0:T(8,128)(2,1)S(1)}, u32[]{:S(2)}, u32[]{:S(2)}) collective-permute-start(bf16[8,32,256]{2,1,0:T(8,128)(2,1)} %get-tuple-element.18), channel_id=1, source_target_pairs={{0,2},{1,3},{2,10},{3,11},{4,18},{5,19},{6,26},{7,27},{8,4},{9,5},... | collective-permute-start | bytes 393224 | tf_op jit(solution)/shard_map/ppermute | solution.py:405
  63.8 12.1 %collective-permute-start.2 = (bf16[8,32,256]{2,1,0:T(8,128)(2,1)}, bf16[8,32,256]{2,1,0:T(8,128)(2,1)S(1)}, u32[]{:S(2)}, u32[]{:S(2)}) collective-permute-start(bf16[8,32,256]{2,1,0:T(8,128)(2,1)} %get-tuple-element.18), channel_id=1, source_target_pairs={{0,4},{1,5},{2,12},{3,13},{4,20},{5,21},{6,28},{7,29},{8,6},{9,7},... | collective-permute-start | bytes 393224 | tf_op jit(solution)/shard_map/ppermute | solution.py:405
  67.4 10.5 %collective-permute-start.3 = (bf16[8,32,256]{2,1,0:T(8,128)(2,1)}, bf16[8,32,256]{2,1,0:T(8,128)(2,1)S(1)}, u32[]{:S(2)}, u32[]{:S(2)}) collective-permute-start(bf16[8,32,256]{2,1,0:T(8,128)(2,1)} %get-tuple-element.18), channel_id=1, source_target_pairs={{0,6},{1,7},{2,14},{3,15},{4,22},{5,23},{6,30},{7,31},{8,0},{9,1},... | collective-permute-start | bytes 393224 | tf_op jit(solution)/shard_map/ppermute | solution.py:405
  70.1 9.4 %collective-permute-start.5 = (bf16[8,32,256]{2,1,0:T(8,128)(2,1)}, bf16[8,32,256]{2,1,0:T(8,128)(2,1)S(1)}, u32[]{:S(2)}, u32[]{:S(2)}) collective-permute-start(bf16[8,32,256]{2,1,0:T(8,128)(2,1)} %get-tuple-element.19), channel_id=1, source_target_pairs={{0,8},{8,0},{16,24},{24,16},{1,9},{9,1},{17,25},{25,17},{2,10},{10... | collective-permute-start | bytes 393224 | tf_op jit(solution)/shard_map/ppermute | solution.py:417
  71.6 7.9 %collective-permute-start.6 = (bf16[8,32,256]{2,1,0:T(8,128)(2,1)}, bf16[8,32,256]{2,1,0:T(8,128)(2,1)S(1)}, u32[]{:S(2)}, u32[]{:S(2)}) collective-permute-start(bf16[8,32,256]{2,1,0:T(8,128)(2,1)} %get-tuple-element.19), channel_id=1, source_target_pairs={{0,16},{8,24},{16,0},{24,8},{1,17},{9,25},{17,1},{25,9},{2,18},{10... | collective-permute-start | bytes 393224 | tf_op jit(solution)/shard_map/ppermute | solution.py:417
  75.9 6.1 %collective-permute-start.7 = (bf16[8,32,256]{2,1,0:T(8,128)(2,1)}, bf16[8,32,256]{2,1,0:T(8,128)(2,1)S(1)}, u32[]{:S(2)}, u32[]{:S(2)}) collective-permute-start(bf16[8,32,256]{2,1,0:T(8,128)(2,1)} %get-tuple-element.19), channel_id=1, source_target_pairs={{0,24},{8,16},{16,8},{24,0},{1,25},{9,17},{17,9},{25,1},{2,26},{10... | collective-permute-start | bytes 393224 | tf_op jit(solution)/shard_map/ppermute | solution.py:417
  78.7 5.0 %collective-permute-start.4 = (bf16[4,8,32,256]{3,2,1,0:T(8,128)(2,1)S(1)}, bf16[4,8,32,256]{3,2,1,0:T(8,128)(2,1)S(1)}, u32[]{:S(2)}, u32[]{:S(2)}) collective-permute-start(bf16[4,8,32,256]{3,2,1,0:T(8,128)(2,1)S(1)} %broadcast_select_fusion.1), channel_id=1, source_target_pairs={{0,1},{1,0},{2,3},{3,2},{4,5},{5,4},{6,7},{7,6},{8,9},{9,8},{10,11... | collective-permute-start | bytes 1572872 | tf_op jit(solution)/shard_map/ppermute | solution.py:386
  135.3 17.2 %all-to-all-start.2 = ((bf16[4,8,64,256]{3,2,1,0:T(8,128)(2,1)}), bf16[4,8,64,256]{3,2,1,0:T(8,128)(2,1)S(1)}, u32[]{:S(2)}, u32[]{:S(2)}) async-start(bf16[4,8,64,256]{3,2,1,0:T(8,128)(2,1)} %get-tuple-element.21), calls=%async_computation.2 | async-start | bytes 2097152 | tf_op jit(solution)/shard_map/all_to_all | solution.py:458
  138.9 17.1 %copy-start = (f32[64,32,256]{2,1,0:T(8,128)S(1)}, f32[64,32,256]{2,1,0:T(8,128)}, u32[]{:S(2)}) copy-start(f32[64,32,256]{2,1,0:T(8,128)} %second_ref.1) | copy-start | bytes 6291460
  152.6 19.7 %all-to-all-start.4 = ((bf16[32,4,16,128]{3,2,1,0:T(8,128)(2,1)}), bf16[32,4,16,128]{3,2,1,0:T(8,128)(2,1)}, u32[]{:S(2)}, u32[]{:S(2)}) async-start(bf16[32,4,16,128]{3,2,1,0:T(8,128)(2,1)} %triangle_product.1), calls=%async_computation.4 | async-start | bytes 1048576 | tf_op jit(solution)/shard_map/all_to_all | solution.py:480

commit v3 on v2

--- a/solution.py
+++ b/solution.py
@@ -30,7 +30,7 @@
 
 
 def sigmoid(values):
-    return 1.0 / (1.0 + jnp.exp(-values))
+    return 0.5 * jnp.tanh(0.5 * values) + 0.5
 
 
 def cost(microseconds):
@@ -96,7 +96,9 @@
     )(block, block)
 
 
-def attention_kernel(normed_ref, key_ref, others_ref, gated_ref, turned_ref):
+def attention_kernel(
+    normed_ref, key_ref, others_ref, gated_ref, turned_ref, scores_ref, weights_ref
+):
     blocks, _, seqs, depth = normed_ref.shape
     total = blocks * seqs
     inner = ATTENTION_UNITS * UNIT_WIDTH
@@ -106,21 +108,35 @@
     queries = (projected[:inner] * UNIT_WIDTH ** (-0.5)).astype(BF16)
     value_rows = projected[inner : 2 * inner].astype(BF16)
     gates = sigmoid(projected[2 * inner :])
-    ones = jnp.ones((16, total), BF16)
     parts = []
-    for h in range(ATTENTION_UNITS):
+
+    def score(h):
         low, high = h * UNIT_WIDTH, (h + 1) * UNIT_WIDTH
         pieces = [queries[low:high]]
         if low > 0:
             pieces.insert(0, jnp.zeros((low, total), BF16))
         if high < inner:
             pieces.append(jnp.zeros((inner - high, total), BF16))
-        scores = matmul(key_rows, jnp.concatenate(pieces, axis=0))
-        weights = jnp.exp(scores - jnp.max(scores, axis=0, keepdims=True)).astype(BF16)
-        attended = matmul(jnp.concatenate([value_rows[low:high], ones], axis=0), weights)
-        parts.append(
-            attended[:UNIT_WIDTH] * (gates[low:high] / attended[UNIT_WIDTH : UNIT_WIDTH + 1])
-        )
+        scores_ref[h] = matmul(key_rows, jnp.concatenate(pieces, axis=0))
+
+    def weigh(h):
+        for low in range(0, total, 128):
+            scores = scores_ref[h, :, low : low + 128]
+            weights = jnp.exp(scores - jnp.max(scores, axis=0, keepdims=True))
+            scale = 1.0 / jnp.sum(weights, axis=0, keepdims=True)
+            weights_ref[h, :, low : low + 128] = (weights * scale).astype(BF16)
+
+    def attend(h):
+        low, high = h * UNIT_WIDTH, (h + 1) * UNIT_WIDTH
+        parts.append(matmul(value_rows[low:high], weights_ref[h]) * gates[low:high])
+
+    for step in range(ATTENTION_UNITS + 2):
+        if step < ATTENTION_UNITS:
+            score(step)
+        if 1 <= step <= ATTENTION_UNITS:
+            weigh(step - 1)
+        if step >= 2:
+            attend(step - 2)
     gated = jnp.concatenate(parts, axis=0)
     turned_ref[0] = gated.astype(BF16)
     gated_ref[...] = gated.T.astype(BF16).reshape(gated_ref.shape)
@@ -146,48 +162,80 @@
             jax.ShapeDtypeStruct((blocks, residues, seqs, inner), BF16),
             jax.ShapeDtypeStruct((residues, inner, total), BF16),
         ],
+        scratch_shapes=[
+            pltpu.VMEM((ATTENTION_UNITS, total, total), F32),
+            pltpu.VMEM((ATTENTION_UNITS, total, total), BF16),
+        ],
         compiler_params=params("arbitrary"),
         cost_estimate=cost(20),
         name="attention",
     )(normed, key_matrix, other_matrices)
 
 
-def alignment_kernel(high_ref, low_ref, turned_ref, final_ref, entry_ref, left_ref, right_ref):
-    blocks, _, seqs, depth = high_ref.shape
+def alignment_kernel(
+    high_ref, low_ref, turned_ref, final_ref, entry_ref, left_ref, right_ref, rows_ref
+):
+    blocks, residues, seqs, depth = high_ref.shape
     total = blocks * seqs
-    low = low_ref[:, 0, :seqs, :].reshape(total, depth)
-    column = high_ref[...].reshape(total, depth).astype(F32) + low.astype(F32)
-    spreads = []
-    for block in range(blocks):
-        kept = low_ref[block, 0, seqs:, :seqs].astype(F32)
-        spreads.append(jnp.sum(kept, axis=0, keepdims=True))
-    spread = jnp.concatenate(spreads, axis=1)
-    updated = column.T * spread + matmul(final_ref[...], turned_ref[0])
-    centred = updated - jnp.mean(updated, axis=0, keepdims=True)
-    variance = jnp.mean(centred * centred, axis=0, keepdims=True)
-    normed = (centred * lax.rsqrt(variance + EPS)).astype(BF16)
-    projected = matmul(entry_ref[...], normed).astype(BF16)
-    left_ref[0] = projected[:TENSOR_FEATURES]
-    right_ref[0] = projected[TENSOR_FEATURES:]
+    features = TENSOR_FEATURES
+    step = pl.program_id(0)
+    for n in range(residues):
+        low = low_ref[:, n, :seqs, :].reshape(total, depth)
+        column = high_ref[:, n].reshape(total, depth).astype(F32) + low.astype(F32)
+        spreads = []
+        for block in range(blocks):
+            kept = low_ref[block, n, seqs:, :seqs].astype(F32)
+            spreads.append(jnp.sum(kept, axis=0, keepdims=True))
+        spread = jnp.concatenate(spreads, axis=1)
+        updated = column.T * spread + matmul(final_ref[...], turned_ref[n])
+        centred = updated - jnp.mean(updated, axis=0, keepdims=True)
+        variance = jnp.mean(centred * centred, axis=0, keepdims=True)
+        normed = (centred * lax.rsqrt(variance + EPS)).astype(BF16)
+        projected = matmul(entry_ref[...], normed)
+        right_ref[n] = projected[features:].astype(BF16)
+        first = pl.multiple_of((step * residues + n) * features, features)
+        for tile in range(total // 128):
+            rows_ref[tile, pl.ds(first, features), :] = projected[
+                :features, tile * 128 : (tile + 1) * 128
+            ]
+
+    @pl.when(step == pl.num_programs(0) - 1)
+    def _():
+        count = rows_ref.shape[1] // features
+        together = max(1, 16 // count)
+        for c in range(0, features, together):
+            pieces = []
+            for e in range(together):
+                chosen = pl.ds(c + e, count, stride=features)
+                tiles = [rows_ref[tile, chosen, :] for tile in range(total // 128)]
+                pieces.append(jnp.concatenate(tiles, axis=1))
+            piece = jnp.concatenate(pieces, axis=0).astype(BF16)
+            left_ref[c * count : (c + together) * count, :] = piece
 
 
 def alignment(high, low, turned, final_matrix, entry_matrices):
     blocks, residues, seqs, depth = high.shape
     total = blocks * seqs
-    side = jax.ShapeDtypeStruct((residues, TENSOR_FEATURES, total), BF16)
-    side_spec = pl.BlockSpec((1, TENSOR_FEATURES, total), lambda n: (n, 0, 0))
+    features = TENSOR_FEATURES
     return pl.pallas_call(
         alignment_kernel,
-        grid=(residues,),
+        grid=(residues // 2,),
         in_specs=[
-            pl.BlockSpec((blocks, 1, seqs, depth), lambda n: (0, n, 0, 0)),
-            pl.BlockSpec((blocks, 1, seqs + 16, depth), lambda n: (0, n, 0, 0)),
-            pl.BlockSpec((1, depth, total), lambda n: (n, 0, 0)),
+            pl.BlockSpec((blocks, 2, seqs, depth), lambda n: (0, n, 0, 0)),
+            pl.BlockSpec((blocks, 2, seqs + 16, depth), lambda n: (0, n, 0, 0)),
+            pl.BlockSpec((2, depth, total), lambda n: (n, 0, 0)),
             pl.BlockSpec(final_matrix.shape, lambda n: (0, 0)),
             pl.BlockSpec(entry_matrices.shape, lambda n: (0, 0)),
         ],
-        out_specs=[side_spec, side_spec],
-        out_shape=[side, side],
+        out_specs=[
+            pl.BlockSpec((features * residues, total), lambda n: (0, 0)),
+            pl.BlockSpec((2, features, total), lambda n: (n, 0, 0)),
+        ],
+        out_shape=[
+            jax.ShapeDtypeStruct((features * residues, total), BF16),
+            jax.ShapeDtypeStruct((residues, features, total), BF16),
+        ],
+        scratch_shapes=[pltpu.VMEM((total // 128, residues * features, 128), F32)],
         compiler_params=params("arbitrary"),
         cost_estimate=cost(6),
         name="alignment",
@@ -203,19 +251,16 @@
     switch_ref,
     mid_ref,
     gate_ref,
-    sides_ref,
-    outer_ref,
-    spread_ref,
-    sum_ref,
-    rows_ref,
+    *rest,
 ):
+    *sides_refs, outer_ref, spread_ref, sum_ref, rows_ref = rest
     features = TENSOR_FEATURES
     total = left_ref.shape[1]
     rows = left_ref.shape[0] // features
     columns = right_ref.shape[0] // features
     groups = columns // GROUP
-    pairs = features // 2
     step = 512
+    together = spread_ref.shape[1] // 128
 
     def outer_step(m, carry):
         target = pl.ds(pl.multiple_of(m * step, step), step)
@@ -223,8 +268,7 @@
         for g in range(0, groups, 2):
             wide = right_ref[g * 128 : (g + 2) * 128, :]
             outer = matmul_nt(piece, wide) * (1.0 / total)
-            outer_ref[g, target, :] = outer[:, :128]
-            outer_ref[g + 1, target, :] = outer[:, 128:]
+            outer_ref[target, g * 128 : (g + 2) * 128] = outer.astype(BF16)
         return carry
 
     lax.fori_loop(0, left_ref.shape[0] // step, outer_step, 0)
@@ -232,18 +276,20 @@
     spread_ref[...] = jnp.zeros_like(spread_ref)
 
     def channel_step(p, carry):
+        slot = lax.rem(p, 2)
+        for e in range(together):
+            source = pl.multiple_of((p * together + e) * features, features)
+            piece = weights_ref[pl.ds(source, features), :]
+            for place in range(GROUP):
+                low = e * 128 + place * features
+                spread_ref[slot, low : low + features, place * C_Z : (place + 1) * C_Z] = piece
         pieces = []
         for g in range(groups):
-            first = outer_ref[g, pl.ds(2 * p, rows, stride=features), :]
-            second = outer_ref[g, pl.ds(2 * p + 1, rows, stride=features), :]
-            pieces.append(jnp.concatenate([first, second], axis=1).astype(BF16))
-        slot = lax.rem(p, 2)
-        for half in range(2):
-            source = pl.multiple_of((2 * p + half) * features, features)
-            piece = weights_ref[pl.ds(source, features), :]
-            for place in range(GROUP):
-                low = half * 128 + place * features
-                spread_ref[slot, low : low + features, place * C_Z : (place + 1) * C_Z] = piece
+            parts = []
+            for e in range(together):
+                source = pl.multiple_of((p * together + e) * rows, rows)
+                parts.append(outer_ref[pl.ds(source, rows), g * 128 : (g + 1) * 128])
+            pieces.append(jnp.concatenate(parts, axis=1))
         update = matmul(jnp.concatenate(pieces, axis=0), spread_ref[slot])
 
         @pl.when(p == 0)
@@ -256,52 +302,62 @@
 
         return carry
 
-    lax.fori_loop(0, pairs, channel_step, 0)
-
-    for b in range(columns):
-        g, place = b // GROUP, b % GROUP
-        mid = sum_ref[g * rows : (g + 1) * rows, place * C_Z : (place + 1) * C_Z]
-        mid = mid + couplings_ref[pl.ds(b, rows, stride=columns), :]
-        mid_ref[b] = mid
-        centred = mid - jnp.mean(mid, axis=1, keepdims=True)
-        variance = jnp.mean(centred * centred, axis=1, keepdims=True)
-        normed = (centred * lax.rsqrt(variance + EPS)).astype(BF16)
-        gate_ref[b] = sigmoid(matmul(normed, switch_ref[...]))
-        blank = jnp.zeros_like(normed)
-        twice = jnp.concatenate(
-            [
-                jnp.concatenate([normed, blank], axis=1),
-                jnp.concatenate([blank, normed], axis=1),
-            ],
-            axis=0,
-        )
-        sides = matmul_nt(entry_ref[...], twice)
-        rows_ref[b * C_TRI : (b + 1) * C_TRI, :] = sigmoid(sides[C_TRI:]) * sides[:C_TRI]
-
-    def turn_step(c, carry):
-        sides_ref[c] = rows_ref[pl.ds(c, columns, stride=C_TRI), :].astype(BF16)
-        return carry
-
-    lax.fori_loop(0, C_TRI, turn_step, 0)
-
-
-def pair_update(left, right, weights, couplings, entry_matrices, switch_matrix):
+    lax.fori_loop(0, features // together, channel_step, 0)
+
+    for g in range(groups):
+        normed = []
+        for place in range(GROUP):
+            b = g * GROUP + place
+            mid = sum_ref[g * rows : (g + 1) * rows, place * C_Z : (place + 1) * C_Z]
+            mid = mid + couplings_ref[pl.ds(b, rows, stride=columns), :]
+            mid_ref[b] = mid
+            centred = mid - jnp.mean(mid, axis=1, keepdims=True)
+            variance = jnp.mean(centred * centred, axis=1, keepdims=True)
+            normed.append((centred * lax.rsqrt(variance + EPS)).astype(BF16))
+        gates = sigmoid(matmul(jnp.concatenate(normed, axis=0), switch_ref[...]))
+        blank = jnp.zeros_like(normed[0])
+        for place in range(0, GROUP, 2):
+            twice = []
+            for e in range(2):
+                b = g * GROUP + place + e
+                gate_ref[b] = gates[(place + e) * rows : (place + e + 1) * rows]
+                twice.append(jnp.concatenate([normed[place + e], blank], axis=1))
+                twice.append(jnp.concatenate([blank, normed[place + e]], axis=1))
+            sides = matmul_nt(entry_ref[...], jnp.concatenate(twice, axis=0))
+            sides = sigmoid(sides[C_TRI:]) * sides[:C_TRI]
+            b = g * GROUP + place
+            rows_ref[b * C_TRI : (b + 1) * C_TRI, :] = sides[:, : 2 * rows]
+            rows_ref[(b + 1) * C_TRI : (b + 2) * C_TRI, :] = sides[:, 2 * rows :]
+
+    share = C_TRI // len(sides_refs)
+    for part, sides_ref in enumerate(sides_refs):
+
+        def turn_step(c, carry, part=part, sides_ref=sides_ref):
+            chosen = pl.ds(part * share + c, columns, stride=C_TRI)
+            sides_ref[c] = rows_ref[chosen, :].astype(BF16)
+            return carry
+
+        lax.fori_loop(0, share, turn_step, 0, unroll=8)
+
+
+def pair_update(left, right, weights, couplings, entry_matrices, switch_matrix, parts):
     rows, columns, depth = couplings.shape
     whole = jax.ShapeDtypeStruct((columns, rows, depth), F32)
+    sides = jax.ShapeDtypeStruct((C_TRI // parts, columns, 2 * rows), BF16)
     vmem = pl.BlockSpec(memory_space=pltpu.VMEM)
     return pl.pallas_call(
         pair_kernel,
         in_specs=[vmem] * 6,
-        out_specs=[vmem] * 3,
-        out_shape=[whole, whole, jax.ShapeDtypeStruct((C_TRI, columns, 2 * rows), BF16)],
+        out_specs=[vmem] * (2 + parts),
+        out_shape=[whole, whole] + [sides] * parts,
         scratch_shapes=[
-            pltpu.VMEM((columns // GROUP, rows * TENSOR_FEATURES, 128), F32),
-            pltpu.VMEM((2, 2 * 128, GROUP * depth), BF16),
+            pltpu.VMEM((rows * TENSOR_FEATURES, columns * TENSOR_FEATURES), BF16),
+            pltpu.VMEM((2, 8 * 128, GROUP * depth), BF16),
             pltpu.VMEM((columns // GROUP * rows, GROUP * depth), F32),
             pltpu.VMEM((columns * C_TRI, 2 * rows), F32),
         ],
         compiler_params=params(),
-        cost_estimate=cost(15),
+        cost_estimate=cost(12),
         name="pair_update",
     )(left, right, weights, couplings.reshape(rows * columns, depth), entry_matrices, switch_matrix)
 
@@ -348,10 +404,15 @@
     )(sides)
 
 
-def output_kernel(product_ref, mid_ref, gate_ref, final_ref, out_ref, wide_ref):
-    channels, part, lanes = product_ref.shape
+def output_kernel(mid_ref, gate_ref, final_ref, *rest):
+    *product_refs, out_ref, wide_ref = rest
+    share, part, lanes = product_refs[0].shape
+    channels = share * len(product_refs)
     columns, rows, _ = mid_ref.shape
-    wide_ref[...] = product_ref[...].astype(F32).reshape(channels * part, lanes)
+    for e, product_ref in enumerate(product_refs):
+        wide_ref[e * share * part : (e + 1) * share * part, :] = (
+            product_ref[...].astype(F32).reshape(share * part, lanes)
+        )
     for j in range(part):
         product = wide_ref[pl.ds(j, channels, stride=part), :]
         centred = product - jnp.mean(product, axis=0, keepdims=True)
@@ -364,20 +425,20 @@
             out_ref[pl.ds(b, rows, stride=columns), :] = mid_ref[b] + gate_ref[b] * piece
 
 
-def pair_result(product, mid, gate, final_matrix):
-    channels, part, lanes = product.shape
+def pair_result(products, mid, gate, final_matrix):
+    _, part, lanes = products[0].shape
     columns, rows, depth = mid.shape
     vmem = pl.BlockSpec(memory_space=pltpu.VMEM)
     out = pl.pallas_call(
         output_kernel,
-        in_specs=[vmem] * 4,
+        in_specs=[vmem] * (3 + len(products)),
         out_specs=vmem,
         out_shape=jax.ShapeDtypeStruct((rows * columns, depth), F32),
-        scratch_shapes=[pltpu.VMEM((channels * part, lanes), F32)],
+        scratch_shapes=[pltpu.VMEM((C_TRI * part, lanes), F32)],
         compiler_params=params(),
-        cost_estimate=cost(5),
+        cost_estimate=cost(4),
         name="pair_result",
-    )(product, mid, gate, final_matrix)
+    )(mid, gate, final_matrix, *products)
     return out.reshape(rows, columns, depth)
 
 
@@ -454,32 +515,40 @@
 
     right = gather_rows(right_piece)
     left = gather_turned_direct(left_piece)
-    left, right, gated = lax.optimization_barrier((left, right, gated))
+    total = left.shape[-1]
+    left = left.reshape(2, row_count, TENSOR_FEATURES, own_residues, total)
+    left = jnp.transpose(left, (2, 0, 1, 3, 4)).reshape(-1, total)
+    left, right, gated = lax.optimization_barrier((left, right.reshape(-1, total), gated))
     gated = lax.all_to_all(gated, "row", split_axis=0, concat_axis=0)
-    total = left.shape[-1]
-    mid, gate, sides = pair_update(
-        left.reshape(-1, total),
-        right.reshape(-1, total),
+    column_count = lax.axis_size("col")
+    devices = row_count * column_count
+    channels = C_TRI // devices
+    parts = 2 if channels % 2 == 0 else 1
+    mid, gate, *sides = pair_update(
+        left,
+        right,
         tensor_final_matrix,
         couplings,
         paired_entries(incoming_entry_matrices),
         incoming_switch_matrix,
-    )
-    column_count = lax.axis_size("col")
-    devices = row_count * column_count
-    sides = sides.reshape(devices, C_TRI // devices, *sides.shape[1:])
-    sides = lax.all_to_all(sides, ("row", "col"), split_axis=0, concat_axis=0)
-    product = triangle_product(sides, row_count, column_count)
-
+        parts,
+    )
+    gated, *sides = lax.optimization_barrier((gated, *sides))
     gated = jnp.transpose(gated.reshape(residues, seqs, inner), (1, 0, 2))
     change = jnp.dot(
         gated.reshape(-1, inner), attention_final_matrix, preferred_element_type=F32
     )
     refreshed_homologs = homolog_tensor + change.reshape(homolog_tensor.shape)
 
-    product = lax.all_to_all(product, ("row", "col"), split_axis=0, concat_axis=0)
-    product = product.reshape(C_TRI, *product.shape[2:])
-    pair_output = pair_result(product, mid, gate, incoming_final_matrix)
+    everywhere = ("row", "col")
+    sides = [side.reshape(devices, channels // parts, *side.shape[1:]) for side in sides]
+    sides = [lax.all_to_all(side, everywhere, split_axis=0, concat_axis=0) for side in sides]
+    products = []
+    for side in sides:
+        product = triangle_product(side, row_count, column_count)
+        product = lax.all_to_all(product, everywhere, split_axis=0, concat_axis=0)
+        products.append(product.reshape(C_TRI // parts, *product.shape[2:]))
+    pair_output = pair_result(products, mid, gate, incoming_final_matrix)
     return (refreshed_homologs, pair_output)
 
 

time: 177 us -> 164 us (0.927)
  Pallas kernels: 60.9 us -> 45.2 us
  waiting for transfers between devices: 40 us -> 49.6 us
  blocking collectives: 31.9 us -> 22.5 us
    all_to_all x1 -> x3, waiting for transfers between devices: 14.1 us -> 30 us  [the longest x2 16 us: body(): product = lax.all_to_all(product, everywhere, split_axis=0, concat_axis=0)]
    all_to_all x1, blocking collectives: 31.9 us -> 22.5 us  [body(): lax.all_to_all(side, everywhere, split_axis=0, concat_axis=0)]
    pallas_call x3, Pallas kernels: 30.1 us -> 21.4 us  [the longest x1 11.8 us: pair_update(): pl.pallas_call(pair_kernel, in_specs=[vmem] * 6, out_specs=[vmem] * (2 +...]
    all_to_all x1, waiting for transfers between devices: 9.56 us -> 1.19 us  [body(): gated = lax.all_to_all(gated, 'row', split_axis=0, concat_axis=0)]
    pallas_call x1, Pallas kernels: 22.4 us -> 14.6 us  [attention(): pl.pallas_call(attention_kernel, grid=(residues,), in_specs=[pl.BlockSpec...]
    all_to_all x1 -> x3, starting transfers between devices: 3.33 us -> 8.5 us  [the longest x2 5.89 us: body(): product = lax.all_to_all(product, everywhere, split_axis=0, concat_axis=0)]
    ppermute x4, starting transfers between devices: 11 us -> 6.88 us  [gather_turned_direct(): arrived.append(lax.ppermute(block, ('row', 'col'), moves))]
    ppermute x3, waiting for transfers between devices: 3.22 us -> 6.01 us  [gather_rows(): lax.ppermute(block, 'row', [(r, r ^ shift) for r in range(rows)])]
  transfers between devices with their start and end apart: 12 -> 14, of which waited for: 6 -> 9; matrix products, arithmetic and copies ran while one was open for 5% -> 5% of each run, Pallas kernels for 15% -> 19%
where the time goes in v3:
time: 164 us; the launch traced here: 163 us
  waiting for transfers between devices  49.6 us (30%)
  Pallas kernels  45.2 us (28%)
  starting transfers between devices  33.3 us (20%)
  blocking collectives  22.5 us (14%)
  local copies, waits for them, and re-layouts  5.67 us (3%)
  other arithmetic  3.65 us (2%)
  matrix products  2.2 us (1%)
    all_to_all x1, blocking collectives, body(): lax.all_to_all(side, everywhere, split_axis=0, concat_axis=0)  22.5 us
    all_to_all x2, waiting for transfers between devices, body(): product = lax.all_to_all(product, everywhere, split_axis=0, concat_axis=0)  16 us
    pallas_call x1, Pallas kernels, attention(): pl.pallas_call(attention_kernel, grid=(residues,), in_specs=[pl.BlockSpec...  14.6 us
    all_to_all x1, waiting for transfers between devices, body(): lax.all_to_all(side, everywhere, split_axis=0, concat_axis=0)  14 us
    pallas_call x1, Pallas kernels, pair_update(): pl.pallas_call(pair_kernel, in_specs=[vmem] * 6, out_specs=[vmem] * (2 +...  11.8 us
    all_to_all x1, waiting for transfers between devices, body(): high = lax.all_to_all(high, 'row', split_axis=0, concat_axis=0)  11.1 us
    ppermute x4, starting transfers between devices, gather_turned_direct(): arrived.append(lax.ppermute(block, ('row', 'col'), moves))  6.88 us
    ppermute x3, waiting for transfers between devices, gather_rows(): lax.ppermute(block, 'row', [(r, r ^ shift) for r in range(rows)])  6.01 us
  transfers between devices with their start and end apart: 14, of which 9 were waited for; matrix products, arithmetic and copies ran while one was open for 5% of the time, Pallas kernels for 19%

profile of v3, /device:TPU:0, one launch (start us, length us, event | category | flops | bytes accessed | tf_op | source)
XLA Modules:
  0.0 163.1 jit_solution(13973221087231960702)
XLA Ops:
  0.6 4.3 %standardise.1 = (bf16[32,64,256]{2,1,0:T(8,128)(2,1)}, bf16[32,80,256]{2,1,0:T(8,128)(2,1)}) custom-call(f32[64,32,256]{2,1,0:T(8,128)} %second_ref.1, f32[64,32,256]{2,1,0:T(8,128)} %second_ref.1), custom_call_target="tpu_custom_call" | custom-call | flops 4000000000 | bytes 4000000 | tf_op jit(solution)/shard_map/standardise/pallas_call | solution.py:78
  5.0 0.0 slice-start
  5.0 5.3 %all-to-all-start = ((bf16[4,8,64,256]{3,2,1,0:T(8,128)(2,1)}), bf16[4,8,64,256]{3,2,1,0:T(8,128)(2,1)S(1)}, u32[]{:S(2)}, u32[]{:S(2)}) async-start(bf16[4,8,64,256]{3,2,1,0:T(8,128)(2,1)} %bitcast.52), calls=%async_computation | async-start | bytes 2097152 | tf_op jit(solution)/shard_map/all_to_all | solution.py:506
  10.3 0.0 copy-done.3
  10.3 0.7 slice.6.key_ref
  10.9 0.0 copy-done.7
  10.9 0.1 copy.12
  11.1 0.0 copy-done.5
  11.1 0.8 copy.14
  11.8 0.0 slice-done
  11.8 0.1 copy.20
  12.0 0.8 pad_maximum_fusion.2.others_ref
  12.8 11.1 %all-to-all-done.normed_ref.high_ref = bf16[4,8,64,256]{3,2,1,0:T(8,128)(2,1)S(1)} async-done(((bf16[4,8,64,256]{3,2,1,0:T(8,128)(2,1)}), bf16[4,8,64,256]{3,2,1,0:T(8,128)(2,1)S(1)}, u32[]{:S(2)}, u32[]{:S(2)}) %all-to-all-start) | async-done | bytes 1048608 | tf_op jit(solution)/shard_map/all_to_all | solution.py:506
  23.9 3.5 %all-to-all-start.1 = ((bf16[4,8,80,256]{3,2,1,0:T(8,128)(2,1)}), bf16[4,8,80,256]{3,2,1,0:T(8,128)(2,1)S(1)}, u32[]{:S(2)}, u32[]{:S(2)}) async-start(bf16[4,8,80,256]{3,2,1,0:T(8,128)(2,1)} %bitcast.1), calls=%async_computation.1 | async-start | bytes 2621440 | tf_op jit(solution)/shard_map/all_to_all | solution.py:507
  27.5 14.6 %attention.1 = (bf16[4,8,64,256]{3,2,1,0:T(8,128)(2,1)}, bf16[8,256,256]{2,1,0:T(8,128)(2,1)}) custom-call(bf16[4,8,64,256]{3,2,1,0:T(8,128)(2,1)} %copy-done.2, bf16[256,256]{1,0:T(8,128)(2,1)} %slice.6.key_ref, bf16[768,256]{1,0:T(8,128)(2,1)} %pad_maximum_fusion.2.others_ref), custom_call_target="tpu_custom_call" | custom-call | flops 20000000000 | bytes 20000000 | tf_op jit(solution)/shard_map/attention/pallas_call | solution.py:149
  42.0 1.3 all-to-all-done.1.low_ref
  43.3 1.1 copy-done.1
  44.4 5.6 %alignment.1 = (bf16[256,256]{1,0:T(8,128)(2,1)}, bf16[8,32,256]{2,1,0:T(8,128)(2,1)}) custom-call(bf16[4,8,64,256]{3,2,1,0:T(8,128)(2,1)} %copy-done.2, bf16[4,8,80,256]{3,2,1,0:T(8,128)(2,1)} %copy-done.1, bf16[8,256,256]{2,1,0:T(8,128)(2,1)} %get-tuple-element.20.turned_ref, bf16[256,256]{1,0:T(8,128)(2,1)} %bitcast.59, bf16[64,256]{1,0:T(8,128)(2,1)} %bitcast.69), custom_call_target="tpu_custom_call" | custom-call | flops 6000000000 | bytes 6000000 | tf_op jit(solution)/shard_map/alignment/pallas_call | solution.py:220
  50.0 3.7 %collective-permute-start.3 = (bf16[256,256]{1,0:T(8,128)(2,1)}, bf16[256,256]{1,0:T(8,128)(2,1)S(1)}, u32[]{:S(2)}, u32[]{:S(2)}) collective-permute-start(bf16[256,256]{1,0:T(8,128)(2,1)} %get-tuple-element.21), channel_id=1, source_target_pairs={{0,6},{1,7},{2,14},{3,15},{4,22},{5,23},{6,30},{7,31},{8,0},{9,1},... | collective-permute-start | bytes 393224 | tf_op jit(solution)/shard_map/ppermute | solution.py:466
  53.7 1.5 collective-permute-start.2
  55.2 0.2 collective-permute-start.1
  55.3 1.6 collective-permute-start
  56.9 0.1 broadcast_in_dim.32
  57.0 0.1 broadcast_in_dim.33
  57.1 0.0 copy-done.8
  57.1 0.1 copy.18
  57.2 0.7 copy.30
  57.9 4.8 %collective-permute-start.7 = (bf16[8,32,256]{2,1,0:T(8,128)(2,1)}, bf16[8,32,256]{2,1,0:T(8,128)(2,1)S(1)}, u32[]{:S(2)}, u32[]{:S(2)}) collective-permute-start(bf16[8,32,256]{2,1,0:T(8,128)(2,1)} %get-tuple-element.22), channel_id=1, source_target_pairs={{0,24},{8,16},{16,8},{24,0},{1,25},{9,17},{17,9},{25,1},{2,26},{10... | collective-permute-start | bytes 393224 | tf_op jit(solution)/shard_map/ppermute | solution.py:478
  62.7 0.0 collective-permute-done.3
  62.7 0.0 collective-permute-start.6
  62.7 0.0 collective-permute-done.2
  62.7 0.6 collective-permute-start.5
  63.3 0.0 collective-permute-done.1
  63.3 0.0 collective-permute-done
  63.3 0.1 pad_maximum_fusion
  63.4 0.6 gather_fusion
  64.0 0.1 broadcast_select_fusion
  64.1 0.1 collective-permute-start.4
  64.2 4.6 %collective-permute-done.7 = bf16[8,32,256]{2,1,0:T(8,128)(2,1)S(1)} collective-permute-done((bf16[8,32,256]{2,1,0:T(8,128)(2,1)}, bf16[8,32,256]{2,1,0:T(8,128)(2,1)S(1)}, u32[]{:S(2)}, u32[]{:S(2)}) %collective-permute-start.7) | collective-permute-done | bytes 131104 | tf_op jit(solution)/shard_map/ppermute | solution.py:478
  68.8 0.1 collective-permute-done.6
  68.8 1.3 collective-permute-done.5
  70.2 0.1 pad_maximum_fusion.1
  70.3 0.6 gather_fusion.1
  70.8 0.2 copy_select_fusion
  71.0 1.0 bitcast_select_fusion.right_ref
  72.0 0.0 collective-permute-done.4
  72.0 1.4 maximum_select_fusion
  73.4 3.6 %all-to-all-start.2 = ((bf16[4,8,64,256]{3,2,1,0:T(8,128)(2,1)}), bf16[4,8,64,256]{3,2,1,0:T(8,128)(2,1)S(1)}, u32[]{:S(2)}, u32[]{:S(2)}) async-start(bf16[4,8,64,256]{3,2,1,0:T(8,128)(2,1)} %get-tuple-element.24), calls=%async_computation.2 | async-start | bytes 2097152 | tf_op jit(solution)/shard_map/all_to_all | solution.py:522
  77.1 11.8 %pair_update.1 = (f32[32,64,128]{2,1,0:T(8,128)}, f32[32,64,128]{2,1,0:T(8,128)}, bf16[64,32,128]{2,1,0:T(8,128)(2,1)}, bf16[64,32,128]{2,1,0:T(8,128)(2,1)}) custom-call(bf16[2048,256]{1,0:T(8,128)(2,1)} %bitcast.50, bf16[1024,256]{1,0:T(8,128)(2,1)} %bitcast_select_fusion.right_ref, bf16[1024,128]{1,0:T(8,128)(2,1)} %weights_ref.1, f32[2048,128]{1,0:T(8,128)} %bitcast.68, ...), custom_call_target="tpu_custom_call" | custom-call | flops 12000000000 | bytes 12000000 | tf_op jit(solution)/shard_map/pair_update/pallas_call | solution.py:348
  88.8 1.2 all-to-all-done.2
  90.0 22.5 %all_to_all.35.sides_ref = bf16[32,2,32,128]{3,2,1,0:T(8,128)(2,1)} all-to-all(bf16[32,2,32,128]{3,2,1,0:T(8,128)(2,1)} %bitcast.54), channel_id=1, replica_groups=mesh['row'=4,'col'=8] {'row','col'}, dimensions={0} | all-to-all | bytes 1048576 | tf_op jit(solution)/shard_map/all_to_all | solution.py:545
  112.6 2.6 %all-to-all-start.5 = ((bf16[32,2,32,128]{3,2,1,0:T(8,128)(2,1)}), bf16[32,2,32,128]{3,2,1,0:T(8,128)(2,1)S(1)}, u32[]{:S(2)}, u32[]{:S(2)}) async-start(bf16[32,2,32,128]{3,2,1,0:T(8,128)(2,1)} %bitcast.53), calls=%async_computation.5 | async-start | bytes 1048576 | tf_op jit(solution)/shard_map/all_to_all | solution.py:545
  115.2 2.4 %triangle_product.2 = bf16[32,2,16,128]{3,2,1,0:T(8,128)(2,1)} custom-call(bf16[32,2,32,128]{3,2,1,0:T(8,128)(2,1)} %all_to_all.35.sides_ref), custom_call_target="tpu_custom_call" | custom-call | flops 3000000000 | bytes 3000000 | tf_op jit(solution)/shard_map/triangle_product/pallas_call | solution.py:395
  117.6 14.0 %all-to-all-done.5.sides_ref = bf16[32,2,32,128]{3,2,1,0:T(8,128)(2,1)S(1)} async-done(((bf16[32,2,32,128]{3,2,1,0:T(8,128)(2,1)}), bf16[32,2,32,128]{3,2,1,0:T(8,128)(2,1)S(1)}, u32[]{:S(2)}, u32[]{:S(2)}) %all-to-all-start.5) | async-done | bytes 524320 | tf_op jit(solution)/shard_map/all_to_all | solution.py:545
  131.5 0.8 copy-done.4
  132.3 2.6 %all-to-all-start.4 = ((bf16[32,2,16,128]{3,2,1,0:T(8,128)(2,1)}), bf16[32,2,16,128]{3,2,1,0:T(8,128)(2,1)S(1)}, u32[]{:S(2)}, u32[]{:S(2)}) async-start(bf16[32,2,16,128]{3,2,1,0:T(8,128)(2,1)} %triangle_product.2), calls=%async_computation.4 | async-start | bytes 524288 | tf_op jit(solution)/shard_map/all_to_all | solution.py:549
  134.9 0.0 copy-start
  134.9 2.5 %triangle_product.3 = bf16[32,2,16,128]{3,2,1,0:T(8,128)(2,1)} custom-call(bf16[32,2,32,128]{3,2,1,0:T(8,128)(2,1)} %copy-done.4), custom_call_target="tpu_custom_call" | custom-call | flops 3000000000 | bytes 3000000 | tf_op jit(solution)/shard_map/triangle_product/pallas_call | solution.py:395
  137.5 7.9 %all-to-all-done.4 = bf16[32,2,16,128]{3,2,1,0:T(8,128)(2,1)S(1)} async-done(((bf16[32,2,16,128]{3,2,1,0:T(8,128)(2,1)}), bf16[32,2,16,128]{3,2,1,0:T(8,128)(2,1)S(1)}, u32[]{:S(2)}, u32[]{:S(2)}) %all-to-all-start.4) | async-done | bytes 262176 | tf_op jit(solution)/shard_map/all_to_all | solution.py:549
  145.3 3.3 %all-to-all-start.6 = ((bf16[32,2,16,128]{3,2,1,0:T(8,128)(2,1)}), bf16[32,2,16,128]{3,2,1,0:T(8,128)(2,1)}, u32[]{:S(2)}, u32[]{:S(2)}) async-start(bf16[32,2,16,128]{3,2,1,0:T(8,128)(2,1)} %triangle_product.3), calls=%async_computation.6 | async-start | bytes 524288 | tf_op jit(solution)/shard_map/all_to_all | solution.py:549
  148.6 0.0 copy-done
  148.6 2.2 %convolution_add_fusion = f32[64,32,256]{2,1,0:T(8,128)} fusion(f32[64,32,256]{2,1,0:T(8,128)S(1)} %copy-done, bf16[32,64,256]{2,1,0:T(8,128)(2,1)S(1)} %bitcast.49, bf16[256,256]{1,0:T(8,128)(2,1)S(1)} %copy-done.5), kind=kOutput, calls=%fused_computation.2 | convolution fusion | flops 268959744 | bytes 5373952 | tf_op jit(solution)/shard_map/dot_general | solution.py:538
  150.8 8.1 %all-to-all-done.6 = bf16[32,2,16,128]{3,2,1,0:T(8,128)(2,1)} async-done(((bf16[32,2,16,128]{3,2,1,0:T(8,128)(2,1)}), bf16[32,2,16,128]{3,2,1,0:T(8,128)(2,1)}, u32[]{:S(2)}, u32[]{:S(2)}) %all-to-all-start.6) | async-done | bytes 262176 | tf_op jit(solution)/shard_map/all_to_all | solution.py:549
  159.0 4.1 %pair_result.1 = f32[2048,128]{1,0:T(8,128)} custom-call(f32[32,64,128]{2,1,0:T(8,128)} %get-tuple-element.30.mid_ref, f32[32,64,128]{2,1,0:T(8,128)} %get-tuple-element.31.gate_ref, bf16[128,128]{1,0:T(8,128)(2,1)} %final_ref.1, bf16[64,16,128]{2,1,0:T(8,128)(2,1)} %bitcast.57, bf16[64,16,128]{2,1,0:T(8,128)(2,1)} %bitcast.29.rest_1_), custom_call_target="tpu_custom_call" | custom-call | flops 4000000000 | bytes 4000000 | tf_op jit(solution)/shard_map/pair_result/pallas_call | solution.py:432
  (19 shorter events, 0.1 us)
Async XLA Ops:
  5.0 5.3 %copy-start.3 = (bf16[256,768]{1,0:T(8,128)(2,1)S(1)}, bf16[256,768]{1,0:T(8,128)(2,1)}, u32[]{:S(2)}) copy-start(bf16[256,768]{1,0:T(8,128)(2,1)} %param.13) | copy-start | bytes 1179652
  5.0 6.0 %copy-start.7 = (bf16[256,256]{1,0:T(8,128)(2,1)S(1)}, bf16[256,256]{1,0:T(8,128)(2,1)}, u32[]{:S(2)}) copy-start(bf16[256,256]{1,0:T(8,128)(2,1)} %param.12) | copy-start | bytes 393220
  5.0 6.1 %copy-start.5 = (bf16[256,256]{1,0:T(8,128)(2,1)S(1)}, bf16[256,256]{1,0:T(8,128)(2,1)}, u32[]{:S(2)}) copy-start(bf16[256,256]{1,0:T(8,128)(2,1)} %param.14) | copy-start | bytes 393220
  5.0 6.9 %slice-start = ((bf16[256,768]{1,0:T(8,128)(2,1)}), bf16[256,512]{1,0:T(8,128)(2,1)S(1)}, s32[]{:S(2)}) async-start(bf16[256,768]{1,0:T(8,128)(2,1)} %param.13), calls=%async_computation.7 | async-start | bytes 524288 | tf_op jit(solution)/shard_map/slice | solution.py:509
  5.0 18.9 %all-to-all-start = ((bf16[4,8,64,256]{3,2,1,0:T(8,128)(2,1)}), bf16[4,8,64,256]{3,2,1,0:T(8,128)(2,1)S(1)}, u32[]{:S(2)}, u32[]{:S(2)}) async-start(bf16[4,8,64,256]{3,2,1,0:T(8,128)(2,1)} %bitcast.52), calls=%async_computation | async-start | bytes 2097152 | tf_op jit(solution)/shard_map/all_to_all | solution.py:506
  23.9 3.6 %copy-start.2 = (bf16[4,8,64,256]{3,2,1,0:T(8,128)(2,1)}, bf16[4,8,64,256]{3,2,1,0:T(8,128)(2,1)S(1)}, u32[]{:S(2)}) copy-start(bf16[4,8,64,256]{3,2,1,0:T(8,128)(2,1)S(1)} %all-to-all-done.normed_ref.high_ref) | copy-start | bytes 3145732
  23.9 19.4 %all-to-all-start.1 = ((bf16[4,8,80,256]{3,2,1,0:T(8,128)(2,1)}), bf16[4,8,80,256]{3,2,1,0:T(8,128)(2,1)S(1)}, u32[]{:S(2)}, u32[]{:S(2)}) async-start(bf16[4,8,80,256]{3,2,1,0:T(8,128)(2,1)} %bitcast.1), calls=%async_computation.1 | async-start | bytes 2621440 | tf_op jit(solution)/shard_map/all_to_all | solution.py:507
  43.3 1.1 copy-start.1
  44.4 12.7 %copy-start.8 = (bf16[128,512]{1,0:T(8,128)(2,1)S(1)}, bf16[128,512]{1,0:T(8,128)(2,1)}, u32[]{:S(2)}) copy-start(bf16[128,512]{1,0:T(8,128)(2,1)} %param.17) | copy-start | bytes 393220
  50.0 20.2 %copy-start.9 = (bf16[8,32,256]{2,1,0:T(8,128)(2,1)S(1)}, bf16[8,32,256]{2,1,0:T(8,128)(2,1)}, u32[]{:S(2)}) copy-start(bf16[8,32,256]{2,1,0:T(8,128)(2,1)} %get-tuple-element.22) | copy-start | bytes 393220
  50.0 12.7 %collective-permute-start.3 = (bf16[256,256]{1,0:T(8,128)(2,1)}, bf16[256,256]{1,0:T(8,128)(2,1)S(1)}, u32[]{:S(2)}, u32[]{:S(2)}) collective-permute-start(bf16[256,256]{1,0:T(8,128)(2,1)} %get-tuple-element.21), channel_id=1, source_target_pairs={{0,6},{1,7},{2,14},{3,15},{4,22},{5,23},{6,30},{7,31},{8,0},{9,1},... | collective-permute-start | bytes 393224 | tf_op jit(solution)/shard_map/ppermute | solution.py:466
  53.7 9.0 %collective-permute-start.2 = (bf16[256,256]{1,0:T(8,128)(2,1)}, bf16[256,256]{1,0:T(8,128)(2,1)S(1)}, u32[]{:S(2)}, u32[]{:S(2)}) collective-permute-start(bf16[256,256]{1,0:T(8,128)(2,1)} %get-tuple-element.21), channel_id=1, source_target_pairs={{0,4},{1,5},{2,12},{3,13},{4,20},{5,21},{6,28},{7,29},{8,6},{9,7},... | collective-permute-start | bytes 393224 | tf_op jit(solution)/shard_map/ppermute | solution.py:466
  55.2 8.1 %collective-permute-start.1 = (bf16[256,256]{1,0:T(8,128)(2,1)}, bf16[256,256]{1,0:T(8,128)(2,1)S(1)}, u32[]{:S(2)}, u32[]{:S(2)}) collective-permute-start(bf16[256,256]{1,0:T(8,128)(2,1)} %get-tuple-element.21), channel_id=1, source_target_pairs={{0,2},{1,3},{2,10},{3,11},{4,18},{5,19},{6,26},{7,27},{8,4},{9,5},... | collective-permute-start | bytes 393224 | tf_op jit(solution)/shard_map/ppermute | solution.py:466
  55.3 8.0 %collective-permute-start = (bf16[256,256]{1,0:T(8,128)(2,1)}, bf16[256,256]{1,0:T(8,128)(2,1)S(1)}, u32[]{:S(2)}, u32[]{:S(2)}) collective-permute-start(bf16[256,256]{1,0:T(8,128)(2,1)} %get-tuple-element.21), channel_id=1, source_target_pairs={{0,0},{1,1},{2,8},{3,9},{4,16},{5,17},{6,24},{7,25},{8,2},{9,3},{1... | collective-permute-start | bytes 393224 | tf_op jit(solution)/shard_map/ppermute | solution.py:466
  57.9 10.9 %collective-permute-start.7 = (bf16[8,32,256]{2,1,0:T(8,128)(2,1)}, bf16[8,32,256]{2,1,0:T(8,128)(2,1)S(1)}, u32[]{:S(2)}, u32[]{:S(2)}) collective-permute-start(bf16[8,32,256]{2,1,0:T(8,128)(2,1)} %get-tuple-element.22), channel_id=1, source_target_pairs={{0,24},{8,16},{16,8},{24,0},{1,25},{9,17},{17,9},{25,1},{2,26},{10... | collective-permute-start | bytes 393224 | tf_op jit(solution)/shard_map/ppermute | solution.py:478
  62.7 6.2 %collective-permute-start.6 = (bf16[8,32,256]{2,1,0:T(8,128)(2,1)}, bf16[8,32,256]{2,1,0:T(8,128)(2,1)S(1)}, u32[]{:S(2)}, u32[]{:S(2)}) collective-permute-start(bf16[8,32,256]{2,1,0:T(8,128)(2,1)} %get-tuple-element.22), channel_id=1, source_target_pairs={{0,16},{8,24},{16,0},{24,8},{1,17},{9,25},{17,1},{25,9},{2,18},{10... | collective-permute-start | bytes 393224 | tf_op jit(solution)/shard_map/ppermute | solution.py:478
  62.7 7.5 %collective-permute-start.5 = (bf16[8,32,256]{2,1,0:T(8,128)(2,1)}, bf16[8,32,256]{2,1,0:T(8,128)(2,1)S(1)}, u32[]{:S(2)}, u32[]{:S(2)}) collective-permute-start(bf16[8,32,256]{2,1,0:T(8,128)(2,1)} %get-tuple-element.22), channel_id=1, source_target_pairs={{0,8},{8,0},{16,24},{24,16},{1,9},{9,1},{17,25},{25,17},{2,10},{10... | collective-permute-start | bytes 393224 | tf_op jit(solution)/shard_map/ppermute | solution.py:478
  64.1 8.0 %collective-permute-start.4 = (bf16[4,256,256]{2,1,0:T(8,128)(2,1)S(1)}, bf16[4,256,256]{2,1,0:T(8,128)(2,1)S(1)}, u32[]{:S(2)}, u32[]{:S(2)}) collective-permute-start(bf16[4,256,256]{2,1,0:T(8,128)(2,1)S(1)} %broadcast_select_fusion), channel_id=1, source_target_pairs={{0,1},{1,0},{2,3},{3,2},{4,5},{5,4},{6,7},{7,6},{8,9},{9,8},{10,11... | collective-permute-start | bytes 1572872 | tf_op jit(solution)/shard_map/ppermute | solution.py:447
  73.4 16.6 %all-to-all-start.2 = ((bf16[4,8,64,256]{3,2,1,0:T(8,128)(2,1)}), bf16[4,8,64,256]{3,2,1,0:T(8,128)(2,1)S(1)}, u32[]{:S(2)}, u32[]{:S(2)}) async-start(bf16[4,8,64,256]{3,2,1,0:T(8,128)(2,1)} %get-tuple-element.24), calls=%async_computation.2 | async-start | bytes 2097152 | tf_op jit(solution)/shard_map/all_to_all | solution.py:522
  112.6 19.0 %all-to-all-start.5 = ((bf16[32,2,32,128]{3,2,1,0:T(8,128)(2,1)}), bf16[32,2,32,128]{3,2,1,0:T(8,128)(2,1)S(1)}, u32[]{:S(2)}, u32[]{:S(2)}) async-start(bf16[32,2,32,128]{3,2,1,0:T(8,128)(2,1)} %bitcast.53), calls=%async_computation.5 | async-start | bytes 1048576 | tf_op jit(solution)/shard_map/all_to_all | solution.py:545
  131.5 0.8 copy-start.4
  132.3 13.0 %all-to-all-start.4 = ((bf16[32,2,16,128]{3,2,1,0:T(8,128)(2,1)}), bf16[32,2,16,128]{3,2,1,0:T(8,128)(2,1)S(1)}, u32[]{:S(2)}, u32[]{:S(2)}) async-start(bf16[32,2,16,128]{3,2,1,0:T(8,128)(2,1)} %triangle_product.2), calls=%async_computation.4 | async-start | bytes 524288 | tf_op jit(solution)/shard_map/all_to_all | solution.py:549
  134.9 13.7 %copy-start = (f32[64,32,256]{2,1,0:T(8,128)S(1)}, f32[64,32,256]{2,1,0:T(8,128)}, u32[]{:S(2)}) copy-start(f32[64,32,256]{2,1,0:T(8,128)} %second_ref.1) | copy-start | bytes 6291460
  145.3 5.5 %copy-start.6 = (bf16[32,2,16,128]{3,2,1,0:T(8,128)(2,1)}, bf16[32,2,16,128]{3,2,1,0:T(8,128)(2,1)S(1)}, u32[]{:S(2)}) copy-start(bf16[32,2,16,128]{3,2,1,0:T(8,128)(2,1)S(1)} %all-to-all-done.4) | copy-start | bytes 786436
  145.3 13.7 %all-to-all-start.6 = ((bf16[32,2,16,128]{3,2,1,0:T(8,128)(2,1)}), bf16[32,2,16,128]{3,2,1,0:T(8,128)(2,1)}, u32[]{:S(2)}, u32[]{:S(2)}) async-start(bf16[32,2,16,128]{3,2,1,0:T(8,128)(2,1)} %triangle_product.3), calls=%async_computation.6 | async-start | bytes 524288 | tf_op jit(solution)/shard_map/all_to_all | solution.py:549

commit v4 on v3

v4 whole, which is shorter than its diff:
```python
import functools

import jax
import jax.numpy as jnp
from jax import lax
from jax.experimental import pallas as pl
from jax.experimental.pallas import tpu as pltpu
from jax.sharding import PartitionSpec as P

FEATURE_DEPTH = 256
C_Z = 128
TENSOR_FEATURES = 32
C_TRI = 128
ATTENTION_UNITS = 8
UNIT_WIDTH = 32
EPS = 1e-05
GROUP = 4
F32 = jnp.float32
BF16 = jnp.bfloat16
NT = (((1,), (1,)), ((), ()))
MEGA = 1024 * 1024


def matmul(left, right):
    return jnp.dot(left, right, preferred_element_type=F32)


def matmul_nt(left, right):
    return lax.dot_general(left, right, NT, preferred_element_type=F32)


def sigmoid(values):
    return 0.5 * jnp.tanh(0.5 * values) + 0.5


def cost(microseconds):
    return pl.CostEstimate(
        flops=int(microseconds * 1e9), bytes_accessed=int(microseconds * 1e6), transcendentals=0
    )


def params(megabytes, *semantics):
    return pltpu.CompilerParams(
        dimension_semantics=semantics or None, vmem_limit_bytes=megabytes * MEGA
    )


def standardised_column(first_rows, second_rows, n, residues):
    seqs = first_rows.shape[0] // residues
    rows = pl.ds(n, seqs, stride=residues)
    column = jnp.concatenate([first_rows[rows, :], second_rows[rows, :]], axis=1)
    centred = column - jnp.mean(column, axis=1, keepdims=True)
    variance = jnp.mean(centred * centred, axis=1, keepdims=True) + EPS
    scale = lax.rsqrt(variance)
    return centred * scale, variance * scale


def high_kernel(first_ref, second_ref, high_ref):
    seqs, residues, lanes = first_ref.shape
    first_rows = first_ref.reshape(seqs * residues, lanes)
    second_rows = second_ref.reshape(seqs * residues, lanes)
    for n in range(residues):
        normed, _ = standardised_column(first_rows, second_rows, n, residues)
        high_ref[n] = normed.astype(BF16)


def low_kernel(first_ref, second_ref, low_ref):
    seqs, residues, lanes = first_ref.shape
    first_rows = first_ref.reshape(seqs * residues, lanes)
    second_rows = second_ref.reshape(seqs * residues, lanes)
    lane = lax.broadcasted_iota(jnp.int32, (seqs, 128), 1)
    spreads = jnp.zeros((seqs, 128), F32)
    for n in range(residues):
        normed, spread = standardised_column(first_rows, second_rows, n, residues)
        low_ref[n, :seqs, :] = (normed - normed.astype(BF16).astype(F32)).astype(BF16)
        spreads = jnp.where(lane == n, spread, spreads)
    spreads = spreads.T
    row = lax.broadcasted_iota(jnp.int32, (16, seqs), 0)
    for n in range(residues):
        spread = jnp.broadcast_to(spreads[n : n + 1, :], (16, seqs))
        coarse = spread.astype(BF16).astype(F32)
        kept = jnp.where(row == 0, coarse, jnp.where(row == 1, spread - coarse, 0.0))
        kept = jnp.concatenate([kept, jnp.zeros((16, 2 * lanes - seqs), F32)], axis=1)
        low_ref[n, seqs:, :] = kept.astype(BF16)


def standardise(block, kernel, extra):
    seqs, residues, depth = block.shape
    half = depth // 2
    return pl.pallas_call(
        kernel,
        grid=(residues // 8,),
        in_specs=[
            pl.BlockSpec((seqs, 8, half), lambda g: (0, g, 0)),
            pl.BlockSpec((seqs, 8, half), lambda g: (0, g, 1)),
        ],
        out_specs=pl.BlockSpec((8, seqs + extra, depth), lambda g: (g, 0, 0)),
        out_shape=jax.ShapeDtypeStruct((residues, seqs + extra, depth), BF16),
        compiler_params=params(12, "arbitrary"),
        cost_estimate=cost(3),
        name="standardise",
    )(block, block)


def attention_kernel(
    normed_ref, key_ref, others_ref, gated_ref, turned_ref, scores_ref, weights_ref
):
    blocks, residues, seqs, depth = normed_ref.shape
    total = blocks * seqs
    inner = ATTENTION_UNITS * UNIT_WIDTH
    columns = []
    for n in range(residues):
        column = normed_ref[:, n].reshape(total, depth)
        key_rows = matmul(column, key_ref[...]).astype(BF16)
        projected = matmul_nt(others_ref[...], column)
        queries = (projected[:inner] * UNIT_WIDTH ** (-0.5)).astype(BF16)
        value_rows = projected[inner : 2 * inner].astype(BF16)
        gates = sigmoid(projected[2 * inner :])
        columns.append((key_rows, queries, value_rows, gates))

    def score(n, h):
        key_rows, queries, _, _ = columns[n]
        low, high = h * UNIT_WIDTH, (h + 1) * UNIT_WIDTH
        pieces = [queries[low:high]]
        if low > 0:
            pieces.insert(0, jnp.zeros((low, total), BF16))
        if high < inner:
            pieces.append(jnp.zeros((inner - high, total), BF16))
        scores_ref[n, h] = matmul(key_rows, jnp.concatenate(pieces, axis=0))

    def weigh(n, h):
        for low in range(0, total, 128):
            scores = scores_ref[n, h, :, low : low + 128]
            weights = jnp.exp(scores - jnp.max(scores, axis=0, keepdims=True))
            scale = 1.0 / jnp.sum(weights, axis=0, keepdims=True)
            weights_ref[n, h, :, low : low + 128] = (weights * scale).astype(BF16)

    def attend(n, h):
        _, _, value_rows, gates = columns[n]
        rows = slice(h * UNIT_WIDTH, (h + 1) * UNIT_WIDTH)
        attended = matmul(value_rows[rows], weights_ref[n, h]) * gates[rows]
        turned_ref[n, rows, :] = attended.astype(BF16)

    units = [(n, h) for h in range(ATTENTION_UNITS) for n in range(residues)]
    for step in range(len(units) + 2):
        if step < len(units):
            score(*units[step])
        if 1 <= step <= len(units):
            weigh(*units[step - 1])
        if step >= 2:
            attend(*units[step - 2])
    for n in range(residues):
        gated_ref[:, n] = turned_ref[n].T.reshape(blocks, seqs, inner)


def attention(normed, key_matrix, other_matrices):
    blocks, residues, seqs, depth = normed.shape
    total = blocks * seqs
    inner = ATTENTION_UNITS * UNIT_WIDTH
    return pl.pallas_call(
        attention_kernel,
        grid=(residues // 2,),
        in_specs=[
            pl.BlockSpec((blocks, 2, seqs, depth), lambda n: (0, n, 0, 0)),
            pl.BlockSpec((depth, inner), lambda n: (0, 0)),
            pl.BlockSpec((3 * inner, depth), lambda n: (0, 0)),
        ],
        out_specs=[
            pl.BlockSpec((blocks, 2, seqs, inner), lambda n: (0, n, 0, 0)),
            pl.BlockSpec((2, inner, total), lambda n: (n, 0, 0)),
        ],
        out_shape=[
            jax.ShapeDtypeStruct((blocks, residues, seqs, inner), BF16),
            jax.ShapeDtypeStruct((residues, inner, total), BF16),
        ],
        scratch_shapes=[
            pltpu.VMEM((2, ATTENTION_UNITS, total, total), F32),
            pltpu.VMEM((2, ATTENTION_UNITS, total, total), BF16),
        ],
        compiler_params=params(40, "arbitrary"),
        cost_estimate=cost(14),
        name="attention",
    )(normed, key_matrix, other_matrices)


def alignment_kernel(
    high_ref, low_ref, turned_ref, final_ref, entry_ref, left_ref, right_ref, rows_ref
):
    blocks, residues, seqs, depth = high_ref.shape
    total = blocks * seqs
    features = TENSOR_FEATURES
    step = pl.program_id(0)
    for n in range(residues):
        low = low_ref[:, n, :seqs, :].reshape(total, depth)
        column = high_ref[:, n].reshape(total, depth).astype(F32) + low.astype(F32)
        spreads = []
        for block in range(blocks):
            kept = low_ref[block, n, seqs:, :seqs].astype(F32)
            spreads.append(jnp.sum(kept, axis=0, keepdims=True))
        spread = jnp.concatenate(spreads, axis=1)
        updated = column.T * spread + matmul(final_ref[...], turned_ref[n])
        centred = updated - jnp.mean(updated, axis=0, keepdims=True)
        variance = jnp.mean(centred * centred, axis=0, keepdims=True)
        normed = (centred * lax.rsqrt(variance + EPS)).astype(BF16)
        projected = matmul(entry_ref[...], normed)
        right_ref[n] = projected[features:].astype(BF16)
        first = pl.multiple_of((step * residues + n) * features, features)
        for tile in range(total // 128):
            rows_ref[tile, pl.ds(first, features), :] = projected[
                :features, tile * 128 : (tile + 1) * 128
            ]

    @pl.when(step == pl.num_programs(0) - 1)
    def _():
        count = rows_ref.shape[1] // features
        together = max(1, 16 // count)
        for c in range(0, features, together):
            pieces = []
            for e in range(together):
                chosen = pl.ds(c + e, count, stride=features)
                tiles = [rows_ref[tile, chosen, :] for tile in range(total // 128)]
                pieces.append(jnp.concatenate(tiles, axis=1))
            piece = jnp.concatenate(pieces, axis=0).astype(BF16)
            left_ref[c * count : (c + together) * count, :] = piece


def alignment(high, low, turned, final_matrix, entry_matrices):
    blocks, residues, seqs, depth = high.shape
    total = blocks * seqs
    features = TENSOR_FEATURES
    return pl.pallas_call(
        alignment_kernel,
        grid=(residues // 2,),
        in_specs=[
            pl.BlockSpec((blocks, 2, seqs, depth), lambda n: (0, n, 0, 0)),
            pl.BlockSpec((blocks, 2, seqs + 16, depth), lambda n: (0, n, 0, 0)),
            pl.BlockSpec((2, depth, total), lambda n: (n, 0, 0)),
            pl.BlockSpec(final_matrix.shape, lambda n: (0, 0)),
            pl.BlockSpec(entry_matrices.shape, lambda n: (0, 0)),
        ],
        out_specs=[
            pl.BlockSpec((features * residues, total), lambda n: (0, 0)),
            pl.BlockSpec((2, features, total), lambda n: (n, 0, 0)),
        ],
        out_shape=[
            jax.ShapeDtypeStruct((features * residues, total), BF16),
            jax.ShapeDtypeStruct((residues, features, total), BF16),
        ],
        scratch_shapes=[pltpu.VMEM((total // 128, residues * features, 128), F32)],
        compiler_params=params(20, "arbitrary"),
        cost_estimate=cost(6),
        name="alignment",
    )(high, low, turned, final_matrix, entry_matrices)


def pair_kernel(
    left_slots_ref,
    right_firsts_ref,
    own_ref,
    other_ref,
    *rest,
):
    weights_ref, couplings_ref, entry_ref, switch_ref, mid_ref, gate_ref, sides_ref = rest[-11:-4]
    outer_ref, spread_ref, sum_ref, rows_ref = rest[-4:]
    right_refs = rest[:-11]
    features = TENSOR_FEATURES
    slots, piece_rows, total = own_ref.shape
    residues = piece_rows // features
    rows = 2 * slots * residues
    share = right_refs[0].shape[0]
    columns = len(right_refs) * share
    groups = columns // GROUP
    wide = share * features
    together = spread_ref.shape[1] // 128

    for half, left_ref in enumerate((own_ref, other_ref)):
        piece = left_ref[...].reshape(slots * piece_rows, total)
        target = slice(half * slots * piece_rows, (half + 1) * slots * piece_rows)
        for p, right_ref in enumerate(right_refs):
            right = right_ref[...].reshape(wide, total)
            outer_ref[target, p * wide : (p + 1) * wide] = matmul_nt(piece, right) * (1.0 / total)

    spread_ref[...] = jnp.zeros_like(spread_ref)

    def channel_step(p, carry):
        slot = lax.rem(p, 2)
        for e in range(together):
            source = pl.multiple_of((p * together + e) * features, features)
            piece = weights_ref[pl.ds(source, features), :]
            for place in range(GROUP):
                low = e * 128 + place * features
                spread_ref[slot, low : low + features, place * C_Z : (place + 1) * C_Z] = piece
        pieces = []
        for g in range(groups):
            parts = []
            for e in range(together):
                channel = []
                for slot_number in range(2 * slots):
                    first = slot_number * piece_rows + (p * together + e) * residues
                    source = pl.ds(pl.multiple_of(first, residues), residues)
                    channel.append(outer_ref[source, g * 128 : (g + 1) * 128])
                parts.append(jnp.concatenate(channel, axis=0).astype(BF16))
            pieces.append(jnp.concatenate(parts, axis=1))
        update = matmul(jnp.concatenate(pieces, axis=0), spread_ref[slot])

        @pl.when(p == 0)
        def _():
            sum_ref[...] = update

        @pl.when(p > 0)
        def _():
            sum_ref[...] += update

        return carry

    lax.fori_loop(0, features // together, channel_step, 0)

    left_firsts = [left_slots_ref[j] * residues for j in range(2 * slots)]
    right_firsts = [right_firsts_ref[p] for p in range(len(right_refs))]
    for g in range(groups):
        normed, places = [], []
        for place in range(GROUP):
            p, n = divmod(g * GROUP + place, share)
            b = right_firsts[p] + n
            places.append(b)
            lanes = slice(place * C_Z, (place + 1) * C_Z)
            pieces = []
            for first in left_firsts:
                source = pl.ds(pl.multiple_of(g * rows + first, residues), residues)
                pieces.append(sum_ref[source, lanes])
            mid = jnp.concatenate(pieces, axis=0)
            mid = mid + couplings_ref[pl.ds(b, rows, stride=columns), :]
            mid_ref[b] = mid
            centred = mid - jnp.mean(mid, axis=1, keepdims=True)
            variance = jnp.mean(centred * centred, axis=1, keepdims=True)
            normed.append((centred * lax.rsqrt(variance + EPS)).astype(BF16))
        gates = sigmoid(matmul(jnp.concatenate(normed, axis=0), switch_ref[...]))
        blank = jnp.zeros_like(normed[0])
        for place in range(0, GROUP, 2):
            twice = []
            for e in range(2):
                gate_ref[places[place + e]] = gates[(place + e) * rows : (place + e + 1) * rows]
                twice.append(jnp.concatenate([normed[place + e], blank], axis=1))
                twice.append(jnp.concatenate([blank, normed[place + e]], axis=1))
            sides = matmul_nt(entry_ref[...], jnp.concatenate(twice, axis=0))
            sides = sigmoid(sides[C_TRI:]) * sides[:C_TRI]
            for e in range(2):
                first = pl.multiple_of(places[place + e] * C_TRI, C_TRI)
                rows_ref[pl.ds(first, C_TRI), :] = sides[:, e * 2 * rows : (e + 1) * 2 * rows]

    def turn_step(c, carry):
        sides_ref[c] = rows_ref[pl.ds(c, columns, stride=C_TRI), :].astype(BF16)
        return carry

    lax.fori_loop(0, C_TRI, turn_step, 0, unroll=8)


def pair_update(left_slots, right_firsts, left, rights, weights, couplings, entry, switch):
    rows, columns, depth = couplings.shape
    whole = jax.ShapeDtypeStruct((columns, rows, depth), F32)
    smem = pl.BlockSpec(memory_space=pltpu.SMEM)
    vmem = pl.BlockSpec(memory_space=pltpu.VMEM)
    return pl.pallas_call(
        pair_kernel,
        in_specs=[smem] * 2 + [vmem] * (6 + len(rights)),
        out_specs=[vmem] * 3,
        out_shape=[whole, whole, jax.ShapeDtypeStruct((C_TRI, columns, 2 * rows), BF16)],
        scratch_shapes=[
            pltpu.VMEM((rows * TENSOR_FEATURES, columns * TENSOR_FEATURES), F32),
            pltpu.VMEM((2, 8 * 128, GROUP * depth), BF16),
            pltpu.VMEM((columns // GROUP * rows, GROUP * depth), F32),
            pltpu.VMEM((columns * C_TRI, 2 * rows), F32),
        ],
        compiler_params=params(36),
        cost_estimate=cost(12),
        name="pair_update",
    )(
        left_slots,
        right_firsts,
        *left,
        *rights,
        weights,
        couplings.reshape(rows * columns, depth),
        entry,
        switch,
    )


def product_kernel(sides_ref, out_ref, *, grid_rows, grid_columns):
    channels, part, lanes = sides_ref.shape[1:]
    half = lanes // 2
    lane = lax.broadcasted_iota(jnp.int32, (grid_columns * part, lanes), 1)
    front = lane < half
    cut = front[: part // 2]
    for channel in range(channels):
        lefts, rights = [], []
        for r in range(0, grid_rows, 2):
            even, odd = [
                jnp.concatenate(
                    [sides_ref[(r + e) * grid_columns + c, channel] for c in range(grid_columns)],
                    axis=0,
                )
                for e in range(2)
            ]
            lefts.append(jnp.where(front, even, pltpu.roll(odd, half, 1)))
            rights.append(jnp.where(front, pltpu.roll(even, half, 1), odd))
        product = matmul_nt(jnp.concatenate(rights, axis=1), jnp.concatenate(lefts, axis=1))
        product = product.astype(BF16)
        for c in range(grid_columns):
            for r in range(0, grid_rows, 2):
                block = product[c * part : (c + 1) * part, r * half : (r + 2) * half]
                top, bottom = block[: part // 2], block[part // 2 :]
                even = jnp.where(cut, top, pltpu.roll(bottom, half, 1))
                out_ref[r * grid_columns + c, channel] = even
                odd = jnp.where(cut, pltpu.roll(top, half, 1), bottom)
                out_ref[(r + 1) * grid_columns + c, channel] = odd


def triangle_product(sides, grid_rows, grid_columns):
    devices, channels, part, lanes = sides.shape
    step = 2 if channels % 2 == 0 else 1
    return pl.pallas_call(
        functools.partial(product_kernel, grid_rows=grid_rows, grid_columns=grid_columns),
        grid=(channels // step,),
        in_specs=[pl.BlockSpec((devices, step, part, lanes), lambda c: (0, c, 0, 0))],
        out_specs=pl.BlockSpec((devices, step, part // 2, lanes), lambda c: (0, c, 0, 0)),
        out_shape=jax.ShapeDtypeStruct((devices, channels, part // 2, lanes), BF16),
        compiler_params=params(16, "arbitrary"),
        cost_estimate=cost(3),
        name="triangle_product",
    )(sides)


def output_kernel(product_ref, mid_ref, gate_ref, final_ref, out_ref, wide_ref):
    channels, part, lanes = product_ref.shape
    columns, rows, _ = mid_ref.shape
    wide_ref[...] = product_ref[...].astype(F32).reshape(channels * part, lanes)
    for j in range(part):
        product = wide_ref[pl.ds(j, channels, stride=part), :]
        centred = product - jnp.mean(product, axis=0, keepdims=True)
        variance = jnp.mean(centred * centred, axis=0, keepdims=True)
        normed = (centred * lax.rsqrt(variance + EPS)).T.astype(BF16)
        update = matmul(normed, final_ref[...])
        for half in range(2):
            b = half * part + j
            piece = update[half * rows : (half + 1) * rows]
            out_ref[pl.ds(b, rows, stride=columns), :] = mid_ref[b] + gate_ref[b] * piece


def pair_result(product, mid, gate, final_matrix):
    channels, part, lanes = product.shape
    columns, rows, depth = mid.shape
    vmem = pl.BlockSpec(memory_space=pltpu.VMEM)
    out = pl.pallas_call(
        output_kernel,
        in_specs=[vmem] * 4,
        out_specs=vmem,
        out_shape=jax.ShapeDtypeStruct((rows * columns, depth), F32),
        scratch_shapes=[pltpu.VMEM((channels * part, lanes), F32)],
        compiler_params=params(12),
        cost_estimate=cost(4),
        name="pair_result",
    )(product, mid, gate, final_matrix)
    return out.reshape(rows, columns, depth)


def swap_cores(block):
    count = lax.axis_size("col")
    return lax.ppermute(block, "col", [(c, c ^ 1) for c in range(count)])


def gather_turned(block):
    rows, columns = lax.axis_size("row"), lax.axis_size("col")
    me, core = lax.axis_index("col") // 2, lax.rem(lax.axis_index("col"), 2)
    arrived = []
    for shift in range(rows):
        moves = []
        for r in range(rows):
            for q in range(rows):
                for side in range(2):
                    source = r * columns + 2 * q + side
                    moves.append((source, q * columns + 2 * ((r + shift) % rows) + side))
        arrived.append(lax.ppermute(block, ("row", "col"), moves))
    own = jnp.stack(arrived)
    other = swap_cores(own)
    shifts = lax.rem(me - jnp.arange(rows, dtype=jnp.int32) + rows, rows)
    residues = block.shape[0] // TENSOR_FEATURES
    if residues % 8 == 0:
        return (own, other), jnp.concatenate([shifts + core * rows, shifts + (1 - core) * rows])
    own, other = jnp.take(own, shifts, axis=0), jnp.take(other, shifts, axis=0)
    joined = 8 // residues
    ordered = []
    for side in (jnp.where(core == 0, own, other), jnp.where(core == 0, other, own)):
        side = side.reshape(rows // joined, joined, TENSOR_FEATURES, residues, -1)
        side = jnp.transpose(side, (0, 2, 1, 3, 4))
        ordered.append(side.reshape(rows // joined, joined * block.shape[0], -1))
    return tuple(ordered), jnp.arange(2 * rows // joined, dtype=jnp.int32)


def exchange_rows(pieces):
    rows = lax.axis_size("row")
    arrived = [pieces[0]]
    for shift in range(1, rows):
        moves = [(r, r ^ shift) for r in range(rows)]
        arrived.append(lax.ppermute(pieces[shift], "row", moves))
    return arrived, lax.axis_index("row") ^ jnp.arange(rows, dtype=jnp.int32)


def paired_entries(matrices):
    turned = matrices.reshape(C_Z, 2, 2, C_TRI)
    return jnp.transpose(turned, (2, 3, 1, 0)).reshape(2 * C_TRI, 2 * C_Z)


def body(
    homolog_tensor,
    couplings,
    attention_probe_matrix,
    attention_extra_matrices,
    attention_final_matrix,
    tensor_entry_matrices,
    tensor_final_matrix,
    incoming_entry_matrices,
    incoming_switch_matrix,
    incoming_final_matrix,
):
    inner = ATTENTION_UNITS * UNIT_WIDTH
    row_count = lax.axis_size("row")
    seqs, residues, depth = homolog_tensor.shape
    own_residues = residues // row_count
    high = standardise(homolog_tensor, high_kernel, 0)
    high = high.reshape(row_count, own_residues, seqs, depth)
    low = standardise(homolog_tensor, low_kernel, 16)
    low = low.reshape(row_count, own_residues, seqs + 16, depth)
    high = lax.all_to_all(high, "row", split_axis=0, concat_axis=0)
    low = lax.all_to_all(low, "row", split_axis=0, concat_axis=0)
    others = jnp.concatenate(
        [attention_probe_matrix.T, attention_extra_matrices[:, inner:].T], axis=0
    )
    gated, turned = attention(high, attention_extra_matrices[:, :inner], others)
    left_piece, right_piece = alignment(
        high, low, turned, attention_final_matrix.T, tensor_entry_matrices.T
    )


    rights, sources = exchange_rows([right_piece] * row_count)
    left, left_slots = gather_turned(left_piece)
    mid, gate, sides = pair_update(
        left_slots,
        sources * own_residues,
        left,
        rights,
        tensor_final_matrix,
        couplings,
        paired_entries(incoming_entry_matrices),
        incoming_switch_matrix,
    )
    gated, sides = lax.optimization_barrier((gated, sides))

    everywhere = ("row", "col")
    column_count = lax.axis_size("col")
    devices = row_count * column_count
    sides = sides.reshape(devices, C_TRI // devices, *sides.shape[1:])
    sides = lax.all_to_all(sides, everywhere, split_axis=0, concat_axis=0)

    pieces = [
        lax.dynamic_index_in_dim(gated, sources[shift], keepdims=False)
        for shift in range(row_count)
    ]
    pieces, sources = exchange_rows(pieces)
    gated = jnp.take(jnp.stack(pieces), sources, axis=0)
    gated = jnp.transpose(gated.reshape(residues, seqs, inner), (1, 0, 2))
    change = jnp.dot(
        gated.reshape(-1, inner), attention_final_matrix, preferred_element_type=F32
    )
    refreshed_homologs = homolog_tensor + change.reshape(homolog_tensor.shape)

    product = triangle_product(sides, row_count, column_count)
    product = lax.all_to_all(product, everywhere, split_axis=0, concat_axis=0)
    product = product.reshape(C_TRI, *product.shape[2:])
    pair_output = pair_result(product, mid, gate, incoming_final_matrix)
    return (refreshed_homologs, pair_output)


def solution(mesh):
    in_specs = (
        P("row", "col", None),
        P("row", "col", None),
        P(),
        P(),
        P(),
        P(),
        P(),
        P(),
        P(),
        P(),
    )
    out_specs = (P("row", "col", None), P("row", "col", None))
    return jax.shard_map(body, mesh=mesh, in_specs=in_specs, out_specs=out_specs, check_vma=False)
```

time: 164 us -> 172 us (1.049)
  local copies, waits for them, and re-layouts: 5.67 us -> 35.6 us
  blocking collectives: 22.5 us -> 0 us
  Pallas kernels: 45.2 us -> 31.9 us
  between operations: 0.84 us -> 8.59 us
  starting transfers between devices: 33.3 us -> 36.7 us
    all_to_all x1 -> x0, blocking collectives: 22.5 us -> none  [body(): lax.all_to_all(side, everywhere, split_axis=0, concat_axis=0)]
    unnamed x24 -> x64, local copies, waits for them, and re-layouts: 3.53 us -> 25.8 us
    all_to_all x2 -> x1, waiting for transfers between devices: 16 us -> 0.01 us  [body(): product = lax.all_to_all(product, everywhere, split_axis=0, concat_axis=0)]
    ppermute x7 -> x10, waiting for transfers between devices: 6.02 us -> 19.9 us  [the longest x6 15.1 us: exchange_rows(): arrived.append(lax.ppermute(pieces[shift], 'row', moves))]
    all_to_all x2 -> x1, waiting for transfers between devices: 15.2 us -> 27.5 us  [body(): sides = lax.all_to_all(sides, everywhere, split_axis=0, concat_axis=0)]
    ppermute x7 -> x10, starting transfers between devices: 12.3 us -> 20.6 us  [the longest x4 10.8 us: gather_turned(): arrived.append(lax.ppermute(block, ('row', 'col'), moves))]
    pallas_call x4 -> x5, Pallas kernels: 34.8 us -> 26.4 us  [the longest x1 10.4 us: attention(): pl.pallas_call(attention_kernel, grid=(residues // 2,), in_specs=[pl.Bloc...]
    all_to_all x1, waiting for transfers between devices: 11.1 us -> 3.01 us  [body(): high = lax.all_to_all(high, 'row', split_axis=0, concat_axis=0)]
  transfers between devices with their start and end apart: 14 -> 15, of which waited for: 9 -> 10; matrix products, arithmetic and copies ran while one was open for 5% -> 12% of each run, Pallas kernels for 19% -> 7%
where the time goes in v4:
time: 172 us; the launch traced here: 170 us
  waiting for transfers between devices  50.8 us (30%)
  starting transfers between devices  36.7 us (21%)
  local copies, waits for them, and re-layouts  35.6 us (21%)
  Pallas kernels  31.9 us (19%)
  between operations  8.59 us (5%)
  matrix products  3.5 us (2%)
  other arithmetic  3.16 us (2%)
    all_to_all x1, waiting for transfers between devices, body(): sides = lax.all_to_all(sides, everywhere, split_axis=0, concat_axis=0)  27.5 us
    unnamed x64, local copies, waits for them, and re-layouts  25.8 us
    ppermute x6, waiting for transfers between devices, exchange_rows(): arrived.append(lax.ppermute(pieces[shift], 'row', moves))  15.1 us
    ppermute x4, starting transfers between devices, gather_turned(): arrived.append(lax.ppermute(block, ('row', 'col'), moves))  10.8 us
    pallas_call x1, Pallas kernels, attention(): pl.pallas_call(attention_kernel, grid=(residues // 2,), in_specs=[pl.Bloc...  10.4 us
    ppermute x6, starting transfers between devices, exchange_rows(): arrived.append(lax.ppermute(pieces[shift], 'row', moves))  9.83 us
    pallas_call x1, Pallas kernels, pair_update(): pl.pallas_call(pair_kernel, in_specs=[smem] * 2 + [vmem] * (6 + len(right...  9.34 us
    all_to_all x1, starting transfers between devices, body(): high = lax.all_to_all(high, 'row', split_axis=0, concat_axis=0)  5.29 us
  transfers between devices with their start and end apart: 15, of which 10 were waited for; matrix products, arithmetic and copies ran while one was open for 12% of the time, Pallas kernels for 7%

profile of v4, /device:TPU:0, one launch (start us, length us, event | category | flops | bytes accessed | tf_op | source)
XLA Modules:
  0.0 170.3 jit_solution(12476812141435217463)
XLA Ops:
  0.6 1.6 copy-done
  2.2 1.5 standardise.2
  3.7 1.0 copy-done.8
  4.7 5.3 %all-to-all-start = ((bf16[4,8,64,256]{3,2,1,0:T(8,128)(2,1)}), bf16[4,8,64,256]{3,2,1,0:T(8,128)(2,1)S(1)}, u32[]{:S(2)}, u32[]{:S(2)}) async-start(bf16[4,8,64,256]{3,2,1,0:T(8,128)(2,1)} %bitcast.43), calls=%async_computation | async-start | bytes 2097152 | tf_op jit(solution)/shard_map/all_to_all | solution.py:534
  10.0 1.7 slice.19
  11.7 1.6 slice.18.key_ref
  13.2 1.1 copy.17
  14.3 0.8 copy.12
  15.1 1.0 copy.14
  16.1 1.7 pad_maximum_fusion.2.others_ref
  17.8 1.8 %standardise.3 = bf16[32,80,256]{2,1,0:T(8,128)(2,1)S(1)} custom-call(f32[64,32,256]{2,1,0:T(8,128)S(1)} %copy-done.1, f32[64,32,256]{2,1,0:T(8,128)S(1)} %copy-done.1), custom_call_target="tpu_custom_call" | custom-call | flops 3000000000 | bytes 3000000 | tf_op jit(solution)/shard_map/standardise/pallas_call | solution.py:90
  19.6 1.0 copy-done.2
  20.6 3.0 %all-to-all-done.normed_ref.high_ref = bf16[4,8,64,256]{3,2,1,0:T(8,128)(2,1)S(1)} async-done(((bf16[4,8,64,256]{3,2,1,0:T(8,128)(2,1)}), bf16[4,8,64,256]{3,2,1,0:T(8,128)(2,1)S(1)}, u32[]{:S(2)}, u32[]{:S(2)}) %all-to-all-start) | async-done | bytes 1048608 | tf_op jit(solution)/shard_map/all_to_all | solution.py:534
  23.6 1.0 copy-done.5
  24.6 3.5 %all-to-all-start.1 = ((bf16[4,8,80,256]{3,2,1,0:T(8,128)(2,1)}), bf16[4,8,80,256]{3,2,1,0:T(8,128)(2,1)S(1)}, u32[]{:S(2)}, u32[]{:S(2)}) async-start(bf16[4,8,80,256]{3,2,1,0:T(8,128)(2,1)} %bitcast.42), calls=%async_computation.1 | async-start | bytes 2621440 | tf_op jit(solution)/shard_map/all_to_all | solution.py:535
  28.2 1.2 copy-done.6
  29.4 1.0 copy-done.10
  30.4 0.9 copy-done.11
  31.3 10.4 %attention.1 = (bf16[4,8,64,256]{3,2,1,0:T(8,128)(2,1)S(1)}, bf16[8,256,256]{2,1,0:T(8,128)(2,1)S(1)}) custom-call(bf16[4,8,64,256]{3,2,1,0:T(8,128)(2,1)S(1)} %copy-done.6, bf16[256,256]{1,0:T(8,128)(2,1)S(1)} %copy-done.11, bf16[768,256]{1,0:T(8,128)(2,1)S(1)} %copy-done.10), custom_call_target="tpu_custom_call" | custom-call | flops 14000000000 | bytes 14000000 | tf_op jit(solution)/shard_map/attention/pallas_call | solution.py:160
  41.7 1.0 copy-done.3
  42.7 1.0 copy-done.23
  44.0 1.2 copy-done.7
  45.2 0.8 copy-done.16
  46.0 1.2 copy-done.24
  47.2 3.5 %alignment.1 = (bf16[256,256]{1,0:T(8,128)(2,1)S(1)}, bf16[8,32,256]{2,1,0:T(8,128)(2,1)S(1)}) custom-call(bf16[4,8,64,256]{3,2,1,0:T(8,128)(2,1)S(1)} %copy-done.7, bf16[4,8,80,256]{3,2,1,0:T(8,128)(2,1)S(1)} %all-to-all-done.1.low_ref, bf16[8,256,256]{2,1,0:T(8,128)(2,1)S(1)} %copy-done.24, bf16[256,256]{1,0:T(8,128)(2,1)S(1)} %bitcast.44, ...), custom_call_target="tpu_custom_call" | custom-call | flops 6000000000 | bytes 6000000 | tf_op jit(solution)/shard_map/alignment/pallas_call | solution.py:231
  50.7 0.6 copy-done.14
  51.4 0.7 collective-permute-start
  52.0 4.4 %collective-permute-start.1 = (bf16[256,256]{1,0:T(8,128)(2,1)S(1)}, bf16[256,256]{1,0:T(8,128)(2,1)S(1)}, u32[]{:S(2)}, u32[]{:S(2)}) collective-permute-start(bf16[256,256]{1,0:T(8,128)(2,1)S(1)} %get-tuple-element.13), channel_id=1, source_target_pairs={{0,2},{1,3},{2,10},{3,11},{4,18},{5,19},{6,26},{7,27},{8,4},{9,5},... | collective-permute-start | bytes 393224 | tf_op jit(solution)/shard_map/ppermute | solution.py:483
  56.4 3.5 %collective-permute-start.2 = (bf16[256,256]{1,0:T(8,128)(2,1)S(1)}, bf16[256,256]{1,0:T(8,128)(2,1)S(1)}, u32[]{:S(2)}, u32[]{:S(2)}) collective-permute-start(bf16[256,256]{1,0:T(8,128)(2,1)S(1)} %get-tuple-element.13), channel_id=1, source_target_pairs={{0,4},{1,5},{2,12},{3,13},{4,20},{5,21},{6,28},{7,29},{8,6},{9,7},... | collective-permute-start | bytes 393224 | tf_op jit(solution)/shard_map/ppermute | solution.py:483
  59.9 2.2 %collective-permute-start.3 = (bf16[256,256]{1,0:T(8,128)(2,1)S(1)}, bf16[256,256]{1,0:T(8,128)(2,1)S(1)}, u32[]{:S(2)}, u32[]{:S(2)}) collective-permute-start(bf16[256,256]{1,0:T(8,128)(2,1)S(1)} %get-tuple-element.13), channel_id=1, source_target_pairs={{0,6},{1,7},{2,14},{3,15},{4,22},{5,23},{6,30},{7,31},{8,0},{9,1},... | collective-permute-start | bytes 393224 | tf_op jit(solution)/shard_map/ppermute | solution.py:483
  62.2 1.1 collective-permute-done.1
  63.2 1.3 collective-permute-done.2
  64.5 2.5 %collective-permute-done.3 = bf16[256,256]{1,0:T(8,128)(2,1)S(1)} collective-permute-done((bf16[256,256]{1,0:T(8,128)(2,1)S(1)}, bf16[256,256]{1,0:T(8,128)(2,1)S(1)}, u32[]{:S(2)}, u32[]{:S(2)}) %collective-permute-start.3) | collective-permute-done | bytes 131104 | tf_op jit(solution)/shard_map/ppermute | solution.py:483
  67.2 4.8 %collective-permute-start.5 = (bf16[8,32,256]{2,1,0:T(8,128)(2,1)}, bf16[8,32,256]{2,1,0:T(8,128)(2,1)S(1)}, u32[]{:S(2)}, u32[]{:S(2)}) collective-permute-start(bf16[8,32,256]{2,1,0:T(8,128)(2,1)} %copy-done.14), channel_id=1, source_target_pairs={{0,8},{8,0},{16,24},{24,16},{1,9},{9,1},{17,25},{25,17},{2,10},{10... | collective-permute-start | bytes 393224 | tf_op jit(solution)/shard_map/ppermute | solution.py:505
  72.0 1.5 collective-permute-start.7
  73.5 1.6 reshape.59
  75.1 1.7 %copy.15 = bf16[128,2,2,128]{0,1,3,2:T(2,128)(2,1)} copy(bf16[128,2,2,128]{3,2,1,0:T(2,128)(2,1)} %reshape.59) | data formatting | bytes 262144 | tf_op jit(solution)/shard_map/reshape | solution.py:510
  76.8 0.9 copy.24
  77.8 2.7 %collective-permute-done.6.rest_2_ = bf16[8,32,256]{2,1,0:T(8,128)(2,1)S(1)} collective-permute-done((bf16[8,32,256]{2,1,0:T(8,128)(2,1)}, bf16[8,32,256]{2,1,0:T(8,128)(2,1)S(1)}, u32[]{:S(2)}, u32[]{:S(2)}) %collective-permute-start.6) | collective-permute-done | bytes 131104 | tf_op jit(solution)/shard_map/ppermute | solution.py:505
  80.6 1.2 copy-done.12
  81.8 0.9 copy-done.13
  82.7 0.9 copy-done.15
  83.6 0.8 copy-done.17
  84.4 9.3 %pair_update.1 = (f32[32,64,128]{2,1,0:T(8,128)S(1)}, f32[32,64,128]{2,1,0:T(8,128)S(1)}, bf16[128,32,128]{2,1,0:T(8,128)(2,1)}) custom-call(s32[8]{0:T(128)S(1)} %pad_add_fusion.left_slots_ref, s32[4]{0:T(128)S(1)} %broadcast_multiply_fusion.right_firsts_ref, bf16[4,256,256]{2,1,0:T(8,128)(2,1)S(1)} %pad_maximum_fusion.1.own_ref, ...), custom_call_target="tpu_custom_call" | custom-call | flops 12000000000 | bytes 12000000 | tf_op jit(solution)/shard_map/pair_update/pallas_call | solution.py:363
  93.7 1.0 copy-done.19
  94.7 1.0 copy-done.21
  95.7 3.7 %all-to-all-start.2 = ((bf16[32,4,32,128]{3,2,1,0:T(8,128)(2,1)}), bf16[32,4,32,128]{3,2,1,0:T(8,128)(2,1)}, u32[]{:S(2)}, u32[]{:S(2)}) async-start(bf16[32,4,32,128]{3,2,1,0:T(8,128)(2,1)} %bitcast.26), calls=%async_computation.2 | async-start | bytes 2097152 | tf_op jit(solution)/shard_map/all_to_all | solution.py:563
  99.4 27.5 %all-to-all-done.2.sides_ref = bf16[32,4,32,128]{3,2,1,0:T(8,128)(2,1)} async-done(((bf16[32,4,32,128]{3,2,1,0:T(8,128)(2,1)}), bf16[32,4,32,128]{3,2,1,0:T(8,128)(2,1)}, u32[]{:S(2)}, u32[]{:S(2)}) %all-to-all-start.2) | async-done | bytes 1048608 | tf_op jit(solution)/shard_map/all_to_all | solution.py:563
  127.0 1.9 %triangle_product.1 = bf16[32,4,16,128]{3,2,1,0:T(8,128)(2,1)S(1)} custom-call(bf16[32,4,32,128]{3,2,1,0:T(8,128)(2,1)} %all-to-all-done.2.sides_ref), custom_call_target="tpu_custom_call" | custom-call | flops 3000000000 | bytes 3000000 | tf_op jit(solution)/shard_map/triangle_product/pallas_call | solution.py:422
  128.9 0.8 copy-done.9
  129.7 3.5 %all-to-all-start.3 = ((bf16[32,4,16,128]{3,2,1,0:T(8,128)(2,1)}), bf16[32,4,16,128]{3,2,1,0:T(8,128)(2,1)}, u32[]{:S(2)}, u32[]{:S(2)}) async-start(bf16[32,4,16,128]{3,2,1,0:T(8,128)(2,1)} %copy-done.9), calls=%async_computation.3 | async-start | bytes 1048576 | tf_op jit(solution)/shard_map/all_to_all | solution.py:578
  133.2 0.6 fusion.7
  141.6 0.9 constant_dynamic-slice_fusion
  142.5 1.4 collective-permute-start.8
  143.9 1.5 collective-permute-start.9
  146.2 6.4 %collective-permute-done.8 = bf16[8,64,256]{2,1,0:T(8,128)(2,1)S(1)} collective-permute-done((bf16[8,64,256]{2,1,0:T(8,128)(2,1)}, bf16[8,64,256]{2,1,0:T(8,128)(2,1)S(1)}, u32[]{:S(2)}, u32[]{:S(2)}) %collective-permute-start.8) | collective-permute-done | bytes 262176 | tf_op jit(solution)/shard_map/ppermute | solution.py:505
  152.6 5.0 %collective-permute-done.9 = bf16[8,64,256]{2,1,0:T(8,128)(2,1)S(1)} collective-permute-done((bf16[8,64,256]{2,1,0:T(8,128)(2,1)}, bf16[8,64,256]{2,1,0:T(8,128)(2,1)S(1)}, u32[]{:S(2)}, u32[]{:S(2)}) %collective-permute-start.9) | collective-permute-done | bytes 262176 | tf_op jit(solution)/shard_map/ppermute | solution.py:505
  157.6 0.9 collective-permute-done.10
  158.5 0.7 copy-done.28
  159.2 1.3 pad_maximum_fusion
  160.5 1.6 gather_fusion
  162.1 3.5 %convolution_add_fusion = f32[64,32,256]{2,1,0:T(8,128)} fusion(f32[64,32,256]{2,1,0:T(8,128)S(1)} %copy-done.1, bf16[32,64,256]{2,1,0:T(8,128)(2,1)} %bitcast.48, pred[32]{0:T(512)(128)(4,1)S(1)} %broadcast_in_dim.15, bf16[256,256]{1,0:T(8,128)(2,1)S(1)} %copy-done.25), kind=kOutput, calls=%fused_computation.1 | convolution fusion | flops 269484032 | bytes 5373984 | tf_op jit(solution)/shard_map/dot_general | solution.py:572
  165.6 1.2 copy-done.22
  166.8 3.5 %pair_result.1 = f32[2048,128]{1,0:T(8,128)} custom-call(bf16[128,16,128]{2,1,0:T(8,128)(2,1)} %bitcast.27.product_ref, f32[32,64,128]{2,1,0:T(8,128)S(1)} %copy-done.20, f32[32,64,128]{2,1,0:T(8,128)S(1)} %copy-done.22, bf16[128,128]{1,0:T(8,128)(2,1)S(1)} %copy-done.18), custom_call_target="tpu_custom_call" | custom-call | flops 4000000000 | bytes 4000000 | tf_op jit(solution)/shard_map/pair_result/pallas_call | solution.py:454
  (57 shorter events, 1.5 us)
Async XLA Ops:
  0.6 1.6 copy-start
  3.7 1.0 copy-start.8
  4.7 9.6 %copy-start.29 = (bf16[256,256]{1,0:T(8,128)(2,1)S(1)}, bf16[256,256]{1,0:T(8,128)(2,1)}, u32[]{:S(2)}) copy-start(bf16[256,256]{1,0:T(8,128)(2,1)} %param.12) | copy-start | bytes 393220
  4.7 13.1 %copy-start.1 = (f32[64,32,256]{2,1,0:T(8,128)S(1)}, f32[64,32,256]{2,1,0:T(8,128)}, u32[]{:S(2)}) copy-start(f32[64,32,256]{2,1,0:T(8,128)} %second_ref.3) | copy-start | bytes 6291460
  4.7 18.9 %all-to-all-start = ((bf16[4,8,64,256]{3,2,1,0:T(8,128)(2,1)}), bf16[4,8,64,256]{3,2,1,0:T(8,128)(2,1)S(1)}, u32[]{:S(2)}, u32[]{:S(2)}) async-start(bf16[4,8,64,256]{3,2,1,0:T(8,128)(2,1)} %bitcast.43), calls=%async_computation | async-start | bytes 2097152 | tf_op jit(solution)/shard_map/all_to_all | solution.py:534
  19.6 1.1 copy-start.2
  23.6 1.0 copy-start.5
  24.6 19.4 %all-to-all-start.1 = ((bf16[4,8,80,256]{3,2,1,0:T(8,128)(2,1)}), bf16[4,8,80,256]{3,2,1,0:T(8,128)(2,1)S(1)}, u32[]{:S(2)}, u32[]{:S(2)}) async-start(bf16[4,8,80,256]{3,2,1,0:T(8,128)(2,1)} %bitcast.42), calls=%async_computation.1 | async-start | bytes 2621440 | tf_op jit(solution)/shard_map/all_to_all | solution.py:535
  28.1 1.2 copy-start.6
  29.4 1.0 copy-start.10
  30.4 0.9 copy-start.11
  41.7 1.0 copy-start.3
  42.6 1.0 copy-start.23
  44.0 1.2 copy-start.7
  45.2 0.8 copy-start.16
  46.0 1.2 copy-start.24
  50.7 0.7 copy-start.14
  51.4 10.8 %collective-permute-start = (bf16[256,256]{1,0:T(8,128)(2,1)S(1)}, bf16[256,256]{1,0:T(8,128)(2,1)S(1)}, u32[]{:S(2)}, u32[]{:S(2)}) collective-permute-start(bf16[256,256]{1,0:T(8,128)(2,1)S(1)} %get-tuple-element.13), channel_id=1, source_target_pairs={{0,0},{1,1},{2,8},{3,9},{4,16},{5,17},{6,24},{7,25},{8,2},{9,3},{1... | collective-permute-start | bytes 393224 | tf_op jit(solution)/shard_map/ppermute | solution.py:483
  52.0 11.2 %collective-permute-start.1 = (bf16[256,256]{1,0:T(8,128)(2,1)S(1)}, bf16[256,256]{1,0:T(8,128)(2,1)S(1)}, u32[]{:S(2)}, u32[]{:S(2)}) collective-permute-start(bf16[256,256]{1,0:T(8,128)(2,1)S(1)} %get-tuple-element.13), channel_id=1, source_target_pairs={{0,2},{1,3},{2,10},{3,11},{4,18},{5,19},{6,26},{7,27},{8,4},{9,5},... | collective-permute-start | bytes 393224 | tf_op jit(solution)/shard_map/ppermute | solution.py:483
  56.4 8.1 %collective-permute-start.2 = (bf16[256,256]{1,0:T(8,128)(2,1)S(1)}, bf16[256,256]{1,0:T(8,128)(2,1)S(1)}, u32[]{:S(2)}, u32[]{:S(2)}) collective-permute-start(bf16[256,256]{1,0:T(8,128)(2,1)S(1)} %get-tuple-element.13), channel_id=1, source_target_pairs={{0,4},{1,5},{2,12},{3,13},{4,20},{5,21},{6,28},{7,29},{8,6},{9,7},... | collective-permute-start | bytes 393224 | tf_op jit(solution)/shard_map/ppermute | solution.py:483
  59.9 7.0 %collective-permute-start.3 = (bf16[256,256]{1,0:T(8,128)(2,1)S(1)}, bf16[256,256]{1,0:T(8,128)(2,1)S(1)}, u32[]{:S(2)}, u32[]{:S(2)}) collective-permute-start(bf16[256,256]{1,0:T(8,128)(2,1)S(1)} %get-tuple-element.13), channel_id=1, source_target_pairs={{0,6},{1,7},{2,14},{3,15},{4,22},{5,23},{6,30},{7,31},{8,0},{9,1},... | collective-permute-start | bytes 393224 | tf_op jit(solution)/shard_map/ppermute | solution.py:483
  67.1 13.5 %collective-permute-start.4 = (bf16[4,256,256]{2,1,0:T(8,128)(2,1)S(1)}, bf16[4,256,256]{2,1,0:T(8,128)(2,1)S(1)}, u32[]{:S(2)}, u32[]{:S(2)}) collective-permute-start(bf16[4,256,256]{2,1,0:T(8,128)(2,1)S(1)} %pad_maximum_fusion.1.own_ref), channel_id=1, source_target_pairs={{0,1},{1,0},{2,3},{3,2},{4,5},{5,4},{6,7},{7,6},{8,9},{9,8},{10,11... | collective-permute-start | bytes 1572872 | tf_op jit(solution)/shard_map/ppermute | solution.py:469
  67.2 10.7 %collective-permute-start.5 = (bf16[8,32,256]{2,1,0:T(8,128)(2,1)}, bf16[8,32,256]{2,1,0:T(8,128)(2,1)S(1)}, u32[]{:S(2)}, u32[]{:S(2)}) collective-permute-start(bf16[8,32,256]{2,1,0:T(8,128)(2,1)} %copy-done.14), channel_id=1, source_target_pairs={{0,8},{8,0},{16,24},{24,16},{1,9},{9,1},{17,25},{25,17},{2,10},{10... | collective-permute-start | bytes 393224 | tf_op jit(solution)/shard_map/ppermute | solution.py:505
  72.0 8.6 %collective-permute-start.6 = (bf16[8,32,256]{2,1,0:T(8,128)(2,1)}, bf16[8,32,256]{2,1,0:T(8,128)(2,1)S(1)}, u32[]{:S(2)}, u32[]{:S(2)}) collective-permute-start(bf16[8,32,256]{2,1,0:T(8,128)(2,1)} %copy-done.14), channel_id=1, source_target_pairs={{0,16},{8,24},{16,0},{24,8},{1,17},{9,25},{17,1},{25,9},{2,18},{10... | collective-permute-start | bytes 393224 | tf_op jit(solution)/shard_map/ppermute | solution.py:505
  72.0 8.6 %collective-permute-start.7 = (bf16[8,32,256]{2,1,0:T(8,128)(2,1)}, bf16[8,32,256]{2,1,0:T(8,128)(2,1)S(1)}, u32[]{:S(2)}, u32[]{:S(2)}) collective-permute-start(bf16[8,32,256]{2,1,0:T(8,128)(2,1)} %copy-done.14), channel_id=1, source_target_pairs={{0,24},{8,16},{16,8},{24,0},{1,25},{9,17},{17,9},{25,1},{2,26},{10... | collective-permute-start | bytes 393224 | tf_op jit(solution)/shard_map/ppermute | solution.py:505
  80.5 1.2 copy-start.12
  81.8 0.9 copy-start.13
  82.7 0.9 copy-start.15
  83.6 0.8 copy-start.17
  93.7 1.0 copy-start.19
  94.7 1.0 copy-start.21
  95.7 31.3 %all-to-all-start.2 = ((bf16[32,4,32,128]{3,2,1,0:T(8,128)(2,1)}), bf16[32,4,32,128]{3,2,1,0:T(8,128)(2,1)}, u32[]{:S(2)}, u32[]{:S(2)}) async-start(bf16[32,4,32,128]{3,2,1,0:T(8,128)(2,1)} %bitcast.26), calls=%async_computation.2 | async-start | bytes 2097152 | tf_op jit(solution)/shard_map/all_to_all | solution.py:563
  99.4 42.1 %copy-start.4 = (bf16[4,8,64,256]{3,2,1,0:T(8,128)(2,1)S(1)}, bf16[4,8,64,256]{3,2,1,0:T(8,128)(2,1)}, u32[]{:S(2)}) copy-start(bf16[4,8,64,256]{3,2,1,0:T(8,128)(2,1)} %copy-done.3) | copy-start | bytes 3145732
  128.9 0.8 copy-start.9
  129.7 35.9 %all-to-all-start.3 = ((bf16[32,4,16,128]{3,2,1,0:T(8,128)(2,1)}), bf16[32,4,16,128]{3,2,1,0:T(8,128)(2,1)}, u32[]{:S(2)}, u32[]{:S(2)}) async-start(bf16[32,4,16,128]{3,2,1,0:T(8,128)(2,1)} %copy-done.9), calls=%async_computation.3 | async-start | bytes 1048576 | tf_op jit(solution)/shard_map/all_to_all | solution.py:578
  142.5 10.1 %collective-permute-start.8 = (bf16[8,64,256]{2,1,0:T(8,128)(2,1)}, bf16[8,64,256]{2,1,0:T(8,128)(2,1)S(1)}, u32[]{:S(2)}, u32[]{:S(2)}) collective-permute-start(bf16[8,64,256]{2,1,0:T(8,128)(2,1)} %get-tuple-element.23), channel_id=1, source_target_pairs={{0,8},{8,0},{16,24},{24,16},{1,9},{9,1},{17,25},{25,17},{2,10},{10... | collective-permute-start | bytes 786440 | tf_op jit(solution)/shard_map/ppermute | solution.py:505
  143.9 13.7 %collective-permute-start.9 = (bf16[8,64,256]{2,1,0:T(8,128)(2,1)}, bf16[8,64,256]{2,1,0:T(8,128)(2,1)S(1)}, u32[]{:S(2)}, u32[]{:S(2)}) collective-permute-start(bf16[8,64,256]{2,1,0:T(8,128)(2,1)} %get-tuple-element.22), channel_id=1, source_target_pairs={{0,16},{8,24},{16,0},{24,8},{1,17},{9,25},{17,1},{25,9},{2,18},{10... | collective-permute-start | bytes 786440 | tf_op jit(solution)/shard_map/ppermute | solution.py:505
  145.4 13.2 %collective-permute-start.10 = (bf16[8,64,256]{2,1,0:T(8,128)(2,1)}, bf16[8,64,256]{2,1,0:T(8,128)(2,1)S(1)}, u32[]{:S(2)}, u32[]{:S(2)}) collective-permute-start(bf16[8,64,256]{2,1,0:T(8,128)(2,1)} %get-tuple-element.21), channel_id=1, source_target_pairs={{0,24},{8,16},{16,8},{24,0},{1,25},{9,17},{17,9},{25,1},{2,26},{10... | collective-permute-start | bytes 786440 | tf_op jit(solution)/shard_map/ppermute | solution.py:505
  152.6 6.0 %copy-start.26 = (bf16[8,64,256]{2,1,0:T(8,128)(2,1)}, bf16[8,64,256]{2,1,0:T(8,128)(2,1)S(1)}, u32[]{:S(2)}) copy-start(bf16[8,64,256]{2,1,0:T(8,128)(2,1)S(1)} %collective-permute-done.8) | copy-start | bytes 786436
  157.6 0.9 copy-start.27
  158.5 0.7 copy-start.28
  159.2 2.9 %copy-start.25 = (bf16[256,256]{1,0:T(8,128)(2,1)S(1)}, bf16[256,256]{1,0:T(8,128)(2,1)}, u32[]{:S(2)}) copy-start(bf16[256,256]{1,0:T(8,128)(2,1)} %param.14) | copy-start | bytes 393220
  162.1 3.5 %copy-start.18 = (bf16[128,128]{1,0:T(8,128)(2,1)S(1)}, bf16[128,128]{1,0:T(8,128)(2,1)}, u32[]{:S(2)}) copy-start(bf16[128,128]{1,0:T(8,128)(2,1)} %final_ref.1) | copy-start | bytes 98308
  162.1 3.5 %copy-start.20 = (f32[32,64,128]{2,1,0:T(8,128)S(1)}, f32[32,64,128]{2,1,0:T(8,128)}, u32[]{:S(2)}) copy-start(f32[32,64,128]{2,1,0:T(8,128)} %copy-done.19) | copy-start | bytes 3145732
  165.6 1.2 copy-start.22

commit v5 on v4

v5 whole, which is shorter than its diff:
```python
import functools

import jax
import jax.numpy as jnp
from jax import lax
from jax.experimental import pallas as pl
from jax.experimental.pallas import tpu as pltpu
from jax.sharding import PartitionSpec as P

FEATURE_DEPTH = 256
C_Z = 128
TENSOR_FEATURES = 32
C_TRI = 128
ATTENTION_UNITS = 8
UNIT_WIDTH = 32
EPS = 1e-05
GROUP = 4
F32 = jnp.float32
BF16 = jnp.bfloat16
NT = (((1,), (1,)), ((), ()))
VMEM_LIMIT = 56 * 1024 * 1024


def matmul(left, right):
    return jnp.dot(left, right, preferred_element_type=F32)


def matmul_nt(left, right):
    return lax.dot_general(left, right, NT, preferred_element_type=F32)


def sigmoid(values):
    return 0.5 * jnp.tanh(0.5 * values) + 0.5


def cost(microseconds):
    return pl.CostEstimate(
        flops=int(microseconds * 1e9), bytes_accessed=int(microseconds * 1e6), transcendentals=0
    )


def params(*semantics):
    return pltpu.CompilerParams(
        dimension_semantics=semantics or None, vmem_limit_bytes=VMEM_LIMIT
    )


def standardise_kernel(first_ref, second_ref, out_ref):
    seqs, residues, lanes = first_ref.shape
    cuts, height, _ = out_ref.shape
    own = (height - 16) // seqs
    first_rows = first_ref.reshape(seqs * residues, lanes)
    second_rows = second_ref.reshape(seqs * residues, lanes)
    lane = lax.broadcasted_iota(jnp.int32, (seqs, 128), 1)
    for cut in range(cuts):
        spreads = jnp.zeros((seqs, 128), F32)
        for n in range(own):
            rows = pl.ds(cut * own + n, seqs, stride=residues)
            column = jnp.concatenate([first_rows[rows, :], second_rows[rows, :]], axis=1)
            centred = column - jnp.mean(column, axis=1, keepdims=True)
            variance = jnp.mean(centred * centred, axis=1, keepdims=True) + EPS
            scale = lax.rsqrt(variance)
            out_ref[cut, n * seqs : (n + 1) * seqs, :] = (centred * scale).astype(BF16)
            spreads = jnp.where(lane == n, variance * scale, spreads)
        spreads = spreads.T[:8, :]
        coarse = spreads.astype(BF16).astype(F32)
        kept = jnp.concatenate([coarse, spreads - coarse], axis=0)
        kept = jnp.concatenate([kept, jnp.zeros((16, 2 * lanes - seqs), F32)], axis=1)
        out_ref[cut, own * seqs :, :] = kept.astype(BF16)


def standardise(block, cuts):
    seqs, residues, depth = block.shape
    half = depth // 2
    own = residues // cuts
    height = own * seqs + 16
    return pl.pallas_call(
        standardise_kernel,
        grid=(residues // 8,),
        in_specs=[
            pl.BlockSpec((seqs, 8, half), lambda g: (0, g, 0)),
            pl.BlockSpec((seqs, 8, half), lambda g: (0, g, 1)),
        ],
        out_specs=pl.BlockSpec((8 // own, height, depth), lambda g: (g, 0, 0)),
        out_shape=jax.ShapeDtypeStruct((cuts, height, depth), BF16),
        compiler_params=params("arbitrary"),
        cost_estimate=cost(3),
        name="standardise",
    )(block, block)


def attention_kernel(
    normed_ref, key_ref, others_ref, gated_ref, turned_ref, scores_ref, weights_ref
):
    blocks, residues, seqs, _ = gated_ref.shape
    depth = normed_ref.shape[2]
    total = blocks * seqs
    inner = ATTENTION_UNITS * UNIT_WIDTH
    ring = scores_ref.shape[0]
    columns = []
    for n in range(residues):
        column = normed_ref[:, n * seqs : (n + 1) * seqs, :].reshape(total, depth)
        key_rows = matmul(column, key_ref[...]).astype(BF16)
        projected = matmul_nt(others_ref[...], column)
        queries = (projected[:inner] * UNIT_WIDTH ** (-0.5)).astype(BF16)
        value_rows = projected[inner : 2 * inner].astype(BF16)
        gates = sigmoid(projected[2 * inner :])
        columns.append((key_rows, queries, value_rows, gates))
    units = [(n, h) for h in range(ATTENTION_UNITS) for n in range(residues)]

    def score(unit):
        n, h = units[unit]
        key_rows, queries, _, _ = columns[n]
        low, high = h * UNIT_WIDTH, (h + 1) * UNIT_WIDTH
        pieces = [queries[low:high]]
        if low > 0:
            pieces.insert(0, jnp.zeros((low, total), BF16))
        if high < inner:
            pieces.append(jnp.zeros((inner - high, total), BF16))
        scores_ref[unit % ring] = matmul(key_rows, jnp.concatenate(pieces, axis=0))

    def weigh(unit):
        for low in range(0, total, 128):
            scores = scores_ref[unit % ring, :, low : low + 128]
            weights = jnp.exp(scores - jnp.max(scores, axis=0, keepdims=True))
            scale = 1.0 / jnp.sum(weights, axis=0, keepdims=True)
            weights_ref[unit % ring, :, low : low + 128] = (weights * scale).astype(BF16)

    def attend(unit):
        n, h = units[unit]
        _, _, value_rows, gates = columns[n]
        rows = slice(h * UNIT_WIDTH, (h + 1) * UNIT_WIDTH)
        attended = matmul(value_rows[rows], weights_ref[unit % ring]) * gates[rows]
        turned_ref[n, rows, :] = attended.astype(BF16)

    for step in range(len(units) + 2):
        if step < len(units):
            score(step)
        if 1 <= step <= len(units):
            weigh(step - 1)
        if step >= 2:
            attend(step - 2)
    for n in range(residues):
        gated_ref[:, n] = turned_ref[n].T.reshape(blocks, seqs, inner)


def attention(normed, key_matrix, other_matrices, residues):
    blocks, height, depth = normed.shape
    seqs = (height - 16) // residues
    total = blocks * seqs
    inner = ATTENTION_UNITS * UNIT_WIDTH
    step = 4
    return pl.pallas_call(
        attention_kernel,
        grid=(residues // step,),
        in_specs=[
            pl.BlockSpec((blocks, step * seqs, depth), lambda n: (0, n, 0)),
            pl.BlockSpec((depth, inner), lambda n: (0, 0)),
            pl.BlockSpec((3 * inner, depth), lambda n: (0, 0)),
        ],
        out_specs=[
            pl.BlockSpec((blocks, step, seqs, inner), lambda n: (0, n, 0, 0)),
            pl.BlockSpec((step, inner, total), lambda n: (n, 0, 0)),
        ],
        out_shape=[
            jax.ShapeDtypeStruct((blocks, residues, seqs, inner), BF16),
            jax.ShapeDtypeStruct((residues, inner, total), BF16),
        ],
        scratch_shapes=[
            pltpu.VMEM((4, total, total), F32),
            pltpu.VMEM((4, total, total), BF16),
        ],
        compiler_params=params("arbitrary"),
        cost_estimate=cost(10),
        name="attention",
    )(normed, key_matrix, other_matrices)


def alignment_kernel(
    normed_ref, spread_ref, turned_ref, final_ref, entry_ref, left_ref, right_ref, rows_ref
):
    blocks, _, depth = normed_ref.shape
    residues, _, total = turned_ref.shape
    seqs = total // blocks
    features = TENSOR_FEATURES
    step = pl.program_id(0)
    for n in range(residues):
        column = normed_ref[:, n * seqs : (n + 1) * seqs, :].reshape(total, depth)
        spreads = []
        for block in range(blocks):
            kept = spread_ref[block, :, :seqs].astype(F32)
            row = lax.broadcasted_iota(jnp.int32, kept.shape, 0)
            chosen = lax.rem(row, 8) == step * residues + n
            spreads.append(jnp.sum(jnp.where(chosen, kept, 0.0), axis=0, keepdims=True))
        spread = jnp.concatenate(spreads, axis=1)
        updated = column.T.astype(F32) * spread + matmul(final_ref[...], turned_ref[n])
        centred = updated - jnp.mean(updated, axis=0, keepdims=True)
        variance = jnp.mean(centred * centred, axis=0, keepdims=True)
        normed = (centred * lax.rsqrt(variance + EPS)).astype(BF16)
        projected = matmul(entry_ref[...], normed)
        right_ref[n] = projected[features:].astype(BF16)
        first = pl.multiple_of((step * residues + n) * features, features)
        for tile in range(total // 128):
            rows_ref[tile, pl.ds(first, features), :] = projected[
                :features, tile * 128 : (tile + 1) * 128
            ]

    @pl.when(step == pl.num_programs(0) - 1)
    def _():
        count = rows_ref.shape[1] // features
        together = max(1, 16 // count)
        for c in range(0, features, together):
            pieces = []
            for e in range(together):
                chosen = pl.ds(c + e, count, stride=features)
                tiles = [rows_ref[tile, chosen, :] for tile in range(total // 128)]
                pieces.append(jnp.concatenate(tiles, axis=1))
            piece = jnp.concatenate(pieces, axis=0).astype(BF16)
            left_ref[c * count : (c + together) * count, :] = piece


def alignment(normed, turned, final_matrix, entry_matrices):
    blocks, height, depth = normed.shape
    residues, _, total = turned.shape
    seqs = total // blocks
    features = TENSOR_FEATURES
    step = 4
    return pl.pallas_call(
        alignment_kernel,
        grid=(residues // step,),
        in_specs=[
            pl.BlockSpec((blocks, step * seqs, depth), lambda n: (0, n, 0)),
            pl.BlockSpec((blocks, 16, depth), lambda n: (0, height // 16 - 1, 0)),
            pl.BlockSpec((step, depth, total), lambda n: (n, 0, 0)),
            pl.BlockSpec(final_matrix.shape, lambda n: (0, 0)),
            pl.BlockSpec(entry_matrices.shape, lambda n: (0, 0)),
        ],
        out_specs=[
            pl.BlockSpec((features * residues, total), lambda n: (0, 0)),
            pl.BlockSpec((step, features, total), lambda n: (n, 0, 0)),
        ],
        out_shape=[
            jax.ShapeDtypeStruct((features * residues, total), BF16),
            jax.ShapeDtypeStruct((residues, features, total), BF16),
        ],
        scratch_shapes=[pltpu.VMEM((total // 128, residues * features, 128), F32)],
        compiler_params=params("arbitrary"),
        cost_estimate=cost(4),
        name="alignment",
    )(normed, normed, turned, final_matrix, entry_matrices)


def pair_kernel(
    left_slots_ref,
    right_firsts_ref,
    own_ref,
    other_ref,
    *rest,
):
    weights_ref, entry_ref, switch_ref, couplings_hbm, mid_hbm, gate_hbm, sides_hbm = rest[-16:-9]
    outer_ref, spread_ref, sum_ref, rows_ref, couplings_ref = rest[-9:-4]
    mid_ref, gate_ref, sides_ref, copied = rest[-4:]
    right_refs = rest[:-16]
    fetched = pltpu.make_async_copy(couplings_hbm, couplings_ref, copied.at[0])
    fetched.start()
    copies = []

    def send(source, target):
        copies.append(pltpu.make_async_copy(source, target, copied.at[len(copies) + 1]))
        copies[-1].start()

    features = TENSOR_FEATURES
    slots, piece_rows, total = own_ref.shape
    residues = piece_rows // features
    rows = 2 * slots * residues
    share = right_refs[0].shape[0]
    columns = len(right_refs) * share
    groups = columns // GROUP
    wide = share * features
    together = spread_ref.shape[1] // 128

    for half, left_ref in enumerate((own_ref, other_ref)):
        piece = left_ref[...].reshape(slots * piece_rows, total)
        target = slice(half * slots * piece_rows, (half + 1) * slots * piece_rows)
        for p, right_ref in enumerate(right_refs):
            right = right_ref[...].reshape(wide, total)
            outer_ref[target, p * wide : (p + 1) * wide] = matmul_nt(piece, right) * (1.0 / total)

    spread_ref[...] = jnp.zeros_like(spread_ref)

    def channel_step(p, carry):
        slot = lax.rem(p, 2)
        for e in range(together):
            source = pl.multiple_of((p * together + e) * features, features)
            piece = weights_ref[pl.ds(source, features), :]
            for place in range(GROUP):
                low = e * 128 + place * features
                spread_ref[slot, low : low + features, place * C_Z : (place + 1) * C_Z] = piece
        pieces = []
        for g in range(groups):
            parts = []
            for e in range(together):
                channel = []
                for slot_number in range(2 * slots):
                    first = slot_number * piece_rows + (p * together + e) * residues
                    source = pl.ds(pl.multiple_of(first, residues), residues)
                    channel.append(outer_ref[source, g * 128 : (g + 1) * 128])
                parts.append(jnp.concatenate(channel, axis=0).astype(BF16))
            pieces.append(jnp.concatenate(parts, axis=1))
        update = matmul(jnp.concatenate(pieces, axis=0), spread_ref[slot])

        @pl.when(p == 0)
        def _():
            sum_ref[...] = update

        @pl.when(p > 0)
        def _():
            sum_ref[...] += update

        return carry

    lax.fori_loop(0, features // together, channel_step, 0)

    left_firsts = [left_slots_ref[j] * residues for j in range(2 * slots)]
    right_firsts = [right_firsts_ref[p] for p in range(len(right_refs))]
    fetched.wait()
    for g in range(groups):
        normed, places = [], []
        for place in range(GROUP):
            p, n = divmod(g * GROUP + place, share)
            b = right_firsts[p] + n
            places.append(b)
            lanes = slice(place * C_Z, (place + 1) * C_Z)
            pieces = []
            for first in left_firsts:
                source = pl.ds(pl.multiple_of(g * rows + first, residues), residues)
                pieces.append(sum_ref[source, lanes])
            mid = jnp.concatenate(pieces, axis=0)
            mid = mid + couplings_ref[pl.ds(b, rows, stride=columns), :]
            mid_ref[g * GROUP + place] = mid
            centred = mid - jnp.mean(mid, axis=1, keepdims=True)
            variance = jnp.mean(centred * centred, axis=1, keepdims=True)
            normed.append((centred * lax.rsqrt(variance + EPS)).astype(BF16))
        gates = sigmoid(matmul(jnp.concatenate(normed, axis=0), switch_ref[...]))
        blank = jnp.zeros_like(normed[0])
        for place in range(0, GROUP, 2):
            twice = []
            for e in range(2):
                part = gates[(place + e) * rows : (place + e + 1) * rows]
                gate_ref[g * GROUP + place + e] = part
                twice.append(jnp.concatenate([normed[place + e], blank], axis=1))
                twice.append(jnp.concatenate([blank, normed[place + e]], axis=1))
            sides = matmul_nt(entry_ref[...], jnp.concatenate(twice, axis=0))
            sides = sigmoid(sides[C_TRI:]) * sides[:C_TRI]
            for e in range(2):
                first = pl.multiple_of(places[place + e] * C_TRI, C_TRI)
                rows_ref[pl.ds(first, C_TRI), :] = sides[:, e * 2 * rows : (e + 1) * 2 * rows]

        if (g + 1) * GROUP % share == 0:
            p = (g + 1) * GROUP // share - 1
            source, target = pl.ds(p * share, share), pl.ds(right_firsts[p], share)
            send(mid_ref.at[source], mid_hbm.at[target])
            send(gate_ref.at[source], gate_hbm.at[target])

    cut = C_TRI // 4
    for part in range(4):

        def turn_step(c, carry):
            sides_ref[c] = rows_ref[pl.ds(c, columns, stride=C_TRI), :].astype(BF16)
            return carry

        lax.fori_loop(part * cut, (part + 1) * cut, turn_step, 0, unroll=8)
        chosen = pl.ds(part * cut, cut)
        send(sides_ref.at[chosen], sides_hbm.at[chosen])
    for copy in copies:
        copy.wait()


def pair_update(left_slots, right_firsts, left, rights, weights, couplings, entry, switch):
    rows, columns, depth = couplings.shape
    whole = jax.ShapeDtypeStruct((columns, rows, depth), F32)
    sides = jax.ShapeDtypeStruct((C_TRI, columns, 2 * rows), BF16)
    smem = pl.BlockSpec(memory_space=pltpu.SMEM)
    vmem = pl.BlockSpec(memory_space=pltpu.VMEM)
    anywhere = pl.BlockSpec(memory_space=pl.ANY)
    return pl.pallas_call(
        pair_kernel,
        in_specs=[smem] * 2 + [vmem] * (5 + len(rights)) + [anywhere],
        out_specs=[anywhere] * 3,
        out_shape=[whole, whole, sides],
        scratch_shapes=[
            pltpu.VMEM((rows * TENSOR_FEATURES, columns * TENSOR_FEATURES), F32),
            pltpu.VMEM((2, 8 * 128, GROUP * depth), BF16),
            pltpu.VMEM((columns // GROUP * rows, GROUP * depth), F32),
            pltpu.VMEM((columns * C_TRI, 2 * rows), F32),
            pltpu.VMEM((rows * columns, depth), F32),
            pltpu.VMEM(whole.shape, F32),
            pltpu.VMEM(whole.shape, F32),
            pltpu.VMEM(sides.shape, BF16),
            pltpu.SemaphoreType.DMA((2 * len(rights) + 5,)),
        ],
        compiler_params=params(),
        cost_estimate=cost(12),
        name="pair_update",
    )(
        left_slots,
        right_firsts,
        *left,
        *rights,
        weights,
        entry,
        switch,
        couplings.reshape(rows * columns, depth),
    )


def product_kernel(sides_ref, out_ref, *, grid_rows, grid_columns):
    channels, part, lanes = sides_ref.shape[1:]
    half = lanes // 2
    lane = lax.broadcasted_iota(jnp.int32, (grid_columns * part, lanes), 1)
    front = lane < half
    cut = front[: part // 2]
    for channel in range(channels):
        lefts, rights = [], []
        for r in range(0, grid_rows, 2):
            even, odd = [
                jnp.concatenate(
                    [sides_ref[(r + e) * grid_columns + c, channel] for c in range(grid_columns)],
                    axis=0,
                )
                for e in range(2)
            ]
            lefts.append(jnp.where(front, even, pltpu.roll(odd, half, 1)))
            rights.append(jnp.where(front, pltpu.roll(even, half, 1), odd))
        product = matmul_nt(jnp.concatenate(rights, axis=1), jnp.concatenate(lefts, axis=1))
        product = product.astype(BF16)
        for c in range(grid_columns):
            for r in range(0, grid_rows, 2):
                block = product[c * part : (c + 1) * part, r * half : (r + 2) * half]
                top, bottom = block[: part // 2], block[part // 2 :]
                even = jnp.where(cut, top, pltpu.roll(bottom, half, 1))
                out_ref[r * grid_columns + c, channel] = even
                odd = jnp.where(cut, pltpu.roll(top, half, 1), bottom)
                out_ref[(r + 1) * grid_columns + c, channel] = odd


def triangle_product(sides, grid_rows, grid_columns):
    devices, channels, part, lanes = sides.shape
    step = 2 if channels % 2 == 0 else 1
    return pl.pallas_call(
        functools.partial(product_kernel, grid_rows=grid_rows, grid_columns=grid_columns),
        grid=(channels // step,),
        in_specs=[pl.BlockSpec((devices, step, part, lanes), lambda c: (0, c, 0, 0))],
        out_specs=pl.BlockSpec((devices, step, part // 2, lanes), lambda c: (0, c, 0, 0)),
        out_shape=jax.ShapeDtypeStruct((devices, channels, part // 2, lanes), BF16),
        compiler_params=params("arbitrary"),
        cost_estimate=cost(3),
        name="triangle_product",
    )(sides)


def output_kernel(product_ref, mid_ref, gate_ref, final_ref, out_ref, wide_ref):
    channels, part, lanes = product_ref.shape
    _, own, rows, depth = mid_ref.shape
    out_rows = out_ref.reshape(rows * 2 * own, depth)
    step = pl.program_id(0)

    @pl.when(step == 0)
    def _():
        wide_ref[...] = product_ref[...].astype(F32).reshape(channels * part, lanes)

    for j in range(own):
        product = wide_ref[pl.ds(step * own + j, channels, stride=part), :]
        centred = product - jnp.mean(product, axis=0, keepdims=True)
        variance = jnp.mean(centred * centred, axis=0, keepdims=True)
        normed = (centred * lax.rsqrt(variance + EPS)).astype(BF16).T
        update = matmul(normed, final_ref[...])
        for half in range(2):
            piece = update[half * rows : (half + 1) * rows]
            piece = mid_ref[half, j] + gate_ref[half, j] * piece
            out_rows[pl.ds(half * own + j, rows, stride=2 * own), :] = piece


def pair_result(product, mid, gate, final_matrix):
    channels, part, lanes = product.shape
    columns, rows, depth = mid.shape
    own = 8
    whole = pl.BlockSpec((2, own, rows, depth), lambda j: (0, j, 0, 0))
    out = pl.pallas_call(
        output_kernel,
        grid=(part // own,),
        in_specs=[
            pl.BlockSpec(product.shape, lambda j: (0, 0, 0)),
            whole,
            whole,
            pl.BlockSpec(final_matrix.shape, lambda j: (0, 0)),
        ],
        out_specs=pl.BlockSpec((rows, 2, own, depth), lambda j: (0, 0, j, 0)),
        out_shape=jax.ShapeDtypeStruct((rows, 2, part, depth), F32),
        scratch_shapes=[pltpu.VMEM((channels * part, lanes), F32)],
        compiler_params=params("arbitrary"),
        cost_estimate=cost(4),
        name="pair_result",
    )(
        product,
        mid.reshape(2, part, rows, depth),
        gate.reshape(2, part, rows, depth),
        final_matrix,
    )
    return out.reshape(rows, columns, depth)


def swap_cores(block):
    count = lax.axis_size("col")
    return lax.ppermute(block, "col", [(c, c ^ 1) for c in range(count)])


def gather_turned(block):
    rows, columns = lax.axis_size("row"), lax.axis_size("col")
    arrived = []
    for shift in range(rows):
        moves = []
        for r in range(rows):
            for q in range(rows):
                for side in range(2):
                    source = r * columns + 2 * q + side
                    moves.append((source, q * columns + 2 * ((r + shift) % rows) + side))
        arrived.append(lax.ppermute(block, ("row", "col"), moves))
    return jnp.stack(arrived)


def both_cores(own):
    rows = lax.axis_size("row")
    me, core = lax.axis_index("col") // 2, lax.rem(lax.axis_index("col"), 2)
    other = swap_cores(own)
    shifts = lax.rem(me - jnp.arange(rows, dtype=jnp.int32) + rows, rows)
    residues = own.shape[1] // TENSOR_FEATURES
    if residues % 8 == 0:
        return (own, other), jnp.concatenate([shifts + core * rows, shifts + (1 - core) * rows])
    own, other = jnp.take(own, shifts, axis=0), jnp.take(other, shifts, axis=0)
    joined = 8 // residues
    ordered = []
    for side in (jnp.where(core == 0, own, other), jnp.where(core == 0, other, own)):
        side = side.reshape(rows // joined, joined, TENSOR_FEATURES, residues, -1)
        side = jnp.transpose(side, (0, 2, 1, 3, 4))
        ordered.append(side.reshape(rows // joined, joined * own.shape[1], -1))
    return tuple(ordered), jnp.arange(2 * rows // joined, dtype=jnp.int32)


def exchange_rows(pieces):
    rows = lax.axis_size("row")
    arrived = [pieces[0]]
    for shift in range(1, rows):
        moves = [(r, r ^ shift) for r in range(rows)]
        arrived.append(lax.ppermute(pieces[shift], "row", moves))
    return arrived, lax.axis_index("row") ^ jnp.arange(rows, dtype=jnp.int32)


def paired_entries(matrices):
    turned = matrices.reshape(C_Z, 2, 2, C_TRI)
    return jnp.transpose(turned, (2, 3, 1, 0)).reshape(2 * C_TRI, 2 * C_Z)


def body(
    homolog_tensor,
    couplings,
    attention_probe_matrix,
    attention_extra_matrices,
    attention_final_matrix,
    tensor_entry_matrices,
    tensor_final_matrix,
    incoming_entry_matrices,
    incoming_switch_matrix,
    incoming_final_matrix,
):
    inner = ATTENTION_UNITS * UNIT_WIDTH
    row_count = lax.axis_size("row")
    seqs, residues, depth = homolog_tensor.shape
    own_residues = residues // row_count
    normed = standardise(homolog_tensor, row_count)
    normed = lax.all_to_all(normed, "row", split_axis=0, concat_axis=0)
    others = jnp.concatenate(
        [attention_probe_matrix.T, attention_extra_matrices[:, inner:].T], axis=0
    )
    gated, turned = attention(
        normed, attention_extra_matrices[:, :inner], others, own_residues
    )
    left_piece, right_piece = alignment(
        normed, turned, attention_final_matrix.T, tensor_entry_matrices.T
    )

    rights, sources = exchange_rows([right_piece] * row_count)
    own = gather_turned(left_piece)
    own, rights, gated = lax.optimization_barrier((own, rights, gated))
    gated = lax.all_to_all(gated, "row", split_axis=0, concat_axis=0)
    left, left_slots = both_cores(own)
    mid, gate, sides = pair_update(
        left_slots,
        sources * own_residues,
        left,
        rights,
        tensor_final_matrix,
        couplings,
        paired_entries(incoming_entry_matrices),
        incoming_switch_matrix,
    )
    gated, sides = lax.optimization_barrier((gated, sides))
    gated = jnp.transpose(gated.reshape(residues, seqs, inner), (1, 0, 2))
    change = jnp.dot(
        gated.reshape(-1, inner), attention_final_matrix, preferred_element_type=F32
    )
    refreshed_homologs = homolog_tensor + change.reshape(homolog_tensor.shape)

    everywhere = ("row", "col")
    column_count = lax.axis_size("col")
    devices = row_count * column_count
    sides = sides.reshape(devices, C_TRI // devices, *sides.shape[1:])
    sides = lax.all_to_all(sides, everywhere, split_axis=0, concat_axis=0)
    product = triangle_product(sides, row_count, column_count)
    product = lax.all_to_all(product, everywhere, split_axis=0, concat_axis=0)
    product = product.reshape(C_TRI, *product.shape[2:])
    pair_output = pair_result(product, mid, gate, incoming_final_matrix)
    return (refreshed_homologs, pair_output)


def solution(mesh):
    in_specs = (
        P("row", "col", None),
        P("row", "col", None),
        P(),
        P(),
        P(),
        P(),
        P(),
        P(),
        P(),
        P(),
    )
    out_specs = (P("row", "col", None), P("row", "col", None))
    return jax.shard_map(body, mesh=mesh, in_specs=in_specs, out_specs=out_specs, check_vma=False)
```

time: 172 us -> 142 us (0.83)
  blocking collectives: 0 us -> 32.9 us
  local copies, waits for them, and re-layouts: 35.6 us -> 4.27 us
  waiting for transfers between devices: 50.8 us -> 37.3 us
  starting transfers between devices: 36.7 us -> 24.6 us
  between operations: 8.59 us -> 0.79 us
  Pallas kernels: 31.9 us -> 37.3 us
    all_to_all x0 -> x1, blocking collectives: none -> 32.9 us  [body(): sides = lax.all_to_all(sides, everywhere, split_axis=0, concat_axis=0)]
    unnamed x64 -> x26, local copies, waits for them, and re-layouts: 25.8 us -> 3.43 us
    all_to_all x3 -> x2, waiting for transfers between devices: 30.9 us -> 15.8 us  [the longest x1 11.5 us: body(): normed = lax.all_to_all(normed, 'row', split_axis=0, concat_axis=0)]
    all_to_all x1, waiting for transfers between devices: 0.01 us -> 14.1 us  [body(): product = lax.all_to_all(product, everywhere, split_axis=0, concat_axis=0)]
    ppermute x6 -> x3, waiting for transfers between devices: 15.1 us -> 7.4 us  [exchange_rows(): arrived.append(lax.ppermute(pieces[shift], 'row', moves))]
    ppermute x4, waiting for transfers between devices: 4.83 us -> 0.01 us  [gather_turned(): arrived.append(lax.ppermute(block, ('row', 'col'), moves))]
    pallas_call x6 -> x5, Pallas kernels: 29.9 us -> 34.6 us  [the longest x1 11.8 us: attention(): pl.pallas_call(attention_kernel, grid=(residues // step,), in_specs=[pl.B...]
    ppermute x6 -> x3, starting transfers between devices: 9.83 us -> 5.47 us  [exchange_rows(): arrived.append(lax.ppermute(pieces[shift], 'row', moves))]
  transfers between devices with their start and end apart: 15 -> 11, of which waited for: 10 -> 5; matrix products, arithmetic and copies ran while one was open for 12% -> 5% of each run, Pallas kernels for 7% -> 7%
where the time goes in v5:
time: 142 us; the launch traced here: 141 us
  Pallas kernels  37.3 us (26%)
  waiting for transfers between devices  37.3 us (26%)
  blocking collectives  32.9 us (23%)
  starting transfers between devices  24.6 us (17%)
  local copies, waits for them, and re-layouts  4.27 us (3%)
  matrix products  2.19 us (2%)
  other arithmetic  1.98 us (1%)
    all_to_all x1, blocking collectives, body(): sides = lax.all_to_all(sides, everywhere, split_axis=0, concat_axis=0)  32.9 us
    all_to_all x1, waiting for transfers between devices, body(): product = lax.all_to_all(product, everywhere, split_axis=0, concat_axis=0)  14.1 us
    pallas_call x1, Pallas kernels, attention(): pl.pallas_call(attention_kernel, grid=(residues // step,), in_specs=[pl.B...  11.8 us
    all_to_all x1, waiting for transfers between devices, body(): normed = lax.all_to_all(normed, 'row', split_axis=0, concat_axis=0)  11.5 us
    pallas_call x1, Pallas kernels, pair_update(): pl.pallas_call(pair_kernel, in_specs=[smem] * 2 + [vmem] * (5 + len(right...  10.1 us
    ppermute x3, waiting for transfers between devices, exchange_rows(): arrived.append(lax.ppermute(pieces[shift], 'row', moves))  7.4 us
    ppermute x4, starting transfers between devices, gather_turned(): arrived.append(lax.ppermute(block, ('row', 'col'), moves))  6.84 us
    ppermute x3, starting transfers between devices, exchange_rows(): arrived.append(lax.ppermute(pieces[shift], 'row', moves))  5.47 us
  transfers between devices with their start and end apart: 11, of which 5 were waited for; matrix products, arithmetic and copies ran while one was open for 5% of the time, Pallas kernels for 7%

profile of v5, /device:TPU:0, one launch (start us, length us, event | category | flops | bytes accessed | tf_op | source)
XLA Modules:
  0.0 141.4 jit_solution(5710182071286634405)
XLA Ops:
  0.6 4.2 %standardise.1 = bf16[4,528,256]{2,1,0:T(8,128)(2,1)} custom-call(f32[64,32,256]{2,1,0:T(8,128)} %second_ref.1, f32[64,32,256]{2,1,0:T(8,128)} %second_ref.1), custom_call_target="tpu_custom_call" | custom-call | flops 3000000000 | bytes 3000000 | tf_op jit(solution)/shard_map/standardise/pallas_call | solution.py:77
  4.8 0.0 copy-start.2
  4.8 0.0 copy-start.5
  4.8 0.0 copy-start.4
  4.8 0.0 slice-start
  4.8 5.3 %all-to-all-start = ((bf16[4,528,256]{2,1,0:T(8,128)(2,1)}), bf16[4,528,256]{2,1,0:T(8,128)(2,1)S(1)}, u32[]{:S(2)}, u32[]{:S(2)}) async-start(bf16[4,528,256]{2,1,0:T(8,128)(2,1)} %standardise.1), calls=%async_computation | async-start | bytes 2162688 | tf_op jit(solution)/shard_map/all_to_all | solution.py:581
  10.1 0.0 copy-done.2
  10.1 0.7 slice.6.key_ref
  10.8 0.0 copy-done.5
  10.8 0.1 copy.12
  10.9 0.0 copy-done.4
  10.9 0.8 copy.14
  11.7 0.0 slice-done
  11.7 0.1 copy.17
  11.8 0.8 pad_maximum_fusion.1.others_ref
  12.6 11.5 %all-to-all-done.normed_ref.spread_ref = bf16[4,528,256]{2,1,0:T(8,128)(2,1)S(1)} async-done(((bf16[4,528,256]{2,1,0:T(8,128)(2,1)}), bf16[4,528,256]{2,1,0:T(8,128)(2,1)S(1)}, u32[]{:S(2)}, u32[]{:S(2)}) %all-to-all-start) | async-done | bytes 1081376 | tf_op jit(solution)/shard_map/all_to_all | solution.py:581
  24.1 0.0 copy-start.1
  24.1 1.0 copy-done.1
  25.1 11.8 %attention.1 = (bf16[4,8,64,256]{3,2,1,0:T(8,128)(2,1)}, bf16[8,256,256]{2,1,0:T(8,128)(2,1)}) custom-call(bf16[4,528,256]{2,1,0:T(8,128)(2,1)} %copy-done.1, bf16[256,256]{1,0:T(8,128)(2,1)} %slice.6.key_ref, bf16[768,256]{1,0:T(8,128)(2,1)} %pad_maximum_fusion.1.others_ref), custom_call_target="tpu_custom_call" | custom-call | flops 10000000000 | bytes 10000000 | tf_op jit(solution)/shard_map/attention/pallas_call | solution.py:153
  36.9 0.0 copy-start.6
  36.9 5.0 %alignment.1 = (bf16[256,256]{1,0:T(8,128)(2,1)}, bf16[8,32,256]{2,1,0:T(8,128)(2,1)}) custom-call(bf16[4,528,256]{2,1,0:T(8,128)(2,1)} %copy-done.1, bf16[4,528,256]{2,1,0:T(8,128)(2,1)} %copy-done.1, bf16[8,256,256]{2,1,0:T(8,128)(2,1)} %get-tuple-element.17.turned_ref, bf16[256,256]{1,0:T(8,128)(2,1)} %bitcast.33, bf16[64,256]{1,0:T(8,128)(2,1)} %bitcast.39), custom_call_target="tpu_custom_call" | custom-call | flops 4000000000 | bytes 4000000 | tf_op jit(solution)/shard_map/alignment/pallas_call | solution.py:228
  41.9 3.7 %collective-permute-start.3 = (bf16[256,256]{1,0:T(8,128)(2,1)}, bf16[256,256]{1,0:T(8,128)(2,1)S(1)}, u32[]{:S(2)}, u32[]{:S(2)}) collective-permute-start(bf16[256,256]{1,0:T(8,128)(2,1)} %get-tuple-element.18), channel_id=1, source_target_pairs={{0,6},{1,7},{2,14},{3,15},{4,22},{5,23},{6,30},{7,31},{8,0},{9,1},... | collective-permute-start | bytes 393224 | tf_op jit(solution)/shard_map/ppermute | solution.py:528
  45.5 1.5 %collective-permute-start.2 = (bf16[256,256]{1,0:T(8,128)(2,1)}, bf16[256,256]{1,0:T(8,128)(2,1)S(1)}, u32[]{:S(2)}, u32[]{:S(2)}) collective-permute-start(bf16[256,256]{1,0:T(8,128)(2,1)} %get-tuple-element.18), channel_id=1, source_target_pairs={{0,4},{1,5},{2,12},{3,13},{4,20},{5,21},{6,28},{7,29},{8,6},{9,7},... | collective-permute-start | bytes 393224 | tf_op jit(solution)/shard_map/ppermute | solution.py:528
  47.0 0.2 collective-permute-start.1
  47.2 1.6 %collective-permute-start = (bf16[256,256]{1,0:T(8,128)(2,1)}, bf16[256,256]{1,0:T(8,128)(2,1)S(1)}, u32[]{:S(2)}, u32[]{:S(2)}) collective-permute-start(bf16[256,256]{1,0:T(8,128)(2,1)} %get-tuple-element.18), channel_id=1, source_target_pairs={{0,0},{1,1},{2,8},{3,9},{4,16},{5,17},{6,24},{7,25},{8,2},{9,3},{1... | collective-permute-start | bytes 393224 | tf_op jit(solution)/shard_map/ppermute | solution.py:528
  48.7 4.8 %collective-permute-start.6 = (bf16[8,32,256]{2,1,0:T(8,128)(2,1)}, bf16[8,32,256]{2,1,0:T(8,128)(2,1)S(1)}, u32[]{:S(2)}, u32[]{:S(2)}) collective-permute-start(bf16[8,32,256]{2,1,0:T(8,128)(2,1)} %get-tuple-element.23.rest_0_), channel_id=1, source_target_pairs={{0,24},{8,16},{16,8},{24,0},{1,25},{9,17},{17,9},{25,1},{2,26},{10... | collective-permute-start | bytes 393224 | tf_op jit(solution)/shard_map/ppermute | solution.py:555
  53.6 0.0 collective-permute-done.3
  53.6 0.0 collective-permute-start.5
  53.6 0.0 collective-permute-done.2
  53.6 0.6 collective-permute-start.4
  54.2 0.0 collective-permute-done.1
  54.2 0.0 collective-permute-done
  54.2 0.1 pad_maximum_fusion.own_ref
  54.3 0.0 copy-start.3
  54.3 6.0 %collective-permute-done.6.rest_3_ = bf16[8,32,256]{2,1,0:T(8,128)(2,1)S(1)} collective-permute-done((bf16[8,32,256]{2,1,0:T(8,128)(2,1)}, bf16[8,32,256]{2,1,0:T(8,128)(2,1)S(1)}, u32[]{:S(2)}, u32[]{:S(2)}) %collective-permute-start.6) | collective-permute-done | bytes 131104 | tf_op jit(solution)/shard_map/ppermute | solution.py:555
  60.3 0.0 copy-start.8
  60.3 0.0 collective-permute-done.5.rest_2_
  60.3 0.0 copy-start.9
  60.3 1.4 collective-permute-done.4.rest_1_
  61.7 0.0 copy-start.10
  61.7 0.0 collective-permute-start.7
  61.7 0.0 copy-done.6
  61.7 0.1 copy.15
  61.9 0.7 copy.24
  62.5 0.5 xor_multiply_fusion.right_firsts_ref
  63.1 0.6 pad_add_fusion.left_slots_ref
  63.7 3.7 %all-to-all-start.1 = ((bf16[4,8,64,256]{3,2,1,0:T(8,128)(2,1)}), bf16[4,8,64,256]{3,2,1,0:T(8,128)(2,1)S(1)}, u32[]{:S(2)}, u32[]{:S(2)}) async-start(bf16[4,8,64,256]{3,2,1,0:T(8,128)(2,1)} %get-tuple-element.21), calls=%async_computation.1 | async-start | bytes 2097152 | tf_op jit(solution)/shard_map/all_to_all | solution.py:595
  67.4 0.0 collective-permute-done.7.other_ref
  67.4 0.0 copy-start.7
  67.4 0.0 copy-done.3
  67.4 0.0 copy-done.8
  67.4 0.0 copy-done.9
  67.5 0.0 copy-done.10
  67.5 0.7 copy-done.7
  68.2 10.1 %pair_update.1 = (f32[32,64,128]{2,1,0:T(8,128)}, f32[32,64,128]{2,1,0:T(8,128)}, bf16[128,32,128]{2,1,0:T(8,128)(2,1)}) custom-call(s32[8]{0:T(128)} %pad_add_fusion.left_slots_ref, s32[4]{0:T(128)} %xor_multiply_fusion.right_firsts_ref, bf16[4,256,256]{2,1,0:T(8,128)(2,1)} %copy-done.3, bf16[4,256,256]{2,1,0:T(8,128)(2,1)} %copy-done.7, ...), custom_call_target="tpu_custom_call" | custom-call | flops 12000000000 | bytes 12000000 | tf_op jit(solution)/shard_map/pair_update/pallas_call | solution.py:386
  78.3 4.3 %all-to-all-done.1 = bf16[4,8,64,256]{3,2,1,0:T(8,128)(2,1)S(1)} async-done(((bf16[4,8,64,256]{3,2,1,0:T(8,128)(2,1)}), bf16[4,8,64,256]{3,2,1,0:T(8,128)(2,1)S(1)}, u32[]{:S(2)}, u32[]{:S(2)}) %all-to-all-start.1) | async-done | bytes 1048608 | tf_op jit(solution)/shard_map/all_to_all | solution.py:595
  82.6 32.9 %all_to_all.20.sides_ref = bf16[32,4,32,128]{3,2,1,0:T(8,128)(2,1)} all-to-all(bf16[32,4,32,128]{3,2,1,0:T(8,128)(2,1)} %bitcast.29), channel_id=1, replica_groups=mesh['row'=4,'col'=8] {'row','col'}, dimensions={0} | all-to-all | bytes 2097152 | tf_op jit(solution)/shard_map/all_to_all | solution.py:618
  115.5 0.0 copy-start
  115.5 2.8 %triangle_product.1 = bf16[32,4,16,128]{3,2,1,0:T(8,128)(2,1)} custom-call(bf16[32,4,32,128]{3,2,1,0:T(8,128)(2,1)} %all_to_all.20.sides_ref), custom_call_target="tpu_custom_call" | custom-call | flops 3000000000 | bytes 3000000 | tf_op jit(solution)/shard_map/triangle_product/pallas_call | solution.py:450
  118.3 3.3 %all-to-all-start.3 = ((bf16[32,4,16,128]{3,2,1,0:T(8,128)(2,1)}), bf16[32,4,16,128]{3,2,1,0:T(8,128)(2,1)}, u32[]{:S(2)}, u32[]{:S(2)}) async-start(bf16[32,4,16,128]{3,2,1,0:T(8,128)(2,1)} %triangle_product.1), calls=%async_computation.3 | async-start | bytes 1048576 | tf_op jit(solution)/shard_map/all_to_all | solution.py:620
  121.6 0.0 copy-done
  121.6 2.2 %convolution_add_fusion = f32[64,32,256]{2,1,0:T(8,128)} fusion(f32[64,32,256]{2,1,0:T(8,128)S(1)} %copy-done, bf16[32,64,256]{2,1,0:T(8,128)(2,1)S(1)} %bitcast.27, bf16[256,256]{1,0:T(8,128)(2,1)S(1)} %copy-done.4), kind=kOutput, calls=%fused_computation | convolution fusion | flops 268959744 | bytes 5373952 | tf_op jit(solution)/shard_map/dot_general | solution.py:609
  123.8 14.1 %all-to-all-done.3 = bf16[32,4,16,128]{3,2,1,0:T(8,128)(2,1)} async-done(((bf16[32,4,16,128]{3,2,1,0:T(8,128)(2,1)}), bf16[32,4,16,128]{3,2,1,0:T(8,128)(2,1)}, u32[]{:S(2)}, u32[]{:S(2)}) %all-to-all-start.3) | async-done | bytes 524320 | tf_op jit(solution)/shard_map/all_to_all | solution.py:620
  138.0 3.5 %pair_result.1 = f32[64,2,16,128]{3,2,1,0:T(8,128)} custom-call(bf16[128,16,128]{2,1,0:T(8,128)(2,1)} %bitcast.14.product_ref, f32[2,16,64,128]{3,2,1,0:T(8,128)} %bitcast.40, f32[2,16,64,128]{3,2,1,0:T(8,128)} %bitcast.41, bf16[128,128]{1,0:T(8,128)(2,1)} %final_ref.1), custom_call_target="tpu_custom_call" | custom-call | flops 4000000000 | bytes 4000000 | tf_op jit(solution)/shard_map/pair_result/pallas_call | solution.py:489
  (2 shorter events, 0.0 us)
Async XLA Ops:
  4.8 5.3 %copy-start.2 = (bf16[256,768]{1,0:T(8,128)(2,1)S(1)}, bf16[256,768]{1,0:T(8,128)(2,1)}, u32[]{:S(2)}) copy-start(bf16[256,768]{1,0:T(8,128)(2,1)} %param.13) | copy-start | bytes 1179652
  4.8 6.0 %copy-start.5 = (bf16[256,256]{1,0:T(8,128)(2,1)S(1)}, bf16[256,256]{1,0:T(8,128)(2,1)}, u32[]{:S(2)}) copy-start(bf16[256,256]{1,0:T(8,128)(2,1)} %param.12) | copy-start | bytes 393220
  4.8 6.1 %copy-start.4 = (bf16[256,256]{1,0:T(8,128)(2,1)S(1)}, bf16[256,256]{1,0:T(8,128)(2,1)}, u32[]{:S(2)}) copy-start(bf16[256,256]{1,0:T(8,128)(2,1)} %param.14) | copy-start | bytes 393220
  4.8 6.9 %slice-start = ((bf16[256,768]{1,0:T(8,128)(2,1)}), bf16[256,512]{1,0:T(8,128)(2,1)S(1)}, s32[]{:S(2)}) async-start(bf16[256,768]{1,0:T(8,128)(2,1)} %param.13), calls=%async_computation.4 | async-start | bytes 524288 | tf_op jit(solution)/shard_map/slice | solution.py:583
  4.8 19.3 %all-to-all-start = ((bf16[4,528,256]{2,1,0:T(8,128)(2,1)}), bf16[4,528,256]{2,1,0:T(8,128)(2,1)S(1)}, u32[]{:S(2)}, u32[]{:S(2)}) async-start(bf16[4,528,256]{2,1,0:T(8,128)(2,1)} %standardise.1), calls=%async_computation | async-start | bytes 2162688 | tf_op jit(solution)/shard_map/all_to_all | solution.py:581
  24.1 1.0 copy-start.1
  36.9 24.8 %copy-start.6 = (bf16[128,512]{1,0:T(8,128)(2,1)S(1)}, bf16[128,512]{1,0:T(8,128)(2,1)}, u32[]{:S(2)}) copy-start(bf16[128,512]{1,0:T(8,128)(2,1)} %param.17) | copy-start | bytes 393220
  41.9 11.7 %collective-permute-start.3 = (bf16[256,256]{1,0:T(8,128)(2,1)}, bf16[256,256]{1,0:T(8,128)(2,1)S(1)}, u32[]{:S(2)}, u32[]{:S(2)}) collective-permute-start(bf16[256,256]{1,0:T(8,128)(2,1)} %get-tuple-element.18), channel_id=1, source_target_pairs={{0,6},{1,7},{2,14},{3,15},{4,22},{5,23},{6,30},{7,31},{8,0},{9,1},... | collective-permute-start | bytes 393224 | tf_op jit(solution)/shard_map/ppermute | solution.py:528
  45.5 8.0 %collective-permute-start.2 = (bf16[256,256]{1,0:T(8,128)(2,1)}, bf16[256,256]{1,0:T(8,128)(2,1)S(1)}, u32[]{:S(2)}, u32[]{:S(2)}) collective-permute-start(bf16[256,256]{1,0:T(8,128)(2,1)} %get-tuple-element.18), channel_id=1, source_target_pairs={{0,4},{1,5},{2,12},{3,13},{4,20},{5,21},{6,28},{7,29},{8,6},{9,7},... | collective-permute-start | bytes 393224 | tf_op jit(solution)/shard_map/ppermute | solution.py:528
  47.0 7.2 %collective-permute-start.1 = (bf16[256,256]{1,0:T(8,128)(2,1)}, bf16[256,256]{1,0:T(8,128)(2,1)S(1)}, u32[]{:S(2)}, u32[]{:S(2)}) collective-permute-start(bf16[256,256]{1,0:T(8,128)(2,1)} %get-tuple-element.18), channel_id=1, source_target_pairs={{0,2},{1,3},{2,10},{3,11},{4,18},{5,19},{6,26},{7,27},{8,4},{9,5},... | collective-permute-start | bytes 393224 | tf_op jit(solution)/shard_map/ppermute | solution.py:528
  47.2 7.0 %collective-permute-start = (bf16[256,256]{1,0:T(8,128)(2,1)}, bf16[256,256]{1,0:T(8,128)(2,1)S(1)}, u32[]{:S(2)}, u32[]{:S(2)}) collective-permute-start(bf16[256,256]{1,0:T(8,128)(2,1)} %get-tuple-element.18), channel_id=1, source_target_pairs={{0,0},{1,1},{2,8},{3,9},{4,16},{5,17},{6,24},{7,25},{8,2},{9,3},{1... | collective-permute-start | bytes 393224 | tf_op jit(solution)/shard_map/ppermute | solution.py:528
  48.7 11.6 %collective-permute-start.6 = (bf16[8,32,256]{2,1,0:T(8,128)(2,1)}, bf16[8,32,256]{2,1,0:T(8,128)(2,1)S(1)}, u32[]{:S(2)}, u32[]{:S(2)}) collective-permute-start(bf16[8,32,256]{2,1,0:T(8,128)(2,1)} %get-tuple-element.23.rest_0_), channel_id=1, source_target_pairs={{0,24},{8,16},{16,8},{24,0},{1,25},{9,17},{17,9},{25,1},{2,26},{10... | collective-permute-start | bytes 393224 | tf_op jit(solution)/shard_map/ppermute | solution.py:555
  53.6 6.7 %collective-permute-start.5 = (bf16[8,32,256]{2,1,0:T(8,128)(2,1)}, bf16[8,32,256]{2,1,0:T(8,128)(2,1)S(1)}, u32[]{:S(2)}, u32[]{:S(2)}) collective-permute-start(bf16[8,32,256]{2,1,0:T(8,128)(2,1)} %get-tuple-element.23.rest_0_), channel_id=1, source_target_pairs={{0,16},{8,24},{16,0},{24,8},{1,17},{9,25},{17,1},{25,9},{2,18},{10... | collective-permute-start | bytes 393224 | tf_op jit(solution)/shard_map/ppermute | solution.py:555
  53.6 8.1 %collective-permute-start.4 = (bf16[8,32,256]{2,1,0:T(8,128)(2,1)}, bf16[8,32,256]{2,1,0:T(8,128)(2,1)S(1)}, u32[]{:S(2)}, u32[]{:S(2)}) collective-permute-start(bf16[8,32,256]{2,1,0:T(8,128)(2,1)} %get-tuple-element.23.rest_0_), channel_id=1, source_target_pairs={{0,8},{8,0},{16,24},{24,16},{1,9},{9,1},{17,25},{25,17},{2,10},{10... | collective-permute-start | bytes 393224 | tf_op jit(solution)/shard_map/ppermute | solution.py:555
  54.3 13.1 %copy-start.3 = (bf16[4,256,256]{2,1,0:T(8,128)(2,1)}, bf16[4,256,256]{2,1,0:T(8,128)(2,1)S(1)}, u32[]{:S(2)}) copy-start(bf16[4,256,256]{2,1,0:T(8,128)(2,1)S(1)} %pad_maximum_fusion.own_ref) | copy-start | bytes 1572868
  60.3 7.1 %copy-start.8 = (bf16[8,32,256]{2,1,0:T(8,128)(2,1)}, bf16[8,32,256]{2,1,0:T(8,128)(2,1)S(1)}, u32[]{:S(2)}) copy-start(bf16[8,32,256]{2,1,0:T(8,128)(2,1)S(1)} %collective-permute-done.6.rest_3_) | copy-start | bytes 393220
  60.3 7.1 %copy-start.9 = (bf16[8,32,256]{2,1,0:T(8,128)(2,1)}, bf16[8,32,256]{2,1,0:T(8,128)(2,1)S(1)}, u32[]{:S(2)}) copy-start(bf16[8,32,256]{2,1,0:T(8,128)(2,1)S(1)} %collective-permute-done.5.rest_2_) | copy-start | bytes 393220
  61.7 5.8 %copy-start.10 = (bf16[8,32,256]{2,1,0:T(8,128)(2,1)}, bf16[8,32,256]{2,1,0:T(8,128)(2,1)S(1)}, u32[]{:S(2)}) copy-start(bf16[8,32,256]{2,1,0:T(8,128)(2,1)S(1)} %collective-permute-done.4.rest_1_) | copy-start | bytes 393220
  61.7 5.7 %collective-permute-start.7 = (bf16[4,256,256]{2,1,0:T(8,128)(2,1)S(1)}, bf16[4,256,256]{2,1,0:T(8,128)(2,1)S(1)}, u32[]{:S(2)}, u32[]{:S(2)}) collective-permute-start(bf16[4,256,256]{2,1,0:T(8,128)(2,1)S(1)} %pad_maximum_fusion.own_ref), channel_id=1, source_target_pairs={{0,1},{1,0},{2,3},{3,2},{4,5},{5,4},{6,7},{7,6},{8,9},{9,8},{10,11... | collective-permute-start | bytes 1572872 | tf_op jit(solution)/shard_map/ppermute | solution.py:515
  63.7 18.9 %all-to-all-start.1 = ((bf16[4,8,64,256]{3,2,1,0:T(8,128)(2,1)}), bf16[4,8,64,256]{3,2,1,0:T(8,128)(2,1)S(1)}, u32[]{:S(2)}, u32[]{:S(2)}) async-start(bf16[4,8,64,256]{3,2,1,0:T(8,128)(2,1)} %get-tuple-element.21), calls=%async_computation.1 | async-start | bytes 2097152 | tf_op jit(solution)/shard_map/all_to_all | solution.py:595
  67.4 0.8 copy-start.7
  115.5 6.1 %copy-start = (f32[64,32,256]{2,1,0:T(8,128)S(1)}, f32[64,32,256]{2,1,0:T(8,128)}, u32[]{:S(2)}) copy-start(f32[64,32,256]{2,1,0:T(8,128)} %second_ref.1) | copy-start | bytes 6291460
  118.3 19.7 %all-to-all-start.3 = ((bf16[32,4,16,128]{3,2,1,0:T(8,128)(2,1)}), bf16[32,4,16,128]{3,2,1,0:T(8,128)(2,1)}, u32[]{:S(2)}, u32[]{:S(2)}) async-start(bf16[32,4,16,128]{3,2,1,0:T(8,128)(2,1)} %triangle_product.1), calls=%async_computation.3 | async-start | bytes 1048576 | tf_op jit(solution)/shard_map/all_to_all | solution.py:620

commit v6 on v5

--- a/solution.py
+++ b/solution.py
@@ -45,61 +45,91 @@
     )
 
 
-def standardise_kernel(first_ref, second_ref, out_ref):
+def standardised_column(first_rows, second_rows, n, residues):
+    seqs = first_rows.shape[0] // residues
+    rows = pl.ds(n, seqs, stride=residues)
+    column = jnp.concatenate([first_rows[rows, :], second_rows[rows, :]], axis=1)
+    centred = column - jnp.mean(column, axis=1, keepdims=True)
+    variance = jnp.mean(centred * centred, axis=1, keepdims=True) + EPS
+    scale = lax.rsqrt(variance)
+    return centred * scale, variance * scale
+
+
+def high_kernel(first_ref, second_ref, high_ref):
     seqs, residues, lanes = first_ref.shape
-    cuts, height, _ = out_ref.shape
-    own = (height - 16) // seqs
+    first_rows = first_ref.reshape(seqs * residues, lanes)
+    second_rows = second_ref.reshape(seqs * residues, lanes)
+    for n in range(residues):
+        normed, _ = standardised_column(first_rows, second_rows, n, residues)
+        high_ref[n] = normed.astype(BF16)
+
+
+def standardise_high(block):
+    seqs, residues, depth = block.shape
+    half = depth // 2
+    step = 16
+    return pl.pallas_call(
+        high_kernel,
+        grid=(seqs // step,),
+        in_specs=[
+            pl.BlockSpec((step, residues, half), lambda s: (s, 0, 0)),
+            pl.BlockSpec((step, residues, half), lambda s: (s, 0, 1)),
+        ],
+        out_specs=pl.BlockSpec((residues, step, depth), lambda s: (0, s, 0)),
+        out_shape=jax.ShapeDtypeStruct((residues, seqs, depth), BF16),
+        compiler_params=params("arbitrary"),
+        cost_estimate=cost(3),
+        name="standardise_high",
+    )(block, block)
+
+
+def low_kernel(first_ref, second_ref, low_ref):
+    seqs, residues, lanes = first_ref.shape
     first_rows = first_ref.reshape(seqs * residues, lanes)
     second_rows = second_ref.reshape(seqs * residues, lanes)
     lane = lax.broadcasted_iota(jnp.int32, (seqs, 128), 1)
-    for cut in range(cuts):
-        spreads = jnp.zeros((seqs, 128), F32)
-        for n in range(own):
-            rows = pl.ds(cut * own + n, seqs, stride=residues)
-            column = jnp.concatenate([first_rows[rows, :], second_rows[rows, :]], axis=1)
-            centred = column - jnp.mean(column, axis=1, keepdims=True)
-            variance = jnp.mean(centred * centred, axis=1, keepdims=True) + EPS
-            scale = lax.rsqrt(variance)
-            out_ref[cut, n * seqs : (n + 1) * seqs, :] = (centred * scale).astype(BF16)
-            spreads = jnp.where(lane == n, variance * scale, spreads)
-        spreads = spreads.T[:8, :]
-        coarse = spreads.astype(BF16).astype(F32)
-        kept = jnp.concatenate([coarse, spreads - coarse], axis=0)
+    spreads = jnp.zeros((seqs, 128), F32)
+    for n in range(residues):
+        normed, spread = standardised_column(first_rows, second_rows, n, residues)
+        low_ref[n, :seqs, :] = (normed - normed.astype(BF16).astype(F32)).astype(BF16)
+        spreads = jnp.where(lane == n, spread, spreads)
+    spreads = spreads.T
+    row = lax.broadcasted_iota(jnp.int32, (16, seqs), 0)
+    for n in range(residues):
+        spread = jnp.broadcast_to(spreads[n : n + 1, :], (16, seqs))
+        coarse = spread.astype(BF16).astype(F32)
+        kept = jnp.where(row == 0, coarse, jnp.where(row == 1, spread - coarse, 0.0))
         kept = jnp.concatenate([kept, jnp.zeros((16, 2 * lanes - seqs), F32)], axis=1)
-        out_ref[cut, own * seqs :, :] = kept.astype(BF16)
-
-
-def standardise(block, cuts):
+        low_ref[n, seqs:, :] = kept.astype(BF16)
+
+
+def standardise_low(block):
     seqs, residues, depth = block.shape
     half = depth // 2
-    own = residues // cuts
-    height = own * seqs + 16
     return pl.pallas_call(
-        standardise_kernel,
+        low_kernel,
         grid=(residues // 8,),
         in_specs=[
             pl.BlockSpec((seqs, 8, half), lambda g: (0, g, 0)),
             pl.BlockSpec((seqs, 8, half), lambda g: (0, g, 1)),
         ],
-        out_specs=pl.BlockSpec((8 // own, height, depth), lambda g: (g, 0, 0)),
-        out_shape=jax.ShapeDtypeStruct((cuts, height, depth), BF16),
+        out_specs=pl.BlockSpec((8, seqs + 16, depth), lambda g: (g, 0, 0)),
+        out_shape=jax.ShapeDtypeStruct((residues, seqs + 16, depth), BF16),
         compiler_params=params("arbitrary"),
         cost_estimate=cost(3),
-        name="standardise",
+        name="standardise_low",
     )(block, block)
 
 
-def attention_kernel(
-    normed_ref, key_ref, others_ref, gated_ref, turned_ref, scores_ref, weights_ref
-):
-    blocks, residues, seqs, _ = gated_ref.shape
-    depth = normed_ref.shape[2]
+def attention_kernel(sources_ref, normed_ref, key_ref, others_ref, turned_ref, *rest):
+    *gated_refs, scores_ref, weights_ref, back_ref = rest
+    blocks, residues, seqs, depth = normed_ref.shape
     total = blocks * seqs
     inner = ATTENTION_UNITS * UNIT_WIDTH
     ring = scores_ref.shape[0]
     columns = []
     for n in range(residues):
-        column = normed_ref[:, n * seqs : (n + 1) * seqs, :].reshape(total, depth)
+        column = normed_ref[:, n].reshape(total, depth)
         key_rows = matmul(column, key_ref[...]).astype(BF16)
         projected = matmul_nt(others_ref[...], column)
         queries = (projected[:inner] * UNIT_WIDTH ** (-0.5)).astype(BF16)
@@ -111,13 +141,8 @@
     def score(unit):
         n, h = units[unit]
         key_rows, queries, _, _ = columns[n]
-        low, high = h * UNIT_WIDTH, (h + 1) * UNIT_WIDTH
-        pieces = [queries[low:high]]
-        if low > 0:
-            pieces.insert(0, jnp.zeros((low, total), BF16))
-        if high < inner:
-            pieces.append(jnp.zeros((inner - high, total), BF16))
-        scores_ref[unit % ring] = matmul(key_rows, jnp.concatenate(pieces, axis=0))
+        rows = slice(h * UNIT_WIDTH, (h + 1) * UNIT_WIDTH)
+        scores_ref[unit % ring] = matmul(key_rows[:, rows], queries[rows])
 
     def weigh(unit):
         for low in range(0, total, 128):
@@ -141,59 +166,58 @@
         if step >= 2:
             attend(step - 2)
     for n in range(residues):
-        gated_ref[:, n] = turned_ref[n].T.reshape(blocks, seqs, inner)
-
-
-def attention(normed, key_matrix, other_matrices, residues):
-    blocks, height, depth = normed.shape
-    seqs = (height - 16) // residues
+        back_ref[n] = turned_ref[n].T
+        for shift, gated_ref in enumerate(gated_refs):
+            first = pl.multiple_of(sources_ref[shift] * seqs, seqs)
+            gated_ref[n] = back_ref[n, pl.ds(first, seqs), :]
+
+
+def attention(sources, normed, key_matrix, other_matrices):
+    blocks, residues, seqs, depth = normed.shape
     total = blocks * seqs
     inner = ATTENTION_UNITS * UNIT_WIDTH
-    step = 4
+    step = 2
+    gated = jax.ShapeDtypeStruct((residues, seqs, inner), BF16)
+    gated_spec = pl.BlockSpec((step, seqs, inner), lambda n: (n, 0, 0))
     return pl.pallas_call(
         attention_kernel,
         grid=(residues // step,),
         in_specs=[
-            pl.BlockSpec((blocks, step * seqs, depth), lambda n: (0, n, 0)),
+            pl.BlockSpec(memory_space=pltpu.SMEM),
+            pl.BlockSpec((blocks, step, seqs, depth), lambda n: (0, n, 0, 0)),
             pl.BlockSpec((depth, inner), lambda n: (0, 0)),
             pl.BlockSpec((3 * inner, depth), lambda n: (0, 0)),
         ],
-        out_specs=[
-            pl.BlockSpec((blocks, step, seqs, inner), lambda n: (0, n, 0, 0)),
-            pl.BlockSpec((step, inner, total), lambda n: (n, 0, 0)),
-        ],
-        out_shape=[
-            jax.ShapeDtypeStruct((blocks, residues, seqs, inner), BF16),
-            jax.ShapeDtypeStruct((residues, inner, total), BF16),
-        ],
+        out_specs=[pl.BlockSpec((step, inner, total), lambda n: (n, 0, 0))]
+        + [gated_spec] * blocks,
+        out_shape=[jax.ShapeDtypeStruct((residues, inner, total), BF16)] + [gated] * blocks,
         scratch_shapes=[
             pltpu.VMEM((4, total, total), F32),
             pltpu.VMEM((4, total, total), BF16),
+            pltpu.VMEM((step, total, inner), BF16),
         ],
         compiler_params=params("arbitrary"),
         cost_estimate=cost(10),
         name="attention",
-    )(normed, key_matrix, other_matrices)
+    )(sources, normed, key_matrix, other_matrices)
 
 
 def alignment_kernel(
-    normed_ref, spread_ref, turned_ref, final_ref, entry_ref, left_ref, right_ref, rows_ref
+    high_ref, low_ref, turned_ref, final_ref, entry_ref, left_ref, right_ref, rows_ref
 ):
-    blocks, _, depth = normed_ref.shape
-    residues, _, total = turned_ref.shape
-    seqs = total // blocks
+    blocks, residues, seqs, depth = high_ref.shape
+    total = blocks * seqs
     features = TENSOR_FEATURES
     step = pl.program_id(0)
     for n in range(residues):
-        column = normed_ref[:, n * seqs : (n + 1) * seqs, :].reshape(total, depth)
+        low = low_ref[:, n, :seqs, :].reshape(total, depth)
+        column = high_ref[:, n].reshape(total, depth).astype(F32) + low.astype(F32)
         spreads = []
         for block in range(blocks):
-            kept = spread_ref[block, :, :seqs].astype(F32)
-            row = lax.broadcasted_iota(jnp.int32, kept.shape, 0)
-            chosen = lax.rem(row, 8) == step * residues + n
-            spreads.append(jnp.sum(jnp.where(chosen, kept, 0.0), axis=0, keepdims=True))
+            kept = low_ref[block, n, seqs:, :seqs].astype(F32)
+            spreads.append(jnp.sum(kept, axis=0, keepdims=True))
         spread = jnp.concatenate(spreads, axis=1)
-        updated = column.T.astype(F32) * spread + matmul(final_ref[...], turned_ref[n])
+        updated = column.T * spread + matmul(final_ref[...], turned_ref[n])
         centred = updated - jnp.mean(updated, axis=0, keepdims=True)
         variance = jnp.mean(centred * centred, axis=0, keepdims=True)
         normed = (centred * lax.rsqrt(variance + EPS)).astype(BF16)
@@ -219,25 +243,23 @@
             left_ref[c * count : (c + together) * count, :] = piece
 
 
-def alignment(normed, turned, final_matrix, entry_matrices):
-    blocks, height, depth = normed.shape
-    residues, _, total = turned.shape
-    seqs = total // blocks
+def alignment(high, low, turned, final_matrix, entry_matrices):
+    blocks, residues, seqs, depth = high.shape
+    total = blocks * seqs
     features = TENSOR_FEATURES
-    step = 4
     return pl.pallas_call(
         alignment_kernel,
-        grid=(residues // step,),
+        grid=(residues // 2,),
         in_specs=[
-            pl.BlockSpec((blocks, step * seqs, depth), lambda n: (0, n, 0)),
-            pl.BlockSpec((blocks, 16, depth), lambda n: (0, height // 16 - 1, 0)),
-            pl.BlockSpec((step, depth, total), lambda n: (n, 0, 0)),
+            pl.BlockSpec((blocks, 2, seqs, depth), lambda n: (0, n, 0, 0)),
+            pl.BlockSpec((blocks, 2, seqs + 16, depth), lambda n: (0, n, 0, 0)),
+            pl.BlockSpec((2, depth, total), lambda n: (n, 0, 0)),
             pl.BlockSpec(final_matrix.shape, lambda n: (0, 0)),
             pl.BlockSpec(entry_matrices.shape, lambda n: (0, 0)),
         ],
         out_specs=[
             pl.BlockSpec((features * residues, total), lambda n: (0, 0)),
-            pl.BlockSpec((step, features, total), lambda n: (n, 0, 0)),
+            pl.BlockSpec((2, features, total), lambda n: (n, 0, 0)),
         ],
         out_shape=[
             jax.ShapeDtypeStruct((features * residues, total), BF16),
@@ -247,7 +269,7 @@
         compiler_params=params("arbitrary"),
         cost_estimate=cost(4),
         name="alignment",
-    )(normed, normed, turned, final_matrix, entry_matrices)
+    )(high, low, turned, final_matrix, entry_matrices)
 
 
 def pair_kernel(
@@ -531,29 +553,41 @@
 
 def both_cores(own):
     rows = lax.axis_size("row")
-    me, core = lax.axis_index("col") // 2, lax.rem(lax.axis_index("col"), 2)
+    core = lax.rem(lax.axis_index("col"), 2)
     other = swap_cores(own)
-    shifts = lax.rem(me - jnp.arange(rows, dtype=jnp.int32) + rows, rows)
     residues = own.shape[1] // TENSOR_FEATURES
     if residues % 8 == 0:
-        return (own, other), jnp.concatenate([shifts + core * rows, shifts + (1 - core) * rows])
-    own, other = jnp.take(own, shifts, axis=0), jnp.take(other, shifts, axis=0)
+        return own, other
+    order = left_order(rows)
+    own, other = jnp.take(own, order, axis=0), jnp.take(other, order, axis=0)
     joined = 8 // residues
     ordered = []
     for side in (jnp.where(core == 0, own, other), jnp.where(core == 0, other, own)):
         side = side.reshape(rows // joined, joined, TENSOR_FEATURES, residues, -1)
         side = jnp.transpose(side, (0, 2, 1, 3, 4))
         ordered.append(side.reshape(rows // joined, joined * own.shape[1], -1))
-    return tuple(ordered), jnp.arange(2 * rows // joined, dtype=jnp.int32)
+    return tuple(ordered)
+
+
+def left_order(rows):
+    me = lax.axis_index("col") // 2
+    return lax.rem(me - jnp.arange(rows, dtype=jnp.int32) + rows, rows)
+
+
+def left_groups(rows, residues):
+    if residues % 8:
+        return jnp.arange(2 * rows * residues // 8, dtype=jnp.int32)
+    core = lax.rem(lax.axis_index("col"), 2)
+    order = left_order(rows)
+    return jnp.concatenate([order + core * rows, order + (1 - core) * rows])
 
 
 def exchange_rows(pieces):
-    rows = lax.axis_size("row")
     arrived = [pieces[0]]
-    for shift in range(1, rows):
-        moves = [(r, r ^ shift) for r in range(rows)]
+    for shift in range(1, len(pieces)):
+        moves = [(r, r ^ shift) for r in range(len(pieces))]
         arrived.append(lax.ppermute(pieces[shift], "row", moves))
-    return arrived, lax.axis_index("row") ^ jnp.arange(rows, dtype=jnp.int32)
+    return arrived
 
 
 def paired_entries(matrices):
@@ -577,47 +611,58 @@
     row_count = lax.axis_size("row")
     seqs, residues, depth = homolog_tensor.shape
     own_residues = residues // row_count
-    normed = standardise(homolog_tensor, row_count)
-    normed = lax.all_to_all(normed, "row", split_axis=0, concat_axis=0)
+    high = standardise_high(homolog_tensor)
+    high = high.reshape(row_count, own_residues, seqs, depth)
+    high = lax.all_to_all(high, "row", split_axis=0, concat_axis=0)
+    low = standardise_low(homolog_tensor)
+    low = low.reshape(row_count, own_residues, seqs + 16, depth)
     others = jnp.concatenate(
         [attention_probe_matrix.T, attention_extra_matrices[:, inner:].T], axis=0
     )
-    gated, turned = attention(
-        normed, attention_extra_matrices[:, :inner], others, own_residues
-    )
+    entries = paired_entries(incoming_entry_matrices)
+    sources = lax.axis_index("row") ^ jnp.arange(row_count, dtype=jnp.int32)
+    firsts = sources * own_residues
+    slots = left_groups(row_count, own_residues)
+    high, low, others, entries, sources, firsts, slots = lax.optimization_barrier(
+        (high, low, others, entries, sources, firsts, slots)
+    )
+    low = lax.all_to_all(low, "row", split_axis=0, concat_axis=0)
+    turned, *gated = attention(sources, high, attention_extra_matrices[:, :inner], others)
     left_piece, right_piece = alignment(
-        normed, turned, attention_final_matrix.T, tensor_entry_matrices.T
-    )
-
-    rights, sources = exchange_rows([right_piece] * row_count)
+        high, low, turned, attention_final_matrix.T, tensor_entry_matrices.T
+    )
+
+    rights = exchange_rows([right_piece] * row_count)
     own = gather_turned(left_piece)
-    own, rights, gated = lax.optimization_barrier((own, rights, gated))
-    gated = lax.all_to_all(gated, "row", split_axis=0, concat_axis=0)
-    left, left_slots = both_cores(own)
+    own, rights = lax.optimization_barrier((own, rights))
     mid, gate, sides = pair_update(
-        left_slots,
-        sources * own_residues,
-        left,
+        slots,
+        firsts,
+        both_cores(own),
         rights,
         tensor_final_matrix,
         couplings,
-        paired_entries(incoming_entry_matrices),
+        entries,
         incoming_switch_matrix,
     )
     gated, sides = lax.optimization_barrier((gated, sides))
-    gated = jnp.transpose(gated.reshape(residues, seqs, inner), (1, 0, 2))
-    change = jnp.dot(
-        gated.reshape(-1, inner), attention_final_matrix, preferred_element_type=F32
-    )
-    refreshed_homologs = homolog_tensor + change.reshape(homolog_tensor.shape)
+    gated = exchange_rows(gated)
 
     everywhere = ("row", "col")
     column_count = lax.axis_size("col")
     devices = row_count * column_count
     sides = sides.reshape(devices, C_TRI // devices, *sides.shape[1:])
     sides = lax.all_to_all(sides, everywhere, split_axis=0, concat_axis=0)
+    gated, sides = lax.optimization_barrier((gated, sides))
     product = triangle_product(sides, row_count, column_count)
     product = lax.all_to_all(product, everywhere, split_axis=0, concat_axis=0)
+
+    gated = jnp.take(jnp.stack(gated), sources, axis=0)
+    gated = jnp.transpose(gated.reshape(residues, seqs, inner), (1, 0, 2))
+    change = jnp.dot(
+        gated.reshape(-1, inner), attention_final_matrix, preferred_element_type=F32
+    )
+    refreshed_homologs = homolog_tensor + change.reshape(homolog_tensor.shape)
     product = product.reshape(C_TRI, *product.shape[2:])
     pair_output = pair_result(product, mid, gate, incoming_final_matrix)
     return (refreshed_homologs, pair_output)

time: 142 us -> 144 us (1.014)
  blocking collectives: 32.9 us -> 0 us
  waiting for transfers between devices: 37.3 us -> 51.5 us
  starting transfers between devices: 24.6 us -> 34.3 us
  Pallas kernels: 37.3 us -> 43.1 us
  local copies, waits for them, and re-layouts: 4.27 us -> 6.92 us
  matrix products: 2.19 us -> 3.78 us
    all_to_all x1 -> x0, blocking collectives: 32.9 us -> none  [body(): sides = lax.all_to_all(sides, everywhere, split_axis=0, concat_axis=0)]
    ppermute x3 -> x6, waiting for transfers between devices: 7.4 us -> 28.3 us  [exchange_rows(): arrived.append(lax.ppermute(pieces[shift], 'row', moves))]
    all_to_all x2 -> x3, starting transfers between devices: 9 us -> 15.5 us  [the longest x1 6.67 us: body(): sides = lax.all_to_all(sides, everywhere, split_axis=0, concat_axis=0)]
    all_to_all x2 -> x3, waiting for transfers between devices: 15.8 us -> 10.2 us  [the longest x1 6.31 us: body(): high = lax.all_to_all(high, 'row', split_axis=0, concat_axis=0)]
    pallas_call x2 -> x3, Pallas kernels: 9.15 us -> 14.3 us  [the longest x1 5.54 us: alignment(): pl.pallas_call(alignment_kernel, grid=(residues // 2,), in_specs=[pl.Bloc...]
    all_to_all x1, waiting for transfers between devices: 14.1 us -> 10.6 us  [body(): product = lax.all_to_all(product, everywhere, split_axis=0, concat_axis=0)]
    ppermute x3 -> x6, starting transfers between devices: 5.47 us -> 9.01 us  [exchange_rows(): arrived.append(lax.ppermute(pieces[shift], 'row', moves))]
    ppermute x1, waiting for transfers between devices: 0.01 us -> 1.91 us  [swap_cores(): return lax.ppermute(block, 'col', [(c, c ^ 1) for c in range(count)])]
  transfers between devices with their start and end apart: 11 -> 15, of which waited for: 5 -> 10; matrix products, arithmetic and copies ran while one was open for 5% -> 7% of each run, Pallas kernels for 7% -> 12%
where the time goes in v6:
time: 144 us
  waiting for transfers between devices  51.5 us (36%)
  Pallas kernels  43.1 us (30%)
  starting transfers between devices  34.3 us (24%)
  local copies, waits for them, and re-layouts  6.92 us (5%)
  matrix products  3.78 us (3%)
  other arithmetic  3.2 us (2%)
    ppermute x6, waiting for transfers between devices, exchange_rows(): arrived.append(lax.ppermute(pieces[shift], 'row', moves))  28.3 us
    pallas_call x1, Pallas kernels, attention(): pl.pallas_call(attention_kernel, grid=(residues // step,), in_specs=[pl.B...  12.5 us
    all_to_all x1, waiting for transfers between devices, body(): product = lax.all_to_all(product, everywhere, split_axis=0, concat_axis=0)  10.6 us
    pallas_call x1, Pallas kernels, pair_update(): pl.pallas_call(pair_kernel, in_specs=[smem] * 2 + [vmem] * (5 + len(right...  10.1 us
    ppermute x6, starting transfers between devices, exchange_rows(): arrived.append(lax.ppermute(pieces[shift], 'row', moves))  9.01 us
    ppermute x4, starting transfers between devices, gather_turned(): arrived.append(lax.ppermute(block, ('row', 'col'), moves))  6.84 us
    all_to_all x1, starting transfers between devices, body(): sides = lax.all_to_all(sides, everywhere, split_axis=0, concat_axis=0)  6.67 us
    all_to_all x1, waiting for transfers between devices, body(): high = lax.all_to_all(high, 'row', split_axis=0, concat_axis=0)  6.31 us
  transfers between devices with their start and end apart: 15, of which 10 were waited for; matrix products, arithmetic and copies ran while one was open for 7% of the time, Pallas kernels for 12%

profile of v6, /device:TPU:0, one launch (start us, length us, event | category | flops | bytes accessed | tf_op | source)
XLA Modules:
  0.0 143.7 jit_solution(11111782640830506036)
XLA Ops:
  0.6 4.5 %standardise_high.1 = bf16[32,64,256]{2,1,0:T(8,128)(2,1)} custom-call(f32[64,32,256]{2,1,0:T(8,128)} %second_ref.3, f32[64,32,256]{2,1,0:T(8,128)} %second_ref.3), custom_call_target="tpu_custom_call" | custom-call | flops 3000000000 | bytes 3000000 | tf_op jit(solution)/shard_map/standardise_high/pallas_call | solution.py:71
  5.1 5.3 %all-to-all-start = ((bf16[4,8,64,256]{3,2,1,0:T(8,128)(2,1)}), bf16[4,8,64,256]{3,2,1,0:T(8,128)(2,1)S(1)}, u32[]{:S(2)}, u32[]{:S(2)}) async-start(bf16[4,8,64,256]{3,2,1,0:T(8,128)(2,1)} %bitcast.36), calls=%async_computation | async-start | bytes 2097152 | tf_op jit(solution)/shard_map/all_to_all | solution.py:616
  10.5 0.0 copy-done.10
  10.5 0.1 copy.12
  10.6 0.0 copy-done.11
  10.6 0.1 copy.14
  10.7 0.7 copy.24
  11.4 0.0 slice-done
  11.4 0.1 copy.17
  11.6 0.6 pad_add_fusion.left_slots_ref
  12.2 0.6 iota_xor_fusion
  12.8 0.8 pad_maximum_fusion.2.others_ref
  13.5 4.3 %standardise_low.1 = bf16[32,80,256]{2,1,0:T(8,128)(2,1)} custom-call(f32[64,32,256]{2,1,0:T(8,128)} %second_ref.3, f32[64,32,256]{2,1,0:T(8,128)} %second_ref.3), custom_call_target="tpu_custom_call" | custom-call | flops 3000000000 | bytes 3000000 | tf_op jit(solution)/shard_map/standardise_low/pallas_call | solution.py:109
  17.8 6.3 %all-to-all-done.normed_ref.high_ref = bf16[4,8,64,256]{3,2,1,0:T(8,128)(2,1)S(1)} async-done(((bf16[4,8,64,256]{3,2,1,0:T(8,128)(2,1)}), bf16[4,8,64,256]{3,2,1,0:T(8,128)(2,1)S(1)}, u32[]{:S(2)}, u32[]{:S(2)}) %all-to-all-start) | async-done | bytes 1048608 | tf_op jit(solution)/shard_map/all_to_all | solution.py:616
  24.1 3.5 %all-to-all-start.1 = ((bf16[4,8,80,256]{3,2,1,0:T(8,128)(2,1)}), bf16[4,8,80,256]{3,2,1,0:T(8,128)(2,1)S(1)}, u32[]{:S(2)}, u32[]{:S(2)}) async-start(bf16[4,8,80,256]{3,2,1,0:T(8,128)(2,1)} %bitcast.34), calls=%async_computation.1 | async-start | bytes 2621440 | tf_op jit(solution)/shard_map/all_to_all | solution.py:629
  27.6 0.0 copy-done.3
  27.7 0.7 slice.7.key_ref
  28.3 0.0 copy-done.4
  28.3 0.8 copy.15
  29.1 12.5 %attention.1 = (bf16[8,256,256]{2,1,0:T(8,128)(2,1)}, bf16[8,64,256]{2,1,0:T(8,128)(2,1)}, bf16[8,64,256]{2,1,0:T(8,128)(2,1)}, bf16[8,64,256]{2,1,0:T(8,128)(2,1)}, bf16[8,64,256]{2,1,0:T(8,128)(2,1)}) custom-call(s32[4]{0:T(128)} %get-tuple-element.34.sources_ref, bf16[4,8,64,256]{3,2,1,0:T(8,128)(2,1)} %copy-done.1, bf16[256,256]{1,0:T(8,128)(2,1)} %slice.7.key_ref, ...), custom_call_target="tpu_custom_call" | custom-call | flops 10000000000 | bytes 10000000 | tf_op jit(solution)/shard_map/attention/pallas_call | solution.py:182
  41.6 1.9 %all-to-all-done.1.low_ref = bf16[4,8,80,256]{3,2,1,0:T(8,128)(2,1)S(1)} async-done(((bf16[4,8,80,256]{3,2,1,0:T(8,128)(2,1)}), bf16[4,8,80,256]{3,2,1,0:T(8,128)(2,1)S(1)}, u32[]{:S(2)}, u32[]{:S(2)}) %all-to-all-start.1) | async-done | bytes 1310752 | tf_op jit(solution)/shard_map/all_to_all | solution.py:629
  43.5 1.1 copy-done
  44.6 5.5 %alignment.1 = (bf16[256,256]{1,0:T(8,128)(2,1)}, bf16[8,32,256]{2,1,0:T(8,128)(2,1)}) custom-call(bf16[4,8,64,256]{3,2,1,0:T(8,128)(2,1)} %copy-done.1, bf16[4,8,80,256]{3,2,1,0:T(8,128)(2,1)} %copy-done, bf16[8,256,256]{2,1,0:T(8,128)(2,1)} %get-tuple-element.44.turned_ref, bf16[256,256]{1,0:T(8,128)(2,1)} %bitcast.46, bf16[64,256]{1,0:T(8,128)(2,1)} %bitcast.52), custom_call_target="tpu_custom_call" | custom-call | flops 4000000000 | bytes 4000000 | tf_op jit(solution)/shard_map/alignment/pallas_call | solution.py:250
  50.1 3.7 %collective-permute-start.3 = (bf16[256,256]{1,0:T(8,128)(2,1)}, bf16[256,256]{1,0:T(8,128)(2,1)S(1)}, u32[]{:S(2)}, u32[]{:S(2)}) collective-permute-start(bf16[256,256]{1,0:T(8,128)(2,1)} %get-tuple-element.45), channel_id=1, source_target_pairs={{0,6},{1,7},{2,14},{3,15},{4,22},{5,23},{6,30},{7,31},{8,0},{9,1},... | collective-permute-start | bytes 393224 | tf_op jit(solution)/shard_map/ppermute | solution.py:550
  53.8 1.5 %collective-permute-start.2 = (bf16[256,256]{1,0:T(8,128)(2,1)}, bf16[256,256]{1,0:T(8,128)(2,1)S(1)}, u32[]{:S(2)}, u32[]{:S(2)}) collective-permute-start(bf16[256,256]{1,0:T(8,128)(2,1)} %get-tuple-element.45), channel_id=1, source_target_pairs={{0,4},{1,5},{2,12},{3,13},{4,20},{5,21},{6,28},{7,29},{8,6},{9,7},... | collective-permute-start | bytes 393224 | tf_op jit(solution)/shard_map/ppermute | solution.py:550
  55.2 0.2 collective-permute-start.1
  55.4 1.6 %collective-permute-start = (bf16[256,256]{1,0:T(8,128)(2,1)}, bf16[256,256]{1,0:T(8,128)(2,1)S(1)}, u32[]{:S(2)}, u32[]{:S(2)}) collective-permute-start(bf16[256,256]{1,0:T(8,128)(2,1)} %get-tuple-element.45), channel_id=1, source_target_pairs={{0,0},{1,1},{2,8},{3,9},{4,16},{5,17},{6,24},{7,25},{8,2},{9,3},{1... | collective-permute-start | bytes 393224 | tf_op jit(solution)/shard_map/ppermute | solution.py:550
  57.0 4.8 %collective-permute-start.6 = (bf16[8,32,256]{2,1,0:T(8,128)(2,1)}, bf16[8,32,256]{2,1,0:T(8,128)(2,1)S(1)}, u32[]{:S(2)}, u32[]{:S(2)}) collective-permute-start(bf16[8,32,256]{2,1,0:T(8,128)(2,1)} %get-tuple-element.48.rest_0_), channel_id=1, source_target_pairs={{0,24},{8,16},{16,8},{24,0},{1,25},{9,17},{17,9},{25,1},{2,26},{10... | collective-permute-start | bytes 393224 | tf_op jit(solution)/shard_map/ppermute | solution.py:589
  61.8 0.0 collective-permute-done.3
  61.8 0.0 collective-permute-start.5
  61.8 0.0 collective-permute-done.2
  61.8 0.6 collective-permute-start.4
  62.4 0.4 collective-permute-done.1
  62.9 0.0 collective-permute-done
  62.9 0.1 pad_maximum_fusion.1.own_ref
  62.9 0.0 copy-start.6
  63.0 5.0 %collective-permute-done.6.rest_3_ = bf16[8,32,256]{2,1,0:T(8,128)(2,1)S(1)} collective-permute-done((bf16[8,32,256]{2,1,0:T(8,128)(2,1)}, bf16[8,32,256]{2,1,0:T(8,128)(2,1)S(1)}, u32[]{:S(2)}, u32[]{:S(2)}) %collective-permute-start.6) | collective-permute-done | bytes 131104 | tf_op jit(solution)/shard_map/ppermute | solution.py:589
  67.9 0.0 collective-permute-done.5.rest_2_
  67.9 1.4 collective-permute-done.4.rest_1_
  69.3 0.0 collective-permute-start.7
  69.3 1.9 %collective-permute-done.7.other_ref = bf16[4,256,256]{2,1,0:T(8,128)(2,1)S(1)} collective-permute-done((bf16[4,256,256]{2,1,0:T(8,128)(2,1)S(1)}, bf16[4,256,256]{2,1,0:T(8,128)(2,1)S(1)}, u32[]{:S(2)}, u32[]{:S(2)}) %collective-permute-start.7) | collective-permute-done | bytes 524320 | tf_op jit(solution)/shard_map/ppermute | solution.py:537
  71.2 0.0 copy-done.17
  71.3 0.8 copy-done.12
  72.0 10.1 %pair_update.1 = (f32[32,64,128]{2,1,0:T(8,128)}, f32[32,64,128]{2,1,0:T(8,128)}, bf16[128,32,128]{2,1,0:T(8,128)(2,1)}) custom-call(s32[8]{0:T(128)} %pad_add_fusion.left_slots_ref, s32[4]{0:T(128)} %get-tuple-element.42.right_firsts_ref, bf16[4,256,256]{2,1,0:T(8,128)(2,1)} %copy-done.6, bf16[4,256,256]{2,1,0:T(8,128)(2,1)} %copy-done.12, ...), custom_call_target="tpu_custom_call" | custom-call | flops 12000000000 | bytes 12000000 | tf_op jit(solution)/shard_map/pair_update/pallas_call | solution.py:408
  82.2 6.7 %all-to-all-start.2 = ((bf16[32,4,32,128]{3,2,1,0:T(8,128)(2,1)}), bf16[32,4,32,128]{3,2,1,0:T(8,128)(2,1)S(1)}, u32[]{:S(2)}, u32[]{:S(2)}) async-start(bf16[32,4,32,128]{3,2,1,0:T(8,128)(2,1)} %bitcast.37), calls=%async_computation.2 | async-start | bytes 2097152 | tf_op jit(solution)/shard_map/all_to_all | solution.py:655
  88.9 1.8 %collective-permute-start.8 = (bf16[8,64,256]{2,1,0:T(8,128)(2,1)S(1)}, bf16[8,64,256]{2,1,0:T(8,128)(2,1)S(1)}, u32[]{:S(2)}, u32[]{:S(2)}) collective-permute-start(bf16[8,64,256]{2,1,0:T(8,128)(2,1)S(1)} %copy-done.15), channel_id=1, source_target_pairs={{0,8},{8,0},{16,24},{24,16},{1,9},{9,1},{17,25},{25,17},{2,10},{10... | collective-permute-start | bytes 786440 | tf_op jit(solution)/shard_map/ppermute | solution.py:589
  90.7 1.5 %collective-permute-start.9 = (bf16[8,64,256]{2,1,0:T(8,128)(2,1)S(1)}, bf16[8,64,256]{2,1,0:T(8,128)(2,1)S(1)}, u32[]{:S(2)}, u32[]{:S(2)}) collective-permute-start(bf16[8,64,256]{2,1,0:T(8,128)(2,1)S(1)} %copy-done.14), channel_id=1, source_target_pairs={{0,16},{8,24},{16,0},{24,8},{1,17},{9,25},{17,1},{25,9},{2,18},{10... | collective-permute-start | bytes 786440 | tf_op jit(solution)/shard_map/ppermute | solution.py:589
  92.2 0.0 copy-done.13
  92.2 0.3 collective-permute-start.10
  92.5 13.7 %collective-permute-done.8 = bf16[8,64,256]{2,1,0:T(8,128)(2,1)S(1)} collective-permute-done((bf16[8,64,256]{2,1,0:T(8,128)(2,1)S(1)}, bf16[8,64,256]{2,1,0:T(8,128)(2,1)S(1)}, u32[]{:S(2)}, u32[]{:S(2)}) %collective-permute-start.8) | collective-permute-done | bytes 262176 | tf_op jit(solution)/shard_map/ppermute | solution.py:589
  106.2 0.0 collective-permute-done.9
  106.2 8.2 %collective-permute-done.10 = bf16[8,64,256]{2,1,0:T(8,128)(2,1)S(1)} collective-permute-done((bf16[8,64,256]{2,1,0:T(8,128)(2,1)S(1)}, bf16[8,64,256]{2,1,0:T(8,128)(2,1)S(1)}, u32[]{:S(2)}, u32[]{:S(2)}) %collective-permute-start.10) | collective-permute-done | bytes 262176 | tf_op jit(solution)/shard_map/ppermute | solution.py:589
  114.4 2.0 %all-to-all-done.2.sides_ref = bf16[32,4,32,128]{3,2,1,0:T(8,128)(2,1)S(1)} async-done(((bf16[32,4,32,128]{3,2,1,0:T(8,128)(2,1)}), bf16[32,4,32,128]{3,2,1,0:T(8,128)(2,1)S(1)}, u32[]{:S(2)}, u32[]{:S(2)}) %all-to-all-start.2) | async-done | bytes 1048608 | tf_op jit(solution)/shard_map/all_to_all | solution.py:655
  116.5 1.0 copy-done.2
  117.4 2.6 %triangle_product.1 = bf16[32,4,16,128]{3,2,1,0:T(8,128)(2,1)} custom-call(bf16[32,4,32,128]{3,2,1,0:T(8,128)(2,1)} %copy-done.2), custom_call_target="tpu_custom_call" | custom-call | flops 3000000000 | bytes 3000000 | tf_op jit(solution)/shard_map/triangle_product/pallas_call | solution.py:472
  120.1 3.0 %all-to-all-start.3 = ((bf16[32,4,16,128]{3,2,1,0:T(8,128)(2,1)}), bf16[32,4,16,128]{3,2,1,0:T(8,128)(2,1)S(1)}, u32[]{:S(2)}, u32[]{:S(2)}) async-start(bf16[32,4,16,128]{3,2,1,0:T(8,128)(2,1)} %triangle_product.1), calls=%async_computation.3 | async-start | bytes 1048576 | tf_op jit(solution)/shard_map/all_to_all | solution.py:658
  123.1 0.1 broadcast_in_dim.16
  123.1 0.1 broadcast_in_dim.17
  123.3 1.2 pad_maximum_fusion
  124.4 0.6 gather_fusion
  125.0 3.8 %convolution_add_fusion = f32[64,32,256]{2,1,0:T(8,128)} fusion(f32[64,32,256]{2,1,0:T(8,128)} %second_ref.3, bf16[32,64,256]{2,1,0:T(8,128)(2,1)S(1)} %bitcast.33, pred[32]{0:T(512)(128)(4,1)S(1)} %broadcast_in_dim.17, bf16[256,256]{1,0:T(8,128)(2,1)S(1)} %copy-done.4), kind=kOutput, calls=%fused_computation.1 | convolution fusion | flops 269484032 | bytes 5373984 | tf_op jit(solution)/shard_map/dot_general | solution.py:662
  128.8 10.6 %all-to-all-done.3 = bf16[32,4,16,128]{3,2,1,0:T(8,128)(2,1)S(1)} async-done(((bf16[32,4,16,128]{3,2,1,0:T(8,128)(2,1)}), bf16[32,4,16,128]{3,2,1,0:T(8,128)(2,1)S(1)}, u32[]{:S(2)}, u32[]{:S(2)}) %all-to-all-start.3) | async-done | bytes 524320 | tf_op jit(solution)/shard_map/all_to_all | solution.py:658
  139.4 0.8 copy-done.5
  140.2 3.5 %pair_result.1 = f32[64,2,16,128]{3,2,1,0:T(8,128)} custom-call(bf16[128,16,128]{2,1,0:T(8,128)(2,1)} %bitcast.38, f32[2,16,64,128]{3,2,1,0:T(8,128)} %bitcast.53, f32[2,16,64,128]{3,2,1,0:T(8,128)} %bitcast.54, bf16[128,128]{1,0:T(8,128)(2,1)} %final_ref.1), custom_call_target="tpu_custom_call" | custom-call | flops 4000000000 | bytes 4000000 | tf_op jit(solution)/shard_map/pair_result/pallas_call | solution.py:511
  (35 shorter events, 0.1 us)
Async XLA Ops:
  5.1 5.3 %copy-start.10 = (bf16[256,256]{1,0:T(8,128)(2,1)S(1)}, bf16[256,256]{1,0:T(8,128)(2,1)}, u32[]{:S(2)}) copy-start(bf16[256,256]{1,0:T(8,128)(2,1)} %param.12) | copy-start | bytes 393220
  5.1 5.4 %copy-start.11 = (bf16[128,512]{1,0:T(8,128)(2,1)S(1)}, bf16[128,512]{1,0:T(8,128)(2,1)}, u32[]{:S(2)}) copy-start(bf16[128,512]{1,0:T(8,128)(2,1)} %param.17) | copy-start | bytes 393220
  5.1 6.3 %slice-start = ((bf16[256,768]{1,0:T(8,128)(2,1)}), bf16[256,512]{1,0:T(8,128)(2,1)S(1)}, s32[]{:S(2)}) async-start(bf16[256,768]{1,0:T(8,128)(2,1)} %param.13), calls=%async_computation.4 | async-start | bytes 524288 | tf_op jit(solution)/shard_map/slice | solution.py:620
  5.1 18.9 %all-to-all-start = ((bf16[4,8,64,256]{3,2,1,0:T(8,128)(2,1)}), bf16[4,8,64,256]{3,2,1,0:T(8,128)(2,1)S(1)}, u32[]{:S(2)}, u32[]{:S(2)}) async-start(bf16[4,8,64,256]{3,2,1,0:T(8,128)(2,1)} %bitcast.36), calls=%async_computation | async-start | bytes 2097152 | tf_op jit(solution)/shard_map/all_to_all | solution.py:616
  17.8 9.9 %copy-start.3 = (bf16[256,768]{1,0:T(8,128)(2,1)S(1)}, bf16[256,768]{1,0:T(8,128)(2,1)}, u32[]{:S(2)}) copy-start(bf16[256,768]{1,0:T(8,128)(2,1)} %param.13) | copy-start | bytes 1179652
  17.8 10.5 %copy-start.4 = (bf16[256,256]{1,0:T(8,128)(2,1)S(1)}, bf16[256,256]{1,0:T(8,128)(2,1)}, u32[]{:S(2)}) copy-start(bf16[256,256]{1,0:T(8,128)(2,1)} %param.14) | copy-start | bytes 393220
  24.1 5.0 %copy-start.1 = (bf16[4,8,64,256]{3,2,1,0:T(8,128)(2,1)}, bf16[4,8,64,256]{3,2,1,0:T(8,128)(2,1)S(1)}, u32[]{:S(2)}) copy-start(bf16[4,8,64,256]{3,2,1,0:T(8,128)(2,1)S(1)} %all-to-all-done.normed_ref.high_ref) | copy-start | bytes 3145732
  24.1 19.4 %all-to-all-start.1 = ((bf16[4,8,80,256]{3,2,1,0:T(8,128)(2,1)}), bf16[4,8,80,256]{3,2,1,0:T(8,128)(2,1)S(1)}, u32[]{:S(2)}, u32[]{:S(2)}) async-start(bf16[4,8,80,256]{3,2,1,0:T(8,128)(2,1)} %bitcast.34), calls=%async_computation.1 | async-start | bytes 2621440 | tf_op jit(solution)/shard_map/all_to_all | solution.py:629
  43.5 1.1 copy-start
  50.1 11.7 %collective-permute-start.3 = (bf16[256,256]{1,0:T(8,128)(2,1)}, bf16[256,256]{1,0:T(8,128)(2,1)S(1)}, u32[]{:S(2)}, u32[]{:S(2)}) collective-permute-start(bf16[256,256]{1,0:T(8,128)(2,1)} %get-tuple-element.45), channel_id=1, source_target_pairs={{0,6},{1,7},{2,14},{3,15},{4,22},{5,23},{6,30},{7,31},{8,0},{9,1},... | collective-permute-start | bytes 393224 | tf_op jit(solution)/shard_map/ppermute | solution.py:550
  53.8 8.0 %collective-permute-start.2 = (bf16[256,256]{1,0:T(8,128)(2,1)}, bf16[256,256]{1,0:T(8,128)(2,1)S(1)}, u32[]{:S(2)}, u32[]{:S(2)}) collective-permute-start(bf16[256,256]{1,0:T(8,128)(2,1)} %get-tuple-element.45), channel_id=1, source_target_pairs={{0,4},{1,5},{2,12},{3,13},{4,20},{5,21},{6,28},{7,29},{8,6},{9,7},... | collective-permute-start | bytes 393224 | tf_op jit(solution)/shard_map/ppermute | solution.py:550
  55.2 7.6 %collective-permute-start.1 = (bf16[256,256]{1,0:T(8,128)(2,1)}, bf16[256,256]{1,0:T(8,128)(2,1)S(1)}, u32[]{:S(2)}, u32[]{:S(2)}) collective-permute-start(bf16[256,256]{1,0:T(8,128)(2,1)} %get-tuple-element.45), channel_id=1, source_target_pairs={{0,2},{1,3},{2,10},{3,11},{4,18},{5,19},{6,26},{7,27},{8,4},{9,5},... | collective-permute-start | bytes 393224 | tf_op jit(solution)/shard_map/ppermute | solution.py:550
  55.4 7.5 %collective-permute-start = (bf16[256,256]{1,0:T(8,128)(2,1)}, bf16[256,256]{1,0:T(8,128)(2,1)S(1)}, u32[]{:S(2)}, u32[]{:S(2)}) collective-permute-start(bf16[256,256]{1,0:T(8,128)(2,1)} %get-tuple-element.45), channel_id=1, source_target_pairs={{0,0},{1,1},{2,8},{3,9},{4,16},{5,17},{6,24},{7,25},{8,2},{9,3},{1... | collective-permute-start | bytes 393224 | tf_op jit(solution)/shard_map/ppermute | solution.py:550
  57.0 11.0 %collective-permute-start.6 = (bf16[8,32,256]{2,1,0:T(8,128)(2,1)}, bf16[8,32,256]{2,1,0:T(8,128)(2,1)S(1)}, u32[]{:S(2)}, u32[]{:S(2)}) collective-permute-start(bf16[8,32,256]{2,1,0:T(8,128)(2,1)} %get-tuple-element.48.rest_0_), channel_id=1, source_target_pairs={{0,24},{8,16},{16,8},{24,0},{1,25},{9,17},{17,9},{25,1},{2,26},{10... | collective-permute-start | bytes 393224 | tf_op jit(solution)/shard_map/ppermute | solution.py:589
  61.8 6.2 %collective-permute-start.5 = (bf16[8,32,256]{2,1,0:T(8,128)(2,1)}, bf16[8,32,256]{2,1,0:T(8,128)(2,1)S(1)}, u32[]{:S(2)}, u32[]{:S(2)}) collective-permute-start(bf16[8,32,256]{2,1,0:T(8,128)(2,1)} %get-tuple-element.48.rest_0_), channel_id=1, source_target_pairs={{0,16},{8,24},{16,0},{24,8},{1,17},{9,25},{17,1},{25,9},{2,18},{10... | collective-permute-start | bytes 393224 | tf_op jit(solution)/shard_map/ppermute | solution.py:589
  61.8 7.5 %collective-permute-start.4 = (bf16[8,32,256]{2,1,0:T(8,128)(2,1)}, bf16[8,32,256]{2,1,0:T(8,128)(2,1)S(1)}, u32[]{:S(2)}, u32[]{:S(2)}) collective-permute-start(bf16[8,32,256]{2,1,0:T(8,128)(2,1)} %get-tuple-element.48.rest_0_), channel_id=1, source_target_pairs={{0,8},{8,0},{16,24},{24,16},{1,9},{9,1},{17,25},{25,17},{2,10},{10... | collective-permute-start | bytes 393224 | tf_op jit(solution)/shard_map/ppermute | solution.py:589
  62.9 8.3 %copy-start.6 = (bf16[4,256,256]{2,1,0:T(8,128)(2,1)}, bf16[4,256,256]{2,1,0:T(8,128)(2,1)S(1)}, u32[]{:S(2)}) copy-start(bf16[4,256,256]{2,1,0:T(8,128)(2,1)S(1)} %pad_maximum_fusion.1.own_ref) | copy-start | bytes 1572868
  67.9 3.3 %copy-start.16 = (bf16[8,32,256]{2,1,0:T(8,128)(2,1)}, bf16[8,32,256]{2,1,0:T(8,128)(2,1)S(1)}, u32[]{:S(2)}) copy-start(bf16[8,32,256]{2,1,0:T(8,128)(2,1)S(1)} %collective-permute-done.6.rest_3_) | copy-start | bytes 393220
  67.9 3.3 %copy-start.17 = (bf16[8,32,256]{2,1,0:T(8,128)(2,1)}, bf16[8,32,256]{2,1,0:T(8,128)(2,1)S(1)}, u32[]{:S(2)}) copy-start(bf16[8,32,256]{2,1,0:T(8,128)(2,1)S(1)} %collective-permute-done.5.rest_2_) | copy-start | bytes 393220
  69.3 1.9 %copy-start.18 = (bf16[8,32,256]{2,1,0:T(8,128)(2,1)}, bf16[8,32,256]{2,1,0:T(8,128)(2,1)S(1)}, u32[]{:S(2)}) copy-start(bf16[8,32,256]{2,1,0:T(8,128)(2,1)S(1)} %collective-permute-done.4.rest_1_) | copy-start | bytes 393220
  69.3 1.9 %collective-permute-start.7 = (bf16[4,256,256]{2,1,0:T(8,128)(2,1)S(1)}, bf16[4,256,256]{2,1,0:T(8,128)(2,1)S(1)}, u32[]{:S(2)}, u32[]{:S(2)}) collective-permute-start(bf16[4,256,256]{2,1,0:T(8,128)(2,1)S(1)} %pad_maximum_fusion.1.own_ref), channel_id=1, source_target_pairs={{0,1},{1,0},{2,3},{3,2},{4,5},{5,4},{6,7},{7,6},{8,9},{9,8},{10,11... | collective-permute-start | bytes 1572872 | tf_op jit(solution)/shard_map/ppermute | solution.py:537
  71.2 0.8 copy-start.12
  82.2 6.7 %copy-start.15 = (bf16[8,64,256]{2,1,0:T(8,128)(2,1)S(1)}, bf16[8,64,256]{2,1,0:T(8,128)(2,1)}, u32[]{:S(2)}) copy-start(bf16[8,64,256]{2,1,0:T(8,128)(2,1)} %get-tuple-element.55) | copy-start | bytes 786436
  82.2 8.6 %copy-start.14 = (bf16[8,64,256]{2,1,0:T(8,128)(2,1)S(1)}, bf16[8,64,256]{2,1,0:T(8,128)(2,1)}, u32[]{:S(2)}) copy-start(bf16[8,64,256]{2,1,0:T(8,128)(2,1)} %get-tuple-element.56) | copy-start | bytes 786436
  82.2 10.0 %copy-start.13 = (bf16[8,64,256]{2,1,0:T(8,128)(2,1)S(1)}, bf16[8,64,256]{2,1,0:T(8,128)(2,1)}, u32[]{:S(2)}) copy-start(bf16[8,64,256]{2,1,0:T(8,128)(2,1)} %get-tuple-element.57) | copy-start | bytes 786436
  82.2 34.3 %all-to-all-start.2 = ((bf16[32,4,32,128]{3,2,1,0:T(8,128)(2,1)}), bf16[32,4,32,128]{3,2,1,0:T(8,128)(2,1)S(1)}, u32[]{:S(2)}, u32[]{:S(2)}) async-start(bf16[32,4,32,128]{3,2,1,0:T(8,128)(2,1)} %bitcast.37), calls=%async_computation.2 | async-start | bytes 2097152 | tf_op jit(solution)/shard_map/all_to_all | solution.py:655
  88.9 34.1 %copy-start.19 = (s32[4]{0:T(128)S(1)}, s32[4]{0:T(128)}, u32[]{:S(2)}) copy-start(s32[4]{0:T(128)} %get-tuple-element.34.sources_ref) | copy-start | bytes 52
  88.9 34.3 %copy-start.7 = (bf16[8,64,256]{2,1,0:T(8,128)(2,1)S(1)}, bf16[8,64,256]{2,1,0:T(8,128)(2,1)}, u32[]{:S(2)}) copy-start(bf16[8,64,256]{2,1,0:T(8,128)(2,1)} %get-tuple-element.59) | copy-start | bytes 786436
  88.9 17.3 %collective-permute-start.8 = (bf16[8,64,256]{2,1,0:T(8,128)(2,1)S(1)}, bf16[8,64,256]{2,1,0:T(8,128)(2,1)S(1)}, u32[]{:S(2)}, u32[]{:S(2)}) collective-permute-start(bf16[8,64,256]{2,1,0:T(8,128)(2,1)S(1)} %copy-done.15), channel_id=1, source_target_pairs={{0,8},{8,0},{16,24},{24,16},{1,9},{9,1},{17,25},{25,17},{2,10},{10... | collective-permute-start | bytes 786440 | tf_op jit(solution)/shard_map/ppermute | solution.py:589
  90.7 15.4 %collective-permute-start.9 = (bf16[8,64,256]{2,1,0:T(8,128)(2,1)S(1)}, bf16[8,64,256]{2,1,0:T(8,128)(2,1)S(1)}, u32[]{:S(2)}, u32[]{:S(2)}) collective-permute-start(bf16[8,64,256]{2,1,0:T(8,128)(2,1)S(1)} %copy-done.14), channel_id=1, source_target_pairs={{0,16},{8,24},{16,0},{24,8},{1,17},{9,25},{17,1},{25,9},{2,18},{10... | collective-permute-start | bytes 786440 | tf_op jit(solution)/shard_map/ppermute | solution.py:589
  92.2 22.2 %collective-permute-start.10 = (bf16[8,64,256]{2,1,0:T(8,128)(2,1)S(1)}, bf16[8,64,256]{2,1,0:T(8,128)(2,1)S(1)}, u32[]{:S(2)}, u32[]{:S(2)}) collective-permute-start(bf16[8,64,256]{2,1,0:T(8,128)(2,1)S(1)} %copy-done.13), channel_id=1, source_target_pairs={{0,24},{8,16},{16,8},{24,0},{1,25},{9,17},{17,9},{25,1},{2,26},{10... | collective-permute-start | bytes 786440 | tf_op jit(solution)/shard_map/ppermute | solution.py:589
  106.2 17.0 %copy-start.8 = (bf16[8,64,256]{2,1,0:T(8,128)(2,1)}, bf16[8,64,256]{2,1,0:T(8,128)(2,1)S(1)}, u32[]{:S(2)}) copy-start(bf16[8,64,256]{2,1,0:T(8,128)(2,1)S(1)} %collective-permute-done.9) | copy-start | bytes 786436
  114.4 8.8 %copy-start.9 = (bf16[8,64,256]{2,1,0:T(8,128)(2,1)}, bf16[8,64,256]{2,1,0:T(8,128)(2,1)S(1)}, u32[]{:S(2)}) copy-start(bf16[8,64,256]{2,1,0:T(8,128)(2,1)S(1)} %collective-permute-done.10) | copy-start | bytes 786436
  116.5 1.0 copy-start.2
  120.1 19.3 %all-to-all-start.3 = ((bf16[32,4,16,128]{3,2,1,0:T(8,128)(2,1)}), bf16[32,4,16,128]{3,2,1,0:T(8,128)(2,1)S(1)}, u32[]{:S(2)}, u32[]{:S(2)}) async-start(bf16[32,4,16,128]{3,2,1,0:T(8,128)(2,1)} %triangle_product.1), calls=%async_computation.3 | async-start | bytes 1048576 | tf_op jit(solution)/shard_map/all_to_all | solution.py:658
  139.4 0.8 copy-start.5

commit v7 on v6

--- a/solution.py
+++ b/solution.py
@@ -18,7 +18,6 @@
 F32 = jnp.float32
 BF16 = jnp.bfloat16
 NT = (((1,), (1,)), ((), ()))
-VMEM_LIMIT = 56 * 1024 * 1024
 
 
 def matmul(left, right):
@@ -39,10 +38,32 @@
     )
 
 
-def params(*semantics):
+def params(megabytes, *semantics):
     return pltpu.CompilerParams(
-        dimension_semantics=semantics or None, vmem_limit_bytes=VMEM_LIMIT
-    )
+        dimension_semantics=semantics or None, vmem_limit_bytes=megabytes * 1024 * 1024
+    )
+
+
+def fold(values, combine):
+    while values.shape[0] > 8:
+        half = values.shape[0] // 2
+        values = combine(values[:half], values[half:])
+    return values
+
+
+def top_rows(values):
+    return jnp.max(fold(values, jnp.maximum), axis=0, keepdims=True)
+
+
+def sum_rows(values):
+    return jnp.sum(fold(values, jnp.add), axis=0, keepdims=True)
+
+
+def normalise_rows(values):
+    count = values.shape[0]
+    centred = values - sum_rows(values) * (1.0 / count)
+    variance = sum_rows(centred * centred) * (1.0 / count)
+    return (centred * lax.rsqrt(variance + EPS)).astype(BF16)
 
 
 def standardised_column(first_rows, second_rows, n, residues):
@@ -55,32 +76,57 @@
     return centred * scale, variance * scale
 
 
-def high_kernel(first_ref, second_ref, high_ref):
+def high_kernel(block_hbm, high_hbm, first_ref, second_ref, high_ref, fetched, sent):
     seqs, residues, lanes = first_ref.shape
-    first_rows = first_ref.reshape(seqs * residues, lanes)
-    second_rows = second_ref.reshape(seqs * residues, lanes)
-    for n in range(residues):
-        normed, _ = standardised_column(first_rows, second_rows, n, residues)
-        high_ref[n] = normed.astype(BF16)
+    step = 16
+    fetches, sends = [], []
+    for s in range(0, seqs, step):
+        chosen = pl.ds(s, step)
+        for half, ref in enumerate((first_ref, second_ref)):
+            source = block_hbm.at[chosen, :, pl.ds(half * lanes, lanes)]
+            fetches.append(
+                pltpu.make_async_copy(source, ref.at[chosen], fetched.at[len(fetches)])
+            )
+            fetches[-1].start()
+    for part in range(seqs // step):
+        chosen = pl.ds(part * step, step)
+        fetches[2 * part].wait()
+        fetches[2 * part + 1].wait()
+        first_rows = first_ref.at[chosen].reshape(step * residues, lanes)
+        second_rows = second_ref.at[chosen].reshape(step * residues, lanes)
+        for n in range(residues):
+            normed, _ = standardised_column(first_rows, second_rows, n, residues)
+            high_ref[n, chosen, :] = normed.astype(BF16)
+        sends.append(
+            pltpu.make_async_copy(
+                high_ref.at[:, chosen], high_hbm.at[:, chosen], sent.at[part]
+            )
+        )
+        sends[-1].start()
+    for send in sends:
+        send.wait()
 
 
 def standardise_high(block):
     seqs, residues, depth = block.shape
     half = depth // 2
-    step = 16
+    anywhere = pl.BlockSpec(memory_space=pltpu.HBM)
     return pl.pallas_call(
         high_kernel,
-        grid=(seqs // step,),
-        in_specs=[
-            pl.BlockSpec((step, residues, half), lambda s: (s, 0, 0)),
-            pl.BlockSpec((step, residues, half), lambda s: (s, 0, 1)),
-        ],
-        out_specs=pl.BlockSpec((residues, step, depth), lambda s: (0, s, 0)),
-        out_shape=jax.ShapeDtypeStruct((residues, seqs, depth), BF16),
-        compiler_params=params("arbitrary"),
+        in_specs=[anywhere],
+        out_specs=anywhere,
+        out_shape=pltpu.HBM((residues, seqs, depth), BF16),
+        scratch_shapes=[
+            pltpu.VMEM((seqs, residues, half), F32),
+            pltpu.VMEM((seqs, residues, half), F32),
+            pltpu.VMEM((residues, seqs, depth), BF16),
+            pltpu.SemaphoreType.DMA((seqs // 8,)),
+            pltpu.SemaphoreType.DMA((seqs // 16,)),
+        ],
+        compiler_params=params(10),
         cost_estimate=cost(3),
         name="standardise_high",
-    )(block, block)
+    )(pltpu.with_memory_space_constraint(block, pltpu.HBM))
 
 
 def low_kernel(first_ref, second_ref, low_ref):
@@ -114,8 +160,8 @@
             pl.BlockSpec((seqs, 8, half), lambda g: (0, g, 1)),
         ],
         out_specs=pl.BlockSpec((8, seqs + 16, depth), lambda g: (g, 0, 0)),
-        out_shape=jax.ShapeDtypeStruct((residues, seqs + 16, depth), BF16),
-        compiler_params=params("arbitrary"),
+        out_shape=pltpu.HBM((residues, seqs + 16, depth), BF16),
+        compiler_params=params(10, "arbitrary"),
         cost_estimate=cost(3),
         name="standardise_low",
     )(block, block)
@@ -141,14 +187,19 @@
     def score(unit):
         n, h = units[unit]
         key_rows, queries, _, _ = columns[n]
-        rows = slice(h * UNIT_WIDTH, (h + 1) * UNIT_WIDTH)
-        scores_ref[unit % ring] = matmul(key_rows[:, rows], queries[rows])
+        low, high = h * UNIT_WIDTH, (h + 1) * UNIT_WIDTH
+        pieces = [queries[low:high]]
+        if low > 0:
+            pieces.insert(0, jnp.zeros((low, total), BF16))
+        if high < inner:
+            pieces.append(jnp.zeros((inner - high, total), BF16))
+        scores_ref[unit % ring] = matmul(key_rows, jnp.concatenate(pieces, axis=0))
 
     def weigh(unit):
         for low in range(0, total, 128):
             scores = scores_ref[unit % ring, :, low : low + 128]
-            weights = jnp.exp(scores - jnp.max(scores, axis=0, keepdims=True))
-            scale = 1.0 / jnp.sum(weights, axis=0, keepdims=True)
+            weights = jnp.exp(scores - top_rows(scores))
+            scale = 1.0 / sum_rows(weights)
             weights_ref[unit % ring, :, low : low + 128] = (weights * scale).astype(BF16)
 
     def attend(unit):
@@ -196,7 +247,7 @@
             pltpu.VMEM((4, total, total), BF16),
             pltpu.VMEM((step, total, inner), BF16),
         ],
-        compiler_params=params("arbitrary"),
+        compiler_params=params(8 + (total // 128) ** 2, "arbitrary"),
         cost_estimate=cost(10),
         name="attention",
     )(sources, normed, key_matrix, other_matrices)
@@ -218,10 +269,7 @@
             spreads.append(jnp.sum(kept, axis=0, keepdims=True))
         spread = jnp.concatenate(spreads, axis=1)
         updated = column.T * spread + matmul(final_ref[...], turned_ref[n])
-        centred = updated - jnp.mean(updated, axis=0, keepdims=True)
-        variance = jnp.mean(centred * centred, axis=0, keepdims=True)
-        normed = (centred * lax.rsqrt(variance + EPS)).astype(BF16)
-        projected = matmul(entry_ref[...], normed)
+        projected = matmul(entry_ref[...], normalise_rows(updated))
         right_ref[n] = projected[features:].astype(BF16)
         first = pl.multiple_of((step * residues + n) * features, features)
         for tile in range(total // 128):
@@ -266,7 +314,7 @@
             jax.ShapeDtypeStruct((residues, features, total), BF16),
         ],
         scratch_shapes=[pltpu.VMEM((total // 128, residues * features, 128), F32)],
-        compiler_params=params("arbitrary"),
+        compiler_params=params(16, "arbitrary"),
         cost_estimate=cost(4),
         name="alignment",
     )(high, low, turned, final_matrix, entry_matrices)
@@ -409,7 +457,7 @@
         pair_kernel,
         in_specs=[smem] * 2 + [vmem] * (5 + len(rights)) + [anywhere],
         out_specs=[anywhere] * 3,
-        out_shape=[whole, whole, sides],
+        out_shape=[whole, whole, pltpu.HBM(sides.shape, BF16)],
         scratch_shapes=[
             pltpu.VMEM((rows * TENSOR_FEATURES, columns * TENSOR_FEATURES), F32),
             pltpu.VMEM((2, 8 * 128, GROUP * depth), BF16),
@@ -421,7 +469,7 @@
             pltpu.VMEM(sides.shape, BF16),
             pltpu.SemaphoreType.DMA((2 * len(rights) + 5,)),
         ],
-        compiler_params=params(),
+        compiler_params=params(28),
         cost_estimate=cost(12),
         name="pair_update",
     )(
@@ -474,8 +522,8 @@
         grid=(channels // step,),
         in_specs=[pl.BlockSpec((devices, step, part, lanes), lambda c: (0, c, 0, 0))],
         out_specs=pl.BlockSpec((devices, step, part // 2, lanes), lambda c: (0, c, 0, 0)),
-        out_shape=jax.ShapeDtypeStruct((devices, channels, part // 2, lanes), BF16),
-        compiler_params=params("arbitrary"),
+        out_shape=pltpu.HBM((devices, channels, part // 2, lanes), BF16),
+        compiler_params=params(8, "arbitrary"),
         cost_estimate=cost(3),
         name="triangle_product",
     )(sides)
@@ -493,10 +541,7 @@
 
     for j in range(own):
         product = wide_ref[pl.ds(step * own + j, channels, stride=part), :]
-        centred = product - jnp.mean(product, axis=0, keepdims=True)
-        variance = jnp.mean(centred * centred, axis=0, keepdims=True)
-        normed = (centred * lax.rsqrt(variance + EPS)).astype(BF16).T
-        update = matmul(normed, final_ref[...])
+        update = matmul(normalise_rows(product).T, final_ref[...])
         for half in range(2):
             piece = update[half * rows : (half + 1) * rows]
             piece = mid_ref[half, j] + gate_ref[half, j] * piece
@@ -520,7 +565,7 @@
         out_specs=pl.BlockSpec((rows, 2, own, depth), lambda j: (0, 0, j, 0)),
         out_shape=jax.ShapeDtypeStruct((rows, 2, part, depth), F32),
         scratch_shapes=[pltpu.VMEM((channels * part, lanes), F32)],
-        compiler_params=params("arbitrary"),
+        compiler_params=params(12, "arbitrary"),
         cost_estimate=cost(4),
         name="pair_result",
     )(

time: 144 us -> 150 us (1.042)
  local copies, waits for them, and re-layouts: 6.92 us -> 27.7 us
  Pallas kernels: 43.1 us -> 34.8 us
  waiting for transfers between devices: 51.5 us -> 44.9 us
    unnamed x44 -> x60, local copies, waits for them, and re-layouts: 5.33 us -> 21.4 us
    all_to_all x1, waiting for transfers between devices: 10.6 us -> 7.68 us  [body(): product = lax.all_to_all(product, everywhere, split_axis=0, concat_axis=0)]
    gather x1, local copies, waits for them, and re-layouts: 0.61 us -> 2.79 us  [body(): gated = jnp.take(jnp.stack(gated), sources, axis=0)]
    pallas_call x1, Pallas kernels: 5.54 us -> 3.48 us  [alignment(): pl.pallas_call(alignment_kernel, grid=(residues // 2,), in_specs=[pl.Bloc...]
    pallas_call x1, Pallas kernels: 12.5 us -> 10.6 us  [attention(): pl.pallas_call(attention_kernel, grid=(residues // step,), in_specs=[pl.B...]
    all_to_all x1, waiting for transfers between devices: 1.9 us -> 0.01 us  [body(): low = lax.all_to_all(low, 'row', split_axis=0, concat_axis=0)]
    slice x2 -> x1, local copies, waits for them, and re-layouts: 0.01 us -> 1.67 us  [body(): attention_extra_matrices[:, inner:]]
    all_to_all x1, starting transfers between devices: 6.67 us -> 5.06 us  [body(): sides = lax.all_to_all(sides, everywhere, split_axis=0, concat_axis=0)]
  transfers between devices with their start and end apart: 15 -> 15, of which waited for: 10 -> 8; matrix products, arithmetic and copies ran while one was open for 7% -> 12% of each run, Pallas kernels for 12% -> 9%
where the time goes in v7:
time: 150 us; the launch traced here: 149 us
  waiting for transfers between devices  44.9 us (30%)
  Pallas kernels  34.8 us (23%)
  starting transfers between devices  33.6 us (22%)
  local copies, waits for them, and re-layouts  27.7 us (18%)
  other arithmetic  4.1 us (3%)
  matrix products  3.41 us (2%)
    ppermute x6, waiting for transfers between devices, exchange_rows(): arrived.append(lax.ppermute(pieces[shift], 'row', moves))  28 us
    unnamed x60, local copies, waits for them, and re-layouts  21.4 us
    pallas_call x1, Pallas kernels, attention(): pl.pallas_call(attention_kernel, grid=(residues // step,), in_specs=[pl.B...  10.6 us
    pallas_call x1, Pallas kernels, pair_update(): pl.pallas_call(pair_kernel, in_specs=[smem] * 2 + [vmem] * (5 + len(right...  10.3 us
    ppermute x6, starting transfers between devices, exchange_rows(): arrived.append(lax.ppermute(pieces[shift], 'row', moves))  9.95 us
    all_to_all x1, waiting for transfers between devices, body(): product = lax.all_to_all(product, everywhere, split_axis=0, concat_axis=0)  7.68 us
    ppermute x4, starting transfers between devices, gather_turned(): arrived.append(lax.ppermute(block, ('row', 'col'), moves))  6.7 us
    all_to_all x1, waiting for transfers between devices, body(): high = lax.all_to_all(high, 'row', split_axis=0, concat_axis=0)  5.39 us
  transfers between devices with their start and end apart: 15, of which 8 were waited for; matrix products, arithmetic and copies ran while one was open for 12% of the time, Pallas kernels for 9%

profile of v7, /device:TPU:0, one launch (start us, length us, event | category | flops | bytes accessed | tf_op | source)
XLA Modules:
  0.0 149.3 jit_solution(8579446827858203863)
XLA Ops:
  0.6 3.8 %standardise_high.1 = bf16[32,64,256]{2,1,0:T(8,128)(2,1)} custom-call(f32[64,32,256]{2,1,0:T(8,128)} %second_ref.1), custom_call_target="tpu_custom_call" | custom-call | flops 3000000000 | bytes 3000000 | tf_op jit(solution)/shard_map/standardise_high/pallas_call | solution.py:114
  4.4 0.0 copy-start.26
  4.4 0.0 copy-start.27
  4.4 5.3 %all-to-all-start = ((bf16[4,8,64,256]{3,2,1,0:T(8,128)(2,1)}), bf16[4,8,64,256]{3,2,1,0:T(8,128)(2,1)S(1)}, u32[]{:S(2)}, u32[]{:S(2)}) async-start(bf16[4,8,64,256]{3,2,1,0:T(8,128)(2,1)} %bitcast.44), calls=%async_computation | async-start | bytes 2097152 | tf_op jit(solution)/shard_map/all_to_all | solution.py:661
  9.8 0.7 copy.12
  10.5 0.1 copy.14
  10.7 1.7 %slice.6 = bf16[256,512]{1,0:T(8,128)(2,1)} slice(bf16[256,768]{1,0:T(8,128)(2,1)} %param.13), slice={[0:256], [256:768]} | slice | bytes 524288 | tf_op jit(solution)/shard_map/slice | solution.py:665
  12.4 1.1 copy.17
  13.5 0.1 pad_add_fusion.left_slots_ref
  13.6 1.7 %pad_maximum_fusion.2.others_ref = bf16[768,256]{1,0:T(8,128)(2,1)} fusion(bf16[512,256]{1,0:T(8,128)(2,1)S(1)} %bitcast.43, bf16[256,256]{1,0:T(8,128)(2,1)} %bitcast.47), kind=kLoop, calls=%fused_computation.8 | loop fusion | flops 786432 | bytes 786432 | tf_op jit(solution)/shard_map/concatenate | solution.py:664
  15.2 2.8 %standardise_low.1 = bf16[32,80,256]{2,1,0:T(8,128)(2,1)} custom-call(f32[64,32,256]{2,1,0:T(8,128)S(1)} %copy-done, f32[64,32,256]{2,1,0:T(8,128)S(1)} %copy-done), custom_call_target="tpu_custom_call" | custom-call | flops 3000000000 | bytes 3000000 | tf_op jit(solution)/shard_map/standardise_low/pallas_call | solution.py:155
  18.0 5.4 %all-to-all-done.normed_ref.high_ref = bf16[4,8,64,256]{3,2,1,0:T(8,128)(2,1)S(1)} async-done(((bf16[4,8,64,256]{3,2,1,0:T(8,128)(2,1)}), bf16[4,8,64,256]{3,2,1,0:T(8,128)(2,1)S(1)}, u32[]{:S(2)}, u32[]{:S(2)}) %all-to-all-start) | async-done | bytes 1048608 | tf_op jit(solution)/shard_map/all_to_all | solution.py:661
  23.4 1.0 copy-done.1
  24.4 3.5 %all-to-all-start.1 = ((bf16[4,8,80,256]{3,2,1,0:T(8,128)(2,1)}), bf16[4,8,80,256]{3,2,1,0:T(8,128)(2,1)S(1)}, u32[]{:S(2)}, u32[]{:S(2)}) async-start(bf16[4,8,80,256]{3,2,1,0:T(8,128)(2,1)} %bitcast.42), calls=%async_computation.1 | async-start | bytes 2621440 | tf_op jit(solution)/shard_map/all_to_all | solution.py:674
  27.9 1.5 %slice.7.key_ref = bf16[256,256]{1,0:T(8,128)(2,1)} slice(bf16[256,768]{1,0:T(8,128)(2,1)} %param.13), slice={[0:256], [0:256]} | slice | bytes 262144 | tf_op jit(solution)/shard_map/slice | solution.py:675
  29.5 1.7 %copy.15 = bf16[256,256]{0,1:T(8,128)(2,1)} copy(bf16[256,256]{1,0:T(8,128)(2,1)} %param.14) | data formatting | bytes 262144 | tf_op args[4]
  31.1 1.2 copy-done.2
  32.4 1.0 copy-done.4
  33.3 0.9 copy-done.8
  34.3 10.6 %attention.1 = (bf16[8,256,256]{2,1,0:T(8,128)(2,1)S(1)}, bf16[8,64,256]{2,1,0:T(8,128)(2,1)S(1)}, bf16[8,64,256]{2,1,0:T(8,128)(2,1)S(1)}, bf16[8,64,256]{2,1,0:T(8,128)(2,1)S(1)}, bf16[8,64,256]{2,1,0:T(8,128)(2,1)S(1)}) custom-call(s32[4]{0:T(128)S(1)} %get-tuple-element.34.sources_ref, bf16[4,8,64,256]{3,2,1,0:T(8,128)(2,1)S(1)} %copy-done.2, ...), custom_call_target="tpu_custom_call" | custom-call | flops 10000000000 | bytes 10000000 | tf_op jit(solution)/shard_map/attention/pallas_call | solution.py:233
  44.8 0.7 copy-done.5
  45.6 0.7 copy-done.11
  46.2 0.7 copy-done.12
  47.0 0.7 copy-done.13
  47.7 1.0 copy-done.21
  48.7 1.2 copy-done.3
  49.9 0.9 copy-done.7
  50.8 0.8 copy-done.14
  51.5 1.2 copy-done.22
  52.8 3.5 %alignment.1 = (bf16[256,256]{1,0:T(8,128)(2,1)S(1)}, bf16[8,32,256]{2,1,0:T(8,128)(2,1)S(1)}) custom-call(bf16[4,8,64,256]{3,2,1,0:T(8,128)(2,1)S(1)} %copy-done.3, bf16[4,8,80,256]{3,2,1,0:T(8,128)(2,1)S(1)} %all-to-all-done.1.low_ref, bf16[8,256,256]{2,1,0:T(8,128)(2,1)S(1)} %copy-done.22, bf16[256,256]{1,0:T(8,128)(2,1)S(1)} %bitcast.36, ...), custom_call_target="tpu_custom_call" | custom-call | flops 4000000000 | bytes 4000000 | tf_op jit(solution)/shard_map/alignment/pallas_call | solution.py:298
  56.3 3.7 %collective-permute-start.3 = (bf16[256,256]{1,0:T(8,128)(2,1)S(1)}, bf16[256,256]{1,0:T(8,128)(2,1)S(1)}, u32[]{:S(2)}, u32[]{:S(2)}) collective-permute-start(bf16[256,256]{1,0:T(8,128)(2,1)S(1)} %get-tuple-element.45), channel_id=1, source_target_pairs={{0,6},{1,7},{2,14},{3,15},{4,22},{5,23},{6,30},{7,31},{8,0},{9,1},... | collective-permute-start | bytes 393224 | tf_op jit(solution)/shard_map/ppermute | solution.py:595
  60.0 2.0 %collective-permute-start.2 = (bf16[256,256]{1,0:T(8,128)(2,1)S(1)}, bf16[256,256]{1,0:T(8,128)(2,1)S(1)}, u32[]{:S(2)}, u32[]{:S(2)}) collective-permute-start(bf16[256,256]{1,0:T(8,128)(2,1)S(1)} %get-tuple-element.45), channel_id=1, source_target_pairs={{0,4},{1,5},{2,12},{3,13},{4,20},{5,21},{6,28},{7,29},{8,6},{9,7},... | collective-permute-start | bytes 393224 | tf_op jit(solution)/shard_map/ppermute | solution.py:595
  62.0 0.2 collective-permute-start.1
  62.1 0.8 collective-permute-start
  63.0 5.7 %collective-permute-start.6 = (bf16[8,32,256]{2,1,0:T(8,128)(2,1)S(1)}, bf16[8,32,256]{2,1,0:T(8,128)(2,1)S(1)}, u32[]{:S(2)}, u32[]{:S(2)}) collective-permute-start(bf16[8,32,256]{2,1,0:T(8,128)(2,1)S(1)} %get-tuple-element.48.rest_0_), channel_id=1, source_target_pairs={{0,24},{8,16},{16,8},{24,0},{1,25},{9,17},{17,9},{25,1},{2,26},{10... | collective-permute-start | bytes 393224 | tf_op jit(solution)/shard_map/ppermute | solution.py:634
  68.7 0.6 collective-permute-start.4
  69.4 0.1 pad_maximum_fusion.1.own_ref
  69.4 5.9 %collective-permute-done.6.rest_3_ = bf16[8,32,256]{2,1,0:T(8,128)(2,1)S(1)} collective-permute-done((bf16[8,32,256]{2,1,0:T(8,128)(2,1)S(1)}, bf16[8,32,256]{2,1,0:T(8,128)(2,1)S(1)}, u32[]{:S(2)}, u32[]{:S(2)}) %collective-permute-start.6) | collective-permute-done | bytes 131104 | tf_op jit(solution)/shard_map/ppermute | solution.py:634
  75.3 1.4 collective-permute-done.4.rest_1_
  76.7 1.9 %collective-permute-done.7.other_ref = bf16[4,256,256]{2,1,0:T(8,128)(2,1)S(1)} collective-permute-done((bf16[4,256,256]{2,1,0:T(8,128)(2,1)S(1)}, bf16[4,256,256]{2,1,0:T(8,128)(2,1)S(1)}, u32[]{:S(2)}, u32[]{:S(2)}) %collective-permute-start.7) | collective-permute-done | bytes 524320 | tf_op jit(solution)/shard_map/ppermute | solution.py:582
  78.7 10.3 %pair_update.1 = (f32[32,64,128]{2,1,0:T(8,128)S(1)}, f32[32,64,128]{2,1,0:T(8,128)S(1)}, bf16[128,32,128]{2,1,0:T(8,128)(2,1)}) custom-call(s32[8]{0:T(128)S(1)} %pad_add_fusion.left_slots_ref, s32[4]{0:T(128)S(1)} %get-tuple-element.42.right_firsts_ref, bf16[4,256,256]{2,1,0:T(8,128)(2,1)S(1)} %pad_maximum_fusion.1.own_ref, ...), custom_call_target="tpu_custom_call" | custom-call | flops 12000000000 | bytes 12000000 | tf_op jit(solution)/shard_map/pair_update/pallas_call | solution.py:456
  88.9 1.0 copy-done.17
  89.9 1.0 copy-done.19
  90.9 5.1 %all-to-all-start.2 = ((bf16[32,4,32,128]{3,2,1,0:T(8,128)(2,1)}), bf16[32,4,32,128]{3,2,1,0:T(8,128)(2,1)S(1)}, u32[]{:S(2)}, u32[]{:S(2)}) async-start(bf16[32,4,32,128]{3,2,1,0:T(8,128)(2,1)} %bitcast.45), calls=%async_computation.2 | async-start | bytes 2097152 | tf_op jit(solution)/shard_map/all_to_all | solution.py:700
  96.0 1.8 %collective-permute-start.8 = (bf16[8,64,256]{2,1,0:T(8,128)(2,1)}, bf16[8,64,256]{2,1,0:T(8,128)(2,1)S(1)}, u32[]{:S(2)}, u32[]{:S(2)}) collective-permute-start(bf16[8,64,256]{2,1,0:T(8,128)(2,1)} %copy-done.13), channel_id=1, source_target_pairs={{0,8},{8,0},{16,24},{24,16},{1,9},{9,1},{17,25},{25,17},{2,10},{10... | collective-permute-start | bytes 786440 | tf_op jit(solution)/shard_map/ppermute | solution.py:634
  97.8 1.5 collective-permute-start.9
  99.3 0.3 collective-permute-start.10
  99.5 13.7 %collective-permute-done.8 = bf16[8,64,256]{2,1,0:T(8,128)(2,1)S(1)} collective-permute-done((bf16[8,64,256]{2,1,0:T(8,128)(2,1)}, bf16[8,64,256]{2,1,0:T(8,128)(2,1)S(1)}, u32[]{:S(2)}, u32[]{:S(2)}) %collective-permute-start.8) | collective-permute-done | bytes 262176 | tf_op jit(solution)/shard_map/ppermute | solution.py:634
  113.3 0.7 copy-done.24
  114.0 0.7 copy-done.25
  114.7 7.0 %collective-permute-done.10 = bf16[8,64,256]{2,1,0:T(8,128)(2,1)} collective-permute-done((bf16[8,64,256]{2,1,0:T(8,128)(2,1)}, bf16[8,64,256]{2,1,0:T(8,128)(2,1)}, u32[]{:S(2)}, u32[]{:S(2)}) %collective-permute-start.10) | collective-permute-done | bytes 262176 | tf_op jit(solution)/shard_map/ppermute | solution.py:634
  121.6 1.9 %all-to-all-done.2.sides_ref = bf16[32,4,32,128]{3,2,1,0:T(8,128)(2,1)S(1)} async-done(((bf16[32,4,32,128]{3,2,1,0:T(8,128)(2,1)}), bf16[32,4,32,128]{3,2,1,0:T(8,128)(2,1)S(1)}, u32[]{:S(2)}, u32[]{:S(2)}) %all-to-all-start.2) | async-done | bytes 1048608 | tf_op jit(solution)/shard_map/all_to_all | solution.py:700
  123.6 1.7 %triangle_product.1 = bf16[32,4,16,128]{3,2,1,0:T(8,128)(2,1)} custom-call(bf16[32,4,32,128]{3,2,1,0:T(8,128)(2,1)S(1)} %all-to-all-done.2.sides_ref), custom_call_target="tpu_custom_call" | custom-call | flops 3000000000 | bytes 3000000 | tf_op jit(solution)/shard_map/triangle_product/pallas_call | solution.py:520
  125.2 3.0 %all-to-all-start.3 = ((bf16[32,4,16,128]{3,2,1,0:T(8,128)(2,1)}), bf16[32,4,16,128]{3,2,1,0:T(8,128)(2,1)S(1)}, u32[]{:S(2)}, u32[]{:S(2)}) async-start(bf16[32,4,16,128]{3,2,1,0:T(8,128)(2,1)} %triangle_product.1), calls=%async_computation.3 | async-start | bytes 1048576 | tf_op jit(solution)/shard_map/all_to_all | solution.py:703
  128.3 0.1 broadcast_in_dim.16
  128.4 0.1 broadcast_in_dim.17
  128.5 0.0 copy-start.23
  128.5 2.2 %pad_maximum_fusion = bf16[4,8,64,256]{3,2,1,0:T(8,128)(2,1)} fusion(bf16[1,8,64,256]{3,2,1,0:T(8,128)(2,1)} %bitcast.16, bf16[1,8,64,256]{3,2,1,0:T(8,128)(2,1)} %bitcast.49, bf16[1,8,64,256]{3,2,1,0:T(8,128)(2,1)} %bitcast.48, bf16[1,8,64,256]{3,2,1,0:T(8,128)(2,1)S(1)} %bitcast.34), kind=kLoop, calls=%fused_computation.2 | loop fusion | flops 1572864 | bytes 2097152 | tf_op jit(solution)/shard_map/stack | solution.py:705
  130.7 2.8 %gather_fusion = bf16[4,8,64,256]{3,2,1,0:T(8,128)(2,1)} fusion(bf16[4,8,64,256]{3,2,1,0:T(8,128)(2,1)} %pad_maximum_fusion, s32[1024]{0:T(1024)S(1)} %pad_clamp_fusion), kind=kCustom, calls=%fused_computation | custom fusion | bytes 2097168 | tf_op jit(solution)/shard_map/jit(_take)/gather | solution.py:705
  133.5 3.4 %convolution_add_fusion = f32[64,32,256]{2,1,0:T(8,128)} fusion(f32[64,32,256]{2,1,0:T(8,128)S(1)} %copy-done, bf16[32,64,256]{2,1,0:T(8,128)(2,1)} %bitcast.41, pred[32]{0:T(512)(128)(4,1)S(1)} %broadcast_in_dim.17, bf16[256,256]{1,0:T(8,128)(2,1)S(1)} %copy-done.23), kind=kOutput, calls=%fused_computation.1 | convolution fusion | flops 269484032 | bytes 5373984 | tf_op jit(solution)/shard_map/dot_general | solution.py:707
  136.9 7.7 %all-to-all-done.3 = bf16[32,4,16,128]{3,2,1,0:T(8,128)(2,1)S(1)} async-done(((bf16[32,4,16,128]{3,2,1,0:T(8,128)(2,1)}), bf16[32,4,16,128]{3,2,1,0:T(8,128)(2,1)S(1)}, u32[]{:S(2)}, u32[]{:S(2)}) %all-to-all-start.3) | async-done | bytes 524320 | tf_op jit(solution)/shard_map/all_to_all | solution.py:703
  144.6 1.2 copy-done.18
  145.8 1.2 copy-done.20
  147.1 2.3 %pair_result.1 = f32[64,2,16,128]{3,2,1,0:T(8,128)} custom-call(bf16[128,16,128]{2,1,0:T(8,128)(2,1)S(1)} %bitcast.33, f32[2,16,64,128]{3,2,1,0:T(8,128)S(1)} %bitcast.39, f32[2,16,64,128]{3,2,1,0:T(8,128)S(1)} %bitcast.40, bf16[128,128]{1,0:T(8,128)(2,1)S(1)} %copy-done.16), custom_call_target="tpu_custom_call" | custom-call | flops 4000000000 | bytes 4000000 | tf_op jit(solution)/shard_map/pair_result/pallas_call | solution.py:556
  (50 shorter events, 0.2 us)
Async XLA Ops:
  4.4 5.3 %copy-start.26 = (bf16[256,256]{1,0:T(8,128)(2,1)S(1)}, bf16[256,256]{1,0:T(8,128)(2,1)}, u32[]{:S(2)}) copy-start(bf16[256,256]{1,0:T(8,128)(2,1)} %param.12) | copy-start | bytes 393220
  4.4 6.1 %copy-start.27 = (bf16[128,512]{1,0:T(8,128)(2,1)S(1)}, bf16[128,512]{1,0:T(8,128)(2,1)}, u32[]{:S(2)}) copy-start(bf16[128,512]{1,0:T(8,128)(2,1)} %param.17) | copy-start | bytes 393220
  4.4 10.8 %copy-start = (f32[64,32,256]{2,1,0:T(8,128)S(1)}, f32[64,32,256]{2,1,0:T(8,128)}, u32[]{:S(2)}) copy-start(f32[64,32,256]{2,1,0:T(8,128)} %second_ref.1) | copy-start | bytes 6291460
  4.4 18.9 %all-to-all-start = ((bf16[4,8,64,256]{3,2,1,0:T(8,128)(2,1)}), bf16[4,8,64,256]{3,2,1,0:T(8,128)(2,1)S(1)}, u32[]{:S(2)}, u32[]{:S(2)}) async-start(bf16[4,8,64,256]{3,2,1,0:T(8,128)(2,1)} %bitcast.44), calls=%async_computation | async-start | bytes 2097152 | tf_op jit(solution)/shard_map/all_to_all | solution.py:661
  23.4 1.0 copy-start.1
  24.4 24.3 %all-to-all-start.1 = ((bf16[4,8,80,256]{3,2,1,0:T(8,128)(2,1)}), bf16[4,8,80,256]{3,2,1,0:T(8,128)(2,1)S(1)}, u32[]{:S(2)}, u32[]{:S(2)}) async-start(bf16[4,8,80,256]{3,2,1,0:T(8,128)(2,1)} %bitcast.42), calls=%async_computation.1 | async-start | bytes 2621440 | tf_op jit(solution)/shard_map/all_to_all | solution.py:674
  31.1 1.2 copy-start.2
  32.4 1.0 copy-start.4
  33.3 0.9 copy-start.8
  44.8 0.7 copy-start.5
  45.6 0.7 copy-start.11
  46.2 0.7 copy-start.12
  47.0 0.7 copy-start.13
  47.7 1.0 copy-start.21
  48.6 1.2 copy-start.3
  49.9 0.9 copy-start.7
  50.8 0.8 copy-start.14
  51.5 1.2 copy-start.22
  52.8 25.9 %copy-start.9 = (f32[64,32,128]{2,1,0:T(8,128)S(1)}, f32[64,32,128]{2,1,0:T(8,128)}, u32[]{:S(2)}) copy-start(f32[64,32,128]{2,1,0:T(8,128)} %param.11) | copy-start | bytes 3145732
  52.8 25.9 %copy-start.10 = (bf16[1024,128]{1,0:T(8,128)(2,1)S(1)}, bf16[1024,128]{1,0:T(8,128)(2,1)}, u32[]{:S(2)}) copy-start(bf16[1024,128]{1,0:T(8,128)(2,1)} %rest_4_.1) | copy-start | bytes 786436
  52.8 25.9 %copy-start.15 = (bf16[128,128]{1,0:T(8,128)(2,1)S(1)}, bf16[128,128]{1,0:T(8,128)(2,1)}, u32[]{:S(2)}) copy-start(bf16[128,128]{1,0:T(8,128)(2,1)} %rest_6_.1) | copy-start | bytes 98308
  56.3 12.5 %collective-permute-start.3 = (bf16[256,256]{1,0:T(8,128)(2,1)S(1)}, bf16[256,256]{1,0:T(8,128)(2,1)S(1)}, u32[]{:S(2)}, u32[]{:S(2)}) collective-permute-start(bf16[256,256]{1,0:T(8,128)(2,1)S(1)} %get-tuple-element.45), channel_id=1, source_target_pairs={{0,6},{1,7},{2,14},{3,15},{4,22},{5,23},{6,30},{7,31},{8,0},{9,1},... | collective-permute-start | bytes 393224 | tf_op jit(solution)/shard_map/ppermute | solution.py:595
  60.0 8.8 %collective-permute-start.2 = (bf16[256,256]{1,0:T(8,128)(2,1)S(1)}, bf16[256,256]{1,0:T(8,128)(2,1)S(1)}, u32[]{:S(2)}, u32[]{:S(2)}) collective-permute-start(bf16[256,256]{1,0:T(8,128)(2,1)S(1)} %get-tuple-element.45), channel_id=1, source_target_pairs={{0,4},{1,5},{2,12},{3,13},{4,20},{5,21},{6,28},{7,29},{8,6},{9,7},... | collective-permute-start | bytes 393224 | tf_op jit(solution)/shard_map/ppermute | solution.py:595
  62.0 7.4 %collective-permute-start.1 = (bf16[256,256]{1,0:T(8,128)(2,1)S(1)}, bf16[256,256]{1,0:T(8,128)(2,1)S(1)}, u32[]{:S(2)}, u32[]{:S(2)}) collective-permute-start(bf16[256,256]{1,0:T(8,128)(2,1)S(1)} %get-tuple-element.45), channel_id=1, source_target_pairs={{0,2},{1,3},{2,10},{3,11},{4,18},{5,19},{6,26},{7,27},{8,4},{9,5},... | collective-permute-start | bytes 393224 | tf_op jit(solution)/shard_map/ppermute | solution.py:595
  62.1 7.3 %collective-permute-start = (bf16[256,256]{1,0:T(8,128)(2,1)S(1)}, bf16[256,256]{1,0:T(8,128)(2,1)S(1)}, u32[]{:S(2)}, u32[]{:S(2)}) collective-permute-start(bf16[256,256]{1,0:T(8,128)(2,1)S(1)} %get-tuple-element.45), channel_id=1, source_target_pairs={{0,0},{1,1},{2,8},{3,9},{4,16},{5,17},{6,24},{7,25},{8,2},{9,3},{1... | collective-permute-start | bytes 393224 | tf_op jit(solution)/shard_map/ppermute | solution.py:595
  63.0 12.4 %collective-permute-start.6 = (bf16[8,32,256]{2,1,0:T(8,128)(2,1)S(1)}, bf16[8,32,256]{2,1,0:T(8,128)(2,1)S(1)}, u32[]{:S(2)}, u32[]{:S(2)}) collective-permute-start(bf16[8,32,256]{2,1,0:T(8,128)(2,1)S(1)} %get-tuple-element.48.rest_0_), channel_id=1, source_target_pairs={{0,24},{8,16},{16,8},{24,0},{1,25},{9,17},{17,9},{25,1},{2,26},{10... | collective-permute-start | bytes 393224 | tf_op jit(solution)/shard_map/ppermute | solution.py:634
  68.7 6.6 %collective-permute-start.5 = (bf16[8,32,256]{2,1,0:T(8,128)(2,1)S(1)}, bf16[8,32,256]{2,1,0:T(8,128)(2,1)S(1)}, u32[]{:S(2)}, u32[]{:S(2)}) collective-permute-start(bf16[8,32,256]{2,1,0:T(8,128)(2,1)S(1)} %get-tuple-element.48.rest_0_), channel_id=1, source_target_pairs={{0,16},{8,24},{16,0},{24,8},{1,17},{9,25},{17,1},{25,9},{2,18},{10... | collective-permute-start | bytes 393224 | tf_op jit(solution)/shard_map/ppermute | solution.py:634
  68.7 8.0 %collective-permute-start.4 = (bf16[8,32,256]{2,1,0:T(8,128)(2,1)S(1)}, bf16[8,32,256]{2,1,0:T(8,128)(2,1)S(1)}, u32[]{:S(2)}, u32[]{:S(2)}) collective-permute-start(bf16[8,32,256]{2,1,0:T(8,128)(2,1)S(1)} %get-tuple-element.48.rest_0_), channel_id=1, source_target_pairs={{0,8},{8,0},{16,24},{24,16},{1,9},{9,1},{17,25},{25,17},{2,10},{10... | collective-permute-start | bytes 393224 | tf_op jit(solution)/shard_map/ppermute | solution.py:634
  76.7 1.9 %collective-permute-start.7 = (bf16[4,256,256]{2,1,0:T(8,128)(2,1)S(1)}, bf16[4,256,256]{2,1,0:T(8,128)(2,1)S(1)}, u32[]{:S(2)}, u32[]{:S(2)}) collective-permute-start(bf16[4,256,256]{2,1,0:T(8,128)(2,1)S(1)} %pad_maximum_fusion.1.own_ref), channel_id=1, source_target_pairs={{0,1},{1,0},{2,3},{3,2},{4,5},{5,4},{6,7},{7,6},{8,9},{9,8},{10,11... | collective-permute-start | bytes 1572872 | tf_op jit(solution)/shard_map/ppermute | solution.py:582
  88.9 1.0 copy-start.17
  89.9 1.0 copy-start.19
  90.9 32.7 %all-to-all-start.2 = ((bf16[32,4,32,128]{3,2,1,0:T(8,128)(2,1)}), bf16[32,4,32,128]{3,2,1,0:T(8,128)(2,1)S(1)}, u32[]{:S(2)}, u32[]{:S(2)}) async-start(bf16[32,4,32,128]{3,2,1,0:T(8,128)(2,1)} %bitcast.45), calls=%async_computation.2 | async-start | bytes 2097152 | tf_op jit(solution)/shard_map/all_to_all | solution.py:700
  96.0 32.5 %copy-start.6 = (bf16[8,64,256]{2,1,0:T(8,128)(2,1)S(1)}, bf16[8,64,256]{2,1,0:T(8,128)(2,1)}, u32[]{:S(2)}) copy-start(bf16[8,64,256]{2,1,0:T(8,128)(2,1)} %copy-done.5) | copy-start | bytes 786436
  96.0 17.3 %collective-permute-start.8 = (bf16[8,64,256]{2,1,0:T(8,128)(2,1)}, bf16[8,64,256]{2,1,0:T(8,128)(2,1)S(1)}, u32[]{:S(2)}, u32[]{:S(2)}) collective-permute-start(bf16[8,64,256]{2,1,0:T(8,128)(2,1)} %copy-done.13), channel_id=1, source_target_pairs={{0,8},{8,0},{16,24},{24,16},{1,9},{9,1},{17,25},{25,17},{2,10},{10... | collective-permute-start | bytes 786440 | tf_op jit(solution)/shard_map/ppermute | solution.py:634
  97.8 15.4 %collective-permute-start.9 = (bf16[8,64,256]{2,1,0:T(8,128)(2,1)}, bf16[8,64,256]{2,1,0:T(8,128)(2,1)S(1)}, u32[]{:S(2)}, u32[]{:S(2)}) collective-permute-start(bf16[8,64,256]{2,1,0:T(8,128)(2,1)} %copy-done.12), channel_id=1, source_target_pairs={{0,16},{8,24},{16,0},{24,8},{1,17},{9,25},{17,1},{25,9},{2,18},{10... | collective-permute-start | bytes 786440 | tf_op jit(solution)/shard_map/ppermute | solution.py:634
  99.3 22.4 %collective-permute-start.10 = (bf16[8,64,256]{2,1,0:T(8,128)(2,1)}, bf16[8,64,256]{2,1,0:T(8,128)(2,1)}, u32[]{:S(2)}, u32[]{:S(2)}) collective-permute-start(bf16[8,64,256]{2,1,0:T(8,128)(2,1)} %copy-done.11), channel_id=1, source_target_pairs={{0,24},{8,16},{16,8},{24,0},{1,25},{9,17},{17,9},{25,1},{2,26},{10... | collective-permute-start | bytes 786440 | tf_op jit(solution)/shard_map/ppermute | solution.py:634
  113.3 0.7 copy-start.24
  114.0 0.7 copy-start.25
  125.2 19.4 %all-to-all-start.3 = ((bf16[32,4,16,128]{3,2,1,0:T(8,128)(2,1)}), bf16[32,4,16,128]{3,2,1,0:T(8,128)(2,1)S(1)}, u32[]{:S(2)}, u32[]{:S(2)}) async-start(bf16[32,4,16,128]{3,2,1,0:T(8,128)(2,1)} %triangle_product.1), calls=%async_computation.3 | async-start | bytes 1048576 | tf_op jit(solution)/shard_map/all_to_all | solution.py:703
  128.5 5.1 %copy-start.23 = (bf16[256,256]{1,0:T(8,128)(2,1)S(1)}, bf16[256,256]{1,0:T(8,128)(2,1)}, u32[]{:S(2)}) copy-start(bf16[256,256]{1,0:T(8,128)(2,1)} %param.14) | copy-start | bytes 393220
  133.5 11.1 %copy-start.16 = (bf16[128,128]{1,0:T(8,128)(2,1)S(1)}, bf16[128,128]{1,0:T(8,128)(2,1)}, u32[]{:S(2)}) copy-start(bf16[128,128]{1,0:T(8,128)(2,1)} %final_ref.1) | copy-start | bytes 98308
  144.6 1.2 copy-start.18
  145.8 1.2 copy-start.20

commit v8 on v7

--- a/solution.py
+++ b/solution.py
@@ -76,8 +76,10 @@
     return centred * scale, variance * scale
 
 
-def high_kernel(block_hbm, high_hbm, first_ref, second_ref, high_ref, fetched, sent):
+def high_kernel(sources_ref, block_hbm, *rest):
+    *pieces_hbm, first_ref, second_ref, high_ref, fetched, sent = rest
     seqs, residues, lanes = first_ref.shape
+    own = residues // len(pieces_hbm)
     step = 16
     fetches, sends = [], []
     for s in range(0, seqs, step):
@@ -96,41 +98,44 @@
         second_rows = second_ref.at[chosen].reshape(step * residues, lanes)
         for n in range(residues):
             normed, _ = standardised_column(first_rows, second_rows, n, residues)
-            high_ref[n, chosen, :] = normed.astype(BF16)
-        sends.append(
-            pltpu.make_async_copy(
-                high_ref.at[:, chosen], high_hbm.at[:, chosen], sent.at[part]
+            high_ref[part, n] = normed.astype(BF16)
+        for p, piece_hbm in enumerate(pieces_hbm):
+            source = high_ref.at[part, pl.ds(sources_ref[p] * own, own)]
+            sends.append(
+                pltpu.make_async_copy(source, piece_hbm.at[:, chosen], sent.at[len(sends)])
             )
-        )
-        sends[-1].start()
+            sends[-1].start()
     for send in sends:
         send.wait()
 
 
-def standardise_high(block):
+def standardise_high(sources, block):
     seqs, residues, depth = block.shape
     half = depth // 2
-    anywhere = pl.BlockSpec(memory_space=pltpu.HBM)
+    count = sources.shape[0]
+    hbm = pl.BlockSpec(memory_space=pltpu.HBM)
     return pl.pallas_call(
         high_kernel,
-        in_specs=[anywhere],
-        out_specs=anywhere,
-        out_shape=pltpu.HBM((residues, seqs, depth), BF16),
+        in_specs=[pl.BlockSpec(memory_space=pltpu.SMEM), hbm],
+        out_specs=[hbm] * count,
+        out_shape=[pltpu.HBM((residues // count, seqs, depth), BF16)] * count,
         scratch_shapes=[
             pltpu.VMEM((seqs, residues, half), F32),
             pltpu.VMEM((seqs, residues, half), F32),
-            pltpu.VMEM((residues, seqs, depth), BF16),
+            pltpu.VMEM((seqs // 16, residues, 16, depth), BF16),
             pltpu.SemaphoreType.DMA((seqs // 8,)),
-            pltpu.SemaphoreType.DMA((seqs // 16,)),
+            pltpu.SemaphoreType.DMA((seqs // 16 * count,)),
         ],
         compiler_params=params(10),
         cost_estimate=cost(3),
         name="standardise_high",
-    )(pltpu.with_memory_space_constraint(block, pltpu.HBM))
-
-
-def low_kernel(first_ref, second_ref, low_ref):
+    )(sources, pltpu.with_memory_space_constraint(block, pltpu.HBM))
+
+
+def low_kernel(sources_ref, first_ref, second_ref, *rest):
+    *pieces_hbm, low_ref, sent = rest
     seqs, residues, lanes = first_ref.shape
+    own = residues // len(pieces_hbm)
     first_rows = first_ref.reshape(seqs * residues, lanes)
     second_rows = second_ref.reshape(seqs * residues, lanes)
     lane = lax.broadcasted_iota(jnp.int32, (seqs, 128), 1)
@@ -147,35 +152,51 @@
         kept = jnp.where(row == 0, coarse, jnp.where(row == 1, spread - coarse, 0.0))
         kept = jnp.concatenate([kept, jnp.zeros((16, 2 * lanes - seqs), F32)], axis=1)
         low_ref[n, seqs:, :] = kept.astype(BF16)
-
-
-def standardise_low(block):
+    sends = []
+    for p, piece_hbm in enumerate(pieces_hbm):
+        source = low_ref.at[pl.ds(sources_ref[p] * own, own)]
+        sends.append(pltpu.make_async_copy(source, piece_hbm, sent.at[p]))
+        sends[-1].start()
+    for send in sends:
+        send.wait()
+
+
+def standardise_low(sources, block):
     seqs, residues, depth = block.shape
     half = depth // 2
+    count = sources.shape[0]
+    hbm = pl.BlockSpec(memory_space=pltpu.HBM)
     return pl.pallas_call(
         low_kernel,
-        grid=(residues // 8,),
+        grid=(1,),
         in_specs=[
-            pl.BlockSpec((seqs, 8, half), lambda g: (0, g, 0)),
-            pl.BlockSpec((seqs, 8, half), lambda g: (0, g, 1)),
+            pl.BlockSpec(memory_space=pltpu.SMEM),
+            pl.BlockSpec((seqs, residues, half), lambda g: (0, 0, 0)),
+            pl.BlockSpec((seqs, residues, half), lambda g: (0, 0, 1)),
         ],
-        out_specs=pl.BlockSpec((8, seqs + 16, depth), lambda g: (g, 0, 0)),
-        out_shape=pltpu.HBM((residues, seqs + 16, depth), BF16),
-        compiler_params=params(10, "arbitrary"),
-        cost_estimate=cost(3),
+        out_specs=[hbm] * count,
+        out_shape=[pltpu.HBM((residues // count, seqs + 16, depth), BF16)] * count,
+        scratch_shapes=[
+            pltpu.VMEM((residues, seqs + 16, depth), BF16),
+            pltpu.SemaphoreType.DMA((count,)),
+        ],
+        compiler_params=params(14, "arbitrary"),
+        cost_estimate=cost(4),
         name="standardise_low",
-    )(block, block)
-
-
-def attention_kernel(sources_ref, normed_ref, key_ref, others_ref, turned_ref, *rest):
-    *gated_refs, scores_ref, weights_ref, back_ref = rest
-    blocks, residues, seqs, depth = normed_ref.shape
+    )(sources, block, block)
+
+
+def attention_kernel(key_ref, others_ref, *rest):
+    *refs, scores_ref, weights_ref = rest
+    blocks = len(refs) // 2
+    normed_refs, turned_ref, gated_refs = refs[:blocks], refs[blocks], refs[blocks + 1 :]
+    residues, seqs, _ = normed_refs[0].shape
     total = blocks * seqs
     inner = ATTENTION_UNITS * UNIT_WIDTH
     ring = scores_ref.shape[0]
     columns = []
     for n in range(residues):
-        column = normed_ref[:, n].reshape(total, depth)
+        column = jnp.concatenate([ref[n] for ref in normed_refs], axis=0)
         key_rows = matmul(column, key_ref[...]).astype(BF16)
         projected = matmul_nt(others_ref[...], column)
         queries = (projected[:inner] * UNIT_WIDTH ** (-0.5)).astype(BF16)
@@ -217,65 +238,74 @@
         if step >= 2:
             attend(step - 2)
     for n in range(residues):
-        back_ref[n] = turned_ref[n].T
-        for shift, gated_ref in enumerate(gated_refs):
-            first = pl.multiple_of(sources_ref[shift] * seqs, seqs)
-            gated_ref[n] = back_ref[n, pl.ds(first, seqs), :]
-
-
-def attention(sources, normed, key_matrix, other_matrices):
-    blocks, residues, seqs, depth = normed.shape
+        back = turned_ref[n].T
+        for block, gated_ref in enumerate(gated_refs):
+            gated_ref[n] = back[block * seqs : (block + 1) * seqs]
+
+
+def attention(normed, key_matrix, other_matrices):
+    blocks = len(normed)
+    residues, seqs, depth = normed[0].shape
     total = blocks * seqs
     inner = ATTENTION_UNITS * UNIT_WIDTH
     step = 2
-    gated = jax.ShapeDtypeStruct((residues, seqs, inner), BF16)
-    gated_spec = pl.BlockSpec((step, seqs, inner), lambda n: (n, 0, 0))
     return pl.pallas_call(
         attention_kernel,
         grid=(residues // step,),
         in_specs=[
-            pl.BlockSpec(memory_space=pltpu.SMEM),
-            pl.BlockSpec((blocks, step, seqs, depth), lambda n: (0, n, 0, 0)),
             pl.BlockSpec((depth, inner), lambda n: (0, 0)),
             pl.BlockSpec((3 * inner, depth), lambda n: (0, 0)),
-        ],
+        ]
+        + [pl.BlockSpec((step, seqs, depth), lambda n: (n, 0, 0))] * blocks,
         out_specs=[pl.BlockSpec((step, inner, total), lambda n: (n, 0, 0))]
-        + [gated_spec] * blocks,
-        out_shape=[jax.ShapeDtypeStruct((residues, inner, total), BF16)] + [gated] * blocks,
+        + [pl.BlockSpec((step, seqs, inner), lambda n: (n, 0, 0))] * blocks,
+        out_shape=[jax.ShapeDtypeStruct((residues, inner, total), BF16)]
+        + [pltpu.HBM((residues, seqs, inner), BF16)] * blocks,
         scratch_shapes=[
             pltpu.VMEM((4, total, total), F32),
             pltpu.VMEM((4, total, total), BF16),
-            pltpu.VMEM((step, total, inner), BF16),
         ],
         compiler_params=params(8 + (total // 128) ** 2, "arbitrary"),
         cost_estimate=cost(10),
         name="attention",
-    )(sources, normed, key_matrix, other_matrices)
-
-
-def alignment_kernel(
-    high_ref, low_ref, turned_ref, final_ref, entry_ref, left_ref, right_ref, rows_ref
-):
-    blocks, residues, seqs, depth = high_ref.shape
+    )(key_matrix, other_matrices, *normed)
+
+
+def alignment_kernel(sources_ref, turned_ref, final_ref, entry_ref, *rest):
+    *refs, left_ref, right_ref, rows_ref = rest
+    blocks = len(refs) // 2
+    high_refs, low_refs = refs[:blocks], refs[blocks:]
+    residues, seqs, depth = high_refs[0].shape
     total = blocks * seqs
     features = TENSOR_FEATURES
     step = pl.program_id(0)
     for n in range(residues):
-        low = low_ref[:, n, :seqs, :].reshape(total, depth)
-        column = high_ref[:, n].reshape(total, depth).astype(F32) + low.astype(F32)
+        column = jnp.concatenate([ref[n] for ref in high_refs], axis=0).astype(F32)
+        column = column + jnp.concatenate(
+            [ref[n, :seqs, :] for ref in low_refs], axis=0
+        ).astype(F32)
         spreads = []
-        for block in range(blocks):
-            kept = low_ref[block, n, seqs:, :seqs].astype(F32)
+        for ref in low_refs:
+            kept = ref[n, seqs:, :seqs].astype(F32)
             spreads.append(jnp.sum(kept, axis=0, keepdims=True))
         spread = jnp.concatenate(spreads, axis=1)
         updated = column.T * spread + matmul(final_ref[...], turned_ref[n])
         projected = matmul(entry_ref[...], normalise_rows(updated))
-        right_ref[n] = projected[features:].astype(BF16)
+        me = sources_ref[0]
+        tiles = [projected[:, low : low + 128] for low in range(0, total, 128)]
+        odd = lax.rem(me, 2) == 1
+        tiles = [jnp.where(odd, pltpu.roll(tile, seqs, 1), tile) for tile in tiles]
+        width = 1
+        while width < len(tiles):
+            crossed = lax.rem(lax.div(me, 2 * width), 2) == 1
+            tiles = [
+                jnp.where(crossed, tiles[t ^ width], tiles[t]) for t in range(len(tiles))
+            ]
+            width *= 2
         first = pl.multiple_of((step * residues + n) * features, features)
-        for tile in range(total // 128):
-            rows_ref[tile, pl.ds(first, features), :] = projected[
-                :features, tile * 128 : (tile + 1) * 128
-            ]
+        for t, tile in enumerate(tiles):
+            right_ref[n, :, t * 128 : (t + 1) * 128] = tile[features:].astype(BF16)
+            rows_ref[t, pl.ds(first, features), :] = tile[:features]
 
     @pl.when(step == pl.num_programs(0) - 1)
     def _():
@@ -291,20 +321,22 @@
             left_ref[c * count : (c + together) * count, :] = piece
 
 
-def alignment(high, low, turned, final_matrix, entry_matrices):
-    blocks, residues, seqs, depth = high.shape
+def alignment(sources, high, low, turned, final_matrix, entry_matrices):
+    blocks = len(high)
+    residues, seqs, depth = high[0].shape
     total = blocks * seqs
     features = TENSOR_FEATURES
     return pl.pallas_call(
         alignment_kernel,
         grid=(residues // 2,),
         in_specs=[
-            pl.BlockSpec((blocks, 2, seqs, depth), lambda n: (0, n, 0, 0)),
-            pl.BlockSpec((blocks, 2, seqs + 16, depth), lambda n: (0, n, 0, 0)),
+            pl.BlockSpec(memory_space=pltpu.SMEM),
             pl.BlockSpec((2, depth, total), lambda n: (n, 0, 0)),
             pl.BlockSpec(final_matrix.shape, lambda n: (0, 0)),
             pl.BlockSpec(entry_matrices.shape, lambda n: (0, 0)),
-        ],
+        ]
+        + [pl.BlockSpec((2, seqs, depth), lambda n: (n, 0, 0))] * blocks
+        + [pl.BlockSpec((2, seqs + 16, depth), lambda n: (n, 0, 0))] * blocks,
         out_specs=[
             pl.BlockSpec((features * residues, total), lambda n: (0, 0)),
             pl.BlockSpec((2, features, total), lambda n: (n, 0, 0)),
@@ -317,7 +349,7 @@
         compiler_params=params(16, "arbitrary"),
         cost_estimate=cost(4),
         name="alignment",
-    )(high, low, turned, final_matrix, entry_matrices)
+    )(sources, turned, final_matrix, entry_matrices, *high, *low)
 
 
 def pair_kernel(
@@ -457,7 +489,7 @@
         pair_kernel,
         in_specs=[smem] * 2 + [vmem] * (5 + len(rights)) + [anywhere],
         out_specs=[anywhere] * 3,
-        out_shape=[whole, whole, pltpu.HBM(sides.shape, BF16)],
+        out_shape=[pltpu.HBM(whole.shape, F32)] * 2 + [pltpu.HBM(sides.shape, BF16)],
         scratch_shapes=[
             pltpu.VMEM((rows * TENSOR_FEATURES, columns * TENSOR_FEATURES), F32),
             pltpu.VMEM((2, 8 * 128, GROUP * depth), BF16),
@@ -570,8 +602,8 @@
         name="pair_result",
     )(
         product,
-        mid.reshape(2, part, rows, depth),
-        gate.reshape(2, part, rows, depth),
+        pltpu.with_memory_space_constraint(mid.reshape(2, part, rows, depth), pltpu.HBM),
+        pltpu.with_memory_space_constraint(gate.reshape(2, part, rows, depth), pltpu.HBM),
         final_matrix,
     )
     return out.reshape(rows, columns, depth)
@@ -656,25 +688,27 @@
     row_count = lax.axis_size("row")
     seqs, residues, depth = homolog_tensor.shape
     own_residues = residues // row_count
-    high = standardise_high(homolog_tensor)
-    high = high.reshape(row_count, own_residues, seqs, depth)
-    high = lax.all_to_all(high, "row", split_axis=0, concat_axis=0)
-    low = standardise_low(homolog_tensor)
-    low = low.reshape(row_count, own_residues, seqs + 16, depth)
+    sources = lax.axis_index("row") ^ jnp.arange(row_count, dtype=jnp.int32)
+    high = exchange_rows(standardise_high(sources, homolog_tensor))
+    low = standardise_low(sources, homolog_tensor)
     others = jnp.concatenate(
         [attention_probe_matrix.T, attention_extra_matrices[:, inner:].T], axis=0
     )
-    entries = paired_entries(incoming_entry_matrices)
-    sources = lax.axis_index("row") ^ jnp.arange(row_count, dtype=jnp.int32)
-    firsts = sources * own_residues
-    slots = left_groups(row_count, own_residues)
-    high, low, others, entries, sources, firsts, slots = lax.optimization_barrier(
-        (high, low, others, entries, sources, firsts, slots)
-    )
-    low = lax.all_to_all(low, "row", split_axis=0, concat_axis=0)
-    turned, *gated = attention(sources, high, attention_extra_matrices[:, :inner], others)
+    early = (
+        attention_extra_matrices[:, :inner],
+        others,
+        attention_final_matrix.T,
+        tensor_entry_matrices.T,
+        paired_entries(incoming_entry_matrices),
+        sources * own_residues,
+        left_groups(row_count, own_residues),
+    )
+    high, low, early = lax.optimization_barrier((high, low, early))
+    key_matrix, others, final_turned, tensor_turned, entries, firsts, slots = early
+    low = exchange_rows(low)
+    turned, *gated = attention(high, key_matrix, others)
     left_piece, right_piece = alignment(
-        high, low, turned, attention_final_matrix.T, tensor_entry_matrices.T
+        sources, high, low, turned, final_turned, tensor_turned
     )
 
     rights = exchange_rows([right_piece] * row_count)

time: 150 us -> 132 us (0.88)
  local copies, waits for them, and re-layouts: 27.7 us -> 9.1 us
  Pallas kernels: 34.8 us -> 38 us
  waiting for transfers between devices: 44.9 us -> 42.3 us
    unnamed x60 -> x32, local copies, waits for them, and re-layouts: 21.4 us -> 4.34 us
    all_to_all x2 -> x0, starting transfers between devices: 8.85 us -> none  [the longest x1 5.31 us: body(): high = lax.all_to_all(high, 'row', split_axis=0, concat_axis=0)]
    ppermute x6 -> x12, starting transfers between devices: 9.95 us -> 16.1 us  [exchange_rows(): arrived.append(lax.ppermute(pieces[shift], 'row', moves))]
    all_to_all x2 -> x0, waiting for transfers between devices: 5.39 us -> none  [the longest x1 5.39 us: body(): high = lax.all_to_all(high, 'row', split_axis=0, concat_axis=0)]
    ppermute x4, starting transfers between devices: 6.7 us -> 10.7 us  [gather_turned(): arrived.append(lax.ppermute(block, ('row', 'col'), moves))]
    pallas_call x2, Pallas kernels: 6.53 us -> 8.99 us  [the longest x1 4.52 us: standardise_low(): pl.pallas_call(low_kernel, grid=(1,), in_specs=[pl.BlockSpec(memory_space...]
    ppermute x4, waiting for transfers between devices: 0.01 us -> 1.75 us  [gather_turned(): arrived.append(lax.ppermute(block, ('row', 'col'), moves))]
    slice x1, local copies, waits for them, and re-layouts: 1.55 us -> 0.01 us  [body(): attention_extra_matrices[:, :inner]]
  transfers between devices with their start and end apart: 15 -> 19, of which waited for: 8 -> 10; matrix products, arithmetic and copies ran while one was open for 12% -> 11% of each run, Pallas kernels for 9% -> 12%
where the time goes in v8:
time: 132 us; the launch traced here: 131 us
  waiting for transfers between devices  42.3 us (32%)
  Pallas kernels  38 us (29%)
  starting transfers between devices  34.1 us (26%)
  local copies, waits for them, and re-layouts  9.1 us (7%)
  matrix products  3.41 us (3%)
  other arithmetic  3.36 us (3%)
    ppermute x12, waiting for transfers between devices, exchange_rows(): arrived.append(lax.ppermute(pieces[shift], 'row', moves))  29.1 us
    ppermute x12, starting transfers between devices, exchange_rows(): arrived.append(lax.ppermute(pieces[shift], 'row', moves))  16.1 us
    ppermute x4, starting transfers between devices, gather_turned(): arrived.append(lax.ppermute(block, ('row', 'col'), moves))  10.7 us
    pallas_call x1, Pallas kernels, attention(): pl.pallas_call(attention_kernel, grid=(residues // step,), in_specs=[pl.B...  10.6 us
    pallas_call x1, Pallas kernels, pair_update(): pl.pallas_call(pair_kernel, in_specs=[smem] * 2 + [vmem] * (5 + len(right...  9.3 us
    all_to_all x1, waiting for transfers between devices, body(): product = lax.all_to_all(product, everywhere, split_axis=0, concat_axis=0)  7.66 us
    pallas_call x1, Pallas kernels, standardise_low(): pl.pallas_call(low_kernel, grid=(1,), in_specs=[pl.BlockSpec(memory_space...  4.52 us
    pallas_call x1, Pallas kernels, standardise_high(): pl.pallas_call(high_kernel, in_specs=[pl.BlockSpec(memory_space=pltpu.SME...  4.47 us
  transfers between devices with their start and end apart: 19, of which 10 were waited for; matrix products, arithmetic and copies ran while one was open for 11% of the time, Pallas kernels for 12%

profile of v8, /device:TPU:0, one launch (start us, length us, event | category | flops | bytes accessed | tf_op | source)
XLA Modules:
  0.0 131.3 jit_solution(7282534819921238011)
XLA Ops:
  0.6 0.0 copy-start.9
  0.7 0.0 copy-start.13
  0.7 4.5 %standardise_high.1 = (bf16[8,64,256]{2,1,0:T(8,128)(2,1)}, bf16[8,64,256]{2,1,0:T(8,128)(2,1)}, bf16[8,64,256]{2,1,0:T(8,128)(2,1)}, bf16[8,64,256]{2,1,0:T(8,128)(2,1)}) custom-call(s32[4]{0:T(128)S(1)} %iota_xor_fusion.sources_ref, f32[64,32,256]{2,1,0:T(8,128)} %second_ref.1), custom_call_target="tpu_custom_call" | custom-call | flops 3000000000 | bytes 3000000 | tf_op jit(solution)/shard_map/standardise_high/pallas_call | solution.py:117
  5.1 0.0 copy-start
  5.2 3.0 %collective-permute-start = (bf16[8,64,256]{2,1,0:T(8,128)(2,1)}, bf16[8,64,256]{2,1,0:T(8,128)(2,1)S(1)}, u32[]{:S(2)}, u32[]{:S(2)}) collective-permute-start(bf16[8,64,256]{2,1,0:T(8,128)(2,1)} %get-tuple-element.51), channel_id=1, source_target_pairs={{0,8},{8,0},{16,24},{24,16},{1,9},{9,1},{17,25},{25,17},{2,10},{10... | collective-permute-start | bytes 786440 | tf_op jit(solution)/shard_map/ppermute | solution.py:666
  8.2 1.5 %collective-permute-start.1 = (bf16[8,64,256]{2,1,0:T(8,128)(2,1)}, bf16[8,64,256]{2,1,0:T(8,128)(2,1)S(1)}, u32[]{:S(2)}, u32[]{:S(2)}) collective-permute-start(bf16[8,64,256]{2,1,0:T(8,128)(2,1)} %get-tuple-element.52), channel_id=1, source_target_pairs={{0,16},{8,24},{16,0},{24,8},{1,17},{9,25},{17,1},{25,9},{2,18},{10... | collective-permute-start | bytes 786440 | tf_op jit(solution)/shard_map/ppermute | solution.py:666
  9.7 0.0 collective-permute-start.2
  9.7 0.7 slice.7
  10.5 1.1 copy.17
  11.6 0.8 copy.12
  12.3 0.9 reshape.56
  13.3 0.1 copy.15
  13.4 1.0 copy.14
  14.5 0.1 pad_add_fusion.left_slots_ref
  14.5 0.9 pad_maximum_fusion.2.others_ref
  15.5 4.5 %standardise_low.1 = (bf16[8,80,256]{2,1,0:T(8,128)(2,1)}, bf16[8,80,256]{2,1,0:T(8,128)(2,1)}, bf16[8,80,256]{2,1,0:T(8,128)(2,1)}, bf16[8,80,256]{2,1,0:T(8,128)(2,1)}) custom-call(s32[4]{0:T(128)S(1)} %iota_xor_fusion.sources_ref, f32[64,32,256]{2,1,0:T(8,128)S(1)} %copy-done, f32[64,32,256]{2,1,0:T(8,128)S(1)} %copy-done), custom_call_target="tpu_custom_call" | custom-call | flops 4000000000 | bytes 4000000 | tf_op jit(solution)/shard_map/standardise_low/pallas_call | solution.py:169
  20.0 0.0 collective-permute-done.rest_1_
  20.0 1.7 %collective-permute-done.1.rest_2_ = bf16[8,64,256]{2,1,0:T(8,128)(2,1)S(1)} collective-permute-done((bf16[8,64,256]{2,1,0:T(8,128)(2,1)}, bf16[8,64,256]{2,1,0:T(8,128)(2,1)S(1)}, u32[]{:S(2)}, u32[]{:S(2)}) %collective-permute-start.1) | collective-permute-done | bytes 262176 | tf_op jit(solution)/shard_map/ppermute | solution.py:666
  21.8 0.0 collective-permute-done.2.rest_3_
  21.8 1.2 collective-permute-start.3
  23.0 0.9 collective-permute-start.4
  23.9 1.4 %collective-permute-start.5 = (bf16[8,80,256]{2,1,0:T(8,128)(2,1)}, bf16[8,80,256]{2,1,0:T(8,128)(2,1)S(1)}, u32[]{:S(2)}, u32[]{:S(2)}) collective-permute-start(bf16[8,80,256]{2,1,0:T(8,128)(2,1)} %get-tuple-element.76), channel_id=1, source_target_pairs={{0,24},{8,16},{16,8},{24,0},{1,25},{9,17},{17,9},{25,1},{2,26},{10... | collective-permute-start | bytes 983048 | tf_op jit(solution)/shard_map/ppermute | solution.py:666
  25.3 10.6 %attention.1 = (bf16[8,256,256]{2,1,0:T(8,128)(2,1)S(1)}, bf16[8,64,256]{2,1,0:T(8,128)(2,1)}, bf16[8,64,256]{2,1,0:T(8,128)(2,1)}, bf16[8,64,256]{2,1,0:T(8,128)(2,1)}, bf16[8,64,256]{2,1,0:T(8,128)(2,1)}) custom-call(bf16[256,256]{1,0:T(8,128)(2,1)S(1)} %slice.6.key_ref, bf16[768,256]{1,0:T(8,128)(2,1)S(1)} %pad_maximum_fusion.2.others_ref, ...), custom_call_target="tpu_custom_call" | custom-call | flops 10000000000 | bytes 10000000 | tf_op jit(solution)/shard_map/attention/pallas_call | solution.py:252
  35.9 2.6 %collective-permute-done.4.rest_6_ = bf16[8,80,256]{2,1,0:T(8,128)(2,1)S(1)} collective-permute-done((bf16[8,80,256]{2,1,0:T(8,128)(2,1)}, bf16[8,80,256]{2,1,0:T(8,128)(2,1)S(1)}, u32[]{:S(2)}, u32[]{:S(2)}) %collective-permute-start.4) | collective-permute-done | bytes 327712 | tf_op jit(solution)/shard_map/ppermute | solution.py:666
  38.5 0.0 collective-permute-done.5.rest_7_
  38.5 0.0 copy-start.1
  38.6 0.0 copy-start.2
  38.6 0.0 copy-start.4
  38.6 4.2 %alignment.1 = (bf16[256,256]{1,0:T(8,128)(2,1)S(1)}, bf16[8,32,256]{2,1,0:T(8,128)(2,1)S(1)}) custom-call(s32[4]{0:T(128)S(1)} %iota_xor_fusion.sources_ref, bf16[8,256,256]{2,1,0:T(8,128)(2,1)S(1)} %get-tuple-element.70.turned_ref, bf16[256,256]{1,0:T(8,128)(2,1)S(1)} %bitcast.35, bf16[64,256]{1,0:T(8,128)(2,1)S(1)} %bitcast.37, ...), custom_call_target="tpu_custom_call" | custom-call | flops 4000000000 | bytes 4000000 | tf_op jit(solution)/shard_map/alignment/pallas_call | solution.py:329
  42.8 0.7 collective-permute-start.6
  43.5 3.3 %collective-permute-start.7 = (bf16[256,256]{1,0:T(8,128)(2,1)S(1)}, bf16[256,256]{1,0:T(8,128)(2,1)S(1)}, u32[]{:S(2)}, u32[]{:S(2)}) collective-permute-start(bf16[256,256]{1,0:T(8,128)(2,1)S(1)} %get-tuple-element.77), channel_id=1, source_target_pairs={{0,2},{1,3},{2,10},{3,11},{4,18},{5,19},{6,26},{7,27},{8,4},{9,5},... | collective-permute-start | bytes 393224 | tf_op jit(solution)/shard_map/ppermute | solution.py:627
  46.8 3.5 %collective-permute-start.8 = (bf16[256,256]{1,0:T(8,128)(2,1)S(1)}, bf16[256,256]{1,0:T(8,128)(2,1)S(1)}, u32[]{:S(2)}, u32[]{:S(2)}) collective-permute-start(bf16[256,256]{1,0:T(8,128)(2,1)S(1)} %get-tuple-element.77), channel_id=1, source_target_pairs={{0,4},{1,5},{2,12},{3,13},{4,20},{5,21},{6,28},{7,29},{8,6},{9,7},... | collective-permute-start | bytes 393224 | tf_op jit(solution)/shard_map/ppermute | solution.py:627
  50.3 3.2 %collective-permute-start.9 = (bf16[256,256]{1,0:T(8,128)(2,1)S(1)}, bf16[256,256]{1,0:T(8,128)(2,1)S(1)}, u32[]{:S(2)}, u32[]{:S(2)}) collective-permute-start(bf16[256,256]{1,0:T(8,128)(2,1)S(1)} %get-tuple-element.77), channel_id=1, source_target_pairs={{0,6},{1,7},{2,14},{3,15},{4,22},{5,23},{6,30},{7,31},{8,0},{9,1},... | collective-permute-start | bytes 393224 | tf_op jit(solution)/shard_map/ppermute | solution.py:627
  53.5 0.1 collective-permute-start.10
  53.7 0.0 collective-permute-done.6
  53.7 4.3 %collective-permute-start.11 = (bf16[8,32,256]{2,1,0:T(8,128)(2,1)S(1)}, bf16[8,32,256]{2,1,0:T(8,128)(2,1)S(1)}, u32[]{:S(2)}, u32[]{:S(2)}) collective-permute-start(bf16[8,32,256]{2,1,0:T(8,128)(2,1)S(1)} %get-tuple-element.80.rest_0_), channel_id=1, source_target_pairs={{0,16},{8,24},{16,0},{24,8},{1,17},{9,25},{17,1},{25,9},{2,18},{10... | collective-permute-start | bytes 393224 | tf_op jit(solution)/shard_map/ppermute | solution.py:666
  58.0 0.0 collective-permute-done.7
  58.0 0.0 collective-permute-start.12
  58.0 1.7 %collective-permute-done.9 = bf16[256,256]{1,0:T(8,128)(2,1)S(1)} collective-permute-done((bf16[256,256]{1,0:T(8,128)(2,1)S(1)}, bf16[256,256]{1,0:T(8,128)(2,1)S(1)}, u32[]{:S(2)}, u32[]{:S(2)}) %collective-permute-start.9) | collective-permute-done | bytes 131104 | tf_op jit(solution)/shard_map/ppermute | solution.py:627
  59.7 0.1 pad_maximum_fusion.1.own_ref
  59.8 1.3 %collective-permute-done.10.rest_1_ = bf16[8,32,256]{2,1,0:T(8,128)(2,1)S(1)} collective-permute-done((bf16[8,32,256]{2,1,0:T(8,128)(2,1)S(1)}, bf16[8,32,256]{2,1,0:T(8,128)(2,1)S(1)}, u32[]{:S(2)}, u32[]{:S(2)}) %collective-permute-start.10) | collective-permute-done | bytes 131104 | tf_op jit(solution)/shard_map/ppermute | solution.py:666
  61.1 2.7 %collective-permute-done.12.rest_3_ = bf16[8,32,256]{2,1,0:T(8,128)(2,1)S(1)} collective-permute-done((bf16[8,32,256]{2,1,0:T(8,128)(2,1)S(1)}, bf16[8,32,256]{2,1,0:T(8,128)(2,1)S(1)}, u32[]{:S(2)}, u32[]{:S(2)}) %collective-permute-start.12) | collective-permute-done | bytes 131104 | tf_op jit(solution)/shard_map/ppermute | solution.py:666
  63.8 1.9 %collective-permute-done.13.other_ref = bf16[4,256,256]{2,1,0:T(8,128)(2,1)S(1)} collective-permute-done((bf16[4,256,256]{2,1,0:T(8,128)(2,1)S(1)}, bf16[4,256,256]{2,1,0:T(8,128)(2,1)S(1)}, u32[]{:S(2)}, u32[]{:S(2)}) %collective-permute-start.13) | collective-permute-done | bytes 524320 | tf_op jit(solution)/shard_map/ppermute | solution.py:614
  65.8 9.3 %pair_update.1 = (f32[32,64,128]{2,1,0:T(8,128)}, f32[32,64,128]{2,1,0:T(8,128)}, bf16[128,32,128]{2,1,0:T(8,128)(2,1)}) custom-call(s32[8]{0:T(128)S(1)} %pad_add_fusion.left_slots_ref, s32[4]{0:T(128)S(1)} %broadcast_multiply_fusion.right_firsts_ref, bf16[4,256,256]{2,1,0:T(8,128)(2,1)S(1)} %pad_maximum_fusion.1.own_ref, ...), custom_call_target="tpu_custom_call" | custom-call | flops 12000000000 | bytes 12000000 | tf_op jit(solution)/shard_map/pair_update/pallas_call | solution.py:488
  75.1 4.3 %all-to-all-start = ((bf16[32,4,32,128]{3,2,1,0:T(8,128)(2,1)}), bf16[32,4,32,128]{3,2,1,0:T(8,128)(2,1)S(1)}, u32[]{:S(2)}, u32[]{:S(2)}) async-start(bf16[32,4,32,128]{3,2,1,0:T(8,128)(2,1)} %bitcast.40), calls=%async_computation | async-start | bytes 2097152 | tf_op jit(solution)/shard_map/all_to_all | solution.py:734
  79.3 1.8 %collective-permute-start.14 = (bf16[8,64,256]{2,1,0:T(8,128)(2,1)}, bf16[8,64,256]{2,1,0:T(8,128)(2,1)S(1)}, u32[]{:S(2)}, u32[]{:S(2)}) collective-permute-start(bf16[8,64,256]{2,1,0:T(8,128)(2,1)} %get-tuple-element.87), channel_id=1, source_target_pairs={{0,8},{8,0},{16,24},{24,16},{1,9},{9,1},{17,25},{25,17},{2,10},{10... | collective-permute-start | bytes 786440 | tf_op jit(solution)/shard_map/ppermute | solution.py:666
  81.2 1.5 %collective-permute-start.15 = (bf16[8,64,256]{2,1,0:T(8,128)(2,1)}, bf16[8,64,256]{2,1,0:T(8,128)(2,1)S(1)}, u32[]{:S(2)}, u32[]{:S(2)}) collective-permute-start(bf16[8,64,256]{2,1,0:T(8,128)(2,1)} %get-tuple-element.88), channel_id=1, source_target_pairs={{0,16},{8,24},{16,0},{24,8},{1,17},{9,25},{17,1},{25,9},{2,18},{10... | collective-permute-start | bytes 786440 | tf_op jit(solution)/shard_map/ppermute | solution.py:666
  82.6 0.3 collective-permute-start.16
  82.9 13.7 %collective-permute-done.14 = bf16[8,64,256]{2,1,0:T(8,128)(2,1)S(1)} collective-permute-done((bf16[8,64,256]{2,1,0:T(8,128)(2,1)}, bf16[8,64,256]{2,1,0:T(8,128)(2,1)S(1)}, u32[]{:S(2)}, u32[]{:S(2)}) %collective-permute-start.14) | collective-permute-done | bytes 262176 | tf_op jit(solution)/shard_map/ppermute | solution.py:666
  96.6 0.0 collective-permute-done.15
  96.6 0.7 copy-done.11
  97.3 0.7 copy-done.12
  98.0 7.0 %collective-permute-done.16 = bf16[8,64,256]{2,1,0:T(8,128)(2,1)} collective-permute-done((bf16[8,64,256]{2,1,0:T(8,128)(2,1)}, bf16[8,64,256]{2,1,0:T(8,128)(2,1)}, u32[]{:S(2)}, u32[]{:S(2)}) %collective-permute-start.16) | collective-permute-done | bytes 262176 | tf_op jit(solution)/shard_map/ppermute | solution.py:666
  105.0 1.9 %all-to-all-done.sides_ref = bf16[32,4,32,128]{3,2,1,0:T(8,128)(2,1)S(1)} async-done(((bf16[32,4,32,128]{3,2,1,0:T(8,128)(2,1)}), bf16[32,4,32,128]{3,2,1,0:T(8,128)(2,1)S(1)}, u32[]{:S(2)}, u32[]{:S(2)}) %all-to-all-start) | async-done | bytes 1048608 | tf_op jit(solution)/shard_map/all_to_all | solution.py:734
  106.9 1.7 %triangle_product.1 = bf16[32,4,16,128]{3,2,1,0:T(8,128)(2,1)} custom-call(bf16[32,4,32,128]{3,2,1,0:T(8,128)(2,1)S(1)} %all-to-all-done.sides_ref), custom_call_target="tpu_custom_call" | custom-call | flops 3000000000 | bytes 3000000 | tf_op jit(solution)/shard_map/triangle_product/pallas_call | solution.py:552
  108.6 3.0 %all-to-all-start.1 = ((bf16[32,4,16,128]{3,2,1,0:T(8,128)(2,1)}), bf16[32,4,16,128]{3,2,1,0:T(8,128)(2,1)S(1)}, u32[]{:S(2)}, u32[]{:S(2)}) async-start(bf16[32,4,16,128]{3,2,1,0:T(8,128)(2,1)} %triangle_product.1), calls=%async_computation.1 | async-start | bytes 1048576 | tf_op jit(solution)/shard_map/all_to_all | solution.py:737
  111.6 0.1 broadcast_in_dim.14
  111.7 0.1 broadcast_in_dim.15
  111.8 0.0 copy-start.8
  111.8 2.2 %pad_maximum_fusion = bf16[4,8,64,256]{3,2,1,0:T(8,128)(2,1)} fusion(bf16[1,8,64,256]{3,2,1,0:T(8,128)(2,1)} %bitcast.14, bf16[1,8,64,256]{3,2,1,0:T(8,128)(2,1)} %bitcast.45, bf16[1,8,64,256]{3,2,1,0:T(8,128)(2,1)} %bitcast.44, bf16[1,8,64,256]{3,2,1,0:T(8,128)(2,1)S(1)} %bitcast.43), kind=kLoop, calls=%fused_computation.2 | loop fusion | flops 1572864 | bytes 2097152 | tf_op jit(solution)/shard_map/stack | solution.py:739
  114.1 2.8 %gather_fusion = bf16[4,8,64,256]{3,2,1,0:T(8,128)(2,1)} fusion(bf16[4,8,64,256]{3,2,1,0:T(8,128)(2,1)} %pad_maximum_fusion, s32[1024]{0:T(1024)S(1)} %pad_clamp_fusion), kind=kCustom, calls=%fused_computation | custom fusion | bytes 2097168 | tf_op jit(solution)/shard_map/jit(_take)/gather | solution.py:739
  116.9 3.4 %convolution_add_fusion = f32[64,32,256]{2,1,0:T(8,128)} fusion(f32[64,32,256]{2,1,0:T(8,128)S(1)} %copy-done, bf16[32,64,256]{2,1,0:T(8,128)(2,1)} %bitcast.38, pred[32]{0:T(512)(128)(4,1)S(1)} %broadcast_in_dim.15, bf16[256,256]{1,0:T(8,128)(2,1)S(1)} %copy-done.8), kind=kOutput, calls=%fused_computation.1 | convolution fusion | flops 269484032 | bytes 5373984 | tf_op jit(solution)/shard_map/dot_general | solution.py:741
  120.3 7.7 %all-to-all-done.1 = bf16[32,4,16,128]{3,2,1,0:T(8,128)(2,1)S(1)} async-done(((bf16[32,4,16,128]{3,2,1,0:T(8,128)(2,1)}), bf16[32,4,16,128]{3,2,1,0:T(8,128)(2,1)S(1)}, u32[]{:S(2)}, u32[]{:S(2)}) %all-to-all-start.1) | async-done | bytes 524320 | tf_op jit(solution)/shard_map/all_to_all | solution.py:737
  128.0 3.3 %pair_result.1 = f32[64,2,16,128]{3,2,1,0:T(8,128)} custom-call(bf16[128,16,128]{2,1,0:T(8,128)(2,1)S(1)} %bitcast.33, f32[2,16,64,128]{3,2,1,0:T(8,128)} %bitcast.50, f32[2,16,64,128]{3,2,1,0:T(8,128)} %bitcast.51, bf16[128,128]{1,0:T(8,128)(2,1)S(1)} %copy-done.5), custom_call_target="tpu_custom_call" | custom-call | flops 4000000000 | bytes 4000000 | tf_op jit(solution)/shard_map/pair_result/pallas_call | solution.py:588
  (31 shorter events, 0.1 us)
Async XLA Ops:
  0.6 9.1 %copy-start.9 = (bf16[256,768]{1,0:T(8,128)(2,1)S(1)}, bf16[256,768]{1,0:T(8,128)(2,1)}, u32[]{:S(2)}) copy-start(bf16[256,768]{1,0:T(8,128)(2,1)} %param.13) | copy-start | bytes 1179652
  0.7 10.9 %copy-start.13 = (bf16[256,256]{1,0:T(8,128)(2,1)S(1)}, bf16[256,256]{1,0:T(8,128)(2,1)}, u32[]{:S(2)}) copy-start(bf16[256,256]{1,0:T(8,128)(2,1)} %param.12) | copy-start | bytes 393220
  5.1 10.3 %copy-start = (f32[64,32,256]{2,1,0:T(8,128)S(1)}, f32[64,32,256]{2,1,0:T(8,128)}, u32[]{:S(2)}) copy-start(f32[64,32,256]{2,1,0:T(8,128)} %second_ref.1) | copy-start | bytes 6291460
  5.2 14.9 %collective-permute-start = (bf16[8,64,256]{2,1,0:T(8,128)(2,1)}, bf16[8,64,256]{2,1,0:T(8,128)(2,1)S(1)}, u32[]{:S(2)}, u32[]{:S(2)}) collective-permute-start(bf16[8,64,256]{2,1,0:T(8,128)(2,1)} %get-tuple-element.51), channel_id=1, source_target_pairs={{0,8},{8,0},{16,24},{24,16},{1,9},{9,1},{17,25},{25,17},{2,10},{10... | collective-permute-start | bytes 786440 | tf_op jit(solution)/shard_map/ppermute | solution.py:666
  8.2 13.6 %collective-permute-start.1 = (bf16[8,64,256]{2,1,0:T(8,128)(2,1)}, bf16[8,64,256]{2,1,0:T(8,128)(2,1)S(1)}, u32[]{:S(2)}, u32[]{:S(2)}) collective-permute-start(bf16[8,64,256]{2,1,0:T(8,128)(2,1)} %get-tuple-element.52), channel_id=1, source_target_pairs={{0,16},{8,24},{16,0},{24,8},{1,17},{9,25},{17,1},{25,9},{2,18},{10... | collective-permute-start | bytes 786440 | tf_op jit(solution)/shard_map/ppermute | solution.py:666
  9.7 12.1 %collective-permute-start.2 = (bf16[8,64,256]{2,1,0:T(8,128)(2,1)}, bf16[8,64,256]{2,1,0:T(8,128)(2,1)S(1)}, u32[]{:S(2)}, u32[]{:S(2)}) collective-permute-start(bf16[8,64,256]{2,1,0:T(8,128)(2,1)} %get-tuple-element.53), channel_id=1, source_target_pairs={{0,24},{8,16},{16,8},{24,0},{1,25},{9,17},{17,9},{25,1},{2,26},{10... | collective-permute-start | bytes 786440 | tf_op jit(solution)/shard_map/ppermute | solution.py:666
  15.5 9.8 %copy-start.6 = (bf16[8,64,256]{2,1,0:T(8,128)(2,1)S(1)}, bf16[8,64,256]{2,1,0:T(8,128)(2,1)}, u32[]{:S(2)}) copy-start(bf16[8,64,256]{2,1,0:T(8,128)(2,1)} %get-tuple-element.60.rest_0_) | copy-start | bytes 786436
  21.8 16.8 %copy-start.3 = (bf16[256,64]{0,1:T(8,128)(2,1)S(1)}, bf16[256,64]{0,1:T(8,128)(2,1)}, u32[]{:S(2)}) copy-start(bf16[256,64]{0,1:T(8,128)(2,1)} %param.15) | copy-start | bytes 98308
  21.8 16.8 %copy-start.7 = (bf16[8,80,256]{2,1,0:T(8,128)(2,1)S(1)}, bf16[8,80,256]{2,1,0:T(8,128)(2,1)}, u32[]{:S(2)}) copy-start(bf16[8,80,256]{2,1,0:T(8,128)(2,1)} %get-tuple-element.73.rest_4_) | copy-start | bytes 983044
  21.8 14.1 %collective-permute-start.3 = (bf16[8,80,256]{2,1,0:T(8,128)(2,1)}, bf16[8,80,256]{2,1,0:T(8,128)(2,1)S(1)}, u32[]{:S(2)}, u32[]{:S(2)}) collective-permute-start(bf16[8,80,256]{2,1,0:T(8,128)(2,1)} %get-tuple-element.74), channel_id=1, source_target_pairs={{0,8},{8,0},{16,24},{24,16},{1,9},{9,1},{17,25},{25,17},{2,10},{10... | collective-permute-start | bytes 983048 | tf_op jit(solution)/shard_map/ppermute | solution.py:666
  23.0 15.5 %collective-permute-start.4 = (bf16[8,80,256]{2,1,0:T(8,128)(2,1)}, bf16[8,80,256]{2,1,0:T(8,128)(2,1)S(1)}, u32[]{:S(2)}, u32[]{:S(2)}) collective-permute-start(bf16[8,80,256]{2,1,0:T(8,128)(2,1)} %get-tuple-element.75), channel_id=1, source_target_pairs={{0,16},{8,24},{16,0},{24,8},{1,17},{9,25},{17,1},{25,9},{2,18},{10... | collective-permute-start | bytes 983048 | tf_op jit(solution)/shard_map/ppermute | solution.py:666
  23.9 14.7 %collective-permute-start.5 = (bf16[8,80,256]{2,1,0:T(8,128)(2,1)}, bf16[8,80,256]{2,1,0:T(8,128)(2,1)S(1)}, u32[]{:S(2)}, u32[]{:S(2)}) collective-permute-start(bf16[8,80,256]{2,1,0:T(8,128)(2,1)} %get-tuple-element.76), channel_id=1, source_target_pairs={{0,24},{8,16},{16,8},{24,0},{1,25},{9,17},{17,9},{25,1},{2,26},{10... | collective-permute-start | bytes 983048 | tf_op jit(solution)/shard_map/ppermute | solution.py:666
  38.5 27.2 %copy-start.1 = (f32[64,32,128]{2,1,0:T(8,128)S(1)}, f32[64,32,128]{2,1,0:T(8,128)}, u32[]{:S(2)}) copy-start(f32[64,32,128]{2,1,0:T(8,128)} %param.11) | copy-start | bytes 3145732
  38.6 27.2 %copy-start.2 = (bf16[1024,128]{1,0:T(8,128)(2,1)S(1)}, bf16[1024,128]{1,0:T(8,128)(2,1)}, u32[]{:S(2)}) copy-start(bf16[1024,128]{1,0:T(8,128)(2,1)} %rest_4_.1) | copy-start | bytes 786436
  38.6 27.2 %copy-start.4 = (bf16[128,128]{1,0:T(8,128)(2,1)S(1)}, bf16[128,128]{1,0:T(8,128)(2,1)}, u32[]{:S(2)}) copy-start(bf16[128,128]{1,0:T(8,128)(2,1)} %rest_6_.1) | copy-start | bytes 98308
  42.8 10.9 %collective-permute-start.6 = (bf16[256,256]{1,0:T(8,128)(2,1)S(1)}, bf16[256,256]{1,0:T(8,128)(2,1)S(1)}, u32[]{:S(2)}, u32[]{:S(2)}) collective-permute-start(bf16[256,256]{1,0:T(8,128)(2,1)S(1)} %get-tuple-element.77), channel_id=1, source_target_pairs={{0,0},{1,1},{2,8},{3,9},{4,16},{5,17},{6,24},{7,25},{8,2},{9,3},{1... | collective-permute-start | bytes 393224 | tf_op jit(solution)/shard_map/ppermute | solution.py:627
  43.5 14.5 %collective-permute-start.7 = (bf16[256,256]{1,0:T(8,128)(2,1)S(1)}, bf16[256,256]{1,0:T(8,128)(2,1)S(1)}, u32[]{:S(2)}, u32[]{:S(2)}) collective-permute-start(bf16[256,256]{1,0:T(8,128)(2,1)S(1)} %get-tuple-element.77), channel_id=1, source_target_pairs={{0,2},{1,3},{2,10},{3,11},{4,18},{5,19},{6,26},{7,27},{8,4},{9,5},... | collective-permute-start | bytes 393224 | tf_op jit(solution)/shard_map/ppermute | solution.py:627
  46.8 11.2 %collective-permute-start.8 = (bf16[256,256]{1,0:T(8,128)(2,1)S(1)}, bf16[256,256]{1,0:T(8,128)(2,1)S(1)}, u32[]{:S(2)}, u32[]{:S(2)}) collective-permute-start(bf16[256,256]{1,0:T(8,128)(2,1)S(1)} %get-tuple-element.77), channel_id=1, source_target_pairs={{0,4},{1,5},{2,12},{3,13},{4,20},{5,21},{6,28},{7,29},{8,6},{9,7},... | collective-permute-start | bytes 393224 | tf_op jit(solution)/shard_map/ppermute | solution.py:627
  50.3 9.4 %collective-permute-start.9 = (bf16[256,256]{1,0:T(8,128)(2,1)S(1)}, bf16[256,256]{1,0:T(8,128)(2,1)S(1)}, u32[]{:S(2)}, u32[]{:S(2)}) collective-permute-start(bf16[256,256]{1,0:T(8,128)(2,1)S(1)} %get-tuple-element.77), channel_id=1, source_target_pairs={{0,6},{1,7},{2,14},{3,15},{4,22},{5,23},{6,30},{7,31},{8,0},{9,1},... | collective-permute-start | bytes 393224 | tf_op jit(solution)/shard_map/ppermute | solution.py:627
  53.5 7.6 %collective-permute-start.10 = (bf16[8,32,256]{2,1,0:T(8,128)(2,1)S(1)}, bf16[8,32,256]{2,1,0:T(8,128)(2,1)S(1)}, u32[]{:S(2)}, u32[]{:S(2)}) collective-permute-start(bf16[8,32,256]{2,1,0:T(8,128)(2,1)S(1)} %get-tuple-element.80.rest_0_), channel_id=1, source_target_pairs={{0,8},{8,0},{16,24},{24,16},{1,9},{9,1},{17,25},{25,17},{2,10},{10... | collective-permute-start | bytes 393224 | tf_op jit(solution)/shard_map/ppermute | solution.py:666
  53.7 7.4 %collective-permute-start.11 = (bf16[8,32,256]{2,1,0:T(8,128)(2,1)S(1)}, bf16[8,32,256]{2,1,0:T(8,128)(2,1)S(1)}, u32[]{:S(2)}, u32[]{:S(2)}) collective-permute-start(bf16[8,32,256]{2,1,0:T(8,128)(2,1)S(1)} %get-tuple-element.80.rest_0_), channel_id=1, source_target_pairs={{0,16},{8,24},{16,0},{24,8},{1,17},{9,25},{17,1},{25,9},{2,18},{10... | collective-permute-start | bytes 393224 | tf_op jit(solution)/shard_map/ppermute | solution.py:666
  58.0 5.9 %collective-permute-start.12 = (bf16[8,32,256]{2,1,0:T(8,128)(2,1)S(1)}, bf16[8,32,256]{2,1,0:T(8,128)(2,1)S(1)}, u32[]{:S(2)}, u32[]{:S(2)}) collective-permute-start(bf16[8,32,256]{2,1,0:T(8,128)(2,1)S(1)} %get-tuple-element.80.rest_0_), channel_id=1, source_target_pairs={{0,24},{8,16},{16,8},{24,0},{1,25},{9,17},{17,9},{25,1},{2,26},{10... | collective-permute-start | bytes 393224 | tf_op jit(solution)/shard_map/ppermute | solution.py:666
  63.8 1.9 %collective-permute-start.13 = (bf16[4,256,256]{2,1,0:T(8,128)(2,1)S(1)}, bf16[4,256,256]{2,1,0:T(8,128)(2,1)S(1)}, u32[]{:S(2)}, u32[]{:S(2)}) collective-permute-start(bf16[4,256,256]{2,1,0:T(8,128)(2,1)S(1)} %pad_maximum_fusion.1.own_ref), channel_id=1, source_target_pairs={{0,1},{1,0},{2,3},{3,2},{4,5},{5,4},{6,7},{7,6},{8,9},{9,8},{10,11... | collective-permute-start | bytes 1572872 | tf_op jit(solution)/shard_map/ppermute | solution.py:614
  75.1 31.9 %all-to-all-start = ((bf16[32,4,32,128]{3,2,1,0:T(8,128)(2,1)}), bf16[32,4,32,128]{3,2,1,0:T(8,128)(2,1)S(1)}, u32[]{:S(2)}, u32[]{:S(2)}) async-start(bf16[32,4,32,128]{3,2,1,0:T(8,128)(2,1)} %bitcast.40), calls=%async_computation | async-start | bytes 2097152 | tf_op jit(solution)/shard_map/all_to_all | solution.py:734
  79.3 32.5 %copy-start.10 = (bf16[8,64,256]{2,1,0:T(8,128)(2,1)S(1)}, bf16[8,64,256]{2,1,0:T(8,128)(2,1)}, u32[]{:S(2)}) copy-start(bf16[8,64,256]{2,1,0:T(8,128)(2,1)} %get-tuple-element.91) | copy-start | bytes 786436
  79.3 17.3 %collective-permute-start.14 = (bf16[8,64,256]{2,1,0:T(8,128)(2,1)}, bf16[8,64,256]{2,1,0:T(8,128)(2,1)S(1)}, u32[]{:S(2)}, u32[]{:S(2)}) collective-permute-start(bf16[8,64,256]{2,1,0:T(8,128)(2,1)} %get-tuple-element.87), channel_id=1, source_target_pairs={{0,8},{8,0},{16,24},{24,16},{1,9},{9,1},{17,25},{25,17},{2,10},{10... | collective-permute-start | bytes 786440 | tf_op jit(solution)/shard_map/ppermute | solution.py:666
  81.2 15.4 %collective-permute-start.15 = (bf16[8,64,256]{2,1,0:T(8,128)(2,1)}, bf16[8,64,256]{2,1,0:T(8,128)(2,1)S(1)}, u32[]{:S(2)}, u32[]{:S(2)}) collective-permute-start(bf16[8,64,256]{2,1,0:T(8,128)(2,1)} %get-tuple-element.88), channel_id=1, source_target_pairs={{0,16},{8,24},{16,0},{24,8},{1,17},{9,25},{17,1},{25,9},{2,18},{10... | collective-permute-start | bytes 786440 | tf_op jit(solution)/shard_map/ppermute | solution.py:666
  82.6 22.4 %collective-permute-start.16 = (bf16[8,64,256]{2,1,0:T(8,128)(2,1)}, bf16[8,64,256]{2,1,0:T(8,128)(2,1)}, u32[]{:S(2)}, u32[]{:S(2)}) collective-permute-start(bf16[8,64,256]{2,1,0:T(8,128)(2,1)} %get-tuple-element.89), channel_id=1, source_target_pairs={{0,24},{8,16},{16,8},{24,0},{1,25},{9,17},{17,9},{25,1},{2,26},{10... | collective-permute-start | bytes 786440 | tf_op jit(solution)/shard_map/ppermute | solution.py:666
  96.6 0.7 copy-start.11
  97.3 0.7 copy-start.12
  108.6 19.4 %all-to-all-start.1 = ((bf16[32,4,16,128]{3,2,1,0:T(8,128)(2,1)}), bf16[32,4,16,128]{3,2,1,0:T(8,128)(2,1)S(1)}, u32[]{:S(2)}, u32[]{:S(2)}) async-start(bf16[32,4,16,128]{3,2,1,0:T(8,128)(2,1)} %triangle_product.1), calls=%async_computation.1 | async-start | bytes 1048576 | tf_op jit(solution)/shard_map/all_to_all | solution.py:737
  111.8 5.1 %copy-start.8 = (bf16[256,256]{1,0:T(8,128)(2,1)S(1)}, bf16[256,256]{1,0:T(8,128)(2,1)}, u32[]{:S(2)}) copy-start(bf16[256,256]{1,0:T(8,128)(2,1)} %param.14) | copy-start | bytes 393220
  116.9 11.1 %copy-start.5 = (bf16[128,128]{1,0:T(8,128)(2,1)S(1)}, bf16[128,128]{1,0:T(8,128)(2,1)}, u32[]{:S(2)}) copy-start(bf16[128,128]{1,0:T(8,128)(2,1)} %final_ref.1) | copy-start | bytes 98308

commit v9 on v8

--- a/solution.py
+++ b/solution.py
@@ -139,22 +139,21 @@
     first_rows = first_ref.reshape(seqs * residues, lanes)
     second_rows = second_ref.reshape(seqs * residues, lanes)
     lane = lax.broadcasted_iota(jnp.int32, (seqs, 128), 1)
-    spreads = jnp.zeros((seqs, 128), F32)
-    for n in range(residues):
-        normed, spread = standardised_column(first_rows, second_rows, n, residues)
-        low_ref[n, :seqs, :] = (normed - normed.astype(BF16).astype(F32)).astype(BF16)
-        spreads = jnp.where(lane == n, spread, spreads)
-    spreads = spreads.T
-    row = lax.broadcasted_iota(jnp.int32, (16, seqs), 0)
-    for n in range(residues):
-        spread = jnp.broadcast_to(spreads[n : n + 1, :], (16, seqs))
-        coarse = spread.astype(BF16).astype(F32)
-        kept = jnp.where(row == 0, coarse, jnp.where(row == 1, spread - coarse, 0.0))
+    for p in range(len(pieces_hbm)):
+        spreads = jnp.zeros((seqs, 128), F32)
+        for n in range(own):
+            normed, spread = standardised_column(first_rows, second_rows, p * own + n, residues)
+            left = (normed - normed.astype(BF16).astype(F32)).astype(BF16)
+            low_ref[p, n * seqs : (n + 1) * seqs, :] = left
+            spreads = jnp.where(lane == n, spread, spreads)
+        spreads = spreads.T[:8, :]
+        coarse = spreads.astype(BF16).astype(F32)
+        kept = jnp.concatenate([coarse, spreads - coarse], axis=0)
         kept = jnp.concatenate([kept, jnp.zeros((16, 2 * lanes - seqs), F32)], axis=1)
-        low_ref[n, seqs:, :] = kept.astype(BF16)
+        low_ref[p, own * seqs :, :] = kept.astype(BF16)
     sends = []
     for p, piece_hbm in enumerate(pieces_hbm):
-        source = low_ref.at[pl.ds(sources_ref[p] * own, own)]
+        source = low_ref.at[sources_ref[p]]
         sends.append(pltpu.make_async_copy(source, piece_hbm, sent.at[p]))
         sends[-1].start()
     for send in sends:
@@ -165,6 +164,7 @@
     seqs, residues, depth = block.shape
     half = depth // 2
     count = sources.shape[0]
+    height = residues // count * seqs + 16
     hbm = pl.BlockSpec(memory_space=pltpu.HBM)
     return pl.pallas_call(
         low_kernel,
@@ -175,9 +175,9 @@
             pl.BlockSpec((seqs, residues, half), lambda g: (0, 0, 1)),
         ],
         out_specs=[hbm] * count,
-        out_shape=[pltpu.HBM((residues // count, seqs + 16, depth), BF16)] * count,
+        out_shape=[pltpu.HBM((height, depth), BF16)] * count,
         scratch_shapes=[
-            pltpu.VMEM((residues, seqs + 16, depth), BF16),
+            pltpu.VMEM((count, height, depth), BF16),
             pltpu.SemaphoreType.DMA((count,)),
         ],
         compiler_params=params(14, "arbitrary"),
@@ -195,7 +195,8 @@
     inner = ATTENTION_UNITS * UNIT_WIDTH
     ring = scores_ref.shape[0]
     columns = []
-    for n in range(residues):
+
+    def project(n):
         column = jnp.concatenate([ref[n] for ref in normed_refs], axis=0)
         key_rows = matmul(column, key_ref[...]).astype(BF16)
         projected = matmul_nt(others_ref[...], column)
@@ -203,7 +204,7 @@
         value_rows = projected[inner : 2 * inner].astype(BF16)
         gates = sigmoid(projected[2 * inner :])
         columns.append((key_rows, queries, value_rows, gates))
-    units = [(n, h) for h in range(ATTENTION_UNITS) for n in range(residues)]
+    units = [(n, h) for n in range(residues) for h in range(ATTENTION_UNITS)]
 
     def score(unit):
         n, h = units[unit]
@@ -230,17 +231,25 @@
         attended = matmul(value_rows[rows], weights_ref[unit % ring]) * gates[rows]
         turned_ref[n, rows, :] = attended.astype(BF16)
 
+    def turn_back(n):
+        back = turned_ref[n].T
+        for block, gated_ref in enumerate(gated_refs):
+            gated_ref[n] = back[block * seqs : (block + 1) * seqs]
+
+    project(0)
     for step in range(len(units) + 2):
         if step < len(units):
             score(step)
+            n, h = units[step]
+            if h == ATTENTION_UNITS // 2 and n + 1 < residues:
+                project(n + 1)
         if 1 <= step <= len(units):
             weigh(step - 1)
         if step >= 2:
             attend(step - 2)
-    for n in range(residues):
-        back = turned_ref[n].T
-        for block, gated_ref in enumerate(gated_refs):
-            gated_ref[n] = back[block * seqs : (block + 1) * seqs]
+            n, h = units[step - 2]
+            if h == ATTENTION_UNITS - 1:
+                turn_back(n)
 
 
 def attention(normed, key_matrix, other_matrices):
@@ -248,7 +257,7 @@
     residues, seqs, depth = normed[0].shape
     total = blocks * seqs
     inner = ATTENTION_UNITS * UNIT_WIDTH
-    step = 2
+    step = 4
     return pl.pallas_call(
         attention_kernel,
         grid=(residues // step,),
@@ -265,7 +274,7 @@
             pltpu.VMEM((4, total, total), F32),
             pltpu.VMEM((4, total, total), BF16),
         ],
-        compiler_params=params(8 + (total // 128) ** 2, "arbitrary"),
+        compiler_params=params(12 + (total // 128) ** 2, "arbitrary"),
         cost_estimate=cost(10),
         name="attention",
     )(key_matrix, other_matrices, *normed)
@@ -273,8 +282,8 @@
 
 def alignment_kernel(sources_ref, turned_ref, final_ref, entry_ref, *rest):
     *refs, left_ref, right_ref, rows_ref = rest
-    blocks = len(refs) // 2
-    high_refs, low_refs = refs[:blocks], refs[blocks:]
+    blocks = len(refs) // 3
+    high_refs, low_refs, spread_refs = refs[:blocks], refs[blocks : 2 * blocks], refs[2 * blocks :]
     residues, seqs, depth = high_refs[0].shape
     total = blocks * seqs
     features = TENSOR_FEATURES
@@ -282,12 +291,14 @@
     for n in range(residues):
         column = jnp.concatenate([ref[n] for ref in high_refs], axis=0).astype(F32)
         column = column + jnp.concatenate(
-            [ref[n, :seqs, :] for ref in low_refs], axis=0
+            [ref[n * seqs : (n + 1) * seqs, :] for ref in low_refs], axis=0
         ).astype(F32)
         spreads = []
-        for ref in low_refs:
-            kept = ref[n, seqs:, :seqs].astype(F32)
-            spreads.append(jnp.sum(kept, axis=0, keepdims=True))
+        for ref in spread_refs:
+            kept = ref[:, :seqs].astype(F32)
+            row = lax.broadcasted_iota(jnp.int32, kept.shape, 0)
+            chosen = lax.rem(row, 8) == step * residues + n
+            spreads.append(jnp.sum(jnp.where(chosen, kept, 0.0), axis=0, keepdims=True))
         spread = jnp.concatenate(spreads, axis=1)
         updated = column.T * spread + matmul(final_ref[...], turned_ref[n])
         projected = matmul(entry_ref[...], normalise_rows(updated))
@@ -326,20 +337,23 @@
     residues, seqs, depth = high[0].shape
     total = blocks * seqs
     features = TENSOR_FEATURES
+    step = 4
+    height = residues * seqs + 16
     return pl.pallas_call(
         alignment_kernel,
-        grid=(residues // 2,),
+        grid=(residues // step,),
         in_specs=[
             pl.BlockSpec(memory_space=pltpu.SMEM),
-            pl.BlockSpec((2, depth, total), lambda n: (n, 0, 0)),
+            pl.BlockSpec((step, depth, total), lambda n: (n, 0, 0)),
             pl.BlockSpec(final_matrix.shape, lambda n: (0, 0)),
             pl.BlockSpec(entry_matrices.shape, lambda n: (0, 0)),
         ]
-        + [pl.BlockSpec((2, seqs, depth), lambda n: (n, 0, 0))] * blocks
-        + [pl.BlockSpec((2, seqs + 16, depth), lambda n: (n, 0, 0))] * blocks,
+        + [pl.BlockSpec((step, seqs, depth), lambda n: (n, 0, 0))] * blocks
+        + [pl.BlockSpec((step * seqs, depth), lambda n: (n, 0))] * blocks
+        + [pl.BlockSpec((16, depth), lambda n: (height // 16 - 1, 0))] * blocks,
         out_specs=[
             pl.BlockSpec((features * residues, total), lambda n: (0, 0)),
-            pl.BlockSpec((2, features, total), lambda n: (n, 0, 0)),
+            pl.BlockSpec((step, features, total), lambda n: (n, 0, 0)),
         ],
         out_shape=[
             jax.ShapeDtypeStruct((features * residues, total), BF16),
@@ -349,7 +363,7 @@
         compiler_params=params(16, "arbitrary"),
         cost_estimate=cost(4),
         name="alignment",
-    )(sources, turned, final_matrix, entry_matrices, *high, *low)
+    )(sources, turned, final_matrix, entry_matrices, *high, *low, *low)
 
 
 def pair_kernel(
@@ -561,52 +575,74 @@
     )(sides)
 
 
-def output_kernel(product_ref, mid_ref, gate_ref, final_ref, out_ref, wide_ref):
+def output_kernel(
+    product_ref, final_ref, mid_hbm, gate_hbm, out_hbm, wide_ref, mid_ref, gate_ref, out_ref, *copied
+):
     channels, part, lanes = product_ref.shape
-    _, own, rows, depth = mid_ref.shape
-    out_rows = out_ref.reshape(rows * 2 * own, depth)
-    step = pl.program_id(0)
-
-    @pl.when(step == 0)
-    def _():
-        wide_ref[...] = product_ref[...].astype(F32).reshape(channels * part, lanes)
-
-    for j in range(own):
-        product = wide_ref[pl.ds(step * own + j, channels, stride=part), :]
-        update = matmul(normalise_rows(product).T, final_ref[...])
+    columns, rows, depth = mid_ref.shape
+    own = 8
+    fetched, sent = copied
+    fetches, sends = [], []
+    for first in range(0, columns, own):
+        chosen = pl.ds(first, own)
+        for source, target in ((mid_hbm, mid_ref), (gate_hbm, gate_ref)):
+            fetches.append(
+                pltpu.make_async_copy(
+                    source.at[chosen], target.at[chosen], fetched.at[len(fetches)]
+                )
+            )
+            fetches[-1].start()
+    wide_ref[...] = product_ref[...].astype(F32).reshape(channels * part, lanes)
+    for group in range(part // own):
+        updates = []
+        for j in range(own):
+            product = wide_ref[pl.ds(group * own + j, channels, stride=part), :]
+            updates.append(matmul(normalise_rows(product).T, final_ref[...]))
         for half in range(2):
-            piece = update[half * rows : (half + 1) * rows]
-            piece = mid_ref[half, j] + gate_ref[half, j] * piece
-            out_rows[pl.ds(half * own + j, rows, stride=2 * own), :] = piece
+            cut = half * (part // own) + group
+            fetches[2 * cut].wait()
+            fetches[2 * cut + 1].wait()
+            out_rows = out_ref.at[cut].reshape(rows * own, depth)
+            for j in range(own):
+                b = cut * own + j
+                piece = updates[j][half * rows : (half + 1) * rows]
+                out_rows[pl.ds(j, rows, stride=own), :] = mid_ref[b] + gate_ref[b] * piece
+            sends.append(
+                pltpu.make_async_copy(
+                    out_ref.at[cut], out_hbm.at[:, pl.ds(cut * own, own)], sent.at[len(sends)]
+                )
+            )
+            sends[-1].start()
+    for send in sends:
+        send.wait()
 
 
 def pair_result(product, mid, gate, final_matrix):
     channels, part, lanes = product.shape
     columns, rows, depth = mid.shape
-    own = 8
-    whole = pl.BlockSpec((2, own, rows, depth), lambda j: (0, j, 0, 0))
-    out = pl.pallas_call(
+    vmem, hbm = pl.BlockSpec(memory_space=pltpu.VMEM), pl.BlockSpec(memory_space=pltpu.HBM)
+    return pl.pallas_call(
         output_kernel,
-        grid=(part // own,),
-        in_specs=[
-            pl.BlockSpec(product.shape, lambda j: (0, 0, 0)),
-            whole,
-            whole,
-            pl.BlockSpec(final_matrix.shape, lambda j: (0, 0)),
+        in_specs=[vmem, vmem, hbm, hbm],
+        out_specs=hbm,
+        out_shape=pltpu.HBM((rows, columns, depth), F32),
+        scratch_shapes=[
+            pltpu.VMEM((channels * part, lanes), F32),
+            pltpu.VMEM(mid.shape, F32),
+            pltpu.VMEM(mid.shape, F32),
+            pltpu.VMEM((columns // 8, rows, 8, depth), F32),
+            pltpu.SemaphoreType.DMA((columns // 4,)),
+            pltpu.SemaphoreType.DMA((columns // 8,)),
         ],
-        out_specs=pl.BlockSpec((rows, 2, own, depth), lambda j: (0, 0, j, 0)),
-        out_shape=jax.ShapeDtypeStruct((rows, 2, part, depth), F32),
-        scratch_shapes=[pltpu.VMEM((channels * part, lanes), F32)],
-        compiler_params=params(12, "arbitrary"),
-        cost_estimate=cost(4),
+        compiler_params=params(16),
+        cost_estimate=cost(3),
         name="pair_result",
     )(
         product,
-        pltpu.with_memory_space_constraint(mid.reshape(2, part, rows, depth), pltpu.HBM),
-        pltpu.with_memory_space_constraint(gate.reshape(2, part, rows, depth), pltpu.HBM),
         final_matrix,
-    )
-    return out.reshape(rows, columns, depth)
+        pltpu.with_memory_space_constraint(mid, pltpu.HBM),
+        pltpu.with_memory_space_constraint(gate, pltpu.HBM),
+    )
 
 
 def swap_cores(block):
@@ -614,7 +650,7 @@
     return lax.ppermute(block, "col", [(c, c ^ 1) for c in range(count)])
 
 
-def gather_turned(block):
+def gather_turned(block, later):
     rows, columns = lax.axis_size("row"), lax.axis_size("col")
     arrived = []
     for shift in range(rows):
@@ -624,7 +660,8 @@
                 for side in range(2):
                     source = r * columns + 2 * q + side
                     moves.append((source, q * columns + 2 * ((r + shift) % rows) + side))
-        arrived.append(lax.ppermute(block, ("row", "col"), moves))
+        source = block if shift < 2 else later
+        arrived.append(lax.ppermute(source, ("row", "col"), moves))
     return jnp.stack(arrived)
 
 
@@ -712,7 +749,8 @@
     )
 
     rights = exchange_rows([right_piece] * row_count)
-    own = gather_turned(left_piece)
+    later, rights[1] = lax.optimization_barrier((left_piece, rights[1]))
+    own = gather_turned(left_piece, later)
     own, rights = lax.optimization_barrier((own, rights))
     mid, gate, sides = pair_update(
         slots,

time: 132 us -> 128 us (0.970)
  waiting for transfers between devices: 42.3 us -> 39.9 us
  Pallas kernels: 38 us -> 35.9 us
    ppermute x12, waiting for transfers between devices: 29.1 us -> 25.5 us  [exchange_rows(): arrived.append(lax.ppermute(pieces[shift], 'row', moves))]
    ppermute x12, starting transfers between devices: 16.1 us -> 14 us  [exchange_rows(): arrived.append(lax.ppermute(pieces[shift], 'row', moves))]
    ppermute x4, starting transfers between devices: 10.7 us -> 12.3 us  [gather_turned(): arrived.append(lax.ppermute(source, ('row', 'col'), moves))]
  transfers between devices with their start and end apart: 19 -> 19, of which waited for: 10 -> 10; matrix products, arithmetic and copies ran while one was open for 11% -> 11% of each run, Pallas kernels for 12% -> 11%
where the time goes in v9:
time: 128 us; the launch traced here: 127 us
  waiting for transfers between devices  39.9 us (31%)
  Pallas kernels  35.9 us (28%)
  starting transfers between devices  34.4 us (27%)
  local copies, waits for them, and re-layouts  9.1 us (7%)
  matrix products  3.41 us (3%)
  other arithmetic  3.36 us (3%)
    ppermute x12, waiting for transfers between devices, exchange_rows(): arrived.append(lax.ppermute(pieces[shift], 'row', moves))  25.5 us
    ppermute x12, starting transfers between devices, exchange_rows(): arrived.append(lax.ppermute(pieces[shift], 'row', moves))  14 us
    ppermute x4, starting transfers between devices, gather_turned(): arrived.append(lax.ppermute(source, ('row', 'col'), moves))  12.3 us
    pallas_call x1, Pallas kernels, attention(): pl.pallas_call(attention_kernel, grid=(residues // step,), in_specs=[pl.B...  9.37 us
    pallas_call x1, Pallas kernels, pair_update(): pl.pallas_call(pair_kernel, in_specs=[smem] * 2 + [vmem] * (5 + len(right...  9.3 us
    all_to_all x1, waiting for transfers between devices, body(): product = lax.all_to_all(product, everywhere, split_axis=0, concat_axis=0)  7.66 us
    all_to_all x1, starting transfers between devices, body(): sides = lax.all_to_all(sides, everywhere, split_axis=0, concat_axis=0)  5.03 us
    pallas_call x1, Pallas kernels, standardise_low(): pl.pallas_call(low_kernel, grid=(1,), in_specs=[pl.BlockSpec(memory_space...  4.5 us
  transfers between devices with their start and end apart: 19, of which 10 were waited for; matrix products, arithmetic and copies ran while one was open for 11% of the time, Pallas kernels for 11%

profile of v9, /device:TPU:0, one launch (start us, length us, event | category | flops | bytes accessed | tf_op | source)
XLA Modules:
  0.0 127.1 jit_solution(4636821764849989169)
XLA Ops:
  0.6 0.0 copy-start.9
  0.7 0.0 copy-start.13
  0.7 4.5 %standardise_high.1 = (bf16[8,64,256]{2,1,0:T(8,128)(2,1)}, bf16[8,64,256]{2,1,0:T(8,128)(2,1)}, bf16[8,64,256]{2,1,0:T(8,128)(2,1)}, bf16[8,64,256]{2,1,0:T(8,128)(2,1)}) custom-call(s32[4]{0:T(128)S(1)} %iota_xor_fusion.sources_ref, f32[64,32,256]{2,1,0:T(8,128)} %second_ref.1), custom_call_target="tpu_custom_call" | custom-call | flops 3000000000 | bytes 3000000 | tf_op jit(solution)/shard_map/standardise_high/pallas_call | solution.py:117
  5.1 0.0 copy-start
  5.1 3.0 %collective-permute-start = (bf16[8,64,256]{2,1,0:T(8,128)(2,1)}, bf16[8,64,256]{2,1,0:T(8,128)(2,1)S(1)}, u32[]{:S(2)}, u32[]{:S(2)}) collective-permute-start(bf16[8,64,256]{2,1,0:T(8,128)(2,1)} %get-tuple-element.53), channel_id=1, source_target_pairs={{0,8},{8,0},{16,24},{24,16},{1,9},{9,1},{17,25},{25,17},{2,10},{10... | collective-permute-start | bytes 786440 | tf_op jit(solution)/shard_map/ppermute | solution.py:703
  8.2 1.5 %collective-permute-start.1 = (bf16[8,64,256]{2,1,0:T(8,128)(2,1)}, bf16[8,64,256]{2,1,0:T(8,128)(2,1)S(1)}, u32[]{:S(2)}, u32[]{:S(2)}) collective-permute-start(bf16[8,64,256]{2,1,0:T(8,128)(2,1)} %get-tuple-element.54), channel_id=1, source_target_pairs={{0,16},{8,24},{16,0},{24,8},{1,17},{9,25},{17,1},{25,9},{2,18},{10... | collective-permute-start | bytes 786440 | tf_op jit(solution)/shard_map/ppermute | solution.py:703
  9.7 0.0 collective-permute-start.2
  9.7 0.7 slice.7
  10.4 1.1 copy.17
  11.5 0.8 copy.12
  12.3 0.9 reshape.47
  13.2 0.1 copy.15
  13.4 1.0 copy.14
  14.4 0.1 pad_add_fusion.left_slots_ref
  14.5 0.9 pad_maximum_fusion.2.others_ref
  15.5 4.5 %standardise_low.1 = (bf16[528,256]{1,0:T(8,128)(2,1)}, bf16[528,256]{1,0:T(8,128)(2,1)}, bf16[528,256]{1,0:T(8,128)(2,1)}, bf16[528,256]{1,0:T(8,128)(2,1)}) custom-call(s32[4]{0:T(128)S(1)} %iota_xor_fusion.sources_ref, f32[64,32,256]{2,1,0:T(8,128)S(1)} %copy-done, f32[64,32,256]{2,1,0:T(8,128)S(1)} %copy-done), custom_call_target="tpu_custom_call" | custom-call | flops 4000000000 | bytes 4000000 | tf_op jit(solution)/shard_map/standardise_low/pallas_call | solution.py:169
  20.0 0.0 collective-permute-done.rest_1_
  20.0 1.8 %collective-permute-done.1.rest_2_ = bf16[8,64,256]{2,1,0:T(8,128)(2,1)S(1)} collective-permute-done((bf16[8,64,256]{2,1,0:T(8,128)(2,1)}, bf16[8,64,256]{2,1,0:T(8,128)(2,1)S(1)}, u32[]{:S(2)}, u32[]{:S(2)}) %collective-permute-start.1) | collective-permute-done | bytes 262176 | tf_op jit(solution)/shard_map/ppermute | solution.py:703
  21.7 0.0 collective-permute-done.2.rest_3_
  21.8 1.2 collective-permute-start.3
  23.0 0.9 collective-permute-start.4
  23.9 1.4 %collective-permute-start.5 = (bf16[528,256]{1,0:T(8,128)(2,1)}, bf16[528,256]{1,0:T(8,128)(2,1)S(1)}, u32[]{:S(2)}, u32[]{:S(2)}) collective-permute-start(bf16[528,256]{1,0:T(8,128)(2,1)} %get-tuple-element.78), channel_id=1, source_target_pairs={{0,24},{8,16},{16,8},{24,0},{1,25},{9,17},{17,9},{25,1},{2,26},{10... | collective-permute-start | bytes 811016 | tf_op jit(solution)/shard_map/ppermute | solution.py:703
  25.3 9.4 %attention.1 = (bf16[8,256,256]{2,1,0:T(8,128)(2,1)S(1)}, bf16[8,64,256]{2,1,0:T(8,128)(2,1)}, bf16[8,64,256]{2,1,0:T(8,128)(2,1)}, bf16[8,64,256]{2,1,0:T(8,128)(2,1)}, bf16[8,64,256]{2,1,0:T(8,128)(2,1)}) custom-call(bf16[256,256]{1,0:T(8,128)(2,1)S(1)} %slice.6.key_ref, bf16[768,256]{1,0:T(8,128)(2,1)S(1)} %pad_maximum_fusion.2.others_ref, ...), custom_call_target="tpu_custom_call" | custom-call | flops 10000000000 | bytes 10000000 | tf_op jit(solution)/shard_map/attention/pallas_call | solution.py:261
  34.7 0.0 collective-permute-done.3.rest_5_.rest_9_
  34.7 1.4 %collective-permute-done.4.rest_6_.rest_10_ = bf16[528,256]{1,0:T(8,128)(2,1)S(1)} collective-permute-done((bf16[528,256]{1,0:T(8,128)(2,1)}, bf16[528,256]{1,0:T(8,128)(2,1)S(1)}, u32[]{:S(2)}, u32[]{:S(2)}) %collective-permute-start.4) | collective-permute-done | bytes 270368 | tf_op jit(solution)/shard_map/ppermute | solution.py:703
  36.1 0.0 collective-permute-done.5.rest_7_.rest_11_
  36.1 0.0 copy-start.1
  36.1 0.0 copy-start.2
  36.1 0.0 copy-start.4
  36.1 3.8 %alignment.1 = (bf16[256,256]{1,0:T(8,128)(2,1)S(1)}, bf16[8,32,256]{2,1,0:T(8,128)(2,1)S(1)}) custom-call(s32[4]{0:T(128)S(1)} %iota_xor_fusion.sources_ref, bf16[8,256,256]{2,1,0:T(8,128)(2,1)S(1)} %get-tuple-element.72.turned_ref, bf16[256,256]{1,0:T(8,128)(2,1)S(1)} %bitcast.32, bf16[64,256]{1,0:T(8,128)(2,1)S(1)} %bitcast.34, ...), custom_call_target="tpu_custom_call" | custom-call | flops 4000000000 | bytes 4000000 | tf_op jit(solution)/shard_map/alignment/pallas_call | solution.py:342
  39.9 0.6 collective-permute-start.8
  40.6 0.7 collective-permute-start.6
  41.2 4.2 %collective-permute-start.7 = (bf16[256,256]{1,0:T(8,128)(2,1)S(1)}, bf16[256,256]{1,0:T(8,128)(2,1)S(1)}, u32[]{:S(2)}, u32[]{:S(2)}) collective-permute-start(bf16[256,256]{1,0:T(8,128)(2,1)S(1)} %get-tuple-element.81), channel_id=1, source_target_pairs={{0,2},{1,3},{2,10},{3,11},{4,18},{5,19},{6,26},{7,27},{8,4},{9,5},... | collective-permute-start | bytes 393224 | tf_op jit(solution)/shard_map/ppermute | solution.py:664
  45.4 0.0 collective-permute-done.8.rest_1_
  45.4 4.7 %collective-permute-start.9 = (bf16[256,256]{1,0:T(8,128)(2,1)S(1)}, bf16[256,256]{1,0:T(8,128)(2,1)S(1)}, u32[]{:S(2)}, u32[]{:S(2)}) collective-permute-start(bf16[256,256]{1,0:T(8,128)(2,1)S(1)} %get-tuple-element.81), channel_id=1, source_target_pairs={{0,4},{1,5},{2,12},{3,13},{4,20},{5,21},{6,28},{7,29},{8,6},{9,7},... | collective-permute-start | bytes 393224 | tf_op jit(solution)/shard_map/ppermute | solution.py:664
  50.1 2.7 %collective-permute-start.10 = (bf16[256,256]{1,0:T(8,128)(2,1)S(1)}, bf16[256,256]{1,0:T(8,128)(2,1)S(1)}, u32[]{:S(2)}, u32[]{:S(2)}) collective-permute-start(bf16[256,256]{1,0:T(8,128)(2,1)S(1)} %get-tuple-element.81), channel_id=1, source_target_pairs={{0,6},{1,7},{2,14},{3,15},{4,22},{5,23},{6,30},{7,31},{8,0},{9,1},... | collective-permute-start | bytes 393224 | tf_op jit(solution)/shard_map/ppermute | solution.py:664
  52.9 0.0 collective-permute-done.6
  52.9 1.7 %collective-permute-start.12 = (bf16[8,32,256]{2,1,0:T(8,128)(2,1)S(1)}, bf16[8,32,256]{2,1,0:T(8,128)(2,1)S(1)}, u32[]{:S(2)}, u32[]{:S(2)}) collective-permute-start(bf16[8,32,256]{2,1,0:T(8,128)(2,1)S(1)} %get-tuple-element.84.rest_0_), channel_id=1, source_target_pairs={{0,24},{8,16},{16,8},{24,0},{1,25},{9,17},{17,9},{25,1},{2,26},{10... | collective-permute-start | bytes 393224 | tf_op jit(solution)/shard_map/ppermute | solution.py:703
  54.6 1.0 collective-permute-done.9
  55.6 1.9 %collective-permute-done.10 = bf16[256,256]{1,0:T(8,128)(2,1)S(1)} collective-permute-done((bf16[256,256]{1,0:T(8,128)(2,1)S(1)}, bf16[256,256]{1,0:T(8,128)(2,1)S(1)}, u32[]{:S(2)}, u32[]{:S(2)}) %collective-permute-start.10) | collective-permute-done | bytes 131104 | tf_op jit(solution)/shard_map/ppermute | solution.py:664
  57.5 0.1 pad_maximum_fusion.1.own_ref
  57.6 1.6 %collective-permute-done.11.rest_2_ = bf16[8,32,256]{2,1,0:T(8,128)(2,1)S(1)} collective-permute-done((bf16[8,32,256]{2,1,0:T(8,128)(2,1)S(1)}, bf16[8,32,256]{2,1,0:T(8,128)(2,1)S(1)}, u32[]{:S(2)}, u32[]{:S(2)}) %collective-permute-start.11) | collective-permute-done | bytes 131104 | tf_op jit(solution)/shard_map/ppermute | solution.py:703
  59.2 0.0 collective-permute-done.12.rest_3_
  59.2 1.9 %collective-permute-done.13.other_ref = bf16[4,256,256]{2,1,0:T(8,128)(2,1)S(1)} collective-permute-done((bf16[4,256,256]{2,1,0:T(8,128)(2,1)S(1)}, bf16[4,256,256]{2,1,0:T(8,128)(2,1)S(1)}, u32[]{:S(2)}, u32[]{:S(2)}) %collective-permute-start.13) | collective-permute-done | bytes 524320 | tf_op jit(solution)/shard_map/ppermute | solution.py:650
  61.2 9.3 %pair_update.1 = (f32[32,64,128]{2,1,0:T(8,128)}, f32[32,64,128]{2,1,0:T(8,128)}, bf16[128,32,128]{2,1,0:T(8,128)(2,1)}) custom-call(s32[8]{0:T(128)S(1)} %pad_add_fusion.left_slots_ref, s32[4]{0:T(128)S(1)} %broadcast_multiply_fusion.right_firsts_ref, bf16[4,256,256]{2,1,0:T(8,128)(2,1)S(1)} %pad_maximum_fusion.1.own_ref, ...), custom_call_target="tpu_custom_call" | custom-call | flops 12000000000 | bytes 12000000 | tf_op jit(solution)/shard_map/pair_update/pallas_call | solution.py:502
  70.5 5.0 %all-to-all-start = ((bf16[32,4,32,128]{3,2,1,0:T(8,128)(2,1)}), bf16[32,4,32,128]{3,2,1,0:T(8,128)(2,1)S(1)}, u32[]{:S(2)}, u32[]{:S(2)}) async-start(bf16[32,4,32,128]{3,2,1,0:T(8,128)(2,1)} %bitcast.37), calls=%async_computation | async-start | bytes 2097152 | tf_op jit(solution)/shard_map/all_to_all | solution.py:772
  75.5 1.8 %collective-permute-start.14 = (bf16[8,64,256]{2,1,0:T(8,128)(2,1)}, bf16[8,64,256]{2,1,0:T(8,128)(2,1)S(1)}, u32[]{:S(2)}, u32[]{:S(2)}) collective-permute-start(bf16[8,64,256]{2,1,0:T(8,128)(2,1)} %get-tuple-element.91), channel_id=1, source_target_pairs={{0,8},{8,0},{16,24},{24,16},{1,9},{9,1},{17,25},{25,17},{2,10},{10... | collective-permute-start | bytes 786440 | tf_op jit(solution)/shard_map/ppermute | solution.py:703
  77.4 1.5 %collective-permute-start.15 = (bf16[8,64,256]{2,1,0:T(8,128)(2,1)}, bf16[8,64,256]{2,1,0:T(8,128)(2,1)S(1)}, u32[]{:S(2)}, u32[]{:S(2)}) collective-permute-start(bf16[8,64,256]{2,1,0:T(8,128)(2,1)} %get-tuple-element.92), channel_id=1, source_target_pairs={{0,16},{8,24},{16,0},{24,8},{1,17},{9,25},{17,1},{25,9},{2,18},{10... | collective-permute-start | bytes 786440 | tf_op jit(solution)/shard_map/ppermute | solution.py:703
  78.8 0.3 collective-permute-start.16
  79.1 13.7 %collective-permute-done.14 = bf16[8,64,256]{2,1,0:T(8,128)(2,1)S(1)} collective-permute-done((bf16[8,64,256]{2,1,0:T(8,128)(2,1)}, bf16[8,64,256]{2,1,0:T(8,128)(2,1)S(1)}, u32[]{:S(2)}, u32[]{:S(2)}) %collective-permute-start.14) | collective-permute-done | bytes 262176 | tf_op jit(solution)/shard_map/ppermute | solution.py:703
  92.8 0.7 copy-done.11
  93.5 0.7 copy-done.12
  94.2 7.0 %collective-permute-done.16 = bf16[8,64,256]{2,1,0:T(8,128)(2,1)} collective-permute-done((bf16[8,64,256]{2,1,0:T(8,128)(2,1)}, bf16[8,64,256]{2,1,0:T(8,128)(2,1)}, u32[]{:S(2)}, u32[]{:S(2)}) %collective-permute-start.16) | collective-permute-done | bytes 262176 | tf_op jit(solution)/shard_map/ppermute | solution.py:703
  101.2 1.9 %all-to-all-done.sides_ref = bf16[32,4,32,128]{3,2,1,0:T(8,128)(2,1)S(1)} async-done(((bf16[32,4,32,128]{3,2,1,0:T(8,128)(2,1)}), bf16[32,4,32,128]{3,2,1,0:T(8,128)(2,1)S(1)}, u32[]{:S(2)}, u32[]{:S(2)}) %all-to-all-start) | async-done | bytes 1048608 | tf_op jit(solution)/shard_map/all_to_all | solution.py:772
  103.1 1.7 %triangle_product.1 = bf16[32,4,16,128]{3,2,1,0:T(8,128)(2,1)} custom-call(bf16[32,4,32,128]{3,2,1,0:T(8,128)(2,1)S(1)} %all-to-all-done.sides_ref), custom_call_target="tpu_custom_call" | custom-call | flops 3000000000 | bytes 3000000 | tf_op jit(solution)/shard_map/triangle_product/pallas_call | solution.py:566
  104.8 3.0 %all-to-all-start.1 = ((bf16[32,4,16,128]{3,2,1,0:T(8,128)(2,1)}), bf16[32,4,16,128]{3,2,1,0:T(8,128)(2,1)S(1)}, u32[]{:S(2)}, u32[]{:S(2)}) async-start(bf16[32,4,16,128]{3,2,1,0:T(8,128)(2,1)} %triangle_product.1), calls=%async_computation.1 | async-start | bytes 1048576 | tf_op jit(solution)/shard_map/all_to_all | solution.py:775
  107.8 0.1 broadcast_in_dim.14
  107.9 0.1 broadcast_in_dim.15
  108.0 0.0 copy-start.8
  108.0 2.2 %pad_maximum_fusion = bf16[4,8,64,256]{3,2,1,0:T(8,128)(2,1)} fusion(bf16[1,8,64,256]{3,2,1,0:T(8,128)(2,1)} %bitcast.14, bf16[1,8,64,256]{3,2,1,0:T(8,128)(2,1)} %bitcast.42, bf16[1,8,64,256]{3,2,1,0:T(8,128)(2,1)} %bitcast.41, bf16[1,8,64,256]{3,2,1,0:T(8,128)(2,1)S(1)} %bitcast.40), kind=kLoop, calls=%fused_computation.2 | loop fusion | flops 1572864 | bytes 2097152 | tf_op jit(solution)/shard_map/stack | solution.py:777
  110.3 2.8 %gather_fusion = bf16[4,8,64,256]{3,2,1,0:T(8,128)(2,1)} fusion(bf16[4,8,64,256]{3,2,1,0:T(8,128)(2,1)} %pad_maximum_fusion, s32[1024]{0:T(1024)S(1)} %pad_clamp_fusion), kind=kCustom, calls=%fused_computation | custom fusion | bytes 2097168 | tf_op jit(solution)/shard_map/jit(_take)/gather | solution.py:777
  113.1 3.4 %convolution_add_fusion = f32[64,32,256]{2,1,0:T(8,128)} fusion(f32[64,32,256]{2,1,0:T(8,128)S(1)} %copy-done, bf16[32,64,256]{2,1,0:T(8,128)(2,1)} %bitcast.35, pred[32]{0:T(512)(128)(4,1)S(1)} %broadcast_in_dim.15, bf16[256,256]{1,0:T(8,128)(2,1)S(1)} %copy-done.8), kind=kOutput, calls=%fused_computation.1 | convolution fusion | flops 269484032 | bytes 5373984 | tf_op jit(solution)/shard_map/dot_general | solution.py:779
  116.5 7.7 %all-to-all-done.1 = bf16[32,4,16,128]{3,2,1,0:T(8,128)(2,1)S(1)} async-done(((bf16[32,4,16,128]{3,2,1,0:T(8,128)(2,1)}), bf16[32,4,16,128]{3,2,1,0:T(8,128)(2,1)S(1)}, u32[]{:S(2)}, u32[]{:S(2)}) %all-to-all-start.1) | async-done | bytes 524320 | tf_op jit(solution)/shard_map/all_to_all | solution.py:775
  124.1 2.8 %pair_result.1 = f32[64,32,128]{2,1,0:T(8,128)} custom-call(bf16[128,16,128]{2,1,0:T(8,128)(2,1)S(1)} %bitcast.30, bf16[128,128]{1,0:T(8,128)(2,1)S(1)} %copy-done.5, f32[32,64,128]{2,1,0:T(8,128)} %get-tuple-element.100.mid_hbm, f32[32,64,128]{2,1,0:T(8,128)} %get-tuple-element.101.gate_hbm), custom_call_target="tpu_custom_call" | custom-call | flops 3000000000 | bytes 3000000 | tf_op jit(solution)/shard_map/pair_result/pallas_call | solution.py:624
  (31 shorter events, 0.1 us)
Async XLA Ops:
  0.6 9.1 %copy-start.9 = (bf16[256,768]{1,0:T(8,128)(2,1)S(1)}, bf16[256,768]{1,0:T(8,128)(2,1)}, u32[]{:S(2)}) copy-start(bf16[256,768]{1,0:T(8,128)(2,1)} %param.13) | copy-start | bytes 1179652
  0.7 10.9 %copy-start.13 = (bf16[256,256]{1,0:T(8,128)(2,1)S(1)}, bf16[256,256]{1,0:T(8,128)(2,1)}, u32[]{:S(2)}) copy-start(bf16[256,256]{1,0:T(8,128)(2,1)} %param.12) | copy-start | bytes 393220
  5.1 10.3 %copy-start = (f32[64,32,256]{2,1,0:T(8,128)S(1)}, f32[64,32,256]{2,1,0:T(8,128)}, u32[]{:S(2)}) copy-start(f32[64,32,256]{2,1,0:T(8,128)} %second_ref.1) | copy-start | bytes 6291460
  5.1 14.8 %collective-permute-start = (bf16[8,64,256]{2,1,0:T(8,128)(2,1)}, bf16[8,64,256]{2,1,0:T(8,128)(2,1)S(1)}, u32[]{:S(2)}, u32[]{:S(2)}) collective-permute-start(bf16[8,64,256]{2,1,0:T(8,128)(2,1)} %get-tuple-element.53), channel_id=1, source_target_pairs={{0,8},{8,0},{16,24},{24,16},{1,9},{9,1},{17,25},{25,17},{2,10},{10... | collective-permute-start | bytes 786440 | tf_op jit(solution)/shard_map/ppermute | solution.py:703
  8.2 13.6 %collective-permute-start.1 = (bf16[8,64,256]{2,1,0:T(8,128)(2,1)}, bf16[8,64,256]{2,1,0:T(8,128)(2,1)S(1)}, u32[]{:S(2)}, u32[]{:S(2)}) collective-permute-start(bf16[8,64,256]{2,1,0:T(8,128)(2,1)} %get-tuple-element.54), channel_id=1, source_target_pairs={{0,16},{8,24},{16,0},{24,8},{1,17},{9,25},{17,1},{25,9},{2,18},{10... | collective-permute-start | bytes 786440 | tf_op jit(solution)/shard_map/ppermute | solution.py:703
  9.7 12.1 %collective-permute-start.2 = (bf16[8,64,256]{2,1,0:T(8,128)(2,1)}, bf16[8,64,256]{2,1,0:T(8,128)(2,1)S(1)}, u32[]{:S(2)}, u32[]{:S(2)}) collective-permute-start(bf16[8,64,256]{2,1,0:T(8,128)(2,1)} %get-tuple-element.55), channel_id=1, source_target_pairs={{0,24},{8,16},{16,8},{24,0},{1,25},{9,17},{17,9},{25,1},{2,26},{10... | collective-permute-start | bytes 786440 | tf_op jit(solution)/shard_map/ppermute | solution.py:703
  15.5 9.8 %copy-start.6 = (bf16[8,64,256]{2,1,0:T(8,128)(2,1)S(1)}, bf16[8,64,256]{2,1,0:T(8,128)(2,1)}, u32[]{:S(2)}) copy-start(bf16[8,64,256]{2,1,0:T(8,128)(2,1)} %get-tuple-element.62.rest_0_) | copy-start | bytes 786436
  21.8 14.3 %copy-start.3 = (bf16[256,64]{0,1:T(8,128)(2,1)S(1)}, bf16[256,64]{0,1:T(8,128)(2,1)}, u32[]{:S(2)}) copy-start(bf16[256,64]{0,1:T(8,128)(2,1)} %param.15) | copy-start | bytes 98308
  21.8 14.3 %copy-start.7 = (bf16[528,256]{1,0:T(8,128)(2,1)S(1)}, bf16[528,256]{1,0:T(8,128)(2,1)}, u32[]{:S(2)}) copy-start(bf16[528,256]{1,0:T(8,128)(2,1)} %get-tuple-element.75.rest_4_.rest_8_) | copy-start | bytes 811012
  21.8 12.9 %collective-permute-start.3 = (bf16[528,256]{1,0:T(8,128)(2,1)}, bf16[528,256]{1,0:T(8,128)(2,1)S(1)}, u32[]{:S(2)}, u32[]{:S(2)}) collective-permute-start(bf16[528,256]{1,0:T(8,128)(2,1)} %get-tuple-element.76), channel_id=1, source_target_pairs={{0,8},{8,0},{16,24},{24,16},{1,9},{9,1},{17,25},{25,17},{2,10},{10... | collective-permute-start | bytes 811016 | tf_op jit(solution)/shard_map/ppermute | solution.py:703
  23.0 13.1 %collective-permute-start.4 = (bf16[528,256]{1,0:T(8,128)(2,1)}, bf16[528,256]{1,0:T(8,128)(2,1)S(1)}, u32[]{:S(2)}, u32[]{:S(2)}) collective-permute-start(bf16[528,256]{1,0:T(8,128)(2,1)} %get-tuple-element.77), channel_id=1, source_target_pairs={{0,16},{8,24},{16,0},{24,8},{1,17},{9,25},{17,1},{25,9},{2,18},{10... | collective-permute-start | bytes 811016 | tf_op jit(solution)/shard_map/ppermute | solution.py:703
  23.9 12.2 %collective-permute-start.5 = (bf16[528,256]{1,0:T(8,128)(2,1)}, bf16[528,256]{1,0:T(8,128)(2,1)S(1)}, u32[]{:S(2)}, u32[]{:S(2)}) collective-permute-start(bf16[528,256]{1,0:T(8,128)(2,1)} %get-tuple-element.78), channel_id=1, source_target_pairs={{0,24},{8,16},{16,8},{24,0},{1,25},{9,17},{17,9},{25,1},{2,26},{10... | collective-permute-start | bytes 811016 | tf_op jit(solution)/shard_map/ppermute | solution.py:703
  36.1 25.1 %copy-start.1 = (f32[64,32,128]{2,1,0:T(8,128)S(1)}, f32[64,32,128]{2,1,0:T(8,128)}, u32[]{:S(2)}) copy-start(f32[64,32,128]{2,1,0:T(8,128)} %param.11) | copy-start | bytes 3145732
  36.1 25.1 %copy-start.2 = (bf16[1024,128]{1,0:T(8,128)(2,1)S(1)}, bf16[1024,128]{1,0:T(8,128)(2,1)}, u32[]{:S(2)}) copy-start(bf16[1024,128]{1,0:T(8,128)(2,1)} %rest_4_.1) | copy-start | bytes 786436
  36.1 25.1 %copy-start.4 = (bf16[128,128]{1,0:T(8,128)(2,1)S(1)}, bf16[128,128]{1,0:T(8,128)(2,1)}, u32[]{:S(2)}) copy-start(bf16[128,128]{1,0:T(8,128)(2,1)} %rest_6_.1) | copy-start | bytes 98308
  39.9 5.5 %collective-permute-start.8 = (bf16[8,32,256]{2,1,0:T(8,128)(2,1)S(1)}, bf16[8,32,256]{2,1,0:T(8,128)(2,1)S(1)}, u32[]{:S(2)}, u32[]{:S(2)}) collective-permute-start(bf16[8,32,256]{2,1,0:T(8,128)(2,1)S(1)} %get-tuple-element.84.rest_0_), channel_id=1, source_target_pairs={{0,8},{8,0},{16,24},{24,16},{1,9},{9,1},{17,25},{25,17},{2,10},{10... | collective-permute-start | bytes 393224 | tf_op jit(solution)/shard_map/ppermute | solution.py:703
  40.6 12.3 %collective-permute-start.6 = (bf16[256,256]{1,0:T(8,128)(2,1)S(1)}, bf16[256,256]{1,0:T(8,128)(2,1)S(1)}, u32[]{:S(2)}, u32[]{:S(2)}) collective-permute-start(bf16[256,256]{1,0:T(8,128)(2,1)S(1)} %get-tuple-element.81), channel_id=1, source_target_pairs={{0,0},{1,1},{2,8},{3,9},{4,16},{5,17},{6,24},{7,25},{8,2},{9,3},{1... | collective-permute-start | bytes 393224 | tf_op jit(solution)/shard_map/ppermute | solution.py:664
  41.2 13.4 %collective-permute-start.7 = (bf16[256,256]{1,0:T(8,128)(2,1)S(1)}, bf16[256,256]{1,0:T(8,128)(2,1)S(1)}, u32[]{:S(2)}, u32[]{:S(2)}) collective-permute-start(bf16[256,256]{1,0:T(8,128)(2,1)S(1)} %get-tuple-element.81), channel_id=1, source_target_pairs={{0,2},{1,3},{2,10},{3,11},{4,18},{5,19},{6,26},{7,27},{8,4},{9,5},... | collective-permute-start | bytes 393224 | tf_op jit(solution)/shard_map/ppermute | solution.py:664
  45.4 10.2 %collective-permute-start.9 = (bf16[256,256]{1,0:T(8,128)(2,1)S(1)}, bf16[256,256]{1,0:T(8,128)(2,1)S(1)}, u32[]{:S(2)}, u32[]{:S(2)}) collective-permute-start(bf16[256,256]{1,0:T(8,128)(2,1)S(1)} %get-tuple-element.81), channel_id=1, source_target_pairs={{0,4},{1,5},{2,12},{3,13},{4,20},{5,21},{6,28},{7,29},{8,6},{9,7},... | collective-permute-start | bytes 393224 | tf_op jit(solution)/shard_map/ppermute | solution.py:664
  50.1 7.4 %collective-permute-start.10 = (bf16[256,256]{1,0:T(8,128)(2,1)S(1)}, bf16[256,256]{1,0:T(8,128)(2,1)S(1)}, u32[]{:S(2)}, u32[]{:S(2)}) collective-permute-start(bf16[256,256]{1,0:T(8,128)(2,1)S(1)} %get-tuple-element.81), channel_id=1, source_target_pairs={{0,6},{1,7},{2,14},{3,15},{4,22},{5,23},{6,30},{7,31},{8,0},{9,1},... | collective-permute-start | bytes 393224 | tf_op jit(solution)/shard_map/ppermute | solution.py:664
  52.9 6.4 %collective-permute-start.11 = (bf16[8,32,256]{2,1,0:T(8,128)(2,1)S(1)}, bf16[8,32,256]{2,1,0:T(8,128)(2,1)S(1)}, u32[]{:S(2)}, u32[]{:S(2)}) collective-permute-start(bf16[8,32,256]{2,1,0:T(8,128)(2,1)S(1)} %get-tuple-element.84.rest_0_), channel_id=1, source_target_pairs={{0,16},{8,24},{16,0},{24,8},{1,17},{9,25},{17,1},{25,9},{2,18},{10... | collective-permute-start | bytes 393224 | tf_op jit(solution)/shard_map/ppermute | solution.py:703
  52.9 6.4 %collective-permute-start.12 = (bf16[8,32,256]{2,1,0:T(8,128)(2,1)S(1)}, bf16[8,32,256]{2,1,0:T(8,128)(2,1)S(1)}, u32[]{:S(2)}, u32[]{:S(2)}) collective-permute-start(bf16[8,32,256]{2,1,0:T(8,128)(2,1)S(1)} %get-tuple-element.84.rest_0_), channel_id=1, source_target_pairs={{0,24},{8,16},{16,8},{24,0},{1,25},{9,17},{17,9},{25,1},{2,26},{10... | collective-permute-start | bytes 393224 | tf_op jit(solution)/shard_map/ppermute | solution.py:703
  59.2 1.9 %collective-permute-start.13 = (bf16[4,256,256]{2,1,0:T(8,128)(2,1)S(1)}, bf16[4,256,256]{2,1,0:T(8,128)(2,1)S(1)}, u32[]{:S(2)}, u32[]{:S(2)}) collective-permute-start(bf16[4,256,256]{2,1,0:T(8,128)(2,1)S(1)} %pad_maximum_fusion.1.own_ref), channel_id=1, source_target_pairs={{0,1},{1,0},{2,3},{3,2},{4,5},{5,4},{6,7},{7,6},{8,9},{9,8},{10,11... | collective-permute-start | bytes 1572872 | tf_op jit(solution)/shard_map/ppermute | solution.py:650
  70.5 32.6 %all-to-all-start = ((bf16[32,4,32,128]{3,2,1,0:T(8,128)(2,1)}), bf16[32,4,32,128]{3,2,1,0:T(8,128)(2,1)S(1)}, u32[]{:S(2)}, u32[]{:S(2)}) async-start(bf16[32,4,32,128]{3,2,1,0:T(8,128)(2,1)} %bitcast.37), calls=%async_computation | async-start | bytes 2097152 | tf_op jit(solution)/shard_map/all_to_all | solution.py:772
  75.5 32.5 %copy-start.10 = (bf16[8,64,256]{2,1,0:T(8,128)(2,1)S(1)}, bf16[8,64,256]{2,1,0:T(8,128)(2,1)}, u32[]{:S(2)}) copy-start(bf16[8,64,256]{2,1,0:T(8,128)(2,1)} %get-tuple-element.95) | copy-start | bytes 786436
  75.5 17.3 %collective-permute-start.14 = (bf16[8,64,256]{2,1,0:T(8,128)(2,1)}, bf16[8,64,256]{2,1,0:T(8,128)(2,1)S(1)}, u32[]{:S(2)}, u32[]{:S(2)}) collective-permute-start(bf16[8,64,256]{2,1,0:T(8,128)(2,1)} %get-tuple-element.91), channel_id=1, source_target_pairs={{0,8},{8,0},{16,24},{24,16},{1,9},{9,1},{17,25},{25,17},{2,10},{10... | collective-permute-start | bytes 786440 | tf_op jit(solution)/shard_map/ppermute | solution.py:703
  77.4 15.4 %collective-permute-start.15 = (bf16[8,64,256]{2,1,0:T(8,128)(2,1)}, bf16[8,64,256]{2,1,0:T(8,128)(2,1)S(1)}, u32[]{:S(2)}, u32[]{:S(2)}) collective-permute-start(bf16[8,64,256]{2,1,0:T(8,128)(2,1)} %get-tuple-element.92), channel_id=1, source_target_pairs={{0,16},{8,24},{16,0},{24,8},{1,17},{9,25},{17,1},{25,9},{2,18},{10... | collective-permute-start | bytes 786440 | tf_op jit(solution)/shard_map/ppermute | solution.py:703
  78.8 22.4 %collective-permute-start.16 = (bf16[8,64,256]{2,1,0:T(8,128)(2,1)}, bf16[8,64,256]{2,1,0:T(8,128)(2,1)}, u32[]{:S(2)}, u32[]{:S(2)}) collective-permute-start(bf16[8,64,256]{2,1,0:T(8,128)(2,1)} %get-tuple-element.93), channel_id=1, source_target_pairs={{0,24},{8,16},{16,8},{24,0},{1,25},{9,17},{17,9},{25,1},{2,26},{10... | collective-permute-start | bytes 786440 | tf_op jit(solution)/shard_map/ppermute | solution.py:703
  92.8 0.7 copy-start.11
  93.5 0.7 copy-start.12
  104.8 19.4 %all-to-all-start.1 = ((bf16[32,4,16,128]{3,2,1,0:T(8,128)(2,1)}), bf16[32,4,16,128]{3,2,1,0:T(8,128)(2,1)S(1)}, u32[]{:S(2)}, u32[]{:S(2)}) async-start(bf16[32,4,16,128]{3,2,1,0:T(8,128)(2,1)} %triangle_product.1), calls=%async_computation.1 | async-start | bytes 1048576 | tf_op jit(solution)/shard_map/all_to_all | solution.py:775
  108.0 5.1 %copy-start.8 = (bf16[256,256]{1,0:T(8,128)(2,1)S(1)}, bf16[256,256]{1,0:T(8,128)(2,1)}, u32[]{:S(2)}) copy-start(bf16[256,256]{1,0:T(8,128)(2,1)} %param.14) | copy-start | bytes 393220
  113.1 11.1 %copy-start.5 = (bf16[128,128]{1,0:T(8,128)(2,1)S(1)}, bf16[128,128]{1,0:T(8,128)(2,1)}, u32[]{:S(2)}) copy-start(bf16[128,128]{1,0:T(8,128)(2,1)} %final_ref.1) | copy-start | bytes 98308

commit v10 on v9

--- a/solution.py
+++ b/solution.py
@@ -366,64 +366,66 @@
     )(sources, turned, final_matrix, entry_matrices, *high, *low, *low)
 
 
-def pair_kernel(
-    left_slots_ref,
-    right_firsts_ref,
-    own_ref,
-    other_ref,
-    *rest,
-):
-    weights_ref, entry_ref, switch_ref, couplings_hbm, mid_hbm, gate_hbm, sides_hbm = rest[-16:-9]
-    outer_ref, spread_ref, sum_ref, rows_ref, couplings_ref = rest[-9:-4]
-    mid_ref, gate_ref, sides_ref, copied = rest[-4:]
-    right_refs = rest[:-16]
-    fetched = pltpu.make_async_copy(couplings_hbm, couplings_ref, copied.at[0])
-    fetched.start()
+def pair_kernel(places_ref, *rest, slots, pieces):
+    *refs, outer_ref, spread_ref, sum_ref, rows_ref, near_ref, far_ref, mids_ref, gates_ref = rest[:-2]
+    sides_ref, copied = rest[-2:]
+    left_refs, right_refs = refs[:slots], refs[slots : slots + pieces]
+    rights_ref, weights_ref, entry_ref, switch_ref = refs[slots + pieces : slots + pieces + 4]
+    near_hbm, far_hbm, mid_hbm, gate_hbm, away_hbm, sides_hbm = refs[slots + pieces + 4 :]
+    features = TENSOR_FEATURES
+    piece_rows, total = left_refs[0].shape
+    residues = piece_rows // features
+    rows = slots * residues
+    share = right_refs[0].shape[0]
+    columns = pieces * share
+    groups = 2 * columns // GROUP
+    wide = share * features
+    together = spread_ref.shape[1] // 64
+    core = places_ref[slots + pieces]
+    fetches = []
+    for source, target in ((near_hbm, near_ref), (far_hbm, far_ref)):
+        fetches.append(pltpu.make_async_copy(source, target, copied.at[len(fetches)]))
+        fetches[-1].start()
     copies = []
 
     def send(source, target):
-        copies.append(pltpu.make_async_copy(source, target, copied.at[len(copies) + 1]))
+        copies.append(pltpu.make_async_copy(source, target, copied.at[len(copies) + 2]))
         copies[-1].start()
 
-    features = TENSOR_FEATURES
-    slots, piece_rows, total = own_ref.shape
-    residues = piece_rows // features
-    rows = 2 * slots * residues
-    share = right_refs[0].shape[0]
-    columns = len(right_refs) * share
-    groups = columns // GROUP
-    wide = share * features
-    together = spread_ref.shape[1] // 128
-
-    for half, left_ref in enumerate((own_ref, other_ref)):
-        piece = left_ref[...].reshape(slots * piece_rows, total)
-        target = slice(half * slots * piece_rows, (half + 1) * slots * piece_rows)
-        for p, right_ref in enumerate(right_refs):
-            right = right_ref[...].reshape(wide, total)
-            outer_ref[target, p * wide : (p + 1) * wide] = matmul_nt(piece, right) * (1.0 / total)
+    left = jnp.concatenate([ref[...] for ref in left_refs], axis=0)
+    for p in range(2 * pieces):
+        right = right_refs[p][...] if p < pieces else rights_ref[p - pieces]
+        outer = matmul_nt(left, right.reshape(wide, total)) * (1.0 / total)
+        outer_ref[:, p * wide : (p + 1) * wide] = outer
 
     spread_ref[...] = jnp.zeros_like(spread_ref)
+    front = lax.broadcasted_iota(jnp.int32, (rows, 128), 1) < 64
 
     def channel_step(p, carry):
         slot = lax.rem(p, 2)
         for e in range(together):
             source = pl.multiple_of((p * together + e) * features, features)
             piece = weights_ref[pl.ds(source, features), :]
-            for place in range(GROUP):
-                low = e * 128 + place * features
+            for place in range(2):
+                low = e * 64 + place * features
                 spread_ref[slot, low : low + features, place * C_Z : (place + 1) * C_Z] = piece
-        pieces = []
+        blocks = []
         for g in range(groups):
             parts = []
             for e in range(together):
                 channel = []
-                for slot_number in range(2 * slots):
+                for slot_number in range(slots):
                     first = slot_number * piece_rows + (p * together + e) * residues
                     source = pl.ds(pl.multiple_of(first, residues), residues)
                     channel.append(outer_ref[source, g * 128 : (g + 1) * 128])
                 parts.append(jnp.concatenate(channel, axis=0).astype(BF16))
-            pieces.append(jnp.concatenate(parts, axis=1))
-        update = matmul(jnp.concatenate(pieces, axis=0), spread_ref[slot])
+            lows, highs = [], []
+            for e in range(0, together, 2):
+                lows.append(jnp.where(front, parts[e], pltpu.roll(parts[e + 1], 64, 1)))
+                highs.append(jnp.where(front, pltpu.roll(parts[e], 64, 1), parts[e + 1]))
+            blocks.append(jnp.concatenate(lows, axis=1))
+            blocks.append(jnp.concatenate(highs, axis=1))
+        update = matmul(jnp.concatenate(blocks, axis=0), spread_ref[slot])
 
         @pl.when(p == 0)
         def _():
@@ -437,46 +439,56 @@
 
     lax.fori_loop(0, features // together, channel_step, 0)
 
-    left_firsts = [left_slots_ref[j] * residues for j in range(2 * slots)]
-    right_firsts = [right_firsts_ref[p] for p in range(len(right_refs))]
-    fetched.wait()
-    for g in range(groups):
+    left_firsts = [places_ref[j] * residues for j in range(slots)]
+    right_firsts = [places_ref[slots + p] for p in range(pieces)]
+    for fetch in fetches:
+        fetch.wait()
+    for g in range(groups // 2):
         normed, places = [], []
         for place in range(GROUP):
             p, n = divmod(g * GROUP + place, share)
             b = right_firsts[p] + n
             places.append(b)
-            lanes = slice(place * C_Z, (place + 1) * C_Z)
-            pieces = []
-            for first in left_firsts:
-                source = pl.ds(pl.multiple_of(g * rows + first, residues), residues)
-                pieces.append(sum_ref[source, lanes])
-            mid = jnp.concatenate(pieces, axis=0)
-            mid = mid + couplings_ref[pl.ds(b, rows, stride=columns), :]
-            mid_ref[g * GROUP + place] = mid
-            centred = mid - jnp.mean(mid, axis=1, keepdims=True)
-            variance = jnp.mean(centred * centred, axis=1, keepdims=True)
-            normed.append((centred * lax.rsqrt(variance + EPS)).astype(BF16))
+            for side in range(2):
+                lanes = slice(place % 2 * C_Z, (place % 2 + 1) * C_Z)
+                start = ((g + side * groups // 2) * 2 + place // 2) * rows
+                parts = []
+                for first in left_firsts:
+                    source = pl.ds(pl.multiple_of(start + first, residues), residues)
+                    parts.append(sum_ref[source, lanes])
+                mid = jnp.concatenate(parts, axis=0)
+                if side == 0:
+                    mid = mid + near_ref[pl.ds(core * rows * columns + b, rows, stride=columns), :]
+                else:
+                    mid = mid + far_ref[pl.ds(b, rows, stride=columns), :]
+                mids_ref[side, g * GROUP + place] = mid
+                centred = mid - jnp.mean(mid, axis=1, keepdims=True)
+                variance = jnp.mean(centred * centred, axis=1, keepdims=True)
+                normed.append((centred * lax.rsqrt(variance + EPS)).astype(BF16))
         gates = sigmoid(matmul(jnp.concatenate(normed, axis=0), switch_ref[...]))
+        for place in range(GROUP):
+            for side in range(2):
+                first = (2 * place + side) * rows
+                gates_ref[side, g * GROUP + place] = gates[first : first + rows]
         blank = jnp.zeros_like(normed[0])
         for place in range(0, GROUP, 2):
             twice = []
-            for e in range(2):
-                part = gates[(place + e) * rows : (place + e + 1) * rows]
-                gate_ref[g * GROUP + place + e] = part
-                twice.append(jnp.concatenate([normed[place + e], blank], axis=1))
-                twice.append(jnp.concatenate([blank, normed[place + e]], axis=1))
+            for piece in normed[2 * place : 2 * place + 4]:
+                twice.append(jnp.concatenate([piece, blank], axis=1))
+                twice.append(jnp.concatenate([blank, piece], axis=1))
             sides = matmul_nt(entry_ref[...], jnp.concatenate(twice, axis=0))
             sides = sigmoid(sides[C_TRI:]) * sides[:C_TRI]
             for e in range(2):
                 first = pl.multiple_of(places[place + e] * C_TRI, C_TRI)
-                rows_ref[pl.ds(first, C_TRI), :] = sides[:, e * 2 * rows : (e + 1) * 2 * rows]
+                rows_ref[pl.ds(first, C_TRI), :] = sides[:, e * 4 * rows : (e + 1) * 4 * rows]
 
         if (g + 1) * GROUP % share == 0:
             p = (g + 1) * GROUP // share - 1
             source, target = pl.ds(p * share, share), pl.ds(right_firsts[p], share)
-            send(mid_ref.at[source], mid_hbm.at[target])
-            send(gate_ref.at[source], gate_hbm.at[target])
+            send(mids_ref.at[0, source], mid_hbm.at[target])
+            send(gates_ref.at[0, source], gate_hbm.at[target])
+            send(mids_ref.at[1, source], away_hbm.at[0, target])
+            send(gates_ref.at[1, source], away_hbm.at[1, target])
 
     cut = C_TRI // 4
     for part in range(4):
@@ -492,62 +504,92 @@
         copy.wait()
 
 
-def pair_update(left_slots, right_firsts, left, rights, weights, couplings, entry, switch):
-    rows, columns, depth = couplings.shape
-    whole = jax.ShapeDtypeStruct((columns, rows, depth), F32)
-    sides = jax.ShapeDtypeStruct((C_TRI, columns, 2 * rows), BF16)
+def pair_update(places, lefts, rights, far_rights, weights, near, far, entry, switch):
+    all_rows, columns, depth = near.shape
+    rows = all_rows // 2
+    whole = (columns, rows, depth)
+    sides = (C_TRI, columns, 4 * rows)
     smem = pl.BlockSpec(memory_space=pltpu.SMEM)
     vmem = pl.BlockSpec(memory_space=pltpu.VMEM)
     anywhere = pl.BlockSpec(memory_space=pl.ANY)
     return pl.pallas_call(
-        pair_kernel,
-        in_specs=[smem] * 2 + [vmem] * (5 + len(rights)) + [anywhere],
-        out_specs=[anywhere] * 3,
-        out_shape=[pltpu.HBM(whole.shape, F32)] * 2 + [pltpu.HBM(sides.shape, BF16)],
+        functools.partial(pair_kernel, slots=len(lefts), pieces=len(rights)),
+        in_specs=[smem] + [vmem] * (4 + len(lefts) + len(rights)) + [anywhere] * 2,
+        out_specs=[anywhere] * 4,
+        out_shape=[
+            pltpu.HBM(whole, F32),
+            pltpu.HBM(whole, F32),
+            pltpu.HBM((2,) + whole, F32),
+            pltpu.HBM(sides, BF16),
+        ],
         scratch_shapes=[
-            pltpu.VMEM((rows * TENSOR_FEATURES, columns * TENSOR_FEATURES), F32),
-            pltpu.VMEM((2, 8 * 128, GROUP * depth), BF16),
-            pltpu.VMEM((columns // GROUP * rows, GROUP * depth), F32),
-            pltpu.VMEM((columns * C_TRI, 2 * rows), F32),
+            pltpu.VMEM((rows * TENSOR_FEATURES, 2 * columns * TENSOR_FEATURES), F32),
+            pltpu.VMEM((2, 8 * 64, 2 * depth), BF16),
+            pltpu.VMEM((columns * rows, 2 * depth), F32),
+            pltpu.VMEM((columns * C_TRI, 4 * rows), F32),
+            pltpu.VMEM((all_rows * columns, depth), F32),
             pltpu.VMEM((rows * columns, depth), F32),
-            pltpu.VMEM(whole.shape, F32),
-            pltpu.VMEM(whole.shape, F32),
-            pltpu.VMEM(sides.shape, BF16),
-            pltpu.SemaphoreType.DMA((2 * len(rights) + 5,)),
+            pltpu.VMEM((2,) + whole, F32),
+            pltpu.VMEM((2,) + whole, F32),
+            pltpu.VMEM(sides, BF16),
+            pltpu.SemaphoreType.DMA((4 * len(rights) + 6,)),
         ],
-        compiler_params=params(28),
-        cost_estimate=cost(12),
+        compiler_params=params(32),
+        cost_estimate=cost(10),
         name="pair_update",
     )(
-        left_slots,
-        right_firsts,
-        *left,
+        places,
+        *lefts,
         *rights,
+        far_rights,
         weights,
         entry,
         switch,
-        couplings.reshape(rows * columns, depth),
+        near.reshape(all_rows * columns, depth),
+        far.reshape(rows * columns, depth),
     )
 
 
 def product_kernel(sides_ref, out_ref, *, grid_rows, grid_columns):
     channels, part, lanes = sides_ref.shape[1:]
-    half = lanes // 2
-    lane = lax.broadcasted_iota(jnp.int32, (grid_columns * part, lanes), 1)
+    half, quarter = lanes // 2, lanes // 4
+    places = grid_columns // 2
+    lane = lax.broadcasted_iota(jnp.int32, (places * part, lanes), 1)
     front = lane < half
     cut = front[: part // 2]
+    quarters = [(lane >= t * quarter) & (lane < (t + 1) * quarter) for t in range(3)]
     for channel in range(channels):
         lefts, rights = [], []
         for r in range(0, grid_rows, 2):
-            even, odd = [
-                jnp.concatenate(
-                    [sides_ref[(r + e) * grid_columns + c, channel] for c in range(grid_columns)],
+            turned = []
+            for target in range(4):
+                row, core = r + target // 2, target % 2
+                tile = jnp.concatenate(
+                    [
+                        sides_ref[row * grid_columns + 2 * place + core, channel]
+                        for place in range(places)
+                    ],
                     axis=0,
                 )
-                for e in range(2)
-            ]
-            lefts.append(jnp.where(front, even, pltpu.roll(odd, half, 1)))
-            rights.append(jnp.where(front, pltpu.roll(even, half, 1), odd))
+                turned.append(
+                    [tile] + [pltpu.roll(tile, t * quarter, 1) for t in range(1, 4)]
+                )
+            for side, made in enumerate((lefts, rights)):
+                by_core = []
+                for core in range(2):
+                    chosen = []
+                    for target in range(4):
+                        source = 2 * int(target % 2 != core) + side
+                        chosen.append(turned[target][(target - source) % 4])
+                    tile = chosen[3]
+                    for t in range(3):
+                        tile = jnp.where(quarters[t], chosen[t], tile)
+                    by_core.append(tile)
+                blocks = []
+                for place in range(places):
+                    for core in range(2):
+                        blocks.append(by_core[core][place * part : (place + 1) * part])
+                made.append(jnp.concatenate(blocks, axis=0))
         product = matmul_nt(jnp.concatenate(rights, axis=1), jnp.concatenate(lefts, axis=1))
         product = product.astype(BF16)
         for c in range(grid_columns):
@@ -576,22 +618,26 @@
 
 
 def output_kernel(
-    product_ref, final_ref, mid_hbm, gate_hbm, out_hbm, wide_ref, mid_ref, gate_ref, out_ref, *copied
+    core_ref, product_ref, final_ref, mid_hbm, gate_hbm, far_hbm, out_hbm, wide_ref, kept_ref, out_ref, *copied
 ):
     channels, part, lanes = product_ref.shape
-    columns, rows, depth = mid_ref.shape
+    _, _, columns, rows, depth = kept_ref.shape
     own = 8
+    core = core_ref[0]
     fetched, sent = copied
     fetches, sends = [], []
     for first in range(0, columns, own):
         chosen = pl.ds(first, own)
-        for source, target in ((mid_hbm, mid_ref), (gate_hbm, gate_ref)):
-            fetches.append(
-                pltpu.make_async_copy(
-                    source.at[chosen], target.at[chosen], fetched.at[len(fetches)]
+        for kind, near_hbm in enumerate((mid_hbm, gate_hbm)):
+            for source, half in ((near_hbm, core), (far_hbm.at[kind], 1 - core)):
+                fetches.append(
+                    pltpu.make_async_copy(
+                        source.at[chosen],
+                        kept_ref.at[kind, half, chosen],
+                        fetched.at[len(fetches)],
+                    )
                 )
-            )
-            fetches[-1].start()
+                fetches[-1].start()
     wide_ref[...] = product_ref[...].astype(F32).reshape(channels * part, lanes)
     for group in range(part // own):
         updates = []
@@ -600,13 +646,16 @@
             updates.append(matmul(normalise_rows(product).T, final_ref[...]))
         for half in range(2):
             cut = half * (part // own) + group
-            fetches[2 * cut].wait()
-            fetches[2 * cut + 1].wait()
-            out_rows = out_ref.at[cut].reshape(rows * own, depth)
+            for fetch in fetches[4 * cut : 4 * cut + 4]:
+                fetch.wait()
+            out_rows = out_ref.at[cut].reshape(2 * rows * own, depth)
             for j in range(own):
                 b = cut * own + j
-                piece = updates[j][half * rows : (half + 1) * rows]
-                out_rows[pl.ds(j, rows, stride=own), :] = mid_ref[b] + gate_ref[b] * piece
+                for side in range(2):
+                    first = (2 * half + side) * rows
+                    piece = kept_ref[1, side, b] * updates[j][first : first + rows]
+                    target = pl.ds(side * rows * own + j, rows, stride=own)
+                    out_rows[target, :] = kept_ref[0, side, b] + piece
             sends.append(
                 pltpu.make_async_copy(
                     out_ref.at[cut], out_hbm.at[:, pl.ds(cut * own, own)], sent.at[len(sends)]
@@ -617,31 +666,33 @@
         send.wait()
 
 
-def pair_result(product, mid, gate, final_matrix):
+def pair_result(core, product, mid, gate, far, final_matrix):
     channels, part, lanes = product.shape
     columns, rows, depth = mid.shape
+    smem = pl.BlockSpec(memory_space=pltpu.SMEM)
     vmem, hbm = pl.BlockSpec(memory_space=pltpu.VMEM), pl.BlockSpec(memory_space=pltpu.HBM)
     return pl.pallas_call(
         output_kernel,
-        in_specs=[vmem, vmem, hbm, hbm],
+        in_specs=[smem, vmem, vmem, hbm, hbm, hbm],
         out_specs=hbm,
-        out_shape=pltpu.HBM((rows, columns, depth), F32),
+        out_shape=pltpu.HBM((2 * rows, columns, depth), F32),
         scratch_shapes=[
             pltpu.VMEM((channels * part, lanes), F32),
-            pltpu.VMEM(mid.shape, F32),
-            pltpu.VMEM(mid.shape, F32),
-            pltpu.VMEM((columns // 8, rows, 8, depth), F32),
-            pltpu.SemaphoreType.DMA((columns // 4,)),
+            pltpu.VMEM((2, 2, columns, rows, depth), F32),
+            pltpu.VMEM((columns // 8, 2 * rows, 8, depth), F32),
+            pltpu.SemaphoreType.DMA((columns // 2,)),
             pltpu.SemaphoreType.DMA((columns // 8,)),
         ],
         compiler_params=params(16),
         cost_estimate=cost(3),
         name="pair_result",
     )(
+        core,
         product,
         final_matrix,
         pltpu.with_memory_space_constraint(mid, pltpu.HBM),
         pltpu.with_memory_space_constraint(gate, pltpu.HBM),
+        pltpu.with_memory_space_constraint(far, pltpu.HBM),
     )
 
 
@@ -657,43 +708,34 @@
         moves = []
         for r in range(rows):
             for q in range(rows):
-                for side in range(2):
-                    source = r * columns + 2 * q + side
-                    moves.append((source, q * columns + 2 * ((r + shift) % rows) + side))
+                for core in range(2):
+                    source = r * columns + 2 * q + core
+                    moves.append((source, q * columns + 2 * ((r + shift) % rows) + core))
         source = block if shift < 2 else later
         arrived.append(lax.ppermute(source, ("row", "col"), moves))
-    return jnp.stack(arrived)
-
-
-def both_cores(own):
+    residues = block.shape[0] // TENSOR_FEATURES
+    if residues % 8 == 0:
+        return arrived
+    joined = 8 // residues
+    own = jnp.take(jnp.stack(arrived), left_order(), axis=0)
+    own = own.reshape(rows // joined, joined, TENSOR_FEATURES, residues, -1)
+    own = jnp.transpose(own, (0, 2, 1, 3, 4))
+    return list(own.reshape(rows // joined, joined * block.shape[0], -1))
+
+
+def left_order():
     rows = lax.axis_size("row")
-    core = lax.rem(lax.axis_index("col"), 2)
-    other = swap_cores(own)
-    residues = own.shape[1] // TENSOR_FEATURES
-    if residues % 8 == 0:
-        return own, other
-    order = left_order(rows)
-    own, other = jnp.take(own, order, axis=0), jnp.take(other, order, axis=0)
-    joined = 8 // residues
-    ordered = []
-    for side in (jnp.where(core == 0, own, other), jnp.where(core == 0, other, own)):
-        side = side.reshape(rows // joined, joined, TENSOR_FEATURES, residues, -1)
-        side = jnp.transpose(side, (0, 2, 1, 3, 4))
-        ordered.append(side.reshape(rows // joined, joined * own.shape[1], -1))
-    return tuple(ordered)
-
-
-def left_order(rows):
     me = lax.axis_index("col") // 2
     return lax.rem(me - jnp.arange(rows, dtype=jnp.int32) + rows, rows)
 
 
-def left_groups(rows, residues):
+def pair_places(sources, residues):
     if residues % 8:
-        return jnp.arange(2 * rows * residues // 8, dtype=jnp.int32)
+        order = jnp.arange(lax.axis_size("row") * residues // 8, dtype=jnp.int32)
+    else:
+        order = left_order()
     core = lax.rem(lax.axis_index("col"), 2)
-    order = left_order(rows)
-    return jnp.concatenate([order + core * rows, order + (1 - core) * rows])
+    return order, sources * residues, core.astype(jnp.int32).reshape(1)
 
 
 def exchange_rows(pieces):
@@ -737,11 +779,10 @@
         attention_final_matrix.T,
         tensor_entry_matrices.T,
         paired_entries(incoming_entry_matrices),
-        sources * own_residues,
-        left_groups(row_count, own_residues),
+        *pair_places(sources, own_residues),
     )
     high, low, early = lax.optimization_barrier((high, low, early))
-    key_matrix, others, final_turned, tensor_turned, entries, firsts, slots = early
+    key_matrix, others, final_turned, tensor_turned, entries, slots, firsts, core = early
     low = exchange_rows(low)
     turned, *gated = attention(high, key_matrix, others)
     left_piece, right_piece = alignment(
@@ -750,19 +791,25 @@
 
     rights = exchange_rows([right_piece] * row_count)
     later, rights[1] = lax.optimization_barrier((left_piece, rights[1]))
-    own = gather_turned(left_piece, later)
-    own, rights = lax.optimization_barrier((own, rights))
-    mid, gate, sides = pair_update(
-        slots,
-        firsts,
-        both_cores(own),
+    lefts = gather_turned(left_piece, later)
+    far_rights = swap_cores(jnp.stack(rights))
+    half = couplings.shape[0] // 2
+    far = lax.dynamic_slice_in_dim(couplings, (1 - core[0]) * half, half)
+    far, rights[1] = lax.optimization_barrier((far, rights[1]))
+    far = swap_cores(far)
+    mid, gate, away, sides = pair_update(
+        jnp.concatenate([slots, firsts, core]),
+        lefts,
         rights,
+        far_rights,
         tensor_final_matrix,
         couplings,
+        far,
         entries,
         incoming_switch_matrix,
     )
-    gated, sides = lax.optimization_barrier((gated, sides))
+    gated, away, sides = lax.optimization_barrier((gated, away, sides))
+    away = swap_cores(away)
     gated = exchange_rows(gated)
 
     everywhere = ("row", "col")
@@ -770,7 +817,7 @@
     devices = row_count * column_count
     sides = sides.reshape(devices, C_TRI // devices, *sides.shape[1:])
     sides = lax.all_to_all(sides, everywhere, split_axis=0, concat_axis=0)
-    gated, sides = lax.optimization_barrier((gated, sides))
+    gated, away, sides = lax.optimization_barrier((gated, away, sides))
     product = triangle_product(sides, row_count, column_count)
     product = lax.all_to_all(product, everywhere, split_axis=0, concat_axis=0)
 
@@ -781,7 +828,7 @@
     )
     refreshed_homologs = homolog_tensor + change.reshape(homolog_tensor.shape)
     product = product.reshape(C_TRI, *product.shape[2:])
-    pair_output = pair_result(product, mid, gate, incoming_final_matrix)
+    pair_output = pair_result(core, product, mid, gate, away, incoming_final_matrix)
     return (refreshed_homologs, pair_output)
 
 

time: 128 us -> 143 us (1.12)
  starting transfers between devices: 34.4 us -> 44.8 us
  waiting for transfers between devices: 39.9 us -> 42.3 us
    ppermute x12, waiting for transfers between devices: 25.5 us -> 30.9 us  [exchange_rows(): arrived.append(lax.ppermute(pieces[shift], 'row', moves))]
    ppermute x4, starting transfers between devices: 12.3 us -> 17 us  [gather_turned(): arrived.append(lax.ppermute(source, ('row', 'col'), moves))]
    all_to_all x1, starting transfers between devices: 5.03 us -> 8.25 us  [body(): sides = lax.all_to_all(sides, everywhere, split_axis=0, concat_axis=0)]
    ppermute x1 -> x3, waiting for transfers between devices: 1.91 us -> 0.01 us  [swap_cores(): return lax.ppermute(block, 'col', [(c, c ^ 1) for c in range(count)])]
    unnamed x32 -> x52, local copies, waits for them, and re-layouts: 4.34 us -> 6.01 us
  transfers between devices with their start and end apart: 19 -> 21, of which waited for: 10 -> 10; matrix products, arithmetic and copies ran while one was open for 11% -> 9% of each run, Pallas kernels for 11% -> 10%
where the time goes in v10:
time: 143 us
  starting transfers between devices  44.8 us (31%)
  waiting for transfers between devices  42.3 us (30%)
  Pallas kernels  36.4 us (25%)
  local copies, waits for them, and re-layouts  10.1 us (7%)
  other arithmetic  4.4 us (3%)
  matrix products  3.41 us (2%)
    ppermute x12, waiting for transfers between devices, exchange_rows(): arrived.append(lax.ppermute(pieces[shift], 'row', moves))  30.9 us
    ppermute x4, starting transfers between devices, gather_turned(): arrived.append(lax.ppermute(source, ('row', 'col'), moves))  17 us
    ppermute x12, starting transfers between devices, exchange_rows(): arrived.append(lax.ppermute(pieces[shift], 'row', moves))  15.1 us
    pallas_call x1, Pallas kernels, attention(): pl.pallas_call(attention_kernel, grid=(residues // step,), in_specs=[pl.B...  9.32 us
    pallas_call x1, Pallas kernels, pair_update(): pl.pallas_call(functools.partial(pair_kernel, slots=len(lefts), pieces=le...  9.07 us
    all_to_all x1, starting transfers between devices, body(): sides = lax.all_to_all(sides, everywhere, split_axis=0, concat_axis=0)  8.25 us
    all_to_all x1, waiting for transfers between devices, body(): product = lax.all_to_all(product, everywhere, split_axis=0, concat_axis=0)  7.65 us
    unnamed x52, local copies, waits for them, and re-layouts  6.01 us
  transfers between devices with their start and end apart: 21, of which 10 were waited for; matrix products, arithmetic and copies ran while one was open for 9% of the time, Pallas kernels for 10%

profile of v10, /device:TPU:0, one launch (start us, length us, event | category | flops | bytes accessed | tf_op | source)
XLA Modules:
  0.0 142.6 jit_solution(13937632088990421493)
XLA Ops:
  0.6 0.0 copy-start.18
  0.7 0.0 copy-start.23
  0.7 0.0 copy-start.16
  0.7 4.5 %standardise_high.1 = (bf16[8,64,256]{2,1,0:T(8,128)(2,1)}, bf16[8,64,256]{2,1,0:T(8,128)(2,1)}, bf16[8,64,256]{2,1,0:T(8,128)(2,1)}, bf16[8,64,256]{2,1,0:T(8,128)(2,1)}) custom-call(s32[4]{0:T(128)S(1)} %iota_xor_fusion.sources_ref, f32[64,32,256]{2,1,0:T(8,128)} %second_ref.1), custom_call_target="tpu_custom_call" | custom-call | flops 3000000000 | bytes 3000000 | tf_op jit(solution)/shard_map/standardise_high/pallas_call | solution.py:117
  5.2 0.0 copy-start
  5.2 3.0 %collective-permute-start = (bf16[8,64,256]{2,1,0:T(8,128)(2,1)}, bf16[8,64,256]{2,1,0:T(8,128)(2,1)S(1)}, u32[]{:S(2)}, u32[]{:S(2)}) collective-permute-start(bf16[8,64,256]{2,1,0:T(8,128)(2,1)} %get-tuple-element.54), channel_id=1, source_target_pairs={{0,8},{8,0},{16,24},{24,16},{1,9},{9,1},{17,25},{25,17},{2,10},{10... | collective-permute-start | bytes 786440 | tf_op jit(solution)/shard_map/ppermute | solution.py:745
  8.2 1.5 %collective-permute-start.1 = (bf16[8,64,256]{2,1,0:T(8,128)(2,1)}, bf16[8,64,256]{2,1,0:T(8,128)(2,1)S(1)}, u32[]{:S(2)}, u32[]{:S(2)}) collective-permute-start(bf16[8,64,256]{2,1,0:T(8,128)(2,1)} %get-tuple-element.55), channel_id=1, source_target_pairs={{0,16},{8,24},{16,0},{24,8},{1,17},{9,25},{17,1},{25,9},{2,18},{10... | collective-permute-start | bytes 786440 | tf_op jit(solution)/shard_map/ppermute | solution.py:745
  9.7 0.0 collective-permute-start.2
  9.8 0.8 copy.17
  10.6 0.8 copy.12
  11.4 0.1 copy.14
  11.5 0.9 reshape.57
  12.4 0.1 copy.15
  12.6 1.0 pad_maximum_fusion.2.others_ref
  13.7 4.5 %standardise_low.1 = (bf16[528,256]{1,0:T(8,128)(2,1)}, bf16[528,256]{1,0:T(8,128)(2,1)}, bf16[528,256]{1,0:T(8,128)(2,1)}, bf16[528,256]{1,0:T(8,128)(2,1)}) custom-call(s32[4]{0:T(128)S(1)} %iota_xor_fusion.sources_ref, f32[64,32,256]{2,1,0:T(8,128)S(1)} %copy-done, f32[64,32,256]{2,1,0:T(8,128)S(1)} %copy-done), custom_call_target="tpu_custom_call" | custom-call | flops 4000000000 | bytes 4000000 | tf_op jit(solution)/shard_map/standardise_low/pallas_call | solution.py:169
  18.2 3.6 %collective-permute-done.1.rest_2_ = bf16[8,64,256]{2,1,0:T(8,128)(2,1)S(1)} collective-permute-done((bf16[8,64,256]{2,1,0:T(8,128)(2,1)}, bf16[8,64,256]{2,1,0:T(8,128)(2,1)S(1)}, u32[]{:S(2)}, u32[]{:S(2)}) %collective-permute-start.1) | collective-permute-done | bytes 262176 | tf_op jit(solution)/shard_map/ppermute | solution.py:745
  21.8 0.0 copy-start.15
  21.8 1.2 collective-permute-start.3
  23.0 0.9 collective-permute-start.4
  23.9 1.4 %collective-permute-start.5 = (bf16[528,256]{1,0:T(8,128)(2,1)}, bf16[528,256]{1,0:T(8,128)(2,1)S(1)}, u32[]{:S(2)}, u32[]{:S(2)}) collective-permute-start(bf16[528,256]{1,0:T(8,128)(2,1)} %get-tuple-element.80), channel_id=1, source_target_pairs={{0,24},{8,16},{16,8},{24,0},{1,25},{9,17},{17,9},{25,1},{2,26},{10... | collective-permute-start | bytes 811016 | tf_op jit(solution)/shard_map/ppermute | solution.py:745
  25.4 9.3 %attention.1 = (bf16[8,256,256]{2,1,0:T(8,128)(2,1)S(1)}, bf16[8,64,256]{2,1,0:T(8,128)(2,1)}, bf16[8,64,256]{2,1,0:T(8,128)(2,1)}, bf16[8,64,256]{2,1,0:T(8,128)(2,1)}, bf16[8,64,256]{2,1,0:T(8,128)(2,1)}) custom-call(bf16[256,256]{1,0:T(8,128)(2,1)S(1)} %slice.6.key_ref, bf16[768,256]{1,0:T(8,128)(2,1)S(1)} %pad_maximum_fusion.2.others_ref, ...), custom_call_target="tpu_custom_call" | custom-call | flops 10000000000 | bytes 10000000 | tf_op jit(solution)/shard_map/attention/pallas_call | solution.py:261
  34.7 0.0 collective-permute-done.3.rest_5_.rest_9_
  34.7 1.4 collective-permute-done.4.rest_6_.rest_10_
  36.1 0.9 copy-done.4
  37.1 0.9 copy-done.6
  38.0 0.9 copy-done.8
  39.0 3.8 %alignment.1 = (bf16[256,256]{1,0:T(8,128)(2,1)S(1)}, bf16[8,32,256]{2,1,0:T(8,128)(2,1)S(1)}) custom-call(s32[4]{0:T(128)S(1)} %iota_xor_fusion.sources_ref, bf16[8,256,256]{2,1,0:T(8,128)(2,1)S(1)} %get-tuple-element.74.turned_ref, bf16[256,256]{1,0:T(8,128)(2,1)S(1)} %bitcast.36, bf16[64,256]{1,0:T(8,128)(2,1)S(1)} %bitcast.40, ...), custom_call_target="tpu_custom_call" | custom-call | flops 4000000000 | bytes 4000000 | tf_op jit(solution)/shard_map/alignment/pallas_call | solution.py:342
  42.7 0.0 copy-start.9
  42.8 0.6 copy-done.9
  43.4 0.6 collective-permute-start.8
  44.0 1.2 collective-permute-start.11
  45.2 1.7 %collective-permute-start.12 = (bf16[8,32,256]{2,1,0:T(8,128)(2,1)S(1)}, bf16[8,32,256]{2,1,0:T(8,128)(2,1)}, u32[]{:S(2)}, u32[]{:S(2)}) collective-permute-start(bf16[8,32,256]{2,1,0:T(8,128)(2,1)S(1)} %get-tuple-element.82.rest_4_), channel_id=1, source_target_pairs={{0,24},{8,16},{16,8},{24,0},{1,25},{9,17},{17,9},{25,1},{2,26},{10... | collective-permute-start | bytes 393224 | tf_op jit(solution)/shard_map/ppermute | solution.py:745
  47.0 1.4 collective-permute-done.8.rest_5_
  48.4 1.0 collective-permute-done.11.rest_6_
  49.3 1.8 %collective-permute-done.12.rest_7_ = bf16[8,32,256]{2,1,0:T(8,128)(2,1)} collective-permute-done((bf16[8,32,256]{2,1,0:T(8,128)(2,1)S(1)}, bf16[8,32,256]{2,1,0:T(8,128)(2,1)}, u32[]{:S(2)}, u32[]{:S(2)}) %collective-permute-start.12) | collective-permute-done | bytes 131104 | tf_op jit(solution)/shard_map/ppermute | solution.py:745
  51.2 1.0 pad_maximum_fusion.1
  52.2 0.1 collective-permute-start.13
  52.3 0.5 collective-permute-start.14
  52.8 0.8 collective-permute-start.6
  53.6 3.6 %collective-permute-start.7 = (bf16[256,256]{1,0:T(8,128)(2,1)S(1)}, bf16[256,256]{1,0:T(8,128)(2,1)S(1)}, u32[]{:S(2)}, u32[]{:S(2)}) collective-permute-start(bf16[256,256]{1,0:T(8,128)(2,1)S(1)} %copy-done.10), channel_id=1, source_target_pairs={{0,2},{1,3},{2,10},{3,11},{4,18},{5,19},{6,26},{7,27},{8,4},{9,5},... | collective-permute-start | bytes 393224 | tf_op jit(solution)/shard_map/ppermute | solution.py:715
  57.2 3.5 %collective-permute-start.9 = (bf16[256,256]{1,0:T(8,128)(2,1)S(1)}, bf16[256,256]{1,0:T(8,128)(2,1)S(1)}, u32[]{:S(2)}, u32[]{:S(2)}) collective-permute-start(bf16[256,256]{1,0:T(8,128)(2,1)S(1)} %copy-done.10), channel_id=1, source_target_pairs={{0,4},{1,5},{2,12},{3,13},{4,20},{5,21},{6,28},{7,29},{8,6},{9,7},... | collective-permute-start | bytes 393224 | tf_op jit(solution)/shard_map/ppermute | solution.py:715
  60.7 9.1 %collective-permute-start.10 = (bf16[256,256]{1,0:T(8,128)(2,1)S(1)}, bf16[256,256]{1,0:T(8,128)(2,1)S(1)}, u32[]{:S(2)}, u32[]{:S(2)}) collective-permute-start(bf16[256,256]{1,0:T(8,128)(2,1)S(1)} %copy-done.10), channel_id=1, source_target_pairs={{0,6},{1,7},{2,14},{3,15},{4,22},{5,23},{6,30},{7,31},{8,0},{9,1},... | collective-permute-start | bytes 393224 | tf_op jit(solution)/shard_map/ppermute | solution.py:715
  69.8 0.1 pad_add_fusion.places_ref
  69.9 2.4 %collective-permute-done.10.rest_3_ = bf16[256,256]{1,0:T(8,128)(2,1)S(1)} collective-permute-done((bf16[256,256]{1,0:T(8,128)(2,1)S(1)}, bf16[256,256]{1,0:T(8,128)(2,1)S(1)}, u32[]{:S(2)}, u32[]{:S(2)}) %collective-permute-start.10) | collective-permute-done | bytes 131104 | tf_op jit(solution)/shard_map/ppermute | solution.py:715
  72.3 9.1 %pair_update.1 = (f32[32,32,128]{2,1,0:T(8,128)}, f32[32,32,128]{2,1,0:T(8,128)}, f32[2,32,32,128]{3,2,1,0:T(8,128)}, bf16[128,32,128]{2,1,0:T(8,128)(2,1)}) custom-call(s32[9]{0:T(128)S(1)} %pad_add_fusion.places_ref, bf16[256,256]{1,0:T(8,128)(2,1)S(1)} %collective-permute-done.6.rest_0_, bf16[256,256]{1,0:T(8,128)(2,1)S(1)} %collective-permute-done.7.rest_1_, ...), custom_call_target="tpu_custom_call" | custom-call | flops 10000000000 | bytes 10000000 | tf_op jit(solution)/shard_map/pair_update/pallas_call | solution.py:515
  81.4 8.3 %all-to-all-start = ((bf16[32,4,32,128]{3,2,1,0:T(8,128)(2,1)}), bf16[32,4,32,128]{3,2,1,0:T(8,128)(2,1)S(1)}, u32[]{:S(2)}, u32[]{:S(2)}) async-start(bf16[32,4,32,128]{3,2,1,0:T(8,128)(2,1)} %bitcast.43), calls=%async_computation | async-start | bytes 2097152 | tf_op jit(solution)/shard_map/all_to_all | solution.py:819
  89.7 0.3 collective-permute-start.18
  90.0 1.7 %collective-permute-start.15 = (bf16[8,64,256]{2,1,0:T(8,128)(2,1)}, bf16[8,64,256]{2,1,0:T(8,128)(2,1)S(1)}, u32[]{:S(2)}, u32[]{:S(2)}) collective-permute-start(bf16[8,64,256]{2,1,0:T(8,128)(2,1)} %get-tuple-element.91), channel_id=1, source_target_pairs={{0,8},{8,0},{16,24},{24,16},{1,9},{9,1},{17,25},{25,17},{2,10},{10... | collective-permute-start | bytes 786440 | tf_op jit(solution)/shard_map/ppermute | solution.py:745
  91.7 1.5 %collective-permute-start.16 = (bf16[8,64,256]{2,1,0:T(8,128)(2,1)}, bf16[8,64,256]{2,1,0:T(8,128)(2,1)S(1)}, u32[]{:S(2)}, u32[]{:S(2)}) collective-permute-start(bf16[8,64,256]{2,1,0:T(8,128)(2,1)} %get-tuple-element.92), channel_id=1, source_target_pairs={{0,16},{8,24},{16,0},{24,8},{1,17},{9,25},{17,1},{25,9},{2,18},{10... | collective-permute-start | bytes 786440 | tf_op jit(solution)/shard_map/ppermute | solution.py:745
  93.1 0.3 collective-permute-start.17
  93.5 13.5 %collective-permute-done.15 = bf16[8,64,256]{2,1,0:T(8,128)(2,1)S(1)} collective-permute-done((bf16[8,64,256]{2,1,0:T(8,128)(2,1)}, bf16[8,64,256]{2,1,0:T(8,128)(2,1)S(1)}, u32[]{:S(2)}, u32[]{:S(2)}) %collective-permute-start.15) | collective-permute-done | bytes 262176 | tf_op jit(solution)/shard_map/ppermute | solution.py:745
  106.9 8.3 %collective-permute-done.17 = bf16[8,64,256]{2,1,0:T(8,128)(2,1)S(1)} collective-permute-done((bf16[8,64,256]{2,1,0:T(8,128)(2,1)}, bf16[8,64,256]{2,1,0:T(8,128)(2,1)S(1)}, u32[]{:S(2)}, u32[]{:S(2)}) %collective-permute-start.17) | collective-permute-done | bytes 262176 | tf_op jit(solution)/shard_map/ppermute | solution.py:745
  115.2 0.7 copy-done.22
  115.9 1.3 all-to-all-done.sides_ref
  117.2 2.2 %triangle_product.1 = bf16[32,4,16,128]{3,2,1,0:T(8,128)(2,1)} custom-call(bf16[32,4,32,128]{3,2,1,0:T(8,128)(2,1)S(1)} %all-to-all-done.sides_ref), custom_call_target="tpu_custom_call" | custom-call | flops 3000000000 | bytes 3000000 | tf_op jit(solution)/shard_map/triangle_product/pallas_call | solution.py:608
  119.4 3.6 %all-to-all-start.1 = ((bf16[32,4,16,128]{3,2,1,0:T(8,128)(2,1)}), bf16[32,4,16,128]{3,2,1,0:T(8,128)(2,1)S(1)}, u32[]{:S(2)}, u32[]{:S(2)}) async-start(bf16[32,4,16,128]{3,2,1,0:T(8,128)(2,1)} %triangle_product.1), calls=%async_computation.1 | async-start | bytes 1048576 | tf_op jit(solution)/shard_map/all_to_all | solution.py:822
  123.1 0.1 broadcast_in_dim.14
  123.2 0.1 broadcast_in_dim.15
  123.3 0.0 copy-start.17
  123.3 2.2 %pad_maximum_fusion = bf16[4,8,64,256]{3,2,1,0:T(8,128)(2,1)} fusion(bf16[1,8,64,256]{3,2,1,0:T(8,128)(2,1)} %bitcast.49, bf16[1,8,64,256]{3,2,1,0:T(8,128)(2,1)} %bitcast.48, bf16[1,8,64,256]{3,2,1,0:T(8,128)(2,1)} %bitcast.47, bf16[1,8,64,256]{3,2,1,0:T(8,128)(2,1)S(1)} %bitcast.46), kind=kLoop, calls=%fused_computation.2 | loop fusion | flops 1572864 | bytes 2097152 | tf_op jit(solution)/shard_map/stack | solution.py:824
  125.6 2.8 %gather_fusion = bf16[4,8,64,256]{3,2,1,0:T(8,128)(2,1)} fusion(bf16[4,8,64,256]{3,2,1,0:T(8,128)(2,1)} %pad_maximum_fusion, s32[1024]{0:T(1024)S(1)} %pad_clamp_fusion), kind=kCustom, calls=%fused_computation | custom fusion | bytes 2097168 | tf_op jit(solution)/shard_map/jit(_take)/gather | solution.py:824
  128.4 3.4 %convolution_add_fusion = f32[64,32,256]{2,1,0:T(8,128)} fusion(f32[64,32,256]{2,1,0:T(8,128)S(1)} %copy-done, bf16[32,64,256]{2,1,0:T(8,128)(2,1)} %bitcast.41, pred[32]{0:T(512)(128)(4,1)S(1)} %broadcast_in_dim.15, bf16[256,256]{1,0:T(8,128)(2,1)S(1)} %copy-done.17), kind=kOutput, calls=%fused_computation.1 | convolution fusion | flops 269484032 | bytes 5373984 | tf_op jit(solution)/shard_map/dot_general | solution.py:826
  131.8 7.7 %all-to-all-done.1 = bf16[32,4,16,128]{3,2,1,0:T(8,128)(2,1)S(1)} async-done(((bf16[32,4,16,128]{3,2,1,0:T(8,128)(2,1)}), bf16[32,4,16,128]{3,2,1,0:T(8,128)(2,1)S(1)}, u32[]{:S(2)}, u32[]{:S(2)}) %all-to-all-start.1) | async-done | bytes 524320 | tf_op jit(solution)/shard_map/all_to_all | solution.py:822
  139.4 3.0 %pair_result.1 = f32[64,32,128]{2,1,0:T(8,128)} custom-call(s32[1]{0:T(128)} %bitcast.5.core_ref, bf16[128,16,128]{2,1,0:T(8,128)(2,1)S(1)} %bitcast.33, bf16[128,128]{1,0:T(8,128)(2,1)S(1)} %copy-done.13, f32[32,32,128]{2,1,0:T(8,128)} %get-tuple-element.101.mid_hbm, f32[32,32,128]{2,1,0:T(8,128)} %get-tuple-element.102.gate_hbm, ...), custom_call_target="tpu_custom_call" | custom-call | flops 3000000000 | bytes 3000000 | tf_op jit(solution)/shard_map/pair_result/pallas_call | solution.py:674
  (55 shorter events, 0.2 us)
Async XLA Ops:
  0.6 9.1 %copy-start.18 = (bf16[256,768]{1,0:T(8,128)(2,1)S(1)}, bf16[256,768]{1,0:T(8,128)(2,1)}, u32[]{:S(2)}) copy-start(bf16[256,768]{1,0:T(8,128)(2,1)} %param.13) | copy-start | bytes 1179652
  0.7 10.0 %copy-start.23 = (bf16[256,256]{1,0:T(8,128)(2,1)S(1)}, bf16[256,256]{1,0:T(8,128)(2,1)}, u32[]{:S(2)}) copy-start(bf16[256,256]{1,0:T(8,128)(2,1)} %param.12) | copy-start | bytes 393220
  0.7 10.7 %copy-start.16 = (bf16[256,256]{1,0:T(8,128)(2,1)S(1)}, bf16[256,256]{1,0:T(8,128)(2,1)}, u32[]{:S(2)}) copy-start(bf16[256,256]{1,0:T(8,128)(2,1)} %param.14) | copy-start | bytes 393220
  5.2 8.5 %copy-start = (f32[64,32,256]{2,1,0:T(8,128)S(1)}, f32[64,32,256]{2,1,0:T(8,128)}, u32[]{:S(2)}) copy-start(f32[64,32,256]{2,1,0:T(8,128)} %second_ref.1) | copy-start | bytes 6291460
  5.2 13.0 %collective-permute-start = (bf16[8,64,256]{2,1,0:T(8,128)(2,1)}, bf16[8,64,256]{2,1,0:T(8,128)(2,1)S(1)}, u32[]{:S(2)}, u32[]{:S(2)}) collective-permute-start(bf16[8,64,256]{2,1,0:T(8,128)(2,1)} %get-tuple-element.54), channel_id=1, source_target_pairs={{0,8},{8,0},{16,24},{24,16},{1,9},{9,1},{17,25},{25,17},{2,10},{10... | collective-permute-start | bytes 786440 | tf_op jit(solution)/shard_map/ppermute | solution.py:745
  8.2 13.6 %collective-permute-start.1 = (bf16[8,64,256]{2,1,0:T(8,128)(2,1)}, bf16[8,64,256]{2,1,0:T(8,128)(2,1)S(1)}, u32[]{:S(2)}, u32[]{:S(2)}) collective-permute-start(bf16[8,64,256]{2,1,0:T(8,128)(2,1)} %get-tuple-element.55), channel_id=1, source_target_pairs={{0,16},{8,24},{16,0},{24,8},{1,17},{9,25},{17,1},{25,9},{2,18},{10... | collective-permute-start | bytes 786440 | tf_op jit(solution)/shard_map/ppermute | solution.py:745
  9.7 12.1 %collective-permute-start.2 = (bf16[8,64,256]{2,1,0:T(8,128)(2,1)}, bf16[8,64,256]{2,1,0:T(8,128)(2,1)S(1)}, u32[]{:S(2)}, u32[]{:S(2)}) collective-permute-start(bf16[8,64,256]{2,1,0:T(8,128)(2,1)} %get-tuple-element.56), channel_id=1, source_target_pairs={{0,24},{8,16},{16,8},{24,0},{1,25},{9,17},{17,9},{25,1},{2,26},{10... | collective-permute-start | bytes 786440 | tf_op jit(solution)/shard_map/ppermute | solution.py:745
  13.7 11.7 %copy-start.14 = (bf16[8,64,256]{2,1,0:T(8,128)(2,1)S(1)}, bf16[8,64,256]{2,1,0:T(8,128)(2,1)}, u32[]{:S(2)}) copy-start(bf16[8,64,256]{2,1,0:T(8,128)(2,1)} %get-tuple-element.63.rest_0_) | copy-start | bytes 786436
  18.2 16.5 %copy-start.3 = (bf16[8,64,256]{2,1,0:T(8,128)(2,1)}, bf16[8,64,256]{2,1,0:T(8,128)(2,1)S(1)}, u32[]{:S(2)}) copy-start(bf16[8,64,256]{2,1,0:T(8,128)(2,1)S(1)} %collective-permute-done.rest_1_) | copy-start | bytes 786436
  21.8 12.9 %copy-start.5 = (bf16[8,64,256]{2,1,0:T(8,128)(2,1)}, bf16[8,64,256]{2,1,0:T(8,128)(2,1)S(1)}, u32[]{:S(2)}) copy-start(bf16[8,64,256]{2,1,0:T(8,128)(2,1)S(1)} %collective-permute-done.1.rest_2_) | copy-start | bytes 786436
  21.8 12.9 %copy-start.7 = (bf16[8,64,256]{2,1,0:T(8,128)(2,1)}, bf16[8,64,256]{2,1,0:T(8,128)(2,1)S(1)}, u32[]{:S(2)}) copy-start(bf16[8,64,256]{2,1,0:T(8,128)(2,1)S(1)} %collective-permute-done.2.rest_3_) | copy-start | bytes 786436
  21.8 14.3 %copy-start.11 = (bf16[256,64]{0,1:T(8,128)(2,1)S(1)}, bf16[256,64]{0,1:T(8,128)(2,1)}, u32[]{:S(2)}) copy-start(bf16[256,64]{0,1:T(8,128)(2,1)} %param.15) | copy-start | bytes 98308
  21.8 14.3 %copy-start.15 = (bf16[528,256]{1,0:T(8,128)(2,1)S(1)}, bf16[528,256]{1,0:T(8,128)(2,1)}, u32[]{:S(2)}) copy-start(bf16[528,256]{1,0:T(8,128)(2,1)} %get-tuple-element.77.rest_4_.rest_8_) | copy-start | bytes 811012
  21.8 12.9 %collective-permute-start.3 = (bf16[528,256]{1,0:T(8,128)(2,1)}, bf16[528,256]{1,0:T(8,128)(2,1)S(1)}, u32[]{:S(2)}, u32[]{:S(2)}) collective-permute-start(bf16[528,256]{1,0:T(8,128)(2,1)} %get-tuple-element.78), channel_id=1, source_target_pairs={{0,8},{8,0},{16,24},{24,16},{1,9},{9,1},{17,25},{25,17},{2,10},{10... | collective-permute-start | bytes 811016 | tf_op jit(solution)/shard_map/ppermute | solution.py:745
  23.0 13.1 %collective-permute-start.4 = (bf16[528,256]{1,0:T(8,128)(2,1)}, bf16[528,256]{1,0:T(8,128)(2,1)S(1)}, u32[]{:S(2)}, u32[]{:S(2)}) collective-permute-start(bf16[528,256]{1,0:T(8,128)(2,1)} %get-tuple-element.79), channel_id=1, source_target_pairs={{0,16},{8,24},{16,0},{24,8},{1,17},{9,25},{17,1},{25,9},{2,18},{10... | collective-permute-start | bytes 811016 | tf_op jit(solution)/shard_map/ppermute | solution.py:745
  23.9 12.2 %collective-permute-start.5 = (bf16[528,256]{1,0:T(8,128)(2,1)}, bf16[528,256]{1,0:T(8,128)(2,1)S(1)}, u32[]{:S(2)}, u32[]{:S(2)}) collective-permute-start(bf16[528,256]{1,0:T(8,128)(2,1)} %get-tuple-element.80), channel_id=1, source_target_pairs={{0,24},{8,16},{16,8},{24,0},{1,25},{9,17},{17,9},{25,1},{2,26},{10... | collective-permute-start | bytes 811016 | tf_op jit(solution)/shard_map/ppermute | solution.py:745
  36.1 1.0 copy-start.4
  37.1 0.9 copy-start.6
  38.0 0.9 copy-start.8
  39.0 7.9 %copy-start.1 = (f32[64,32,128]{2,1,0:T(8,128)S(1)}, f32[64,32,128]{2,1,0:T(8,128)}, u32[]{:S(2)}) copy-start(f32[64,32,128]{2,1,0:T(8,128)} %param.11) | copy-start | bytes 3145732
  42.7 0.7 copy-start.9
  43.4 5.0 %collective-permute-start.8 = (bf16[8,32,256]{2,1,0:T(8,128)(2,1)S(1)}, bf16[8,32,256]{2,1,0:T(8,128)(2,1)S(1)}, u32[]{:S(2)}, u32[]{:S(2)}) collective-permute-start(bf16[8,32,256]{2,1,0:T(8,128)(2,1)S(1)} %get-tuple-element.82.rest_4_), channel_id=1, source_target_pairs={{0,8},{8,0},{16,24},{24,16},{1,9},{9,1},{17,25},{25,17},{2,10},{10... | collective-permute-start | bytes 393224 | tf_op jit(solution)/shard_map/ppermute | solution.py:745
  44.0 5.4 %collective-permute-start.11 = (bf16[8,32,256]{2,1,0:T(8,128)(2,1)S(1)}, bf16[8,32,256]{2,1,0:T(8,128)(2,1)}, u32[]{:S(2)}, u32[]{:S(2)}) collective-permute-start(bf16[8,32,256]{2,1,0:T(8,128)(2,1)S(1)} %get-tuple-element.82.rest_4_), channel_id=1, source_target_pairs={{0,16},{8,24},{16,0},{24,8},{1,17},{9,25},{17,1},{25,9},{2,18},{10... | collective-permute-start | bytes 393224 | tf_op jit(solution)/shard_map/ppermute | solution.py:745
  45.2 6.0 %collective-permute-start.12 = (bf16[8,32,256]{2,1,0:T(8,128)(2,1)S(1)}, bf16[8,32,256]{2,1,0:T(8,128)(2,1)}, u32[]{:S(2)}, u32[]{:S(2)}) collective-permute-start(bf16[8,32,256]{2,1,0:T(8,128)(2,1)S(1)} %get-tuple-element.82.rest_4_), channel_id=1, source_target_pairs={{0,24},{8,16},{16,8},{24,0},{1,25},{9,17},{17,9},{25,1},{2,26},{10... | collective-permute-start | bytes 393224 | tf_op jit(solution)/shard_map/ppermute | solution.py:745
  46.9 5.9 %copy-start.10 = (bf16[256,256]{1,0:T(8,128)(2,1)S(1)}, bf16[256,256]{1,0:T(8,128)(2,1)}, u32[]{:S(2)}) copy-start(bf16[256,256]{1,0:T(8,128)(2,1)} %copy-done.9) | copy-start | bytes 393220
  46.9 25.4 %copy-start.2 = (bf16[1024,128]{1,0:T(8,128)(2,1)S(1)}, bf16[1024,128]{1,0:T(8,128)(2,1)}, u32[]{:S(2)}) copy-start(bf16[1024,128]{1,0:T(8,128)(2,1)} %rest_9_.1) | copy-start | bytes 786436
  46.9 25.4 %copy-start.12 = (bf16[128,128]{1,0:T(8,128)(2,1)S(1)}, bf16[128,128]{1,0:T(8,128)(2,1)}, u32[]{:S(2)}) copy-start(bf16[128,128]{1,0:T(8,128)(2,1)} %rest_11_.1) | copy-start | bytes 98308
  52.2 20.1 %collective-permute-start.13 = (bf16[4,8,32,256]{3,2,1,0:T(8,128)(2,1)S(1)}, bf16[4,8,32,256]{3,2,1,0:T(8,128)(2,1)S(1)}, u32[]{:S(2)}, u32[]{:S(2)}) collective-permute-start(bf16[4,8,32,256]{3,2,1,0:T(8,128)(2,1)S(1)} %pad_maximum_fusion.1), channel_id=1, source_target_pairs={{0,1},{1,0},{2,3},{3,2},{4,5},{5,4},{6,7},{7,6},{8,9},{9,8},{10,11... | collective-permute-start | bytes 1572872 | tf_op jit(solution)/shard_map/ppermute | solution.py:701
  52.3 20.0 %collective-permute-start.14 = (f32[32,32,128]{2,1,0:T(8,128)S(1)}, f32[32,32,128]{2,1,0:T(8,128)S(1)}, u32[]{:S(2)}, u32[]{:S(2)}) collective-permute-start(f32[32,32,128]{2,1,0:T(8,128)S(1)} %constant_dynamic-slice_fusion), channel_id=1, source_target_pairs={{0,1},{1,0},{2,3},{3,2},{4,5},{5,4},{6,7},{7,6},{8,9},{9,8},{10,11... | collective-permute-start | bytes 1572872 | tf_op jit(solution)/shard_map/ppermute | solution.py:701
  52.8 7.9 %collective-permute-start.6 = (bf16[256,256]{1,0:T(8,128)(2,1)S(1)}, bf16[256,256]{1,0:T(8,128)(2,1)S(1)}, u32[]{:S(2)}, u32[]{:S(2)}) collective-permute-start(bf16[256,256]{1,0:T(8,128)(2,1)S(1)} %copy-done.10), channel_id=1, source_target_pairs={{0,0},{1,1},{2,8},{3,9},{4,16},{5,17},{6,24},{7,25},{8,2},{9,3},{1... | collective-permute-start | bytes 393224 | tf_op jit(solution)/shard_map/ppermute | solution.py:715
  53.6 16.2 %collective-permute-start.7 = (bf16[256,256]{1,0:T(8,128)(2,1)S(1)}, bf16[256,256]{1,0:T(8,128)(2,1)S(1)}, u32[]{:S(2)}, u32[]{:S(2)}) collective-permute-start(bf16[256,256]{1,0:T(8,128)(2,1)S(1)} %copy-done.10), channel_id=1, source_target_pairs={{0,2},{1,3},{2,10},{3,11},{4,18},{5,19},{6,26},{7,27},{8,4},{9,5},... | collective-permute-start | bytes 393224 | tf_op jit(solution)/shard_map/ppermute | solution.py:715
  57.2 12.7 %collective-permute-start.9 = (bf16[256,256]{1,0:T(8,128)(2,1)S(1)}, bf16[256,256]{1,0:T(8,128)(2,1)S(1)}, u32[]{:S(2)}, u32[]{:S(2)}) collective-permute-start(bf16[256,256]{1,0:T(8,128)(2,1)S(1)} %copy-done.10), channel_id=1, source_target_pairs={{0,4},{1,5},{2,12},{3,13},{4,20},{5,21},{6,28},{7,29},{8,6},{9,7},... | collective-permute-start | bytes 393224 | tf_op jit(solution)/shard_map/ppermute | solution.py:715
  60.7 11.6 %collective-permute-start.10 = (bf16[256,256]{1,0:T(8,128)(2,1)S(1)}, bf16[256,256]{1,0:T(8,128)(2,1)S(1)}, u32[]{:S(2)}, u32[]{:S(2)}) collective-permute-start(bf16[256,256]{1,0:T(8,128)(2,1)S(1)} %copy-done.10), channel_id=1, source_target_pairs={{0,6},{1,7},{2,14},{3,15},{4,22},{5,23},{6,30},{7,31},{8,0},{9,1},... | collective-permute-start | bytes 393224 | tf_op jit(solution)/shard_map/ppermute | solution.py:715
  81.4 35.9 %all-to-all-start = ((bf16[32,4,32,128]{3,2,1,0:T(8,128)(2,1)}), bf16[32,4,32,128]{3,2,1,0:T(8,128)(2,1)S(1)}, u32[]{:S(2)}, u32[]{:S(2)}) async-start(bf16[32,4,32,128]{3,2,1,0:T(8,128)(2,1)} %bitcast.43), calls=%async_computation | async-start | bytes 2097152 | tf_op jit(solution)/shard_map/all_to_all | solution.py:819
  89.7 33.6 %copy-start.19 = (bf16[8,64,256]{2,1,0:T(8,128)(2,1)S(1)}, bf16[8,64,256]{2,1,0:T(8,128)(2,1)}, u32[]{:S(2)}) copy-start(bf16[8,64,256]{2,1,0:T(8,128)(2,1)} %get-tuple-element.96) | copy-start | bytes 786436
  89.7 26.3 %collective-permute-start.18 = (f32[2,32,32,128]{3,2,1,0:T(8,128)}, f32[2,32,32,128]{3,2,1,0:T(8,128)}, u32[]{:S(2)}, u32[]{:S(2)}) collective-permute-start(f32[2,32,32,128]{3,2,1,0:T(8,128)} %get-tuple-element.94), channel_id=1, source_target_pairs={{0,1},{1,0},{2,3},{3,2},{4,5},{5,4},{6,7},{7,6},{8,9},{9,8},{10,11... | collective-permute-start | bytes 3145736 | tf_op jit(solution)/shard_map/ppermute | solution.py:701
  90.0 16.9 %collective-permute-start.15 = (bf16[8,64,256]{2,1,0:T(8,128)(2,1)}, bf16[8,64,256]{2,1,0:T(8,128)(2,1)S(1)}, u32[]{:S(2)}, u32[]{:S(2)}) collective-permute-start(bf16[8,64,256]{2,1,0:T(8,128)(2,1)} %get-tuple-element.91), channel_id=1, source_target_pairs={{0,8},{8,0},{16,24},{24,16},{1,9},{9,1},{17,25},{25,17},{2,10},{10... | collective-permute-start | bytes 786440 | tf_op jit(solution)/shard_map/ppermute | solution.py:745
  91.7 15.3 %collective-permute-start.16 = (bf16[8,64,256]{2,1,0:T(8,128)(2,1)}, bf16[8,64,256]{2,1,0:T(8,128)(2,1)S(1)}, u32[]{:S(2)}, u32[]{:S(2)}) collective-permute-start(bf16[8,64,256]{2,1,0:T(8,128)(2,1)} %get-tuple-element.92), channel_id=1, source_target_pairs={{0,16},{8,24},{16,0},{24,8},{1,17},{9,25},{17,1},{25,9},{2,18},{10... | collective-permute-start | bytes 786440 | tf_op jit(solution)/shard_map/ppermute | solution.py:745
  93.1 22.1 %collective-permute-start.17 = (bf16[8,64,256]{2,1,0:T(8,128)(2,1)}, bf16[8,64,256]{2,1,0:T(8,128)(2,1)S(1)}, u32[]{:S(2)}, u32[]{:S(2)}) collective-permute-start(bf16[8,64,256]{2,1,0:T(8,128)(2,1)} %get-tuple-element.93), channel_id=1, source_target_pairs={{0,24},{8,16},{16,8},{24,0},{1,25},{9,17},{17,9},{25,1},{2,26},{10... | collective-permute-start | bytes 786440 | tf_op jit(solution)/shard_map/ppermute | solution.py:745
  106.9 8.3 %copy-start.20 = (bf16[8,64,256]{2,1,0:T(8,128)(2,1)}, bf16[8,64,256]{2,1,0:T(8,128)(2,1)S(1)}, u32[]{:S(2)}) copy-start(bf16[8,64,256]{2,1,0:T(8,128)(2,1)S(1)} %collective-permute-done.15) | copy-start | bytes 786436
  106.9 8.3 %copy-start.21 = (bf16[8,64,256]{2,1,0:T(8,128)(2,1)}, bf16[8,64,256]{2,1,0:T(8,128)(2,1)S(1)}, u32[]{:S(2)}) copy-start(bf16[8,64,256]{2,1,0:T(8,128)(2,1)S(1)} %collective-permute-done.16) | copy-start | bytes 786436
  115.2 0.7 copy-start.22
  119.4 20.0 %all-to-all-start.1 = ((bf16[32,4,16,128]{3,2,1,0:T(8,128)(2,1)}), bf16[32,4,16,128]{3,2,1,0:T(8,128)(2,1)S(1)}, u32[]{:S(2)}, u32[]{:S(2)}) async-start(bf16[32,4,16,128]{3,2,1,0:T(8,128)(2,1)} %triangle_product.1), calls=%async_computation.1 | async-start | bytes 1048576 | tf_op jit(solution)/shard_map/all_to_all | solution.py:822
  123.3 5.1 %copy-start.17 = (bf16[256,256]{1,0:T(8,128)(2,1)S(1)}, bf16[256,256]{1,0:T(8,128)(2,1)}, u32[]{:S(2)}) copy-start(bf16[256,256]{1,0:T(8,128)(2,1)} %param.14) | copy-start | bytes 393220
  128.4 11.1 %copy-start.13 = (bf16[128,128]{1,0:T(8,128)(2,1)S(1)}, bf16[128,128]{1,0:T(8,128)(2,1)}, u32[]{:S(2)}) copy-start(bf16[128,128]{1,0:T(8,128)(2,1)} %final_ref.1) | copy-start | bytes 98308

commit v11 on v9

--- a/solution.py
+++ b/solution.py
@@ -393,7 +393,7 @@
     columns = len(right_refs) * share
     groups = columns // GROUP
     wide = share * features
-    together = spread_ref.shape[1] // 128
+    together = spread_ref.shape[1] // 64
 
     for half, left_ref in enumerate((own_ref, other_ref)):
         piece = left_ref[...].reshape(slots * piece_rows, total)
@@ -403,14 +403,15 @@
             outer_ref[target, p * wide : (p + 1) * wide] = matmul_nt(piece, right) * (1.0 / total)
 
     spread_ref[...] = jnp.zeros_like(spread_ref)
+    front = lax.broadcasted_iota(jnp.int32, (rows, 128), 1) < 64
 
     def channel_step(p, carry):
         slot = lax.rem(p, 2)
         for e in range(together):
             source = pl.multiple_of((p * together + e) * features, features)
             piece = weights_ref[pl.ds(source, features), :]
-            for place in range(GROUP):
-                low = e * 128 + place * features
+            for place in range(2):
+                low = e * 64 + place * features
                 spread_ref[slot, low : low + features, place * C_Z : (place + 1) * C_Z] = piece
         pieces = []
         for g in range(groups):
@@ -422,7 +423,12 @@
                     source = pl.ds(pl.multiple_of(first, residues), residues)
                     channel.append(outer_ref[source, g * 128 : (g + 1) * 128])
                 parts.append(jnp.concatenate(channel, axis=0).astype(BF16))
-            pieces.append(jnp.concatenate(parts, axis=1))
+            lows, highs = [], []
+            for e in range(0, together, 2):
+                lows.append(jnp.where(front, parts[e], pltpu.roll(parts[e + 1], 64, 1)))
+                highs.append(jnp.where(front, pltpu.roll(parts[e], 64, 1), parts[e + 1]))
+            pieces.append(jnp.concatenate(lows, axis=1))
+            pieces.append(jnp.concatenate(highs, axis=1))
         update = matmul(jnp.concatenate(pieces, axis=0), spread_ref[slot])
 
         @pl.when(p == 0)
@@ -446,10 +452,11 @@
             p, n = divmod(g * GROUP + place, share)
             b = right_firsts[p] + n
             places.append(b)
-            lanes = slice(place * C_Z, (place + 1) * C_Z)
+            lanes = slice(place % 2 * C_Z, (place % 2 + 1) * C_Z)
+            start = (2 * g + place // 2) * rows
             pieces = []
             for first in left_firsts:
-                source = pl.ds(pl.multiple_of(g * rows + first, residues), residues)
+                source = pl.ds(pl.multiple_of(start + first, residues), residues)
                 pieces.append(sum_ref[source, lanes])
             mid = jnp.concatenate(pieces, axis=0)
             mid = mid + couplings_ref[pl.ds(b, rows, stride=columns), :]
@@ -506,8 +513,8 @@
         out_shape=[pltpu.HBM(whole.shape, F32)] * 2 + [pltpu.HBM(sides.shape, BF16)],
         scratch_shapes=[
             pltpu.VMEM((rows * TENSOR_FEATURES, columns * TENSOR_FEATURES), F32),
-            pltpu.VMEM((2, 8 * 128, GROUP * depth), BF16),
-            pltpu.VMEM((columns // GROUP * rows, GROUP * depth), F32),
+            pltpu.VMEM((2, 8 * 64, 2 * depth), BF16),
+            pltpu.VMEM((columns // 2 * rows, 2 * depth), F32),
             pltpu.VMEM((columns * C_TRI, 2 * rows), F32),
             pltpu.VMEM((rows * columns, depth), F32),
             pltpu.VMEM(whole.shape, F32),
@@ -650,7 +657,7 @@
     return lax.ppermute(block, "col", [(c, c ^ 1) for c in range(count)])
 
 
-def gather_turned(block, later):
+def gather_turned(block):
     rows, columns = lax.axis_size("row"), lax.axis_size("col")
     arrived = []
     for shift in range(rows):
@@ -660,9 +667,8 @@
                 for side in range(2):
                     source = r * columns + 2 * q + side
                     moves.append((source, q * columns + 2 * ((r + shift) % rows) + side))
-        source = block if shift < 2 else later
-        arrived.append(lax.ppermute(source, ("row", "col"), moves))
-    return jnp.stack(arrived)
+        arrived.append(lax.ppermute(block, ("row", "col"), moves))
+    return arrived
 
 
 def both_cores(own):
@@ -740,7 +746,7 @@
         sources * own_residues,
         left_groups(row_count, own_residues),
     )
-    high, low, early = lax.optimization_barrier((high, low, early))
+    high, _, early = lax.optimization_barrier((high, low, early))
     key_matrix, others, final_turned, tensor_turned, entries, firsts, slots = early
     low = exchange_rows(low)
     turned, *gated = attention(high, key_matrix, others)
@@ -748,9 +754,10 @@
         sources, high, low, turned, final_turned, tensor_turned
     )
 
+    lefts = gather_turned(left_piece)
+    right_piece, lefts[0] = lax.optimization_barrier((right_piece, lefts[0]))
     rights = exchange_rows([right_piece] * row_count)
-    later, rights[1] = lax.optimization_barrier((left_piece, rights[1]))
-    own = gather_turned(left_piece, later)
+    own = jnp.stack(lefts)
     own, rights = lax.optimization_barrier((own, rights))
     mid, gate, sides = pair_update(
         slots,

time: 128 us -> 134 us (1.047)
  starting transfers between devices: 34.4 us -> 38 us
  local copies, waits for them, and re-layouts: 9.1 us -> 12.6 us
  waiting for transfers between devices: 39.9 us -> 36.5 us
  other arithmetic: 3.36 us -> 5.24 us
    ppermute x12, starting transfers between devices: 14 us -> 18.7 us  [exchange_rows(): arrived.append(lax.ppermute(pieces[shift], 'row', moves))]
    unnamed x32 -> x36, local copies, waits for them, and re-layouts: 4.34 us -> 6.88 us
    ppermute x4, waiting for transfers between devices: 2.91 us -> 0.65 us  [gather_turned(): arrived.append(lax.ppermute(block, ('row', 'col'), moves))]
  transfers between devices with their start and end apart: 19 -> 19, of which waited for: 10 -> 8; matrix products, arithmetic and copies ran while one was open for 11% -> 14% of each run, Pallas kernels for 11% -> 11%
where the time goes in v11:
time: 134 us
  starting transfers between devices  38 us (28%)
  Pallas kernels  36.9 us (28%)
  waiting for transfers between devices  36.5 us (27%)
  local copies, waits for them, and re-layouts  12.6 us (9%)
  other arithmetic  5.24 us (4%)
  matrix products  3.41 us (3%)
    ppermute x12, waiting for transfers between devices, exchange_rows(): arrived.append(lax.ppermute(pieces[shift], 'row', moves))  24.4 us
    ppermute x12, starting transfers between devices, exchange_rows(): arrived.append(lax.ppermute(pieces[shift], 'row', moves))  18.7 us
    ppermute x4, starting transfers between devices, gather_turned(): arrived.append(lax.ppermute(block, ('row', 'col'), moves))  11.2 us
    pallas_call x1, Pallas kernels, attention(): pl.pallas_call(attention_kernel, grid=(residues // step,), in_specs=[pl.B...  10.4 us
    pallas_call x1, Pallas kernels, pair_update(): pl.pallas_call(pair_kernel, in_specs=[smem] * 2 + [vmem] * (5 + len(right...  8.66 us
    all_to_all x1, waiting for transfers between devices, body(): product = lax.all_to_all(product, everywhere, split_axis=0, concat_axis=0)  7.64 us
    unnamed x36, local copies, waits for them, and re-layouts  6.88 us
    all_to_all x1, starting transfers between devices, body(): sides = lax.all_to_all(sides, everywhere, split_axis=0, concat_axis=0)  5.07 us
  transfers between devices with their start and end apart: 19, of which 8 were waited for; matrix products, arithmetic and copies ran while one was open for 14% of the time, Pallas kernels for 11%

profile of v11, /device:TPU:0, one launch (start us, length us, event | category | flops | bytes accessed | tf_op | source)
XLA Modules:
  0.0 133.7 jit_solution(3750591002944213409)
XLA Ops:
  0.7 0.0 copy-start
  0.7 4.5 %standardise_high.1 = (bf16[8,64,256]{2,1,0:T(8,128)(2,1)}, bf16[8,64,256]{2,1,0:T(8,128)(2,1)}, bf16[8,64,256]{2,1,0:T(8,128)(2,1)}, bf16[8,64,256]{2,1,0:T(8,128)(2,1)}) custom-call(s32[4]{0:T(128)S(1)} %iota_xor_fusion.sources_ref, f32[64,32,256]{2,1,0:T(8,128)} %second_ref.1), custom_call_target="tpu_custom_call" | custom-call | flops 3000000000 | bytes 3000000 | tf_op jit(solution)/shard_map/standardise_high/pallas_call | solution.py:117
  5.2 3.0 %collective-permute-start = (bf16[8,64,256]{2,1,0:T(8,128)(2,1)}, bf16[8,64,256]{2,1,0:T(8,128)(2,1)S(1)}, u32[]{:S(2)}, u32[]{:S(2)}) collective-permute-start(bf16[8,64,256]{2,1,0:T(8,128)(2,1)} %get-tuple-element.49), channel_id=1, source_target_pairs={{0,8},{8,0},{16,24},{24,16},{1,9},{9,1},{17,25},{25,17},{2,10},{10... | collective-permute-start | bytes 786440 | tf_op jit(solution)/shard_map/ppermute | solution.py:709
  8.2 1.5 %collective-permute-start.1 = (bf16[8,64,256]{2,1,0:T(8,128)(2,1)}, bf16[8,64,256]{2,1,0:T(8,128)(2,1)S(1)}, u32[]{:S(2)}, u32[]{:S(2)}) collective-permute-start(bf16[8,64,256]{2,1,0:T(8,128)(2,1)} %get-tuple-element.50), channel_id=1, source_target_pairs={{0,16},{8,24},{16,0},{24,8},{1,17},{9,25},{17,1},{25,9},{2,18},{10... | collective-permute-start | bytes 786440 | tf_op jit(solution)/shard_map/ppermute | solution.py:709
  9.8 0.0 collective-permute-start.2
  9.8 4.5 %standardise_low.1 = (bf16[528,256]{1,0:T(8,128)(2,1)}, bf16[528,256]{1,0:T(8,128)(2,1)}, bf16[528,256]{1,0:T(8,128)(2,1)}, bf16[528,256]{1,0:T(8,128)(2,1)}) custom-call(s32[4]{0:T(128)S(1)} %iota_xor_fusion.sources_ref, f32[64,32,256]{2,1,0:T(8,128)S(1)} %copy-done, f32[64,32,256]{2,1,0:T(8,128)S(1)} %copy-done), custom_call_target="tpu_custom_call" | custom-call | flops 4000000000 | bytes 4000000 | tf_op jit(solution)/shard_map/standardise_low/pallas_call | solution.py:169
  14.3 2.0 %collective-permute-start.3 = (bf16[528,256]{1,0:T(8,128)(2,1)}, bf16[528,256]{1,0:T(8,128)(2,1)S(1)}, u32[]{:S(2)}, u32[]{:S(2)}) collective-permute-start(bf16[528,256]{1,0:T(8,128)(2,1)} %get-tuple-element.53), channel_id=1, source_target_pairs={{0,8},{8,0},{16,24},{24,16},{1,9},{9,1},{17,25},{25,17},{2,10},{10... | collective-permute-start | bytes 811016 | tf_op jit(solution)/shard_map/ppermute | solution.py:709
  16.3 1.5 %collective-permute-start.4 = (bf16[528,256]{1,0:T(8,128)(2,1)}, bf16[528,256]{1,0:T(8,128)(2,1)S(1)}, u32[]{:S(2)}, u32[]{:S(2)}) collective-permute-start(bf16[528,256]{1,0:T(8,128)(2,1)} %get-tuple-element.54), channel_id=1, source_target_pairs={{0,16},{8,24},{16,0},{24,8},{1,17},{9,25},{17,1},{25,9},{2,18},{10... | collective-permute-start | bytes 811016 | tf_op jit(solution)/shard_map/ppermute | solution.py:709
  17.8 0.6 broadcast_add_fusion
  18.4 0.5 broadcast_multiply_fusion.right_firsts_ref
  19.0 0.7 slice.7
  19.7 0.9 slice.6.key_ref
  20.6 1.8 %copy.17 = bf16[256,512]{0,1:T(8,128)(2,1)} copy(bf16[256,512]{1,0:T(8,128)(2,1)} %slice.7) | data formatting | bytes 524288
  22.4 1.7 %copy.12 = bf16[256,256]{0,1:T(8,128)(2,1)} copy(bf16[256,256]{1,0:T(8,128)(2,1)} %param.12) | data formatting | bytes 262144 | tf_op args[2]
  24.1 0.9 reshape.47
  25.0 0.1 copy.15
  25.2 1.0 copy.14
  26.2 0.8 pad_add_fusion.left_slots_ref
  26.9 1.0 pad_maximum_fusion.2.others_ref
  27.9 0.0 collective-permute-done.rest_1_
  28.0 0.1 collective-permute-start.5
  28.0 0.0 collective-permute-done.1.rest_2_
  28.1 0.9 copy-done.9
  29.0 10.4 %attention.1 = (bf16[8,256,256]{2,1,0:T(8,128)(2,1)S(1)}, bf16[8,64,256]{2,1,0:T(8,128)(2,1)}, bf16[8,64,256]{2,1,0:T(8,128)(2,1)}, bf16[8,64,256]{2,1,0:T(8,128)(2,1)}, bf16[8,64,256]{2,1,0:T(8,128)(2,1)}) custom-call(bf16[256,256]{1,0:T(8,128)(2,1)S(1)} %slice.6.key_ref, bf16[768,256]{1,0:T(8,128)(2,1)S(1)} %pad_maximum_fusion.2.others_ref, ...), custom_call_target="tpu_custom_call" | custom-call | flops 10000000000 | bytes 10000000 | tf_op jit(solution)/shard_map/attention/pallas_call | solution.py:261
  39.4 0.0 collective-permute-done.5.rest_7_.rest_11_
  39.5 0.0 copy-start.1
  39.5 0.0 copy-start.2
  39.5 0.0 copy-start.4
  39.5 4.3 %alignment.1 = (bf16[256,256]{1,0:T(8,128)(2,1)S(1)}, bf16[8,32,256]{2,1,0:T(8,128)(2,1)S(1)}) custom-call(s32[4]{0:T(128)S(1)} %copy-done.7, bf16[8,256,256]{2,1,0:T(8,128)(2,1)S(1)} %get-tuple-element.68.turned_ref, bf16[256,256]{1,0:T(8,128)(2,1)S(1)} %bitcast.32, bf16[64,256]{1,0:T(8,128)(2,1)S(1)} %bitcast.34, bf16[8,64,256]{2,1,0:T(8,128)(2,1)S(1)} %copy-done.9, ...), custom_call_target="tpu_custom_call" | custom-call | flops 4000000000 | bytes 4000000 | tf_op jit(solution)/shard_map/alignment/pallas_call | solution.py:342
  43.8 0.7 collective-permute-start.6
  44.5 4.7 %collective-permute-start.7 = (bf16[256,256]{1,0:T(8,128)(2,1)S(1)}, bf16[256,256]{1,0:T(8,128)(2,1)S(1)}, u32[]{:S(2)}, u32[]{:S(2)}) collective-permute-start(bf16[256,256]{1,0:T(8,128)(2,1)S(1)} %get-tuple-element.72), channel_id=1, source_target_pairs={{0,2},{1,3},{2,10},{3,11},{4,18},{5,19},{6,26},{7,27},{8,4},{9,5},... | collective-permute-start | bytes 393224 | tf_op jit(solution)/shard_map/ppermute | solution.py:670
  49.2 3.5 %collective-permute-start.8 = (bf16[256,256]{1,0:T(8,128)(2,1)S(1)}, bf16[256,256]{1,0:T(8,128)(2,1)S(1)}, u32[]{:S(2)}, u32[]{:S(2)}) collective-permute-start(bf16[256,256]{1,0:T(8,128)(2,1)S(1)} %get-tuple-element.72), channel_id=1, source_target_pairs={{0,4},{1,5},{2,12},{3,13},{4,20},{5,21},{6,28},{7,29},{8,6},{9,7},... | collective-permute-start | bytes 393224 | tf_op jit(solution)/shard_map/ppermute | solution.py:670
  52.7 2.3 %collective-permute-start.9 = (bf16[256,256]{1,0:T(8,128)(2,1)S(1)}, bf16[256,256]{1,0:T(8,128)(2,1)S(1)}, u32[]{:S(2)}, u32[]{:S(2)}) collective-permute-start(bf16[256,256]{1,0:T(8,128)(2,1)S(1)} %get-tuple-element.72), channel_id=1, source_target_pairs={{0,6},{1,7},{2,14},{3,15},{4,22},{5,23},{6,30},{7,31},{8,0},{9,1},... | collective-permute-start | bytes 393224 | tf_op jit(solution)/shard_map/ppermute | solution.py:670
  55.0 0.0 collective-permute-done.6
  55.0 1.0 collective-permute-start.10
  56.0 4.5 %collective-permute-start.11 = (bf16[8,32,256]{2,1,0:T(8,128)(2,1)S(1)}, bf16[8,32,256]{2,1,0:T(8,128)(2,1)S(1)}, u32[]{:S(2)}, u32[]{:S(2)}) collective-permute-start(bf16[8,32,256]{2,1,0:T(8,128)(2,1)S(1)} %get-tuple-element.76.rest_0_), channel_id=1, source_target_pairs={{0,16},{8,24},{16,0},{24,8},{1,17},{9,25},{17,1},{25,9},{2,18},{10... | collective-permute-start | bytes 393224 | tf_op jit(solution)/shard_map/ppermute | solution.py:709
  60.5 0.0 collective-permute-done.7
  60.5 1.5 %collective-permute-start.12 = (bf16[8,32,256]{2,1,0:T(8,128)(2,1)S(1)}, bf16[8,32,256]{2,1,0:T(8,128)(2,1)S(1)}, u32[]{:S(2)}, u32[]{:S(2)}) collective-permute-start(bf16[8,32,256]{2,1,0:T(8,128)(2,1)S(1)} %get-tuple-element.76.rest_0_), channel_id=1, source_target_pairs={{0,24},{8,16},{16,8},{24,0},{1,25},{9,17},{17,9},{25,1},{2,26},{10... | collective-permute-start | bytes 393224 | tf_op jit(solution)/shard_map/ppermute | solution.py:709
  62.0 0.6 collective-permute-done.9
  62.6 0.1 pad_maximum_fusion.1.own_ref
  62.7 1.3 collective-permute-done.10.rest_1_
  64.0 0.0 collective-permute-done.11.rest_2_
  64.0 2.4 %collective-permute-done.12.rest_3_ = bf16[8,32,256]{2,1,0:T(8,128)(2,1)S(1)} collective-permute-done((bf16[8,32,256]{2,1,0:T(8,128)(2,1)S(1)}, bf16[8,32,256]{2,1,0:T(8,128)(2,1)S(1)}, u32[]{:S(2)}, u32[]{:S(2)}) %collective-permute-start.12) | collective-permute-done | bytes 131104 | tf_op jit(solution)/shard_map/ppermute | solution.py:709
  66.4 1.9 %collective-permute-done.13.other_ref = bf16[4,256,256]{2,1,0:T(8,128)(2,1)S(1)} collective-permute-done((bf16[4,256,256]{2,1,0:T(8,128)(2,1)S(1)}, bf16[4,256,256]{2,1,0:T(8,128)(2,1)S(1)}, u32[]{:S(2)}, u32[]{:S(2)}) %collective-permute-start.13) | collective-permute-done | bytes 524320 | tf_op jit(solution)/shard_map/ppermute | solution.py:657
  68.3 8.7 %pair_update.1 = (f32[32,64,128]{2,1,0:T(8,128)}, f32[32,64,128]{2,1,0:T(8,128)}, bf16[128,32,128]{2,1,0:T(8,128)(2,1)}) custom-call(s32[8]{0:T(128)S(1)} %pad_add_fusion.left_slots_ref, s32[4]{0:T(128)S(1)} %copy-done.8, bf16[4,256,256]{2,1,0:T(8,128)(2,1)S(1)} %pad_maximum_fusion.1.own_ref, bf16[4,256,256]{2,1,0:T(8,128)(2,1)S(1)} %collective-permute-done.13.other_ref, ...), custom_call_target="tpu_custom_call" | custom-call | flops 12000000000 | bytes 12000000 | tf_op jit(solution)/shard_map/pair_update/pallas_call | solution.py:509
  77.0 5.1 %all-to-all-start = ((bf16[32,4,32,128]{3,2,1,0:T(8,128)(2,1)}), bf16[32,4,32,128]{3,2,1,0:T(8,128)(2,1)S(1)}, u32[]{:S(2)}, u32[]{:S(2)}) async-start(bf16[32,4,32,128]{3,2,1,0:T(8,128)(2,1)} %bitcast.37), calls=%async_computation | async-start | bytes 2097152 | tf_op jit(solution)/shard_map/all_to_all | solution.py:779
  82.1 1.8 %collective-permute-start.14 = (bf16[8,64,256]{2,1,0:T(8,128)(2,1)}, bf16[8,64,256]{2,1,0:T(8,128)(2,1)S(1)}, u32[]{:S(2)}, u32[]{:S(2)}) collective-permute-start(bf16[8,64,256]{2,1,0:T(8,128)(2,1)} %get-tuple-element.83), channel_id=1, source_target_pairs={{0,8},{8,0},{16,24},{24,16},{1,9},{9,1},{17,25},{25,17},{2,10},{10... | collective-permute-start | bytes 786440 | tf_op jit(solution)/shard_map/ppermute | solution.py:709
  83.9 1.5 %collective-permute-start.15 = (bf16[8,64,256]{2,1,0:T(8,128)(2,1)}, bf16[8,64,256]{2,1,0:T(8,128)(2,1)S(1)}, u32[]{:S(2)}, u32[]{:S(2)}) collective-permute-start(bf16[8,64,256]{2,1,0:T(8,128)(2,1)} %get-tuple-element.84), channel_id=1, source_target_pairs={{0,16},{8,24},{16,0},{24,8},{1,17},{9,25},{17,1},{25,9},{2,18},{10... | collective-permute-start | bytes 786440 | tf_op jit(solution)/shard_map/ppermute | solution.py:709
  85.4 0.3 collective-permute-start.16
  85.6 13.7 %collective-permute-done.14 = bf16[8,64,256]{2,1,0:T(8,128)(2,1)S(1)} collective-permute-done((bf16[8,64,256]{2,1,0:T(8,128)(2,1)}, bf16[8,64,256]{2,1,0:T(8,128)(2,1)S(1)}, u32[]{:S(2)}, u32[]{:S(2)}) %collective-permute-start.14) | collective-permute-done | bytes 262176 | tf_op jit(solution)/shard_map/ppermute | solution.py:709
  99.4 0.7 copy-done.14
  100.1 0.7 copy-done.15
  100.8 7.0 %collective-permute-done.16 = bf16[8,64,256]{2,1,0:T(8,128)(2,1)} collective-permute-done((bf16[8,64,256]{2,1,0:T(8,128)(2,1)}, bf16[8,64,256]{2,1,0:T(8,128)(2,1)}, u32[]{:S(2)}, u32[]{:S(2)}) %collective-permute-start.16) | collective-permute-done | bytes 262176 | tf_op jit(solution)/shard_map/ppermute | solution.py:709
  107.7 1.9 %all-to-all-done.sides_ref = bf16[32,4,32,128]{3,2,1,0:T(8,128)(2,1)S(1)} async-done(((bf16[32,4,32,128]{3,2,1,0:T(8,128)(2,1)}), bf16[32,4,32,128]{3,2,1,0:T(8,128)(2,1)S(1)}, u32[]{:S(2)}, u32[]{:S(2)}) %all-to-all-start) | async-done | bytes 1048608 | tf_op jit(solution)/shard_map/all_to_all | solution.py:779
  109.7 1.6 %triangle_product.1 = bf16[32,4,16,128]{3,2,1,0:T(8,128)(2,1)} custom-call(bf16[32,4,32,128]{3,2,1,0:T(8,128)(2,1)S(1)} %all-to-all-done.sides_ref), custom_call_target="tpu_custom_call" | custom-call | flops 3000000000 | bytes 3000000 | tf_op jit(solution)/shard_map/triangle_product/pallas_call | solution.py:573
  111.3 3.0 %all-to-all-start.1 = ((bf16[32,4,16,128]{3,2,1,0:T(8,128)(2,1)}), bf16[32,4,16,128]{3,2,1,0:T(8,128)(2,1)S(1)}, u32[]{:S(2)}, u32[]{:S(2)}) async-start(bf16[32,4,16,128]{3,2,1,0:T(8,128)(2,1)} %triangle_product.1), calls=%async_computation.1 | async-start | bytes 1048576 | tf_op jit(solution)/shard_map/all_to_all | solution.py:782
  114.4 0.1 broadcast_in_dim.14
  114.4 0.1 broadcast_in_dim.15
  114.5 0.0 copy-start.11
  114.6 2.2 %pad_maximum_fusion = bf16[4,8,64,256]{3,2,1,0:T(8,128)(2,1)} fusion(bf16[1,8,64,256]{3,2,1,0:T(8,128)(2,1)} %bitcast.14, bf16[1,8,64,256]{3,2,1,0:T(8,128)(2,1)} %bitcast.42, bf16[1,8,64,256]{3,2,1,0:T(8,128)(2,1)} %bitcast.41, bf16[1,8,64,256]{3,2,1,0:T(8,128)(2,1)S(1)} %bitcast.40), kind=kLoop, calls=%fused_computation.2 | loop fusion | flops 1572864 | bytes 2097152 | tf_op jit(solution)/shard_map/stack | solution.py:784
  116.8 2.8 %gather_fusion = bf16[4,8,64,256]{3,2,1,0:T(8,128)(2,1)} fusion(bf16[4,8,64,256]{3,2,1,0:T(8,128)(2,1)} %pad_maximum_fusion, s32[1024]{0:T(1024)S(1)} %pad_clamp_fusion), kind=kCustom, calls=%fused_computation | custom fusion | bytes 2097168 | tf_op jit(solution)/shard_map/jit(_take)/gather | solution.py:784
  119.6 3.4 %convolution_add_fusion = f32[64,32,256]{2,1,0:T(8,128)} fusion(f32[64,32,256]{2,1,0:T(8,128)S(1)} %copy-done, bf16[32,64,256]{2,1,0:T(8,128)(2,1)} %bitcast.35, pred[32]{0:T(512)(128)(4,1)S(1)} %broadcast_in_dim.15, bf16[256,256]{1,0:T(8,128)(2,1)S(1)} %copy-done.11), kind=kOutput, calls=%fused_computation.1 | convolution fusion | flops 269484032 | bytes 5373984 | tf_op jit(solution)/shard_map/dot_general | solution.py:786
  123.0 7.6 %all-to-all-done.1 = bf16[32,4,16,128]{3,2,1,0:T(8,128)(2,1)S(1)} async-done(((bf16[32,4,16,128]{3,2,1,0:T(8,128)(2,1)}), bf16[32,4,16,128]{3,2,1,0:T(8,128)(2,1)S(1)}, u32[]{:S(2)}, u32[]{:S(2)}) %all-to-all-start.1) | async-done | bytes 524320 | tf_op jit(solution)/shard_map/all_to_all | solution.py:782
  130.7 2.8 %pair_result.1 = f32[64,32,128]{2,1,0:T(8,128)} custom-call(bf16[128,16,128]{2,1,0:T(8,128)(2,1)S(1)} %bitcast.30, bf16[128,128]{1,0:T(8,128)(2,1)S(1)} %copy-done.5, f32[32,64,128]{2,1,0:T(8,128)} %get-tuple-element.92.mid_hbm, f32[32,64,128]{2,1,0:T(8,128)} %get-tuple-element.93.gate_hbm), custom_call_target="tpu_custom_call" | custom-call | flops 3000000000 | bytes 3000000 | tf_op jit(solution)/shard_map/pair_result/pallas_call | solution.py:631
  (35 shorter events, 0.1 us)
Async XLA Ops:
  0.6 9.1 %copy-start.6 = (s32[4]{0:T(128)}, s32[4]{0:T(128)S(1)}, u32[]{:S(2)}) copy-start(s32[4]{0:T(128)S(1)} %iota_xor_fusion.sources_ref) | copy-start | bytes 52
  0.7 9.1 %copy-start = (f32[64,32,256]{2,1,0:T(8,128)S(1)}, f32[64,32,256]{2,1,0:T(8,128)}, u32[]{:S(2)}) copy-start(f32[64,32,256]{2,1,0:T(8,128)} %second_ref.1) | copy-start | bytes 6291460
  5.2 22.7 %collective-permute-start = (bf16[8,64,256]{2,1,0:T(8,128)(2,1)}, bf16[8,64,256]{2,1,0:T(8,128)(2,1)S(1)}, u32[]{:S(2)}, u32[]{:S(2)}) collective-permute-start(bf16[8,64,256]{2,1,0:T(8,128)(2,1)} %get-tuple-element.49), channel_id=1, source_target_pairs={{0,8},{8,0},{16,24},{24,16},{1,9},{9,1},{17,25},{25,17},{2,10},{10... | collective-permute-start | bytes 786440 | tf_op jit(solution)/shard_map/ppermute | solution.py:709
  8.2 19.8 %collective-permute-start.1 = (bf16[8,64,256]{2,1,0:T(8,128)(2,1)}, bf16[8,64,256]{2,1,0:T(8,128)(2,1)S(1)}, u32[]{:S(2)}, u32[]{:S(2)}) collective-permute-start(bf16[8,64,256]{2,1,0:T(8,128)(2,1)} %get-tuple-element.50), channel_id=1, source_target_pairs={{0,16},{8,24},{16,0},{24,8},{1,17},{9,25},{17,1},{25,9},{2,18},{10... | collective-permute-start | bytes 786440 | tf_op jit(solution)/shard_map/ppermute | solution.py:709
  9.7 9.2 %copy-start.12 = (bf16[256,768]{1,0:T(8,128)(2,1)S(1)}, bf16[256,768]{1,0:T(8,128)(2,1)}, u32[]{:S(2)}) copy-start(bf16[256,768]{1,0:T(8,128)(2,1)} %param.13) | copy-start | bytes 1179652
  9.8 18.3 %collective-permute-start.2 = (bf16[8,64,256]{2,1,0:T(8,128)(2,1)}, bf16[8,64,256]{2,1,0:T(8,128)(2,1)}, u32[]{:S(2)}, u32[]{:S(2)}) collective-permute-start(bf16[8,64,256]{2,1,0:T(8,128)(2,1)} %get-tuple-element.51), channel_id=1, source_target_pairs={{0,24},{8,16},{16,8},{24,0},{1,25},{9,17},{17,9},{25,1},{2,26},{10... | collective-permute-start | bytes 786440 | tf_op jit(solution)/shard_map/ppermute | solution.py:709
  14.3 25.1 %collective-permute-start.3 = (bf16[528,256]{1,0:T(8,128)(2,1)}, bf16[528,256]{1,0:T(8,128)(2,1)S(1)}, u32[]{:S(2)}, u32[]{:S(2)}) collective-permute-start(bf16[528,256]{1,0:T(8,128)(2,1)} %get-tuple-element.53), channel_id=1, source_target_pairs={{0,8},{8,0},{16,24},{24,16},{1,9},{9,1},{17,25},{25,17},{2,10},{10... | collective-permute-start | bytes 811016 | tf_op jit(solution)/shard_map/ppermute | solution.py:709
  16.3 23.1 %collective-permute-start.4 = (bf16[528,256]{1,0:T(8,128)(2,1)}, bf16[528,256]{1,0:T(8,128)(2,1)S(1)}, u32[]{:S(2)}, u32[]{:S(2)}) collective-permute-start(bf16[528,256]{1,0:T(8,128)(2,1)} %get-tuple-element.54), channel_id=1, source_target_pairs={{0,16},{8,24},{16,0},{24,8},{1,17},{9,25},{17,1},{25,9},{2,18},{10... | collective-permute-start | bytes 811016 | tf_op jit(solution)/shard_map/ppermute | solution.py:709
  28.0 11.5 %collective-permute-start.5 = (bf16[528,256]{1,0:T(8,128)(2,1)}, bf16[528,256]{1,0:T(8,128)(2,1)S(1)}, u32[]{:S(2)}, u32[]{:S(2)}) collective-permute-start(bf16[528,256]{1,0:T(8,128)(2,1)} %get-tuple-element.55), channel_id=1, source_target_pairs={{0,24},{8,16},{16,8},{24,0},{1,25},{9,17},{17,9},{25,1},{2,26},{10... | collective-permute-start | bytes 811016 | tf_op jit(solution)/shard_map/ppermute | solution.py:709
  28.1 1.0 copy-start.9
  29.0 10.4 %copy-start.3 = (bf16[256,64]{0,1:T(8,128)(2,1)S(1)}, bf16[256,64]{0,1:T(8,128)(2,1)}, u32[]{:S(2)}) copy-start(bf16[256,64]{0,1:T(8,128)(2,1)} %param.15) | copy-start | bytes 98308
  29.0 10.4 %copy-start.7 = (s32[4]{0:T(128)S(1)}, s32[4]{0:T(128)}, u32[]{:S(2)}) copy-start(s32[4]{0:T(128)} %copy-done.6) | copy-start | bytes 52
  29.0 10.4 %copy-start.10 = (bf16[528,256]{1,0:T(8,128)(2,1)S(1)}, bf16[528,256]{1,0:T(8,128)(2,1)}, u32[]{:S(2)}) copy-start(bf16[528,256]{1,0:T(8,128)(2,1)} %get-tuple-element.52.rest_4_.rest_8_) | copy-start | bytes 811012
  39.5 28.8 %copy-start.1 = (f32[64,32,128]{2,1,0:T(8,128)S(1)}, f32[64,32,128]{2,1,0:T(8,128)}, u32[]{:S(2)}) copy-start(f32[64,32,128]{2,1,0:T(8,128)} %param.11) | copy-start | bytes 3145732
  39.5 28.8 %copy-start.2 = (bf16[1024,128]{1,0:T(8,128)(2,1)S(1)}, bf16[1024,128]{1,0:T(8,128)(2,1)}, u32[]{:S(2)}) copy-start(bf16[1024,128]{1,0:T(8,128)(2,1)} %rest_4_.1) | copy-start | bytes 786436
  39.5 28.8 %copy-start.4 = (bf16[128,128]{1,0:T(8,128)(2,1)S(1)}, bf16[128,128]{1,0:T(8,128)(2,1)}, u32[]{:S(2)}) copy-start(bf16[128,128]{1,0:T(8,128)(2,1)} %rest_6_.1) | copy-start | bytes 98308
  39.5 28.8 %copy-start.8 = (s32[4]{0:T(128)S(1)}, s32[4]{0:T(128)}, u32[]{:S(2)}) copy-start(s32[4]{0:T(128)} %broadcast_multiply_fusion.right_firsts_ref) | copy-start | bytes 52
  43.8 11.2 %collective-permute-start.6 = (bf16[256,256]{1,0:T(8,128)(2,1)S(1)}, bf16[256,256]{1,0:T(8,128)(2,1)S(1)}, u32[]{:S(2)}, u32[]{:S(2)}) collective-permute-start(bf16[256,256]{1,0:T(8,128)(2,1)S(1)} %get-tuple-element.72), channel_id=1, source_target_pairs={{0,0},{1,1},{2,8},{3,9},{4,16},{5,17},{6,24},{7,25},{8,2},{9,3},{1... | collective-permute-start | bytes 393224 | tf_op jit(solution)/shard_map/ppermute | solution.py:670
  44.5 16.0 %collective-permute-start.7 = (bf16[256,256]{1,0:T(8,128)(2,1)S(1)}, bf16[256,256]{1,0:T(8,128)(2,1)S(1)}, u32[]{:S(2)}, u32[]{:S(2)}) collective-permute-start(bf16[256,256]{1,0:T(8,128)(2,1)S(1)} %get-tuple-element.72), channel_id=1, source_target_pairs={{0,2},{1,3},{2,10},{3,11},{4,18},{5,19},{6,26},{7,27},{8,4},{9,5},... | collective-permute-start | bytes 393224 | tf_op jit(solution)/shard_map/ppermute | solution.py:670
  49.2 12.8 %collective-permute-start.8 = (bf16[256,256]{1,0:T(8,128)(2,1)S(1)}, bf16[256,256]{1,0:T(8,128)(2,1)S(1)}, u32[]{:S(2)}, u32[]{:S(2)}) collective-permute-start(bf16[256,256]{1,0:T(8,128)(2,1)S(1)} %get-tuple-element.72), channel_id=1, source_target_pairs={{0,4},{1,5},{2,12},{3,13},{4,20},{5,21},{6,28},{7,29},{8,6},{9,7},... | collective-permute-start | bytes 393224 | tf_op jit(solution)/shard_map/ppermute | solution.py:670
  52.7 10.0 %collective-permute-start.9 = (bf16[256,256]{1,0:T(8,128)(2,1)S(1)}, bf16[256,256]{1,0:T(8,128)(2,1)S(1)}, u32[]{:S(2)}, u32[]{:S(2)}) collective-permute-start(bf16[256,256]{1,0:T(8,128)(2,1)S(1)} %get-tuple-element.72), channel_id=1, source_target_pairs={{0,6},{1,7},{2,14},{3,15},{4,22},{5,23},{6,30},{7,31},{8,0},{9,1},... | collective-permute-start | bytes 393224 | tf_op jit(solution)/shard_map/ppermute | solution.py:670
  55.0 9.0 %collective-permute-start.10 = (bf16[8,32,256]{2,1,0:T(8,128)(2,1)S(1)}, bf16[8,32,256]{2,1,0:T(8,128)(2,1)S(1)}, u32[]{:S(2)}, u32[]{:S(2)}) collective-permute-start(bf16[8,32,256]{2,1,0:T(8,128)(2,1)S(1)} %get-tuple-element.76.rest_0_), channel_id=1, source_target_pairs={{0,8},{8,0},{16,24},{24,16},{1,9},{9,1},{17,25},{25,17},{2,10},{10... | collective-permute-start | bytes 393224 | tf_op jit(solution)/shard_map/ppermute | solution.py:709
  56.0 8.0 %collective-permute-start.11 = (bf16[8,32,256]{2,1,0:T(8,128)(2,1)S(1)}, bf16[8,32,256]{2,1,0:T(8,128)(2,1)S(1)}, u32[]{:S(2)}, u32[]{:S(2)}) collective-permute-start(bf16[8,32,256]{2,1,0:T(8,128)(2,1)S(1)} %get-tuple-element.76.rest_0_), channel_id=1, source_target_pairs={{0,16},{8,24},{16,0},{24,8},{1,17},{9,25},{17,1},{25,9},{2,18},{10... | collective-permute-start | bytes 393224 | tf_op jit(solution)/shard_map/ppermute | solution.py:709
  60.5 5.9 %collective-permute-start.12 = (bf16[8,32,256]{2,1,0:T(8,128)(2,1)S(1)}, bf16[8,32,256]{2,1,0:T(8,128)(2,1)S(1)}, u32[]{:S(2)}, u32[]{:S(2)}) collective-permute-start(bf16[8,32,256]{2,1,0:T(8,128)(2,1)S(1)} %get-tuple-element.76.rest_0_), channel_id=1, source_target_pairs={{0,24},{8,16},{16,8},{24,0},{1,25},{9,17},{17,9},{25,1},{2,26},{10... | collective-permute-start | bytes 393224 | tf_op jit(solution)/shard_map/ppermute | solution.py:709
  66.4 1.9 %collective-permute-start.13 = (bf16[4,256,256]{2,1,0:T(8,128)(2,1)S(1)}, bf16[4,256,256]{2,1,0:T(8,128)(2,1)S(1)}, u32[]{:S(2)}, u32[]{:S(2)}) collective-permute-start(bf16[4,256,256]{2,1,0:T(8,128)(2,1)S(1)} %pad_maximum_fusion.1.own_ref), channel_id=1, source_target_pairs={{0,1},{1,0},{2,3},{3,2},{4,5},{5,4},{6,7},{7,6},{8,9},{9,8},{10,11... | collective-permute-start | bytes 1572872 | tf_op jit(solution)/shard_map/ppermute | solution.py:657
  77.0 32.7 %all-to-all-start = ((bf16[32,4,32,128]{3,2,1,0:T(8,128)(2,1)}), bf16[32,4,32,128]{3,2,1,0:T(8,128)(2,1)S(1)}, u32[]{:S(2)}, u32[]{:S(2)}) async-start(bf16[32,4,32,128]{3,2,1,0:T(8,128)(2,1)} %bitcast.37), calls=%async_computation | async-start | bytes 2097152 | tf_op jit(solution)/shard_map/all_to_all | solution.py:779
  82.1 32.5 %copy-start.13 = (bf16[8,64,256]{2,1,0:T(8,128)(2,1)S(1)}, bf16[8,64,256]{2,1,0:T(8,128)(2,1)}, u32[]{:S(2)}) copy-start(bf16[8,64,256]{2,1,0:T(8,128)(2,1)} %get-tuple-element.87) | copy-start | bytes 786436
  82.1 17.3 %collective-permute-start.14 = (bf16[8,64,256]{2,1,0:T(8,128)(2,1)}, bf16[8,64,256]{2,1,0:T(8,128)(2,1)S(1)}, u32[]{:S(2)}, u32[]{:S(2)}) collective-permute-start(bf16[8,64,256]{2,1,0:T(8,128)(2,1)} %get-tuple-element.83), channel_id=1, source_target_pairs={{0,8},{8,0},{16,24},{24,16},{1,9},{9,1},{17,25},{25,17},{2,10},{10... | collective-permute-start | bytes 786440 | tf_op jit(solution)/shard_map/ppermute | solution.py:709
  83.9 15.4 %collective-permute-start.15 = (bf16[8,64,256]{2,1,0:T(8,128)(2,1)}, bf16[8,64,256]{2,1,0:T(8,128)(2,1)S(1)}, u32[]{:S(2)}, u32[]{:S(2)}) collective-permute-start(bf16[8,64,256]{2,1,0:T(8,128)(2,1)} %get-tuple-element.84), channel_id=1, source_target_pairs={{0,16},{8,24},{16,0},{24,8},{1,17},{9,25},{17,1},{25,9},{2,18},{10... | collective-permute-start | bytes 786440 | tf_op jit(solution)/shard_map/ppermute | solution.py:709
  85.4 22.4 %collective-permute-start.16 = (bf16[8,64,256]{2,1,0:T(8,128)(2,1)}, bf16[8,64,256]{2,1,0:T(8,128)(2,1)}, u32[]{:S(2)}, u32[]{:S(2)}) collective-permute-start(bf16[8,64,256]{2,1,0:T(8,128)(2,1)} %get-tuple-element.85), channel_id=1, source_target_pairs={{0,24},{8,16},{16,8},{24,0},{1,25},{9,17},{17,9},{25,1},{2,26},{10... | collective-permute-start | bytes 786440 | tf_op jit(solution)/shard_map/ppermute | solution.py:709
  99.3 0.7 copy-start.14
  100.1 0.7 copy-start.15
  111.3 19.4 %all-to-all-start.1 = ((bf16[32,4,16,128]{3,2,1,0:T(8,128)(2,1)}), bf16[32,4,16,128]{3,2,1,0:T(8,128)(2,1)S(1)}, u32[]{:S(2)}, u32[]{:S(2)}) async-start(bf16[32,4,16,128]{3,2,1,0:T(8,128)(2,1)} %triangle_product.1), calls=%async_computation.1 | async-start | bytes 1048576 | tf_op jit(solution)/shard_map/all_to_all | solution.py:782
  114.5 5.1 %copy-start.11 = (bf16[256,256]{1,0:T(8,128)(2,1)S(1)}, bf16[256,256]{1,0:T(8,128)(2,1)}, u32[]{:S(2)}) copy-start(bf16[256,256]{1,0:T(8,128)(2,1)} %param.14) | copy-start | bytes 393220
  119.6 11.1 %copy-start.5 = (bf16[128,128]{1,0:T(8,128)(2,1)S(1)}, bf16[128,128]{1,0:T(8,128)(2,1)}, u32[]{:S(2)}) copy-start(bf16[128,128]{1,0:T(8,128)(2,1)} %final_ref.1) | copy-start | bytes 98308

commit v12 on v11

--- a/solution.py
+++ b/solution.py
@@ -77,23 +77,24 @@
 
 
 def high_kernel(sources_ref, block_hbm, *rest):
-    *pieces_hbm, first_ref, second_ref, high_ref, fetched, sent = rest
+    *pieces_hbm, block_ref, first_ref, second_ref, high_ref, fetched, sent = rest
     seqs, residues, lanes = first_ref.shape
     own = residues // len(pieces_hbm)
     step = 16
     fetches, sends = [], []
     for s in range(0, seqs, step):
         chosen = pl.ds(s, step)
-        for half, ref in enumerate((first_ref, second_ref)):
-            source = block_hbm.at[chosen, :, pl.ds(half * lanes, lanes)]
-            fetches.append(
-                pltpu.make_async_copy(source, ref.at[chosen], fetched.at[len(fetches)])
+        fetches.append(
+            pltpu.make_async_copy(
+                block_hbm.at[chosen], block_ref.at[chosen], fetched.at[len(fetches)]
             )
-            fetches[-1].start()
+        )
+        fetches[-1].start()
     for part in range(seqs // step):
         chosen = pl.ds(part * step, step)
-        fetches[2 * part].wait()
-        fetches[2 * part + 1].wait()
+        fetches[part].wait()
+        first_ref[chosen] = block_ref[chosen, :, :lanes]
+        second_ref[chosen] = block_ref[chosen, :, lanes:]
         first_rows = first_ref.at[chosen].reshape(step * residues, lanes)
         second_rows = second_ref.at[chosen].reshape(step * residues, lanes)
         for n in range(residues):
@@ -120,10 +121,11 @@
         out_specs=[hbm] * count,
         out_shape=[pltpu.HBM((residues // count, seqs, depth), BF16)] * count,
         scratch_shapes=[
+            pltpu.VMEM((seqs, residues, depth), F32),
             pltpu.VMEM((seqs, residues, half), F32),
             pltpu.VMEM((seqs, residues, half), F32),
             pltpu.VMEM((seqs // 16, residues, 16, depth), BF16),
-            pltpu.SemaphoreType.DMA((seqs // 8,)),
+            pltpu.SemaphoreType.DMA((seqs // 16,)),
             pltpu.SemaphoreType.DMA((seqs // 16 * count,)),
         ],
         compiler_params=params(10),
@@ -187,9 +189,8 @@
 
 
 def attention_kernel(key_ref, others_ref, *rest):
-    *refs, scores_ref, weights_ref = rest
-    blocks = len(refs) // 2
-    normed_refs, turned_ref, gated_refs = refs[:blocks], refs[blocks], refs[blocks + 1 :]
+    *normed_refs, turned_ref, scores_ref, weights_ref = rest
+    blocks = len(normed_refs)
     residues, seqs, _ = normed_refs[0].shape
     total = blocks * seqs
     inner = ATTENTION_UNITS * UNIT_WIDTH
@@ -230,11 +231,6 @@
         rows = slice(h * UNIT_WIDTH, (h + 1) * UNIT_WIDTH)
         attended = matmul(value_rows[rows], weights_ref[unit % ring]) * gates[rows]
         turned_ref[n, rows, :] = attended.astype(BF16)
-
-    def turn_back(n):
-        back = turned_ref[n].T
-        for block, gated_ref in enumerate(gated_refs):
-            gated_ref[n] = back[block * seqs : (block + 1) * seqs]
 
     project(0)
     for step in range(len(units) + 2):
@@ -247,9 +243,6 @@
             weigh(step - 1)
         if step >= 2:
             attend(step - 2)
-            n, h = units[step - 2]
-            if h == ATTENTION_UNITS - 1:
-                turn_back(n)
 
 
 def attention(normed, key_matrix, other_matrices):
@@ -266,10 +259,8 @@
             pl.BlockSpec((3 * inner, depth), lambda n: (0, 0)),
         ]
         + [pl.BlockSpec((step, seqs, depth), lambda n: (n, 0, 0))] * blocks,
-        out_specs=[pl.BlockSpec((step, inner, total), lambda n: (n, 0, 0))]
-        + [pl.BlockSpec((step, seqs, inner), lambda n: (n, 0, 0))] * blocks,
-        out_shape=[jax.ShapeDtypeStruct((residues, inner, total), BF16)]
-        + [pltpu.HBM((residues, seqs, inner), BF16)] * blocks,
+        out_specs=pl.BlockSpec((step, inner, total), lambda n: (n, 0, 0)),
+        out_shape=jax.ShapeDtypeStruct((residues, inner, total), BF16),
         scratch_shapes=[
             pltpu.VMEM((4, total, total), F32),
             pltpu.VMEM((4, total, total), BF16),
@@ -278,6 +269,29 @@
         cost_estimate=cost(10),
         name="attention",
     )(key_matrix, other_matrices, *normed)
+
+
+def turn_kernel(turned_ref, *gated_refs):
+    seqs = gated_refs[0].shape[1]
+    for n in range(turned_ref.shape[0]):
+        back = turned_ref[n].T
+        for block, gated_ref in enumerate(gated_refs):
+            gated_ref[n] = back[block * seqs : (block + 1) * seqs]
+
+
+def turn_back(turned, blocks):
+    residues, inner, total = turned.shape
+    seqs = total // blocks
+    return pl.pallas_call(
+        turn_kernel,
+        grid=(residues // 2,),
+        in_specs=[pl.BlockSpec((2, inner, total), lambda n: (n, 0, 0))],
+        out_specs=[pl.BlockSpec((2, seqs, inner), lambda n: (n, 0, 0))] * blocks,
+        out_shape=[pltpu.HBM((residues, seqs, inner), BF16)] * blocks,
+        compiler_params=params(12, "arbitrary"),
+        cost_estimate=cost(2),
+        name="turn_back",
+    )(turned)
 
 
 def alignment_kernel(sources_ref, turned_ref, final_ref, entry_ref, *rest):
@@ -657,7 +671,7 @@
     return lax.ppermute(block, "col", [(c, c ^ 1) for c in range(count)])
 
 
-def gather_turned(block):
+def gather_turned(block, later):
     rows, columns = lax.axis_size("row"), lax.axis_size("col")
     arrived = []
     for shift in range(rows):
@@ -667,8 +681,9 @@
                 for side in range(2):
                     source = r * columns + 2 * q + side
                     moves.append((source, q * columns + 2 * ((r + shift) % rows) + side))
-        arrived.append(lax.ppermute(block, ("row", "col"), moves))
-    return arrived
+        source = block if shift < 2 else later
+        arrived.append(lax.ppermute(source, ("row", "col"), moves))
+    return jnp.stack(arrived)
 
 
 def both_cores(own):
@@ -746,18 +761,18 @@
         sources * own_residues,
         left_groups(row_count, own_residues),
     )
-    high, _, early = lax.optimization_barrier((high, low, early))
+    high, low, early = lax.optimization_barrier((high, low, early))
     key_matrix, others, final_turned, tensor_turned, entries, firsts, slots = early
     low = exchange_rows(low)
-    turned, *gated = attention(high, key_matrix, others)
+    turned = attention(high, key_matrix, others)
+    gated = turn_back(turned, row_count)
     left_piece, right_piece = alignment(
         sources, high, low, turned, final_turned, tensor_turned
     )
 
-    lefts = gather_turned(left_piece)
-    right_piece, lefts[0] = lax.optimization_barrier((right_piece, lefts[0]))
     rights = exchange_rows([right_piece] * row_count)
-    own = jnp.stack(lefts)
+    later, rights[1] = lax.optimization_barrier((left_piece, rights[1]))
+    own = gather_turned(left_piece, later)
     own, rights = lax.optimization_barrier((own, rights))
     mid, gate, sides = pair_update(
         slots,

time: 134 us -> 127 us (0.948)
  local copies, waits for them, and re-layouts: 12.6 us -> 9.12 us
  starting transfers between devices: 38 us -> 34.7 us
  waiting for transfers between devices: 36.5 us -> 38.8 us
  other arithmetic: 5.24 us -> 3.36 us
    ppermute x12, starting transfers between devices: 18.7 us -> 14.3 us  [exchange_rows(): arrived.append(lax.ppermute(pieces[shift], 'row', moves))]
    unnamed x36 -> x32, local copies, waits for them, and re-layouts: 6.88 us -> 4.35 us
    ppermute x4, waiting for transfers between devices: 0.65 us -> 2.87 us  [gather_turned(): arrived.append(lax.ppermute(source, ('row', 'col'), moves))]
    pallas_call x1, Pallas kernels: 10.4 us -> 8.4 us  [attention(): pl.pallas_call(attention_kernel, grid=(residues // step,), in_specs=[pl.B...]
    ppermute x12, waiting for transfers between devices: 24.4 us -> 26.2 us  [exchange_rows(): arrived.append(lax.ppermute(pieces[shift], 'row', moves))]
    pallas_call x0 -> x1, Pallas kernels: none -> 1.73 us  [turn_back(): pl.pallas_call(turn_kernel, grid=(residues // 2,), in_specs=[pl.BlockSpec...]
    ppermute x1, waiting for transfers between devices: 1.91 us -> 0.18 us  [swap_cores(): return lax.ppermute(block, 'col', [(c, c ^ 1) for c in range(count)])]
  transfers between devices with their start and end apart: 19 -> 19, of which waited for: 8 -> 10; matrix products, arithmetic and copies ran while one was open for 14% -> 11% of each run, Pallas kernels for 11% -> 12%
where the time goes in v12:
time: 127 us
  waiting for transfers between devices  38.8 us (31%)
  Pallas kernels  36.2 us (29%)
  starting transfers between devices  34.7 us (27%)
  local copies, waits for them, and re-layouts  9.12 us (7%)
  matrix products  3.41 us (3%)
  other arithmetic  3.36 us (3%)
    ppermute x12, waiting for transfers between devices, exchange_rows(): arrived.append(lax.ppermute(pieces[shift], 'row', moves))  26.2 us
    ppermute x12, starting transfers between devices, exchange_rows(): arrived.append(lax.ppermute(pieces[shift], 'row', moves))  14.3 us
    ppermute x4, starting transfers between devices, gather_turned(): arrived.append(lax.ppermute(source, ('row', 'col'), moves))  12 us
    pallas_call x1, Pallas kernels, pair_update(): pl.pallas_call(pair_kernel, in_specs=[smem] * 2 + [vmem] * (5 + len(right...  8.67 us
    pallas_call x1, Pallas kernels, attention(): pl.pallas_call(attention_kernel, grid=(residues // step,), in_specs=[pl.B...  8.4 us
    all_to_all x1, waiting for transfers between devices, body(): product = lax.all_to_all(product, everywhere, split_axis=0, concat_axis=0)  7.66 us
    all_to_all x1, starting transfers between devices, body(): sides = lax.all_to_all(sides, everywhere, split_axis=0, concat_axis=0)  5.29 us
    pallas_call x1, Pallas kernels, standardise_high(): pl.pallas_call(high_kernel, in_specs=[pl.BlockSpec(memory_space=pltpu.SME...  4.65 us
  transfers between devices with their start and end apart: 19, of which 10 were waited for; matrix products, arithmetic and copies ran while one was open for 11% of the time, Pallas kernels for 12%

profile of v12, /device:TPU:0, one launch (start us, length us, event | category | flops | bytes accessed | tf_op | source)
XLA Modules:
  0.0 126.7 jit_solution(14091164137508185137)
XLA Ops:
  0.6 0.0 copy-start.9
  0.7 0.0 copy-start.13
  0.7 4.7 %standardise_high.1 = (bf16[8,64,256]{2,1,0:T(8,128)(2,1)}, bf16[8,64,256]{2,1,0:T(8,128)(2,1)}, bf16[8,64,256]{2,1,0:T(8,128)(2,1)}, bf16[8,64,256]{2,1,0:T(8,128)(2,1)}) custom-call(s32[4]{0:T(128)S(1)} %iota_xor_fusion.sources_ref, f32[64,32,256]{2,1,0:T(8,128)} %second_ref.1), custom_call_target="tpu_custom_call" | custom-call | flops 3000000000 | bytes 3000000 | tf_op jit(solution)/shard_map/standardise_high/pallas_call | solution.py:118
  5.3 0.0 copy-start
  5.3 3.0 %collective-permute-start = (bf16[8,64,256]{2,1,0:T(8,128)(2,1)}, bf16[8,64,256]{2,1,0:T(8,128)(2,1)S(1)}, u32[]{:S(2)}, u32[]{:S(2)}) collective-permute-start(bf16[8,64,256]{2,1,0:T(8,128)(2,1)} %get-tuple-element.52), channel_id=1, source_target_pairs={{0,8},{8,0},{16,24},{24,16},{1,9},{9,1},{17,25},{25,17},{2,10},{10... | collective-permute-start | bytes 786440 | tf_op jit(solution)/shard_map/ppermute | solution.py:724
  8.3 1.5 %collective-permute-start.1 = (bf16[8,64,256]{2,1,0:T(8,128)(2,1)}, bf16[8,64,256]{2,1,0:T(8,128)(2,1)S(1)}, u32[]{:S(2)}, u32[]{:S(2)}) collective-permute-start(bf16[8,64,256]{2,1,0:T(8,128)(2,1)} %get-tuple-element.53), channel_id=1, source_target_pairs={{0,16},{8,24},{16,0},{24,8},{1,17},{9,25},{17,1},{25,9},{2,18},{10... | collective-permute-start | bytes 786440 | tf_op jit(solution)/shard_map/ppermute | solution.py:724
  9.9 0.0 collective-permute-start.2
  9.9 0.7 slice.7
  10.6 1.1 copy.17
  11.7 0.8 copy.12
  12.5 0.9 reshape.47
  13.4 0.1 copy.15
  13.6 1.0 copy.14
  14.6 0.1 pad_add_fusion.left_slots_ref
  14.7 0.9 pad_maximum_fusion.2.others_ref
  15.7 4.5 %standardise_low.1 = (bf16[528,256]{1,0:T(8,128)(2,1)}, bf16[528,256]{1,0:T(8,128)(2,1)}, bf16[528,256]{1,0:T(8,128)(2,1)}, bf16[528,256]{1,0:T(8,128)(2,1)}) custom-call(s32[4]{0:T(128)S(1)} %iota_xor_fusion.sources_ref, f32[64,32,256]{2,1,0:T(8,128)S(1)} %copy-done, f32[64,32,256]{2,1,0:T(8,128)S(1)} %copy-done), custom_call_target="tpu_custom_call" | custom-call | flops 4000000000 | bytes 4000000 | tf_op jit(solution)/shard_map/standardise_low/pallas_call | solution.py:171
  20.2 1.8 %collective-permute-done.1.rest_2_ = bf16[8,64,256]{2,1,0:T(8,128)(2,1)S(1)} collective-permute-done((bf16[8,64,256]{2,1,0:T(8,128)(2,1)}, bf16[8,64,256]{2,1,0:T(8,128)(2,1)S(1)}, u32[]{:S(2)}, u32[]{:S(2)}) %collective-permute-start.1) | collective-permute-done | bytes 262176 | tf_op jit(solution)/shard_map/ppermute | solution.py:724
  22.0 1.2 collective-permute-start.3
  23.2 0.9 collective-permute-start.4
  24.1 1.4 %collective-permute-start.5 = (bf16[528,256]{1,0:T(8,128)(2,1)}, bf16[528,256]{1,0:T(8,128)(2,1)S(1)}, u32[]{:S(2)}, u32[]{:S(2)}) collective-permute-start(bf16[528,256]{1,0:T(8,128)(2,1)} %get-tuple-element.76), channel_id=1, source_target_pairs={{0,24},{8,16},{16,8},{24,0},{1,25},{9,17},{17,9},{25,1},{2,26},{10... | collective-permute-start | bytes 811016 | tf_op jit(solution)/shard_map/ppermute | solution.py:724
  25.5 8.4 %attention.1.turned_ref = bf16[8,256,256]{2,1,0:T(8,128)(2,1)S(1)} custom-call(bf16[256,256]{1,0:T(8,128)(2,1)S(1)} %slice.6.key_ref, bf16[768,256]{1,0:T(8,128)(2,1)S(1)} %pad_maximum_fusion.2.others_ref, bf16[8,64,256]{2,1,0:T(8,128)(2,1)S(1)} %copy-done.6, bf16[8,64,256]{2,1,0:T(8,128)(2,1)S(1)} %collective-permute-done.rest_1_, ...), custom_call_target="tpu_custom_call" | custom-call | flops 10000000000 | bytes 10000000 | tf_op jit(solution)/shard_map/attention/pallas_call | solution.py:254
  33.9 2.3 %collective-permute-done.4.rest_6_.rest_10_ = bf16[528,256]{1,0:T(8,128)(2,1)S(1)} collective-permute-done((bf16[528,256]{1,0:T(8,128)(2,1)}, bf16[528,256]{1,0:T(8,128)(2,1)S(1)}, u32[]{:S(2)}, u32[]{:S(2)}) %collective-permute-start.4) | collective-permute-done | bytes 270368 | tf_op jit(solution)/shard_map/ppermute | solution.py:724
  36.3 0.0 collective-permute-done.5.rest_7_.rest_11_
  36.3 3.8 %alignment.1 = (bf16[256,256]{1,0:T(8,128)(2,1)S(1)}, bf16[8,32,256]{2,1,0:T(8,128)(2,1)S(1)}) custom-call(s32[4]{0:T(128)S(1)} %iota_xor_fusion.sources_ref, bf16[8,256,256]{2,1,0:T(8,128)(2,1)S(1)} %attention.1.turned_ref, bf16[256,256]{1,0:T(8,128)(2,1)S(1)} %bitcast.32, bf16[64,256]{1,0:T(8,128)(2,1)S(1)} %bitcast.34, bf16[8,64,256]{2,1,0:T(8,128)(2,1)S(1)} %copy-done.6, ...), custom_call_target="tpu_custom_call" | custom-call | flops 4000000000 | bytes 4000000 | tf_op jit(solution)/shard_map/alignment/pallas_call | solution.py:356
  40.1 0.6 collective-permute-start.8
  40.7 0.7 collective-permute-start.6
  41.4 4.2 %collective-permute-start.7 = (bf16[256,256]{1,0:T(8,128)(2,1)S(1)}, bf16[256,256]{1,0:T(8,128)(2,1)S(1)}, u32[]{:S(2)}, u32[]{:S(2)}) collective-permute-start(bf16[256,256]{1,0:T(8,128)(2,1)S(1)} %get-tuple-element.79), channel_id=1, source_target_pairs={{0,2},{1,3},{2,10},{3,11},{4,18},{5,19},{6,26},{7,27},{8,4},{9,5},... | collective-permute-start | bytes 393224 | tf_op jit(solution)/shard_map/ppermute | solution.py:685
  45.6 0.0 collective-permute-done.8.rest_1_
  45.6 4.7 %collective-permute-start.9 = (bf16[256,256]{1,0:T(8,128)(2,1)S(1)}, bf16[256,256]{1,0:T(8,128)(2,1)S(1)}, u32[]{:S(2)}, u32[]{:S(2)}) collective-permute-start(bf16[256,256]{1,0:T(8,128)(2,1)S(1)} %get-tuple-element.79), channel_id=1, source_target_pairs={{0,4},{1,5},{2,12},{3,13},{4,20},{5,21},{6,28},{7,29},{8,6},{9,7},... | collective-permute-start | bytes 393224 | tf_op jit(solution)/shard_map/ppermute | solution.py:685
  50.3 2.5 %collective-permute-start.10 = (bf16[256,256]{1,0:T(8,128)(2,1)S(1)}, bf16[256,256]{1,0:T(8,128)(2,1)S(1)}, u32[]{:S(2)}, u32[]{:S(2)}) collective-permute-start(bf16[256,256]{1,0:T(8,128)(2,1)S(1)} %get-tuple-element.79), channel_id=1, source_target_pairs={{0,6},{1,7},{2,14},{3,15},{4,22},{5,23},{6,30},{7,31},{8,0},{9,1},... | collective-permute-start | bytes 393224 | tf_op jit(solution)/shard_map/ppermute | solution.py:685
  52.8 0.0 collective-permute-start.11
  52.8 2.0 %collective-permute-start.12 = (bf16[8,32,256]{2,1,0:T(8,128)(2,1)S(1)}, bf16[8,32,256]{2,1,0:T(8,128)(2,1)S(1)}, u32[]{:S(2)}, u32[]{:S(2)}) collective-permute-start(bf16[8,32,256]{2,1,0:T(8,128)(2,1)S(1)} %get-tuple-element.82.rest_0_), channel_id=1, source_target_pairs={{0,24},{8,16},{16,8},{24,0},{1,25},{9,17},{17,9},{25,1},{2,26},{10... | collective-permute-start | bytes 393224 | tf_op jit(solution)/shard_map/ppermute | solution.py:724
  54.8 0.0 collective-permute-done.7
  54.8 1.0 collective-permute-done.9
  55.8 1.8 %collective-permute-done.10 = bf16[256,256]{1,0:T(8,128)(2,1)S(1)} collective-permute-done((bf16[256,256]{1,0:T(8,128)(2,1)S(1)}, bf16[256,256]{1,0:T(8,128)(2,1)S(1)}, u32[]{:S(2)}, u32[]{:S(2)}) %collective-permute-start.10) | collective-permute-done | bytes 131104 | tf_op jit(solution)/shard_map/ppermute | solution.py:685
  57.6 0.1 pad_maximum_fusion.1.own_ref
  57.7 0.0 copy-start.1
  57.7 0.0 copy-start.2
  57.7 0.0 copy-start.4
  57.7 1.4 %collective-permute-done.11.rest_2_ = bf16[8,32,256]{2,1,0:T(8,128)(2,1)S(1)} collective-permute-done((bf16[8,32,256]{2,1,0:T(8,128)(2,1)S(1)}, bf16[8,32,256]{2,1,0:T(8,128)(2,1)S(1)}, u32[]{:S(2)}, u32[]{:S(2)}) %collective-permute-start.11) | collective-permute-done | bytes 131104 | tf_op jit(solution)/shard_map/ppermute | solution.py:724
  59.1 0.0 collective-permute-start.13
  59.1 1.7 %turn_back.1 = (bf16[8,64,256]{2,1,0:T(8,128)(2,1)}, bf16[8,64,256]{2,1,0:T(8,128)(2,1)}, bf16[8,64,256]{2,1,0:T(8,128)(2,1)}, bf16[8,64,256]{2,1,0:T(8,128)(2,1)}) custom-call(bf16[8,256,256]{2,1,0:T(8,128)(2,1)S(1)} %attention.1.turned_ref), custom_call_target="tpu_custom_call" | custom-call | flops 2000000000 | bytes 2000000 | tf_op jit(solution)/shard_map/turn_back/pallas_call | solution.py:285
  60.9 0.2 collective-permute-done.13.other_ref
  61.1 8.7 %pair_update.1 = (f32[32,64,128]{2,1,0:T(8,128)}, f32[32,64,128]{2,1,0:T(8,128)}, bf16[128,32,128]{2,1,0:T(8,128)(2,1)}) custom-call(s32[8]{0:T(128)S(1)} %pad_add_fusion.left_slots_ref, s32[4]{0:T(128)S(1)} %broadcast_multiply_fusion.right_firsts_ref, bf16[4,256,256]{2,1,0:T(8,128)(2,1)S(1)} %pad_maximum_fusion.1.own_ref, ...), custom_call_target="tpu_custom_call" | custom-call | flops 12000000000 | bytes 12000000 | tf_op jit(solution)/shard_map/pair_update/pallas_call | solution.py:523
  69.7 5.3 %all-to-all-start = ((bf16[32,4,32,128]{3,2,1,0:T(8,128)(2,1)}), bf16[32,4,32,128]{3,2,1,0:T(8,128)(2,1)S(1)}, u32[]{:S(2)}, u32[]{:S(2)}) async-start(bf16[32,4,32,128]{3,2,1,0:T(8,128)(2,1)} %bitcast.37), calls=%async_computation | async-start | bytes 2097152 | tf_op jit(solution)/shard_map/all_to_all | solution.py:794
  75.0 0.0 copy-start.10
  75.0 1.8 %collective-permute-start.14 = (bf16[8,64,256]{2,1,0:T(8,128)(2,1)}, bf16[8,64,256]{2,1,0:T(8,128)(2,1)S(1)}, u32[]{:S(2)}, u32[]{:S(2)}) collective-permute-start(bf16[8,64,256]{2,1,0:T(8,128)(2,1)} %get-tuple-element.89), channel_id=1, source_target_pairs={{0,8},{8,0},{16,24},{24,16},{1,9},{9,1},{17,25},{25,17},{2,10},{10... | collective-permute-start | bytes 786440 | tf_op jit(solution)/shard_map/ppermute | solution.py:724
  76.9 1.5 %collective-permute-start.15 = (bf16[8,64,256]{2,1,0:T(8,128)(2,1)}, bf16[8,64,256]{2,1,0:T(8,128)(2,1)S(1)}, u32[]{:S(2)}, u32[]{:S(2)}) collective-permute-start(bf16[8,64,256]{2,1,0:T(8,128)(2,1)} %get-tuple-element.90), channel_id=1, source_target_pairs={{0,16},{8,24},{16,0},{24,8},{1,17},{9,25},{17,1},{25,9},{2,18},{10... | collective-permute-start | bytes 786440 | tf_op jit(solution)/shard_map/ppermute | solution.py:724
  78.3 0.3 collective-permute-start.16
  78.6 13.7 %collective-permute-done.14 = bf16[8,64,256]{2,1,0:T(8,128)(2,1)S(1)} collective-permute-done((bf16[8,64,256]{2,1,0:T(8,128)(2,1)}, bf16[8,64,256]{2,1,0:T(8,128)(2,1)S(1)}, u32[]{:S(2)}, u32[]{:S(2)}) %collective-permute-start.14) | collective-permute-done | bytes 262176 | tf_op jit(solution)/shard_map/ppermute | solution.py:724
  92.3 0.7 copy-done.11
  93.0 0.7 copy-done.12
  93.7 7.0 %collective-permute-done.16 = bf16[8,64,256]{2,1,0:T(8,128)(2,1)} collective-permute-done((bf16[8,64,256]{2,1,0:T(8,128)(2,1)}, bf16[8,64,256]{2,1,0:T(8,128)(2,1)}, u32[]{:S(2)}, u32[]{:S(2)}) %collective-permute-start.16) | collective-permute-done | bytes 262176 | tf_op jit(solution)/shard_map/ppermute | solution.py:724
  100.7 1.9 %all-to-all-done.sides_ref = bf16[32,4,32,128]{3,2,1,0:T(8,128)(2,1)S(1)} async-done(((bf16[32,4,32,128]{3,2,1,0:T(8,128)(2,1)}), bf16[32,4,32,128]{3,2,1,0:T(8,128)(2,1)S(1)}, u32[]{:S(2)}, u32[]{:S(2)}) %all-to-all-start) | async-done | bytes 1048608 | tf_op jit(solution)/shard_map/all_to_all | solution.py:794
  102.6 1.7 %triangle_product.1 = bf16[32,4,16,128]{3,2,1,0:T(8,128)(2,1)} custom-call(bf16[32,4,32,128]{3,2,1,0:T(8,128)(2,1)S(1)} %all-to-all-done.sides_ref), custom_call_target="tpu_custom_call" | custom-call | flops 3000000000 | bytes 3000000 | tf_op jit(solution)/shard_map/triangle_product/pallas_call | solution.py:587
  104.3 3.0 %all-to-all-start.1 = ((bf16[32,4,16,128]{3,2,1,0:T(8,128)(2,1)}), bf16[32,4,16,128]{3,2,1,0:T(8,128)(2,1)S(1)}, u32[]{:S(2)}, u32[]{:S(2)}) async-start(bf16[32,4,16,128]{3,2,1,0:T(8,128)(2,1)} %triangle_product.1), calls=%async_computation.1 | async-start | bytes 1048576 | tf_op jit(solution)/shard_map/all_to_all | solution.py:797
  107.3 0.1 broadcast_in_dim.14
  107.4 0.1 broadcast_in_dim.15
  107.5 0.0 copy-start.8
  107.5 2.2 %pad_maximum_fusion = bf16[4,8,64,256]{3,2,1,0:T(8,128)(2,1)} fusion(bf16[1,8,64,256]{3,2,1,0:T(8,128)(2,1)} %bitcast.14, bf16[1,8,64,256]{3,2,1,0:T(8,128)(2,1)} %bitcast.42, bf16[1,8,64,256]{3,2,1,0:T(8,128)(2,1)} %bitcast.41, bf16[1,8,64,256]{3,2,1,0:T(8,128)(2,1)S(1)} %bitcast.40), kind=kLoop, calls=%fused_computation.2 | loop fusion | flops 1572864 | bytes 2097152 | tf_op jit(solution)/shard_map/stack | solution.py:799
  109.8 2.8 %gather_fusion = bf16[4,8,64,256]{3,2,1,0:T(8,128)(2,1)} fusion(bf16[4,8,64,256]{3,2,1,0:T(8,128)(2,1)} %pad_maximum_fusion, s32[1024]{0:T(1024)S(1)} %pad_clamp_fusion), kind=kCustom, calls=%fused_computation | custom fusion | bytes 2097168 | tf_op jit(solution)/shard_map/jit(_take)/gather | solution.py:799
  112.6 3.4 %convolution_add_fusion = f32[64,32,256]{2,1,0:T(8,128)} fusion(f32[64,32,256]{2,1,0:T(8,128)S(1)} %copy-done, bf16[32,64,256]{2,1,0:T(8,128)(2,1)} %bitcast.35, pred[32]{0:T(512)(128)(4,1)S(1)} %broadcast_in_dim.15, bf16[256,256]{1,0:T(8,128)(2,1)S(1)} %copy-done.8), kind=kOutput, calls=%fused_computation.1 | convolution fusion | flops 269484032 | bytes 5373984 | tf_op jit(solution)/shard_map/dot_general | solution.py:801
  116.0 7.7 %all-to-all-done.1 = bf16[32,4,16,128]{3,2,1,0:T(8,128)(2,1)S(1)} async-done(((bf16[32,4,16,128]{3,2,1,0:T(8,128)(2,1)}), bf16[32,4,16,128]{3,2,1,0:T(8,128)(2,1)S(1)}, u32[]{:S(2)}, u32[]{:S(2)}) %all-to-all-start.1) | async-done | bytes 524320 | tf_op jit(solution)/shard_map/all_to_all | solution.py:797
  123.7 2.8 %pair_result.1 = f32[64,32,128]{2,1,0:T(8,128)} custom-call(bf16[128,16,128]{2,1,0:T(8,128)(2,1)S(1)} %bitcast.30, bf16[128,128]{1,0:T(8,128)(2,1)S(1)} %copy-done.5, f32[32,64,128]{2,1,0:T(8,128)} %get-tuple-element.98.mid_hbm, f32[32,64,128]{2,1,0:T(8,128)} %get-tuple-element.99.gate_hbm), custom_call_target="tpu_custom_call" | custom-call | flops 3000000000 | bytes 3000000 | tf_op jit(solution)/shard_map/pair_result/pallas_call | solution.py:645
  (32 shorter events, 0.1 us)
Async XLA Ops:
  0.6 9.3 %copy-start.9 = (bf16[256,768]{1,0:T(8,128)(2,1)S(1)}, bf16[256,768]{1,0:T(8,128)(2,1)}, u32[]{:S(2)}) copy-start(bf16[256,768]{1,0:T(8,128)(2,1)} %param.13) | copy-start | bytes 1179652
  0.7 11.1 %copy-start.13 = (bf16[256,256]{1,0:T(8,128)(2,1)S(1)}, bf16[256,256]{1,0:T(8,128)(2,1)}, u32[]{:S(2)}) copy-start(bf16[256,256]{1,0:T(8,128)(2,1)} %param.12) | copy-start | bytes 393220
  5.3 10.3 %copy-start = (f32[64,32,256]{2,1,0:T(8,128)S(1)}, f32[64,32,256]{2,1,0:T(8,128)}, u32[]{:S(2)}) copy-start(f32[64,32,256]{2,1,0:T(8,128)} %second_ref.1) | copy-start | bytes 6291460
  5.3 14.8 %collective-permute-start = (bf16[8,64,256]{2,1,0:T(8,128)(2,1)}, bf16[8,64,256]{2,1,0:T(8,128)(2,1)S(1)}, u32[]{:S(2)}, u32[]{:S(2)}) collective-permute-start(bf16[8,64,256]{2,1,0:T(8,128)(2,1)} %get-tuple-element.52), channel_id=1, source_target_pairs={{0,8},{8,0},{16,24},{24,16},{1,9},{9,1},{17,25},{25,17},{2,10},{10... | collective-permute-start | bytes 786440 | tf_op jit(solution)/shard_map/ppermute | solution.py:724
  8.3 13.6 %collective-permute-start.1 = (bf16[8,64,256]{2,1,0:T(8,128)(2,1)}, bf16[8,64,256]{2,1,0:T(8,128)(2,1)S(1)}, u32[]{:S(2)}, u32[]{:S(2)}) collective-permute-start(bf16[8,64,256]{2,1,0:T(8,128)(2,1)} %get-tuple-element.53), channel_id=1, source_target_pairs={{0,16},{8,24},{16,0},{24,8},{1,17},{9,25},{17,1},{25,9},{2,18},{10... | collective-permute-start | bytes 786440 | tf_op jit(solution)/shard_map/ppermute | solution.py:724
  9.9 12.1 %collective-permute-start.2 = (bf16[8,64,256]{2,1,0:T(8,128)(2,1)}, bf16[8,64,256]{2,1,0:T(8,128)(2,1)S(1)}, u32[]{:S(2)}, u32[]{:S(2)}) collective-permute-start(bf16[8,64,256]{2,1,0:T(8,128)(2,1)} %get-tuple-element.54), channel_id=1, source_target_pairs={{0,24},{8,16},{16,8},{24,0},{1,25},{9,17},{17,9},{25,1},{2,26},{10... | collective-permute-start | bytes 786440 | tf_op jit(solution)/shard_map/ppermute | solution.py:724
  15.7 9.8 %copy-start.6 = (bf16[8,64,256]{2,1,0:T(8,128)(2,1)S(1)}, bf16[8,64,256]{2,1,0:T(8,128)(2,1)}, u32[]{:S(2)}) copy-start(bf16[8,64,256]{2,1,0:T(8,128)(2,1)} %get-tuple-element.61.rest_0_) | copy-start | bytes 786436
  21.9 14.3 %copy-start.3 = (bf16[256,64]{0,1:T(8,128)(2,1)S(1)}, bf16[256,64]{0,1:T(8,128)(2,1)}, u32[]{:S(2)}) copy-start(bf16[256,64]{0,1:T(8,128)(2,1)} %param.15) | copy-start | bytes 98308
  21.9 14.3 %copy-start.7 = (bf16[528,256]{1,0:T(8,128)(2,1)S(1)}, bf16[528,256]{1,0:T(8,128)(2,1)}, u32[]{:S(2)}) copy-start(bf16[528,256]{1,0:T(8,128)(2,1)} %get-tuple-element.73.rest_4_.rest_8_) | copy-start | bytes 811012
  22.0 12.0 %collective-permute-start.3 = (bf16[528,256]{1,0:T(8,128)(2,1)}, bf16[528,256]{1,0:T(8,128)(2,1)S(1)}, u32[]{:S(2)}, u32[]{:S(2)}) collective-permute-start(bf16[528,256]{1,0:T(8,128)(2,1)} %get-tuple-element.74), channel_id=1, source_target_pairs={{0,8},{8,0},{16,24},{24,16},{1,9},{9,1},{17,25},{25,17},{2,10},{10... | collective-permute-start | bytes 811016 | tf_op jit(solution)/shard_map/ppermute | solution.py:724
  23.2 13.1 %collective-permute-start.4 = (bf16[528,256]{1,0:T(8,128)(2,1)}, bf16[528,256]{1,0:T(8,128)(2,1)S(1)}, u32[]{:S(2)}, u32[]{:S(2)}) collective-permute-start(bf16[528,256]{1,0:T(8,128)(2,1)} %get-tuple-element.75), channel_id=1, source_target_pairs={{0,16},{8,24},{16,0},{24,8},{1,17},{9,25},{17,1},{25,9},{2,18},{10... | collective-permute-start | bytes 811016 | tf_op jit(solution)/shard_map/ppermute | solution.py:724
  24.1 12.2 %collective-permute-start.5 = (bf16[528,256]{1,0:T(8,128)(2,1)}, bf16[528,256]{1,0:T(8,128)(2,1)S(1)}, u32[]{:S(2)}, u32[]{:S(2)}) collective-permute-start(bf16[528,256]{1,0:T(8,128)(2,1)} %get-tuple-element.76), channel_id=1, source_target_pairs={{0,24},{8,16},{16,8},{24,0},{1,25},{9,17},{17,9},{25,1},{2,26},{10... | collective-permute-start | bytes 811016 | tf_op jit(solution)/shard_map/ppermute | solution.py:724
  40.1 5.5 %collective-permute-start.8 = (bf16[8,32,256]{2,1,0:T(8,128)(2,1)S(1)}, bf16[8,32,256]{2,1,0:T(8,128)(2,1)S(1)}, u32[]{:S(2)}, u32[]{:S(2)}) collective-permute-start(bf16[8,32,256]{2,1,0:T(8,128)(2,1)S(1)} %get-tuple-element.82.rest_0_), channel_id=1, source_target_pairs={{0,8},{8,0},{16,24},{24,16},{1,9},{9,1},{17,25},{25,17},{2,10},{10... | collective-permute-start | bytes 393224 | tf_op jit(solution)/shard_map/ppermute | solution.py:724
  40.7 12.1 %collective-permute-start.6 = (bf16[256,256]{1,0:T(8,128)(2,1)S(1)}, bf16[256,256]{1,0:T(8,128)(2,1)S(1)}, u32[]{:S(2)}, u32[]{:S(2)}) collective-permute-start(bf16[256,256]{1,0:T(8,128)(2,1)S(1)} %get-tuple-element.79), channel_id=1, source_target_pairs={{0,0},{1,1},{2,8},{3,9},{4,16},{5,17},{6,24},{7,25},{8,2},{9,3},{1... | collective-permute-start | bytes 393224 | tf_op jit(solution)/shard_map/ppermute | solution.py:685
  41.4 13.4 %collective-permute-start.7 = (bf16[256,256]{1,0:T(8,128)(2,1)S(1)}, bf16[256,256]{1,0:T(8,128)(2,1)S(1)}, u32[]{:S(2)}, u32[]{:S(2)}) collective-permute-start(bf16[256,256]{1,0:T(8,128)(2,1)S(1)} %get-tuple-element.79), channel_id=1, source_target_pairs={{0,2},{1,3},{2,10},{3,11},{4,18},{5,19},{6,26},{7,27},{8,4},{9,5},... | collective-permute-start | bytes 393224 | tf_op jit(solution)/shard_map/ppermute | solution.py:685
  45.6 10.2 %collective-permute-start.9 = (bf16[256,256]{1,0:T(8,128)(2,1)S(1)}, bf16[256,256]{1,0:T(8,128)(2,1)S(1)}, u32[]{:S(2)}, u32[]{:S(2)}) collective-permute-start(bf16[256,256]{1,0:T(8,128)(2,1)S(1)} %get-tuple-element.79), channel_id=1, source_target_pairs={{0,4},{1,5},{2,12},{3,13},{4,20},{5,21},{6,28},{7,29},{8,6},{9,7},... | collective-permute-start | bytes 393224 | tf_op jit(solution)/shard_map/ppermute | solution.py:685
  50.3 7.3 %collective-permute-start.10 = (bf16[256,256]{1,0:T(8,128)(2,1)S(1)}, bf16[256,256]{1,0:T(8,128)(2,1)S(1)}, u32[]{:S(2)}, u32[]{:S(2)}) collective-permute-start(bf16[256,256]{1,0:T(8,128)(2,1)S(1)} %get-tuple-element.79), channel_id=1, source_target_pairs={{0,6},{1,7},{2,14},{3,15},{4,22},{5,23},{6,30},{7,31},{8,0},{9,1},... | collective-permute-start | bytes 393224 | tf_op jit(solution)/shard_map/ppermute | solution.py:685
  52.8 6.4 %collective-permute-start.11 = (bf16[8,32,256]{2,1,0:T(8,128)(2,1)S(1)}, bf16[8,32,256]{2,1,0:T(8,128)(2,1)S(1)}, u32[]{:S(2)}, u32[]{:S(2)}) collective-permute-start(bf16[8,32,256]{2,1,0:T(8,128)(2,1)S(1)} %get-tuple-element.82.rest_0_), channel_id=1, source_target_pairs={{0,16},{8,24},{16,0},{24,8},{1,17},{9,25},{17,1},{25,9},{2,18},{10... | collective-permute-start | bytes 393224 | tf_op jit(solution)/shard_map/ppermute | solution.py:724
  52.8 6.4 %collective-permute-start.12 = (bf16[8,32,256]{2,1,0:T(8,128)(2,1)S(1)}, bf16[8,32,256]{2,1,0:T(8,128)(2,1)S(1)}, u32[]{:S(2)}, u32[]{:S(2)}) collective-permute-start(bf16[8,32,256]{2,1,0:T(8,128)(2,1)S(1)} %get-tuple-element.82.rest_0_), channel_id=1, source_target_pairs={{0,24},{8,16},{16,8},{24,0},{1,25},{9,17},{17,9},{25,1},{2,26},{10... | collective-permute-start | bytes 393224 | tf_op jit(solution)/shard_map/ppermute | solution.py:724
  57.7 3.3 %copy-start.1 = (f32[64,32,128]{2,1,0:T(8,128)S(1)}, f32[64,32,128]{2,1,0:T(8,128)}, u32[]{:S(2)}) copy-start(f32[64,32,128]{2,1,0:T(8,128)} %param.11) | copy-start | bytes 3145732
  57.7 3.3 %copy-start.2 = (bf16[1024,128]{1,0:T(8,128)(2,1)S(1)}, bf16[1024,128]{1,0:T(8,128)(2,1)}, u32[]{:S(2)}) copy-start(bf16[1024,128]{1,0:T(8,128)(2,1)} %rest_4_.1) | copy-start | bytes 786436
  57.7 3.3 %copy-start.4 = (bf16[128,128]{1,0:T(8,128)(2,1)S(1)}, bf16[128,128]{1,0:T(8,128)(2,1)}, u32[]{:S(2)}) copy-start(bf16[128,128]{1,0:T(8,128)(2,1)} %rest_6_.1) | copy-start | bytes 98308
  59.1 1.9 %collective-permute-start.13 = (bf16[4,256,256]{2,1,0:T(8,128)(2,1)S(1)}, bf16[4,256,256]{2,1,0:T(8,128)(2,1)S(1)}, u32[]{:S(2)}, u32[]{:S(2)}) collective-permute-start(bf16[4,256,256]{2,1,0:T(8,128)(2,1)S(1)} %pad_maximum_fusion.1.own_ref), channel_id=1, source_target_pairs={{0,1},{1,0},{2,3},{3,2},{4,5},{5,4},{6,7},{7,6},{8,9},{9,8},{10,11... | collective-permute-start | bytes 1572872 | tf_op jit(solution)/shard_map/ppermute | solution.py:671
  69.7 32.9 %all-to-all-start = ((bf16[32,4,32,128]{3,2,1,0:T(8,128)(2,1)}), bf16[32,4,32,128]{3,2,1,0:T(8,128)(2,1)S(1)}, u32[]{:S(2)}, u32[]{:S(2)}) async-start(bf16[32,4,32,128]{3,2,1,0:T(8,128)(2,1)} %bitcast.37), calls=%async_computation | async-start | bytes 2097152 | tf_op jit(solution)/shard_map/all_to_all | solution.py:794
  75.0 32.5 %copy-start.10 = (bf16[8,64,256]{2,1,0:T(8,128)(2,1)S(1)}, bf16[8,64,256]{2,1,0:T(8,128)(2,1)}, u32[]{:S(2)}) copy-start(bf16[8,64,256]{2,1,0:T(8,128)(2,1)} %get-tuple-element.93) | copy-start | bytes 786436
  75.0 17.3 %collective-permute-start.14 = (bf16[8,64,256]{2,1,0:T(8,128)(2,1)}, bf16[8,64,256]{2,1,0:T(8,128)(2,1)S(1)}, u32[]{:S(2)}, u32[]{:S(2)}) collective-permute-start(bf16[8,64,256]{2,1,0:T(8,128)(2,1)} %get-tuple-element.89), channel_id=1, source_target_pairs={{0,8},{8,0},{16,24},{24,16},{1,9},{9,1},{17,25},{25,17},{2,10},{10... | collective-permute-start | bytes 786440 | tf_op jit(solution)/shard_map/ppermute | solution.py:724
  76.9 15.4 %collective-permute-start.15 = (bf16[8,64,256]{2,1,0:T(8,128)(2,1)}, bf16[8,64,256]{2,1,0:T(8,128)(2,1)S(1)}, u32[]{:S(2)}, u32[]{:S(2)}) collective-permute-start(bf16[8,64,256]{2,1,0:T(8,128)(2,1)} %get-tuple-element.90), channel_id=1, source_target_pairs={{0,16},{8,24},{16,0},{24,8},{1,17},{9,25},{17,1},{25,9},{2,18},{10... | collective-permute-start | bytes 786440 | tf_op jit(solution)/shard_map/ppermute | solution.py:724
  78.3 22.4 %collective-permute-start.16 = (bf16[8,64,256]{2,1,0:T(8,128)(2,1)}, bf16[8,64,256]{2,1,0:T(8,128)(2,1)}, u32[]{:S(2)}, u32[]{:S(2)}) collective-permute-start(bf16[8,64,256]{2,1,0:T(8,128)(2,1)} %get-tuple-element.91), channel_id=1, source_target_pairs={{0,24},{8,16},{16,8},{24,0},{1,25},{9,17},{17,9},{25,1},{2,26},{10... | collective-permute-start | bytes 786440 | tf_op jit(solution)/shard_map/ppermute | solution.py:724
  92.3 0.7 copy-start.11
  93.0 0.7 copy-start.12
  104.3 19.4 %all-to-all-start.1 = ((bf16[32,4,16,128]{3,2,1,0:T(8,128)(2,1)}), bf16[32,4,16,128]{3,2,1,0:T(8,128)(2,1)S(1)}, u32[]{:S(2)}, u32[]{:S(2)}) async-start(bf16[32,4,16,128]{3,2,1,0:T(8,128)(2,1)} %triangle_product.1), calls=%async_computation.1 | async-start | bytes 1048576 | tf_op jit(solution)/shard_map/all_to_all | solution.py:797
  107.5 5.1 %copy-start.8 = (bf16[256,256]{1,0:T(8,128)(2,1)S(1)}, bf16[256,256]{1,0:T(8,128)(2,1)}, u32[]{:S(2)}) copy-start(bf16[256,256]{1,0:T(8,128)(2,1)} %param.14) | copy-start | bytes 393220
  112.6 11.1 %copy-start.5 = (bf16[128,128]{1,0:T(8,128)(2,1)S(1)}, bf16[128,128]{1,0:T(8,128)(2,1)}, u32[]{:S(2)}) copy-start(bf16[128,128]{1,0:T(8,128)(2,1)} %final_ref.1) | copy-start | bytes 98308

commit v13 on v12

--- a/solution.py
+++ b/solution.py
@@ -77,56 +77,49 @@
 
 
 def high_kernel(sources_ref, block_hbm, *rest):
-    *pieces_hbm, block_ref, first_ref, second_ref, high_ref, fetched, sent = rest
+    *pieces, first_ref, second_ref, fetched = rest
     seqs, residues, lanes = first_ref.shape
-    own = residues // len(pieces_hbm)
+    own = residues // len(pieces)
     step = 16
-    fetches, sends = [], []
+    fetches = []
     for s in range(0, seqs, step):
         chosen = pl.ds(s, step)
-        fetches.append(
-            pltpu.make_async_copy(
-                block_hbm.at[chosen], block_ref.at[chosen], fetched.at[len(fetches)]
+        for half, ref in enumerate((first_ref, second_ref)):
+            source = block_hbm.at[chosen, :, pl.ds(half * lanes, lanes)]
+            fetches.append(
+                pltpu.make_async_copy(source, ref.at[chosen], fetched.at[len(fetches)])
             )
-        )
-        fetches[-1].start()
+            fetches[-1].start()
+    firsts = [sources_ref[p] * own for p in range(len(pieces))]
     for part in range(seqs // step):
         chosen = pl.ds(part * step, step)
-        fetches[part].wait()
-        first_ref[chosen] = block_ref[chosen, :, :lanes]
-        second_ref[chosen] = block_ref[chosen, :, lanes:]
+        fetches[2 * part].wait()
+        fetches[2 * part + 1].wait()
         first_rows = first_ref.at[chosen].reshape(step * residues, lanes)
         second_rows = second_ref.at[chosen].reshape(step * residues, lanes)
-        for n in range(residues):
-            normed, _ = standardised_column(first_rows, second_rows, n, residues)
-            high_ref[part, n] = normed.astype(BF16)
-        for p, piece_hbm in enumerate(pieces_hbm):
-            source = high_ref.at[part, pl.ds(sources_ref[p] * own, own)]
-            sends.append(
-                pltpu.make_async_copy(source, piece_hbm.at[:, chosen], sent.at[len(sends)])
-            )
-            sends[-1].start()
-    for send in sends:
-        send.wait()
+        for piece_ref, first in zip(pieces, firsts):
+            for n in range(own):
+                normed, _ = standardised_column(first_rows, second_rows, first + n, residues)
+                piece_ref[n, part * step : (part + 1) * step, :] = normed.astype(BF16)
 
 
 def standardise_high(sources, block):
     seqs, residues, depth = block.shape
     half = depth // 2
     count = sources.shape[0]
-    hbm = pl.BlockSpec(memory_space=pltpu.HBM)
+    piece = jax.ShapeDtypeStruct((residues // count, seqs, depth), BF16)
     return pl.pallas_call(
         high_kernel,
-        in_specs=[pl.BlockSpec(memory_space=pltpu.SMEM), hbm],
-        out_specs=[hbm] * count,
-        out_shape=[pltpu.HBM((residues // count, seqs, depth), BF16)] * count,
+        in_specs=[
+            pl.BlockSpec(memory_space=pltpu.SMEM),
+            pl.BlockSpec(memory_space=pltpu.HBM),
+        ],
+        out_specs=[pl.BlockSpec(memory_space=pltpu.VMEM)] * count,
+        out_shape=[piece] * count,
         scratch_shapes=[
-            pltpu.VMEM((seqs, residues, depth), F32),
             pltpu.VMEM((seqs, residues, half), F32),
             pltpu.VMEM((seqs, residues, half), F32),
-            pltpu.VMEM((seqs // 16, residues, 16, depth), BF16),
-            pltpu.SemaphoreType.DMA((seqs // 16,)),
-            pltpu.SemaphoreType.DMA((seqs // 16 * count,)),
+            pltpu.SemaphoreType.DMA((seqs // 8,)),
         ],
         compiler_params=params(10),
         cost_estimate=cost(3),
@@ -134,32 +127,25 @@
     )(sources, pltpu.with_memory_space_constraint(block, pltpu.HBM))
 
 
-def low_kernel(sources_ref, first_ref, second_ref, *rest):
-    *pieces_hbm, low_ref, sent = rest
+def low_kernel(sources_ref, first_ref, second_ref, *pieces):
     seqs, residues, lanes = first_ref.shape
-    own = residues // len(pieces_hbm)
+    own = residues // len(pieces)
     first_rows = first_ref.reshape(seqs * residues, lanes)
     second_rows = second_ref.reshape(seqs * residues, lanes)
     lane = lax.broadcasted_iota(jnp.int32, (seqs, 128), 1)
-    for p in range(len(pieces_hbm)):
+    for p, piece_ref in enumerate(pieces):
+        first = sources_ref[p] * own
         spreads = jnp.zeros((seqs, 128), F32)
         for n in range(own):
-            normed, spread = standardised_column(first_rows, second_rows, p * own + n, residues)
+            normed, spread = standardised_column(first_rows, second_rows, first + n, residues)
             left = (normed - normed.astype(BF16).astype(F32)).astype(BF16)
-            low_ref[p, n * seqs : (n + 1) * seqs, :] = left
+            piece_ref[n * seqs : (n + 1) * seqs, :] = left
             spreads = jnp.where(lane == n, spread, spreads)
         spreads = spreads.T[:8, :]
         coarse = spreads.astype(BF16).astype(F32)
         kept = jnp.concatenate([coarse, spreads - coarse], axis=0)
         kept = jnp.concatenate([kept, jnp.zeros((16, 2 * lanes - seqs), F32)], axis=1)
-        low_ref[p, own * seqs :, :] = kept.astype(BF16)
-    sends = []
-    for p, piece_hbm in enumerate(pieces_hbm):
-        source = low_ref.at[sources_ref[p]]
-        sends.append(pltpu.make_async_copy(source, piece_hbm, sent.at[p]))
-        sends[-1].start()
-    for send in sends:
-        send.wait()
+        piece_ref[own * seqs :, :] = kept.astype(BF16)
 
 
 def standardise_low(sources, block):
@@ -167,7 +153,6 @@
     half = depth // 2
     count = sources.shape[0]
     height = residues // count * seqs + 16
-    hbm = pl.BlockSpec(memory_space=pltpu.HBM)
     return pl.pallas_call(
         low_kernel,
         grid=(1,),
@@ -176,20 +161,16 @@
             pl.BlockSpec((seqs, residues, half), lambda g: (0, 0, 0)),
             pl.BlockSpec((seqs, residues, half), lambda g: (0, 0, 1)),
         ],
-        out_specs=[hbm] * count,
-        out_shape=[pltpu.HBM((height, depth), BF16)] * count,
-        scratch_shapes=[
-            pltpu.VMEM((count, height, depth), BF16),
-            pltpu.SemaphoreType.DMA((count,)),
-        ],
+        out_specs=[pl.BlockSpec((height, depth), lambda g: (0, 0))] * count,
+        out_shape=[jax.ShapeDtypeStruct((height, depth), BF16)] * count,
         compiler_params=params(14, "arbitrary"),
         cost_estimate=cost(4),
         name="standardise_low",
     )(sources, block, block)
 
 
-def attention_kernel(key_ref, others_ref, *rest):
-    *normed_refs, turned_ref, scores_ref, weights_ref = rest
+def attention_kernel(probe_ref, extra_ref, *rest):
+    *normed_refs, turned_ref, scores_ref, weights_ref, others_ref = rest
     blocks = len(normed_refs)
     residues, seqs, _ = normed_refs[0].shape
     total = blocks * seqs
@@ -197,9 +178,14 @@
     ring = scores_ref.shape[0]
     columns = []
 
+    @pl.when(pl.program_id(0) == 0)
+    def _():
+        others_ref[:inner, :] = probe_ref[...].T
+        others_ref[inner:, :] = extra_ref[:, inner:].T
+
     def project(n):
         column = jnp.concatenate([ref[n] for ref in normed_refs], axis=0)
-        key_rows = matmul(column, key_ref[...]).astype(BF16)
+        key_rows = matmul(column, extra_ref[:, :inner]).astype(BF16)
         projected = matmul_nt(others_ref[...], column)
         queries = (projected[:inner] * UNIT_WIDTH ** (-0.5)).astype(BF16)
         value_rows = projected[inner : 2 * inner].astype(BF16)
@@ -245,7 +231,7 @@
             attend(step - 2)
 
 
-def attention(normed, key_matrix, other_matrices):
+def attention(normed, probe_matrix, extra_matrices):
     blocks = len(normed)
     residues, seqs, depth = normed[0].shape
     total = blocks * seqs
@@ -255,8 +241,8 @@
         attention_kernel,
         grid=(residues // step,),
         in_specs=[
-            pl.BlockSpec((depth, inner), lambda n: (0, 0)),
-            pl.BlockSpec((3 * inner, depth), lambda n: (0, 0)),
+            pl.BlockSpec(probe_matrix.shape, lambda n: (0, 0)),
+            pl.BlockSpec(extra_matrices.shape, lambda n: (0, 0)),
         ]
         + [pl.BlockSpec((step, seqs, depth), lambda n: (n, 0, 0))] * blocks,
         out_specs=pl.BlockSpec((step, inner, total), lambda n: (n, 0, 0)),
@@ -264,11 +250,12 @@
         scratch_shapes=[
             pltpu.VMEM((4, total, total), F32),
             pltpu.VMEM((4, total, total), BF16),
+            pltpu.VMEM((3 * inner, depth), BF16),
         ],
         compiler_params=params(12 + (total // 128) ** 2, "arbitrary"),
         cost_estimate=cost(10),
         name="attention",
-    )(key_matrix, other_matrices, *normed)
+    )(probe_matrix, extra_matrices, *normed)
 
 
 def turn_kernel(turned_ref, *gated_refs):
@@ -295,13 +282,18 @@
 
 
 def alignment_kernel(sources_ref, turned_ref, final_ref, entry_ref, *rest):
-    *refs, left_ref, right_ref, rows_ref = rest
+    *refs, left_ref, right_ref, rows_ref, turned_final_ref = rest
     blocks = len(refs) // 3
     high_refs, low_refs, spread_refs = refs[:blocks], refs[blocks : 2 * blocks], refs[2 * blocks :]
     residues, seqs, depth = high_refs[0].shape
     total = blocks * seqs
     features = TENSOR_FEATURES
     step = pl.program_id(0)
+
+    @pl.when(step == 0)
+    def _():
+        turned_final_ref[...] = final_ref[...].T
+
     for n in range(residues):
         column = jnp.concatenate([ref[n] for ref in high_refs], axis=0).astype(F32)
         column = column + jnp.concatenate(
@@ -314,7 +306,7 @@
             chosen = lax.rem(row, 8) == step * residues + n
             spreads.append(jnp.sum(jnp.where(chosen, kept, 0.0), axis=0, keepdims=True))
         spread = jnp.concatenate(spreads, axis=1)
-        updated = column.T * spread + matmul(final_ref[...], turned_ref[n])
+        updated = column.T * spread + matmul(turned_final_ref[...], turned_ref[n])
         projected = matmul(entry_ref[...], normalise_rows(updated))
         me = sources_ref[0]
         tiles = [projected[:, low : low + 128] for low in range(0, total, 128)]
@@ -373,7 +365,10 @@
             jax.ShapeDtypeStruct((features * residues, total), BF16),
             jax.ShapeDtypeStruct((residues, features, total), BF16),
         ],
-        scratch_shapes=[pltpu.VMEM((total // 128, residues * features, 128), F32)],
+        scratch_shapes=[
+            pltpu.VMEM((total // 128, residues * features, 128), F32),
+            pltpu.VMEM(final_matrix.shape, BF16),
+        ],
         compiler_params=params(16, "arbitrary"),
         cost_estimate=cost(4),
         name="alignment",
@@ -749,25 +744,20 @@
     sources = lax.axis_index("row") ^ jnp.arange(row_count, dtype=jnp.int32)
     high = exchange_rows(standardise_high(sources, homolog_tensor))
     low = standardise_low(sources, homolog_tensor)
-    others = jnp.concatenate(
-        [attention_probe_matrix.T, attention_extra_matrices[:, inner:].T], axis=0
-    )
     early = (
-        attention_extra_matrices[:, :inner],
-        others,
-        attention_final_matrix.T,
         tensor_entry_matrices.T,
         paired_entries(incoming_entry_matrices),
         sources * own_residues,
         left_groups(row_count, own_residues),
     )
-    high, low, early = lax.optimization_barrier((high, low, early))
-    key_matrix, others, final_turned, tensor_turned, entries, firsts, slots = early
+    low, high[1] = lax.optimization_barrier((low, high[1]))
+    high, early = lax.optimization_barrier((high, early))
+    tensor_turned, entries, firsts, slots = early
     low = exchange_rows(low)
-    turned = attention(high, key_matrix, others)
+    turned = attention(high, attention_probe_matrix, attention_extra_matrices)
     gated = turn_back(turned, row_count)
     left_piece, right_piece = alignment(
-        sources, high, low, turned, final_turned, tensor_turned
+        sources, high, low, turned, attention_final_matrix, tensor_turned
     )
 
     rights = exchange_rows([right_piece] * row_count)

time: 127 us -> 129 us (1.016)
  waiting for transfers between devices: 38.8 us -> 42.5 us
  local copies, waits for them, and re-layouts: 9.12 us -> 7.02 us
    ppermute x12, waiting for transfers between devices: 26.2 us -> 30.8 us  [exchange_rows(): arrived.append(lax.ppermute(pieces[shift], 'row', moves))]
    ppermute x12, starting transfers between devices: 14.3 us -> 15.9 us  [exchange_rows(): arrived.append(lax.ppermute(pieces[shift], 'row', moves))]
    unnamed x32 -> x37, local copies, waits for them, and re-layouts: 4.35 us -> 3.88 us
  transfers between devices with their start and end apart: 19 -> 19, of which waited for: 10 -> 10; matrix products, arithmetic and copies ran while one was open for 11% -> 7% of each run, Pallas kernels for 12% -> 11%
where the time goes in v13:
time: 129 us
  waiting for transfers between devices  42.5 us (33%)
  Pallas kernels  36.7 us (28%)
  starting transfers between devices  35.5 us (28%)
  local copies, waits for them, and re-layouts  7.02 us (5%)
  matrix products  3.41 us (3%)
  other arithmetic  2.4 us (2%)
    ppermute x12, waiting for transfers between devices, exchange_rows(): arrived.append(lax.ppermute(pieces[shift], 'row', moves))  30.8 us
    ppermute x12, starting transfers between devices, exchange_rows(): arrived.append(lax.ppermute(pieces[shift], 'row', moves))  15.9 us
    ppermute x4, starting transfers between devices, gather_turned(): arrived.append(lax.ppermute(source, ('row', 'col'), moves))  11 us
    pallas_call x1, Pallas kernels, attention(): pl.pallas_call(attention_kernel, grid=(residues // step,), in_specs=[pl.B...  9.48 us
    pallas_call x1, Pallas kernels, pair_update(): pl.pallas_call(pair_kernel, in_specs=[smem] * 2 + [vmem] * (5 + len(right...  8.66 us
    all_to_all x1, waiting for transfers between devices, body(): product = lax.all_to_all(product, everywhere, split_axis=0, concat_axis=0)  7.71 us
    all_to_all x1, starting transfers between devices, body(): sides = lax.all_to_all(sides, everywhere, split_axis=0, concat_axis=0)  5.58 us
    pallas_call x1, Pallas kernels, standardise_high(): pl.pallas_call(high_kernel, in_specs=[pl.BlockSpec(memory_space=pltpu.SME...  4.56 us
  transfers between devices with their start and end apart: 19, of which 10 were waited for; matrix products, arithmetic and copies ran while one was open for 7% of the time, Pallas kernels for 11%

profile of v13, /device:TPU:0, one launch (start us, length us, event | category | flops | bytes accessed | tf_op | source)
XLA Modules:
  0.0 128.6 jit_solution(9334992587097201264)
XLA Ops:
  0.6 0.0 copy-start.17
  0.7 0.0 copy-start
  0.7 4.6 %standardise_high.1 = (bf16[8,64,256]{2,1,0:T(8,128)(2,1)S(1)}, bf16[8,64,256]{2,1,0:T(8,128)(2,1)}, bf16[8,64,256]{2,1,0:T(8,128)(2,1)}, bf16[8,64,256]{2,1,0:T(8,128)(2,1)}) custom-call(s32[4]{0:T(128)S(1)} %iota_xor_fusion.sources_ref, f32[64,32,256]{2,1,0:T(8,128)} %second_ref.1), custom_call_target="tpu_custom_call" | custom-call | flops 3000000000 | bytes 3000000 | tf_op jit(solution)/shard_map/standardise_high/pallas_call | solution.py:111
  5.2 0.7 copy-done.12
  6.0 2.9 %collective-permute-start = (bf16[8,64,256]{2,1,0:T(8,128)(2,1)}, bf16[8,64,256]{2,1,0:T(8,128)(2,1)S(1)}, u32[]{:S(2)}, u32[]{:S(2)}) collective-permute-start(bf16[8,64,256]{2,1,0:T(8,128)(2,1)} %get-tuple-element.54), channel_id=1, source_target_pairs={{0,8},{8,0},{16,24},{24,16},{1,9},{9,1},{17,25},{25,17},{2,10},{10... | collective-permute-start | bytes 786440 | tf_op jit(solution)/shard_map/ppermute | solution.py:719
  8.9 1.5 %collective-permute-start.1 = (bf16[8,64,256]{2,1,0:T(8,128)(2,1)}, bf16[8,64,256]{2,1,0:T(8,128)(2,1)S(1)}, u32[]{:S(2)}, u32[]{:S(2)}) collective-permute-start(bf16[8,64,256]{2,1,0:T(8,128)(2,1)} %get-tuple-element.56), channel_id=1, source_target_pairs={{0,16},{8,24},{16,0},{24,8},{1,17},{9,25},{17,1},{25,9},{2,18},{10... | collective-permute-start | bytes 786440 | tf_op jit(solution)/shard_map/ppermute | solution.py:719
  10.4 0.0 collective-permute-start.2
  10.5 0.1 copy.12
  10.7 0.1 pad_add_fusion.left_slots_ref
  10.7 3.5 %standardise_low.1 = (bf16[528,256]{1,0:T(8,128)(2,1)S(1)}, bf16[528,256]{1,0:T(8,128)(2,1)S(1)}, bf16[528,256]{1,0:T(8,128)(2,1)S(1)}, bf16[528,256]{1,0:T(8,128)(2,1)S(1)}) custom-call(s32[4]{0:T(128)S(1)} %iota_xor_fusion.sources_ref, f32[64,32,256]{2,1,0:T(8,128)S(1)} %copy-done, f32[64,32,256]{2,1,0:T(8,128)S(1)} %copy-done), custom_call_target="tpu_custom_call" | custom-call | flops 4000000000 | bytes 4000000 | tf_op jit(solution)/shard_map/standardise_low/pallas_call | solution.py:156
  14.2 2.0 %collective-permute-done.rest_1_ = bf16[8,64,256]{2,1,0:T(8,128)(2,1)S(1)} collective-permute-done((bf16[8,64,256]{2,1,0:T(8,128)(2,1)}, bf16[8,64,256]{2,1,0:T(8,128)(2,1)S(1)}, u32[]{:S(2)}, u32[]{:S(2)}) %collective-permute-start) | collective-permute-done | bytes 262176 | tf_op jit(solution)/shard_map/ppermute | solution.py:719
  16.2 6.3 %collective-permute-done.1.rest_2_ = bf16[8,64,256]{2,1,0:T(8,128)(2,1)S(1)} collective-permute-done((bf16[8,64,256]{2,1,0:T(8,128)(2,1)}, bf16[8,64,256]{2,1,0:T(8,128)(2,1)S(1)}, u32[]{:S(2)}, u32[]{:S(2)}) %collective-permute-start.1) | collective-permute-done | bytes 262176 | tf_op jit(solution)/shard_map/ppermute | solution.py:719
  22.5 0.7 copy-done.5
  23.2 0.0 collective-permute-done.2.rest_3_
  23.2 0.6 collective-permute-start.3
  23.8 1.4 %collective-permute-start.4 = (bf16[528,256]{1,0:T(8,128)(2,1)S(1)}, bf16[528,256]{1,0:T(8,128)(2,1)S(1)}, u32[]{:S(2)}, u32[]{:S(2)}) collective-permute-start(bf16[528,256]{1,0:T(8,128)(2,1)S(1)} %get-tuple-element.71), channel_id=1, source_target_pairs={{0,16},{8,24},{16,0},{24,8},{1,17},{9,25},{17,1},{25,9},{2,18},{10... | collective-permute-start | bytes 811016 | tf_op jit(solution)/shard_map/ppermute | solution.py:719
  25.3 1.4 %collective-permute-start.5 = (bf16[528,256]{1,0:T(8,128)(2,1)S(1)}, bf16[528,256]{1,0:T(8,128)(2,1)S(1)}, u32[]{:S(2)}, u32[]{:S(2)}) collective-permute-start(bf16[528,256]{1,0:T(8,128)(2,1)S(1)} %get-tuple-element.72), channel_id=1, source_target_pairs={{0,24},{8,16},{16,8},{24,0},{1,25},{9,17},{17,9},{25,1},{2,26},{10... | collective-permute-start | bytes 811016 | tf_op jit(solution)/shard_map/ppermute | solution.py:719
  26.7 0.9 copy-done.6
  27.6 9.5 %attention.1.turned_ref = bf16[8,256,256]{2,1,0:T(8,128)(2,1)S(1)} custom-call(bf16[256,256]{1,0:T(8,128)(2,1)S(1)} %copy-done.8, bf16[256,768]{1,0:T(8,128)(2,1)S(1)} %copy-done.3, bf16[8,64,256]{2,1,0:T(8,128)(2,1)S(1)} %copy-done.13, bf16[8,64,256]{2,1,0:T(8,128)(2,1)S(1)} %collective-permute-done.rest_1_, bf16[8,64,256]{2,1,0:T(8,128)(2,1)S(1)} %copy-done.6, ...), custom_call_target="tpu_custom_call" | custom-call | flops 10000000000 | bytes 10000000 | tf_op jit(solution)/shard_map/attention/pallas_call | solution.py:240
  37.1 0.0 collective-permute-done.3.rest_5_.rest_9_
  37.1 0.0 collective-permute-done.4.rest_6_.rest_10_
  37.2 0.0 collective-permute-done.5.rest_7_.rest_11_
  37.2 4.3 %alignment.1 = (bf16[256,256]{1,0:T(8,128)(2,1)S(1)}, bf16[8,32,256]{2,1,0:T(8,128)(2,1)S(1)}) custom-call(s32[4]{0:T(128)S(1)} %iota_xor_fusion.sources_ref, bf16[8,256,256]{2,1,0:T(8,128)(2,1)S(1)} %attention.1.turned_ref, bf16[256,256]{1,0:T(8,128)(2,1)S(1)} %copy-done.1, bf16[64,256]{1,0:T(8,128)(2,1)S(1)} %bitcast.30, ...), custom_call_target="tpu_custom_call" | custom-call | flops 4000000000 | bytes 4000000 | tf_op jit(solution)/shard_map/alignment/pallas_call | solution.py:348
  41.5 0.7 collective-permute-start.8
  42.2 0.7 collective-permute-start.6
  42.8 4.1 %collective-permute-start.7 = (bf16[256,256]{1,0:T(8,128)(2,1)S(1)}, bf16[256,256]{1,0:T(8,128)(2,1)S(1)}, u32[]{:S(2)}, u32[]{:S(2)}) collective-permute-start(bf16[256,256]{1,0:T(8,128)(2,1)S(1)} %get-tuple-element.75), channel_id=1, source_target_pairs={{0,2},{1,3},{2,10},{3,11},{4,18},{5,19},{6,26},{7,27},{8,4},{9,5},... | collective-permute-start | bytes 393224 | tf_op jit(solution)/shard_map/ppermute | solution.py:680
  47.0 0.0 collective-permute-done.8.rest_1_
  47.0 4.3 %collective-permute-start.9 = (bf16[256,256]{1,0:T(8,128)(2,1)S(1)}, bf16[256,256]{1,0:T(8,128)(2,1)S(1)}, u32[]{:S(2)}, u32[]{:S(2)}) collective-permute-start(bf16[256,256]{1,0:T(8,128)(2,1)S(1)} %get-tuple-element.75), channel_id=1, source_target_pairs={{0,4},{1,5},{2,12},{3,13},{4,20},{5,21},{6,28},{7,29},{8,6},{9,7},... | collective-permute-start | bytes 393224 | tf_op jit(solution)/shard_map/ppermute | solution.py:680
  51.3 1.9 %collective-permute-start.10 = (bf16[256,256]{1,0:T(8,128)(2,1)S(1)}, bf16[256,256]{1,0:T(8,128)(2,1)S(1)}, u32[]{:S(2)}, u32[]{:S(2)}) collective-permute-start(bf16[256,256]{1,0:T(8,128)(2,1)S(1)} %get-tuple-element.75), channel_id=1, source_target_pairs={{0,6},{1,7},{2,14},{3,15},{4,22},{5,23},{6,30},{7,31},{8,0},{9,1},... | collective-permute-start | bytes 393224 | tf_op jit(solution)/shard_map/ppermute | solution.py:680
  53.2 1.2 collective-permute-start.11
  54.4 0.0 collective-permute-done.6
  54.4 2.5 %collective-permute-start.12 = (bf16[8,32,256]{2,1,0:T(8,128)(2,1)S(1)}, bf16[8,32,256]{2,1,0:T(8,128)(2,1)S(1)}, u32[]{:S(2)}, u32[]{:S(2)}) collective-permute-start(bf16[8,32,256]{2,1,0:T(8,128)(2,1)S(1)} %get-tuple-element.78.rest_0_), channel_id=1, source_target_pairs={{0,24},{8,16},{16,8},{24,0},{1,25},{9,17},{17,9},{25,1},{2,26},{10... | collective-permute-start | bytes 393224 | tf_op jit(solution)/shard_map/ppermute | solution.py:719
  56.9 0.0 collective-permute-done.7
  56.9 0.3 collective-permute-done.9
  57.2 1.5 %collective-permute-done.10 = bf16[256,256]{1,0:T(8,128)(2,1)S(1)} collective-permute-done((bf16[256,256]{1,0:T(8,128)(2,1)S(1)}, bf16[256,256]{1,0:T(8,128)(2,1)S(1)}, u32[]{:S(2)}, u32[]{:S(2)}) %collective-permute-start.10) | collective-permute-done | bytes 131104 | tf_op jit(solution)/shard_map/ppermute | solution.py:680
  58.8 0.1 pad_maximum_fusion.1.own_ref
  58.9 0.0 copy-start.2
  58.9 0.0 copy-start.4
  58.9 0.0 copy-start.10
  58.9 0.0 collective-permute-done.11.rest_2_
  58.9 1.9 %collective-permute-done.12.rest_3_ = bf16[8,32,256]{2,1,0:T(8,128)(2,1)S(1)} collective-permute-done((bf16[8,32,256]{2,1,0:T(8,128)(2,1)S(1)}, bf16[8,32,256]{2,1,0:T(8,128)(2,1)S(1)}, u32[]{:S(2)}, u32[]{:S(2)}) %collective-permute-start.12) | collective-permute-done | bytes 131104 | tf_op jit(solution)/shard_map/ppermute | solution.py:719
  60.8 1.7 %turn_back.1 = (bf16[8,64,256]{2,1,0:T(8,128)(2,1)}, bf16[8,64,256]{2,1,0:T(8,128)(2,1)}, bf16[8,64,256]{2,1,0:T(8,128)(2,1)}, bf16[8,64,256]{2,1,0:T(8,128)(2,1)}) custom-call(bf16[8,256,256]{2,1,0:T(8,128)(2,1)S(1)} %attention.1.turned_ref), custom_call_target="tpu_custom_call" | custom-call | flops 2000000000 | bytes 2000000 | tf_op jit(solution)/shard_map/turn_back/pallas_call | solution.py:272
  62.5 0.2 collective-permute-done.13.other_ref
  62.7 8.7 %pair_update.1 = (f32[32,64,128]{2,1,0:T(8,128)}, f32[32,64,128]{2,1,0:T(8,128)}, bf16[128,32,128]{2,1,0:T(8,128)(2,1)}) custom-call(s32[8]{0:T(128)S(1)} %pad_add_fusion.left_slots_ref, s32[4]{0:T(128)S(1)} %broadcast_multiply_fusion.right_firsts_ref, bf16[4,256,256]{2,1,0:T(8,128)(2,1)S(1)} %pad_maximum_fusion.1.own_ref, ...), custom_call_target="tpu_custom_call" | custom-call | flops 12000000000 | bytes 12000000 | tf_op jit(solution)/shard_map/pair_update/pallas_call | solution.py:518
  71.4 5.6 %all-to-all-start = ((bf16[32,4,32,128]{3,2,1,0:T(8,128)(2,1)}), bf16[32,4,32,128]{3,2,1,0:T(8,128)(2,1)S(1)}, u32[]{:S(2)}, u32[]{:S(2)}) async-start(bf16[32,4,32,128]{3,2,1,0:T(8,128)(2,1)} %bitcast.32), calls=%async_computation | async-start | bytes 2097152 | tf_op jit(solution)/shard_map/all_to_all | solution.py:784
  77.0 0.0 copy-start.14
  77.0 1.8 %collective-permute-start.14 = (bf16[8,64,256]{2,1,0:T(8,128)(2,1)}, bf16[8,64,256]{2,1,0:T(8,128)(2,1)S(1)}, u32[]{:S(2)}, u32[]{:S(2)}) collective-permute-start(bf16[8,64,256]{2,1,0:T(8,128)(2,1)} %get-tuple-element.85), channel_id=1, source_target_pairs={{0,8},{8,0},{16,24},{24,16},{1,9},{9,1},{17,25},{25,17},{2,10},{10... | collective-permute-start | bytes 786440 | tf_op jit(solution)/shard_map/ppermute | solution.py:719
  78.8 1.5 %collective-permute-start.15 = (bf16[8,64,256]{2,1,0:T(8,128)(2,1)}, bf16[8,64,256]{2,1,0:T(8,128)(2,1)S(1)}, u32[]{:S(2)}, u32[]{:S(2)}) collective-permute-start(bf16[8,64,256]{2,1,0:T(8,128)(2,1)} %get-tuple-element.86), channel_id=1, source_target_pairs={{0,16},{8,24},{16,0},{24,8},{1,17},{9,25},{17,1},{25,9},{2,18},{10... | collective-permute-start | bytes 786440 | tf_op jit(solution)/shard_map/ppermute | solution.py:719
  80.3 0.3 collective-permute-start.16
  80.5 13.7 %collective-permute-done.14 = bf16[8,64,256]{2,1,0:T(8,128)(2,1)S(1)} collective-permute-done((bf16[8,64,256]{2,1,0:T(8,128)(2,1)}, bf16[8,64,256]{2,1,0:T(8,128)(2,1)S(1)}, u32[]{:S(2)}, u32[]{:S(2)}) %collective-permute-start.14) | collective-permute-done | bytes 262176 | tf_op jit(solution)/shard_map/ppermute | solution.py:719
  94.3 0.0 collective-permute-done.15
  94.3 0.7 copy-done.15
  95.0 0.7 copy-done.16
  95.7 6.9 %collective-permute-done.16 = bf16[8,64,256]{2,1,0:T(8,128)(2,1)} collective-permute-done((bf16[8,64,256]{2,1,0:T(8,128)(2,1)}, bf16[8,64,256]{2,1,0:T(8,128)(2,1)}, u32[]{:S(2)}, u32[]{:S(2)}) %collective-permute-start.16) | collective-permute-done | bytes 262176 | tf_op jit(solution)/shard_map/ppermute | solution.py:719
  102.6 1.9 %all-to-all-done.sides_ref = bf16[32,4,32,128]{3,2,1,0:T(8,128)(2,1)S(1)} async-done(((bf16[32,4,32,128]{3,2,1,0:T(8,128)(2,1)}), bf16[32,4,32,128]{3,2,1,0:T(8,128)(2,1)S(1)}, u32[]{:S(2)}, u32[]{:S(2)}) %all-to-all-start) | async-done | bytes 1048608 | tf_op jit(solution)/shard_map/all_to_all | solution.py:784
  104.6 1.7 %triangle_product.1 = bf16[32,4,16,128]{3,2,1,0:T(8,128)(2,1)} custom-call(bf16[32,4,32,128]{3,2,1,0:T(8,128)(2,1)S(1)} %all-to-all-done.sides_ref), custom_call_target="tpu_custom_call" | custom-call | flops 3000000000 | bytes 3000000 | tf_op jit(solution)/shard_map/triangle_product/pallas_call | solution.py:582
  106.2 3.0 %all-to-all-start.1 = ((bf16[32,4,16,128]{3,2,1,0:T(8,128)(2,1)}), bf16[32,4,16,128]{3,2,1,0:T(8,128)(2,1)S(1)}, u32[]{:S(2)}, u32[]{:S(2)}) async-start(bf16[32,4,16,128]{3,2,1,0:T(8,128)(2,1)} %triangle_product.1), calls=%async_computation.1 | async-start | bytes 1048576 | tf_op jit(solution)/shard_map/all_to_all | solution.py:787
  109.3 0.1 broadcast_in_dim.14
  109.3 0.1 broadcast_in_dim.15
  109.5 2.2 %pad_maximum_fusion = bf16[4,8,64,256]{3,2,1,0:T(8,128)(2,1)} fusion(bf16[1,8,64,256]{3,2,1,0:T(8,128)(2,1)} %bitcast.11, bf16[1,8,64,256]{3,2,1,0:T(8,128)(2,1)} %bitcast.36, bf16[1,8,64,256]{3,2,1,0:T(8,128)(2,1)} %bitcast.35, bf16[1,8,64,256]{3,2,1,0:T(8,128)(2,1)S(1)} %bitcast.34), kind=kLoop, calls=%fused_computation.2 | loop fusion | flops 1572864 | bytes 2097152 | tf_op jit(solution)/shard_map/stack | solution.py:789
  111.7 2.8 %gather_fusion = bf16[4,8,64,256]{3,2,1,0:T(8,128)(2,1)} fusion(bf16[4,8,64,256]{3,2,1,0:T(8,128)(2,1)} %pad_maximum_fusion, s32[1024]{0:T(1024)S(1)} %pad_clamp_fusion), kind=kCustom, calls=%fused_computation | custom fusion | bytes 2097168 | tf_op jit(solution)/shard_map/jit(_take)/gather | solution.py:789
  114.5 3.4 %convolution_add_fusion = f32[64,32,256]{2,1,0:T(8,128)} fusion(f32[64,32,256]{2,1,0:T(8,128)S(1)} %copy-done, bf16[32,64,256]{2,1,0:T(8,128)(2,1)} %bitcast.31, pred[32]{0:T(512)(128)(4,1)S(1)} %broadcast_in_dim.15, bf16[256,256]{1,0:T(8,128)(2,1)S(1)} %copy-done.1), kind=kOutput, calls=%fused_computation.1 | convolution fusion | flops 269484032 | bytes 5373984 | tf_op jit(solution)/shard_map/dot_general | solution.py:791
  117.9 7.7 %all-to-all-done.1 = bf16[32,4,16,128]{3,2,1,0:T(8,128)(2,1)S(1)} async-done(((bf16[32,4,16,128]{3,2,1,0:T(8,128)(2,1)}), bf16[32,4,16,128]{3,2,1,0:T(8,128)(2,1)S(1)}, u32[]{:S(2)}, u32[]{:S(2)}) %all-to-all-start.1) | async-done | bytes 524320 | tf_op jit(solution)/shard_map/all_to_all | solution.py:787
  125.6 2.8 %pair_result.1 = f32[64,32,128]{2,1,0:T(8,128)} custom-call(bf16[128,16,128]{2,1,0:T(8,128)(2,1)S(1)} %bitcast.27, bf16[128,128]{1,0:T(8,128)(2,1)S(1)} %copy-done.11, f32[32,64,128]{2,1,0:T(8,128)} %get-tuple-element.94.mid_hbm, f32[32,64,128]{2,1,0:T(8,128)} %get-tuple-element.95.gate_hbm), custom_call_target="tpu_custom_call" | custom-call | flops 3000000000 | bytes 3000000 | tf_op jit(solution)/shard_map/pair_result/pallas_call | solution.py:640
  (34 shorter events, 0.1 us)
Async XLA Ops:
  0.6 9.8 %copy-start.17 = (bf16[128,512]{1,0:T(8,128)(2,1)S(1)}, bf16[128,512]{1,0:T(8,128)(2,1)}, u32[]{:S(2)}) copy-start(bf16[128,512]{1,0:T(8,128)(2,1)} %param.17) | copy-start | bytes 393220
  0.7 10.1 %copy-start = (f32[64,32,256]{2,1,0:T(8,128)S(1)}, f32[64,32,256]{2,1,0:T(8,128)}, u32[]{:S(2)}) copy-start(f32[64,32,256]{2,1,0:T(8,128)} %second_ref.1) | copy-start | bytes 6291460
  5.2 0.7 copy-start.12
  6.0 10.3 %collective-permute-start = (bf16[8,64,256]{2,1,0:T(8,128)(2,1)}, bf16[8,64,256]{2,1,0:T(8,128)(2,1)S(1)}, u32[]{:S(2)}, u32[]{:S(2)}) collective-permute-start(bf16[8,64,256]{2,1,0:T(8,128)(2,1)} %get-tuple-element.54), channel_id=1, source_target_pairs={{0,8},{8,0},{16,24},{24,16},{1,9},{9,1},{17,25},{25,17},{2,10},{10... | collective-permute-start | bytes 786440 | tf_op jit(solution)/shard_map/ppermute | solution.py:719
  8.9 13.6 %collective-permute-start.1 = (bf16[8,64,256]{2,1,0:T(8,128)(2,1)}, bf16[8,64,256]{2,1,0:T(8,128)(2,1)S(1)}, u32[]{:S(2)}, u32[]{:S(2)}) collective-permute-start(bf16[8,64,256]{2,1,0:T(8,128)(2,1)} %get-tuple-element.56), channel_id=1, source_target_pairs={{0,16},{8,24},{16,0},{24,8},{1,17},{9,25},{17,1},{25,9},{2,18},{10... | collective-permute-start | bytes 786440 | tf_op jit(solution)/shard_map/ppermute | solution.py:719
  10.4 12.8 %collective-permute-start.2 = (bf16[8,64,256]{2,1,0:T(8,128)(2,1)}, bf16[8,64,256]{2,1,0:T(8,128)(2,1)}, u32[]{:S(2)}, u32[]{:S(2)}) collective-permute-start(bf16[8,64,256]{2,1,0:T(8,128)(2,1)} %get-tuple-element.57), channel_id=1, source_target_pairs={{0,24},{8,16},{16,8},{24,0},{1,25},{9,17},{17,9},{25,1},{2,26},{10... | collective-permute-start | bytes 786440 | tf_op jit(solution)/shard_map/ppermute | solution.py:719
  10.7 16.0 %copy-start.3 = (bf16[256,768]{1,0:T(8,128)(2,1)S(1)}, bf16[256,768]{1,0:T(8,128)(2,1)}, u32[]{:S(2)}) copy-start(bf16[256,768]{1,0:T(8,128)(2,1)} %extra_ref.1) | copy-start | bytes 1179652
  10.7 16.0 %copy-start.8 = (bf16[256,256]{1,0:T(8,128)(2,1)S(1)}, bf16[256,256]{1,0:T(8,128)(2,1)}, u32[]{:S(2)}) copy-start(bf16[256,256]{1,0:T(8,128)(2,1)} %probe_ref.1) | copy-start | bytes 393220
  10.7 16.0 %copy-start.13 = (bf16[8,64,256]{2,1,0:T(8,128)(2,1)S(1)}, bf16[8,64,256]{2,1,0:T(8,128)(2,1)}, u32[]{:S(2)}) copy-start(bf16[8,64,256]{2,1,0:T(8,128)(2,1)} %copy-done.12) | copy-start | bytes 786436
  22.5 0.7 copy-start.5
  23.2 14.0 %copy-start.1 = (bf16[256,256]{1,0:T(8,128)(2,1)S(1)}, bf16[256,256]{1,0:T(8,128)(2,1)}, u32[]{:S(2)}) copy-start(bf16[256,256]{1,0:T(8,128)(2,1)} %final_ref.2) | copy-start | bytes 393220
  23.2 13.9 %collective-permute-start.3 = (bf16[528,256]{1,0:T(8,128)(2,1)S(1)}, bf16[528,256]{1,0:T(8,128)(2,1)S(1)}, u32[]{:S(2)}, u32[]{:S(2)}) collective-permute-start(bf16[528,256]{1,0:T(8,128)(2,1)S(1)} %get-tuple-element.70), channel_id=1, source_target_pairs={{0,8},{8,0},{16,24},{24,16},{1,9},{9,1},{17,25},{25,17},{2,10},{10... | collective-permute-start | bytes 811016 | tf_op jit(solution)/shard_map/ppermute | solution.py:719
  23.8 13.3 %collective-permute-start.4 = (bf16[528,256]{1,0:T(8,128)(2,1)S(1)}, bf16[528,256]{1,0:T(8,128)(2,1)S(1)}, u32[]{:S(2)}, u32[]{:S(2)}) collective-permute-start(bf16[528,256]{1,0:T(8,128)(2,1)S(1)} %get-tuple-element.71), channel_id=1, source_target_pairs={{0,16},{8,24},{16,0},{24,8},{1,17},{9,25},{17,1},{25,9},{2,18},{10... | collective-permute-start | bytes 811016 | tf_op jit(solution)/shard_map/ppermute | solution.py:719
  25.3 11.9 %collective-permute-start.5 = (bf16[528,256]{1,0:T(8,128)(2,1)S(1)}, bf16[528,256]{1,0:T(8,128)(2,1)S(1)}, u32[]{:S(2)}, u32[]{:S(2)}) collective-permute-start(bf16[528,256]{1,0:T(8,128)(2,1)S(1)} %get-tuple-element.72), channel_id=1, source_target_pairs={{0,24},{8,16},{16,8},{24,0},{1,25},{9,17},{17,9},{25,1},{2,26},{10... | collective-permute-start | bytes 811016 | tf_op jit(solution)/shard_map/ppermute | solution.py:719
  26.7 1.0 copy-start.6
  27.6 9.5 %copy-start.7 = (bf16[8,64,256]{2,1,0:T(8,128)(2,1)S(1)}, bf16[8,64,256]{2,1,0:T(8,128)(2,1)}, u32[]{:S(2)}) copy-start(bf16[8,64,256]{2,1,0:T(8,128)(2,1)} %copy-done.5) | copy-start | bytes 786436
  27.6 9.5 %copy-start.9 = (bf16[256,64]{0,1:T(8,128)(2,1)S(1)}, bf16[256,64]{0,1:T(8,128)(2,1)}, u32[]{:S(2)}) copy-start(bf16[256,64]{0,1:T(8,128)(2,1)} %param.15) | copy-start | bytes 98308
  41.5 5.5 %collective-permute-start.8 = (bf16[8,32,256]{2,1,0:T(8,128)(2,1)S(1)}, bf16[8,32,256]{2,1,0:T(8,128)(2,1)S(1)}, u32[]{:S(2)}, u32[]{:S(2)}) collective-permute-start(bf16[8,32,256]{2,1,0:T(8,128)(2,1)S(1)} %get-tuple-element.78.rest_0_), channel_id=1, source_target_pairs={{0,8},{8,0},{16,24},{24,16},{1,9},{9,1},{17,25},{25,17},{2,10},{10... | collective-permute-start | bytes 393224 | tf_op jit(solution)/shard_map/ppermute | solution.py:719
  42.2 12.2 %collective-permute-start.6 = (bf16[256,256]{1,0:T(8,128)(2,1)S(1)}, bf16[256,256]{1,0:T(8,128)(2,1)S(1)}, u32[]{:S(2)}, u32[]{:S(2)}) collective-permute-start(bf16[256,256]{1,0:T(8,128)(2,1)S(1)} %get-tuple-element.75), channel_id=1, source_target_pairs={{0,0},{1,1},{2,8},{3,9},{4,16},{5,17},{6,24},{7,25},{8,2},{9,3},{1... | collective-permute-start | bytes 393224 | tf_op jit(solution)/shard_map/ppermute | solution.py:680
  42.8 14.1 %collective-permute-start.7 = (bf16[256,256]{1,0:T(8,128)(2,1)S(1)}, bf16[256,256]{1,0:T(8,128)(2,1)S(1)}, u32[]{:S(2)}, u32[]{:S(2)}) collective-permute-start(bf16[256,256]{1,0:T(8,128)(2,1)S(1)} %get-tuple-element.75), channel_id=1, source_target_pairs={{0,2},{1,3},{2,10},{3,11},{4,18},{5,19},{6,26},{7,27},{8,4},{9,5},... | collective-permute-start | bytes 393224 | tf_op jit(solution)/shard_map/ppermute | solution.py:680
  47.0 10.3 %collective-permute-start.9 = (bf16[256,256]{1,0:T(8,128)(2,1)S(1)}, bf16[256,256]{1,0:T(8,128)(2,1)S(1)}, u32[]{:S(2)}, u32[]{:S(2)}) collective-permute-start(bf16[256,256]{1,0:T(8,128)(2,1)S(1)} %get-tuple-element.75), channel_id=1, source_target_pairs={{0,4},{1,5},{2,12},{3,13},{4,20},{5,21},{6,28},{7,29},{8,6},{9,7},... | collective-permute-start | bytes 393224 | tf_op jit(solution)/shard_map/ppermute | solution.py:680
  51.3 7.5 %collective-permute-start.10 = (bf16[256,256]{1,0:T(8,128)(2,1)S(1)}, bf16[256,256]{1,0:T(8,128)(2,1)S(1)}, u32[]{:S(2)}, u32[]{:S(2)}) collective-permute-start(bf16[256,256]{1,0:T(8,128)(2,1)S(1)} %get-tuple-element.75), channel_id=1, source_target_pairs={{0,6},{1,7},{2,14},{3,15},{4,22},{5,23},{6,30},{7,31},{8,0},{9,1},... | collective-permute-start | bytes 393224 | tf_op jit(solution)/shard_map/ppermute | solution.py:680
  53.2 5.7 %collective-permute-start.11 = (bf16[8,32,256]{2,1,0:T(8,128)(2,1)S(1)}, bf16[8,32,256]{2,1,0:T(8,128)(2,1)S(1)}, u32[]{:S(2)}, u32[]{:S(2)}) collective-permute-start(bf16[8,32,256]{2,1,0:T(8,128)(2,1)S(1)} %get-tuple-element.78.rest_0_), channel_id=1, source_target_pairs={{0,16},{8,24},{16,0},{24,8},{1,17},{9,25},{17,1},{25,9},{2,18},{10... | collective-permute-start | bytes 393224 | tf_op jit(solution)/shard_map/ppermute | solution.py:719
  54.4 6.4 %collective-permute-start.12 = (bf16[8,32,256]{2,1,0:T(8,128)(2,1)S(1)}, bf16[8,32,256]{2,1,0:T(8,128)(2,1)S(1)}, u32[]{:S(2)}, u32[]{:S(2)}) collective-permute-start(bf16[8,32,256]{2,1,0:T(8,128)(2,1)S(1)} %get-tuple-element.78.rest_0_), channel_id=1, source_target_pairs={{0,24},{8,16},{16,8},{24,0},{1,25},{9,17},{17,9},{25,1},{2,26},{10... | collective-permute-start | bytes 393224 | tf_op jit(solution)/shard_map/ppermute | solution.py:719
  58.9 3.9 %copy-start.2 = (f32[64,32,128]{2,1,0:T(8,128)S(1)}, f32[64,32,128]{2,1,0:T(8,128)}, u32[]{:S(2)}) copy-start(f32[64,32,128]{2,1,0:T(8,128)} %param.11) | copy-start | bytes 3145732
  58.9 3.8 %copy-start.4 = (bf16[1024,128]{1,0:T(8,128)(2,1)S(1)}, bf16[1024,128]{1,0:T(8,128)(2,1)}, u32[]{:S(2)}) copy-start(bf16[1024,128]{1,0:T(8,128)(2,1)} %rest_4_.1) | copy-start | bytes 786436
  58.9 3.8 %copy-start.10 = (bf16[128,128]{1,0:T(8,128)(2,1)S(1)}, bf16[128,128]{1,0:T(8,128)(2,1)}, u32[]{:S(2)}) copy-start(bf16[128,128]{1,0:T(8,128)(2,1)} %rest_6_.1) | copy-start | bytes 98308
  60.8 1.9 %collective-permute-start.13 = (bf16[4,256,256]{2,1,0:T(8,128)(2,1)S(1)}, bf16[4,256,256]{2,1,0:T(8,128)(2,1)S(1)}, u32[]{:S(2)}, u32[]{:S(2)}) collective-permute-start(bf16[4,256,256]{2,1,0:T(8,128)(2,1)S(1)} %pad_maximum_fusion.1.own_ref), channel_id=1, source_target_pairs={{0,1},{1,0},{2,3},{3,2},{4,5},{5,4},{6,7},{7,6},{8,9},{9,8},{10,11... | collective-permute-start | bytes 1572872 | tf_op jit(solution)/shard_map/ppermute | solution.py:666
  71.4 33.2 %all-to-all-start = ((bf16[32,4,32,128]{3,2,1,0:T(8,128)(2,1)}), bf16[32,4,32,128]{3,2,1,0:T(8,128)(2,1)S(1)}, u32[]{:S(2)}, u32[]{:S(2)}) async-start(bf16[32,4,32,128]{3,2,1,0:T(8,128)(2,1)} %bitcast.32), calls=%async_computation | async-start | bytes 2097152 | tf_op jit(solution)/shard_map/all_to_all | solution.py:784
  77.0 32.5 %copy-start.14 = (bf16[8,64,256]{2,1,0:T(8,128)(2,1)S(1)}, bf16[8,64,256]{2,1,0:T(8,128)(2,1)}, u32[]{:S(2)}) copy-start(bf16[8,64,256]{2,1,0:T(8,128)(2,1)} %get-tuple-element.89) | copy-start | bytes 786436
  77.0 17.3 %collective-permute-start.14 = (bf16[8,64,256]{2,1,0:T(8,128)(2,1)}, bf16[8,64,256]{2,1,0:T(8,128)(2,1)S(1)}, u32[]{:S(2)}, u32[]{:S(2)}) collective-permute-start(bf16[8,64,256]{2,1,0:T(8,128)(2,1)} %get-tuple-element.85), channel_id=1, source_target_pairs={{0,8},{8,0},{16,24},{24,16},{1,9},{9,1},{17,25},{25,17},{2,10},{10... | collective-permute-start | bytes 786440 | tf_op jit(solution)/shard_map/ppermute | solution.py:719
  78.8 15.4 %collective-permute-start.15 = (bf16[8,64,256]{2,1,0:T(8,128)(2,1)}, bf16[8,64,256]{2,1,0:T(8,128)(2,1)S(1)}, u32[]{:S(2)}, u32[]{:S(2)}) collective-permute-start(bf16[8,64,256]{2,1,0:T(8,128)(2,1)} %get-tuple-element.86), channel_id=1, source_target_pairs={{0,16},{8,24},{16,0},{24,8},{1,17},{9,25},{17,1},{25,9},{2,18},{10... | collective-permute-start | bytes 786440 | tf_op jit(solution)/shard_map/ppermute | solution.py:719
  80.3 22.4 %collective-permute-start.16 = (bf16[8,64,256]{2,1,0:T(8,128)(2,1)}, bf16[8,64,256]{2,1,0:T(8,128)(2,1)}, u32[]{:S(2)}, u32[]{:S(2)}) collective-permute-start(bf16[8,64,256]{2,1,0:T(8,128)(2,1)} %get-tuple-element.87), channel_id=1, source_target_pairs={{0,24},{8,16},{16,8},{24,0},{1,25},{9,17},{17,9},{25,1},{2,26},{10... | collective-permute-start | bytes 786440 | tf_op jit(solution)/shard_map/ppermute | solution.py:719
  94.3 0.7 copy-start.15
  95.0 0.7 copy-start.16
  106.2 19.4 %all-to-all-start.1 = ((bf16[32,4,16,128]{3,2,1,0:T(8,128)(2,1)}), bf16[32,4,16,128]{3,2,1,0:T(8,128)(2,1)S(1)}, u32[]{:S(2)}, u32[]{:S(2)}) async-start(bf16[32,4,16,128]{3,2,1,0:T(8,128)(2,1)} %triangle_product.1), calls=%async_computation.1 | async-start | bytes 1048576 | tf_op jit(solution)/shard_map/all_to_all | solution.py:787
  114.5 11.1 %copy-start.11 = (bf16[128,128]{1,0:T(8,128)(2,1)S(1)}, bf16[128,128]{1,0:T(8,128)(2,1)}, u32[]{:S(2)}) copy-start(bf16[128,128]{1,0:T(8,128)(2,1)} %final_ref.3) | copy-start | bytes 98308

commit v14 on v12

--- a/solution.py
+++ b/solution.py
@@ -66,10 +66,13 @@
     return (centred * lax.rsqrt(variance + EPS)).astype(BF16)
 
 
-def standardised_column(first_rows, second_rows, n, residues):
+def standardised_columns(first_rows, second_rows, first, count, residues):
     seqs = first_rows.shape[0] // residues
-    rows = pl.ds(n, seqs, stride=residues)
-    column = jnp.concatenate([first_rows[rows, :], second_rows[rows, :]], axis=1)
+    columns = []
+    for n in range(first, first + count):
+        rows = pl.ds(n, seqs, stride=residues)
+        columns.append(jnp.concatenate([first_rows[rows, :], second_rows[rows, :]], axis=1))
+    column = jnp.concatenate(columns, axis=0)
     centred = column - jnp.mean(column, axis=1, keepdims=True)
     variance = jnp.mean(centred * centred, axis=1, keepdims=True) + EPS
     scale = lax.rsqrt(variance)
@@ -77,29 +80,28 @@
 
 
 def high_kernel(sources_ref, block_hbm, *rest):
-    *pieces_hbm, block_ref, first_ref, second_ref, high_ref, fetched, sent = rest
+    *pieces_hbm, first_ref, second_ref, high_ref, fetched, sent = rest
     seqs, residues, lanes = first_ref.shape
     own = residues // len(pieces_hbm)
     step = 16
     fetches, sends = [], []
     for s in range(0, seqs, step):
         chosen = pl.ds(s, step)
-        fetches.append(
-            pltpu.make_async_copy(
-                block_hbm.at[chosen], block_ref.at[chosen], fetched.at[len(fetches)]
+        for half, ref in enumerate((first_ref, second_ref)):
+            source = block_hbm.at[chosen, :, pl.ds(half * lanes, lanes)]
+            fetches.append(
+                pltpu.make_async_copy(source, ref.at[chosen], fetched.at[len(fetches)])
             )
-        )
-        fetches[-1].start()
+            fetches[-1].start()
     for part in range(seqs // step):
         chosen = pl.ds(part * step, step)
-        fetches[part].wait()
-        first_ref[chosen] = block_ref[chosen, :, :lanes]
-        second_ref[chosen] = block_ref[chosen, :, lanes:]
+        fetches[2 * part].wait()
+        fetches[2 * part + 1].wait()
         first_rows = first_ref.at[chosen].reshape(step * residues, lanes)
         second_rows = second_ref.at[chosen].reshape(step * residues, lanes)
-        for n in range(residues):
-            normed, _ = standardised_column(first_rows, second_rows, n, residues)
-            high_ref[part, n] = normed.astype(BF16)
+        for n in range(0, residues, 8):
+            normed, _ = standardised_columns(first_rows, second_rows, n, 8, residues)
+            high_ref[part, n : n + 8] = normed.astype(BF16).reshape(8, step, 2 * lanes)
         for p, piece_hbm in enumerate(pieces_hbm):
             source = high_ref.at[part, pl.ds(sources_ref[p] * own, own)]
             sends.append(
@@ -121,11 +123,10 @@
         out_specs=[hbm] * count,
         out_shape=[pltpu.HBM((residues // count, seqs, depth), BF16)] * count,
         scratch_shapes=[
-            pltpu.VMEM((seqs, residues, depth), F32),
             pltpu.VMEM((seqs, residues, half), F32),
             pltpu.VMEM((seqs, residues, half), F32),
             pltpu.VMEM((seqs // 16, residues, 16, depth), BF16),
-            pltpu.SemaphoreType.DMA((seqs // 16,)),
+            pltpu.SemaphoreType.DMA((seqs // 8,)),
             pltpu.SemaphoreType.DMA((seqs // 16 * count,)),
         ],
         compiler_params=params(10),
@@ -144,7 +145,9 @@
     for p in range(len(pieces_hbm)):
         spreads = jnp.zeros((seqs, 128), F32)
         for n in range(own):
-            normed, spread = standardised_column(first_rows, second_rows, p * own + n, residues)
+            normed, spread = standardised_columns(
+                first_rows, second_rows, p * own + n, 1, residues
+            )
             left = (normed - normed.astype(BF16).astype(F32)).astype(BF16)
             low_ref[p, n * seqs : (n + 1) * seqs, :] = left
             spreads = jnp.where(lane == n, spread, spreads)
@@ -383,14 +386,13 @@
 def pair_kernel(
     left_slots_ref,
     right_firsts_ref,
-    own_ref,
-    other_ref,
     *rest,
+    slots,
 ):
     weights_ref, entry_ref, switch_ref, couplings_hbm, mid_hbm, gate_hbm, sides_hbm = rest[-16:-9]
     outer_ref, spread_ref, sum_ref, rows_ref, couplings_ref = rest[-9:-4]
     mid_ref, gate_ref, sides_ref, copied = rest[-4:]
-    right_refs = rest[:-16]
+    left_refs, right_refs = rest[: 2 * slots], rest[2 * slots : -16]
     fetched = pltpu.make_async_copy(couplings_hbm, couplings_ref, copied.at[0])
     fetched.start()
     copies = []
@@ -400,7 +402,7 @@
         copies[-1].start()
 
     features = TENSOR_FEATURES
-    slots, piece_rows, total = own_ref.shape
+    piece_rows, total = left_refs[0].shape
     residues = piece_rows // features
     rows = 2 * slots * residues
     share = right_refs[0].shape[0]
@@ -409,8 +411,9 @@
     wide = share * features
     together = spread_ref.shape[1] // 64
 
-    for half, left_ref in enumerate((own_ref, other_ref)):
-        piece = left_ref[...].reshape(slots * piece_rows, total)
+    for half in range(2):
+        halves = left_refs[half * slots : (half + 1) * slots]
+        piece = jnp.concatenate([ref[...] for ref in halves], axis=0)
         target = slice(half * slots * piece_rows, (half + 1) * slots * piece_rows)
         for p, right_ref in enumerate(right_refs):
             right = right_ref[...].reshape(wide, total)
@@ -521,8 +524,8 @@
     vmem = pl.BlockSpec(memory_space=pltpu.VMEM)
     anywhere = pl.BlockSpec(memory_space=pl.ANY)
     return pl.pallas_call(
-        pair_kernel,
-        in_specs=[smem] * 2 + [vmem] * (5 + len(rights)) + [anywhere],
+        functools.partial(pair_kernel, slots=len(left) // 2),
+        in_specs=[smem] * 2 + [vmem] * (3 + len(left) + len(rights)) + [anywhere],
         out_specs=[anywhere] * 3,
         out_shape=[pltpu.HBM(whole.shape, F32)] * 2 + [pltpu.HBM(sides.shape, BF16)],
         scratch_shapes=[
@@ -683,25 +686,25 @@
                     moves.append((source, q * columns + 2 * ((r + shift) % rows) + side))
         source = block if shift < 2 else later
         arrived.append(lax.ppermute(source, ("row", "col"), moves))
-    return jnp.stack(arrived)
+    return arrived
 
 
 def both_cores(own):
     rows = lax.axis_size("row")
     core = lax.rem(lax.axis_index("col"), 2)
-    other = swap_cores(own)
-    residues = own.shape[1] // TENSOR_FEATURES
+    other = [swap_cores(piece) for piece in own]
+    residues = own[0].shape[0] // TENSOR_FEATURES
     if residues % 8 == 0:
-        return own, other
+        return own + other
     order = left_order(rows)
-    own, other = jnp.take(own, order, axis=0), jnp.take(other, order, axis=0)
+    own, other = [jnp.take(jnp.stack(side), order, axis=0) for side in (own, other)]
     joined = 8 // residues
     ordered = []
     for side in (jnp.where(core == 0, own, other), jnp.where(core == 0, other, own)):
         side = side.reshape(rows // joined, joined, TENSOR_FEATURES, residues, -1)
         side = jnp.transpose(side, (0, 2, 1, 3, 4))
-        ordered.append(side.reshape(rows // joined, joined * own.shape[1], -1))
-    return tuple(ordered)
+        ordered.extend(side.reshape(rows // joined, joined * own.shape[1], -1))
+    return ordered
 
 
 def left_order(rows):
@@ -773,7 +776,7 @@
     rights = exchange_rows([right_piece] * row_count)
     later, rights[1] = lax.optimization_barrier((left_piece, rights[1]))
     own = gather_turned(left_piece, later)
-    own, rights = lax.optimization_barrier((own, rights))
+    own[-1], rights = lax.optimization_barrier((own[-1], rights))
     mid, gate, sides = pair_update(
         slots,
         firsts,

time: 127 us -> 127 us (level)
    ppermute x4, starting transfers between devices: 12 us -> 9.52 us  [gather_turned(): arrived.append(lax.ppermute(source, ('row', 'col'), moves))]
    ppermute x4, waiting for transfers between devices: 2.87 us -> 4.87 us  [gather_turned(): arrived.append(lax.ppermute(source, ('row', 'col'), moves))]
    ppermute x12, waiting for transfers between devices: 26.2 us -> 24.8 us  [exchange_rows(): arrived.append(lax.ppermute(pieces[shift], 'row', moves))]
  transfers between devices with their start and end apart: 19 -> 22, of which waited for: 10 -> 9; matrix products, arithmetic and copies ran while one was open for 11% -> 11% of each run, Pallas kernels for 12% -> 12%
where the time goes in v14:
time: 127 us; the launch traced here: 126 us
  waiting for transfers between devices  39.2 us (31%)
  Pallas kernels  36 us (28%)
  starting transfers between devices  34.2 us (27%)
  local copies, waits for them, and re-layouts  9.15 us (7%)
  matrix products  3.41 us (3%)
  other arithmetic  3.29 us (3%)
    ppermute x12, waiting for transfers between devices, exchange_rows(): arrived.append(lax.ppermute(pieces[shift], 'row', moves))  24.8 us
    ppermute x12, starting transfers between devices, exchange_rows(): arrived.append(lax.ppermute(pieces[shift], 'row', moves))  15.2 us
    ppermute x4, starting transfers between devices, gather_turned(): arrived.append(lax.ppermute(source, ('row', 'col'), moves))  9.52 us
    pallas_call x1, Pallas kernels, pair_update(): pl.pallas_call(functools.partial(pair_kernel, slots=len(left) // 2), in_s...  8.67 us
    pallas_call x1, Pallas kernels, attention(): pl.pallas_call(attention_kernel, grid=(residues // step,), in_specs=[pl.B...  8.4 us
    all_to_all x1, waiting for transfers between devices, body(): product = lax.all_to_all(product, everywhere, split_axis=0, concat_axis=0)  7.64 us
    all_to_all x1, starting transfers between devices, body(): sides = lax.all_to_all(sides, everywhere, split_axis=0, concat_axis=0)  6.37 us
    ppermute x4, waiting for transfers between devices, gather_turned(): arrived.append(lax.ppermute(source, ('row', 'col'), moves))  4.87 us
  transfers between devices with their start and end apart: 22, of which 9 were waited for; matrix products, arithmetic and copies ran while one was open for 11% of the time, Pallas kernels for 12%

profile of v14, /device:TPU:0, one launch (start us, length us, event | category | flops | bytes accessed | tf_op | source)
XLA Modules:
  0.0 126.4 jit_solution(126606982691755252)
XLA Ops:
  0.6 0.0 copy-start.9
  0.7 0.0 copy-start.13
  0.7 4.5 %standardise_high.1 = (bf16[8,64,256]{2,1,0:T(8,128)(2,1)}, bf16[8,64,256]{2,1,0:T(8,128)(2,1)}, bf16[8,64,256]{2,1,0:T(8,128)(2,1)}, bf16[8,64,256]{2,1,0:T(8,128)(2,1)}) custom-call(s32[4]{0:T(128)S(1)} %iota_xor_fusion.sources_ref, f32[64,32,256]{2,1,0:T(8,128)} %second_ref.1), custom_call_target="tpu_custom_call" | custom-call | flops 3000000000 | bytes 3000000 | tf_op jit(solution)/shard_map/standardise_high/pallas_call | solution.py:120
  5.1 0.0 copy-start
  5.1 3.0 %collective-permute-start = (bf16[8,64,256]{2,1,0:T(8,128)(2,1)}, bf16[8,64,256]{2,1,0:T(8,128)(2,1)S(1)}, u32[]{:S(2)}, u32[]{:S(2)}) collective-permute-start(bf16[8,64,256]{2,1,0:T(8,128)(2,1)} %get-tuple-element.52), channel_id=1, source_target_pairs={{0,8},{8,0},{16,24},{24,16},{1,9},{9,1},{17,25},{25,17},{2,10},{10... | collective-permute-start | bytes 786440 | tf_op jit(solution)/shard_map/ppermute | solution.py:727
  8.2 1.5 %collective-permute-start.1 = (bf16[8,64,256]{2,1,0:T(8,128)(2,1)}, bf16[8,64,256]{2,1,0:T(8,128)(2,1)S(1)}, u32[]{:S(2)}, u32[]{:S(2)}) collective-permute-start(bf16[8,64,256]{2,1,0:T(8,128)(2,1)} %get-tuple-element.53), channel_id=1, source_target_pairs={{0,16},{8,24},{16,0},{24,8},{1,17},{9,25},{17,1},{25,9},{2,18},{10... | collective-permute-start | bytes 786440 | tf_op jit(solution)/shard_map/ppermute | solution.py:727
  9.7 0.0 collective-permute-start.2
  9.7 0.7 slice.7
  10.4 1.1 copy.17
  11.5 0.8 copy.12
  12.3 0.9 reshape.47
  13.2 0.1 copy.15
  13.4 1.0 copy.14
  14.4 0.1 pad_add_fusion.left_slots_ref
  14.5 0.9 pad_maximum_fusion.1.others_ref
  15.5 4.5 %standardise_low.1 = (bf16[528,256]{1,0:T(8,128)(2,1)}, bf16[528,256]{1,0:T(8,128)(2,1)}, bf16[528,256]{1,0:T(8,128)(2,1)}, bf16[528,256]{1,0:T(8,128)(2,1)}) custom-call(s32[4]{0:T(128)S(1)} %iota_xor_fusion.sources_ref, f32[64,32,256]{2,1,0:T(8,128)S(1)} %copy-done, f32[64,32,256]{2,1,0:T(8,128)S(1)} %copy-done), custom_call_target="tpu_custom_call" | custom-call | flops 4000000000 | bytes 4000000 | tf_op jit(solution)/shard_map/standardise_low/pallas_call | solution.py:174
  20.0 0.0 collective-permute-done.rest_1_
  20.0 1.7 %collective-permute-done.1.rest_2_ = bf16[8,64,256]{2,1,0:T(8,128)(2,1)S(1)} collective-permute-done((bf16[8,64,256]{2,1,0:T(8,128)(2,1)}, bf16[8,64,256]{2,1,0:T(8,128)(2,1)S(1)}, u32[]{:S(2)}, u32[]{:S(2)}) %collective-permute-start.1) | collective-permute-done | bytes 262176 | tf_op jit(solution)/shard_map/ppermute | solution.py:727
  21.7 0.0 collective-permute-done.2.rest_3_
  21.8 1.2 collective-permute-start.3
  23.0 0.9 collective-permute-start.4
  23.9 1.4 %collective-permute-start.5 = (bf16[528,256]{1,0:T(8,128)(2,1)}, bf16[528,256]{1,0:T(8,128)(2,1)S(1)}, u32[]{:S(2)}, u32[]{:S(2)}) collective-permute-start(bf16[528,256]{1,0:T(8,128)(2,1)} %get-tuple-element.76), channel_id=1, source_target_pairs={{0,24},{8,16},{16,8},{24,0},{1,25},{9,17},{17,9},{25,1},{2,26},{10... | collective-permute-start | bytes 811016 | tf_op jit(solution)/shard_map/ppermute | solution.py:727
  25.3 8.4 %attention.1.turned_ref = bf16[8,256,256]{2,1,0:T(8,128)(2,1)S(1)} custom-call(bf16[256,256]{1,0:T(8,128)(2,1)S(1)} %slice.6.key_ref, bf16[768,256]{1,0:T(8,128)(2,1)S(1)} %pad_maximum_fusion.1.others_ref, bf16[8,64,256]{2,1,0:T(8,128)(2,1)S(1)} %copy-done.6, bf16[8,64,256]{2,1,0:T(8,128)(2,1)S(1)} %collective-permute-done.rest_1_, ...), custom_call_target="tpu_custom_call" | custom-call | flops 10000000000 | bytes 10000000 | tf_op jit(solution)/shard_map/attention/pallas_call | solution.py:257
  33.7 0.0 collective-permute-done.3.rest_5_.rest_9_
  33.7 2.3 %collective-permute-done.4.rest_6_.rest_10_ = bf16[528,256]{1,0:T(8,128)(2,1)S(1)} collective-permute-done((bf16[528,256]{1,0:T(8,128)(2,1)}, bf16[528,256]{1,0:T(8,128)(2,1)S(1)}, u32[]{:S(2)}, u32[]{:S(2)}) %collective-permute-start.4) | collective-permute-done | bytes 270368 | tf_op jit(solution)/shard_map/ppermute | solution.py:727
  36.1 3.8 %alignment.1 = (bf16[256,256]{1,0:T(8,128)(2,1)S(1)}, bf16[8,32,256]{2,1,0:T(8,128)(2,1)S(1)}) custom-call(s32[4]{0:T(128)S(1)} %iota_xor_fusion.sources_ref, bf16[8,256,256]{2,1,0:T(8,128)(2,1)S(1)} %attention.1.turned_ref, bf16[256,256]{1,0:T(8,128)(2,1)S(1)} %bitcast.28, bf16[64,256]{1,0:T(8,128)(2,1)S(1)} %bitcast.30, bf16[8,64,256]{2,1,0:T(8,128)(2,1)S(1)} %copy-done.6, ...), custom_call_target="tpu_custom_call" | custom-call | flops 4000000000 | bytes 4000000 | tf_op jit(solution)/shard_map/alignment/pallas_call | solution.py:359
  39.9 0.6 collective-permute-start.8
  40.5 1.2 collective-permute-start.11
  41.7 1.8 %collective-permute-start.12 = (bf16[8,32,256]{2,1,0:T(8,128)(2,1)S(1)}, bf16[8,32,256]{2,1,0:T(8,128)(2,1)S(1)}, u32[]{:S(2)}, u32[]{:S(2)}) collective-permute-start(bf16[8,32,256]{2,1,0:T(8,128)(2,1)S(1)} %get-tuple-element.82.rest_8_), channel_id=1, source_target_pairs={{0,24},{8,16},{16,8},{24,0},{1,25},{9,17},{17,9},{25,1},{2,26},{10... | collective-permute-start | bytes 393224 | tf_op jit(solution)/shard_map/ppermute | solution.py:727
  43.4 0.8 collective-permute-start.6
  44.2 3.3 %collective-permute-start.7 = (bf16[256,256]{1,0:T(8,128)(2,1)S(1)}, bf16[256,256]{1,0:T(8,128)(2,1)S(1)}, u32[]{:S(2)}, u32[]{:S(2)}) collective-permute-start(bf16[256,256]{1,0:T(8,128)(2,1)S(1)} %get-tuple-element.79), channel_id=1, source_target_pairs={{0,2},{1,3},{2,10},{3,11},{4,18},{5,19},{6,26},{7,27},{8,4},{9,5},... | collective-permute-start | bytes 393224 | tf_op jit(solution)/shard_map/ppermute | solution.py:688
  47.6 5.4 %collective-permute-start.10 = (bf16[256,256]{1,0:T(8,128)(2,1)S(1)}, bf16[256,256]{1,0:T(8,128)(2,1)S(1)}, u32[]{:S(2)}, u32[]{:S(2)}) collective-permute-start(bf16[256,256]{1,0:T(8,128)(2,1)S(1)} %get-tuple-element.79), channel_id=1, source_target_pairs={{0,6},{1,7},{2,14},{3,15},{4,22},{5,23},{6,30},{7,31},{8,0},{9,1},... | collective-permute-start | bytes 393224 | tf_op jit(solution)/shard_map/ppermute | solution.py:688
  53.0 0.0 collective-permute-start.9
  53.0 0.1 collective-permute-start.13
  53.1 1.4 %collective-permute-done.7.rest_1_ = bf16[256,256]{1,0:T(8,128)(2,1)S(1)} collective-permute-done((bf16[256,256]{1,0:T(8,128)(2,1)S(1)}, bf16[256,256]{1,0:T(8,128)(2,1)S(1)}, u32[]{:S(2)}, u32[]{:S(2)}) %collective-permute-start.7) | collective-permute-done | bytes 131104 | tf_op jit(solution)/shard_map/ppermute | solution.py:688
  54.4 0.0 collective-permute-start.14
  54.4 1.1 collective-permute-done.10.rest_3_
  55.5 0.0 collective-permute-start.16
  55.5 2.4 %collective-permute-done.9.rest_2_ = bf16[256,256]{1,0:T(8,128)(2,1)S(1)} collective-permute-done((bf16[256,256]{1,0:T(8,128)(2,1)S(1)}, bf16[256,256]{1,0:T(8,128)(2,1)S(1)}, u32[]{:S(2)}, u32[]{:S(2)}) %collective-permute-start.9) | collective-permute-done | bytes 131104 | tf_op jit(solution)/shard_map/ppermute | solution.py:688
  57.9 0.0 collective-permute-start.15
  57.9 1.7 %turn_back.1 = (bf16[8,64,256]{2,1,0:T(8,128)(2,1)}, bf16[8,64,256]{2,1,0:T(8,128)(2,1)}, bf16[8,64,256]{2,1,0:T(8,128)(2,1)}, bf16[8,64,256]{2,1,0:T(8,128)(2,1)}) custom-call(bf16[8,256,256]{2,1,0:T(8,128)(2,1)S(1)} %attention.1.turned_ref), custom_call_target="tpu_custom_call" | custom-call | flops 2000000000 | bytes 2000000 | tf_op jit(solution)/shard_map/turn_back/pallas_call | solution.py:288
  59.7 0.0 collective-permute-done.13.rest_4_
  59.7 0.0 collective-permute-done.16.rest_7_
  59.7 8.7 %pair_update.1 = (f32[32,64,128]{2,1,0:T(8,128)}, f32[32,64,128]{2,1,0:T(8,128)}, bf16[128,32,128]{2,1,0:T(8,128)(2,1)}) custom-call(s32[8]{0:T(128)S(1)} %pad_add_fusion.left_slots_ref, s32[4]{0:T(128)S(1)} %broadcast_multiply_fusion.right_firsts_ref, bf16[256,256]{1,0:T(8,128)(2,1)S(1)} %collective-permute-done.6.rest_0_, ...), custom_call_target="tpu_custom_call" | custom-call | flops 12000000000 | bytes 12000000 | tf_op jit(solution)/shard_map/pair_update/pallas_call | solution.py:526
  68.4 6.4 %all-to-all-start = ((bf16[32,4,32,128]{3,2,1,0:T(8,128)(2,1)}), bf16[32,4,32,128]{3,2,1,0:T(8,128)(2,1)S(1)}, u32[]{:S(2)}, u32[]{:S(2)}) async-start(bf16[32,4,32,128]{3,2,1,0:T(8,128)(2,1)} %bitcast.33), calls=%async_computation | async-start | bytes 2097152 | tf_op jit(solution)/shard_map/all_to_all | solution.py:797
  74.8 0.0 copy-start.10
  74.8 1.8 %collective-permute-start.17 = (bf16[8,64,256]{2,1,0:T(8,128)(2,1)}, bf16[8,64,256]{2,1,0:T(8,128)(2,1)S(1)}, u32[]{:S(2)}, u32[]{:S(2)}) collective-permute-start(bf16[8,64,256]{2,1,0:T(8,128)(2,1)} %get-tuple-element.89), channel_id=1, source_target_pairs={{0,8},{8,0},{16,24},{24,16},{1,9},{9,1},{17,25},{25,17},{2,10},{10... | collective-permute-start | bytes 786440 | tf_op jit(solution)/shard_map/ppermute | solution.py:727
  76.6 1.5 %collective-permute-start.18 = (bf16[8,64,256]{2,1,0:T(8,128)(2,1)}, bf16[8,64,256]{2,1,0:T(8,128)(2,1)S(1)}, u32[]{:S(2)}, u32[]{:S(2)}) collective-permute-start(bf16[8,64,256]{2,1,0:T(8,128)(2,1)} %get-tuple-element.90), channel_id=1, source_target_pairs={{0,16},{8,24},{16,0},{24,8},{1,17},{9,25},{17,1},{25,9},{2,18},{10... | collective-permute-start | bytes 786440 | tf_op jit(solution)/shard_map/ppermute | solution.py:727
  78.1 0.3 collective-permute-start.19
  78.3 13.7 %collective-permute-done.17 = bf16[8,64,256]{2,1,0:T(8,128)(2,1)S(1)} collective-permute-done((bf16[8,64,256]{2,1,0:T(8,128)(2,1)}, bf16[8,64,256]{2,1,0:T(8,128)(2,1)S(1)}, u32[]{:S(2)}, u32[]{:S(2)}) %collective-permute-start.17) | collective-permute-done | bytes 262176 | tf_op jit(solution)/shard_map/ppermute | solution.py:727
  92.1 0.7 copy-done.11
  92.8 0.7 copy-done.12
  93.5 6.9 %collective-permute-done.19 = bf16[8,64,256]{2,1,0:T(8,128)(2,1)} collective-permute-done((bf16[8,64,256]{2,1,0:T(8,128)(2,1)}, bf16[8,64,256]{2,1,0:T(8,128)(2,1)}, u32[]{:S(2)}, u32[]{:S(2)}) %collective-permute-start.19) | collective-permute-done | bytes 262176 | tf_op jit(solution)/shard_map/ppermute | solution.py:727
  100.4 1.9 %all-to-all-done.sides_ref = bf16[32,4,32,128]{3,2,1,0:T(8,128)(2,1)S(1)} async-done(((bf16[32,4,32,128]{3,2,1,0:T(8,128)(2,1)}), bf16[32,4,32,128]{3,2,1,0:T(8,128)(2,1)S(1)}, u32[]{:S(2)}, u32[]{:S(2)}) %all-to-all-start) | async-done | bytes 1048608 | tf_op jit(solution)/shard_map/all_to_all | solution.py:797
  102.4 1.7 %triangle_product.1 = bf16[32,4,16,128]{3,2,1,0:T(8,128)(2,1)} custom-call(bf16[32,4,32,128]{3,2,1,0:T(8,128)(2,1)S(1)} %all-to-all-done.sides_ref), custom_call_target="tpu_custom_call" | custom-call | flops 3000000000 | bytes 3000000 | tf_op jit(solution)/shard_map/triangle_product/pallas_call | solution.py:590
  104.0 3.0 %all-to-all-start.1 = ((bf16[32,4,16,128]{3,2,1,0:T(8,128)(2,1)}), bf16[32,4,16,128]{3,2,1,0:T(8,128)(2,1)S(1)}, u32[]{:S(2)}, u32[]{:S(2)}) async-start(bf16[32,4,16,128]{3,2,1,0:T(8,128)(2,1)} %triangle_product.1), calls=%async_computation.1 | async-start | bytes 1048576 | tf_op jit(solution)/shard_map/all_to_all | solution.py:800
  107.1 0.1 broadcast_in_dim.14
  107.1 0.1 broadcast_in_dim.15
  107.2 0.0 copy-start.8
  107.3 2.2 %pad_maximum_fusion = bf16[4,8,64,256]{3,2,1,0:T(8,128)(2,1)} fusion(bf16[1,8,64,256]{3,2,1,0:T(8,128)(2,1)} %bitcast.10, bf16[1,8,64,256]{3,2,1,0:T(8,128)(2,1)} %bitcast.38, bf16[1,8,64,256]{3,2,1,0:T(8,128)(2,1)} %bitcast.37, bf16[1,8,64,256]{3,2,1,0:T(8,128)(2,1)S(1)} %bitcast.36), kind=kLoop, calls=%fused_computation.2 | loop fusion | flops 1572864 | bytes 2097152 | tf_op jit(solution)/shard_map/stack | solution.py:802
  109.5 2.8 %gather_fusion = bf16[4,8,64,256]{3,2,1,0:T(8,128)(2,1)} fusion(bf16[4,8,64,256]{3,2,1,0:T(8,128)(2,1)} %pad_maximum_fusion, s32[1024]{0:T(1024)S(1)} %pad_clamp_fusion), kind=kCustom, calls=%fused_computation | custom fusion | bytes 2097168 | tf_op jit(solution)/shard_map/jit(_take)/gather | solution.py:802
  112.3 3.4 %convolution_add_fusion = f32[64,32,256]{2,1,0:T(8,128)} fusion(f32[64,32,256]{2,1,0:T(8,128)S(1)} %copy-done, bf16[32,64,256]{2,1,0:T(8,128)(2,1)} %bitcast.31, pred[32]{0:T(512)(128)(4,1)S(1)} %broadcast_in_dim.15, bf16[256,256]{1,0:T(8,128)(2,1)S(1)} %copy-done.8), kind=kOutput, calls=%fused_computation.1 | convolution fusion | flops 269484032 | bytes 5373984 | tf_op jit(solution)/shard_map/dot_general | solution.py:804
  115.8 7.6 %all-to-all-done.1 = bf16[32,4,16,128]{3,2,1,0:T(8,128)(2,1)S(1)} async-done(((bf16[32,4,16,128]{3,2,1,0:T(8,128)(2,1)}), bf16[32,4,16,128]{3,2,1,0:T(8,128)(2,1)S(1)}, u32[]{:S(2)}, u32[]{:S(2)}) %all-to-all-start.1) | async-done | bytes 524320 | tf_op jit(solution)/shard_map/all_to_all | solution.py:800
  123.4 2.8 %pair_result.1 = f32[64,32,128]{2,1,0:T(8,128)} custom-call(bf16[128,16,128]{2,1,0:T(8,128)(2,1)S(1)} %bitcast.26, bf16[128,128]{1,0:T(8,128)(2,1)S(1)} %copy-done.5, f32[32,64,128]{2,1,0:T(8,128)} %get-tuple-element.98.mid_hbm, f32[32,64,128]{2,1,0:T(8,128)} %get-tuple-element.99.gate_hbm), custom_call_target="tpu_custom_call" | custom-call | flops 3000000000 | bytes 3000000 | tf_op jit(solution)/shard_map/pair_result/pallas_call | solution.py:648
  (37 shorter events, 0.1 us)
Async XLA Ops:
  0.6 9.1 %copy-start.9 = (bf16[256,768]{1,0:T(8,128)(2,1)S(1)}, bf16[256,768]{1,0:T(8,128)(2,1)}, u32[]{:S(2)}) copy-start(bf16[256,768]{1,0:T(8,128)(2,1)} %param.13) | copy-start | bytes 1179652
  0.7 10.9 %copy-start.13 = (bf16[256,256]{1,0:T(8,128)(2,1)S(1)}, bf16[256,256]{1,0:T(8,128)(2,1)}, u32[]{:S(2)}) copy-start(bf16[256,256]{1,0:T(8,128)(2,1)} %param.12) | copy-start | bytes 393220
  5.1 10.3 %copy-start = (f32[64,32,256]{2,1,0:T(8,128)S(1)}, f32[64,32,256]{2,1,0:T(8,128)}, u32[]{:S(2)}) copy-start(f32[64,32,256]{2,1,0:T(8,128)} %second_ref.1) | copy-start | bytes 6291460
  5.1 14.8 %collective-permute-start = (bf16[8,64,256]{2,1,0:T(8,128)(2,1)}, bf16[8,64,256]{2,1,0:T(8,128)(2,1)S(1)}, u32[]{:S(2)}, u32[]{:S(2)}) collective-permute-start(bf16[8,64,256]{2,1,0:T(8,128)(2,1)} %get-tuple-element.52), channel_id=1, source_target_pairs={{0,8},{8,0},{16,24},{24,16},{1,9},{9,1},{17,25},{25,17},{2,10},{10... | collective-permute-start | bytes 786440 | tf_op jit(solution)/shard_map/ppermute | solution.py:727
  8.2 13.6 %collective-permute-start.1 = (bf16[8,64,256]{2,1,0:T(8,128)(2,1)}, bf16[8,64,256]{2,1,0:T(8,128)(2,1)S(1)}, u32[]{:S(2)}, u32[]{:S(2)}) collective-permute-start(bf16[8,64,256]{2,1,0:T(8,128)(2,1)} %get-tuple-element.53), channel_id=1, source_target_pairs={{0,16},{8,24},{16,0},{24,8},{1,17},{9,25},{17,1},{25,9},{2,18},{10... | collective-permute-start | bytes 786440 | tf_op jit(solution)/shard_map/ppermute | solution.py:727
  9.7 12.1 %collective-permute-start.2 = (bf16[8,64,256]{2,1,0:T(8,128)(2,1)}, bf16[8,64,256]{2,1,0:T(8,128)(2,1)S(1)}, u32[]{:S(2)}, u32[]{:S(2)}) collective-permute-start(bf16[8,64,256]{2,1,0:T(8,128)(2,1)} %get-tuple-element.54), channel_id=1, source_target_pairs={{0,24},{8,16},{16,8},{24,0},{1,25},{9,17},{17,9},{25,1},{2,26},{10... | collective-permute-start | bytes 786440 | tf_op jit(solution)/shard_map/ppermute | solution.py:727
  15.5 9.8 %copy-start.6 = (bf16[8,64,256]{2,1,0:T(8,128)(2,1)S(1)}, bf16[8,64,256]{2,1,0:T(8,128)(2,1)}, u32[]{:S(2)}) copy-start(bf16[8,64,256]{2,1,0:T(8,128)(2,1)} %get-tuple-element.61.rest_0_) | copy-start | bytes 786436
  21.7 14.3 %copy-start.3 = (bf16[256,64]{0,1:T(8,128)(2,1)S(1)}, bf16[256,64]{0,1:T(8,128)(2,1)}, u32[]{:S(2)}) copy-start(bf16[256,64]{0,1:T(8,128)(2,1)} %param.15) | copy-start | bytes 98308
  21.8 14.3 %copy-start.7 = (bf16[528,256]{1,0:T(8,128)(2,1)S(1)}, bf16[528,256]{1,0:T(8,128)(2,1)}, u32[]{:S(2)}) copy-start(bf16[528,256]{1,0:T(8,128)(2,1)} %get-tuple-element.73.rest_4_.rest_8_) | copy-start | bytes 811012
  21.8 12.0 %collective-permute-start.3 = (bf16[528,256]{1,0:T(8,128)(2,1)}, bf16[528,256]{1,0:T(8,128)(2,1)S(1)}, u32[]{:S(2)}, u32[]{:S(2)}) collective-permute-start(bf16[528,256]{1,0:T(8,128)(2,1)} %get-tuple-element.74), channel_id=1, source_target_pairs={{0,8},{8,0},{16,24},{24,16},{1,9},{9,1},{17,25},{25,17},{2,10},{10... | collective-permute-start | bytes 811016 | tf_op jit(solution)/shard_map/ppermute | solution.py:727
  23.0 13.1 %collective-permute-start.4 = (bf16[528,256]{1,0:T(8,128)(2,1)}, bf16[528,256]{1,0:T(8,128)(2,1)S(1)}, u32[]{:S(2)}, u32[]{:S(2)}) collective-permute-start(bf16[528,256]{1,0:T(8,128)(2,1)} %get-tuple-element.75), channel_id=1, source_target_pairs={{0,16},{8,24},{16,0},{24,8},{1,17},{9,25},{17,1},{25,9},{2,18},{10... | collective-permute-start | bytes 811016 | tf_op jit(solution)/shard_map/ppermute | solution.py:727
  23.9 12.2 %collective-permute-start.5 = (bf16[528,256]{1,0:T(8,128)(2,1)}, bf16[528,256]{1,0:T(8,128)(2,1)S(1)}, u32[]{:S(2)}, u32[]{:S(2)}) collective-permute-start(bf16[528,256]{1,0:T(8,128)(2,1)} %get-tuple-element.76), channel_id=1, source_target_pairs={{0,24},{8,16},{16,8},{24,0},{1,25},{9,17},{17,9},{25,1},{2,26},{10... | collective-permute-start | bytes 811016 | tf_op jit(solution)/shard_map/ppermute | solution.py:727
  39.9 7.7 %collective-permute-start.8 = (bf16[8,32,256]{2,1,0:T(8,128)(2,1)S(1)}, bf16[8,32,256]{2,1,0:T(8,128)(2,1)S(1)}, u32[]{:S(2)}, u32[]{:S(2)}) collective-permute-start(bf16[8,32,256]{2,1,0:T(8,128)(2,1)S(1)} %get-tuple-element.82.rest_8_), channel_id=1, source_target_pairs={{0,8},{8,0},{16,24},{24,16},{1,9},{9,1},{17,25},{25,17},{2,10},{10... | collective-permute-start | bytes 393224 | tf_op jit(solution)/shard_map/ppermute | solution.py:727
  40.5 12.5 %collective-permute-start.11 = (bf16[8,32,256]{2,1,0:T(8,128)(2,1)S(1)}, bf16[8,32,256]{2,1,0:T(8,128)(2,1)S(1)}, u32[]{:S(2)}, u32[]{:S(2)}) collective-permute-start(bf16[8,32,256]{2,1,0:T(8,128)(2,1)S(1)} %get-tuple-element.82.rest_8_), channel_id=1, source_target_pairs={{0,16},{8,24},{16,0},{24,8},{1,17},{9,25},{17,1},{25,9},{2,18},{10... | collective-permute-start | bytes 393224 | tf_op jit(solution)/shard_map/ppermute | solution.py:727
  41.7 12.8 %collective-permute-start.12 = (bf16[8,32,256]{2,1,0:T(8,128)(2,1)S(1)}, bf16[8,32,256]{2,1,0:T(8,128)(2,1)S(1)}, u32[]{:S(2)}, u32[]{:S(2)}) collective-permute-start(bf16[8,32,256]{2,1,0:T(8,128)(2,1)S(1)} %get-tuple-element.82.rest_8_), channel_id=1, source_target_pairs={{0,24},{8,16},{16,8},{24,0},{1,25},{9,17},{17,9},{25,1},{2,26},{10... | collective-permute-start | bytes 393224 | tf_op jit(solution)/shard_map/ppermute | solution.py:727
  43.4 16.3 %copy-start.1 = (f32[64,32,128]{2,1,0:T(8,128)S(1)}, f32[64,32,128]{2,1,0:T(8,128)}, u32[]{:S(2)}) copy-start(f32[64,32,128]{2,1,0:T(8,128)} %param.11) | copy-start | bytes 3145732
  43.4 16.3 %copy-start.2 = (bf16[1024,128]{1,0:T(8,128)(2,1)S(1)}, bf16[1024,128]{1,0:T(8,128)(2,1)}, u32[]{:S(2)}) copy-start(bf16[1024,128]{1,0:T(8,128)(2,1)} %rest_12_.1) | copy-start | bytes 786436
  43.4 16.3 %copy-start.4 = (bf16[128,128]{1,0:T(8,128)(2,1)S(1)}, bf16[128,128]{1,0:T(8,128)(2,1)}, u32[]{:S(2)}) copy-start(bf16[128,128]{1,0:T(8,128)(2,1)} %rest_14_.1) | copy-start | bytes 98308
  43.4 9.5 %collective-permute-start.6 = (bf16[256,256]{1,0:T(8,128)(2,1)S(1)}, bf16[256,256]{1,0:T(8,128)(2,1)S(1)}, u32[]{:S(2)}, u32[]{:S(2)}) collective-permute-start(bf16[256,256]{1,0:T(8,128)(2,1)S(1)} %get-tuple-element.79), channel_id=1, source_target_pairs={{0,0},{1,1},{2,8},{3,9},{4,16},{5,17},{6,24},{7,25},{8,2},{9,3},{1... | collective-permute-start | bytes 393224 | tf_op jit(solution)/shard_map/ppermute | solution.py:688
  44.2 10.2 %collective-permute-start.7 = (bf16[256,256]{1,0:T(8,128)(2,1)S(1)}, bf16[256,256]{1,0:T(8,128)(2,1)S(1)}, u32[]{:S(2)}, u32[]{:S(2)}) collective-permute-start(bf16[256,256]{1,0:T(8,128)(2,1)S(1)} %get-tuple-element.79), channel_id=1, source_target_pairs={{0,2},{1,3},{2,10},{3,11},{4,18},{5,19},{6,26},{7,27},{8,4},{9,5},... | collective-permute-start | bytes 393224 | tf_op jit(solution)/shard_map/ppermute | solution.py:688
  47.6 7.9 %collective-permute-start.10 = (bf16[256,256]{1,0:T(8,128)(2,1)S(1)}, bf16[256,256]{1,0:T(8,128)(2,1)S(1)}, u32[]{:S(2)}, u32[]{:S(2)}) collective-permute-start(bf16[256,256]{1,0:T(8,128)(2,1)S(1)} %get-tuple-element.79), channel_id=1, source_target_pairs={{0,6},{1,7},{2,14},{3,15},{4,22},{5,23},{6,30},{7,31},{8,0},{9,1},... | collective-permute-start | bytes 393224 | tf_op jit(solution)/shard_map/ppermute | solution.py:688
  53.0 5.0 %collective-permute-start.9 = (bf16[256,256]{1,0:T(8,128)(2,1)S(1)}, bf16[256,256]{1,0:T(8,128)(2,1)S(1)}, u32[]{:S(2)}, u32[]{:S(2)}) collective-permute-start(bf16[256,256]{1,0:T(8,128)(2,1)S(1)} %get-tuple-element.79), channel_id=1, source_target_pairs={{0,4},{1,5},{2,12},{3,13},{4,20},{5,21},{6,28},{7,29},{8,6},{9,7},... | collective-permute-start | bytes 393224 | tf_op jit(solution)/shard_map/ppermute | solution.py:688
  53.0 6.7 %collective-permute-start.13 = (bf16[256,256]{1,0:T(8,128)(2,1)S(1)}, bf16[256,256]{1,0:T(8,128)(2,1)S(1)}, u32[]{:S(2)}, u32[]{:S(2)}) collective-permute-start(bf16[256,256]{1,0:T(8,128)(2,1)S(1)} %collective-permute-done.6.rest_0_), channel_id=1, source_target_pairs={{0,1},{1,0},{2,3},{3,2},{4,5},{5,4},{6,7},{7,6},{8,9},{9,8},{10,11... | collective-permute-start | bytes 393224 | tf_op jit(solution)/shard_map/ppermute | solution.py:674
  54.4 5.2 %collective-permute-start.14 = (bf16[256,256]{1,0:T(8,128)(2,1)S(1)}, bf16[256,256]{1,0:T(8,128)(2,1)S(1)}, u32[]{:S(2)}, u32[]{:S(2)}) collective-permute-start(bf16[256,256]{1,0:T(8,128)(2,1)S(1)} %collective-permute-done.7.rest_1_), channel_id=1, source_target_pairs={{0,1},{1,0},{2,3},{3,2},{4,5},{5,4},{6,7},{7,6},{8,9},{9,8},{10,11... | collective-permute-start | bytes 393224 | tf_op jit(solution)/shard_map/ppermute | solution.py:674
  55.5 4.2 %collective-permute-start.16 = (bf16[256,256]{1,0:T(8,128)(2,1)S(1)}, bf16[256,256]{1,0:T(8,128)(2,1)S(1)}, u32[]{:S(2)}, u32[]{:S(2)}) collective-permute-start(bf16[256,256]{1,0:T(8,128)(2,1)S(1)} %collective-permute-done.10.rest_3_), channel_id=1, source_target_pairs={{0,1},{1,0},{2,3},{3,2},{4,5},{5,4},{6,7},{7,6},{8,9},{9,8},{10,11... | collective-permute-start | bytes 393224 | tf_op jit(solution)/shard_map/ppermute | solution.py:674
  57.9 1.7 %collective-permute-start.15 = (bf16[256,256]{1,0:T(8,128)(2,1)S(1)}, bf16[256,256]{1,0:T(8,128)(2,1)S(1)}, u32[]{:S(2)}, u32[]{:S(2)}) collective-permute-start(bf16[256,256]{1,0:T(8,128)(2,1)S(1)} %collective-permute-done.9.rest_2_), channel_id=1, source_target_pairs={{0,1},{1,0},{2,3},{3,2},{4,5},{5,4},{6,7},{7,6},{8,9},{9,8},{10,11... | collective-permute-start | bytes 393224 | tf_op jit(solution)/shard_map/ppermute | solution.py:674
  68.4 34.0 %all-to-all-start = ((bf16[32,4,32,128]{3,2,1,0:T(8,128)(2,1)}), bf16[32,4,32,128]{3,2,1,0:T(8,128)(2,1)S(1)}, u32[]{:S(2)}, u32[]{:S(2)}) async-start(bf16[32,4,32,128]{3,2,1,0:T(8,128)(2,1)} %bitcast.33), calls=%async_computation | async-start | bytes 2097152 | tf_op jit(solution)/shard_map/all_to_all | solution.py:797
  74.8 32.5 %copy-start.10 = (bf16[8,64,256]{2,1,0:T(8,128)(2,1)S(1)}, bf16[8,64,256]{2,1,0:T(8,128)(2,1)}, u32[]{:S(2)}) copy-start(bf16[8,64,256]{2,1,0:T(8,128)(2,1)} %get-tuple-element.93) | copy-start | bytes 786436
  74.8 17.3 %collective-permute-start.17 = (bf16[8,64,256]{2,1,0:T(8,128)(2,1)}, bf16[8,64,256]{2,1,0:T(8,128)(2,1)S(1)}, u32[]{:S(2)}, u32[]{:S(2)}) collective-permute-start(bf16[8,64,256]{2,1,0:T(8,128)(2,1)} %get-tuple-element.89), channel_id=1, source_target_pairs={{0,8},{8,0},{16,24},{24,16},{1,9},{9,1},{17,25},{25,17},{2,10},{10... | collective-permute-start | bytes 786440 | tf_op jit(solution)/shard_map/ppermute | solution.py:727
  76.6 15.4 %collective-permute-start.18 = (bf16[8,64,256]{2,1,0:T(8,128)(2,1)}, bf16[8,64,256]{2,1,0:T(8,128)(2,1)S(1)}, u32[]{:S(2)}, u32[]{:S(2)}) collective-permute-start(bf16[8,64,256]{2,1,0:T(8,128)(2,1)} %get-tuple-element.90), channel_id=1, source_target_pairs={{0,16},{8,24},{16,0},{24,8},{1,17},{9,25},{17,1},{25,9},{2,18},{10... | collective-permute-start | bytes 786440 | tf_op jit(solution)/shard_map/ppermute | solution.py:727
  78.1 22.4 %collective-permute-start.19 = (bf16[8,64,256]{2,1,0:T(8,128)(2,1)}, bf16[8,64,256]{2,1,0:T(8,128)(2,1)}, u32[]{:S(2)}, u32[]{:S(2)}) collective-permute-start(bf16[8,64,256]{2,1,0:T(8,128)(2,1)} %get-tuple-element.91), channel_id=1, source_target_pairs={{0,24},{8,16},{16,8},{24,0},{1,25},{9,17},{17,9},{25,1},{2,26},{10... | collective-permute-start | bytes 786440 | tf_op jit(solution)/shard_map/ppermute | solution.py:727
  92.0 0.7 copy-start.11
  92.8 0.7 copy-start.12
  104.0 19.4 %all-to-all-start.1 = ((bf16[32,4,16,128]{3,2,1,0:T(8,128)(2,1)}), bf16[32,4,16,128]{3,2,1,0:T(8,128)(2,1)S(1)}, u32[]{:S(2)}, u32[]{:S(2)}) async-start(bf16[32,4,16,128]{3,2,1,0:T(8,128)(2,1)} %triangle_product.1), calls=%async_computation.1 | async-start | bytes 1048576 | tf_op jit(solution)/shard_map/all_to_all | solution.py:800
  107.2 5.1 %copy-start.8 = (bf16[256,256]{1,0:T(8,128)(2,1)S(1)}, bf16[256,256]{1,0:T(8,128)(2,1)}, u32[]{:S(2)}) copy-start(bf16[256,256]{1,0:T(8,128)(2,1)} %param.14) | copy-start | bytes 393220
  112.3 11.1 %copy-start.5 = (bf16[128,128]{1,0:T(8,128)(2,1)S(1)}, bf16[128,128]{1,0:T(8,128)(2,1)}, u32[]{:S(2)}) copy-start(bf16[128,128]{1,0:T(8,128)(2,1)} %final_ref.1) | copy-start | bytes 98308

commit v15 on v14

--- a/solution.py
+++ b/solution.py
@@ -69,8 +69,8 @@
 def standardised_columns(first_rows, second_rows, first, count, residues):
     seqs = first_rows.shape[0] // residues
     columns = []
-    for n in range(first, first + count):
-        rows = pl.ds(n, seqs, stride=residues)
+    for n in range(count):
+        rows = pl.ds(first + n, seqs, stride=residues)
         columns.append(jnp.concatenate([first_rows[rows, :], second_rows[rows, :]], axis=1))
     column = jnp.concatenate(columns, axis=0)
     centred = column - jnp.mean(column, axis=1, keepdims=True)
@@ -79,60 +79,62 @@
     return centred * scale, variance * scale
 
 
-def high_kernel(sources_ref, block_hbm, *rest):
-    *pieces_hbm, first_ref, second_ref, high_ref, fetched, sent = rest
+def high_kernel(sources_ref, first_ref, second_ref, *rest):
+    *pieces_hbm, high_ref, sent = rest
     seqs, residues, lanes = first_ref.shape
-    own = residues // len(pieces_hbm)
-    step = 16
-    fetches, sends = [], []
-    for s in range(0, seqs, step):
-        chosen = pl.ds(s, step)
-        for half, ref in enumerate((first_ref, second_ref)):
-            source = block_hbm.at[chosen, :, pl.ds(half * lanes, lanes)]
-            fetches.append(
-                pltpu.make_async_copy(source, ref.at[chosen], fetched.at[len(fetches)])
-            )
-            fetches[-1].start()
-    for part in range(seqs // step):
-        chosen = pl.ds(part * step, step)
-        fetches[2 * part].wait()
-        fetches[2 * part + 1].wait()
-        first_rows = first_ref.at[chosen].reshape(step * residues, lanes)
-        second_rows = second_ref.at[chosen].reshape(step * residues, lanes)
-        for n in range(0, residues, 8):
-            normed, _ = standardised_columns(first_rows, second_rows, n, 8, residues)
-            high_ref[part, n : n + 8] = normed.astype(BF16).reshape(8, step, 2 * lanes)
-        for p, piece_hbm in enumerate(pieces_hbm):
-            source = high_ref.at[part, pl.ds(sources_ref[p] * own, own)]
-            sends.append(
-                pltpu.make_async_copy(source, piece_hbm.at[:, chosen], sent.at[len(sends)])
-            )
-            sends[-1].start()
-    for send in sends:
-        send.wait()
+    count = len(pieces_hbm)
+    own = high_ref.shape[1]
+    step = pl.program_id(0)
+    first_rows = first_ref.reshape(seqs * residues, lanes)
+    second_rows = second_ref.reshape(seqs * residues, lanes)
+    shift = lax.rem(sources_ref[step] * own, residues) if own < residues else 0
+    for n in range(own):
+        normed, _ = standardised_columns(first_rows, second_rows, shift + n, 1, residues)
+        high_ref[step, n] = normed.astype(BF16)
+    copies = [
+        pltpu.make_async_copy(high_ref.at[p], piece_hbm, sent.at[p])
+        for p, piece_hbm in enumerate(pieces_hbm)
+    ]
+    for p in range(count):
+
+        @pl.when(step == p)
+        def _(p=p):
+            copies[p].start()
+
+    @pl.when(step == count - 1)
+    def _():
+        for copy in copies:
+            copy.wait()
 
 
 def standardise_high(sources, block):
     seqs, residues, depth = block.shape
     half = depth // 2
     count = sources.shape[0]
+    own = residues // count
     hbm = pl.BlockSpec(memory_space=pltpu.HBM)
+    together = 8 // own
+    block = pltpu.with_memory_space_constraint(block, pltpu.HBM)
     return pl.pallas_call(
         high_kernel,
-        in_specs=[pl.BlockSpec(memory_space=pltpu.SMEM), hbm],
-        out_specs=[hbm] * count,
-        out_shape=[pltpu.HBM((residues // count, seqs, depth), BF16)] * count,
-        scratch_shapes=[
-            pltpu.VMEM((seqs, residues, half), F32),
-            pltpu.VMEM((seqs, residues, half), F32),
-            pltpu.VMEM((seqs // 16, residues, 16, depth), BF16),
-            pltpu.SemaphoreType.DMA((seqs // 8,)),
-            pltpu.SemaphoreType.DMA((seqs // 16 * count,)),
-        ],
-        compiler_params=params(10),
+        grid_spec=pltpu.PrefetchScalarGridSpec(
+            num_scalar_prefetch=1,
+            grid=(count,),
+            in_specs=[
+                pl.BlockSpec((seqs, 8, half), lambda p, sources: (0, sources[p] // together, 0)),
+                pl.BlockSpec((seqs, 8, half), lambda p, sources: (0, sources[p] // together, 1)),
+            ],
+            out_specs=[hbm] * count,
+            scratch_shapes=[
+                pltpu.VMEM((count, own, seqs, depth), BF16),
+                pltpu.SemaphoreType.DMA((count,)),
+            ],
+        ),
+        out_shape=[pltpu.HBM((own, seqs, depth), BF16)] * count,
+        compiler_params=params(10, "arbitrary"),
         cost_estimate=cost(3),
         name="standardise_high",
-    )(sources, pltpu.with_memory_space_constraint(block, pltpu.HBM))
+    )(sources, block, block)
 
 
 def low_kernel(sources_ref, first_ref, second_ref, *rest):
@@ -398,7 +400,8 @@
     copies = []
 
     def send(source, target):
-        copies.append(pltpu.make_async_copy(source, target, copied.at[len(copies) + 1]))
+        number = 2 * len(right_refs) + 1 + len(copies)
+        copies.append(pltpu.make_async_copy(source, target, copied.at[number]))
         copies[-1].start()
 
     features = TENSOR_FEATURES
@@ -461,46 +464,53 @@
     lax.fori_loop(0, features // together, channel_step, 0)
 
     left_firsts = [left_slots_ref[j] * residues for j in range(2 * slots)]
-    right_firsts = [right_firsts_ref[p] for p in range(len(right_refs))]
     fetched.wait()
-    for g in range(groups):
-        normed, places = [], []
-        for place in range(GROUP):
-            p, n = divmod(g * GROUP + place, share)
-            b = right_firsts[p] + n
-            places.append(b)
-            lanes = slice(place % 2 * C_Z, (place % 2 + 1) * C_Z)
-            start = (2 * g + place // 2) * rows
-            pieces = []
-            for first in left_firsts:
-                source = pl.ds(pl.multiple_of(start + first, residues), residues)
-                pieces.append(sum_ref[source, lanes])
-            mid = jnp.concatenate(pieces, axis=0)
-            mid = mid + couplings_ref[pl.ds(b, rows, stride=columns), :]
-            mid_ref[g * GROUP + place] = mid
-            centred = mid - jnp.mean(mid, axis=1, keepdims=True)
-            variance = jnp.mean(centred * centred, axis=1, keepdims=True)
-            normed.append((centred * lax.rsqrt(variance + EPS)).astype(BF16))
-        gates = sigmoid(matmul(jnp.concatenate(normed, axis=0), switch_ref[...]))
-        blank = jnp.zeros_like(normed[0])
-        for place in range(0, GROUP, 2):
-            twice = []
-            for e in range(2):
-                part = gates[(place + e) * rows : (place + e + 1) * rows]
-                gate_ref[g * GROUP + place + e] = part
-                twice.append(jnp.concatenate([normed[place + e], blank], axis=1))
-                twice.append(jnp.concatenate([blank, normed[place + e]], axis=1))
-            sides = matmul_nt(entry_ref[...], jnp.concatenate(twice, axis=0))
-            sides = sigmoid(sides[C_TRI:]) * sides[:C_TRI]
-            for e in range(2):
-                first = pl.multiple_of(places[place + e] * C_TRI, C_TRI)
-                rows_ref[pl.ds(first, C_TRI), :] = sides[:, e * 2 * rows : (e + 1) * 2 * rows]
-
-        if (g + 1) * GROUP % share == 0:
-            p = (g + 1) * GROUP // share - 1
-            source, target = pl.ds(p * share, share), pl.ds(right_firsts[p], share)
-            send(mid_ref.at[source], mid_hbm.at[target])
-            send(gate_ref.at[source], gate_hbm.at[target])
+
+    def piece_copies(p):
+        source, target = pl.ds(p * share, share), pl.ds(right_firsts_ref[p], share)
+        return [
+            pltpu.make_async_copy(ref.at[source], hbm.at[target], copied.at[2 * p + kind + 1])
+            for kind, (ref, hbm) in enumerate(((mid_ref, mid_hbm), (gate_ref, gate_hbm)))
+        ]
+
+    def piece_step(p, carry):
+        first_column = right_firsts_ref[p]
+        for g in range(share // GROUP):
+            normed = []
+            for place in range(GROUP):
+                n = g * GROUP + place
+                lanes = slice(place % 2 * C_Z, (place % 2 + 1) * C_Z)
+                start = ((p * (share // GROUP) + g) * 2 + place // 2) * rows
+                pieces = []
+                for first in left_firsts:
+                    source = pl.ds(pl.multiple_of(start + first, residues), residues)
+                    pieces.append(sum_ref[source, lanes])
+                mid = jnp.concatenate(pieces, axis=0)
+                mid = mid + couplings_ref[pl.ds(first_column + n, rows, stride=columns), :]
+                mid_ref[p * share + n] = mid
+                centred = mid - jnp.mean(mid, axis=1, keepdims=True)
+                variance = jnp.mean(centred * centred, axis=1, keepdims=True)
+                normed.append((centred * lax.rsqrt(variance + EPS)).astype(BF16))
+            gates = sigmoid(matmul(jnp.concatenate(normed, axis=0), switch_ref[...]))
+            blank = jnp.zeros_like(normed[0])
+            for place in range(0, GROUP, 2):
+                twice = []
+                for e in range(2):
+                    part = gates[(place + e) * rows : (place + e + 1) * rows]
+                    gate_ref[p * share + g * GROUP + place + e] = part
+                    twice.append(jnp.concatenate([normed[place + e], blank], axis=1))
+                    twice.append(jnp.concatenate([blank, normed[place + e]], axis=1))
+                sides = matmul_nt(entry_ref[...], jnp.concatenate(twice, axis=0))
+                sides = sigmoid(sides[C_TRI:]) * sides[:C_TRI]
+                for e in range(2):
+                    column = first_column + g * GROUP + place + e
+                    first = pl.multiple_of(column * C_TRI, C_TRI)
+                    rows_ref[pl.ds(first, C_TRI), :] = sides[:, e * 2 * rows : (e + 1) * 2 * rows]
+        for copy in piece_copies(p):
+            copy.start()
+        return carry
+
+    lax.fori_loop(0, len(right_refs), piece_step, 0)
 
     cut = C_TRI // 4
     for part in range(4):
@@ -512,6 +522,8 @@
         lax.fori_loop(part * cut, (part + 1) * cut, turn_step, 0, unroll=8)
         chosen = pl.ds(part * cut, cut)
         send(sides_ref.at[chosen], sides_hbm.at[chosen])
+    for p in range(len(right_refs)):
+        copies.extend(piece_copies(p))
     for copy in copies:
         copy.wait()
 
@@ -606,7 +618,7 @@
     columns, rows, depth = mid_ref.shape
     own = 8
     fetched, sent = copied
-    fetches, sends = [], []
+    fetches = []
     for first in range(0, columns, own):
         chosen = pl.ds(first, own)
         for source, target in ((mid_hbm, mid_ref), (gate_hbm, gate_ref)):
@@ -617,28 +629,35 @@
             )
             fetches[-1].start()
     wide_ref[...] = product_ref[...].astype(F32).reshape(channels * part, lanes)
-    for group in range(part // own):
+    turns = part // own
+
+    def send(cut):
+        target = pl.ds(pl.multiple_of(cut * own, own), own)
+        return pltpu.make_async_copy(out_ref.at[cut], out_hbm.at[:, target], sent.at[cut])
+
+    def group_step(group, carry):
         updates = []
         for j in range(own):
             product = wide_ref[pl.ds(group * own + j, channels, stride=part), :]
             updates.append(matmul(normalise_rows(product).T, final_ref[...]))
         for half in range(2):
-            cut = half * (part // own) + group
-            fetches[2 * cut].wait()
-            fetches[2 * cut + 1].wait()
+            cut = half * turns + group
+            chosen = pl.ds(cut * own, own)
+            for kind, (source, target) in enumerate(((mid_hbm, mid_ref), (gate_hbm, gate_ref))):
+                pltpu.make_async_copy(
+                    source.at[chosen], target.at[chosen], fetched.at[2 * cut + kind]
+                ).wait()
             out_rows = out_ref.at[cut].reshape(rows * own, depth)
             for j in range(own):
                 b = cut * own + j
                 piece = updates[j][half * rows : (half + 1) * rows]
                 out_rows[pl.ds(j, rows, stride=own), :] = mid_ref[b] + gate_ref[b] * piece
-            sends.append(
-                pltpu.make_async_copy(
-                    out_ref.at[cut], out_hbm.at[:, pl.ds(cut * own, own)], sent.at[len(sends)]
-                )
-            )
-            sends[-1].start()
-    for send in sends:
-        send.wait()
+            send(cut).start()
+        return carry
+
+    lax.fori_loop(0, turns, group_step, 0)
+    for cut in range(2 * turns):
+        send(cut).wait()
 
 
 def pair_result(product, mid, gate, final_matrix):

time: 127 us -> 128 us (level)
  transfers between devices with their start and end apart: 22 -> 22, of which waited for: 9 -> 9; matrix products, arithmetic and copies ran while one was open for 11% -> 11% of each run, Pallas kernels for 12% -> 11%
where the time goes in v15:
time: 128 us; the launch traced here: 127 us
  waiting for transfers between devices  39.2 us (31%)
  Pallas kernels  36.9 us (29%)
  starting transfers between devices  34.2 us (27%)
  local copies, waits for them, and re-layouts  9.15 us (7%)
  matrix products  3.41 us (3%)
  other arithmetic  3.29 us (3%)
    ppermute x12, waiting for transfers between devices, exchange_rows(): arrived.append(lax.ppermute(pieces[shift], 'row', moves))  24.8 us
    ppermute x12, starting transfers between devices, exchange_rows(): arrived.append(lax.ppermute(pieces[shift], 'row', moves))  15.2 us
    pallas_call x1, Pallas kernels, pair_update(): pl.pallas_call(functools.partial(pair_kernel, slots=len(left) // 2), in_s...  9.56 us
    ppermute x4, starting transfers between devices, gather_turned(): arrived.append(lax.ppermute(source, ('row', 'col'), moves))  9.53 us
    pallas_call x1, Pallas kernels, attention(): pl.pallas_call(attention_kernel, grid=(residues // step,), in_specs=[pl.B...  8.4 us
    all_to_all x1, waiting for transfers between devices, body(): product = lax.all_to_all(product, everywhere, split_axis=0, concat_axis=0)  7.64 us
    all_to_all x1, starting transfers between devices, body(): sides = lax.all_to_all(sides, everywhere, split_axis=0, concat_axis=0)  6.35 us
    ppermute x4, waiting for transfers between devices, gather_turned(): arrived.append(lax.ppermute(source, ('row', 'col'), moves))  4.87 us
  transfers between devices with their start and end apart: 22, of which 9 were waited for; matrix products, arithmetic and copies ran while one was open for 11% of the time, Pallas kernels for 11%

profile of v15, /device:TPU:0, one launch (start us, length us, event | category | flops | bytes accessed | tf_op | source)
XLA Modules:
  0.0 127.3 jit_solution(18099751879053814319)
XLA Ops:
  0.6 0.0 copy-start.9
  0.7 0.0 copy-start.13
  0.7 4.4 %standardise_high.1 = (bf16[8,64,256]{2,1,0:T(8,128)(2,1)}, bf16[8,64,256]{2,1,0:T(8,128)(2,1)}, bf16[8,64,256]{2,1,0:T(8,128)(2,1)}, bf16[8,64,256]{2,1,0:T(8,128)(2,1)}) custom-call(s32[4]{0:T(128)S(1)} %iota_xor_fusion.sources_ref, f32[64,32,256]{2,1,0:T(8,128)} %second_ref.3, f32[64,32,256]{2,1,0:T(8,128)} %second_ref.3), custom_call_target="tpu_custom_call" | custom-call | flops 3000000000 | bytes 3000000 | tf_op jit(solution)/shard_map/standardise_high/pallas_call | solution.py:118
  5.0 0.0 copy-start
  5.1 3.0 %collective-permute-start = (bf16[8,64,256]{2,1,0:T(8,128)(2,1)}, bf16[8,64,256]{2,1,0:T(8,128)(2,1)S(1)}, u32[]{:S(2)}, u32[]{:S(2)}) collective-permute-start(bf16[8,64,256]{2,1,0:T(8,128)(2,1)} %get-tuple-element.52), channel_id=1, source_target_pairs={{0,8},{8,0},{16,24},{24,16},{1,9},{9,1},{17,25},{25,17},{2,10},{10... | collective-permute-start | bytes 786440 | tf_op jit(solution)/shard_map/ppermute | solution.py:746
  8.1 1.5 %collective-permute-start.1 = (bf16[8,64,256]{2,1,0:T(8,128)(2,1)}, bf16[8,64,256]{2,1,0:T(8,128)(2,1)S(1)}, u32[]{:S(2)}, u32[]{:S(2)}) collective-permute-start(bf16[8,64,256]{2,1,0:T(8,128)(2,1)} %get-tuple-element.53), channel_id=1, source_target_pairs={{0,16},{8,24},{16,0},{24,8},{1,17},{9,25},{17,1},{25,9},{2,18},{10... | collective-permute-start | bytes 786440 | tf_op jit(solution)/shard_map/ppermute | solution.py:746
  9.6 0.0 collective-permute-start.2
  9.6 0.7 slice.7
  10.4 1.1 copy.17
  11.5 0.8 copy.12
  12.2 0.9 reshape.47
  13.2 0.1 copy.15
  13.3 1.0 copy.14
  14.4 0.1 pad_add_fusion.left_slots_ref
  14.4 0.9 pad_maximum_fusion.1.others_ref
  15.4 4.5 %standardise_low.1 = (bf16[528,256]{1,0:T(8,128)(2,1)}, bf16[528,256]{1,0:T(8,128)(2,1)}, bf16[528,256]{1,0:T(8,128)(2,1)}, bf16[528,256]{1,0:T(8,128)(2,1)}) custom-call(s32[4]{0:T(128)S(1)} %iota_xor_fusion.sources_ref, f32[64,32,256]{2,1,0:T(8,128)S(1)} %copy-done, f32[64,32,256]{2,1,0:T(8,128)S(1)} %copy-done), custom_call_target="tpu_custom_call" | custom-call | flops 4000000000 | bytes 4000000 | tf_op jit(solution)/shard_map/standardise_low/pallas_call | solution.py:176
  19.9 1.7 %collective-permute-done.1.rest_2_ = bf16[8,64,256]{2,1,0:T(8,128)(2,1)S(1)} collective-permute-done((bf16[8,64,256]{2,1,0:T(8,128)(2,1)}, bf16[8,64,256]{2,1,0:T(8,128)(2,1)S(1)}, u32[]{:S(2)}, u32[]{:S(2)}) %collective-permute-start.1) | collective-permute-done | bytes 262176 | tf_op jit(solution)/shard_map/ppermute | solution.py:746
  21.7 0.0 collective-permute-done.2.rest_3_
  21.7 1.2 collective-permute-start.3
  22.9 0.9 collective-permute-start.4
  23.8 1.4 %collective-permute-start.5 = (bf16[528,256]{1,0:T(8,128)(2,1)}, bf16[528,256]{1,0:T(8,128)(2,1)S(1)}, u32[]{:S(2)}, u32[]{:S(2)}) collective-permute-start(bf16[528,256]{1,0:T(8,128)(2,1)} %get-tuple-element.76), channel_id=1, source_target_pairs={{0,24},{8,16},{16,8},{24,0},{1,25},{9,17},{17,9},{25,1},{2,26},{10... | collective-permute-start | bytes 811016 | tf_op jit(solution)/shard_map/ppermute | solution.py:746
  25.2 8.4 %attention.1.turned_ref = bf16[8,256,256]{2,1,0:T(8,128)(2,1)S(1)} custom-call(bf16[256,256]{1,0:T(8,128)(2,1)S(1)} %slice.6.key_ref, bf16[768,256]{1,0:T(8,128)(2,1)S(1)} %pad_maximum_fusion.1.others_ref, bf16[8,64,256]{2,1,0:T(8,128)(2,1)S(1)} %copy-done.6, bf16[8,64,256]{2,1,0:T(8,128)(2,1)S(1)} %collective-permute-done.rest_1_, ...), custom_call_target="tpu_custom_call" | custom-call | flops 10000000000 | bytes 10000000 | tf_op jit(solution)/shard_map/attention/pallas_call | solution.py:259
  33.6 2.3 %collective-permute-done.4.rest_6_.rest_10_ = bf16[528,256]{1,0:T(8,128)(2,1)S(1)} collective-permute-done((bf16[528,256]{1,0:T(8,128)(2,1)}, bf16[528,256]{1,0:T(8,128)(2,1)S(1)}, u32[]{:S(2)}, u32[]{:S(2)}) %collective-permute-start.4) | collective-permute-done | bytes 270368 | tf_op jit(solution)/shard_map/ppermute | solution.py:746
  36.0 0.0 collective-permute-done.5.rest_7_.rest_11_
  36.0 3.8 %alignment.1 = (bf16[256,256]{1,0:T(8,128)(2,1)S(1)}, bf16[8,32,256]{2,1,0:T(8,128)(2,1)S(1)}) custom-call(s32[4]{0:T(128)S(1)} %iota_xor_fusion.sources_ref, bf16[8,256,256]{2,1,0:T(8,128)(2,1)S(1)} %attention.1.turned_ref, bf16[256,256]{1,0:T(8,128)(2,1)S(1)} %bitcast.28, bf16[64,256]{1,0:T(8,128)(2,1)S(1)} %bitcast.30, bf16[8,64,256]{2,1,0:T(8,128)(2,1)S(1)} %copy-done.6, ...), custom_call_target="tpu_custom_call" | custom-call | flops 4000000000 | bytes 4000000 | tf_op jit(solution)/shard_map/alignment/pallas_call | solution.py:361
  39.8 0.6 collective-permute-start.8
  40.4 1.2 collective-permute-start.11
  41.6 1.8 %collective-permute-start.12 = (bf16[8,32,256]{2,1,0:T(8,128)(2,1)S(1)}, bf16[8,32,256]{2,1,0:T(8,128)(2,1)S(1)}, u32[]{:S(2)}, u32[]{:S(2)}) collective-permute-start(bf16[8,32,256]{2,1,0:T(8,128)(2,1)S(1)} %get-tuple-element.82.rest_8_), channel_id=1, source_target_pairs={{0,24},{8,16},{16,8},{24,0},{1,25},{9,17},{17,9},{25,1},{2,26},{10... | collective-permute-start | bytes 393224 | tf_op jit(solution)/shard_map/ppermute | solution.py:746
  43.3 0.8 collective-permute-start.6
  44.1 3.3 %collective-permute-start.7 = (bf16[256,256]{1,0:T(8,128)(2,1)S(1)}, bf16[256,256]{1,0:T(8,128)(2,1)S(1)}, u32[]{:S(2)}, u32[]{:S(2)}) collective-permute-start(bf16[256,256]{1,0:T(8,128)(2,1)S(1)} %get-tuple-element.79), channel_id=1, source_target_pairs={{0,2},{1,3},{2,10},{3,11},{4,18},{5,19},{6,26},{7,27},{8,4},{9,5},... | collective-permute-start | bytes 393224 | tf_op jit(solution)/shard_map/ppermute | solution.py:707
  47.5 0.0 collective-permute-done.8.rest_9_
  47.5 5.4 %collective-permute-start.10 = (bf16[256,256]{1,0:T(8,128)(2,1)S(1)}, bf16[256,256]{1,0:T(8,128)(2,1)S(1)}, u32[]{:S(2)}, u32[]{:S(2)}) collective-permute-start(bf16[256,256]{1,0:T(8,128)(2,1)S(1)} %get-tuple-element.79), channel_id=1, source_target_pairs={{0,6},{1,7},{2,14},{3,15},{4,22},{5,23},{6,30},{7,31},{8,0},{9,1},... | collective-permute-start | bytes 393224 | tf_op jit(solution)/shard_map/ppermute | solution.py:707
  52.9 0.0 collective-permute-done.11.rest_10_
  52.9 0.0 collective-permute-start.9
  52.9 0.0 collective-permute-done.6.rest_0_
  52.9 0.1 collective-permute-start.13
  53.0 1.4 %collective-permute-done.7.rest_1_ = bf16[256,256]{1,0:T(8,128)(2,1)S(1)} collective-permute-done((bf16[256,256]{1,0:T(8,128)(2,1)S(1)}, bf16[256,256]{1,0:T(8,128)(2,1)S(1)}, u32[]{:S(2)}, u32[]{:S(2)}) %collective-permute-start.7) | collective-permute-done | bytes 131104 | tf_op jit(solution)/shard_map/ppermute | solution.py:707
  54.3 1.1 collective-permute-done.10.rest_3_
  55.4 0.0 collective-permute-start.16
  55.4 2.4 %collective-permute-done.9.rest_2_ = bf16[256,256]{1,0:T(8,128)(2,1)S(1)} collective-permute-done((bf16[256,256]{1,0:T(8,128)(2,1)S(1)}, bf16[256,256]{1,0:T(8,128)(2,1)S(1)}, u32[]{:S(2)}, u32[]{:S(2)}) %collective-permute-start.9) | collective-permute-done | bytes 131104 | tf_op jit(solution)/shard_map/ppermute | solution.py:707
  57.9 1.7 %turn_back.1 = (bf16[8,64,256]{2,1,0:T(8,128)(2,1)}, bf16[8,64,256]{2,1,0:T(8,128)(2,1)}, bf16[8,64,256]{2,1,0:T(8,128)(2,1)}, bf16[8,64,256]{2,1,0:T(8,128)(2,1)}) custom-call(bf16[8,256,256]{2,1,0:T(8,128)(2,1)S(1)} %attention.1.turned_ref), custom_call_target="tpu_custom_call" | custom-call | flops 2000000000 | bytes 2000000 | tf_op jit(solution)/shard_map/turn_back/pallas_call | solution.py:290
  59.6 0.0 collective-permute-done.13.rest_4_
  59.6 0.0 collective-permute-done.14.rest_5_
  59.6 9.6 %pair_update.1 = (f32[32,64,128]{2,1,0:T(8,128)}, f32[32,64,128]{2,1,0:T(8,128)}, bf16[128,32,128]{2,1,0:T(8,128)(2,1)}) custom-call(s32[8]{0:T(128)S(1)} %pad_add_fusion.left_slots_ref, s32[4]{0:T(128)S(1)} %broadcast_multiply_fusion.right_firsts_ref, bf16[256,256]{1,0:T(8,128)(2,1)S(1)} %collective-permute-done.6.rest_0_, ...), custom_call_target="tpu_custom_call" | custom-call | flops 12000000000 | bytes 12000000 | tf_op jit(solution)/shard_map/pair_update/pallas_call | solution.py:538
  69.2 6.4 %all-to-all-start = ((bf16[32,4,32,128]{3,2,1,0:T(8,128)(2,1)}), bf16[32,4,32,128]{3,2,1,0:T(8,128)(2,1)S(1)}, u32[]{:S(2)}, u32[]{:S(2)}) async-start(bf16[32,4,32,128]{3,2,1,0:T(8,128)(2,1)} %bitcast.33), calls=%async_computation | async-start | bytes 2097152 | tf_op jit(solution)/shard_map/all_to_all | solution.py:816
  75.6 0.0 copy-start.10
  75.6 1.8 %collective-permute-start.17 = (bf16[8,64,256]{2,1,0:T(8,128)(2,1)}, bf16[8,64,256]{2,1,0:T(8,128)(2,1)S(1)}, u32[]{:S(2)}, u32[]{:S(2)}) collective-permute-start(bf16[8,64,256]{2,1,0:T(8,128)(2,1)} %get-tuple-element.89), channel_id=1, source_target_pairs={{0,8},{8,0},{16,24},{24,16},{1,9},{9,1},{17,25},{25,17},{2,10},{10... | collective-permute-start | bytes 786440 | tf_op jit(solution)/shard_map/ppermute | solution.py:746
  77.4 1.5 %collective-permute-start.18 = (bf16[8,64,256]{2,1,0:T(8,128)(2,1)}, bf16[8,64,256]{2,1,0:T(8,128)(2,1)S(1)}, u32[]{:S(2)}, u32[]{:S(2)}) collective-permute-start(bf16[8,64,256]{2,1,0:T(8,128)(2,1)} %get-tuple-element.90), channel_id=1, source_target_pairs={{0,16},{8,24},{16,0},{24,8},{1,17},{9,25},{17,1},{25,9},{2,18},{10... | collective-permute-start | bytes 786440 | tf_op jit(solution)/shard_map/ppermute | solution.py:746
  78.9 0.3 collective-permute-start.19
  79.1 13.7 %collective-permute-done.17 = bf16[8,64,256]{2,1,0:T(8,128)(2,1)S(1)} collective-permute-done((bf16[8,64,256]{2,1,0:T(8,128)(2,1)}, bf16[8,64,256]{2,1,0:T(8,128)(2,1)S(1)}, u32[]{:S(2)}, u32[]{:S(2)}) %collective-permute-start.17) | collective-permute-done | bytes 262176 | tf_op jit(solution)/shard_map/ppermute | solution.py:746
  92.9 0.7 copy-done.11
  93.6 0.7 copy-done.12
  94.3 6.9 %collective-permute-done.19 = bf16[8,64,256]{2,1,0:T(8,128)(2,1)} collective-permute-done((bf16[8,64,256]{2,1,0:T(8,128)(2,1)}, bf16[8,64,256]{2,1,0:T(8,128)(2,1)}, u32[]{:S(2)}, u32[]{:S(2)}) %collective-permute-start.19) | collective-permute-done | bytes 262176 | tf_op jit(solution)/shard_map/ppermute | solution.py:746
  101.2 1.9 %all-to-all-done.sides_ref = bf16[32,4,32,128]{3,2,1,0:T(8,128)(2,1)S(1)} async-done(((bf16[32,4,32,128]{3,2,1,0:T(8,128)(2,1)}), bf16[32,4,32,128]{3,2,1,0:T(8,128)(2,1)S(1)}, u32[]{:S(2)}, u32[]{:S(2)}) %all-to-all-start) | async-done | bytes 1048608 | tf_op jit(solution)/shard_map/all_to_all | solution.py:816
  103.1 1.7 %triangle_product.1 = bf16[32,4,16,128]{3,2,1,0:T(8,128)(2,1)} custom-call(bf16[32,4,32,128]{3,2,1,0:T(8,128)(2,1)S(1)} %all-to-all-done.sides_ref), custom_call_target="tpu_custom_call" | custom-call | flops 3000000000 | bytes 3000000 | tf_op jit(solution)/shard_map/triangle_product/pallas_call | solution.py:602
  104.8 3.0 %all-to-all-start.1 = ((bf16[32,4,16,128]{3,2,1,0:T(8,128)(2,1)}), bf16[32,4,16,128]{3,2,1,0:T(8,128)(2,1)S(1)}, u32[]{:S(2)}, u32[]{:S(2)}) async-start(bf16[32,4,16,128]{3,2,1,0:T(8,128)(2,1)} %triangle_product.1), calls=%async_computation.1 | async-start | bytes 1048576 | tf_op jit(solution)/shard_map/all_to_all | solution.py:819
  107.9 0.1 broadcast_in_dim.14
  107.9 0.1 broadcast_in_dim.15
  108.0 0.0 copy-start.8
  108.1 2.2 %pad_maximum_fusion = bf16[4,8,64,256]{3,2,1,0:T(8,128)(2,1)} fusion(bf16[1,8,64,256]{3,2,1,0:T(8,128)(2,1)} %bitcast.10, bf16[1,8,64,256]{3,2,1,0:T(8,128)(2,1)} %bitcast.38, bf16[1,8,64,256]{3,2,1,0:T(8,128)(2,1)} %bitcast.37, bf16[1,8,64,256]{3,2,1,0:T(8,128)(2,1)S(1)} %bitcast.36), kind=kLoop, calls=%fused_computation.2 | loop fusion | flops 1572864 | bytes 2097152 | tf_op jit(solution)/shard_map/stack | solution.py:821
  110.3 2.8 %gather_fusion = bf16[4,8,64,256]{3,2,1,0:T(8,128)(2,1)} fusion(bf16[4,8,64,256]{3,2,1,0:T(8,128)(2,1)} %pad_maximum_fusion, s32[1024]{0:T(1024)S(1)} %pad_clamp_fusion), kind=kCustom, calls=%fused_computation | custom fusion | bytes 2097168 | tf_op jit(solution)/shard_map/jit(_take)/gather | solution.py:821
  113.1 3.4 %convolution_add_fusion = f32[64,32,256]{2,1,0:T(8,128)} fusion(f32[64,32,256]{2,1,0:T(8,128)S(1)} %copy-done, bf16[32,64,256]{2,1,0:T(8,128)(2,1)} %bitcast.31, pred[32]{0:T(512)(128)(4,1)S(1)} %broadcast_in_dim.15, bf16[256,256]{1,0:T(8,128)(2,1)S(1)} %copy-done.8), kind=kOutput, calls=%fused_computation.1 | convolution fusion | flops 269484032 | bytes 5373984 | tf_op jit(solution)/shard_map/dot_general | solution.py:823
  116.6 7.6 %all-to-all-done.1 = bf16[32,4,16,128]{3,2,1,0:T(8,128)(2,1)S(1)} async-done(((bf16[32,4,16,128]{3,2,1,0:T(8,128)(2,1)}), bf16[32,4,16,128]{3,2,1,0:T(8,128)(2,1)S(1)}, u32[]{:S(2)}, u32[]{:S(2)}) %all-to-all-start.1) | async-done | bytes 524320 | tf_op jit(solution)/shard_map/all_to_all | solution.py:819
  124.2 2.9 %pair_result.1 = f32[64,32,128]{2,1,0:T(8,128)} custom-call(bf16[128,16,128]{2,1,0:T(8,128)(2,1)S(1)} %bitcast.26, bf16[128,128]{1,0:T(8,128)(2,1)S(1)} %copy-done.5, f32[32,64,128]{2,1,0:T(8,128)} %get-tuple-element.98.mid_hbm, f32[32,64,128]{2,1,0:T(8,128)} %get-tuple-element.99.gate_hbm), custom_call_target="tpu_custom_call" | custom-call | flops 3000000000 | bytes 3000000 | tf_op jit(solution)/shard_map/pair_result/pallas_call | solution.py:667
  (37 shorter events, 0.1 us)
Async XLA Ops:
  0.6 9.0 %copy-start.9 = (bf16[256,768]{1,0:T(8,128)(2,1)S(1)}, bf16[256,768]{1,0:T(8,128)(2,1)}, u32[]{:S(2)}) copy-start(bf16[256,768]{1,0:T(8,128)(2,1)} %param.13) | copy-start | bytes 1179652
  0.7 10.8 %copy-start.13 = (bf16[256,256]{1,0:T(8,128)(2,1)S(1)}, bf16[256,256]{1,0:T(8,128)(2,1)}, u32[]{:S(2)}) copy-start(bf16[256,256]{1,0:T(8,128)(2,1)} %param.12) | copy-start | bytes 393220
  5.0 10.3 %copy-start = (f32[64,32,256]{2,1,0:T(8,128)S(1)}, f32[64,32,256]{2,1,0:T(8,128)}, u32[]{:S(2)}) copy-start(f32[64,32,256]{2,1,0:T(8,128)} %second_ref.3) | copy-start | bytes 6291460
  5.1 14.8 %collective-permute-start = (bf16[8,64,256]{2,1,0:T(8,128)(2,1)}, bf16[8,64,256]{2,1,0:T(8,128)(2,1)S(1)}, u32[]{:S(2)}, u32[]{:S(2)}) collective-permute-start(bf16[8,64,256]{2,1,0:T(8,128)(2,1)} %get-tuple-element.52), channel_id=1, source_target_pairs={{0,8},{8,0},{16,24},{24,16},{1,9},{9,1},{17,25},{25,17},{2,10},{10... | collective-permute-start | bytes 786440 | tf_op jit(solution)/shard_map/ppermute | solution.py:746
  8.1 13.6 %collective-permute-start.1 = (bf16[8,64,256]{2,1,0:T(8,128)(2,1)}, bf16[8,64,256]{2,1,0:T(8,128)(2,1)S(1)}, u32[]{:S(2)}, u32[]{:S(2)}) collective-permute-start(bf16[8,64,256]{2,1,0:T(8,128)(2,1)} %get-tuple-element.53), channel_id=1, source_target_pairs={{0,16},{8,24},{16,0},{24,8},{1,17},{9,25},{17,1},{25,9},{2,18},{10... | collective-permute-start | bytes 786440 | tf_op jit(solution)/shard_map/ppermute | solution.py:746
  9.6 12.1 %collective-permute-start.2 = (bf16[8,64,256]{2,1,0:T(8,128)(2,1)}, bf16[8,64,256]{2,1,0:T(8,128)(2,1)S(1)}, u32[]{:S(2)}, u32[]{:S(2)}) collective-permute-start(bf16[8,64,256]{2,1,0:T(8,128)(2,1)} %get-tuple-element.54), channel_id=1, source_target_pairs={{0,24},{8,16},{16,8},{24,0},{1,25},{9,17},{17,9},{25,1},{2,26},{10... | collective-permute-start | bytes 786440 | tf_op jit(solution)/shard_map/ppermute | solution.py:746
  15.4 9.8 %copy-start.6 = (bf16[8,64,256]{2,1,0:T(8,128)(2,1)S(1)}, bf16[8,64,256]{2,1,0:T(8,128)(2,1)}, u32[]{:S(2)}) copy-start(bf16[8,64,256]{2,1,0:T(8,128)(2,1)} %get-tuple-element.61.rest_0_) | copy-start | bytes 786436
  21.7 14.3 %copy-start.3 = (bf16[256,64]{0,1:T(8,128)(2,1)S(1)}, bf16[256,64]{0,1:T(8,128)(2,1)}, u32[]{:S(2)}) copy-start(bf16[256,64]{0,1:T(8,128)(2,1)} %param.15) | copy-start | bytes 98308
  21.7 14.3 %copy-start.7 = (bf16[528,256]{1,0:T(8,128)(2,1)S(1)}, bf16[528,256]{1,0:T(8,128)(2,1)}, u32[]{:S(2)}) copy-start(bf16[528,256]{1,0:T(8,128)(2,1)} %get-tuple-element.73.rest_4_.rest_8_) | copy-start | bytes 811012
  21.7 12.0 %collective-permute-start.3 = (bf16[528,256]{1,0:T(8,128)(2,1)}, bf16[528,256]{1,0:T(8,128)(2,1)S(1)}, u32[]{:S(2)}, u32[]{:S(2)}) collective-permute-start(bf16[528,256]{1,0:T(8,128)(2,1)} %get-tuple-element.74), channel_id=1, source_target_pairs={{0,8},{8,0},{16,24},{24,16},{1,9},{9,1},{17,25},{25,17},{2,10},{10... | collective-permute-start | bytes 811016 | tf_op jit(solution)/shard_map/ppermute | solution.py:746
  22.9 13.1 %collective-permute-start.4 = (bf16[528,256]{1,0:T(8,128)(2,1)}, bf16[528,256]{1,0:T(8,128)(2,1)S(1)}, u32[]{:S(2)}, u32[]{:S(2)}) collective-permute-start(bf16[528,256]{1,0:T(8,128)(2,1)} %get-tuple-element.75), channel_id=1, source_target_pairs={{0,16},{8,24},{16,0},{24,8},{1,17},{9,25},{17,1},{25,9},{2,18},{10... | collective-permute-start | bytes 811016 | tf_op jit(solution)/shard_map/ppermute | solution.py:746
  23.8 12.2 %collective-permute-start.5 = (bf16[528,256]{1,0:T(8,128)(2,1)}, bf16[528,256]{1,0:T(8,128)(2,1)S(1)}, u32[]{:S(2)}, u32[]{:S(2)}) collective-permute-start(bf16[528,256]{1,0:T(8,128)(2,1)} %get-tuple-element.76), channel_id=1, source_target_pairs={{0,24},{8,16},{16,8},{24,0},{1,25},{9,17},{17,9},{25,1},{2,26},{10... | collective-permute-start | bytes 811016 | tf_op jit(solution)/shard_map/ppermute | solution.py:746
  39.8 7.7 %collective-permute-start.8 = (bf16[8,32,256]{2,1,0:T(8,128)(2,1)S(1)}, bf16[8,32,256]{2,1,0:T(8,128)(2,1)S(1)}, u32[]{:S(2)}, u32[]{:S(2)}) collective-permute-start(bf16[8,32,256]{2,1,0:T(8,128)(2,1)S(1)} %get-tuple-element.82.rest_8_), channel_id=1, source_target_pairs={{0,8},{8,0},{16,24},{24,16},{1,9},{9,1},{17,25},{25,17},{2,10},{10... | collective-permute-start | bytes 393224 | tf_op jit(solution)/shard_map/ppermute | solution.py:746
  40.4 12.5 %collective-permute-start.11 = (bf16[8,32,256]{2,1,0:T(8,128)(2,1)S(1)}, bf16[8,32,256]{2,1,0:T(8,128)(2,1)S(1)}, u32[]{:S(2)}, u32[]{:S(2)}) collective-permute-start(bf16[8,32,256]{2,1,0:T(8,128)(2,1)S(1)} %get-tuple-element.82.rest_8_), channel_id=1, source_target_pairs={{0,16},{8,24},{16,0},{24,8},{1,17},{9,25},{17,1},{25,9},{2,18},{10... | collective-permute-start | bytes 393224 | tf_op jit(solution)/shard_map/ppermute | solution.py:746
  41.6 12.8 %collective-permute-start.12 = (bf16[8,32,256]{2,1,0:T(8,128)(2,1)S(1)}, bf16[8,32,256]{2,1,0:T(8,128)(2,1)S(1)}, u32[]{:S(2)}, u32[]{:S(2)}) collective-permute-start(bf16[8,32,256]{2,1,0:T(8,128)(2,1)S(1)} %get-tuple-element.82.rest_8_), channel_id=1, source_target_pairs={{0,24},{8,16},{16,8},{24,0},{1,25},{9,17},{17,9},{25,1},{2,26},{10... | collective-permute-start | bytes 393224 | tf_op jit(solution)/shard_map/ppermute | solution.py:746
  43.3 16.3 %copy-start.1 = (f32[64,32,128]{2,1,0:T(8,128)S(1)}, f32[64,32,128]{2,1,0:T(8,128)}, u32[]{:S(2)}) copy-start(f32[64,32,128]{2,1,0:T(8,128)} %param.11) | copy-start | bytes 3145732
  43.3 16.3 %copy-start.2 = (bf16[1024,128]{1,0:T(8,128)(2,1)S(1)}, bf16[1024,128]{1,0:T(8,128)(2,1)}, u32[]{:S(2)}) copy-start(bf16[1024,128]{1,0:T(8,128)(2,1)} %rest_12_.1) | copy-start | bytes 786436
  43.3 16.3 %copy-start.4 = (bf16[128,128]{1,0:T(8,128)(2,1)S(1)}, bf16[128,128]{1,0:T(8,128)(2,1)}, u32[]{:S(2)}) copy-start(bf16[128,128]{1,0:T(8,128)(2,1)} %rest_14_.1) | copy-start | bytes 98308
  43.3 9.5 %collective-permute-start.6 = (bf16[256,256]{1,0:T(8,128)(2,1)S(1)}, bf16[256,256]{1,0:T(8,128)(2,1)S(1)}, u32[]{:S(2)}, u32[]{:S(2)}) collective-permute-start(bf16[256,256]{1,0:T(8,128)(2,1)S(1)} %get-tuple-element.79), channel_id=1, source_target_pairs={{0,0},{1,1},{2,8},{3,9},{4,16},{5,17},{6,24},{7,25},{8,2},{9,3},{1... | collective-permute-start | bytes 393224 | tf_op jit(solution)/shard_map/ppermute | solution.py:707
  44.1 10.2 %collective-permute-start.7 = (bf16[256,256]{1,0:T(8,128)(2,1)S(1)}, bf16[256,256]{1,0:T(8,128)(2,1)S(1)}, u32[]{:S(2)}, u32[]{:S(2)}) collective-permute-start(bf16[256,256]{1,0:T(8,128)(2,1)S(1)} %get-tuple-element.79), channel_id=1, source_target_pairs={{0,2},{1,3},{2,10},{3,11},{4,18},{5,19},{6,26},{7,27},{8,4},{9,5},... | collective-permute-start | bytes 393224 | tf_op jit(solution)/shard_map/ppermute | solution.py:707
  47.5 7.9 %collective-permute-start.10 = (bf16[256,256]{1,0:T(8,128)(2,1)S(1)}, bf16[256,256]{1,0:T(8,128)(2,1)S(1)}, u32[]{:S(2)}, u32[]{:S(2)}) collective-permute-start(bf16[256,256]{1,0:T(8,128)(2,1)S(1)} %get-tuple-element.79), channel_id=1, source_target_pairs={{0,6},{1,7},{2,14},{3,15},{4,22},{5,23},{6,30},{7,31},{8,0},{9,1},... | collective-permute-start | bytes 393224 | tf_op jit(solution)/shard_map/ppermute | solution.py:707
  52.9 5.0 %collective-permute-start.9 = (bf16[256,256]{1,0:T(8,128)(2,1)S(1)}, bf16[256,256]{1,0:T(8,128)(2,1)S(1)}, u32[]{:S(2)}, u32[]{:S(2)}) collective-permute-start(bf16[256,256]{1,0:T(8,128)(2,1)S(1)} %get-tuple-element.79), channel_id=1, source_target_pairs={{0,4},{1,5},{2,12},{3,13},{4,20},{5,21},{6,28},{7,29},{8,6},{9,7},... | collective-permute-start | bytes 393224 | tf_op jit(solution)/shard_map/ppermute | solution.py:707
  52.9 6.7 %collective-permute-start.13 = (bf16[256,256]{1,0:T(8,128)(2,1)S(1)}, bf16[256,256]{1,0:T(8,128)(2,1)S(1)}, u32[]{:S(2)}, u32[]{:S(2)}) collective-permute-start(bf16[256,256]{1,0:T(8,128)(2,1)S(1)} %collective-permute-done.6.rest_0_), channel_id=1, source_target_pairs={{0,1},{1,0},{2,3},{3,2},{4,5},{5,4},{6,7},{7,6},{8,9},{9,8},{10,11... | collective-permute-start | bytes 393224 | tf_op jit(solution)/shard_map/ppermute | solution.py:693
  54.3 5.2 %collective-permute-start.14 = (bf16[256,256]{1,0:T(8,128)(2,1)S(1)}, bf16[256,256]{1,0:T(8,128)(2,1)S(1)}, u32[]{:S(2)}, u32[]{:S(2)}) collective-permute-start(bf16[256,256]{1,0:T(8,128)(2,1)S(1)} %collective-permute-done.7.rest_1_), channel_id=1, source_target_pairs={{0,1},{1,0},{2,3},{3,2},{4,5},{5,4},{6,7},{7,6},{8,9},{9,8},{10,11... | collective-permute-start | bytes 393224 | tf_op jit(solution)/shard_map/ppermute | solution.py:693
  55.4 4.2 %collective-permute-start.16 = (bf16[256,256]{1,0:T(8,128)(2,1)S(1)}, bf16[256,256]{1,0:T(8,128)(2,1)S(1)}, u32[]{:S(2)}, u32[]{:S(2)}) collective-permute-start(bf16[256,256]{1,0:T(8,128)(2,1)S(1)} %collective-permute-done.10.rest_3_), channel_id=1, source_target_pairs={{0,1},{1,0},{2,3},{3,2},{4,5},{5,4},{6,7},{7,6},{8,9},{9,8},{10,11... | collective-permute-start | bytes 393224 | tf_op jit(solution)/shard_map/ppermute | solution.py:693
  57.9 1.7 %collective-permute-start.15 = (bf16[256,256]{1,0:T(8,128)(2,1)S(1)}, bf16[256,256]{1,0:T(8,128)(2,1)S(1)}, u32[]{:S(2)}, u32[]{:S(2)}) collective-permute-start(bf16[256,256]{1,0:T(8,128)(2,1)S(1)} %collective-permute-done.9.rest_2_), channel_id=1, source_target_pairs={{0,1},{1,0},{2,3},{3,2},{4,5},{5,4},{6,7},{7,6},{8,9},{9,8},{10,11... | collective-permute-start | bytes 393224 | tf_op jit(solution)/shard_map/ppermute | solution.py:693
  69.2 33.9 %all-to-all-start = ((bf16[32,4,32,128]{3,2,1,0:T(8,128)(2,1)}), bf16[32,4,32,128]{3,2,1,0:T(8,128)(2,1)S(1)}, u32[]{:S(2)}, u32[]{:S(2)}) async-start(bf16[32,4,32,128]{3,2,1,0:T(8,128)(2,1)} %bitcast.33), calls=%async_computation | async-start | bytes 2097152 | tf_op jit(solution)/shard_map/all_to_all | solution.py:816
  75.6 32.5 %copy-start.10 = (bf16[8,64,256]{2,1,0:T(8,128)(2,1)S(1)}, bf16[8,64,256]{2,1,0:T(8,128)(2,1)}, u32[]{:S(2)}) copy-start(bf16[8,64,256]{2,1,0:T(8,128)(2,1)} %get-tuple-element.93) | copy-start | bytes 786436
  75.6 17.3 %collective-permute-start.17 = (bf16[8,64,256]{2,1,0:T(8,128)(2,1)}, bf16[8,64,256]{2,1,0:T(8,128)(2,1)S(1)}, u32[]{:S(2)}, u32[]{:S(2)}) collective-permute-start(bf16[8,64,256]{2,1,0:T(8,128)(2,1)} %get-tuple-element.89), channel_id=1, source_target_pairs={{0,8},{8,0},{16,24},{24,16},{1,9},{9,1},{17,25},{25,17},{2,10},{10... | collective-permute-start | bytes 786440 | tf_op jit(solution)/shard_map/ppermute | solution.py:746
  77.4 15.4 %collective-permute-start.18 = (bf16[8,64,256]{2,1,0:T(8,128)(2,1)}, bf16[8,64,256]{2,1,0:T(8,128)(2,1)S(1)}, u32[]{:S(2)}, u32[]{:S(2)}) collective-permute-start(bf16[8,64,256]{2,1,0:T(8,128)(2,1)} %get-tuple-element.90), channel_id=1, source_target_pairs={{0,16},{8,24},{16,0},{24,8},{1,17},{9,25},{17,1},{25,9},{2,18},{10... | collective-permute-start | bytes 786440 | tf_op jit(solution)/shard_map/ppermute | solution.py:746
  78.9 22.4 %collective-permute-start.19 = (bf16[8,64,256]{2,1,0:T(8,128)(2,1)}, bf16[8,64,256]{2,1,0:T(8,128)(2,1)}, u32[]{:S(2)}, u32[]{:S(2)}) collective-permute-start(bf16[8,64,256]{2,1,0:T(8,128)(2,1)} %get-tuple-element.91), channel_id=1, source_target_pairs={{0,24},{8,16},{16,8},{24,0},{1,25},{9,17},{17,9},{25,1},{2,26},{10... | collective-permute-start | bytes 786440 | tf_op jit(solution)/shard_map/ppermute | solution.py:746
  92.8 0.7 copy-start.11
  93.6 0.7 copy-start.12
  104.8 19.4 %all-to-all-start.1 = ((bf16[32,4,16,128]{3,2,1,0:T(8,128)(2,1)}), bf16[32,4,16,128]{3,2,1,0:T(8,128)(2,1)S(1)}, u32[]{:S(2)}, u32[]{:S(2)}) async-start(bf16[32,4,16,128]{3,2,1,0:T(8,128)(2,1)} %triangle_product.1), calls=%async_computation.1 | async-start | bytes 1048576 | tf_op jit(solution)/shard_map/all_to_all | solution.py:819
  108.0 5.1 %copy-start.8 = (bf16[256,256]{1,0:T(8,128)(2,1)S(1)}, bf16[256,256]{1,0:T(8,128)(2,1)}, u32[]{:S(2)}) copy-start(bf16[256,256]{1,0:T(8,128)(2,1)} %param.14) | copy-start | bytes 393220
  113.1 11.1 %copy-start.5 = (bf16[128,128]{1,0:T(8,128)(2,1)S(1)}, bf16[128,128]{1,0:T(8,128)(2,1)}, u32[]{:S(2)}) copy-start(bf16[128,128]{1,0:T(8,128)(2,1)} %final_ref.1) | copy-start | bytes 98308

commit v16 on v14

--- a/solution.py
+++ b/solution.py
@@ -69,8 +69,8 @@
 def standardised_columns(first_rows, second_rows, first, count, residues):
     seqs = first_rows.shape[0] // residues
     columns = []
-    for n in range(first, first + count):
-        rows = pl.ds(n, seqs, stride=residues)
+    for n in range(count):
+        rows = pl.ds(first + n, seqs, stride=residues)
         columns.append(jnp.concatenate([first_rows[rows, :], second_rows[rows, :]], axis=1))
     column = jnp.concatenate(columns, axis=0)
     centred = column - jnp.mean(column, axis=1, keepdims=True)
@@ -79,60 +79,61 @@
     return centred * scale, variance * scale
 
 
-def high_kernel(sources_ref, block_hbm, *rest):
-    *pieces_hbm, first_ref, second_ref, high_ref, fetched, sent = rest
+def high_kernel(sources_ref, first_ref, second_ref, *rest):
+    *pieces_hbm, high_ref, sent = rest
     seqs, residues, lanes = first_ref.shape
-    own = residues // len(pieces_hbm)
-    step = 16
-    fetches, sends = [], []
-    for s in range(0, seqs, step):
-        chosen = pl.ds(s, step)
-        for half, ref in enumerate((first_ref, second_ref)):
-            source = block_hbm.at[chosen, :, pl.ds(half * lanes, lanes)]
-            fetches.append(
-                pltpu.make_async_copy(source, ref.at[chosen], fetched.at[len(fetches)])
-            )
-            fetches[-1].start()
-    for part in range(seqs // step):
-        chosen = pl.ds(part * step, step)
-        fetches[2 * part].wait()
-        fetches[2 * part + 1].wait()
-        first_rows = first_ref.at[chosen].reshape(step * residues, lanes)
-        second_rows = second_ref.at[chosen].reshape(step * residues, lanes)
-        for n in range(0, residues, 8):
-            normed, _ = standardised_columns(first_rows, second_rows, n, 8, residues)
-            high_ref[part, n : n + 8] = normed.astype(BF16).reshape(8, step, 2 * lanes)
-        for p, piece_hbm in enumerate(pieces_hbm):
-            source = high_ref.at[part, pl.ds(sources_ref[p] * own, own)]
-            sends.append(
-                pltpu.make_async_copy(source, piece_hbm.at[:, chosen], sent.at[len(sends)])
-            )
-            sends[-1].start()
-    for send in sends:
-        send.wait()
+    count = len(pieces_hbm)
+    own = high_ref.shape[1]
+    step = pl.program_id(0)
+    first_rows = first_ref.reshape(seqs * residues, lanes)
+    second_rows = second_ref.reshape(seqs * residues, lanes)
+    shift = lax.rem(sources_ref[step] * own, residues) if own < residues else 0
+    for n in range(own):
+        normed, _ = standardised_columns(first_rows, second_rows, shift + n, 1, residues)
+        high_ref[step, n] = normed.astype(BF16)
+    copies = [
+        pltpu.make_async_copy(high_ref.at[p], piece_hbm, sent.at[p])
+        for p, piece_hbm in enumerate(pieces_hbm)
+    ]
+    for p in range(count):
+
+        @pl.when(step == p)
+        def _(p=p):
+            copies[p].start()
+
+    @pl.when(step == count - 1)
+    def _():
+        for copy in copies:
+            copy.wait()
 
 
 def standardise_high(sources, block):
     seqs, residues, depth = block.shape
     half = depth // 2
     count = sources.shape[0]
+    own = residues // count
     hbm = pl.BlockSpec(memory_space=pltpu.HBM)
+    together = 8 // own
     return pl.pallas_call(
         high_kernel,
-        in_specs=[pl.BlockSpec(memory_space=pltpu.SMEM), hbm],
-        out_specs=[hbm] * count,
-        out_shape=[pltpu.HBM((residues // count, seqs, depth), BF16)] * count,
-        scratch_shapes=[
-            pltpu.VMEM((seqs, residues, half), F32),
-            pltpu.VMEM((seqs, residues, half), F32),
-            pltpu.VMEM((seqs // 16, residues, 16, depth), BF16),
-            pltpu.SemaphoreType.DMA((seqs // 8,)),
-            pltpu.SemaphoreType.DMA((seqs // 16 * count,)),
-        ],
-        compiler_params=params(10),
+        grid_spec=pltpu.PrefetchScalarGridSpec(
+            num_scalar_prefetch=1,
+            grid=(count,),
+            in_specs=[
+                pl.BlockSpec((seqs, 8, half), lambda p, sources: (0, sources[p] // together, 0)),
+                pl.BlockSpec((seqs, 8, half), lambda p, sources: (0, sources[p] // together, 1)),
+            ],
+            out_specs=[hbm] * count,
+            scratch_shapes=[
+                pltpu.VMEM((count, own, seqs, depth), BF16),
+                pltpu.SemaphoreType.DMA((count,)),
+            ],
+        ),
+        out_shape=[pltpu.HBM((own, seqs, depth), BF16)] * count,
+        compiler_params=params(10, "arbitrary"),
         cost_estimate=cost(3),
         name="standardise_high",
-    )(sources, pltpu.with_memory_space_constraint(block, pltpu.HBM))
+    )(sources, block, block)
 
 
 def low_kernel(sources_ref, first_ref, second_ref, *rest):
@@ -213,13 +214,8 @@
     def score(unit):
         n, h = units[unit]
         key_rows, queries, _, _ = columns[n]
-        low, high = h * UNIT_WIDTH, (h + 1) * UNIT_WIDTH
-        pieces = [queries[low:high]]
-        if low > 0:
-            pieces.insert(0, jnp.zeros((low, total), BF16))
-        if high < inner:
-            pieces.append(jnp.zeros((inner - high, total), BF16))
-        scores_ref[unit % ring] = matmul(key_rows, jnp.concatenate(pieces, axis=0))
+        rows = slice(h * UNIT_WIDTH, (h + 1) * UNIT_WIDTH)
+        scores_ref[unit % ring] = matmul(key_rows[:, rows], queries[rows])
 
     def weigh(unit):
         for low in range(0, total, 128):
@@ -305,11 +301,16 @@
     total = blocks * seqs
     features = TENSOR_FEATURES
     step = pl.program_id(0)
+    line = lax.broadcasted_iota(jnp.int32, (depth, depth), 0)
+    same = line == lax.broadcasted_iota(jnp.int32, (depth, depth), 1)
+    same = jnp.where(same, 1.0, 0.0).astype(BF16)
+    twice = jnp.concatenate([same, same], axis=1)
     for n in range(residues):
-        column = jnp.concatenate([ref[n] for ref in high_refs], axis=0).astype(F32)
-        column = column + jnp.concatenate(
+        high = jnp.concatenate([ref[n] for ref in high_refs], axis=0)
+        low = jnp.concatenate(
             [ref[n * seqs : (n + 1) * seqs, :] for ref in low_refs], axis=0
-        ).astype(F32)
+        )
+        column = matmul_nt(twice, jnp.concatenate([high, low], axis=1))
         spreads = []
         for ref in spread_refs:
             kept = ref[:, :seqs].astype(F32)
@@ -317,7 +318,7 @@
             chosen = lax.rem(row, 8) == step * residues + n
             spreads.append(jnp.sum(jnp.where(chosen, kept, 0.0), axis=0, keepdims=True))
         spread = jnp.concatenate(spreads, axis=1)
-        updated = column.T * spread + matmul(final_ref[...], turned_ref[n])
+        updated = column * spread + matmul(final_ref[...], turned_ref[n])
         projected = matmul(entry_ref[...], normalise_rows(updated))
         me = sources_ref[0]
         tiles = [projected[:, low : low + 128] for low in range(0, total, 128)]

time: 127 us -> 127 us (level)
  local copies, waits for them, and re-layouts: 9.15 us -> 10.7 us
    pallas_call x1, Pallas kernels: 4.46 us -> 2.8 us  [standardise_high(): pl.pallas_call(high_kernel, grid_spec=pltpu.PrefetchScalarGridSpec(num_sc...]
    unnamed x32 -> x34, local copies, waits for them, and re-layouts: 4.36 us -> 5.94 us
  transfers between devices with their start and end apart: 22 -> 22, of which waited for: 9 -> 9; matrix products, arithmetic and copies ran while one was open for 11% -> 11% of each run, Pallas kernels for 12% -> 11%
where the time goes in v16:
time: 127 us
  waiting for transfers between devices  39.3 us (31%)
  Pallas kernels  34.8 us (27%)
  starting transfers between devices  34.2 us (27%)
  local copies, waits for them, and re-layouts  10.7 us (8%)
  matrix products  3.41 us (3%)
  other arithmetic  3.29 us (3%)
    ppermute x12, waiting for transfers between devices, exchange_rows(): arrived.append(lax.ppermute(pieces[shift], 'row', moves))  24.9 us
    ppermute x12, starting transfers between devices, exchange_rows(): arrived.append(lax.ppermute(pieces[shift], 'row', moves))  15.2 us
    ppermute x4, starting transfers between devices, gather_turned(): arrived.append(lax.ppermute(source, ('row', 'col'), moves))  9.54 us
    pallas_call x1, Pallas kernels, pair_update(): pl.pallas_call(functools.partial(pair_kernel, slots=len(left) // 2), in_s...  8.67 us
    pallas_call x1, Pallas kernels, attention(): pl.pallas_call(attention_kernel, grid=(residues // step,), in_specs=[pl.B...  8.26 us
    all_to_all x1, waiting for transfers between devices, body(): product = lax.all_to_all(product, everywhere, split_axis=0, concat_axis=0)  7.65 us
    all_to_all x1, starting transfers between devices, body(): sides = lax.all_to_all(sides, everywhere, split_axis=0, concat_axis=0)  6.37 us
    unnamed x34, local copies, waits for them, and re-layouts  5.94 us
  transfers between devices with their start and end apart: 22, of which 9 were waited for; matrix products, arithmetic and copies ran while one was open for 11% of the time, Pallas kernels for 11%

profile of v16, /device:TPU:0, one launch (start us, length us, event | category | flops | bytes accessed | tf_op | source)
XLA Modules:
  0.0 126.9 jit_solution(14045811609194049345)
XLA Ops:
  0.6 0.0 copy-start
  0.7 1.6 %copy-done = f32[64,32,256]{2,1,0:T(8,128)S(1)} copy-done((f32[64,32,256]{2,1,0:T(8,128)S(1)}, f32[64,32,256]{2,1,0:T(8,128)}, u32[]{:S(2)}) %copy-start) | copy-done | bytes 2097176
  2.2 2.8 %standardise_high.1 = (bf16[8,64,256]{2,1,0:T(8,128)(2,1)}, bf16[8,64,256]{2,1,0:T(8,128)(2,1)}, bf16[8,64,256]{2,1,0:T(8,128)(2,1)}, bf16[8,64,256]{2,1,0:T(8,128)(2,1)}) custom-call(s32[4]{0:T(128)S(1)} %iota_xor_fusion.sources_ref, f32[64,32,256]{2,1,0:T(8,128)S(1)} %copy-done, f32[64,32,256]{2,1,0:T(8,128)S(1)} %copy-done), custom_call_target="tpu_custom_call" | custom-call | flops 3000000000 | bytes 3000000 | tf_op jit(solution)/shard_map/standardise_high/pallas_call | solution.py:117
  5.1 0.0 copy-start.1
  5.1 3.0 %collective-permute-start = (bf16[8,64,256]{2,1,0:T(8,128)(2,1)}, bf16[8,64,256]{2,1,0:T(8,128)(2,1)S(1)}, u32[]{:S(2)}, u32[]{:S(2)}) collective-permute-start(bf16[8,64,256]{2,1,0:T(8,128)(2,1)} %get-tuple-element.52), channel_id=1, source_target_pairs={{0,8},{8,0},{16,24},{24,16},{1,9},{9,1},{17,25},{25,17},{2,10},{10... | collective-permute-start | bytes 786440 | tf_op jit(solution)/shard_map/ppermute | solution.py:728
  8.1 1.5 %collective-permute-start.1 = (bf16[8,64,256]{2,1,0:T(8,128)(2,1)}, bf16[8,64,256]{2,1,0:T(8,128)(2,1)S(1)}, u32[]{:S(2)}, u32[]{:S(2)}) collective-permute-start(bf16[8,64,256]{2,1,0:T(8,128)(2,1)} %get-tuple-element.53), channel_id=1, source_target_pairs={{0,16},{8,24},{16,0},{24,8},{1,17},{9,25},{17,1},{25,9},{2,18},{10... | collective-permute-start | bytes 786440 | tf_op jit(solution)/shard_map/ppermute | solution.py:728
  9.6 0.0 collective-permute-start.2
  9.6 0.7 slice.7
  10.4 1.1 copy.17
  11.5 0.8 copy.12
  12.2 0.9 reshape.47
  13.2 0.1 copy.15
  13.3 1.0 copy.14
  14.4 0.1 pad_add_fusion.left_slots_ref
  14.4 0.9 pad_maximum_fusion.1.others_ref
  15.4 4.5 %standardise_low.1 = (bf16[528,256]{1,0:T(8,128)(2,1)}, bf16[528,256]{1,0:T(8,128)(2,1)}, bf16[528,256]{1,0:T(8,128)(2,1)}, bf16[528,256]{1,0:T(8,128)(2,1)}) custom-call(s32[4]{0:T(128)S(1)} %iota_xor_fusion.sources_ref, f32[64,32,256]{2,1,0:T(8,128)S(1)} %copy-done.1, f32[64,32,256]{2,1,0:T(8,128)S(1)} %copy-done.1), custom_call_target="tpu_custom_call" | custom-call | flops 4000000000 | bytes 4000000 | tf_op jit(solution)/shard_map/standardise_low/pallas_call | solution.py:175
  19.9 0.0 collective-permute-done.rest_1_
  19.9 1.7 %collective-permute-done.1.rest_2_ = bf16[8,64,256]{2,1,0:T(8,128)(2,1)S(1)} collective-permute-done((bf16[8,64,256]{2,1,0:T(8,128)(2,1)}, bf16[8,64,256]{2,1,0:T(8,128)(2,1)S(1)}, u32[]{:S(2)}, u32[]{:S(2)}) %collective-permute-start.1) | collective-permute-done | bytes 262176 | tf_op jit(solution)/shard_map/ppermute | solution.py:728
  21.7 0.0 collective-permute-done.2.rest_3_
  21.7 1.2 collective-permute-start.3
  22.9 0.9 collective-permute-start.4
  23.8 1.4 %collective-permute-start.5 = (bf16[528,256]{1,0:T(8,128)(2,1)}, bf16[528,256]{1,0:T(8,128)(2,1)S(1)}, u32[]{:S(2)}, u32[]{:S(2)}) collective-permute-start(bf16[528,256]{1,0:T(8,128)(2,1)} %get-tuple-element.76), channel_id=1, source_target_pairs={{0,24},{8,16},{16,8},{24,0},{1,25},{9,17},{17,9},{25,1},{2,26},{10... | collective-permute-start | bytes 811016 | tf_op jit(solution)/shard_map/ppermute | solution.py:728
  25.2 8.3 %attention.1.turned_ref = bf16[8,256,256]{2,1,0:T(8,128)(2,1)S(1)} custom-call(bf16[256,256]{1,0:T(8,128)(2,1)S(1)} %slice.6.key_ref, bf16[768,256]{1,0:T(8,128)(2,1)S(1)} %pad_maximum_fusion.1.others_ref, bf16[8,64,256]{2,1,0:T(8,128)(2,1)S(1)} %copy-done.7, bf16[8,64,256]{2,1,0:T(8,128)(2,1)S(1)} %collective-permute-done.rest_1_, ...), custom_call_target="tpu_custom_call" | custom-call | flops 10000000000 | bytes 10000000 | tf_op jit(solution)/shard_map/attention/pallas_call | solution.py:253
  33.5 0.0 collective-permute-done.3.rest_5_.rest_9_
  33.5 2.5 %collective-permute-done.4.rest_6_.rest_10_ = bf16[528,256]{1,0:T(8,128)(2,1)S(1)} collective-permute-done((bf16[528,256]{1,0:T(8,128)(2,1)}, bf16[528,256]{1,0:T(8,128)(2,1)S(1)}, u32[]{:S(2)}, u32[]{:S(2)}) %collective-permute-start.4) | collective-permute-done | bytes 270368 | tf_op jit(solution)/shard_map/ppermute | solution.py:728
  36.0 0.0 collective-permute-done.5.rest_7_.rest_11_
  36.0 4.4 %alignment.1 = (bf16[256,256]{1,0:T(8,128)(2,1)S(1)}, bf16[8,32,256]{2,1,0:T(8,128)(2,1)S(1)}) custom-call(s32[4]{0:T(128)S(1)} %iota_xor_fusion.sources_ref, bf16[8,256,256]{2,1,0:T(8,128)(2,1)S(1)} %attention.1.turned_ref, bf16[256,256]{1,0:T(8,128)(2,1)S(1)} %bitcast.28, bf16[64,256]{1,0:T(8,128)(2,1)S(1)} %bitcast.30, bf16[8,64,256]{2,1,0:T(8,128)(2,1)S(1)} %copy-done.7, ...), custom_call_target="tpu_custom_call" | custom-call | flops 4000000000 | bytes 4000000 | tf_op jit(solution)/shard_map/alignment/pallas_call | solution.py:360
  40.4 0.6 collective-permute-start.8
  41.0 1.2 collective-permute-start.11
  42.2 1.7 %collective-permute-start.12 = (bf16[8,32,256]{2,1,0:T(8,128)(2,1)S(1)}, bf16[8,32,256]{2,1,0:T(8,128)(2,1)S(1)}, u32[]{:S(2)}, u32[]{:S(2)}) collective-permute-start(bf16[8,32,256]{2,1,0:T(8,128)(2,1)S(1)} %get-tuple-element.82.rest_8_), channel_id=1, source_target_pairs={{0,24},{8,16},{16,8},{24,0},{1,25},{9,17},{17,9},{25,1},{2,26},{10... | collective-permute-start | bytes 393224 | tf_op jit(solution)/shard_map/ppermute | solution.py:728
  43.9 0.8 collective-permute-start.6
  44.7 3.3 %collective-permute-start.7 = (bf16[256,256]{1,0:T(8,128)(2,1)S(1)}, bf16[256,256]{1,0:T(8,128)(2,1)S(1)}, u32[]{:S(2)}, u32[]{:S(2)}) collective-permute-start(bf16[256,256]{1,0:T(8,128)(2,1)S(1)} %get-tuple-element.79), channel_id=1, source_target_pairs={{0,2},{1,3},{2,10},{3,11},{4,18},{5,19},{6,26},{7,27},{8,4},{9,5},... | collective-permute-start | bytes 393224 | tf_op jit(solution)/shard_map/ppermute | solution.py:689
  48.1 0.0 collective-permute-done.8.rest_9_
  48.1 5.4 %collective-permute-start.10 = (bf16[256,256]{1,0:T(8,128)(2,1)S(1)}, bf16[256,256]{1,0:T(8,128)(2,1)S(1)}, u32[]{:S(2)}, u32[]{:S(2)}) collective-permute-start(bf16[256,256]{1,0:T(8,128)(2,1)S(1)} %get-tuple-element.79), channel_id=1, source_target_pairs={{0,6},{1,7},{2,14},{3,15},{4,22},{5,23},{6,30},{7,31},{8,0},{9,1},... | collective-permute-start | bytes 393224 | tf_op jit(solution)/shard_map/ppermute | solution.py:689
  53.5 0.0 collective-permute-done.11.rest_10_
  53.5 0.0 collective-permute-start.9
  53.5 0.1 collective-permute-start.13
  53.6 1.4 %collective-permute-done.7.rest_1_ = bf16[256,256]{1,0:T(8,128)(2,1)S(1)} collective-permute-done((bf16[256,256]{1,0:T(8,128)(2,1)S(1)}, bf16[256,256]{1,0:T(8,128)(2,1)S(1)}, u32[]{:S(2)}, u32[]{:S(2)}) %collective-permute-start.7) | collective-permute-done | bytes 131104 | tf_op jit(solution)/shard_map/ppermute | solution.py:689
  55.0 1.1 collective-permute-done.10.rest_3_
  56.0 0.0 collective-permute-start.16
  56.0 2.4 %collective-permute-done.9.rest_2_ = bf16[256,256]{1,0:T(8,128)(2,1)S(1)} collective-permute-done((bf16[256,256]{1,0:T(8,128)(2,1)S(1)}, bf16[256,256]{1,0:T(8,128)(2,1)S(1)}, u32[]{:S(2)}, u32[]{:S(2)}) %collective-permute-start.9) | collective-permute-done | bytes 131104 | tf_op jit(solution)/shard_map/ppermute | solution.py:689
  58.5 0.0 collective-permute-start.15
  58.5 1.7 %turn_back.1 = (bf16[8,64,256]{2,1,0:T(8,128)(2,1)}, bf16[8,64,256]{2,1,0:T(8,128)(2,1)}, bf16[8,64,256]{2,1,0:T(8,128)(2,1)}, bf16[8,64,256]{2,1,0:T(8,128)(2,1)}) custom-call(bf16[8,256,256]{2,1,0:T(8,128)(2,1)S(1)} %attention.1.turned_ref), custom_call_target="tpu_custom_call" | custom-call | flops 2000000000 | bytes 2000000 | tf_op jit(solution)/shard_map/turn_back/pallas_call | solution.py:284
  60.2 8.7 %pair_update.1 = (f32[32,64,128]{2,1,0:T(8,128)}, f32[32,64,128]{2,1,0:T(8,128)}, bf16[128,32,128]{2,1,0:T(8,128)(2,1)}) custom-call(s32[8]{0:T(128)S(1)} %pad_add_fusion.left_slots_ref, s32[4]{0:T(128)S(1)} %broadcast_multiply_fusion.right_firsts_ref, bf16[256,256]{1,0:T(8,128)(2,1)S(1)} %collective-permute-done.6.rest_0_, ...), custom_call_target="tpu_custom_call" | custom-call | flops 12000000000 | bytes 12000000 | tf_op jit(solution)/shard_map/pair_update/pallas_call | solution.py:527
  68.9 6.4 %all-to-all-start = ((bf16[32,4,32,128]{3,2,1,0:T(8,128)(2,1)}), bf16[32,4,32,128]{3,2,1,0:T(8,128)(2,1)S(1)}, u32[]{:S(2)}, u32[]{:S(2)}) async-start(bf16[32,4,32,128]{3,2,1,0:T(8,128)(2,1)} %bitcast.33), calls=%async_computation | async-start | bytes 2097152 | tf_op jit(solution)/shard_map/all_to_all | solution.py:798
  75.3 0.0 copy-start.11
  75.3 1.8 %collective-permute-start.17 = (bf16[8,64,256]{2,1,0:T(8,128)(2,1)}, bf16[8,64,256]{2,1,0:T(8,128)(2,1)S(1)}, u32[]{:S(2)}, u32[]{:S(2)}) collective-permute-start(bf16[8,64,256]{2,1,0:T(8,128)(2,1)} %get-tuple-element.89), channel_id=1, source_target_pairs={{0,8},{8,0},{16,24},{24,16},{1,9},{9,1},{17,25},{25,17},{2,10},{10... | collective-permute-start | bytes 786440 | tf_op jit(solution)/shard_map/ppermute | solution.py:728
  77.1 1.5 %collective-permute-start.18 = (bf16[8,64,256]{2,1,0:T(8,128)(2,1)}, bf16[8,64,256]{2,1,0:T(8,128)(2,1)S(1)}, u32[]{:S(2)}, u32[]{:S(2)}) collective-permute-start(bf16[8,64,256]{2,1,0:T(8,128)(2,1)} %get-tuple-element.90), channel_id=1, source_target_pairs={{0,16},{8,24},{16,0},{24,8},{1,17},{9,25},{17,1},{25,9},{2,18},{10... | collective-permute-start | bytes 786440 | tf_op jit(solution)/shard_map/ppermute | solution.py:728
  78.6 0.3 collective-permute-start.19
  78.9 13.7 %collective-permute-done.17 = bf16[8,64,256]{2,1,0:T(8,128)(2,1)S(1)} collective-permute-done((bf16[8,64,256]{2,1,0:T(8,128)(2,1)}, bf16[8,64,256]{2,1,0:T(8,128)(2,1)S(1)}, u32[]{:S(2)}, u32[]{:S(2)}) %collective-permute-start.17) | collective-permute-done | bytes 262176 | tf_op jit(solution)/shard_map/ppermute | solution.py:728
  92.6 0.7 copy-done.12
  93.3 0.7 copy-done.13
  94.0 6.9 %collective-permute-done.19 = bf16[8,64,256]{2,1,0:T(8,128)(2,1)} collective-permute-done((bf16[8,64,256]{2,1,0:T(8,128)(2,1)}, bf16[8,64,256]{2,1,0:T(8,128)(2,1)}, u32[]{:S(2)}, u32[]{:S(2)}) %collective-permute-start.19) | collective-permute-done | bytes 262176 | tf_op jit(solution)/shard_map/ppermute | solution.py:728
  100.9 1.9 %all-to-all-done.sides_ref = bf16[32,4,32,128]{3,2,1,0:T(8,128)(2,1)S(1)} async-done(((bf16[32,4,32,128]{3,2,1,0:T(8,128)(2,1)}), bf16[32,4,32,128]{3,2,1,0:T(8,128)(2,1)S(1)}, u32[]{:S(2)}, u32[]{:S(2)}) %all-to-all-start) | async-done | bytes 1048608 | tf_op jit(solution)/shard_map/all_to_all | solution.py:798
  102.9 1.7 %triangle_product.1 = bf16[32,4,16,128]{3,2,1,0:T(8,128)(2,1)} custom-call(bf16[32,4,32,128]{3,2,1,0:T(8,128)(2,1)S(1)} %all-to-all-done.sides_ref), custom_call_target="tpu_custom_call" | custom-call | flops 3000000000 | bytes 3000000 | tf_op jit(solution)/shard_map/triangle_product/pallas_call | solution.py:591
  104.5 3.0 %all-to-all-start.1 = ((bf16[32,4,16,128]{3,2,1,0:T(8,128)(2,1)}), bf16[32,4,16,128]{3,2,1,0:T(8,128)(2,1)S(1)}, u32[]{:S(2)}, u32[]{:S(2)}) async-start(bf16[32,4,16,128]{3,2,1,0:T(8,128)(2,1)} %triangle_product.1), calls=%async_computation.1 | async-start | bytes 1048576 | tf_op jit(solution)/shard_map/all_to_all | solution.py:801
  107.6 0.1 broadcast_in_dim.14
  107.7 0.1 broadcast_in_dim.15
  107.8 0.0 copy-start.9
  107.8 2.2 %pad_maximum_fusion = bf16[4,8,64,256]{3,2,1,0:T(8,128)(2,1)} fusion(bf16[1,8,64,256]{3,2,1,0:T(8,128)(2,1)} %bitcast.10, bf16[1,8,64,256]{3,2,1,0:T(8,128)(2,1)} %bitcast.38, bf16[1,8,64,256]{3,2,1,0:T(8,128)(2,1)} %bitcast.37, bf16[1,8,64,256]{3,2,1,0:T(8,128)(2,1)S(1)} %bitcast.36), kind=kLoop, calls=%fused_computation.2 | loop fusion | flops 1572864 | bytes 2097152 | tf_op jit(solution)/shard_map/stack | solution.py:803
  110.0 2.8 %gather_fusion = bf16[4,8,64,256]{3,2,1,0:T(8,128)(2,1)} fusion(bf16[4,8,64,256]{3,2,1,0:T(8,128)(2,1)} %pad_maximum_fusion, s32[1024]{0:T(1024)S(1)} %pad_clamp_fusion), kind=kCustom, calls=%fused_computation | custom fusion | bytes 2097168 | tf_op jit(solution)/shard_map/jit(_take)/gather | solution.py:803
  112.9 3.4 %convolution_add_fusion = f32[64,32,256]{2,1,0:T(8,128)} fusion(f32[64,32,256]{2,1,0:T(8,128)S(1)} %copy-done.1, bf16[32,64,256]{2,1,0:T(8,128)(2,1)} %bitcast.31, pred[32]{0:T(512)(128)(4,1)S(1)} %broadcast_in_dim.15, bf16[256,256]{1,0:T(8,128)(2,1)S(1)} %copy-done.9), kind=kOutput, calls=%fused_computation.1 | convolution fusion | flops 269484032 | bytes 5373984 | tf_op jit(solution)/shard_map/dot_general | solution.py:805
  116.3 7.7 %all-to-all-done.1 = bf16[32,4,16,128]{3,2,1,0:T(8,128)(2,1)S(1)} async-done(((bf16[32,4,16,128]{3,2,1,0:T(8,128)(2,1)}), bf16[32,4,16,128]{3,2,1,0:T(8,128)(2,1)S(1)}, u32[]{:S(2)}, u32[]{:S(2)}) %all-to-all-start.1) | async-done | bytes 524320 | tf_op jit(solution)/shard_map/all_to_all | solution.py:801
  123.9 2.8 %pair_result.1 = f32[64,32,128]{2,1,0:T(8,128)} custom-call(bf16[128,16,128]{2,1,0:T(8,128)(2,1)S(1)} %bitcast.26, bf16[128,128]{1,0:T(8,128)(2,1)S(1)} %copy-done.6, f32[32,64,128]{2,1,0:T(8,128)} %get-tuple-element.98.mid_hbm, f32[32,64,128]{2,1,0:T(8,128)} %get-tuple-element.99.gate_hbm), custom_call_target="tpu_custom_call" | custom-call | flops 3000000000 | bytes 3000000 | tf_op jit(solution)/shard_map/pair_result/pallas_call | solution.py:649
  (39 shorter events, 0.1 us)
Async XLA Ops:
  0.6 1.6 %copy-start = (f32[64,32,256]{2,1,0:T(8,128)S(1)}, f32[64,32,256]{2,1,0:T(8,128)}, u32[]{:S(2)}) copy-start(f32[64,32,256]{2,1,0:T(8,128)} %second_ref.3) | copy-start | bytes 6291460
  2.2 7.4 %copy-start.10 = (bf16[256,768]{1,0:T(8,128)(2,1)S(1)}, bf16[256,768]{1,0:T(8,128)(2,1)}, u32[]{:S(2)}) copy-start(bf16[256,768]{1,0:T(8,128)(2,1)} %param.13) | copy-start | bytes 1179652
  2.2 9.2 %copy-start.14 = (bf16[256,256]{1,0:T(8,128)(2,1)S(1)}, bf16[256,256]{1,0:T(8,128)(2,1)}, u32[]{:S(2)}) copy-start(bf16[256,256]{1,0:T(8,128)(2,1)} %param.12) | copy-start | bytes 393220
  5.1 10.3 %copy-start.1 = (f32[64,32,256]{2,1,0:T(8,128)S(1)}, f32[64,32,256]{2,1,0:T(8,128)}, u32[]{:S(2)}) copy-start(f32[64,32,256]{2,1,0:T(8,128)} %second_ref.3) | copy-start | bytes 6291460
  5.1 14.9 %collective-permute-start = (bf16[8,64,256]{2,1,0:T(8,128)(2,1)}, bf16[8,64,256]{2,1,0:T(8,128)(2,1)S(1)}, u32[]{:S(2)}, u32[]{:S(2)}) collective-permute-start(bf16[8,64,256]{2,1,0:T(8,128)(2,1)} %get-tuple-element.52), channel_id=1, source_target_pairs={{0,8},{8,0},{16,24},{24,16},{1,9},{9,1},{17,25},{25,17},{2,10},{10... | collective-permute-start | bytes 786440 | tf_op jit(solution)/shard_map/ppermute | solution.py:728
  8.1 13.6 %collective-permute-start.1 = (bf16[8,64,256]{2,1,0:T(8,128)(2,1)}, bf16[8,64,256]{2,1,0:T(8,128)(2,1)S(1)}, u32[]{:S(2)}, u32[]{:S(2)}) collective-permute-start(bf16[8,64,256]{2,1,0:T(8,128)(2,1)} %get-tuple-element.53), channel_id=1, source_target_pairs={{0,16},{8,24},{16,0},{24,8},{1,17},{9,25},{17,1},{25,9},{2,18},{10... | collective-permute-start | bytes 786440 | tf_op jit(solution)/shard_map/ppermute | solution.py:728
  9.6 12.1 %collective-permute-start.2 = (bf16[8,64,256]{2,1,0:T(8,128)(2,1)}, bf16[8,64,256]{2,1,0:T(8,128)(2,1)S(1)}, u32[]{:S(2)}, u32[]{:S(2)}) collective-permute-start(bf16[8,64,256]{2,1,0:T(8,128)(2,1)} %get-tuple-element.54), channel_id=1, source_target_pairs={{0,24},{8,16},{16,8},{24,0},{1,25},{9,17},{17,9},{25,1},{2,26},{10... | collective-permute-start | bytes 786440 | tf_op jit(solution)/shard_map/ppermute | solution.py:728
  15.4 9.8 %copy-start.7 = (bf16[8,64,256]{2,1,0:T(8,128)(2,1)S(1)}, bf16[8,64,256]{2,1,0:T(8,128)(2,1)}, u32[]{:S(2)}) copy-start(bf16[8,64,256]{2,1,0:T(8,128)(2,1)} %get-tuple-element.61.rest_0_) | copy-start | bytes 786436
  21.7 14.3 %copy-start.4 = (bf16[256,64]{0,1:T(8,128)(2,1)S(1)}, bf16[256,64]{0,1:T(8,128)(2,1)}, u32[]{:S(2)}) copy-start(bf16[256,64]{0,1:T(8,128)(2,1)} %param.15) | copy-start | bytes 98308
  21.7 14.3 %copy-start.8 = (bf16[528,256]{1,0:T(8,128)(2,1)S(1)}, bf16[528,256]{1,0:T(8,128)(2,1)}, u32[]{:S(2)}) copy-start(bf16[528,256]{1,0:T(8,128)(2,1)} %get-tuple-element.73.rest_4_.rest_8_) | copy-start | bytes 811012
  21.7 11.8 %collective-permute-start.3 = (bf16[528,256]{1,0:T(8,128)(2,1)}, bf16[528,256]{1,0:T(8,128)(2,1)S(1)}, u32[]{:S(2)}, u32[]{:S(2)}) collective-permute-start(bf16[528,256]{1,0:T(8,128)(2,1)} %get-tuple-element.74), channel_id=1, source_target_pairs={{0,8},{8,0},{16,24},{24,16},{1,9},{9,1},{17,25},{25,17},{2,10},{10... | collective-permute-start | bytes 811016 | tf_op jit(solution)/shard_map/ppermute | solution.py:728
  22.9 13.1 %collective-permute-start.4 = (bf16[528,256]{1,0:T(8,128)(2,1)}, bf16[528,256]{1,0:T(8,128)(2,1)S(1)}, u32[]{:S(2)}, u32[]{:S(2)}) collective-permute-start(bf16[528,256]{1,0:T(8,128)(2,1)} %get-tuple-element.75), channel_id=1, source_target_pairs={{0,16},{8,24},{16,0},{24,8},{1,17},{9,25},{17,1},{25,9},{2,18},{10... | collective-permute-start | bytes 811016 | tf_op jit(solution)/shard_map/ppermute | solution.py:728
  23.8 12.2 %collective-permute-start.5 = (bf16[528,256]{1,0:T(8,128)(2,1)}, bf16[528,256]{1,0:T(8,128)(2,1)S(1)}, u32[]{:S(2)}, u32[]{:S(2)}) collective-permute-start(bf16[528,256]{1,0:T(8,128)(2,1)} %get-tuple-element.76), channel_id=1, source_target_pairs={{0,24},{8,16},{16,8},{24,0},{1,25},{9,17},{17,9},{25,1},{2,26},{10... | collective-permute-start | bytes 811016 | tf_op jit(solution)/shard_map/ppermute | solution.py:728
  40.4 7.7 %collective-permute-start.8 = (bf16[8,32,256]{2,1,0:T(8,128)(2,1)S(1)}, bf16[8,32,256]{2,1,0:T(8,128)(2,1)S(1)}, u32[]{:S(2)}, u32[]{:S(2)}) collective-permute-start(bf16[8,32,256]{2,1,0:T(8,128)(2,1)S(1)} %get-tuple-element.82.rest_8_), channel_id=1, source_target_pairs={{0,8},{8,0},{16,24},{24,16},{1,9},{9,1},{17,25},{25,17},{2,10},{10... | collective-permute-start | bytes 393224 | tf_op jit(solution)/shard_map/ppermute | solution.py:728
  41.0 12.5 %collective-permute-start.11 = (bf16[8,32,256]{2,1,0:T(8,128)(2,1)S(1)}, bf16[8,32,256]{2,1,0:T(8,128)(2,1)S(1)}, u32[]{:S(2)}, u32[]{:S(2)}) collective-permute-start(bf16[8,32,256]{2,1,0:T(8,128)(2,1)S(1)} %get-tuple-element.82.rest_8_), channel_id=1, source_target_pairs={{0,16},{8,24},{16,0},{24,8},{1,17},{9,25},{17,1},{25,9},{2,18},{10... | collective-permute-start | bytes 393224 | tf_op jit(solution)/shard_map/ppermute | solution.py:728
  42.2 12.8 %collective-permute-start.12 = (bf16[8,32,256]{2,1,0:T(8,128)(2,1)S(1)}, bf16[8,32,256]{2,1,0:T(8,128)(2,1)S(1)}, u32[]{:S(2)}, u32[]{:S(2)}) collective-permute-start(bf16[8,32,256]{2,1,0:T(8,128)(2,1)S(1)} %get-tuple-element.82.rest_8_), channel_id=1, source_target_pairs={{0,24},{8,16},{16,8},{24,0},{1,25},{9,17},{17,9},{25,1},{2,26},{10... | collective-permute-start | bytes 393224 | tf_op jit(solution)/shard_map/ppermute | solution.py:728
  43.9 16.3 %copy-start.2 = (f32[64,32,128]{2,1,0:T(8,128)S(1)}, f32[64,32,128]{2,1,0:T(8,128)}, u32[]{:S(2)}) copy-start(f32[64,32,128]{2,1,0:T(8,128)} %param.11) | copy-start | bytes 3145732
  43.9 16.3 %copy-start.3 = (bf16[1024,128]{1,0:T(8,128)(2,1)S(1)}, bf16[1024,128]{1,0:T(8,128)(2,1)}, u32[]{:S(2)}) copy-start(bf16[1024,128]{1,0:T(8,128)(2,1)} %rest_12_.1) | copy-start | bytes 786436
  43.9 16.3 %copy-start.5 = (bf16[128,128]{1,0:T(8,128)(2,1)S(1)}, bf16[128,128]{1,0:T(8,128)(2,1)}, u32[]{:S(2)}) copy-start(bf16[128,128]{1,0:T(8,128)(2,1)} %rest_14_.1) | copy-start | bytes 98308
  43.9 9.6 %collective-permute-start.6 = (bf16[256,256]{1,0:T(8,128)(2,1)S(1)}, bf16[256,256]{1,0:T(8,128)(2,1)S(1)}, u32[]{:S(2)}, u32[]{:S(2)}) collective-permute-start(bf16[256,256]{1,0:T(8,128)(2,1)S(1)} %get-tuple-element.79), channel_id=1, source_target_pairs={{0,0},{1,1},{2,8},{3,9},{4,16},{5,17},{6,24},{7,25},{8,2},{9,3},{1... | collective-permute-start | bytes 393224 | tf_op jit(solution)/shard_map/ppermute | solution.py:689
  44.7 10.2 %collective-permute-start.7 = (bf16[256,256]{1,0:T(8,128)(2,1)S(1)}, bf16[256,256]{1,0:T(8,128)(2,1)S(1)}, u32[]{:S(2)}, u32[]{:S(2)}) collective-permute-start(bf16[256,256]{1,0:T(8,128)(2,1)S(1)} %get-tuple-element.79), channel_id=1, source_target_pairs={{0,2},{1,3},{2,10},{3,11},{4,18},{5,19},{6,26},{7,27},{8,4},{9,5},... | collective-permute-start | bytes 393224 | tf_op jit(solution)/shard_map/ppermute | solution.py:689
  48.1 7.9 %collective-permute-start.10 = (bf16[256,256]{1,0:T(8,128)(2,1)S(1)}, bf16[256,256]{1,0:T(8,128)(2,1)S(1)}, u32[]{:S(2)}, u32[]{:S(2)}) collective-permute-start(bf16[256,256]{1,0:T(8,128)(2,1)S(1)} %get-tuple-element.79), channel_id=1, source_target_pairs={{0,6},{1,7},{2,14},{3,15},{4,22},{5,23},{6,30},{7,31},{8,0},{9,1},... | collective-permute-start | bytes 393224 | tf_op jit(solution)/shard_map/ppermute | solution.py:689
  53.5 5.0 %collective-permute-start.9 = (bf16[256,256]{1,0:T(8,128)(2,1)S(1)}, bf16[256,256]{1,0:T(8,128)(2,1)S(1)}, u32[]{:S(2)}, u32[]{:S(2)}) collective-permute-start(bf16[256,256]{1,0:T(8,128)(2,1)S(1)} %get-tuple-element.79), channel_id=1, source_target_pairs={{0,4},{1,5},{2,12},{3,13},{4,20},{5,21},{6,28},{7,29},{8,6},{9,7},... | collective-permute-start | bytes 393224 | tf_op jit(solution)/shard_map/ppermute | solution.py:689
  53.5 6.7 %collective-permute-start.13 = (bf16[256,256]{1,0:T(8,128)(2,1)S(1)}, bf16[256,256]{1,0:T(8,128)(2,1)S(1)}, u32[]{:S(2)}, u32[]{:S(2)}) collective-permute-start(bf16[256,256]{1,0:T(8,128)(2,1)S(1)} %collective-permute-done.6.rest_0_), channel_id=1, source_target_pairs={{0,1},{1,0},{2,3},{3,2},{4,5},{5,4},{6,7},{7,6},{8,9},{9,8},{10,11... | collective-permute-start | bytes 393224 | tf_op jit(solution)/shard_map/ppermute | solution.py:675
  54.9 5.2 %collective-permute-start.14 = (bf16[256,256]{1,0:T(8,128)(2,1)S(1)}, bf16[256,256]{1,0:T(8,128)(2,1)S(1)}, u32[]{:S(2)}, u32[]{:S(2)}) collective-permute-start(bf16[256,256]{1,0:T(8,128)(2,1)S(1)} %collective-permute-done.7.rest_1_), channel_id=1, source_target_pairs={{0,1},{1,0},{2,3},{3,2},{4,5},{5,4},{6,7},{7,6},{8,9},{9,8},{10,11... | collective-permute-start | bytes 393224 | tf_op jit(solution)/shard_map/ppermute | solution.py:675
  56.0 4.2 %collective-permute-start.16 = (bf16[256,256]{1,0:T(8,128)(2,1)S(1)}, bf16[256,256]{1,0:T(8,128)(2,1)S(1)}, u32[]{:S(2)}, u32[]{:S(2)}) collective-permute-start(bf16[256,256]{1,0:T(8,128)(2,1)S(1)} %collective-permute-done.10.rest_3_), channel_id=1, source_target_pairs={{0,1},{1,0},{2,3},{3,2},{4,5},{5,4},{6,7},{7,6},{8,9},{9,8},{10,11... | collective-permute-start | bytes 393224 | tf_op jit(solution)/shard_map/ppermute | solution.py:675
  58.5 1.7 %collective-permute-start.15 = (bf16[256,256]{1,0:T(8,128)(2,1)S(1)}, bf16[256,256]{1,0:T(8,128)(2,1)S(1)}, u32[]{:S(2)}, u32[]{:S(2)}) collective-permute-start(bf16[256,256]{1,0:T(8,128)(2,1)S(1)} %collective-permute-done.9.rest_2_), channel_id=1, source_target_pairs={{0,1},{1,0},{2,3},{3,2},{4,5},{5,4},{6,7},{7,6},{8,9},{9,8},{10,11... | collective-permute-start | bytes 393224 | tf_op jit(solution)/shard_map/ppermute | solution.py:675
  68.9 34.0 %all-to-all-start = ((bf16[32,4,32,128]{3,2,1,0:T(8,128)(2,1)}), bf16[32,4,32,128]{3,2,1,0:T(8,128)(2,1)S(1)}, u32[]{:S(2)}, u32[]{:S(2)}) async-start(bf16[32,4,32,128]{3,2,1,0:T(8,128)(2,1)} %bitcast.33), calls=%async_computation | async-start | bytes 2097152 | tf_op jit(solution)/shard_map/all_to_all | solution.py:798
  75.3 32.5 %copy-start.11 = (bf16[8,64,256]{2,1,0:T(8,128)(2,1)S(1)}, bf16[8,64,256]{2,1,0:T(8,128)(2,1)}, u32[]{:S(2)}) copy-start(bf16[8,64,256]{2,1,0:T(8,128)(2,1)} %get-tuple-element.93) | copy-start | bytes 786436
  75.3 17.3 %collective-permute-start.17 = (bf16[8,64,256]{2,1,0:T(8,128)(2,1)}, bf16[8,64,256]{2,1,0:T(8,128)(2,1)S(1)}, u32[]{:S(2)}, u32[]{:S(2)}) collective-permute-start(bf16[8,64,256]{2,1,0:T(8,128)(2,1)} %get-tuple-element.89), channel_id=1, source_target_pairs={{0,8},{8,0},{16,24},{24,16},{1,9},{9,1},{17,25},{25,17},{2,10},{10... | collective-permute-start | bytes 786440 | tf_op jit(solution)/shard_map/ppermute | solution.py:728
  77.1 15.4 %collective-permute-start.18 = (bf16[8,64,256]{2,1,0:T(8,128)(2,1)}, bf16[8,64,256]{2,1,0:T(8,128)(2,1)S(1)}, u32[]{:S(2)}, u32[]{:S(2)}) collective-permute-start(bf16[8,64,256]{2,1,0:T(8,128)(2,1)} %get-tuple-element.90), channel_id=1, source_target_pairs={{0,16},{8,24},{16,0},{24,8},{1,17},{9,25},{17,1},{25,9},{2,18},{10... | collective-permute-start | bytes 786440 | tf_op jit(solution)/shard_map/ppermute | solution.py:728
  78.6 22.4 %collective-permute-start.19 = (bf16[8,64,256]{2,1,0:T(8,128)(2,1)}, bf16[8,64,256]{2,1,0:T(8,128)(2,1)}, u32[]{:S(2)}, u32[]{:S(2)}) collective-permute-start(bf16[8,64,256]{2,1,0:T(8,128)(2,1)} %get-tuple-element.91), channel_id=1, source_target_pairs={{0,24},{8,16},{16,8},{24,0},{1,25},{9,17},{17,9},{25,1},{2,26},{10... | collective-permute-start | bytes 786440 | tf_op jit(solution)/shard_map/ppermute | solution.py:728
  92.6 0.7 copy-start.12
  93.3 0.7 copy-start.13
  104.5 19.4 %all-to-all-start.1 = ((bf16[32,4,16,128]{3,2,1,0:T(8,128)(2,1)}), bf16[32,4,16,128]{3,2,1,0:T(8,128)(2,1)S(1)}, u32[]{:S(2)}, u32[]{:S(2)}) async-start(bf16[32,4,16,128]{3,2,1,0:T(8,128)(2,1)} %triangle_product.1), calls=%async_computation.1 | async-start | bytes 1048576 | tf_op jit(solution)/shard_map/all_to_all | solution.py:801
  107.8 5.1 %copy-start.9 = (bf16[256,256]{1,0:T(8,128)(2,1)S(1)}, bf16[256,256]{1,0:T(8,128)(2,1)}, u32[]{:S(2)}) copy-start(bf16[256,256]{1,0:T(8,128)(2,1)} %param.14) | copy-start | bytes 393220
  112.9 11.1 %copy-start.6 = (bf16[128,128]{1,0:T(8,128)(2,1)S(1)}, bf16[128,128]{1,0:T(8,128)(2,1)}, u32[]{:S(2)}) copy-start(bf16[128,128]{1,0:T(8,128)(2,1)} %final_ref.1) | copy-start | bytes 98308

commit v17 on v14

--- a/solution.py
+++ b/solution.py
@@ -213,13 +213,8 @@
     def score(unit):
         n, h = units[unit]
         key_rows, queries, _, _ = columns[n]
-        low, high = h * UNIT_WIDTH, (h + 1) * UNIT_WIDTH
-        pieces = [queries[low:high]]
-        if low > 0:
-            pieces.insert(0, jnp.zeros((low, total), BF16))
-        if high < inner:
-            pieces.append(jnp.zeros((inner - high, total), BF16))
-        scores_ref[unit % ring] = matmul(key_rows, jnp.concatenate(pieces, axis=0))
+        rows = slice(h * UNIT_WIDTH, (h + 1) * UNIT_WIDTH)
+        scores_ref[unit % ring] = matmul(key_rows[:, rows], queries[rows])
 
     def weigh(unit):
         for low in range(0, total, 128):
@@ -751,7 +746,6 @@
     own_residues = residues // row_count
     sources = lax.axis_index("row") ^ jnp.arange(row_count, dtype=jnp.int32)
     high = exchange_rows(standardise_high(sources, homolog_tensor))
-    low = standardise_low(sources, homolog_tensor)
     others = jnp.concatenate(
         [attention_probe_matrix.T, attention_extra_matrices[:, inner:].T], axis=0
     )
@@ -764,11 +758,14 @@
         sources * own_residues,
         left_groups(row_count, own_residues),
     )
-    high, low, early = lax.optimization_barrier((high, low, early))
+    after, early = lax.optimization_barrier((sources, early))
+    low = standardise_low(after, homolog_tensor)
+    high, _, early = lax.optimization_barrier((high, low, early))
     key_matrix, others, final_turned, tensor_turned, entries, firsts, slots = early
     low = exchange_rows(low)
     turned = attention(high, key_matrix, others)
     gated = turn_back(turned, row_count)
+    low, gated = lax.optimization_barrier((low, gated))
     left_piece, right_piece = alignment(
         sources, high, low, turned, final_turned, tensor_turned
     )

time: 127 us -> 126 us (level)
  waiting for transfers between devices: 39.2 us -> 37.9 us
    ppermute x12, waiting for transfers between devices: 24.8 us -> 22.1 us  [exchange_rows(): arrived.append(lax.ppermute(pieces[shift], 'row', moves))]
    ppermute x4, waiting for transfers between devices: 0.01 us -> 1.33 us  [swap_cores(): return lax.ppermute(block, 'col', [(c, c ^ 1) for c in range(count)])]
where the time goes in v17:
time: 126 us
  waiting for transfers between devices  37.9 us (30%)
  Pallas kernels  36.1 us (29%)
  starting transfers between devices  34.8 us (28%)
  local copies, waits for them, and re-layouts  9.11 us (7%)
  matrix products  3.41 us (3%)
  other arithmetic  3.29 us (3%)
    ppermute x12, waiting for transfers between devices, exchange_rows(): arrived.append(lax.ppermute(pieces[shift], 'row', moves))  22.1 us
    ppermute x12, starting transfers between devices, exchange_rows(): arrived.append(lax.ppermute(pieces[shift], 'row', moves))  15.2 us
    ppermute x4, starting transfers between devices, gather_turned(): arrived.append(lax.ppermute(source, ('row', 'col'), moves))  10 us
    pallas_call x1, Pallas kernels, pair_update(): pl.pallas_call(functools.partial(pair_kernel, slots=len(left) // 2), in_s...  8.65 us
    pallas_call x1, Pallas kernels, attention(): pl.pallas_call(attention_kernel, grid=(residues // step,), in_specs=[pl.B...  8.34 us
    all_to_all x1, waiting for transfers between devices, body(): product = lax.all_to_all(product, everywhere, split_axis=0, concat_axis=0)  7.65 us
    all_to_all x1, starting transfers between devices, body(): sides = lax.all_to_all(sides, everywhere, split_axis=0, concat_axis=0)  6.48 us
    ppermute x4, waiting for transfers between devices, gather_turned(): arrived.append(lax.ppermute(source, ('row', 'col'), moves))  4.87 us
  transfers between devices with their start and end apart: 22, of which 9 were waited for; matrix products, arithmetic and copies ran while one was open for 11% of the time, Pallas kernels for 12%

profile of v17, /device:TPU:0, one launch (start us, length us, event | category | flops | bytes accessed | tf_op | source)
XLA Modules:
  0.0 125.7 jit_solution(5195929618635786264)
XLA Ops:
  0.6 0.0 copy-start.9
  0.7 0.0 copy-start.13
  0.7 4.5 %standardise_high.1 = (bf16[8,64,256]{2,1,0:T(8,128)(2,1)}, bf16[8,64,256]{2,1,0:T(8,128)(2,1)}, bf16[8,64,256]{2,1,0:T(8,128)(2,1)}, bf16[8,64,256]{2,1,0:T(8,128)(2,1)}) custom-call(s32[4]{0:T(128)S(1)} %get-tuple-element.63.sources_ref, f32[64,32,256]{2,1,0:T(8,128)} %block_hbm.1), custom_call_target="tpu_custom_call" | custom-call | flops 3000000000 | bytes 3000000 | tf_op jit(solution)/shard_map/standardise_high/pallas_call | solution.py:120
  5.1 0.0 copy-start
  5.1 3.0 %collective-permute-start.3 = (bf16[8,64,256]{2,1,0:T(8,128)(2,1)}, bf16[8,64,256]{2,1,0:T(8,128)(2,1)S(1)}, u32[]{:S(2)}, u32[]{:S(2)}) collective-permute-start(bf16[8,64,256]{2,1,0:T(8,128)(2,1)} %get-tuple-element.69), channel_id=1, source_target_pairs={{0,8},{8,0},{16,24},{24,16},{1,9},{9,1},{17,25},{25,17},{2,10},{10... | collective-permute-start | bytes 786440 | tf_op jit(solution)/shard_map/ppermute | solution.py:722
  8.1 1.5 %collective-permute-start.4 = (bf16[8,64,256]{2,1,0:T(8,128)(2,1)}, bf16[8,64,256]{2,1,0:T(8,128)(2,1)S(1)}, u32[]{:S(2)}, u32[]{:S(2)}) collective-permute-start(bf16[8,64,256]{2,1,0:T(8,128)(2,1)} %get-tuple-element.70), channel_id=1, source_target_pairs={{0,16},{8,24},{16,0},{24,8},{1,17},{9,25},{17,1},{25,9},{2,18},{10... | collective-permute-start | bytes 786440 | tf_op jit(solution)/shard_map/ppermute | solution.py:722
  9.7 0.0 collective-permute-start.5
  9.7 0.7 slice.7
  10.4 1.1 copy.17
  11.5 0.8 copy.12
  12.3 0.9 reshape.47
  13.2 0.1 copy.15
  13.4 1.0 copy.14
  14.4 0.1 pad_add_fusion.left_slots_ref
  14.5 0.9 pad_maximum_fusion.1.others_ref
  15.5 4.5 %standardise_low.1 = (bf16[528,256]{1,0:T(8,128)(2,1)}, bf16[528,256]{1,0:T(8,128)(2,1)}, bf16[528,256]{1,0:T(8,128)(2,1)}, bf16[528,256]{1,0:T(8,128)(2,1)}) custom-call(s32[4]{0:T(128)S(1)} %get-tuple-element.63.sources_ref, f32[64,32,256]{2,1,0:T(8,128)S(1)} %copy-done, f32[64,32,256]{2,1,0:T(8,128)S(1)} %copy-done), custom_call_target="tpu_custom_call" | custom-call | flops 4000000000 | bytes 4000000 | tf_op jit(solution)/shard_map/standardise_low/pallas_call | solution.py:174
  20.0 2.0 %collective-permute-start = (bf16[528,256]{1,0:T(8,128)(2,1)}, bf16[528,256]{1,0:T(8,128)(2,1)S(1)}, u32[]{:S(2)}, u32[]{:S(2)}) collective-permute-start(bf16[528,256]{1,0:T(8,128)(2,1)} %get-tuple-element.65), channel_id=1, source_target_pairs={{0,8},{8,0},{16,24},{24,16},{1,9},{9,1},{17,25},{25,17},{2,10},{10... | collective-permute-start | bytes 811016 | tf_op jit(solution)/shard_map/ppermute | solution.py:722
  22.0 1.5 %collective-permute-start.1 = (bf16[528,256]{1,0:T(8,128)(2,1)}, bf16[528,256]{1,0:T(8,128)(2,1)S(1)}, u32[]{:S(2)}, u32[]{:S(2)}) collective-permute-start(bf16[528,256]{1,0:T(8,128)(2,1)} %get-tuple-element.66), channel_id=1, source_target_pairs={{0,16},{8,24},{16,0},{24,8},{1,17},{9,25},{17,1},{25,9},{2,18},{10... | collective-permute-start | bytes 811016 | tf_op jit(solution)/shard_map/ppermute | solution.py:722
  23.5 0.0 collective-permute-done.3.rest_1_
  23.5 0.0 collective-permute-start.2
  23.6 0.0 collective-permute-done.4.rest_2_
  23.6 0.0 collective-permute-done.5.rest_3_
  23.6 8.3 %attention.1.turned_ref = bf16[8,256,256]{2,1,0:T(8,128)(2,1)S(1)} custom-call(bf16[256,256]{1,0:T(8,128)(2,1)S(1)} %slice.6.key_ref, bf16[768,256]{1,0:T(8,128)(2,1)S(1)} %pad_maximum_fusion.1.others_ref, bf16[8,64,256]{2,1,0:T(8,128)(2,1)S(1)} %copy-done.6, bf16[8,64,256]{2,1,0:T(8,128)(2,1)S(1)} %collective-permute-done.3.rest_1_, ...), custom_call_target="tpu_custom_call" | custom-call | flops 10000000000 | bytes 10000000 | tf_op jit(solution)/shard_map/attention/pallas_call | solution.py:252
  31.9 1.8 %turn_back.1 = (bf16[8,64,256]{2,1,0:T(8,128)(2,1)}, bf16[8,64,256]{2,1,0:T(8,128)(2,1)}, bf16[8,64,256]{2,1,0:T(8,128)(2,1)}, bf16[8,64,256]{2,1,0:T(8,128)(2,1)}) custom-call(bf16[8,256,256]{2,1,0:T(8,128)(2,1)S(1)} %attention.1.turned_ref), custom_call_target="tpu_custom_call" | custom-call | flops 2000000000 | bytes 2000000 | tf_op jit(solution)/shard_map/turn_back/pallas_call | solution.py:283
  33.7 0.0 collective-permute-done.rest_5_.rest_9_
  33.7 1.4 %collective-permute-done.1.rest_6_.rest_10_ = bf16[528,256]{1,0:T(8,128)(2,1)S(1)} collective-permute-done((bf16[528,256]{1,0:T(8,128)(2,1)}, bf16[528,256]{1,0:T(8,128)(2,1)S(1)}, u32[]{:S(2)}, u32[]{:S(2)}) %collective-permute-start.1) | collective-permute-done | bytes 270368 | tf_op jit(solution)/shard_map/ppermute | solution.py:722
  35.1 0.0 copy-start.1
  35.1 0.0 copy-start.2
  35.2 0.0 copy-start.4
  35.2 3.8 %alignment.1 = (bf16[256,256]{1,0:T(8,128)(2,1)S(1)}, bf16[8,32,256]{2,1,0:T(8,128)(2,1)S(1)}) custom-call(s32[4]{0:T(128)S(1)} %get-tuple-element.63.sources_ref, bf16[8,256,256]{2,1,0:T(8,128)(2,1)S(1)} %attention.1.turned_ref, bf16[256,256]{1,0:T(8,128)(2,1)S(1)} %bitcast.28, bf16[64,256]{1,0:T(8,128)(2,1)S(1)} %bitcast.30, ...), custom_call_target="tpu_custom_call" | custom-call | flops 4000000000 | bytes 4000000 | tf_op jit(solution)/shard_map/alignment/pallas_call | solution.py:354
  39.0 1.3 %collective-permute-start.8 = (bf16[8,32,256]{2,1,0:T(8,128)(2,1)S(1)}, bf16[8,32,256]{2,1,0:T(8,128)(2,1)S(1)}, u32[]{:S(2)}, u32[]{:S(2)}) collective-permute-start(bf16[8,32,256]{2,1,0:T(8,128)(2,1)S(1)} %get-tuple-element.106.rest_8_), channel_id=1, source_target_pairs={{0,8},{8,0},{16,24},{24,16},{1,9},{9,1},{17,25},{25,17},{2,10},{10... | collective-permute-start | bytes 393224 | tf_op jit(solution)/shard_map/ppermute | solution.py:722
  40.2 0.9 collective-permute-start.11
  41.1 1.4 %collective-permute-start.12 = (bf16[8,32,256]{2,1,0:T(8,128)(2,1)S(1)}, bf16[8,32,256]{2,1,0:T(8,128)(2,1)S(1)}, u32[]{:S(2)}, u32[]{:S(2)}) collective-permute-start(bf16[8,32,256]{2,1,0:T(8,128)(2,1)S(1)} %get-tuple-element.106.rest_8_), channel_id=1, source_target_pairs={{0,24},{8,16},{16,8},{24,0},{1,25},{9,17},{17,9},{25,1},{2,26},{10... | collective-permute-start | bytes 393224 | tf_op jit(solution)/shard_map/ppermute | solution.py:722
  42.5 0.7 collective-permute-start.6
  43.2 4.0 %collective-permute-start.7 = (bf16[256,256]{1,0:T(8,128)(2,1)S(1)}, bf16[256,256]{1,0:T(8,128)(2,1)S(1)}, u32[]{:S(2)}, u32[]{:S(2)}) collective-permute-start(bf16[256,256]{1,0:T(8,128)(2,1)S(1)} %get-tuple-element.103), channel_id=1, source_target_pairs={{0,2},{1,3},{2,10},{3,11},{4,18},{5,19},{6,26},{7,27},{8,4},{9,5},... | collective-permute-start | bytes 393224 | tf_op jit(solution)/shard_map/ppermute | solution.py:683
  47.2 5.4 %collective-permute-start.10 = (bf16[256,256]{1,0:T(8,128)(2,1)S(1)}, bf16[256,256]{1,0:T(8,128)(2,1)S(1)}, u32[]{:S(2)}, u32[]{:S(2)}) collective-permute-start(bf16[256,256]{1,0:T(8,128)(2,1)S(1)} %get-tuple-element.103), channel_id=1, source_target_pairs={{0,6},{1,7},{2,14},{3,15},{4,22},{5,23},{6,30},{7,31},{8,0},{9,1},... | collective-permute-start | bytes 393224 | tf_op jit(solution)/shard_map/ppermute | solution.py:683
  52.6 0.0 collective-permute-done.11.rest_10_
  52.6 0.0 collective-permute-start.9
  52.6 0.0 collective-permute-done.6.rest_0_
  52.6 0.1 collective-permute-start.13
  52.7 0.8 collective-permute-done.7.rest_1_
  53.5 1.6 %collective-permute-done.10.rest_3_ = bf16[256,256]{1,0:T(8,128)(2,1)S(1)} collective-permute-done((bf16[256,256]{1,0:T(8,128)(2,1)S(1)}, bf16[256,256]{1,0:T(8,128)(2,1)S(1)}, u32[]{:S(2)}, u32[]{:S(2)}) %collective-permute-start.10) | collective-permute-done | bytes 131104 | tf_op jit(solution)/shard_map/ppermute | solution.py:683
  55.1 2.4 %collective-permute-done.9.rest_2_ = bf16[256,256]{1,0:T(8,128)(2,1)S(1)} collective-permute-done((bf16[256,256]{1,0:T(8,128)(2,1)S(1)}, bf16[256,256]{1,0:T(8,128)(2,1)S(1)}, u32[]{:S(2)}, u32[]{:S(2)}) %collective-permute-start.9) | collective-permute-done | bytes 131104 | tf_op jit(solution)/shard_map/ppermute | solution.py:683
  57.6 1.3 %collective-permute-done.15.rest_6_ = bf16[256,256]{1,0:T(8,128)(2,1)S(1)} collective-permute-done((bf16[256,256]{1,0:T(8,128)(2,1)S(1)}, bf16[256,256]{1,0:T(8,128)(2,1)S(1)}, u32[]{:S(2)}, u32[]{:S(2)}) %collective-permute-start.15) | collective-permute-done | bytes 131104 | tf_op jit(solution)/shard_map/ppermute | solution.py:669
  58.9 8.7 %pair_update.1 = (f32[32,64,128]{2,1,0:T(8,128)}, f32[32,64,128]{2,1,0:T(8,128)}, bf16[128,32,128]{2,1,0:T(8,128)(2,1)}) custom-call(s32[8]{0:T(128)S(1)} %pad_add_fusion.left_slots_ref, s32[4]{0:T(128)S(1)} %get-tuple-element.94.right_firsts_ref, bf16[256,256]{1,0:T(8,128)(2,1)S(1)} %collective-permute-done.6.rest_0_, ...), custom_call_target="tpu_custom_call" | custom-call | flops 12000000000 | bytes 12000000 | tf_op jit(solution)/shard_map/pair_update/pallas_call | solution.py:521
  67.6 6.5 %all-to-all-start = ((bf16[32,4,32,128]{3,2,1,0:T(8,128)(2,1)}), bf16[32,4,32,128]{3,2,1,0:T(8,128)(2,1)S(1)}, u32[]{:S(2)}, u32[]{:S(2)}) async-start(bf16[32,4,32,128]{3,2,1,0:T(8,128)(2,1)} %bitcast.33), calls=%async_computation | async-start | bytes 2097152 | tf_op jit(solution)/shard_map/all_to_all | solution.py:794
  74.1 1.8 %collective-permute-start.17 = (bf16[8,64,256]{2,1,0:T(8,128)(2,1)}, bf16[8,64,256]{2,1,0:T(8,128)(2,1)S(1)}, u32[]{:S(2)}, u32[]{:S(2)}) collective-permute-start(bf16[8,64,256]{2,1,0:T(8,128)(2,1)} %get-tuple-element.113), channel_id=1, source_target_pairs={{0,8},{8,0},{16,24},{24,16},{1,9},{9,1},{17,25},{25,17},{2,10},{10... | collective-permute-start | bytes 786440 | tf_op jit(solution)/shard_map/ppermute | solution.py:722
  75.9 1.5 %collective-permute-start.18 = (bf16[8,64,256]{2,1,0:T(8,128)(2,1)}, bf16[8,64,256]{2,1,0:T(8,128)(2,1)S(1)}, u32[]{:S(2)}, u32[]{:S(2)}) collective-permute-start(bf16[8,64,256]{2,1,0:T(8,128)(2,1)} %get-tuple-element.114), channel_id=1, source_target_pairs={{0,16},{8,24},{16,0},{24,8},{1,17},{9,25},{17,1},{25,9},{2,18},{10... | collective-permute-start | bytes 786440 | tf_op jit(solution)/shard_map/ppermute | solution.py:722
  77.4 0.3 collective-permute-start.19
  77.6 13.7 %collective-permute-done.17 = bf16[8,64,256]{2,1,0:T(8,128)(2,1)S(1)} collective-permute-done((bf16[8,64,256]{2,1,0:T(8,128)(2,1)}, bf16[8,64,256]{2,1,0:T(8,128)(2,1)S(1)}, u32[]{:S(2)}, u32[]{:S(2)}) %collective-permute-start.17) | collective-permute-done | bytes 262176 | tf_op jit(solution)/shard_map/ppermute | solution.py:722
  91.3 0.7 copy-done.11
  92.0 0.7 copy-done.12
  92.7 7.0 %collective-permute-done.19 = bf16[8,64,256]{2,1,0:T(8,128)(2,1)} collective-permute-done((bf16[8,64,256]{2,1,0:T(8,128)(2,1)}, bf16[8,64,256]{2,1,0:T(8,128)(2,1)}, u32[]{:S(2)}, u32[]{:S(2)}) %collective-permute-start.19) | collective-permute-done | bytes 262176 | tf_op jit(solution)/shard_map/ppermute | solution.py:722
  99.7 1.9 %all-to-all-done.sides_ref = bf16[32,4,32,128]{3,2,1,0:T(8,128)(2,1)S(1)} async-done(((bf16[32,4,32,128]{3,2,1,0:T(8,128)(2,1)}), bf16[32,4,32,128]{3,2,1,0:T(8,128)(2,1)S(1)}, u32[]{:S(2)}, u32[]{:S(2)}) %all-to-all-start) | async-done | bytes 1048608 | tf_op jit(solution)/shard_map/all_to_all | solution.py:794
  101.6 1.7 %triangle_product.1 = bf16[32,4,16,128]{3,2,1,0:T(8,128)(2,1)} custom-call(bf16[32,4,32,128]{3,2,1,0:T(8,128)(2,1)S(1)} %all-to-all-done.sides_ref), custom_call_target="tpu_custom_call" | custom-call | flops 3000000000 | bytes 3000000 | tf_op jit(solution)/shard_map/triangle_product/pallas_call | solution.py:585
  103.3 3.0 %all-to-all-start.1 = ((bf16[32,4,16,128]{3,2,1,0:T(8,128)(2,1)}), bf16[32,4,16,128]{3,2,1,0:T(8,128)(2,1)S(1)}, u32[]{:S(2)}, u32[]{:S(2)}) async-start(bf16[32,4,16,128]{3,2,1,0:T(8,128)(2,1)} %triangle_product.1), calls=%async_computation.1 | async-start | bytes 1048576 | tf_op jit(solution)/shard_map/all_to_all | solution.py:797
  106.3 0.1 broadcast_in_dim.14
  106.4 0.1 broadcast_in_dim.15
  106.5 0.0 copy-start.8
  106.5 2.2 %pad_maximum_fusion = bf16[4,8,64,256]{3,2,1,0:T(8,128)(2,1)} fusion(bf16[1,8,64,256]{3,2,1,0:T(8,128)(2,1)} %bitcast.10, bf16[1,8,64,256]{3,2,1,0:T(8,128)(2,1)} %bitcast.38, bf16[1,8,64,256]{3,2,1,0:T(8,128)(2,1)} %bitcast.37, bf16[1,8,64,256]{3,2,1,0:T(8,128)(2,1)S(1)} %bitcast.36), kind=kLoop, calls=%fused_computation.2 | loop fusion | flops 1572864 | bytes 2097152 | tf_op jit(solution)/shard_map/stack | solution.py:799
  108.8 2.8 %gather_fusion = bf16[4,8,64,256]{3,2,1,0:T(8,128)(2,1)} fusion(bf16[4,8,64,256]{3,2,1,0:T(8,128)(2,1)} %pad_maximum_fusion, s32[1024]{0:T(1024)S(1)} %pad_clamp_fusion), kind=kCustom, calls=%fused_computation | custom fusion | bytes 2097168 | tf_op jit(solution)/shard_map/jit(_take)/gather | solution.py:799
  111.6 3.4 %convolution_add_fusion = f32[64,32,256]{2,1,0:T(8,128)} fusion(f32[64,32,256]{2,1,0:T(8,128)S(1)} %copy-done, bf16[32,64,256]{2,1,0:T(8,128)(2,1)} %bitcast.31, pred[32]{0:T(512)(128)(4,1)S(1)} %broadcast_in_dim.15, bf16[256,256]{1,0:T(8,128)(2,1)S(1)} %copy-done.8), kind=kOutput, calls=%fused_computation.1 | convolution fusion | flops 269484032 | bytes 5373984 | tf_op jit(solution)/shard_map/dot_general | solution.py:801
  115.0 7.7 %all-to-all-done.1 = bf16[32,4,16,128]{3,2,1,0:T(8,128)(2,1)S(1)} async-done(((bf16[32,4,16,128]{3,2,1,0:T(8,128)(2,1)}), bf16[32,4,16,128]{3,2,1,0:T(8,128)(2,1)S(1)}, u32[]{:S(2)}, u32[]{:S(2)}) %all-to-all-start.1) | async-done | bytes 524320 | tf_op jit(solution)/shard_map/all_to_all | solution.py:797
  122.7 2.8 %pair_result.1 = f32[64,32,128]{2,1,0:T(8,128)} custom-call(bf16[128,16,128]{2,1,0:T(8,128)(2,1)S(1)} %bitcast.26, bf16[128,128]{1,0:T(8,128)(2,1)S(1)} %copy-done.5, f32[32,64,128]{2,1,0:T(8,128)} %get-tuple-element.122.mid_hbm, f32[32,64,128]{2,1,0:T(8,128)} %get-tuple-element.123.gate_hbm), custom_call_target="tpu_custom_call" | custom-call | flops 3000000000 | bytes 3000000 | tf_op jit(solution)/shard_map/pair_result/pallas_call | solution.py:643
  (36 shorter events, 0.1 us)
Async XLA Ops:
  0.6 9.0 %copy-start.9 = (bf16[256,768]{1,0:T(8,128)(2,1)S(1)}, bf16[256,768]{1,0:T(8,128)(2,1)}, u32[]{:S(2)}) copy-start(bf16[256,768]{1,0:T(8,128)(2,1)} %param.13) | copy-start | bytes 1179652
  0.7 10.9 %copy-start.13 = (bf16[256,256]{1,0:T(8,128)(2,1)S(1)}, bf16[256,256]{1,0:T(8,128)(2,1)}, u32[]{:S(2)}) copy-start(bf16[256,256]{1,0:T(8,128)(2,1)} %param.12) | copy-start | bytes 393220
  5.1 10.3 %copy-start = (f32[64,32,256]{2,1,0:T(8,128)S(1)}, f32[64,32,256]{2,1,0:T(8,128)}, u32[]{:S(2)}) copy-start(f32[64,32,256]{2,1,0:T(8,128)} %block_hbm.1) | copy-start | bytes 6291460
  5.1 18.4 %collective-permute-start.3 = (bf16[8,64,256]{2,1,0:T(8,128)(2,1)}, bf16[8,64,256]{2,1,0:T(8,128)(2,1)S(1)}, u32[]{:S(2)}, u32[]{:S(2)}) collective-permute-start(bf16[8,64,256]{2,1,0:T(8,128)(2,1)} %get-tuple-element.69), channel_id=1, source_target_pairs={{0,8},{8,0},{16,24},{24,16},{1,9},{9,1},{17,25},{25,17},{2,10},{10... | collective-permute-start | bytes 786440 | tf_op jit(solution)/shard_map/ppermute | solution.py:722
  8.1 15.4 %collective-permute-start.4 = (bf16[8,64,256]{2,1,0:T(8,128)(2,1)}, bf16[8,64,256]{2,1,0:T(8,128)(2,1)S(1)}, u32[]{:S(2)}, u32[]{:S(2)}) collective-permute-start(bf16[8,64,256]{2,1,0:T(8,128)(2,1)} %get-tuple-element.70), channel_id=1, source_target_pairs={{0,16},{8,24},{16,0},{24,8},{1,17},{9,25},{17,1},{25,9},{2,18},{10... | collective-permute-start | bytes 786440 | tf_op jit(solution)/shard_map/ppermute | solution.py:722
  9.7 13.9 %collective-permute-start.5 = (bf16[8,64,256]{2,1,0:T(8,128)(2,1)}, bf16[8,64,256]{2,1,0:T(8,128)(2,1)S(1)}, u32[]{:S(2)}, u32[]{:S(2)}) collective-permute-start(bf16[8,64,256]{2,1,0:T(8,128)(2,1)} %get-tuple-element.71), channel_id=1, source_target_pairs={{0,24},{8,16},{16,8},{24,0},{1,25},{9,17},{17,9},{25,1},{2,26},{10... | collective-permute-start | bytes 786440 | tf_op jit(solution)/shard_map/ppermute | solution.py:722
  15.5 8.1 %copy-start.6 = (bf16[8,64,256]{2,1,0:T(8,128)(2,1)S(1)}, bf16[8,64,256]{2,1,0:T(8,128)(2,1)}, u32[]{:S(2)}) copy-start(bf16[8,64,256]{2,1,0:T(8,128)(2,1)} %get-tuple-element.81.rest_0_) | copy-start | bytes 786436
  20.0 13.7 %collective-permute-start = (bf16[528,256]{1,0:T(8,128)(2,1)}, bf16[528,256]{1,0:T(8,128)(2,1)S(1)}, u32[]{:S(2)}, u32[]{:S(2)}) collective-permute-start(bf16[528,256]{1,0:T(8,128)(2,1)} %get-tuple-element.65), channel_id=1, source_target_pairs={{0,8},{8,0},{16,24},{24,16},{1,9},{9,1},{17,25},{25,17},{2,10},{10... | collective-permute-start | bytes 811016 | tf_op jit(solution)/shard_map/ppermute | solution.py:722
  22.0 13.1 %collective-permute-start.1 = (bf16[528,256]{1,0:T(8,128)(2,1)}, bf16[528,256]{1,0:T(8,128)(2,1)S(1)}, u32[]{:S(2)}, u32[]{:S(2)}) collective-permute-start(bf16[528,256]{1,0:T(8,128)(2,1)} %get-tuple-element.66), channel_id=1, source_target_pairs={{0,16},{8,24},{16,0},{24,8},{1,17},{9,25},{17,1},{25,9},{2,18},{10... | collective-permute-start | bytes 811016 | tf_op jit(solution)/shard_map/ppermute | solution.py:722
  23.5 11.6 %collective-permute-start.2 = (bf16[528,256]{1,0:T(8,128)(2,1)}, bf16[528,256]{1,0:T(8,128)(2,1)S(1)}, u32[]{:S(2)}, u32[]{:S(2)}) collective-permute-start(bf16[528,256]{1,0:T(8,128)(2,1)} %get-tuple-element.67), channel_id=1, source_target_pairs={{0,24},{8,16},{16,8},{24,0},{1,25},{9,17},{17,9},{25,1},{2,26},{10... | collective-permute-start | bytes 811016 | tf_op jit(solution)/shard_map/ppermute | solution.py:722
  31.9 3.2 %copy-start.3 = (bf16[256,64]{0,1:T(8,128)(2,1)S(1)}, bf16[256,64]{0,1:T(8,128)(2,1)}, u32[]{:S(2)}) copy-start(bf16[256,64]{0,1:T(8,128)(2,1)} %param.15) | copy-start | bytes 98308
  31.9 3.2 %copy-start.7 = (bf16[528,256]{1,0:T(8,128)(2,1)S(1)}, bf16[528,256]{1,0:T(8,128)(2,1)}, u32[]{:S(2)}) copy-start(bf16[528,256]{1,0:T(8,128)(2,1)} %get-tuple-element.97.rest_4_.rest_8_) | copy-start | bytes 811012
  35.1 23.8 %copy-start.1 = (f32[64,32,128]{2,1,0:T(8,128)S(1)}, f32[64,32,128]{2,1,0:T(8,128)}, u32[]{:S(2)}) copy-start(f32[64,32,128]{2,1,0:T(8,128)} %param.11) | copy-start | bytes 3145732
  35.1 23.7 %copy-start.2 = (bf16[1024,128]{1,0:T(8,128)(2,1)S(1)}, bf16[1024,128]{1,0:T(8,128)(2,1)}, u32[]{:S(2)}) copy-start(bf16[1024,128]{1,0:T(8,128)(2,1)} %rest_12_.1) | copy-start | bytes 786436
  35.2 23.7 %copy-start.4 = (bf16[128,128]{1,0:T(8,128)(2,1)S(1)}, bf16[128,128]{1,0:T(8,128)(2,1)}, u32[]{:S(2)}) copy-start(bf16[128,128]{1,0:T(8,128)(2,1)} %rest_14_.1) | copy-start | bytes 98308
  39.0 8.2 %collective-permute-start.8 = (bf16[8,32,256]{2,1,0:T(8,128)(2,1)S(1)}, bf16[8,32,256]{2,1,0:T(8,128)(2,1)S(1)}, u32[]{:S(2)}, u32[]{:S(2)}) collective-permute-start(bf16[8,32,256]{2,1,0:T(8,128)(2,1)S(1)} %get-tuple-element.106.rest_8_), channel_id=1, source_target_pairs={{0,8},{8,0},{16,24},{24,16},{1,9},{9,1},{17,25},{25,17},{2,10},{10... | collective-permute-start | bytes 393224 | tf_op jit(solution)/shard_map/ppermute | solution.py:722
  40.2 12.3 %collective-permute-start.11 = (bf16[8,32,256]{2,1,0:T(8,128)(2,1)S(1)}, bf16[8,32,256]{2,1,0:T(8,128)(2,1)S(1)}, u32[]{:S(2)}, u32[]{:S(2)}) collective-permute-start(bf16[8,32,256]{2,1,0:T(8,128)(2,1)S(1)} %get-tuple-element.106.rest_8_), channel_id=1, source_target_pairs={{0,16},{8,24},{16,0},{24,8},{1,17},{9,25},{17,1},{25,9},{2,18},{10... | collective-permute-start | bytes 393224 | tf_op jit(solution)/shard_map/ppermute | solution.py:722
  41.1 12.4 %collective-permute-start.12 = (bf16[8,32,256]{2,1,0:T(8,128)(2,1)S(1)}, bf16[8,32,256]{2,1,0:T(8,128)(2,1)S(1)}, u32[]{:S(2)}, u32[]{:S(2)}) collective-permute-start(bf16[8,32,256]{2,1,0:T(8,128)(2,1)S(1)} %get-tuple-element.106.rest_8_), channel_id=1, source_target_pairs={{0,24},{8,16},{16,8},{24,0},{1,25},{9,17},{17,9},{25,1},{2,26},{10... | collective-permute-start | bytes 393224 | tf_op jit(solution)/shard_map/ppermute | solution.py:722
  42.5 10.0 %collective-permute-start.6 = (bf16[256,256]{1,0:T(8,128)(2,1)S(1)}, bf16[256,256]{1,0:T(8,128)(2,1)S(1)}, u32[]{:S(2)}, u32[]{:S(2)}) collective-permute-start(bf16[256,256]{1,0:T(8,128)(2,1)S(1)} %get-tuple-element.103), channel_id=1, source_target_pairs={{0,0},{1,1},{2,8},{3,9},{4,16},{5,17},{6,24},{7,25},{8,2},{9,3},{1... | collective-permute-start | bytes 393224 | tf_op jit(solution)/shard_map/ppermute | solution.py:683
  43.2 10.3 %collective-permute-start.7 = (bf16[256,256]{1,0:T(8,128)(2,1)S(1)}, bf16[256,256]{1,0:T(8,128)(2,1)S(1)}, u32[]{:S(2)}, u32[]{:S(2)}) collective-permute-start(bf16[256,256]{1,0:T(8,128)(2,1)S(1)} %get-tuple-element.103), channel_id=1, source_target_pairs={{0,2},{1,3},{2,10},{3,11},{4,18},{5,19},{6,26},{7,27},{8,4},{9,5},... | collective-permute-start | bytes 393224 | tf_op jit(solution)/shard_map/ppermute | solution.py:683
  47.2 7.9 %collective-permute-start.10 = (bf16[256,256]{1,0:T(8,128)(2,1)S(1)}, bf16[256,256]{1,0:T(8,128)(2,1)S(1)}, u32[]{:S(2)}, u32[]{:S(2)}) collective-permute-start(bf16[256,256]{1,0:T(8,128)(2,1)S(1)} %get-tuple-element.103), channel_id=1, source_target_pairs={{0,6},{1,7},{2,14},{3,15},{4,22},{5,23},{6,30},{7,31},{8,0},{9,1},... | collective-permute-start | bytes 393224 | tf_op jit(solution)/shard_map/ppermute | solution.py:683
  52.6 5.0 %collective-permute-start.9 = (bf16[256,256]{1,0:T(8,128)(2,1)S(1)}, bf16[256,256]{1,0:T(8,128)(2,1)S(1)}, u32[]{:S(2)}, u32[]{:S(2)}) collective-permute-start(bf16[256,256]{1,0:T(8,128)(2,1)S(1)} %get-tuple-element.103), channel_id=1, source_target_pairs={{0,4},{1,5},{2,12},{3,13},{4,20},{5,21},{6,28},{7,29},{8,6},{9,7},... | collective-permute-start | bytes 393224 | tf_op jit(solution)/shard_map/ppermute | solution.py:683
  52.6 5.0 %collective-permute-start.13 = (bf16[256,256]{1,0:T(8,128)(2,1)S(1)}, bf16[256,256]{1,0:T(8,128)(2,1)S(1)}, u32[]{:S(2)}, u32[]{:S(2)}) collective-permute-start(bf16[256,256]{1,0:T(8,128)(2,1)S(1)} %collective-permute-done.6.rest_0_), channel_id=1, source_target_pairs={{0,1},{1,0},{2,3},{3,2},{4,5},{5,4},{6,7},{7,6},{8,9},{9,8},{10,11... | collective-permute-start | bytes 393224 | tf_op jit(solution)/shard_map/ppermute | solution.py:669
  53.5 4.0 %collective-permute-start.14 = (bf16[256,256]{1,0:T(8,128)(2,1)S(1)}, bf16[256,256]{1,0:T(8,128)(2,1)S(1)}, u32[]{:S(2)}, u32[]{:S(2)}) collective-permute-start(bf16[256,256]{1,0:T(8,128)(2,1)S(1)} %collective-permute-done.7.rest_1_), channel_id=1, source_target_pairs={{0,1},{1,0},{2,3},{3,2},{4,5},{5,4},{6,7},{7,6},{8,9},{9,8},{10,11... | collective-permute-start | bytes 393224 | tf_op jit(solution)/shard_map/ppermute | solution.py:669
  55.1 2.5 %collective-permute-start.16 = (bf16[256,256]{1,0:T(8,128)(2,1)S(1)}, bf16[256,256]{1,0:T(8,128)(2,1)S(1)}, u32[]{:S(2)}, u32[]{:S(2)}) collective-permute-start(bf16[256,256]{1,0:T(8,128)(2,1)S(1)} %collective-permute-done.10.rest_3_), channel_id=1, source_target_pairs={{0,1},{1,0},{2,3},{3,2},{4,5},{5,4},{6,7},{7,6},{8,9},{9,8},{10,11... | collective-permute-start | bytes 393224 | tf_op jit(solution)/shard_map/ppermute | solution.py:669
  57.5 1.3 %collective-permute-start.15 = (bf16[256,256]{1,0:T(8,128)(2,1)S(1)}, bf16[256,256]{1,0:T(8,128)(2,1)S(1)}, u32[]{:S(2)}, u32[]{:S(2)}) collective-permute-start(bf16[256,256]{1,0:T(8,128)(2,1)S(1)} %collective-permute-done.9.rest_2_), channel_id=1, source_target_pairs={{0,1},{1,0},{2,3},{3,2},{4,5},{5,4},{6,7},{7,6},{8,9},{9,8},{10,11... | collective-permute-start | bytes 393224 | tf_op jit(solution)/shard_map/ppermute | solution.py:669
  67.6 34.1 %all-to-all-start = ((bf16[32,4,32,128]{3,2,1,0:T(8,128)(2,1)}), bf16[32,4,32,128]{3,2,1,0:T(8,128)(2,1)S(1)}, u32[]{:S(2)}, u32[]{:S(2)}) async-start(bf16[32,4,32,128]{3,2,1,0:T(8,128)(2,1)} %bitcast.33), calls=%async_computation | async-start | bytes 2097152 | tf_op jit(solution)/shard_map/all_to_all | solution.py:794
  74.0 32.5 %copy-start.10 = (bf16[8,64,256]{2,1,0:T(8,128)(2,1)S(1)}, bf16[8,64,256]{2,1,0:T(8,128)(2,1)}, u32[]{:S(2)}) copy-start(bf16[8,64,256]{2,1,0:T(8,128)(2,1)} %get-tuple-element.117) | copy-start | bytes 786436
  74.1 17.3 %collective-permute-start.17 = (bf16[8,64,256]{2,1,0:T(8,128)(2,1)}, bf16[8,64,256]{2,1,0:T(8,128)(2,1)S(1)}, u32[]{:S(2)}, u32[]{:S(2)}) collective-permute-start(bf16[8,64,256]{2,1,0:T(8,128)(2,1)} %get-tuple-element.113), channel_id=1, source_target_pairs={{0,8},{8,0},{16,24},{24,16},{1,9},{9,1},{17,25},{25,17},{2,10},{10... | collective-permute-start | bytes 786440 | tf_op jit(solution)/shard_map/ppermute | solution.py:722
  75.9 15.4 %collective-permute-start.18 = (bf16[8,64,256]{2,1,0:T(8,128)(2,1)}, bf16[8,64,256]{2,1,0:T(8,128)(2,1)S(1)}, u32[]{:S(2)}, u32[]{:S(2)}) collective-permute-start(bf16[8,64,256]{2,1,0:T(8,128)(2,1)} %get-tuple-element.114), channel_id=1, source_target_pairs={{0,16},{8,24},{16,0},{24,8},{1,17},{9,25},{17,1},{25,9},{2,18},{10... | collective-permute-start | bytes 786440 | tf_op jit(solution)/shard_map/ppermute | solution.py:722
  77.4 22.4 %collective-permute-start.19 = (bf16[8,64,256]{2,1,0:T(8,128)(2,1)}, bf16[8,64,256]{2,1,0:T(8,128)(2,1)}, u32[]{:S(2)}, u32[]{:S(2)}) collective-permute-start(bf16[8,64,256]{2,1,0:T(8,128)(2,1)} %get-tuple-element.115), channel_id=1, source_target_pairs={{0,24},{8,16},{16,8},{24,0},{1,25},{9,17},{17,9},{25,1},{2,26},{10... | collective-permute-start | bytes 786440 | tf_op jit(solution)/shard_map/ppermute | solution.py:722
  91.3 0.7 copy-start.11
  92.0 0.7 copy-start.12
  103.3 19.4 %all-to-all-start.1 = ((bf16[32,4,16,128]{3,2,1,0:T(8,128)(2,1)}), bf16[32,4,16,128]{3,2,1,0:T(8,128)(2,1)S(1)}, u32[]{:S(2)}, u32[]{:S(2)}) async-start(bf16[32,4,16,128]{3,2,1,0:T(8,128)(2,1)} %triangle_product.1), calls=%async_computation.1 | async-start | bytes 1048576 | tf_op jit(solution)/shard_map/all_to_all | solution.py:797
  106.5 5.1 %copy-start.8 = (bf16[256,256]{1,0:T(8,128)(2,1)S(1)}, bf16[256,256]{1,0:T(8,128)(2,1)}, u32[]{:S(2)}) copy-start(bf16[256,256]{1,0:T(8,128)(2,1)} %param.14) | copy-start | bytes 393220
  111.6 11.1 %copy-start.5 = (bf16[128,128]{1,0:T(8,128)(2,1)S(1)}, bf16[128,128]{1,0:T(8,128)(2,1)}, u32[]{:S(2)}) copy-start(bf16[128,128]{1,0:T(8,128)(2,1)} %final_ref.1) | copy-start | bytes 98308

commit v18 on v17

--- a/solution.py
+++ b/solution.py
@@ -69,8 +69,8 @@
 def standardised_columns(first_rows, second_rows, first, count, residues):
     seqs = first_rows.shape[0] // residues
     columns = []
-    for n in range(first, first + count):
-        rows = pl.ds(n, seqs, stride=residues)
+    for n in range(count):
+        rows = pl.ds(first + n, seqs, stride=residues)
         columns.append(jnp.concatenate([first_rows[rows, :], second_rows[rows, :]], axis=1))
     column = jnp.concatenate(columns, axis=0)
     centred = column - jnp.mean(column, axis=1, keepdims=True)
@@ -138,54 +138,65 @@
 def low_kernel(sources_ref, first_ref, second_ref, *rest):
     *pieces_hbm, low_ref, sent = rest
     seqs, residues, lanes = first_ref.shape
-    own = residues // len(pieces_hbm)
+    count = len(pieces_hbm)
+    own = (low_ref.shape[1] - 16) // seqs
+    step = pl.program_id(0)
     first_rows = first_ref.reshape(seqs * residues, lanes)
     second_rows = second_ref.reshape(seqs * residues, lanes)
+    shift = lax.rem(sources_ref[step] * own, residues) if own < residues else 0
     lane = lax.broadcasted_iota(jnp.int32, (seqs, 128), 1)
-    for p in range(len(pieces_hbm)):
-        spreads = jnp.zeros((seqs, 128), F32)
-        for n in range(own):
-            normed, spread = standardised_columns(
-                first_rows, second_rows, p * own + n, 1, residues
-            )
-            left = (normed - normed.astype(BF16).astype(F32)).astype(BF16)
-            low_ref[p, n * seqs : (n + 1) * seqs, :] = left
-            spreads = jnp.where(lane == n, spread, spreads)
-        spreads = spreads.T[:8, :]
-        coarse = spreads.astype(BF16).astype(F32)
-        kept = jnp.concatenate([coarse, spreads - coarse], axis=0)
-        kept = jnp.concatenate([kept, jnp.zeros((16, 2 * lanes - seqs), F32)], axis=1)
-        low_ref[p, own * seqs :, :] = kept.astype(BF16)
-    sends = []
-    for p, piece_hbm in enumerate(pieces_hbm):
-        source = low_ref.at[sources_ref[p]]
-        sends.append(pltpu.make_async_copy(source, piece_hbm, sent.at[p]))
-        sends[-1].start()
-    for send in sends:
-        send.wait()
+    spreads = jnp.zeros((seqs, 128), F32)
+    for n in range(own):
+        normed, spread = standardised_columns(first_rows, second_rows, shift + n, 1, residues)
+        left = (normed - normed.astype(BF16).astype(F32)).astype(BF16)
+        low_ref[step, n * seqs : (n + 1) * seqs, :] = left
+        spreads = jnp.where(lane == n, spread, spreads)
+    spreads = spreads.T[:8, :]
+    coarse = spreads.astype(BF16).astype(F32)
+    kept = jnp.concatenate([coarse, spreads - coarse], axis=0)
+    kept = jnp.concatenate([kept, jnp.zeros((16, 2 * lanes - seqs), F32)], axis=1)
+    low_ref[step, own * seqs :, :] = kept.astype(BF16)
+    copies = [
+        pltpu.make_async_copy(low_ref.at[p], piece_hbm, sent.at[p])
+        for p, piece_hbm in enumerate(pieces_hbm)
+    ]
+    for p in range(count):
+
+        @pl.when(step == p)
+        def _(p=p):
+            copies[p].start()
+
+    @pl.when(step == count - 1)
+    def _():
+        for copy in copies:
+            copy.wait()
 
 
 def standardise_low(sources, block):
     seqs, residues, depth = block.shape
     half = depth // 2
     count = sources.shape[0]
-    height = residues // count * seqs + 16
+    own = residues // count
+    height = own * seqs + 16
+    together = 8 // own
     hbm = pl.BlockSpec(memory_space=pltpu.HBM)
     return pl.pallas_call(
         low_kernel,
-        grid=(1,),
-        in_specs=[
-            pl.BlockSpec(memory_space=pltpu.SMEM),
-            pl.BlockSpec((seqs, residues, half), lambda g: (0, 0, 0)),
-            pl.BlockSpec((seqs, residues, half), lambda g: (0, 0, 1)),
-        ],
-        out_specs=[hbm] * count,
+        grid_spec=pltpu.PrefetchScalarGridSpec(
+            num_scalar_prefetch=1,
+            grid=(count,),
+            in_specs=[
+                pl.BlockSpec((seqs, 8, half), lambda p, sources: (0, sources[p] // together, 0)),
+                pl.BlockSpec((seqs, 8, half), lambda p, sources: (0, sources[p] // together, 1)),
+            ],
+            out_specs=[hbm] * count,
+            scratch_shapes=[
+                pltpu.VMEM((count, height, depth), BF16),
+                pltpu.SemaphoreType.DMA((count,)),
+            ],
+        ),
         out_shape=[pltpu.HBM((height, depth), BF16)] * count,
-        scratch_shapes=[
-            pltpu.VMEM((count, height, depth), BF16),
-            pltpu.SemaphoreType.DMA((count,)),
-        ],
-        compiler_params=params(14, "arbitrary"),
+        compiler_params=params(10, "arbitrary"),
         cost_estimate=cost(4),
         name="standardise_low",
     )(sources, block, block)

time: 126 us -> 125 us (level)
  Pallas kernels: 36.1 us -> 34.6 us
    pallas_call x1, Pallas kernels: 4.53 us -> 3.03 us  [standardise_low(): pl.pallas_call(low_kernel, grid_spec=pltpu.PrefetchScalarGridSpec(num_sca...]
  transfers between devices with their start and end apart: 22 -> 22, of which waited for: 9 -> 9; matrix products, arithmetic and copies ran while one was open for 11% -> 12% of each run, Pallas kernels for 12% -> 11%
where the time goes in v18:
time: 125 us; the launch traced here: 124 us
  waiting for transfers between devices  37.9 us (30%)
  starting transfers between devices  34.8 us (28%)
  Pallas kernels  34.6 us (28%)
  local copies, waits for them, and re-layouts  9.11 us (7%)
  matrix products  3.41 us (3%)
  other arithmetic  3.29 us (3%)
    ppermute x12, waiting for transfers between devices, exchange_rows(): arrived.append(lax.ppermute(pieces[shift], 'row', moves))  22.1 us
    ppermute x12, starting transfers between devices, exchange_rows(): arrived.append(lax.ppermute(pieces[shift], 'row', moves))  15.2 us
    ppermute x4, starting transfers between devices, gather_turned(): arrived.append(lax.ppermute(source, ('row', 'col'), moves))  10 us
    pallas_call x1, Pallas kernels, pair_update(): pl.pallas_call(functools.partial(pair_kernel, slots=len(left) // 2), in_s...  8.65 us
    pallas_call x1, Pallas kernels, attention(): pl.pallas_call(attention_kernel, grid=(residues // step,), in_specs=[pl.B...  8.33 us
    all_to_all x1, waiting for transfers between devices, body(): product = lax.all_to_all(product, everywhere, split_axis=0, concat_axis=0)  7.65 us
    all_to_all x1, starting transfers between devices, body(): sides = lax.all_to_all(sides, everywhere, split_axis=0, concat_axis=0)  6.49 us
    ppermute x4, waiting for transfers between devices, gather_turned(): arrived.append(lax.ppermute(source, ('row', 'col'), moves))  4.87 us
  transfers between devices with their start and end apart: 22, of which 9 were waited for; matrix products, arithmetic and copies ran while one was open for 12% of the time, Pallas kernels for 11%

profile of v18, /device:TPU:0, one launch (start us, length us, event | category | flops | bytes accessed | tf_op | source)
XLA Modules:
  0.0 124.2 jit_solution(14881958731010392499)
XLA Ops:
  0.6 0.0 copy-start.9
  0.7 0.0 copy-start.13
  0.7 4.5 %standardise_high.1 = (bf16[8,64,256]{2,1,0:T(8,128)(2,1)}, bf16[8,64,256]{2,1,0:T(8,128)(2,1)}, bf16[8,64,256]{2,1,0:T(8,128)(2,1)}, bf16[8,64,256]{2,1,0:T(8,128)(2,1)}) custom-call(s32[4]{0:T(128)S(1)} %get-tuple-element.63.sources_ref, f32[64,32,256]{2,1,0:T(8,128)} %block_hbm.1), custom_call_target="tpu_custom_call" | custom-call | flops 3000000000 | bytes 3000000 | tf_op jit(solution)/shard_map/standardise_high/pallas_call | solution.py:120
  5.1 0.0 copy-start
  5.1 3.0 %collective-permute-start.3 = (bf16[8,64,256]{2,1,0:T(8,128)(2,1)}, bf16[8,64,256]{2,1,0:T(8,128)(2,1)S(1)}, u32[]{:S(2)}, u32[]{:S(2)}) collective-permute-start(bf16[8,64,256]{2,1,0:T(8,128)(2,1)} %get-tuple-element.69), channel_id=1, source_target_pairs={{0,8},{8,0},{16,24},{24,16},{1,9},{9,1},{17,25},{25,17},{2,10},{10... | collective-permute-start | bytes 786440 | tf_op jit(solution)/shard_map/ppermute | solution.py:733
  8.1 1.5 %collective-permute-start.4 = (bf16[8,64,256]{2,1,0:T(8,128)(2,1)}, bf16[8,64,256]{2,1,0:T(8,128)(2,1)S(1)}, u32[]{:S(2)}, u32[]{:S(2)}) collective-permute-start(bf16[8,64,256]{2,1,0:T(8,128)(2,1)} %get-tuple-element.70), channel_id=1, source_target_pairs={{0,16},{8,24},{16,0},{24,8},{1,17},{9,25},{17,1},{25,9},{2,18},{10... | collective-permute-start | bytes 786440 | tf_op jit(solution)/shard_map/ppermute | solution.py:733
  9.7 0.0 collective-permute-start.5
  9.7 0.7 slice.7
  10.4 1.1 copy.17
  11.5 0.8 copy.12
  12.3 0.9 reshape.47
  13.2 0.1 copy.15
  13.4 1.0 copy.14
  14.4 0.1 pad_add_fusion.left_slots_ref
  14.5 0.9 pad_maximum_fusion.1.others_ref
  15.5 3.0 %standardise_low.1 = (bf16[528,256]{1,0:T(8,128)(2,1)}, bf16[528,256]{1,0:T(8,128)(2,1)}, bf16[528,256]{1,0:T(8,128)(2,1)}, bf16[528,256]{1,0:T(8,128)(2,1)}) custom-call(s32[4]{0:T(128)S(1)} %get-tuple-element.63.sources_ref, f32[64,32,256]{2,1,0:T(8,128)S(1)} %copy-done, f32[64,32,256]{2,1,0:T(8,128)S(1)} %copy-done), custom_call_target="tpu_custom_call" | custom-call | flops 4000000000 | bytes 4000000 | tf_op jit(solution)/shard_map/standardise_low/pallas_call | solution.py:183
  18.5 2.0 %collective-permute-start = (bf16[528,256]{1,0:T(8,128)(2,1)}, bf16[528,256]{1,0:T(8,128)(2,1)S(1)}, u32[]{:S(2)}, u32[]{:S(2)}) collective-permute-start(bf16[528,256]{1,0:T(8,128)(2,1)} %get-tuple-element.65), channel_id=1, source_target_pairs={{0,8},{8,0},{16,24},{24,16},{1,9},{9,1},{17,25},{25,17},{2,10},{10... | collective-permute-start | bytes 811016 | tf_op jit(solution)/shard_map/ppermute | solution.py:733
  20.5 1.5 %collective-permute-start.1 = (bf16[528,256]{1,0:T(8,128)(2,1)}, bf16[528,256]{1,0:T(8,128)(2,1)S(1)}, u32[]{:S(2)}, u32[]{:S(2)}) collective-permute-start(bf16[528,256]{1,0:T(8,128)(2,1)} %get-tuple-element.66), channel_id=1, source_target_pairs={{0,16},{8,24},{16,0},{24,8},{1,17},{9,25},{17,1},{25,9},{2,18},{10... | collective-permute-start | bytes 811016 | tf_op jit(solution)/shard_map/ppermute | solution.py:733
  22.0 0.0 collective-permute-done.3.rest_1_
  22.0 0.0 collective-permute-start.2
  22.1 8.3 %attention.1.turned_ref = bf16[8,256,256]{2,1,0:T(8,128)(2,1)S(1)} custom-call(bf16[256,256]{1,0:T(8,128)(2,1)S(1)} %slice.6.key_ref, bf16[768,256]{1,0:T(8,128)(2,1)S(1)} %pad_maximum_fusion.1.others_ref, bf16[8,64,256]{2,1,0:T(8,128)(2,1)S(1)} %copy-done.6, bf16[8,64,256]{2,1,0:T(8,128)(2,1)S(1)} %collective-permute-done.3.rest_1_, ...), custom_call_target="tpu_custom_call" | custom-call | flops 10000000000 | bytes 10000000 | tf_op jit(solution)/shard_map/attention/pallas_call | solution.py:263
  30.4 1.8 %turn_back.1 = (bf16[8,64,256]{2,1,0:T(8,128)(2,1)}, bf16[8,64,256]{2,1,0:T(8,128)(2,1)}, bf16[8,64,256]{2,1,0:T(8,128)(2,1)}, bf16[8,64,256]{2,1,0:T(8,128)(2,1)}) custom-call(bf16[8,256,256]{2,1,0:T(8,128)(2,1)S(1)} %attention.1.turned_ref), custom_call_target="tpu_custom_call" | custom-call | flops 2000000000 | bytes 2000000 | tf_op jit(solution)/shard_map/turn_back/pallas_call | solution.py:294
  32.2 1.4 %collective-permute-done.1.rest_6_.rest_10_ = bf16[528,256]{1,0:T(8,128)(2,1)S(1)} collective-permute-done((bf16[528,256]{1,0:T(8,128)(2,1)}, bf16[528,256]{1,0:T(8,128)(2,1)S(1)}, u32[]{:S(2)}, u32[]{:S(2)}) %collective-permute-start.1) | collective-permute-done | bytes 270368 | tf_op jit(solution)/shard_map/ppermute | solution.py:733
  33.6 0.0 collective-permute-done.2.rest_7_.rest_11_
  33.6 0.0 copy-start.1
  33.6 0.0 copy-start.2
  33.7 0.0 copy-start.4
  33.7 3.8 %alignment.1 = (bf16[256,256]{1,0:T(8,128)(2,1)S(1)}, bf16[8,32,256]{2,1,0:T(8,128)(2,1)S(1)}) custom-call(s32[4]{0:T(128)S(1)} %get-tuple-element.63.sources_ref, bf16[8,256,256]{2,1,0:T(8,128)(2,1)S(1)} %attention.1.turned_ref, bf16[256,256]{1,0:T(8,128)(2,1)S(1)} %bitcast.28, bf16[64,256]{1,0:T(8,128)(2,1)S(1)} %bitcast.30, ...), custom_call_target="tpu_custom_call" | custom-call | flops 4000000000 | bytes 4000000 | tf_op jit(solution)/shard_map/alignment/pallas_call | solution.py:365
  37.5 1.3 %collective-permute-start.8 = (bf16[8,32,256]{2,1,0:T(8,128)(2,1)S(1)}, bf16[8,32,256]{2,1,0:T(8,128)(2,1)S(1)}, u32[]{:S(2)}, u32[]{:S(2)}) collective-permute-start(bf16[8,32,256]{2,1,0:T(8,128)(2,1)S(1)} %get-tuple-element.106.rest_8_), channel_id=1, source_target_pairs={{0,8},{8,0},{16,24},{24,16},{1,9},{9,1},{17,25},{25,17},{2,10},{10... | collective-permute-start | bytes 393224 | tf_op jit(solution)/shard_map/ppermute | solution.py:733
  38.8 0.9 collective-permute-start.11
  39.7 1.4 %collective-permute-start.12 = (bf16[8,32,256]{2,1,0:T(8,128)(2,1)S(1)}, bf16[8,32,256]{2,1,0:T(8,128)(2,1)S(1)}, u32[]{:S(2)}, u32[]{:S(2)}) collective-permute-start(bf16[8,32,256]{2,1,0:T(8,128)(2,1)S(1)} %get-tuple-element.106.rest_8_), channel_id=1, source_target_pairs={{0,24},{8,16},{16,8},{24,0},{1,25},{9,17},{17,9},{25,1},{2,26},{10... | collective-permute-start | bytes 393224 | tf_op jit(solution)/shard_map/ppermute | solution.py:733
  41.0 0.7 collective-permute-start.6
  41.7 4.0 %collective-permute-start.7 = (bf16[256,256]{1,0:T(8,128)(2,1)S(1)}, bf16[256,256]{1,0:T(8,128)(2,1)S(1)}, u32[]{:S(2)}, u32[]{:S(2)}) collective-permute-start(bf16[256,256]{1,0:T(8,128)(2,1)S(1)} %get-tuple-element.103), channel_id=1, source_target_pairs={{0,2},{1,3},{2,10},{3,11},{4,18},{5,19},{6,26},{7,27},{8,4},{9,5},... | collective-permute-start | bytes 393224 | tf_op jit(solution)/shard_map/ppermute | solution.py:694
  45.7 0.0 collective-permute-done.8.rest_9_
  45.7 5.4 %collective-permute-start.10 = (bf16[256,256]{1,0:T(8,128)(2,1)S(1)}, bf16[256,256]{1,0:T(8,128)(2,1)S(1)}, u32[]{:S(2)}, u32[]{:S(2)}) collective-permute-start(bf16[256,256]{1,0:T(8,128)(2,1)S(1)} %get-tuple-element.103), channel_id=1, source_target_pairs={{0,6},{1,7},{2,14},{3,15},{4,22},{5,23},{6,30},{7,31},{8,0},{9,1},... | collective-permute-start | bytes 393224 | tf_op jit(solution)/shard_map/ppermute | solution.py:694
  51.1 0.0 collective-permute-start.9
  51.1 0.1 collective-permute-start.13
  51.2 0.8 collective-permute-done.7.rest_1_
  52.0 1.6 %collective-permute-done.10.rest_3_ = bf16[256,256]{1,0:T(8,128)(2,1)S(1)} collective-permute-done((bf16[256,256]{1,0:T(8,128)(2,1)S(1)}, bf16[256,256]{1,0:T(8,128)(2,1)S(1)}, u32[]{:S(2)}, u32[]{:S(2)}) %collective-permute-start.10) | collective-permute-done | bytes 131104 | tf_op jit(solution)/shard_map/ppermute | solution.py:694
  53.6 2.4 %collective-permute-done.9.rest_2_ = bf16[256,256]{1,0:T(8,128)(2,1)S(1)} collective-permute-done((bf16[256,256]{1,0:T(8,128)(2,1)S(1)}, bf16[256,256]{1,0:T(8,128)(2,1)S(1)}, u32[]{:S(2)}, u32[]{:S(2)}) %collective-permute-start.9) | collective-permute-done | bytes 131104 | tf_op jit(solution)/shard_map/ppermute | solution.py:694
  56.0 0.0 collective-permute-start.15
  56.0 0.0 collective-permute-done.13.rest_4_
  56.0 0.0 collective-permute-done.14.rest_5_
  56.1 1.3 %collective-permute-done.15.rest_6_ = bf16[256,256]{1,0:T(8,128)(2,1)S(1)} collective-permute-done((bf16[256,256]{1,0:T(8,128)(2,1)S(1)}, bf16[256,256]{1,0:T(8,128)(2,1)S(1)}, u32[]{:S(2)}, u32[]{:S(2)}) %collective-permute-start.15) | collective-permute-done | bytes 131104 | tf_op jit(solution)/shard_map/ppermute | solution.py:680
  57.4 8.7 %pair_update.1 = (f32[32,64,128]{2,1,0:T(8,128)}, f32[32,64,128]{2,1,0:T(8,128)}, bf16[128,32,128]{2,1,0:T(8,128)(2,1)}) custom-call(s32[8]{0:T(128)S(1)} %pad_add_fusion.left_slots_ref, s32[4]{0:T(128)S(1)} %get-tuple-element.94.right_firsts_ref, bf16[256,256]{1,0:T(8,128)(2,1)S(1)} %collective-permute-done.6.rest_0_, ...), custom_call_target="tpu_custom_call" | custom-call | flops 12000000000 | bytes 12000000 | tf_op jit(solution)/shard_map/pair_update/pallas_call | solution.py:532
  66.1 6.5 %all-to-all-start = ((bf16[32,4,32,128]{3,2,1,0:T(8,128)(2,1)}), bf16[32,4,32,128]{3,2,1,0:T(8,128)(2,1)S(1)}, u32[]{:S(2)}, u32[]{:S(2)}) async-start(bf16[32,4,32,128]{3,2,1,0:T(8,128)(2,1)} %bitcast.33), calls=%async_computation | async-start | bytes 2097152 | tf_op jit(solution)/shard_map/all_to_all | solution.py:805
  72.6 1.8 %collective-permute-start.17 = (bf16[8,64,256]{2,1,0:T(8,128)(2,1)}, bf16[8,64,256]{2,1,0:T(8,128)(2,1)S(1)}, u32[]{:S(2)}, u32[]{:S(2)}) collective-permute-start(bf16[8,64,256]{2,1,0:T(8,128)(2,1)} %get-tuple-element.113), channel_id=1, source_target_pairs={{0,8},{8,0},{16,24},{24,16},{1,9},{9,1},{17,25},{25,17},{2,10},{10... | collective-permute-start | bytes 786440 | tf_op jit(solution)/shard_map/ppermute | solution.py:733
  74.4 1.5 %collective-permute-start.18 = (bf16[8,64,256]{2,1,0:T(8,128)(2,1)}, bf16[8,64,256]{2,1,0:T(8,128)(2,1)S(1)}, u32[]{:S(2)}, u32[]{:S(2)}) collective-permute-start(bf16[8,64,256]{2,1,0:T(8,128)(2,1)} %get-tuple-element.114), channel_id=1, source_target_pairs={{0,16},{8,24},{16,0},{24,8},{1,17},{9,25},{17,1},{25,9},{2,18},{10... | collective-permute-start | bytes 786440 | tf_op jit(solution)/shard_map/ppermute | solution.py:733
  75.9 0.3 collective-permute-start.19
  76.1 13.7 %collective-permute-done.17 = bf16[8,64,256]{2,1,0:T(8,128)(2,1)S(1)} collective-permute-done((bf16[8,64,256]{2,1,0:T(8,128)(2,1)}, bf16[8,64,256]{2,1,0:T(8,128)(2,1)S(1)}, u32[]{:S(2)}, u32[]{:S(2)}) %collective-permute-start.17) | collective-permute-done | bytes 262176 | tf_op jit(solution)/shard_map/ppermute | solution.py:733
  89.8 0.7 copy-done.11
  90.5 0.7 copy-done.12
  91.2 7.0 %collective-permute-done.19 = bf16[8,64,256]{2,1,0:T(8,128)(2,1)} collective-permute-done((bf16[8,64,256]{2,1,0:T(8,128)(2,1)}, bf16[8,64,256]{2,1,0:T(8,128)(2,1)}, u32[]{:S(2)}, u32[]{:S(2)}) %collective-permute-start.19) | collective-permute-done | bytes 262176 | tf_op jit(solution)/shard_map/ppermute | solution.py:733
  98.2 1.9 %all-to-all-done.sides_ref = bf16[32,4,32,128]{3,2,1,0:T(8,128)(2,1)S(1)} async-done(((bf16[32,4,32,128]{3,2,1,0:T(8,128)(2,1)}), bf16[32,4,32,128]{3,2,1,0:T(8,128)(2,1)S(1)}, u32[]{:S(2)}, u32[]{:S(2)}) %all-to-all-start) | async-done | bytes 1048608 | tf_op jit(solution)/shard_map/all_to_all | solution.py:805
  100.1 1.7 %triangle_product.1 = bf16[32,4,16,128]{3,2,1,0:T(8,128)(2,1)} custom-call(bf16[32,4,32,128]{3,2,1,0:T(8,128)(2,1)S(1)} %all-to-all-done.sides_ref), custom_call_target="tpu_custom_call" | custom-call | flops 3000000000 | bytes 3000000 | tf_op jit(solution)/shard_map/triangle_product/pallas_call | solution.py:596
  101.8 3.0 %all-to-all-start.1 = ((bf16[32,4,16,128]{3,2,1,0:T(8,128)(2,1)}), bf16[32,4,16,128]{3,2,1,0:T(8,128)(2,1)S(1)}, u32[]{:S(2)}, u32[]{:S(2)}) async-start(bf16[32,4,16,128]{3,2,1,0:T(8,128)(2,1)} %triangle_product.1), calls=%async_computation.1 | async-start | bytes 1048576 | tf_op jit(solution)/shard_map/all_to_all | solution.py:808
  104.8 0.1 broadcast_in_dim.14
  104.9 0.1 broadcast_in_dim.15
  105.0 0.0 copy-start.8
  105.0 2.2 %pad_maximum_fusion = bf16[4,8,64,256]{3,2,1,0:T(8,128)(2,1)} fusion(bf16[1,8,64,256]{3,2,1,0:T(8,128)(2,1)} %bitcast.10, bf16[1,8,64,256]{3,2,1,0:T(8,128)(2,1)} %bitcast.38, bf16[1,8,64,256]{3,2,1,0:T(8,128)(2,1)} %bitcast.37, bf16[1,8,64,256]{3,2,1,0:T(8,128)(2,1)S(1)} %bitcast.36), kind=kLoop, calls=%fused_computation.2 | loop fusion | flops 1572864 | bytes 2097152 | tf_op jit(solution)/shard_map/stack | solution.py:810
  107.3 2.8 %gather_fusion = bf16[4,8,64,256]{3,2,1,0:T(8,128)(2,1)} fusion(bf16[4,8,64,256]{3,2,1,0:T(8,128)(2,1)} %pad_maximum_fusion, s32[1024]{0:T(1024)S(1)} %pad_clamp_fusion), kind=kCustom, calls=%fused_computation | custom fusion | bytes 2097168 | tf_op jit(solution)/shard_map/jit(_take)/gather | solution.py:810
  110.1 3.4 %convolution_add_fusion = f32[64,32,256]{2,1,0:T(8,128)} fusion(f32[64,32,256]{2,1,0:T(8,128)S(1)} %copy-done, bf16[32,64,256]{2,1,0:T(8,128)(2,1)} %bitcast.31, pred[32]{0:T(512)(128)(4,1)S(1)} %broadcast_in_dim.15, bf16[256,256]{1,0:T(8,128)(2,1)S(1)} %copy-done.8), kind=kOutput, calls=%fused_computation.1 | convolution fusion | flops 269484032 | bytes 5373984 | tf_op jit(solution)/shard_map/dot_general | solution.py:812
  113.5 7.7 %all-to-all-done.1 = bf16[32,4,16,128]{3,2,1,0:T(8,128)(2,1)S(1)} async-done(((bf16[32,4,16,128]{3,2,1,0:T(8,128)(2,1)}), bf16[32,4,16,128]{3,2,1,0:T(8,128)(2,1)S(1)}, u32[]{:S(2)}, u32[]{:S(2)}) %all-to-all-start.1) | async-done | bytes 524320 | tf_op jit(solution)/shard_map/all_to_all | solution.py:808
  121.2 2.8 %pair_result.1 = f32[64,32,128]{2,1,0:T(8,128)} custom-call(bf16[128,16,128]{2,1,0:T(8,128)(2,1)S(1)} %bitcast.26, bf16[128,128]{1,0:T(8,128)(2,1)S(1)} %copy-done.5, f32[32,64,128]{2,1,0:T(8,128)} %get-tuple-element.122.mid_hbm, f32[32,64,128]{2,1,0:T(8,128)} %get-tuple-element.123.gate_hbm), custom_call_target="tpu_custom_call" | custom-call | flops 3000000000 | bytes 3000000 | tf_op jit(solution)/shard_map/pair_result/pallas_call | solution.py:654
  (36 shorter events, 0.1 us)
Async XLA Ops:
  0.6 9.0 %copy-start.9 = (bf16[256,768]{1,0:T(8,128)(2,1)S(1)}, bf16[256,768]{1,0:T(8,128)(2,1)}, u32[]{:S(2)}) copy-start(bf16[256,768]{1,0:T(8,128)(2,1)} %param.13) | copy-start | bytes 1179652
  0.7 10.9 %copy-start.13 = (bf16[256,256]{1,0:T(8,128)(2,1)S(1)}, bf16[256,256]{1,0:T(8,128)(2,1)}, u32[]{:S(2)}) copy-start(bf16[256,256]{1,0:T(8,128)(2,1)} %param.12) | copy-start | bytes 393220
  5.1 10.3 %copy-start = (f32[64,32,256]{2,1,0:T(8,128)S(1)}, f32[64,32,256]{2,1,0:T(8,128)}, u32[]{:S(2)}) copy-start(f32[64,32,256]{2,1,0:T(8,128)} %block_hbm.1) | copy-start | bytes 6291460
  5.1 16.9 %collective-permute-start.3 = (bf16[8,64,256]{2,1,0:T(8,128)(2,1)}, bf16[8,64,256]{2,1,0:T(8,128)(2,1)S(1)}, u32[]{:S(2)}, u32[]{:S(2)}) collective-permute-start(bf16[8,64,256]{2,1,0:T(8,128)(2,1)} %get-tuple-element.69), channel_id=1, source_target_pairs={{0,8},{8,0},{16,24},{24,16},{1,9},{9,1},{17,25},{25,17},{2,10},{10... | collective-permute-start | bytes 786440 | tf_op jit(solution)/shard_map/ppermute | solution.py:733
  8.1 13.9 %collective-permute-start.4 = (bf16[8,64,256]{2,1,0:T(8,128)(2,1)}, bf16[8,64,256]{2,1,0:T(8,128)(2,1)S(1)}, u32[]{:S(2)}, u32[]{:S(2)}) collective-permute-start(bf16[8,64,256]{2,1,0:T(8,128)(2,1)} %get-tuple-element.70), channel_id=1, source_target_pairs={{0,16},{8,24},{16,0},{24,8},{1,17},{9,25},{17,1},{25,9},{2,18},{10... | collective-permute-start | bytes 786440 | tf_op jit(solution)/shard_map/ppermute | solution.py:733
  9.7 12.4 %collective-permute-start.5 = (bf16[8,64,256]{2,1,0:T(8,128)(2,1)}, bf16[8,64,256]{2,1,0:T(8,128)(2,1)S(1)}, u32[]{:S(2)}, u32[]{:S(2)}) collective-permute-start(bf16[8,64,256]{2,1,0:T(8,128)(2,1)} %get-tuple-element.71), channel_id=1, source_target_pairs={{0,24},{8,16},{16,8},{24,0},{1,25},{9,17},{17,9},{25,1},{2,26},{10... | collective-permute-start | bytes 786440 | tf_op jit(solution)/shard_map/ppermute | solution.py:733
  15.5 6.6 %copy-start.6 = (bf16[8,64,256]{2,1,0:T(8,128)(2,1)S(1)}, bf16[8,64,256]{2,1,0:T(8,128)(2,1)}, u32[]{:S(2)}) copy-start(bf16[8,64,256]{2,1,0:T(8,128)(2,1)} %get-tuple-element.81.rest_0_) | copy-start | bytes 786436
  18.5 13.7 %collective-permute-start = (bf16[528,256]{1,0:T(8,128)(2,1)}, bf16[528,256]{1,0:T(8,128)(2,1)S(1)}, u32[]{:S(2)}, u32[]{:S(2)}) collective-permute-start(bf16[528,256]{1,0:T(8,128)(2,1)} %get-tuple-element.65), channel_id=1, source_target_pairs={{0,8},{8,0},{16,24},{24,16},{1,9},{9,1},{17,25},{25,17},{2,10},{10... | collective-permute-start | bytes 811016 | tf_op jit(solution)/shard_map/ppermute | solution.py:733
  20.5 13.1 %collective-permute-start.1 = (bf16[528,256]{1,0:T(8,128)(2,1)}, bf16[528,256]{1,0:T(8,128)(2,1)S(1)}, u32[]{:S(2)}, u32[]{:S(2)}) collective-permute-start(bf16[528,256]{1,0:T(8,128)(2,1)} %get-tuple-element.66), channel_id=1, source_target_pairs={{0,16},{8,24},{16,0},{24,8},{1,17},{9,25},{17,1},{25,9},{2,18},{10... | collective-permute-start | bytes 811016 | tf_op jit(solution)/shard_map/ppermute | solution.py:733
  22.0 11.6 %collective-permute-start.2 = (bf16[528,256]{1,0:T(8,128)(2,1)}, bf16[528,256]{1,0:T(8,128)(2,1)S(1)}, u32[]{:S(2)}, u32[]{:S(2)}) collective-permute-start(bf16[528,256]{1,0:T(8,128)(2,1)} %get-tuple-element.67), channel_id=1, source_target_pairs={{0,24},{8,16},{16,8},{24,0},{1,25},{9,17},{17,9},{25,1},{2,26},{10... | collective-permute-start | bytes 811016 | tf_op jit(solution)/shard_map/ppermute | solution.py:733
  30.4 3.2 %copy-start.3 = (bf16[256,64]{0,1:T(8,128)(2,1)S(1)}, bf16[256,64]{0,1:T(8,128)(2,1)}, u32[]{:S(2)}) copy-start(bf16[256,64]{0,1:T(8,128)(2,1)} %param.15) | copy-start | bytes 98308
  30.4 3.2 %copy-start.7 = (bf16[528,256]{1,0:T(8,128)(2,1)S(1)}, bf16[528,256]{1,0:T(8,128)(2,1)}, u32[]{:S(2)}) copy-start(bf16[528,256]{1,0:T(8,128)(2,1)} %get-tuple-element.97.rest_4_.rest_8_) | copy-start | bytes 811012
  33.6 23.8 %copy-start.1 = (f32[64,32,128]{2,1,0:T(8,128)S(1)}, f32[64,32,128]{2,1,0:T(8,128)}, u32[]{:S(2)}) copy-start(f32[64,32,128]{2,1,0:T(8,128)} %param.11) | copy-start | bytes 3145732
  33.6 23.7 %copy-start.2 = (bf16[1024,128]{1,0:T(8,128)(2,1)S(1)}, bf16[1024,128]{1,0:T(8,128)(2,1)}, u32[]{:S(2)}) copy-start(bf16[1024,128]{1,0:T(8,128)(2,1)} %rest_12_.1) | copy-start | bytes 786436
  33.7 23.7 %copy-start.4 = (bf16[128,128]{1,0:T(8,128)(2,1)S(1)}, bf16[128,128]{1,0:T(8,128)(2,1)}, u32[]{:S(2)}) copy-start(bf16[128,128]{1,0:T(8,128)(2,1)} %rest_14_.1) | copy-start | bytes 98308
  37.5 8.2 %collective-permute-start.8 = (bf16[8,32,256]{2,1,0:T(8,128)(2,1)S(1)}, bf16[8,32,256]{2,1,0:T(8,128)(2,1)S(1)}, u32[]{:S(2)}, u32[]{:S(2)}) collective-permute-start(bf16[8,32,256]{2,1,0:T(8,128)(2,1)S(1)} %get-tuple-element.106.rest_8_), channel_id=1, source_target_pairs={{0,8},{8,0},{16,24},{24,16},{1,9},{9,1},{17,25},{25,17},{2,10},{10... | collective-permute-start | bytes 393224 | tf_op jit(solution)/shard_map/ppermute | solution.py:733
  38.8 12.3 %collective-permute-start.11 = (bf16[8,32,256]{2,1,0:T(8,128)(2,1)S(1)}, bf16[8,32,256]{2,1,0:T(8,128)(2,1)S(1)}, u32[]{:S(2)}, u32[]{:S(2)}) collective-permute-start(bf16[8,32,256]{2,1,0:T(8,128)(2,1)S(1)} %get-tuple-element.106.rest_8_), channel_id=1, source_target_pairs={{0,16},{8,24},{16,0},{24,8},{1,17},{9,25},{17,1},{25,9},{2,18},{10... | collective-permute-start | bytes 393224 | tf_op jit(solution)/shard_map/ppermute | solution.py:733
  39.7 12.4 %collective-permute-start.12 = (bf16[8,32,256]{2,1,0:T(8,128)(2,1)S(1)}, bf16[8,32,256]{2,1,0:T(8,128)(2,1)S(1)}, u32[]{:S(2)}, u32[]{:S(2)}) collective-permute-start(bf16[8,32,256]{2,1,0:T(8,128)(2,1)S(1)} %get-tuple-element.106.rest_8_), channel_id=1, source_target_pairs={{0,24},{8,16},{16,8},{24,0},{1,25},{9,17},{17,9},{25,1},{2,26},{10... | collective-permute-start | bytes 393224 | tf_op jit(solution)/shard_map/ppermute | solution.py:733
  41.0 10.0 %collective-permute-start.6 = (bf16[256,256]{1,0:T(8,128)(2,1)S(1)}, bf16[256,256]{1,0:T(8,128)(2,1)S(1)}, u32[]{:S(2)}, u32[]{:S(2)}) collective-permute-start(bf16[256,256]{1,0:T(8,128)(2,1)S(1)} %get-tuple-element.103), channel_id=1, source_target_pairs={{0,0},{1,1},{2,8},{3,9},{4,16},{5,17},{6,24},{7,25},{8,2},{9,3},{1... | collective-permute-start | bytes 393224 | tf_op jit(solution)/shard_map/ppermute | solution.py:694
  41.7 10.3 %collective-permute-start.7 = (bf16[256,256]{1,0:T(8,128)(2,1)S(1)}, bf16[256,256]{1,0:T(8,128)(2,1)S(1)}, u32[]{:S(2)}, u32[]{:S(2)}) collective-permute-start(bf16[256,256]{1,0:T(8,128)(2,1)S(1)} %get-tuple-element.103), channel_id=1, source_target_pairs={{0,2},{1,3},{2,10},{3,11},{4,18},{5,19},{6,26},{7,27},{8,4},{9,5},... | collective-permute-start | bytes 393224 | tf_op jit(solution)/shard_map/ppermute | solution.py:694
  45.7 7.9 %collective-permute-start.10 = (bf16[256,256]{1,0:T(8,128)(2,1)S(1)}, bf16[256,256]{1,0:T(8,128)(2,1)S(1)}, u32[]{:S(2)}, u32[]{:S(2)}) collective-permute-start(bf16[256,256]{1,0:T(8,128)(2,1)S(1)} %get-tuple-element.103), channel_id=1, source_target_pairs={{0,6},{1,7},{2,14},{3,15},{4,22},{5,23},{6,30},{7,31},{8,0},{9,1},... | collective-permute-start | bytes 393224 | tf_op jit(solution)/shard_map/ppermute | solution.py:694
  51.1 5.0 %collective-permute-start.9 = (bf16[256,256]{1,0:T(8,128)(2,1)S(1)}, bf16[256,256]{1,0:T(8,128)(2,1)S(1)}, u32[]{:S(2)}, u32[]{:S(2)}) collective-permute-start(bf16[256,256]{1,0:T(8,128)(2,1)S(1)} %get-tuple-element.103), channel_id=1, source_target_pairs={{0,4},{1,5},{2,12},{3,13},{4,20},{5,21},{6,28},{7,29},{8,6},{9,7},... | collective-permute-start | bytes 393224 | tf_op jit(solution)/shard_map/ppermute | solution.py:694
  51.1 5.0 %collective-permute-start.13 = (bf16[256,256]{1,0:T(8,128)(2,1)S(1)}, bf16[256,256]{1,0:T(8,128)(2,1)S(1)}, u32[]{:S(2)}, u32[]{:S(2)}) collective-permute-start(bf16[256,256]{1,0:T(8,128)(2,1)S(1)} %collective-permute-done.6.rest_0_), channel_id=1, source_target_pairs={{0,1},{1,0},{2,3},{3,2},{4,5},{5,4},{6,7},{7,6},{8,9},{9,8},{10,11... | collective-permute-start | bytes 393224 | tf_op jit(solution)/shard_map/ppermute | solution.py:680
  52.0 4.0 %collective-permute-start.14 = (bf16[256,256]{1,0:T(8,128)(2,1)S(1)}, bf16[256,256]{1,0:T(8,128)(2,1)S(1)}, u32[]{:S(2)}, u32[]{:S(2)}) collective-permute-start(bf16[256,256]{1,0:T(8,128)(2,1)S(1)} %collective-permute-done.7.rest_1_), channel_id=1, source_target_pairs={{0,1},{1,0},{2,3},{3,2},{4,5},{5,4},{6,7},{7,6},{8,9},{9,8},{10,11... | collective-permute-start | bytes 393224 | tf_op jit(solution)/shard_map/ppermute | solution.py:680
  53.6 2.5 %collective-permute-start.16 = (bf16[256,256]{1,0:T(8,128)(2,1)S(1)}, bf16[256,256]{1,0:T(8,128)(2,1)S(1)}, u32[]{:S(2)}, u32[]{:S(2)}) collective-permute-start(bf16[256,256]{1,0:T(8,128)(2,1)S(1)} %collective-permute-done.10.rest_3_), channel_id=1, source_target_pairs={{0,1},{1,0},{2,3},{3,2},{4,5},{5,4},{6,7},{7,6},{8,9},{9,8},{10,11... | collective-permute-start | bytes 393224 | tf_op jit(solution)/shard_map/ppermute | solution.py:680
  56.0 1.3 %collective-permute-start.15 = (bf16[256,256]{1,0:T(8,128)(2,1)S(1)}, bf16[256,256]{1,0:T(8,128)(2,1)S(1)}, u32[]{:S(2)}, u32[]{:S(2)}) collective-permute-start(bf16[256,256]{1,0:T(8,128)(2,1)S(1)} %collective-permute-done.9.rest_2_), channel_id=1, source_target_pairs={{0,1},{1,0},{2,3},{3,2},{4,5},{5,4},{6,7},{7,6},{8,9},{9,8},{10,11... | collective-permute-start | bytes 393224 | tf_op jit(solution)/shard_map/ppermute | solution.py:680
  66.1 34.1 %all-to-all-start = ((bf16[32,4,32,128]{3,2,1,0:T(8,128)(2,1)}), bf16[32,4,32,128]{3,2,1,0:T(8,128)(2,1)S(1)}, u32[]{:S(2)}, u32[]{:S(2)}) async-start(bf16[32,4,32,128]{3,2,1,0:T(8,128)(2,1)} %bitcast.33), calls=%async_computation | async-start | bytes 2097152 | tf_op jit(solution)/shard_map/all_to_all | solution.py:805
  72.5 32.5 %copy-start.10 = (bf16[8,64,256]{2,1,0:T(8,128)(2,1)S(1)}, bf16[8,64,256]{2,1,0:T(8,128)(2,1)}, u32[]{:S(2)}) copy-start(bf16[8,64,256]{2,1,0:T(8,128)(2,1)} %get-tuple-element.117) | copy-start | bytes 786436
  72.6 17.3 %collective-permute-start.17 = (bf16[8,64,256]{2,1,0:T(8,128)(2,1)}, bf16[8,64,256]{2,1,0:T(8,128)(2,1)S(1)}, u32[]{:S(2)}, u32[]{:S(2)}) collective-permute-start(bf16[8,64,256]{2,1,0:T(8,128)(2,1)} %get-tuple-element.113), channel_id=1, source_target_pairs={{0,8},{8,0},{16,24},{24,16},{1,9},{9,1},{17,25},{25,17},{2,10},{10... | collective-permute-start | bytes 786440 | tf_op jit(solution)/shard_map/ppermute | solution.py:733
  74.4 15.4 %collective-permute-start.18 = (bf16[8,64,256]{2,1,0:T(8,128)(2,1)}, bf16[8,64,256]{2,1,0:T(8,128)(2,1)S(1)}, u32[]{:S(2)}, u32[]{:S(2)}) collective-permute-start(bf16[8,64,256]{2,1,0:T(8,128)(2,1)} %get-tuple-element.114), channel_id=1, source_target_pairs={{0,16},{8,24},{16,0},{24,8},{1,17},{9,25},{17,1},{25,9},{2,18},{10... | collective-permute-start | bytes 786440 | tf_op jit(solution)/shard_map/ppermute | solution.py:733
  75.9 22.4 %collective-permute-start.19 = (bf16[8,64,256]{2,1,0:T(8,128)(2,1)}, bf16[8,64,256]{2,1,0:T(8,128)(2,1)}, u32[]{:S(2)}, u32[]{:S(2)}) collective-permute-start(bf16[8,64,256]{2,1,0:T(8,128)(2,1)} %get-tuple-element.115), channel_id=1, source_target_pairs={{0,24},{8,16},{16,8},{24,0},{1,25},{9,17},{17,9},{25,1},{2,26},{10... | collective-permute-start | bytes 786440 | tf_op jit(solution)/shard_map/ppermute | solution.py:733
  89.8 0.7 copy-start.11
  90.5 0.7 copy-start.12
  101.8 19.4 %all-to-all-start.1 = ((bf16[32,4,16,128]{3,2,1,0:T(8,128)(2,1)}), bf16[32,4,16,128]{3,2,1,0:T(8,128)(2,1)S(1)}, u32[]{:S(2)}, u32[]{:S(2)}) async-start(bf16[32,4,16,128]{3,2,1,0:T(8,128)(2,1)} %triangle_product.1), calls=%async_computation.1 | async-start | bytes 1048576 | tf_op jit(solution)/shard_map/all_to_all | solution.py:808
  105.0 5.1 %copy-start.8 = (bf16[256,256]{1,0:T(8,128)(2,1)S(1)}, bf16[256,256]{1,0:T(8,128)(2,1)}, u32[]{:S(2)}) copy-start(bf16[256,256]{1,0:T(8,128)(2,1)} %param.14) | copy-start | bytes 393220
  110.1 11.1 %copy-start.5 = (bf16[128,128]{1,0:T(8,128)(2,1)S(1)}, bf16[128,128]{1,0:T(8,128)(2,1)}, u32[]{:S(2)}) copy-start(bf16[128,128]{1,0:T(8,128)(2,1)} %final_ref.1) | copy-start | bytes 98308

commit v19 on v18

--- a/solution.py
+++ b/solution.py
@@ -202,7 +202,7 @@
     )(sources, block, block)
 
 
-def attention_kernel(key_ref, others_ref, *rest):
+def attention_kernel(key_ref, probe_ref, others_ref, *rest):
     *normed_refs, turned_ref, scores_ref, weights_ref = rest
     blocks = len(normed_refs)
     residues, seqs, _ = normed_refs[0].shape
@@ -214,10 +214,10 @@
     def project(n):
         column = jnp.concatenate([ref[n] for ref in normed_refs], axis=0)
         key_rows = matmul(column, key_ref[...]).astype(BF16)
+        queries = (matmul_nt(probe_ref[...], column) * UNIT_WIDTH ** (-0.5)).astype(BF16)
         projected = matmul_nt(others_ref[...], column)
-        queries = (projected[:inner] * UNIT_WIDTH ** (-0.5)).astype(BF16)
-        value_rows = projected[inner : 2 * inner].astype(BF16)
-        gates = sigmoid(projected[2 * inner :])
+        value_rows = projected[:inner].astype(BF16)
+        gates = sigmoid(projected[inner:])
         columns.append((key_rows, queries, value_rows, gates))
     units = [(n, h) for n in range(residues) for h in range(ATTENTION_UNITS)]
 
@@ -254,7 +254,7 @@
             attend(step - 2)
 
 
-def attention(normed, key_matrix, other_matrices):
+def attention(normed, key_matrix, probe_matrix, other_matrices):
     blocks = len(normed)
     residues, seqs, depth = normed[0].shape
     total = blocks * seqs
@@ -265,7 +265,8 @@
         grid=(residues // step,),
         in_specs=[
             pl.BlockSpec((depth, inner), lambda n: (0, 0)),
-            pl.BlockSpec((3 * inner, depth), lambda n: (0, 0)),
+            pl.BlockSpec((inner, depth), lambda n: (0, 0)),
+            pl.BlockSpec((2 * inner, depth), lambda n: (0, 0)),
         ]
         + [pl.BlockSpec((step, seqs, depth), lambda n: (n, 0, 0))] * blocks,
         out_specs=pl.BlockSpec((step, inner, total), lambda n: (n, 0, 0)),
@@ -277,7 +278,7 @@
         compiler_params=params(12 + (total // 128) ** 2, "arbitrary"),
         cost_estimate=cost(10),
         name="attention",
-    )(key_matrix, other_matrices, *normed)
+    )(key_matrix, probe_matrix, other_matrices, *normed)
 
 
 def turn_kernel(turned_ref, *gated_refs):
@@ -508,8 +509,8 @@
             send(mid_ref.at[source], mid_hbm.at[target])
             send(gate_ref.at[source], gate_hbm.at[target])
 
-    cut = C_TRI // 4
-    for part in range(4):
+    cut = C_TRI // 8
+    for part in range(8):
 
         def turn_step(c, carry):
             sides_ref[c] = rows_ref[pl.ds(c, columns, stride=C_TRI), :].astype(BF16)
@@ -543,7 +544,7 @@
             pltpu.VMEM(whole.shape, F32),
             pltpu.VMEM(whole.shape, F32),
             pltpu.VMEM(sides.shape, BF16),
-            pltpu.SemaphoreType.DMA((2 * len(rights) + 5,)),
+            pltpu.SemaphoreType.DMA((2 * len(rights) + 9,)),
         ],
         compiler_params=params(28),
         cost_estimate=cost(12),
@@ -757,12 +758,10 @@
     own_residues = residues // row_count
     sources = lax.axis_index("row") ^ jnp.arange(row_count, dtype=jnp.int32)
     high = exchange_rows(standardise_high(sources, homolog_tensor))
-    others = jnp.concatenate(
-        [attention_probe_matrix.T, attention_extra_matrices[:, inner:].T], axis=0
-    )
     early = (
         attention_extra_matrices[:, :inner],
-        others,
+        attention_probe_matrix.T,
+        attention_extra_matrices[:, inner:].T,
         attention_final_matrix.T,
         tensor_entry_matrices.T,
         paired_entries(incoming_entry_matrices),
@@ -772,9 +771,9 @@
     after, early = lax.optimization_barrier((sources, early))
     low = standardise_low(after, homolog_tensor)
     high, _, early = lax.optimization_barrier((high, low, early))
-    key_matrix, others, final_turned, tensor_turned, entries, firsts, slots = early
+    key_matrix, probe_turned, others, final_turned, tensor_turned, entries, firsts, slots = early
     low = exchange_rows(low)
-    turned = attention(high, key_matrix, others)
+    turned = attention(high, key_matrix, probe_turned, others)
     gated = turn_back(turned, row_count)
     low, gated = lax.optimization_barrier((low, gated))
     left_piece, right_piece = alignment(

time: 125 us -> 126 us (level)
  waiting for transfers between devices: 37.9 us -> 39.6 us
  local copies, waits for them, and re-layouts: 9.11 us -> 7.68 us
  Pallas kernels: 34.6 us -> 35.9 us
    ppermute x12, waiting for transfers between devices: 22.1 us -> 23.8 us  [exchange_rows(): arrived.append(lax.ppermute(pieces[shift], 'row', moves))]
    unnamed x32 -> x30, local copies, waits for them, and re-layouts: 4.34 us -> 3.62 us
  transfers between devices with their start and end apart: 22 -> 22, of which waited for: 9 -> 10; matrix products, arithmetic and copies ran while one was open for 12% -> 10% of each run, Pallas kernels for 11% -> 11%
where the time goes in v19:
time: 126 us; the launch traced here: 125 us
  waiting for transfers between devices  39.6 us (31%)
  Pallas kernels  35.9 us (28%)
  starting transfers between devices  35.1 us (28%)
  local copies, waits for them, and re-layouts  7.68 us (6%)
  matrix products  3.41 us (3%)
  other arithmetic  2.36 us (2%)
    ppermute x12, waiting for transfers between devices, exchange_rows(): arrived.append(lax.ppermute(pieces[shift], 'row', moves))  23.8 us
    ppermute x12, starting transfers between devices, exchange_rows(): arrived.append(lax.ppermute(pieces[shift], 'row', moves))  15.2 us
    ppermute x4, starting transfers between devices, gather_turned(): arrived.append(lax.ppermute(source, ('row', 'col'), moves))  10.3 us
    pallas_call x1, Pallas kernels, attention(): pl.pallas_call(attention_kernel, grid=(residues // step,), in_specs=[pl.B...  9.27 us
    pallas_call x1, Pallas kernels, pair_update(): pl.pallas_call(functools.partial(pair_kernel, slots=len(left) // 2), in_s...  8.64 us
    all_to_all x1, waiting for transfers between devices, body(): product = lax.all_to_all(product, everywhere, split_axis=0, concat_axis=0)  7.65 us
    all_to_all x1, starting transfers between devices, body(): sides = lax.all_to_all(sides, everywhere, split_axis=0, concat_axis=0)  6.48 us
    ppermute x4, waiting for transfers between devices, gather_turned(): arrived.append(lax.ppermute(source, ('row', 'col'), moves))  4.87 us
  transfers between devices with their start and end apart: 22, of which 10 were waited for; matrix products, arithmetic and copies ran while one was open for 10% of the time, Pallas kernels for 11%

profile of v19, /device:TPU:0, one launch (start us, length us, event | category | flops | bytes accessed | tf_op | source)
XLA Modules:
  0.0 125.1 jit_solution(7483423642178550994)
XLA Ops:
  0.6 0.0 copy-start.8
  0.7 0.0 slice-start
  0.7 4.4 %standardise_high.1 = (bf16[8,64,256]{2,1,0:T(8,128)(2,1)}, bf16[8,64,256]{2,1,0:T(8,128)(2,1)}, bf16[8,64,256]{2,1,0:T(8,128)(2,1)}, bf16[8,64,256]{2,1,0:T(8,128)(2,1)}) custom-call(s32[4]{0:T(128)S(1)} %get-tuple-element.65.sources_ref, f32[64,32,256]{2,1,0:T(8,128)} %block_hbm.1), custom_call_target="tpu_custom_call" | custom-call | flops 3000000000 | bytes 3000000 | tf_op jit(solution)/shard_map/standardise_high/pallas_call | solution.py:120
  5.1 0.0 copy-start
  5.1 3.0 %collective-permute-start.3 = (bf16[8,64,256]{2,1,0:T(8,128)(2,1)}, bf16[8,64,256]{2,1,0:T(8,128)(2,1)S(1)}, u32[]{:S(2)}, u32[]{:S(2)}) collective-permute-start(bf16[8,64,256]{2,1,0:T(8,128)(2,1)} %get-tuple-element.71), channel_id=1, source_target_pairs={{0,8},{8,0},{16,24},{24,16},{1,9},{9,1},{17,25},{25,17},{2,10},{10... | collective-permute-start | bytes 786440 | tf_op jit(solution)/shard_map/ppermute | solution.py:734
  8.1 1.5 %collective-permute-start.4 = (bf16[8,64,256]{2,1,0:T(8,128)(2,1)}, bf16[8,64,256]{2,1,0:T(8,128)(2,1)S(1)}, u32[]{:S(2)}, u32[]{:S(2)}) collective-permute-start(bf16[8,64,256]{2,1,0:T(8,128)(2,1)} %get-tuple-element.72), channel_id=1, source_target_pairs={{0,16},{8,24},{16,0},{24,8},{1,17},{9,25},{17,1},{25,9},{2,18},{10... | collective-permute-start | bytes 786440 | tf_op jit(solution)/shard_map/ppermute | solution.py:734
  9.7 0.0 collective-permute-start.5
  9.7 0.1 copy.17
  9.9 0.9 reshape.47
  10.8 0.1 copy.15
  11.0 1.0 copy.12
  12.0 1.0 copy.14
  13.0 0.1 pad_add_fusion.left_slots_ref
  13.1 3.0 %standardise_low.1 = (bf16[528,256]{1,0:T(8,128)(2,1)}, bf16[528,256]{1,0:T(8,128)(2,1)}, bf16[528,256]{1,0:T(8,128)(2,1)}, bf16[528,256]{1,0:T(8,128)(2,1)}) custom-call(s32[4]{0:T(128)S(1)} %get-tuple-element.65.sources_ref, f32[64,32,256]{2,1,0:T(8,128)S(1)} %copy-done, f32[64,32,256]{2,1,0:T(8,128)S(1)} %copy-done), custom_call_target="tpu_custom_call" | custom-call | flops 4000000000 | bytes 4000000 | tf_op jit(solution)/shard_map/standardise_low/pallas_call | solution.py:183
  16.1 2.0 %collective-permute-start = (bf16[528,256]{1,0:T(8,128)(2,1)}, bf16[528,256]{1,0:T(8,128)(2,1)S(1)}, u32[]{:S(2)}, u32[]{:S(2)}) collective-permute-start(bf16[528,256]{1,0:T(8,128)(2,1)} %get-tuple-element.67), channel_id=1, source_target_pairs={{0,8},{8,0},{16,24},{24,16},{1,9},{9,1},{17,25},{25,17},{2,10},{10... | collective-permute-start | bytes 811016 | tf_op jit(solution)/shard_map/ppermute | solution.py:734
  18.1 1.5 %collective-permute-start.1 = (bf16[528,256]{1,0:T(8,128)(2,1)}, bf16[528,256]{1,0:T(8,128)(2,1)S(1)}, u32[]{:S(2)}, u32[]{:S(2)}) collective-permute-start(bf16[528,256]{1,0:T(8,128)(2,1)} %get-tuple-element.68), channel_id=1, source_target_pairs={{0,16},{8,24},{16,0},{24,8},{1,17},{9,25},{17,1},{25,9},{2,18},{10... | collective-permute-start | bytes 811016 | tf_op jit(solution)/shard_map/ppermute | solution.py:734
  19.6 0.0 collective-permute-done.3.rest_1_
  19.7 0.0 collective-permute-start.2
  19.7 2.5 %collective-permute-done.4.rest_2_ = bf16[8,64,256]{2,1,0:T(8,128)(2,1)S(1)} collective-permute-done((bf16[8,64,256]{2,1,0:T(8,128)(2,1)}, bf16[8,64,256]{2,1,0:T(8,128)(2,1)S(1)}, u32[]{:S(2)}, u32[]{:S(2)}) %collective-permute-start.4) | collective-permute-done | bytes 262176 | tf_op jit(solution)/shard_map/ppermute | solution.py:734
  22.2 0.6 collective-permute-done.5.rest_3_
  22.8 9.3 %attention.1.turned_ref = bf16[8,256,256]{2,1,0:T(8,128)(2,1)S(1)} custom-call(bf16[256,256]{1,0:T(8,128)(2,1)S(1)} %slice.6.key_ref, bf16[256,256]{1,0:T(8,128)(2,1)S(1)} %bitcast.30, bf16[512,256]{1,0:T(8,128)(2,1)S(1)} %bitcast.27, bf16[8,64,256]{2,1,0:T(8,128)(2,1)S(1)} %copy-done.6, bf16[8,64,256]{2,1,0:T(8,128)(2,1)S(1)} %collective-permute-done.3.rest_1_, ...), custom_call_target="tpu_custom_call" | custom-call | flops 10000000000 | bytes 10000000 | tf_op jit(solution)/shard_map/attention/pallas_call | solution.py:263
  32.0 0.0 copy-start.3
  32.1 0.0 copy-start.7
  32.1 1.8 %turn_back.1 = (bf16[8,64,256]{2,1,0:T(8,128)(2,1)}, bf16[8,64,256]{2,1,0:T(8,128)(2,1)}, bf16[8,64,256]{2,1,0:T(8,128)(2,1)}, bf16[8,64,256]{2,1,0:T(8,128)(2,1)}) custom-call(bf16[8,256,256]{2,1,0:T(8,128)(2,1)S(1)} %attention.1.turned_ref), custom_call_target="tpu_custom_call" | custom-call | flops 2000000000 | bytes 2000000 | tf_op jit(solution)/shard_map/turn_back/pallas_call | solution.py:295
  33.8 0.0 collective-permute-done.1.rest_6_.rest_10_
  33.9 0.0 copy-start.1
  33.9 0.0 copy-start.2
  33.9 0.0 copy-start.4
  33.9 4.3 %alignment.1 = (bf16[256,256]{1,0:T(8,128)(2,1)S(1)}, bf16[8,32,256]{2,1,0:T(8,128)(2,1)S(1)}) custom-call(s32[4]{0:T(128)S(1)} %get-tuple-element.65.sources_ref, bf16[8,256,256]{2,1,0:T(8,128)(2,1)S(1)} %attention.1.turned_ref, bf16[256,256]{1,0:T(8,128)(2,1)S(1)} %bitcast.29, bf16[64,256]{1,0:T(8,128)(2,1)S(1)} %bitcast.32, ...), custom_call_target="tpu_custom_call" | custom-call | flops 4000000000 | bytes 4000000 | tf_op jit(solution)/shard_map/alignment/pallas_call | solution.py:366
  38.2 1.6 %collective-permute-start.8 = (bf16[8,32,256]{2,1,0:T(8,128)(2,1)S(1)}, bf16[8,32,256]{2,1,0:T(8,128)(2,1)S(1)}, u32[]{:S(2)}, u32[]{:S(2)}) collective-permute-start(bf16[8,32,256]{2,1,0:T(8,128)(2,1)S(1)} %get-tuple-element.110.rest_8_), channel_id=1, source_target_pairs={{0,8},{8,0},{16,24},{24,16},{1,9},{9,1},{17,25},{25,17},{2,10},{10... | collective-permute-start | bytes 393224 | tf_op jit(solution)/shard_map/ppermute | solution.py:734
  39.8 0.5 collective-permute-start.11
  40.3 1.5 %collective-permute-start.12 = (bf16[8,32,256]{2,1,0:T(8,128)(2,1)S(1)}, bf16[8,32,256]{2,1,0:T(8,128)(2,1)S(1)}, u32[]{:S(2)}, u32[]{:S(2)}) collective-permute-start(bf16[8,32,256]{2,1,0:T(8,128)(2,1)S(1)} %get-tuple-element.110.rest_8_), channel_id=1, source_target_pairs={{0,24},{8,16},{16,8},{24,0},{1,25},{9,17},{17,9},{25,1},{2,26},{10... | collective-permute-start | bytes 393224 | tf_op jit(solution)/shard_map/ppermute | solution.py:734
  41.8 0.7 collective-permute-start.6
  42.4 4.2 %collective-permute-start.7 = (bf16[256,256]{1,0:T(8,128)(2,1)S(1)}, bf16[256,256]{1,0:T(8,128)(2,1)S(1)}, u32[]{:S(2)}, u32[]{:S(2)}) collective-permute-start(bf16[256,256]{1,0:T(8,128)(2,1)S(1)} %get-tuple-element.107), channel_id=1, source_target_pairs={{0,2},{1,3},{2,10},{3,11},{4,18},{5,19},{6,26},{7,27},{8,4},{9,5},... | collective-permute-start | bytes 393224 | tf_op jit(solution)/shard_map/ppermute | solution.py:695
  46.7 0.0 collective-permute-done.8.rest_9_
  46.7 5.4 %collective-permute-start.10 = (bf16[256,256]{1,0:T(8,128)(2,1)S(1)}, bf16[256,256]{1,0:T(8,128)(2,1)S(1)}, u32[]{:S(2)}, u32[]{:S(2)}) collective-permute-start(bf16[256,256]{1,0:T(8,128)(2,1)S(1)} %get-tuple-element.107), channel_id=1, source_target_pairs={{0,6},{1,7},{2,14},{3,15},{4,22},{5,23},{6,30},{7,31},{8,0},{9,1},... | collective-permute-start | bytes 393224 | tf_op jit(solution)/shard_map/ppermute | solution.py:695
  52.1 0.0 collective-permute-done.11.rest_10_
  52.1 0.0 collective-permute-start.9
  52.1 0.0 collective-permute-done.6.rest_0_
  52.1 0.1 collective-permute-start.13
  52.2 0.6 collective-permute-done.7.rest_1_
  52.8 1.8 %collective-permute-done.10.rest_3_ = bf16[256,256]{1,0:T(8,128)(2,1)S(1)} collective-permute-done((bf16[256,256]{1,0:T(8,128)(2,1)S(1)}, bf16[256,256]{1,0:T(8,128)(2,1)S(1)}, u32[]{:S(2)}, u32[]{:S(2)}) %collective-permute-start.10) | collective-permute-done | bytes 131104 | tf_op jit(solution)/shard_map/ppermute | solution.py:695
  54.6 2.4 %collective-permute-done.9.rest_2_ = bf16[256,256]{1,0:T(8,128)(2,1)S(1)} collective-permute-done((bf16[256,256]{1,0:T(8,128)(2,1)S(1)}, bf16[256,256]{1,0:T(8,128)(2,1)S(1)}, u32[]{:S(2)}, u32[]{:S(2)}) %collective-permute-start.9) | collective-permute-done | bytes 131104 | tf_op jit(solution)/shard_map/ppermute | solution.py:695
  57.1 1.3 %collective-permute-done.15.rest_6_ = bf16[256,256]{1,0:T(8,128)(2,1)S(1)} collective-permute-done((bf16[256,256]{1,0:T(8,128)(2,1)S(1)}, bf16[256,256]{1,0:T(8,128)(2,1)S(1)}, u32[]{:S(2)}, u32[]{:S(2)}) %collective-permute-start.15) | collective-permute-done | bytes 131104 | tf_op jit(solution)/shard_map/ppermute | solution.py:681
  58.4 8.6 %pair_update.1 = (f32[32,64,128]{2,1,0:T(8,128)}, f32[32,64,128]{2,1,0:T(8,128)}, bf16[128,32,128]{2,1,0:T(8,128)(2,1)}) custom-call(s32[8]{0:T(128)S(1)} %pad_add_fusion.left_slots_ref, s32[4]{0:T(128)S(1)} %get-tuple-element.98.right_firsts_ref, bf16[256,256]{1,0:T(8,128)(2,1)S(1)} %collective-permute-done.6.rest_0_, ...), custom_call_target="tpu_custom_call" | custom-call | flops 12000000000 | bytes 12000000 | tf_op jit(solution)/shard_map/pair_update/pallas_call | solution.py:533
  67.0 6.5 %all-to-all-start = ((bf16[32,4,32,128]{3,2,1,0:T(8,128)(2,1)}), bf16[32,4,32,128]{3,2,1,0:T(8,128)(2,1)S(1)}, u32[]{:S(2)}, u32[]{:S(2)}) async-start(bf16[32,4,32,128]{3,2,1,0:T(8,128)(2,1)} %bitcast.34), calls=%async_computation | async-start | bytes 2097152 | tf_op jit(solution)/shard_map/all_to_all | solution.py:804
  73.5 1.8 %collective-permute-start.17 = (bf16[8,64,256]{2,1,0:T(8,128)(2,1)}, bf16[8,64,256]{2,1,0:T(8,128)(2,1)S(1)}, u32[]{:S(2)}, u32[]{:S(2)}) collective-permute-start(bf16[8,64,256]{2,1,0:T(8,128)(2,1)} %get-tuple-element.117), channel_id=1, source_target_pairs={{0,8},{8,0},{16,24},{24,16},{1,9},{9,1},{17,25},{25,17},{2,10},{10... | collective-permute-start | bytes 786440 | tf_op jit(solution)/shard_map/ppermute | solution.py:734
  75.4 1.5 %collective-permute-start.18 = (bf16[8,64,256]{2,1,0:T(8,128)(2,1)}, bf16[8,64,256]{2,1,0:T(8,128)(2,1)S(1)}, u32[]{:S(2)}, u32[]{:S(2)}) collective-permute-start(bf16[8,64,256]{2,1,0:T(8,128)(2,1)} %get-tuple-element.118), channel_id=1, source_target_pairs={{0,16},{8,24},{16,0},{24,8},{1,17},{9,25},{17,1},{25,9},{2,18},{10... | collective-permute-start | bytes 786440 | tf_op jit(solution)/shard_map/ppermute | solution.py:734
  76.8 0.3 collective-permute-start.19
  77.1 13.7 %collective-permute-done.17 = bf16[8,64,256]{2,1,0:T(8,128)(2,1)S(1)} collective-permute-done((bf16[8,64,256]{2,1,0:T(8,128)(2,1)}, bf16[8,64,256]{2,1,0:T(8,128)(2,1)S(1)}, u32[]{:S(2)}, u32[]{:S(2)}) %collective-permute-start.17) | collective-permute-done | bytes 262176 | tf_op jit(solution)/shard_map/ppermute | solution.py:734
  90.8 0.7 copy-done.11
  91.5 0.7 copy-done.12
  92.2 7.0 %collective-permute-done.19 = bf16[8,64,256]{2,1,0:T(8,128)(2,1)} collective-permute-done((bf16[8,64,256]{2,1,0:T(8,128)(2,1)}, bf16[8,64,256]{2,1,0:T(8,128)(2,1)}, u32[]{:S(2)}, u32[]{:S(2)}) %collective-permute-start.19) | collective-permute-done | bytes 262176 | tf_op jit(solution)/shard_map/ppermute | solution.py:734
  99.2 1.9 %all-to-all-done.sides_ref = bf16[32,4,32,128]{3,2,1,0:T(8,128)(2,1)S(1)} async-done(((bf16[32,4,32,128]{3,2,1,0:T(8,128)(2,1)}), bf16[32,4,32,128]{3,2,1,0:T(8,128)(2,1)S(1)}, u32[]{:S(2)}, u32[]{:S(2)}) %all-to-all-start) | async-done | bytes 1048608 | tf_op jit(solution)/shard_map/all_to_all | solution.py:804
  101.1 1.6 %triangle_product.1 = bf16[32,4,16,128]{3,2,1,0:T(8,128)(2,1)} custom-call(bf16[32,4,32,128]{3,2,1,0:T(8,128)(2,1)S(1)} %all-to-all-done.sides_ref), custom_call_target="tpu_custom_call" | custom-call | flops 3000000000 | bytes 3000000 | tf_op jit(solution)/shard_map/triangle_product/pallas_call | solution.py:597
  102.8 3.0 %all-to-all-start.1 = ((bf16[32,4,16,128]{3,2,1,0:T(8,128)(2,1)}), bf16[32,4,16,128]{3,2,1,0:T(8,128)(2,1)S(1)}, u32[]{:S(2)}, u32[]{:S(2)}) async-start(bf16[32,4,16,128]{3,2,1,0:T(8,128)(2,1)} %triangle_product.1), calls=%async_computation.1 | async-start | bytes 1048576 | tf_op jit(solution)/shard_map/all_to_all | solution.py:807
  105.8 0.1 broadcast_in_dim.14
  105.9 0.1 broadcast_in_dim.15
  106.0 0.0 copy-start.9
  106.0 2.2 %pad_maximum_fusion = bf16[4,8,64,256]{3,2,1,0:T(8,128)(2,1)} fusion(bf16[1,8,64,256]{3,2,1,0:T(8,128)(2,1)} %bitcast.10, bf16[1,8,64,256]{3,2,1,0:T(8,128)(2,1)} %bitcast.38, bf16[1,8,64,256]{3,2,1,0:T(8,128)(2,1)} %bitcast.37, bf16[1,8,64,256]{3,2,1,0:T(8,128)(2,1)S(1)} %bitcast.36), kind=kLoop, calls=%fused_computation.2 | loop fusion | flops 1572864 | bytes 2097152 | tf_op jit(solution)/shard_map/stack | solution.py:809
  108.3 2.8 %gather_fusion = bf16[4,8,64,256]{3,2,1,0:T(8,128)(2,1)} fusion(bf16[4,8,64,256]{3,2,1,0:T(8,128)(2,1)} %pad_maximum_fusion, s32[1024]{0:T(1024)S(1)} %pad_clamp_fusion), kind=kCustom, calls=%fused_computation | custom fusion | bytes 2097168 | tf_op jit(solution)/shard_map/jit(_take)/gather | solution.py:809
  111.1 3.4 %convolution_add_fusion = f32[64,32,256]{2,1,0:T(8,128)} fusion(f32[64,32,256]{2,1,0:T(8,128)S(1)} %copy-done, bf16[32,64,256]{2,1,0:T(8,128)(2,1)} %bitcast.33, pred[32]{0:T(512)(128)(4,1)S(1)} %broadcast_in_dim.15, bf16[256,256]{1,0:T(8,128)(2,1)S(1)} %copy-done.9), kind=kOutput, calls=%fused_computation.1 | convolution fusion | flops 269484032 | bytes 5373984 | tf_op jit(solution)/shard_map/dot_general | solution.py:811
  114.5 7.7 %all-to-all-done.1 = bf16[32,4,16,128]{3,2,1,0:T(8,128)(2,1)S(1)} async-done(((bf16[32,4,16,128]{3,2,1,0:T(8,128)(2,1)}), bf16[32,4,16,128]{3,2,1,0:T(8,128)(2,1)S(1)}, u32[]{:S(2)}, u32[]{:S(2)}) %all-to-all-start.1) | async-done | bytes 524320 | tf_op jit(solution)/shard_map/all_to_all | solution.py:807
  122.2 2.8 %pair_result.1 = f32[64,32,128]{2,1,0:T(8,128)} custom-call(bf16[128,16,128]{2,1,0:T(8,128)(2,1)S(1)} %bitcast.26, bf16[128,128]{1,0:T(8,128)(2,1)S(1)} %copy-done.5, f32[32,64,128]{2,1,0:T(8,128)} %get-tuple-element.126.mid_hbm, f32[32,64,128]{2,1,0:T(8,128)} %get-tuple-element.127.gate_hbm), custom_call_target="tpu_custom_call" | custom-call | flops 3000000000 | bytes 3000000 | tf_op jit(solution)/shard_map/pair_result/pallas_call | solution.py:655
  (34 shorter events, 0.1 us)
Async XLA Ops:
  0.6 9.0 %copy-start.8 = (bf16[256,768]{1,0:T(8,128)(2,1)S(1)}, bf16[256,768]{1,0:T(8,128)(2,1)}, u32[]{:S(2)}) copy-start(bf16[256,768]{1,0:T(8,128)(2,1)} %param.13) | copy-start | bytes 1179652
  0.7 9.0 %slice-start = ((bf16[256,768]{1,0:T(8,128)(2,1)}), bf16[256,512]{1,0:T(8,128)(2,1)S(1)}, s32[]{:S(2)}) async-start(bf16[256,768]{1,0:T(8,128)(2,1)} %param.13), calls=%async_computation.2 | async-start | bytes 524288 | tf_op jit(solution)/shard_map/slice | solution.py:764
  5.1 8.0 %copy-start = (f32[64,32,256]{2,1,0:T(8,128)S(1)}, f32[64,32,256]{2,1,0:T(8,128)}, u32[]{:S(2)}) copy-start(f32[64,32,256]{2,1,0:T(8,128)} %block_hbm.1) | copy-start | bytes 6291460
  5.1 14.5 %collective-permute-start.3 = (bf16[8,64,256]{2,1,0:T(8,128)(2,1)}, bf16[8,64,256]{2,1,0:T(8,128)(2,1)S(1)}, u32[]{:S(2)}, u32[]{:S(2)}) collective-permute-start(bf16[8,64,256]{2,1,0:T(8,128)(2,1)} %get-tuple-element.71), channel_id=1, source_target_pairs={{0,8},{8,0},{16,24},{24,16},{1,9},{9,1},{17,25},{25,17},{2,10},{10... | collective-permute-start | bytes 786440 | tf_op jit(solution)/shard_map/ppermute | solution.py:734
  8.1 14.0 %collective-permute-start.4 = (bf16[8,64,256]{2,1,0:T(8,128)(2,1)}, bf16[8,64,256]{2,1,0:T(8,128)(2,1)S(1)}, u32[]{:S(2)}, u32[]{:S(2)}) collective-permute-start(bf16[8,64,256]{2,1,0:T(8,128)(2,1)} %get-tuple-element.72), channel_id=1, source_target_pairs={{0,16},{8,24},{16,0},{24,8},{1,17},{9,25},{17,1},{25,9},{2,18},{10... | collective-permute-start | bytes 786440 | tf_op jit(solution)/shard_map/ppermute | solution.py:734
  9.7 13.1 %collective-permute-start.5 = (bf16[8,64,256]{2,1,0:T(8,128)(2,1)}, bf16[8,64,256]{2,1,0:T(8,128)(2,1)}, u32[]{:S(2)}, u32[]{:S(2)}) collective-permute-start(bf16[8,64,256]{2,1,0:T(8,128)(2,1)} %get-tuple-element.73), channel_id=1, source_target_pairs={{0,24},{8,16},{16,8},{24,0},{1,25},{9,17},{17,9},{25,1},{2,26},{10... | collective-permute-start | bytes 786440 | tf_op jit(solution)/shard_map/ppermute | solution.py:734
  13.1 9.7 %copy-start.6 = (bf16[8,64,256]{2,1,0:T(8,128)(2,1)S(1)}, bf16[8,64,256]{2,1,0:T(8,128)(2,1)}, u32[]{:S(2)}) copy-start(bf16[8,64,256]{2,1,0:T(8,128)(2,1)} %get-tuple-element.85.rest_0_) | copy-start | bytes 786436
  16.1 17.7 %collective-permute-start = (bf16[528,256]{1,0:T(8,128)(2,1)}, bf16[528,256]{1,0:T(8,128)(2,1)S(1)}, u32[]{:S(2)}, u32[]{:S(2)}) collective-permute-start(bf16[528,256]{1,0:T(8,128)(2,1)} %get-tuple-element.67), channel_id=1, source_target_pairs={{0,8},{8,0},{16,24},{24,16},{1,9},{9,1},{17,25},{25,17},{2,10},{10... | collective-permute-start | bytes 811016 | tf_op jit(solution)/shard_map/ppermute | solution.py:734
  18.1 15.7 %collective-permute-start.1 = (bf16[528,256]{1,0:T(8,128)(2,1)}, bf16[528,256]{1,0:T(8,128)(2,1)S(1)}, u32[]{:S(2)}, u32[]{:S(2)}) collective-permute-start(bf16[528,256]{1,0:T(8,128)(2,1)} %get-tuple-element.68), channel_id=1, source_target_pairs={{0,16},{8,24},{16,0},{24,8},{1,17},{9,25},{17,1},{25,9},{2,18},{10... | collective-permute-start | bytes 811016 | tf_op jit(solution)/shard_map/ppermute | solution.py:734
  19.7 14.2 %collective-permute-start.2 = (bf16[528,256]{1,0:T(8,128)(2,1)}, bf16[528,256]{1,0:T(8,128)(2,1)S(1)}, u32[]{:S(2)}, u32[]{:S(2)}) collective-permute-start(bf16[528,256]{1,0:T(8,128)(2,1)} %get-tuple-element.69), channel_id=1, source_target_pairs={{0,24},{8,16},{16,8},{24,0},{1,25},{9,17},{17,9},{25,1},{2,26},{10... | collective-permute-start | bytes 811016 | tf_op jit(solution)/shard_map/ppermute | solution.py:734
  32.0 1.8 %copy-start.3 = (bf16[256,64]{0,1:T(8,128)(2,1)S(1)}, bf16[256,64]{0,1:T(8,128)(2,1)}, u32[]{:S(2)}) copy-start(bf16[256,64]{0,1:T(8,128)(2,1)} %param.15) | copy-start | bytes 98308
  32.1 1.8 %copy-start.7 = (bf16[528,256]{1,0:T(8,128)(2,1)S(1)}, bf16[528,256]{1,0:T(8,128)(2,1)}, u32[]{:S(2)}) copy-start(bf16[528,256]{1,0:T(8,128)(2,1)} %get-tuple-element.101.rest_4_.rest_8_) | copy-start | bytes 811012
  33.9 24.5 %copy-start.1 = (f32[64,32,128]{2,1,0:T(8,128)S(1)}, f32[64,32,128]{2,1,0:T(8,128)}, u32[]{:S(2)}) copy-start(f32[64,32,128]{2,1,0:T(8,128)} %param.11) | copy-start | bytes 3145732
  33.9 24.5 %copy-start.2 = (bf16[1024,128]{1,0:T(8,128)(2,1)S(1)}, bf16[1024,128]{1,0:T(8,128)(2,1)}, u32[]{:S(2)}) copy-start(bf16[1024,128]{1,0:T(8,128)(2,1)} %rest_12_.1) | copy-start | bytes 786436
  33.9 24.5 %copy-start.4 = (bf16[128,128]{1,0:T(8,128)(2,1)S(1)}, bf16[128,128]{1,0:T(8,128)(2,1)}, u32[]{:S(2)}) copy-start(bf16[128,128]{1,0:T(8,128)(2,1)} %rest_14_.1) | copy-start | bytes 98308
  38.2 8.5 %collective-permute-start.8 = (bf16[8,32,256]{2,1,0:T(8,128)(2,1)S(1)}, bf16[8,32,256]{2,1,0:T(8,128)(2,1)S(1)}, u32[]{:S(2)}, u32[]{:S(2)}) collective-permute-start(bf16[8,32,256]{2,1,0:T(8,128)(2,1)S(1)} %get-tuple-element.110.rest_8_), channel_id=1, source_target_pairs={{0,8},{8,0},{16,24},{24,16},{1,9},{9,1},{17,25},{25,17},{2,10},{10... | collective-permute-start | bytes 393224 | tf_op jit(solution)/shard_map/ppermute | solution.py:734
  39.8 12.3 %collective-permute-start.11 = (bf16[8,32,256]{2,1,0:T(8,128)(2,1)S(1)}, bf16[8,32,256]{2,1,0:T(8,128)(2,1)S(1)}, u32[]{:S(2)}, u32[]{:S(2)}) collective-permute-start(bf16[8,32,256]{2,1,0:T(8,128)(2,1)S(1)} %get-tuple-element.110.rest_8_), channel_id=1, source_target_pairs={{0,16},{8,24},{16,0},{24,8},{1,17},{9,25},{17,1},{25,9},{2,18},{10... | collective-permute-start | bytes 393224 | tf_op jit(solution)/shard_map/ppermute | solution.py:734
  40.3 12.5 %collective-permute-start.12 = (bf16[8,32,256]{2,1,0:T(8,128)(2,1)S(1)}, bf16[8,32,256]{2,1,0:T(8,128)(2,1)S(1)}, u32[]{:S(2)}, u32[]{:S(2)}) collective-permute-start(bf16[8,32,256]{2,1,0:T(8,128)(2,1)S(1)} %get-tuple-element.110.rest_8_), channel_id=1, source_target_pairs={{0,24},{8,16},{16,8},{24,0},{1,25},{9,17},{17,9},{25,1},{2,26},{10... | collective-permute-start | bytes 393224 | tf_op jit(solution)/shard_map/ppermute | solution.py:734
  41.8 10.3 %collective-permute-start.6 = (bf16[256,256]{1,0:T(8,128)(2,1)S(1)}, bf16[256,256]{1,0:T(8,128)(2,1)S(1)}, u32[]{:S(2)}, u32[]{:S(2)}) collective-permute-start(bf16[256,256]{1,0:T(8,128)(2,1)S(1)} %get-tuple-element.107), channel_id=1, source_target_pairs={{0,0},{1,1},{2,8},{3,9},{4,16},{5,17},{6,24},{7,25},{8,2},{9,3},{1... | collective-permute-start | bytes 393224 | tf_op jit(solution)/shard_map/ppermute | solution.py:695
  42.4 10.3 %collective-permute-start.7 = (bf16[256,256]{1,0:T(8,128)(2,1)S(1)}, bf16[256,256]{1,0:T(8,128)(2,1)S(1)}, u32[]{:S(2)}, u32[]{:S(2)}) collective-permute-start(bf16[256,256]{1,0:T(8,128)(2,1)S(1)} %get-tuple-element.107), channel_id=1, source_target_pairs={{0,2},{1,3},{2,10},{3,11},{4,18},{5,19},{6,26},{7,27},{8,4},{9,5},... | collective-permute-start | bytes 393224 | tf_op jit(solution)/shard_map/ppermute | solution.py:695
  46.7 7.9 %collective-permute-start.10 = (bf16[256,256]{1,0:T(8,128)(2,1)S(1)}, bf16[256,256]{1,0:T(8,128)(2,1)S(1)}, u32[]{:S(2)}, u32[]{:S(2)}) collective-permute-start(bf16[256,256]{1,0:T(8,128)(2,1)S(1)} %get-tuple-element.107), channel_id=1, source_target_pairs={{0,6},{1,7},{2,14},{3,15},{4,22},{5,23},{6,30},{7,31},{8,0},{9,1},... | collective-permute-start | bytes 393224 | tf_op jit(solution)/shard_map/ppermute | solution.py:695
  52.1 5.0 %collective-permute-start.9 = (bf16[256,256]{1,0:T(8,128)(2,1)S(1)}, bf16[256,256]{1,0:T(8,128)(2,1)S(1)}, u32[]{:S(2)}, u32[]{:S(2)}) collective-permute-start(bf16[256,256]{1,0:T(8,128)(2,1)S(1)} %get-tuple-element.107), channel_id=1, source_target_pairs={{0,4},{1,5},{2,12},{3,13},{4,20},{5,21},{6,28},{7,29},{8,6},{9,7},... | collective-permute-start | bytes 393224 | tf_op jit(solution)/shard_map/ppermute | solution.py:695
  52.1 5.0 %collective-permute-start.13 = (bf16[256,256]{1,0:T(8,128)(2,1)S(1)}, bf16[256,256]{1,0:T(8,128)(2,1)S(1)}, u32[]{:S(2)}, u32[]{:S(2)}) collective-permute-start(bf16[256,256]{1,0:T(8,128)(2,1)S(1)} %collective-permute-done.6.rest_0_), channel_id=1, source_target_pairs={{0,1},{1,0},{2,3},{3,2},{4,5},{5,4},{6,7},{7,6},{8,9},{9,8},{10,11... | collective-permute-start | bytes 393224 | tf_op jit(solution)/shard_map/ppermute | solution.py:681
  52.8 4.3 %collective-permute-start.14 = (bf16[256,256]{1,0:T(8,128)(2,1)S(1)}, bf16[256,256]{1,0:T(8,128)(2,1)S(1)}, u32[]{:S(2)}, u32[]{:S(2)}) collective-permute-start(bf16[256,256]{1,0:T(8,128)(2,1)S(1)} %collective-permute-done.7.rest_1_), channel_id=1, source_target_pairs={{0,1},{1,0},{2,3},{3,2},{4,5},{5,4},{6,7},{7,6},{8,9},{9,8},{10,11... | collective-permute-start | bytes 393224 | tf_op jit(solution)/shard_map/ppermute | solution.py:681
  54.6 2.5 %collective-permute-start.16 = (bf16[256,256]{1,0:T(8,128)(2,1)S(1)}, bf16[256,256]{1,0:T(8,128)(2,1)S(1)}, u32[]{:S(2)}, u32[]{:S(2)}) collective-permute-start(bf16[256,256]{1,0:T(8,128)(2,1)S(1)} %collective-permute-done.10.rest_3_), channel_id=1, source_target_pairs={{0,1},{1,0},{2,3},{3,2},{4,5},{5,4},{6,7},{7,6},{8,9},{9,8},{10,11... | collective-permute-start | bytes 393224 | tf_op jit(solution)/shard_map/ppermute | solution.py:681
  57.0 1.3 %collective-permute-start.15 = (bf16[256,256]{1,0:T(8,128)(2,1)S(1)}, bf16[256,256]{1,0:T(8,128)(2,1)S(1)}, u32[]{:S(2)}, u32[]{:S(2)}) collective-permute-start(bf16[256,256]{1,0:T(8,128)(2,1)S(1)} %collective-permute-done.9.rest_2_), channel_id=1, source_target_pairs={{0,1},{1,0},{2,3},{3,2},{4,5},{5,4},{6,7},{7,6},{8,9},{9,8},{10,11... | collective-permute-start | bytes 393224 | tf_op jit(solution)/shard_map/ppermute | solution.py:681
  67.0 34.1 %all-to-all-start = ((bf16[32,4,32,128]{3,2,1,0:T(8,128)(2,1)}), bf16[32,4,32,128]{3,2,1,0:T(8,128)(2,1)S(1)}, u32[]{:S(2)}, u32[]{:S(2)}) async-start(bf16[32,4,32,128]{3,2,1,0:T(8,128)(2,1)} %bitcast.34), calls=%async_computation | async-start | bytes 2097152 | tf_op jit(solution)/shard_map/all_to_all | solution.py:804
  73.5 32.5 %copy-start.10 = (bf16[8,64,256]{2,1,0:T(8,128)(2,1)S(1)}, bf16[8,64,256]{2,1,0:T(8,128)(2,1)}, u32[]{:S(2)}) copy-start(bf16[8,64,256]{2,1,0:T(8,128)(2,1)} %get-tuple-element.121) | copy-start | bytes 786436
  73.5 17.3 %collective-permute-start.17 = (bf16[8,64,256]{2,1,0:T(8,128)(2,1)}, bf16[8,64,256]{2,1,0:T(8,128)(2,1)S(1)}, u32[]{:S(2)}, u32[]{:S(2)}) collective-permute-start(bf16[8,64,256]{2,1,0:T(8,128)(2,1)} %get-tuple-element.117), channel_id=1, source_target_pairs={{0,8},{8,0},{16,24},{24,16},{1,9},{9,1},{17,25},{25,17},{2,10},{10... | collective-permute-start | bytes 786440 | tf_op jit(solution)/shard_map/ppermute | solution.py:734
  75.4 15.4 %collective-permute-start.18 = (bf16[8,64,256]{2,1,0:T(8,128)(2,1)}, bf16[8,64,256]{2,1,0:T(8,128)(2,1)S(1)}, u32[]{:S(2)}, u32[]{:S(2)}) collective-permute-start(bf16[8,64,256]{2,1,0:T(8,128)(2,1)} %get-tuple-element.118), channel_id=1, source_target_pairs={{0,16},{8,24},{16,0},{24,8},{1,17},{9,25},{17,1},{25,9},{2,18},{10... | collective-permute-start | bytes 786440 | tf_op jit(solution)/shard_map/ppermute | solution.py:734
  76.8 22.4 %collective-permute-start.19 = (bf16[8,64,256]{2,1,0:T(8,128)(2,1)}, bf16[8,64,256]{2,1,0:T(8,128)(2,1)}, u32[]{:S(2)}, u32[]{:S(2)}) collective-permute-start(bf16[8,64,256]{2,1,0:T(8,128)(2,1)} %get-tuple-element.119), channel_id=1, source_target_pairs={{0,24},{8,16},{16,8},{24,0},{1,25},{9,17},{17,9},{25,1},{2,26},{10... | collective-permute-start | bytes 786440 | tf_op jit(solution)/shard_map/ppermute | solution.py:734
  90.8 0.7 copy-start.11
  91.5 0.7 copy-start.12
  102.8 19.4 %all-to-all-start.1 = ((bf16[32,4,16,128]{3,2,1,0:T(8,128)(2,1)}), bf16[32,4,16,128]{3,2,1,0:T(8,128)(2,1)S(1)}, u32[]{:S(2)}, u32[]{:S(2)}) async-start(bf16[32,4,16,128]{3,2,1,0:T(8,128)(2,1)} %triangle_product.1), calls=%async_computation.1 | async-start | bytes 1048576 | tf_op jit(solution)/shard_map/all_to_all | solution.py:807
  106.0 5.1 %copy-start.9 = (bf16[256,256]{1,0:T(8,128)(2,1)S(1)}, bf16[256,256]{1,0:T(8,128)(2,1)}, u32[]{:S(2)}) copy-start(bf16[256,256]{1,0:T(8,128)(2,1)} %param.14) | copy-start | bytes 393220
  111.1 11.1 %copy-start.5 = (bf16[128,128]{1,0:T(8,128)(2,1)S(1)}, bf16[128,128]{1,0:T(8,128)(2,1)}, u32[]{:S(2)}) copy-start(bf16[128,128]{1,0:T(8,128)(2,1)} %final_ref.1) | copy-start | bytes 98308
